TPU v7x, 32 devices: a whole 2x2x4 slice. The times are simulated.
32 devices in a mesh: groups: 2 (over y), lon: 4 (over z), lat: 2 (over x), sub: 2 (over core).
Axes of the slice: x: 2, y: 2, z: 4, core: 2. Of those that a mesh axis runs over, the one named last changes fastest.
Arguments:
- grid_latent: bfloat16 [16384, 512], P(('groups', 'lon', 'lat', 'sub')), parts along dimension 0, may hold values from -6 to 6
- mesh_latent: bfloat16 [8192, 512], P(('groups', 'lon', 'lat', 'sub')), parts along dimension 0, may hold values from -6 to 6
- cotangent: bfloat16 [8192, 512], P(('groups', 'lon', 'lat', 'sub')), parts along dimension 0, may hold values from -6 to 6
- embed_weight: bfloat16 [512, 512], replicated, may hold values from -0.25 to 0.25
- merge_weight: bfloat16 [512, 512], replicated, may hold values from -0.125 to 0.125
- send_weight: bfloat16 [2, 512, 512], replicated, may hold values from -0.25 to 0.25
- recv_weight: bfloat16 [2, 512, 512], replicated, may hold values from -0.25 to 0.25
- update_weight: bfloat16 [2, 512, 512], replicated, may hold values from -0.109375 to 0.109375
- target_row: int32 [16384], P(('groups', 'lon', 'lat', 'sub')), parts along dimension 0, may hold values from 0 to 255
- send_rows: int32 [32, 6, 16], P(('groups', 'lon', 'lat', 'sub')), parts along dimension 0, may hold values from 0 to 512, as said below
- incoming_rows: int32 [32, 6, 16], P(('groups', 'lon', 'lat', 'sub')), parts along dimension 0, may hold values from 0 to 256, as said below
- border_mesh_rows: int32 [32, 6, 8], P(('groups', 'lon', 'lat', 'sub')), parts along dimension 0, may hold values from 0 to 255
- mesh_senders: int32 [8192, 6], P(('groups', 'lon', 'lat', 'sub')), parts along dimension 0, may hold values from 0 to 303, as said below
Outputs:
- mesh_out: bfloat16 [8192, 512], P(('groups', 'lon', 'lat', 'sub')), parts along dimension 0
- grid_grad: bfloat16 [16384, 512], P(('groups', 'lon', 'lat', 'sub')), parts along dimension 0
- embed_grad: float32 [1024, 512], P(('groups', 'lon', 'lat', 'sub')), parts along dimension 0
- merge_grad: float32 [1024, 512], P(('groups', 'lon', 'lat', 'sub')), parts along dimension 0
- send_grad: float32 [4, 512, 512], P('groups', ('lon', 'lat', 'sub')), parts along dimension 0
- recv_grad: float32 [4, 512, 512], P('groups', ('lon', 'lat', 'sub')), parts along dimension 0
- update_grad: float32 [4, 512, 512], P('groups', ('lon', 'lat', 'sub')), parts along dimension 0
There are 2 independent parts, one for each index of `groups`. A program takes and returns all parts, laid end to end along the dimension named above; an argument that names none is the same for every part. Nothing has to cross between parts.
Inputs may be any that keep to these rules, and one draw needn't show every extreme that they name: `send_rows`: an entry 512 marks an empty place. In each partition's block the named rows are distinct and each slot's used places come first; slot d % 4 of partition d is empty, every other slot holds 1 or more rows, and one slot of each partition holds all 16. An entry 256 marks an empty place; incoming_rows[d, s, k] < 256 exactly where send_rows[peer(d, s), back(d, s), k] < 512. `mesh_senders`: A partition's table is its own 256 rows followed by 48 received boundary rows, slot after slot; the rows of the partition's own slot d % 4 are never named, and every other received row is the sender of exactly one edge of that partition.
All inputs are finite; a program needn't handle non-finite values.
Results may differ from a plain program's by a relative error of at most 0.02.
Values may be sent and summed in bfloat16 or wider, within the bound.
No kernel may reach another device: no remote copies, remote signals or barrier semaphores. Data moves between devices by JAX's collectives and lax.ppermute only.
A program may use at most 128 MiB of HBM per device.

v0:
```python
import jax
import jax.numpy as jnp
from jax import lax
from jax.sharding import PartitionSpec as P


def extended_2(block, sides, width):
    for axis, dim in sides:
        count = lax.axis_size(axis)
        forward = [(i, i + 1) for i in range(count - 1)]
        forward.append((count - 1, 0))
        backward = [(target, source) for source, target in forward]
        low = lax.ppermute(
            lax.slice_in_dim(block, block.shape[dim] - width, None, axis=dim), axis, forward
        )
        high = lax.ppermute(lax.slice_in_dim(block, 0, width, axis=dim), axis, backward)
        block = jnp.concatenate([low, block, high], axis=dim)
    return block


def silu_slope(value):
    sig = jax.nn.sigmoid(value)
    return sig * (1.0 + value * (1.0 - sig))


def spread_grid(payload):
    column_count = lax.axis_size(("lat", "sub"))
    column = payload[:column_count]
    arrived = lax.all_to_all(column, ("lat", "sub"), split_axis=0, concat_axis=0, tiled=True)
    extended = extended_2(payload[column_count:], (("lon", 0),), 1)
    return jnp.concatenate([arrived, extended[0:1], extended[3:4]], axis=0)


def return_grid(payload):
    column_count = lax.axis_size(("lat", "sub"))
    column = payload[:column_count]
    arrived = lax.all_to_all(column, ("lat", "sub"), split_axis=0, concat_axis=0, tiled=True)
    extended = extended_2(payload[column_count:], (("lon", 0),), 1)
    return jnp.concatenate([arrived, extended[0:1], extended[3:4]], axis=0)


def spread_mesh(payload):
    column_count = lax.axis_size(("lat", "sub"))
    arrived = lax.all_to_all(
        payload[:column_count], ("lat", "sub"), split_axis=0, concat_axis=0, tiled=True
    )
    extended = extended_2(payload[column_count:], (("lon", 0),), 1)
    return jnp.concatenate([arrived, extended[0:1], extended[3:4]], axis=0)


def return_mesh(payload):
    column_count = lax.axis_size(("lat", "sub"))
    arrived = lax.all_to_all(
        payload[:column_count].astype(jnp.bfloat16),
        ("lat", "sub"),
        split_axis=0,
        concat_axis=0,
        tiled=True,
    ).astype(jnp.float32)
    extended = extended_2(payload[column_count:].astype(jnp.bfloat16), (("lon", 0),), 1).astype(
        jnp.float32
    )
    return jnp.concatenate([arrived, extended[0:1], extended[3:4]], axis=0)


def layer_forward(state, weight_send, weight_recv, weight_update, bounds, senders):
    width = state.shape[1]
    sent = jnp.dot(state, weight_send, preferred_element_type=jnp.float32).astype(jnp.bfloat16)
    incoming = spread_mesh(sent[bounds])
    recv = jnp.dot(state, weight_recv, preferred_element_type=jnp.float32)
    table = jnp.concatenate([sent, incoming.reshape(-1, width)], axis=0)
    pre_edge = table[senders].astype(jnp.float32) + recv[:, None, :]
    summed = jnp.sum(jax.nn.silu(pre_edge), axis=1).astype(jnp.bfloat16)
    result = (
        state.astype(jnp.float32)
        + jnp.dot(summed, weight_update, preferred_element_type=jnp.float32)
    ).astype(jnp.bfloat16)
    return (result, (state, table, recv, summed))


def layer_backward(grad_out, saved, weight_send, weight_recv, weight_update, bounds, senders):
    state, table, recv, summed = saved
    node_count, width = state.shape
    slot_count, depth = bounds.shape
    grad_sum = jnp.dot(grad_out, weight_update.T, preferred_element_type=jnp.float32).astype(
        jnp.bfloat16
    )
    pre_edge = table[senders].astype(jnp.float32) + recv[:, None, :]
    edge_grad = grad_sum.astype(jnp.float32)[:, None, :] * silu_slope(pre_edge)
    recv_low = jnp.sum(edge_grad, axis=1).astype(jnp.bfloat16)
    table_grad = jax.ops.segment_sum(
        edge_grad.reshape(-1, width), senders.reshape(-1), node_count + slot_count * depth
    )
    returned = return_mesh(table_grad[node_count:].reshape(slot_count, depth, width))
    grad_sent = table_grad[:node_count] + jax.ops.segment_sum(
        returned.reshape(-1, width), bounds.reshape(-1), node_count
    )
    sent_low = grad_sent.astype(jnp.bfloat16)
    partials = (
        jnp.dot(state.T, sent_low, preferred_element_type=jnp.float32),
        jnp.dot(state.T, recv_low, preferred_element_type=jnp.float32),
        jnp.dot(summed.T, grad_out, preferred_element_type=jnp.float32),
    )
    grad_in = grad_out.astype(jnp.float32) + jnp.dot(
        recv_low, weight_recv.T, preferred_element_type=jnp.float32
    )
    grad_in = (
        grad_in + jnp.dot(sent_low, weight_send.T, preferred_element_type=jnp.float32)
    ).astype(jnp.bfloat16)
    return (grad_in, partials)


def body(
    grid_latent,
    mesh_latent,
    cotangent,
    embed_weight,
    merge_weight,
    send_weight,
    recv_weight,
    update_weight,
    target_row,
    send_rows,
    incoming_rows,
    border_mesh_rows,
    mesh_senders,
):
    chosen_rows, width = grid_latent.shape
    node_count = mesh_latent.shape[0]
    layer_count = send_weight.shape[0]
    sends = send_rows[0]
    arrivals = incoming_rows[0]
    bounds = border_mesh_rows[0]
    flat_sends = sends.reshape(-1)
    kept = jnp.ones((chosen_rows + 1,), jnp.bool_).at[flat_sends].set(False)[:chosen_rows]
    local_labels = jnp.where(kept, target_row, node_count)
    pre_grid = jnp.dot(grid_latent, embed_weight, preferred_element_type=jnp.float32)
    message = jax.nn.silu(pre_grid).astype(jnp.bfloat16)
    padded_message = jnp.concatenate([message, jnp.zeros((1, width), jnp.bfloat16)], axis=0)
    arrived = spread_grid(padded_message[sends])
    all_labels = jnp.concatenate([local_labels, arrivals.reshape(-1)], axis=0)
    all_values = jnp.concatenate([message, arrived.reshape(-1, width)], axis=0).astype(jnp.float32)
    gathered = jax.ops.segment_sum(all_values, all_labels, node_count + 1)[:node_count]
    merged = gathered.astype(jnp.bfloat16)
    state = (
        mesh_latent.astype(jnp.float32)
        + jnp.dot(merged, merge_weight, preferred_element_type=jnp.float32)
    ).astype(jnp.bfloat16)
    saved = []
    for layer in range(layer_count):
        state, keep = layer_forward(
            state,
            send_weight[layer],
            recv_weight[layer],
            update_weight[layer],
            bounds,
            mesh_senders,
        )
        saved.append(keep)
    grad = cotangent
    send_list, recv_list, update_list = ([], [], [])
    for layer in reversed(range(layer_count)):
        grad, partials = layer_backward(
            grad,
            saved[layer],
            send_weight[layer],
            recv_weight[layer],
            update_weight[layer],
            bounds,
            mesh_senders,
        )
        partials = (
            lax.psum_scatter(partials[0], ("lon", "lat", "sub"), scatter_dimension=0, tiled=True),
            lax.psum_scatter(partials[1], ("lon", "lat", "sub"), scatter_dimension=0, tiled=True),
            lax.psum_scatter(partials[2], ("lon", "lat", "sub"), scatter_dimension=0, tiled=True),
        )
        send_list.insert(0, partials[0])
        recv_list.insert(0, partials[1])
        update_list.insert(0, partials[2])
    merge_partial = jnp.dot(merged.T, grad, preferred_element_type=jnp.float32)
    grad_merged = jnp.dot(grad, merge_weight.T, preferred_element_type=jnp.float32).astype(
        jnp.bfloat16
    )
    padded_grad = jnp.concatenate([grad_merged, jnp.zeros((1, width), jnp.bfloat16)], axis=0)
    replies = return_grid(padded_grad[arrivals])
    local_grad = jnp.concatenate(
        [padded_grad[local_labels], jnp.zeros((1, width), jnp.bfloat16)], axis=0
    )
    grid_back = local_grad.at[flat_sends].set(replies.reshape(-1, width))[:chosen_rows]
    grad_pre = (grid_back.astype(jnp.float32) * silu_slope(pre_grid)).astype(jnp.bfloat16)
    embed_partial = jnp.dot(grid_latent.T, grad_pre, preferred_element_type=jnp.float32)
    grid_grad = jnp.dot(grad_pre, embed_weight.T, preferred_element_type=jnp.float32).astype(
        jnp.bfloat16
    )
    embed_grad, merge_grad = (
        lax.psum_scatter(embed_partial, ("lon", "lat", "sub"), scatter_dimension=0, tiled=True),
        lax.psum_scatter(merge_partial, ("lon", "lat", "sub"), scatter_dimension=0, tiled=True),
    )
    send_grad = jnp.stack(send_list)
    recv_grad = jnp.stack(recv_list)
    update_grad = jnp.stack(update_list)
    return (state, grid_grad, embed_grad, merge_grad, send_grad, recv_grad, update_grad)


def solution(mesh):
    in_specs = (
        P(("groups", "lon", "lat", "sub"), None),
        P(("groups", "lon", "lat", "sub"), None),
        P(("groups", "lon", "lat", "sub"), None),
        P(),
        P(),
        P(),
        P(),
        P(),
        P(("groups", "lon", "lat", "sub")),
        P(("groups", "lon", "lat", "sub"), None, None),
        P(("groups", "lon", "lat", "sub"), None, None),
        P(("groups", "lon", "lat", "sub"), None, None),
        P(("groups", "lon", "lat", "sub"), None),
    )
    out_specs = (
        P(("groups", "lon", "lat", "sub"), None),
        P(("groups", "lon", "lat", "sub"), None),
        P(("groups", "lon", "lat", "sub"), None),
        P(("groups", "lon", "lat", "sub"), None),
        P("groups", ("lon", "lat", "sub"), None),
        P("groups", ("lon", "lat", "sub"), None),
        P("groups", ("lon", "lat", "sub"), None),
    )
    return jax.shard_map(body, mesh=mesh, in_specs=in_specs, out_specs=out_specs, check_vma=False)
```

profile of v0, /device:TPU:0, one launch (start us, length us, event | category | flops | bytes accessed | tf_op | source)
XLA Modules:
  0.0 599.5 jit_solution(17314565440162145435)
XLA Ops:
  26.3 4.7 mul.77
  31.3 7.5 %scatter_custom_fusion.1 = f32[257,512]{1,0:T(8,128)S(1)} fusion(s32[608]{0:T(1024)S(1)} %pad_add_fusion, bf16[96,512]{1,0:T(8,128)(2,1)S(1)} %bitcast.128, bf16[]{:T(256)} %constant.54, bf16[512,512]{1,0:T(8,128)(2,1)} %copy-done.17, f32[]{:T(128)} %constant.10.clone.1), kind=kCustom, calls=%fused_computation.46 | custom fusion | flops 1556480 | bytes 1148934 | tf_op jit(solution)/shard_map/scatter-add | solution.py:143
  53.9 4.8 gather_fusion.2
  60.9 5.9 multiply_reduce_fusion.3
  69.2 3.8 collective-permute-start.5
  80.2 4.8 gather_fusion.4
  87.2 7.8 %multiply_reduce_fusion.1 = (bf16[256,512]{1,0:T(8,128)(2,1)S(1)}, bf16[256,512]{1,0:T(8,128)(2,1)}, f32[256,6,512]{2,1,0:T(8,128)}) fusion(f32[256,512]{1,0:T(8,128)S(1)} %fusion.30, f32[256,6,512]{2,1,0:T(8,128)} %reshape.319, f32[256,512]{1,0:T(8,128)} %fusion.37), kind=kLoop, calls=%fused_computation.15 | loop fusion | flops 9175040 | bytes 7864320 | tf_op jit(solution)/shard_map/reduce_sum | solution.py:90
  95.1 4.7 add.201
  99.8 11.9 %scatter_custom_fusion.2 = f32[304,512]{1,0:T(8,128)S(1)} fusion(s32[1536]{0:T(1024)S(1)} %reshape.254, f32[1536,512]{1,0:T(8,128)} %mul.77, f32[1536,512]{1,0:T(8,128)} %add.201, f32[]{:T(128)} %constant.16.clone.1, f32[]{:T(128)} %constant.10.clone.1), kind=kCustom, calls=%fused_computation.30 | custom fusion | flops 7077888 | bytes 6914056 | tf_op jit(solution)/shard_map/scatter-add | solution.py:91
  115.5 3.8 collective-permute-start.7
  126.1 3.8 all-to-all-done.3
  138.6 4.2 multiply_reduce_fusion
  147.4 4.7 add.207
  154.6 4.7 mul.85
  159.3 11.9 %scatter_custom_fusion.4 = f32[304,512]{1,0:T(8,128)S(1)} fusion(s32[1536]{0:T(1024)S(1)} %reshape.254, f32[1536,512]{1,0:T(8,128)} %mul.85, f32[1536,512]{1,0:T(8,128)} %add.207, f32[]{:T(128)} %constant.16.clone.1, f32[]{:T(128)} %constant.10.clone.1), kind=kCustom, calls=%fused_computation.20 | custom fusion | flops 7077888 | bytes 6914056 | tf_op jit(solution)/shard_map/scatter-add | solution.py:91
  179.1 3.8 all-to-all-done.4
  196.9 3.8 collective-permute-start.11
  209.6 20.7 %reduce-scatter.21.cloned.1.call-done = f32[32,512]{1,0:T(8,128)} async-done(((f32[512,512]{1,0:T(8,128)}), f32[32,512]{1,0:T(8,128)}) %reduce-scatter.21.cloned.1.call-update) | async-done | bytes 65552 | tf_op jit(solution)/shard_map/reduce_scatter | solution.py:175
  231.9 58.5 %reduce-scatter.19.cloned.1.call-done = f32[32,512]{1,0:T(8,128)} async-done(((f32[512,512]{1,0:T(8,128)}), f32[32,512]{1,0:T(8,128)}) %reduce-scatter.19.cloned.1.call-update) | async-done | bytes 65552 | tf_op jit(solution)/shard_map/reduce_scatter | solution.py:174
  290.4 60.3 %reduce-scatter.17.cloned.1.call-done = f32[32,512]{1,0:T(8,128)} async-done(((f32[512,512]{1,0:T(8,128)}), f32[32,512]{1,0:T(8,128)}) %reduce-scatter.17.cloned.1.call-update) | async-done | bytes 65552 | tf_op jit(solution)/shard_map/reduce_scatter | solution.py:174
  352.2 58.4 %reduce-scatter.15.cloned.1.call-done = f32[32,512]{1,0:T(8,128)} async-done(((f32[512,512]{1,0:T(8,128)}), f32[32,512]{1,0:T(8,128)}) %reduce-scatter.15.cloned.1.call-update) | async-done | bytes 65552 | tf_op jit(solution)/shard_map/reduce_scatter | solution.py:173
  410.6 60.3 %reduce-scatter.13.cloned.1.call-done = f32[32,512]{1,0:T(8,128)} async-done(((f32[512,512]{1,0:T(8,128)}), f32[32,512]{1,0:T(8,128)}) %reduce-scatter.13.cloned.1.call-update) | async-done | bytes 65552 | tf_op jit(solution)/shard_map/reduce_scatter | solution.py:173
  472.5 59.2 %reduce-scatter.11.cloned.1.call-done = f32[32,512]{1,0:T(8,128)} async-done(((f32[512,512]{1,0:T(8,128)}), f32[32,512]{1,0:T(8,128)}) %reduce-scatter.11.cloned.1.call-update) | async-done | bytes 65552 | tf_op jit(solution)/shard_map/reduce_scatter | solution.py:197
  531.6 61.0 %reduce-scatter.25.cloned.1.call-done = f32[32,512]{1,0:T(8,128)} async-done(((f32[512,512]{1,0:T(8,128)}), f32[32,512]{1,0:T(8,128)}) %reduce-scatter.25.cloned.1.call-update) | async-done | bytes 65552
  (207 shorter events, 109.2 us)
Async XLA Ops:
  12.5 18.7 %collective-permute-start = (bf16[1,16,512]{2,1,0:T(8,128)(2,1)S(1)}, bf16[1,16,512]{2,1,0:T(8,128)(2,1)S(1)}, u32[]{:S(2)}, u32[]{:S(2)}) collective-permute-start(bf16[1,16,512]{2,1,0:T(8,128)(2,1)S(1)} %get-tuple-element.41), channel_id=1, source_target_pairs={{0,4},{4,8},{8,12},{12,0},{1,5},{5,9},{9,13},{13,1},{2,6},{6,10},{... | collective-permute-start | bytes 49160 | tf_op jit(solution)/shard_map/ppermute | solution.py:13
  15.6 15.6 %collective-permute-start.1 = (bf16[1,16,512]{2,1,0:T(8,128)(2,1)S(1)}, bf16[1,16,512]{2,1,0:T(8,128)(2,1)S(1)}, u32[]{:S(2)}, u32[]{:S(2)}) collective-permute-start(bf16[1,16,512]{2,1,0:T(8,128)(2,1)S(1)} %get-tuple-element.42), channel_id=1, source_target_pairs={{4,0},{8,4},{12,8},{0,12},{5,1},{9,5},{13,9},{1,13},{6,2},{10,6},{... | collective-permute-start | bytes 49160 | tf_op jit(solution)/shard_map/ppermute | solution.py:16
  18.3 12.9 %all-to-all-start = ((bf16[4,16,512]{2,1,0:T(8,128)(2,1)}), bf16[4,16,512]{2,1,0:T(8,128)(2,1)S(1)}, u32[]{:S(2)}, u32[]{:S(2)}) async-start(bf16[4,16,512]{2,1,0:T(8,128)(2,1)} %bitcast.2), calls=%async_computation | async-start | bytes 131072 | tf_op jit(solution)/shard_map/all_to_all | solution.py:29
  42.8 8.2 %collective-permute-start.2 = (bf16[1,8,512]{2,1,0:T(8,128)(2,1)S(1)}, bf16[1,8,512]{2,1,0:T(8,128)(2,1)S(1)}, u32[]{:S(2)}, u32[]{:S(2)}) collective-permute-start(bf16[1,8,512]{2,1,0:T(8,128)(2,1)S(1)} %get-tuple-element.45), channel_id=1, source_target_pairs={{0,4},{4,8},{8,12},{12,0},{1,5},{5,9},{9,13},{13,1},{2,6},{6,10},{... | collective-permute-start | bytes 24584 | tf_op jit(solution)/shard_map/ppermute | solution.py:13
  42.8 8.2 %collective-permute-start.3 = (bf16[1,8,512]{2,1,0:T(8,128)(2,1)S(1)}, bf16[1,8,512]{2,1,0:T(8,128)(2,1)S(1)}, u32[]{:S(2)}, u32[]{:S(2)}) collective-permute-start(bf16[1,8,512]{2,1,0:T(8,128)(2,1)S(1)} %get-tuple-element.46), channel_id=1, source_target_pairs={{4,0},{8,4},{12,8},{0,12},{5,1},{9,5},{13,9},{1,13},{6,2},{10,6},{... | collective-permute-start | bytes 24584 | tf_op jit(solution)/shard_map/ppermute | solution.py:16
  46.7 7.2 %all-to-all-start.1 = ((bf16[4,8,512]{2,1,0:T(8,128)(2,1)}), bf16[4,8,512]{2,1,0:T(8,128)(2,1)S(1)}, u32[]{:S(2)}, u32[]{:S(2)}) async-start(bf16[4,8,512]{2,1,0:T(8,128)(2,1)} %slice_bitcast_fusion.3), calls=%async_computation.1 | async-start | bytes 65536 | tf_op jit(solution)/shard_map/all_to_all | solution.py:44
  69.2 8.4 %collective-permute-start.4 = (bf16[1,8,512]{2,1,0:T(8,128)(2,1)S(1)}, bf16[1,8,512]{2,1,0:T(8,128)(2,1)S(1)}, u32[]{:S(2)}, u32[]{:S(2)}) collective-permute-start(bf16[1,8,512]{2,1,0:T(8,128)(2,1)S(1)} %get-tuple-element.43), channel_id=1, source_target_pairs={{0,4},{4,8},{8,12},{12,0},{1,5},{5,9},{9,13},{13,1},{2,6},{6,10},{... | collective-permute-start | bytes 24584 | tf_op jit(solution)/shard_map/ppermute | solution.py:13
  69.2 8.4 %collective-permute-start.5 = (bf16[1,8,512]{2,1,0:T(8,128)(2,1)S(1)}, bf16[1,8,512]{2,1,0:T(8,128)(2,1)S(1)}, u32[]{:S(2)}, u32[]{:S(2)}) collective-permute-start(bf16[1,8,512]{2,1,0:T(8,128)(2,1)S(1)} %get-tuple-element.44), channel_id=1, source_target_pairs={{4,0},{8,4},{12,8},{0,12},{5,1},{9,5},{13,9},{1,13},{6,2},{10,6},{... | collective-permute-start | bytes 24584 | tf_op jit(solution)/shard_map/ppermute | solution.py:16
  73.0 7.2 %all-to-all-start.2 = ((bf16[4,8,512]{2,1,0:T(8,128)(2,1)}), bf16[4,8,512]{2,1,0:T(8,128)(2,1)S(1)}, u32[]{:S(2)}, u32[]{:S(2)}) async-start(bf16[4,8,512]{2,1,0:T(8,128)(2,1)} %slice_bitcast_fusion.2), calls=%async_computation.2 | async-start | bytes 65536 | tf_op jit(solution)/shard_map/all_to_all | solution.py:44
  76.4 133.2 %reduce-scatter.23.cloned.1.call-start = ((), (), s32[]{:S(2)}) async-start(), calls=%async_computation.20 | async-start | bytes 1114112 | tf_op jit(solution)/shard_map/reduce_scatter | solution.py:175
  115.5 10.6 %collective-permute-start.6 = (bf16[1,8,512]{2,1,0:T(8,128)(2,1)S(1)}, bf16[1,8,512]{2,1,0:T(8,128)(2,1)S(1)}, u32[]{:S(2)}, u32[]{:S(2)}) collective-permute-start(bf16[1,8,512]{2,1,0:T(8,128)(2,1)S(1)} %get-tuple-element.37), channel_id=1, source_target_pairs={{0,4},{4,8},{8,12},{12,0},{1,5},{5,9},{9,13},{13,1},{2,6},{6,10},{... | collective-permute-start | bytes 24584 | tf_op jit(solution)/shard_map/ppermute | solution.py:13
  115.5 10.6 %collective-permute-start.7 = (bf16[1,8,512]{2,1,0:T(8,128)(2,1)S(1)}, bf16[1,8,512]{2,1,0:T(8,128)(2,1)S(1)}, u32[]{:S(2)}, u32[]{:S(2)}) collective-permute-start(bf16[1,8,512]{2,1,0:T(8,128)(2,1)S(1)} %get-tuple-element.38), channel_id=1, source_target_pairs={{4,0},{8,4},{12,8},{0,12},{5,1},{9,5},{13,9},{1,13},{6,2},{10,6},{... | collective-permute-start | bytes 24584 | tf_op jit(solution)/shard_map/ppermute | solution.py:16
  122.6 7.3 %all-to-all-start.3 = ((bf16[4,8,512]{2,1,0:T(8,128)(2,1)}), bf16[4,8,512]{2,1,0:T(8,128)(2,1)S(1)}, u32[]{:S(2)}, u32[]{:S(2)}) async-start(bf16[4,8,512]{2,1,0:T(8,128)(2,1)} %slice_bitcast_fusion.1), calls=%async_computation.3 | async-start | bytes 65536 | tf_op jit(solution)/shard_map/all_to_all | solution.py:53
  126.0 104.3 %reduce-scatter.21.cloned.1.call-start = ((), (), s32[]{:S(2)}) async-start(), calls=%async_computation.19 | async-start | bytes 1114112 | tf_op jit(solution)/shard_map/reduce_scatter | solution.py:175
  135.6 154.8 %reduce-scatter.19.cloned.1.call-start = ((), (), s32[]{:S(2)}) async-start(), calls=%async_computation.18 | async-start | bytes 1114112 | tf_op jit(solution)/shard_map/reduce_scatter | solution.py:174
  137.1 213.6 %reduce-scatter.17.cloned.1.call-start = ((), (), s32[]{:S(2)}) async-start(), calls=%async_computation.17 | async-start | bytes 1114112 | tf_op jit(solution)/shard_map/reduce_scatter | solution.py:174
  144.8 265.8 %reduce-scatter.15.cloned.1.call-start = ((), (), s32[]{:S(2)}) async-start(), calls=%async_computation.16 | async-start | bytes 1114112 | tf_op jit(solution)/shard_map/reduce_scatter | solution.py:173
  171.2 7.9 %collective-permute-start.8 = (bf16[1,8,512]{2,1,0:T(8,128)(2,1)S(1)}, bf16[1,8,512]{2,1,0:T(8,128)(2,1)S(1)}, u32[]{:S(2)}, u32[]{:S(2)}) collective-permute-start(bf16[1,8,512]{2,1,0:T(8,128)(2,1)S(1)} %get-tuple-element.35), channel_id=1, source_target_pairs={{0,4},{4,8},{8,12},{12,0},{1,5},{5,9},{9,13},{13,1},{2,6},{6,10},{... | collective-permute-start | bytes 24584 | tf_op jit(solution)/shard_map/ppermute | solution.py:13
  171.3 7.8 %collective-permute-start.9 = (bf16[1,8,512]{2,1,0:T(8,128)(2,1)S(1)}, bf16[1,8,512]{2,1,0:T(8,128)(2,1)S(1)}, u32[]{:S(2)}, u32[]{:S(2)}) collective-permute-start(bf16[1,8,512]{2,1,0:T(8,128)(2,1)S(1)} %get-tuple-element.36), channel_id=1, source_target_pairs={{4,0},{8,4},{12,8},{0,12},{5,1},{9,5},{13,9},{1,13},{6,2},{10,6},{... | collective-permute-start | bytes 24584 | tf_op jit(solution)/shard_map/ppermute | solution.py:16
  175.8 7.2 %all-to-all-start.4 = ((bf16[4,8,512]{2,1,0:T(8,128)(2,1)}), bf16[4,8,512]{2,1,0:T(8,128)(2,1)S(1)}, u32[]{:S(2)}, u32[]{:S(2)}) async-start(bf16[4,8,512]{2,1,0:T(8,128)(2,1)} %slice_bitcast_fusion), calls=%async_computation.4 | async-start | bytes 65536 | tf_op jit(solution)/shard_map/all_to_all | solution.py:53
  179.0 291.9 %reduce-scatter.13.cloned.1.call-start = ((), (), s32[]{:S(2)}) async-start(), calls=%async_computation.15 | async-start | bytes 1114112 | tf_op jit(solution)/shard_map/reduce_scatter | solution.py:173
  186.4 345.2 %reduce-scatter.11.cloned.1.call-start = ((), (), s32[]{:S(2)}) async-start(), calls=%async_computation.14 | async-start | bytes 1114112 | tf_op jit(solution)/shard_map/reduce_scatter | solution.py:197
  193.5 9.3 %all-to-all-start.5 = ((bf16[4,16,512]{2,1,0:T(8,128)(2,1)}), bf16[4,16,512]{2,1,0:T(8,128)(2,1)S(1)}, u32[]{:S(2)}, u32[]{:S(2)}) async-start(bf16[4,16,512]{2,1,0:T(8,128)(2,1)} %bitcast.32), calls=%async_computation.5 | async-start | bytes 131072 | tf_op jit(solution)/shard_map/all_to_all | solution.py:37
  196.7 395.9 %reduce-scatter.25.cloned.1.call-start = ((), (), s32[]{:S(2)}) async-start(), calls=%async_computation.21 | async-start | bytes 1114112
  (32 other events, 291.9 us)
Sparse Core Ops, SparseCore 0:
  114.9 54.8 reduce-scatter.22
  173.8 56.4 reduce-scatter.20
  234.0 56.3 reduce-scatter.18
  294.3 56.3 reduce-scatter.16
  354.2 56.3 reduce-scatter.14
  414.5 56.3 reduce-scatter.12
  475.1 56.4 reduce-scatter.10
  536.2 56.3 reduce-scatter.24
where the time goes:
time: 601 us; the launch traced here: 599 us
  waiting for transfers between devices  392 us (65%)
  other arithmetic  58.3 us (10%)
  local copies, waits for them, and re-layouts  56.1 us (9%)
  starting transfers between devices  44.9 us (7%)
  matrix products  33.5 us (6%)
  between operations  15 us (2%)
    reduce_scatter x2, waiting for transfers between devices, body(): lax.psum_scatter(partials[1], ('lon', 'lat', 'sub'), scatter_dimension=0,...  119 us
    reduce_scatter x2, waiting for transfers between devices, body(): lax.psum_scatter(partials[0], ('lon', 'lat', 'sub'), scatter_dimension=0,...  119 us
    unnamed x9, waiting for transfers between devices  61.2 us
    reduce_scatter x1, waiting for transfers between devices, body(): lax.psum_scatter(merge_partial, ('lon', 'lat', 'sub'), scatter_dimension=...  59.2 us
    scatter-add x2, other arithmetic, layer_backward(): jax.ops.segment_sum(edge_grad.reshape(-1, width), senders.reshape(-1), no...  23.8 us
    ppermute x6, starting transfers between devices, extended_2(): lax.ppermute(lax.slice_in_dim(block, 0, width, axis=dim), axis, backward)  21.2 us
    reduce_scatter x2, waiting for transfers between devices, body(): lax.psum_scatter(partials[2], ('lon', 'lat', 'sub'), scatter_dimension=0,...  20.7 us
    mul x4, local copies, waits for them, and re-layouts, layer_backward(): edge_grad = grad_sum.astype(jnp.float32)[:, None, :] * silu_slope(pre_edge)  14.4 us
  transfers between devices with their start and end apart: 26, of which 11 were waited for; matrix products, arithmetic and copies ran while one was open for 13% of the time, Pallas kernels for 0%

commit v1 on v0

--- a/solution.py
+++ b/solution.py
@@ -61,6 +61,21 @@
         jnp.float32
     )
     return jnp.concatenate([arrived, extended[0:1], extended[3:4]], axis=0)
+
+
+def scatter_weights(partials):
+    lon, lat, sub = (lax.axis_size(axis) for axis in ("lon", "lat", "sub"))
+    rows, width = partials[0].shape
+    depth = rows // (lon * lat * sub)
+    blocks = [
+        part.astype(jnp.bfloat16).reshape(lon, lat, sub, depth, width).transpose(2, 1, 0, 3, 4)
+        for part in partials
+    ]
+    block = jnp.concatenate(blocks, axis=3)
+    for axis in ("sub", "lat", "lon"):
+        block = lax.psum_scatter(block, axis, scatter_dimension=0, tiled=False)
+    block = block.astype(jnp.float32)
+    return [block[i * depth : (i + 1) * depth] for i in range(len(partials))]
 
 
 def layer_forward(state, weight_send, weight_recv, weight_update, bounds, senders):
@@ -169,11 +184,7 @@
             bounds,
             mesh_senders,
         )
-        partials = (
-            lax.psum_scatter(partials[0], ("lon", "lat", "sub"), scatter_dimension=0, tiled=True),
-            lax.psum_scatter(partials[1], ("lon", "lat", "sub"), scatter_dimension=0, tiled=True),
-            lax.psum_scatter(partials[2], ("lon", "lat", "sub"), scatter_dimension=0, tiled=True),
-        )
+        partials = scatter_weights(partials)
         send_list.insert(0, partials[0])
         recv_list.insert(0, partials[1])
         update_list.insert(0, partials[2])
@@ -192,10 +203,7 @@
     grid_grad = jnp.dot(grad_pre, embed_weight.T, preferred_element_type=jnp.float32).astype(
         jnp.bfloat16
     )
-    embed_grad, merge_grad = (
-        lax.psum_scatter(embed_partial, ("lon", "lat", "sub"), scatter_dimension=0, tiled=True),
-        lax.psum_scatter(merge_partial, ("lon", "lat", "sub"), scatter_dimension=0, tiled=True),
-    )
+    embed_grad, merge_grad = scatter_weights((embed_partial, merge_partial))
     send_grad = jnp.stack(send_list)
     recv_grad = jnp.stack(recv_list)
     update_grad = jnp.stack(update_list)

time: 601 us -> 357 us (0.59)
  waiting for transfers between devices: 392 us -> 157 us
  matrix products: 33.5 us -> 23.3 us
    reduce_scatter x7 -> x9, waiting for transfers between devices: 317 us -> 146 us  [scatter_weights(): block = lax.psum_scatter(block, axis, scatter_dimension=0, tiled=False)]
    unnamed x9, waiting for transfers between devices: 61.2 us -> 0.15 us
  transfers between devices with their start and end apart: 26 -> 27, of which waited for: 11 -> 12; matrix products, arithmetic and copies ran while one was open for 13% -> 9% of each run, Pallas kernels for 0% -> 0%
where the time goes in v1:
time: 357 us; the launch traced here: 356 us
  waiting for transfers between devices  157 us (44%)
  other arithmetic  61 us (17%)
  local copies, waits for them, and re-layouts  55.4 us (16%)
  starting transfers between devices  44.5 us (12%)
  matrix products  23.3 us (7%)
  between operations  14.8 us (4%)
    reduce_scatter x9, waiting for transfers between devices, scatter_weights(): block = lax.psum_scatter(block, axis, scatter_dimension=0, tiled=False)  146 us
    scatter-add x2, other arithmetic, layer_backward(): jax.ops.segment_sum(edge_grad.reshape(-1, width), senders.reshape(-1), no...  23.9 us
    ppermute x6, starting transfers between devices, extended_2(): lax.ppermute(lax.slice_in_dim(block, 0, width, axis=dim), axis, backward)  21.2 us
    mul x4, local copies, waits for them, and re-layouts, layer_backward(): edge_grad = grad_sum.astype(jnp.float32)[:, None, :] * silu_slope(pre_edge)  14.4 us
    reduce_sum x2, other arithmetic, layer_backward(): recv_low = jnp.sum(edge_grad, axis=1).astype(jnp.bfloat16)  12 us
    gather x2, local copies, waits for them, and re-layouts, layer_forward(): pre_edge = table[senders].astype(jnp.float32) + recv[:, None, :]  9.63 us
    add x2, local copies, waits for them, and re-layouts, layer_forward(): pre_edge = table[senders].astype(jnp.float32) + recv[:, None, :]  9.34 us
    all_to_all x2, waiting for transfers between devices, return_mesh(): lax.all_to_all(payload[:column_count].astype(jnp.bfloat16), ('lat', 'sub'...  7.76 us
  transfers between devices with their start and end apart: 27, of which 12 were waited for; matrix products, arithmetic and copies ran while one was open for 9% of the time, Pallas kernels for 0%

profile of v1, /device:TPU:0, one launch (start us, length us, event | category | flops | bytes accessed | tf_op | source)
XLA Modules:
  0.0 355.6 jit_solution(14282752651622308018)
XLA Ops:
  26.4 4.7 %mul.77 = f32[1536,512]{1,0:T(8,128)} reshape(f32[256,6,512]{2,1,0:T(8,128)} %mul.73) | data formatting | bytes 6291456 | tf_op jit(solution)/shard_map/mul | solution.py:104
  31.4 7.5 %scatter_custom_fusion.1 = f32[257,512]{1,0:T(8,128)S(1)} fusion(s32[608]{0:T(1024)S(1)} %pad_add_fusion, bf16[96,512]{1,0:T(8,128)(2,1)S(1)} %bitcast.172, bf16[]{:T(256)} %constant.54, bf16[512,512]{1,0:T(8,128)(2,1)} %copy-done.17, f32[]{:T(128)} %constant.10.clone.1), kind=kCustom, calls=%fused_computation.55 | custom fusion | flops 1556480 | bytes 1148934 | tf_op jit(solution)/shard_map/scatter-add | solution.py:158
  54.0 4.8 %gather_fusion.2 = bf16[1536,512]{1,0:T(8,128)(2,1)S(1)} fusion(bf16[304,512]{1,0:T(8,128)(2,1)S(1)} %pad_maximum_fusion.3, s32[2048]{0:T(1024)S(1)} %pad_clamp_fusion), kind=kCustom, calls=%fused_computation.2 | custom fusion | bytes 3151872 | tf_op jit(solution)/shard_map/gather | solution.py:87
  61.0 5.9 %multiply_reduce_fusion.3 = (bf16[256,512]{1,0:T(8,128)(2,1)S(1)}, f32[256,6,512]{2,1,0:T(8,128)}) fusion(f32[256,6,512]{2,1,0:T(8,128)} %reshape.367, f32[256,512]{1,0:T(8,128)} %fusion.44), kind=kLoop, calls=%fused_computation.18 | loop fusion | flops 4587520 | bytes 7077888 | tf_op jit(solution)/shard_map/reduce_sum | solution.py:88
  77.6 4.7 %add.209 = f32[1536,512]{1,0:T(8,128)} reshape(f32[256,6,512]{2,1,0:T(8,128)} %get-tuple-element.13) | data formatting | bytes 6291456 | tf_op jit(solution)/shard_map/add | solution.py:87
  82.3 4.8 %gather_fusion.4 = bf16[1536,512]{1,0:T(8,128)(2,1)S(1)} fusion(bf16[304,512]{1,0:T(8,128)(2,1)S(1)} %pad_maximum_fusion.4, s32[2048]{0:T(1024)S(1)} %pad_clamp_fusion), kind=kCustom, calls=%fused_computation.4 | custom fusion | bytes 3151872 | tf_op jit(solution)/shard_map/gather | solution.py:87
  89.4 7.9 %multiply_reduce_fusion.1 = (bf16[256,512]{1,0:T(8,128)(2,1)}, bf16[256,512]{1,0:T(8,128)(2,1)}, f32[256,6,512]{2,1,0:T(8,128)}) fusion(f32[256,512]{1,0:T(8,128)S(1)} %fusion.30, f32[256,6,512]{2,1,0:T(8,128)} %reshape.368, f32[256,512]{1,0:T(8,128)} %fusion.37), kind=kLoop, calls=%fused_computation.15 | loop fusion | flops 9175040 | bytes 7864320 | tf_op jit(solution)/shard_map/reduce_sum | solution.py:105
  97.3 4.7 %add.203 = f32[1536,512]{1,0:T(8,128)} reshape(f32[256,6,512]{2,1,0:T(8,128)} %get-tuple-element.11) | data formatting | bytes 6291456 | tf_op jit(solution)/shard_map/add | solution.py:87
  102.0 12.0 %scatter_custom_fusion.2 = f32[304,512]{1,0:T(8,128)S(1)} fusion(s32[1536]{0:T(1024)S(1)} %reshape.303, f32[1536,512]{1,0:T(8,128)} %mul.77, f32[1536,512]{1,0:T(8,128)} %add.203, f32[]{:T(128)} %constant.16.clone.1, f32[]{:T(128)} %constant.10.clone.1), kind=kCustom, calls=%fused_computation.30 | custom fusion | flops 7077888 | bytes 6914056 | tf_op jit(solution)/shard_map/scatter-add | solution.py:106
  123.0 3.9 %all-to-all-done.3 = bf16[4,8,512]{2,1,0:T(8,128)(2,1)S(1)} async-done(((bf16[4,8,512]{2,1,0:T(8,128)(2,1)}), bf16[4,8,512]{2,1,0:T(8,128)(2,1)S(1)}, u32[]{:S(2)}, u32[]{:S(2)}) %all-to-all-start.3) | async-done | bytes 32800 | tf_op jit(solution)/shard_map/all_to_all | solution.py:53
  131.1 4.1 %multiply_reduce_fusion = bf16[256,512]{1,0:T(8,128)(2,1)S(1)} fusion(f32[256,6,512]{2,1,0:T(8,128)} %get-tuple-element.13, f32[256,512]{1,0:T(8,128)S(1)} %fusion.29), kind=kLoop, calls=%fused_computation.14 | loop fusion | flops 6946816 | bytes 3932160 | tf_op jit(solution)/shard_map/reduce_sum | solution.py:105
  137.7 4.7 %mul.85 = f32[1536,512]{1,0:T(8,128)} reshape(f32[256,6,512]{2,1,0:T(8,128)} %mul.81) | data formatting | bytes 6291456 | tf_op jit(solution)/shard_map/mul | solution.py:104
  142.3 11.9 %scatter_custom_fusion.4 = f32[304,512]{1,0:T(8,128)S(1)} fusion(s32[1536]{0:T(1024)S(1)} %reshape.303, f32[1536,512]{1,0:T(8,128)} %mul.85, f32[1536,512]{1,0:T(8,128)} %add.209, f32[]{:T(128)} %constant.16.clone.1, f32[]{:T(128)} %constant.10.clone.1), kind=kCustom, calls=%fused_computation.20 | custom fusion | flops 7077888 | bytes 6914056 | tf_op jit(solution)/shard_map/scatter-add | solution.py:106
  164.3 3.9 %all-to-all-done.4 = bf16[4,8,512]{2,1,0:T(8,128)(2,1)S(1)} async-done(((bf16[4,8,512]{2,1,0:T(8,128)(2,1)}), bf16[4,8,512]{2,1,0:T(8,128)(2,1)S(1)}, u32[]{:S(2)}, u32[]{:S(2)}) %all-to-all-start.4) | async-done | bytes 32800 | tf_op jit(solution)/shard_map/all_to_all | solution.py:53
  177.7 3.8 %collective-permute-start.11 = (bf16[1,16,512]{2,1,0:T(8,128)(2,1)S(1)}, bf16[1,16,512]{2,1,0:T(8,128)(2,1)S(1)}, u32[]{:S(2)}, u32[]{:S(2)}) collective-permute-start(bf16[1,16,512]{2,1,0:T(8,128)(2,1)S(1)} %get-tuple-element.27), channel_id=1, source_target_pairs={{4,0},{8,4},{12,8},{0,12},{5,1},{9,5},{13,9},{1,13},{6,2},{10,6},{... | collective-permute-start | bytes 49160 | tf_op jit(solution)/shard_map/ppermute | solution.py:16
  195.5 4.1 %reduce-scatter.10.cloned.1.call-done = bf16[1,2,4,64,512]{4,3,2,1,0:T(8,128)(2,1)} async-done(((bf16[2,2,4,64,512]{4,3,2,1,0:T(8,128)(2,1)}), bf16[1,2,4,64,512]{4,3,2,1,0:T(8,128)(2,1)}) %reduce-scatter.10.cloned.1.call-update) | async-done | bytes 524304 | tf_op jit(solution)/shard_map/reduce_scatter | solution.py:76
  199.6 12.5 %reduce-scatter.22.cloned.1.call-done = bf16[1,2,4,96,512]{4,3,2,1,0:T(8,128)(2,1)} async-done(((bf16[2,2,4,96,512]{4,3,2,1,0:T(8,128)(2,1)}), bf16[1,2,4,96,512]{4,3,2,1,0:T(8,128)(2,1)}) %reduce-scatter.22.cloned.1.call-update) | async-done | bytes 786448 | tf_op jit(solution)/shard_map/reduce_scatter | solution.py:76
  212.2 12.5 %reduce-scatter.16.cloned.1.call-done = bf16[1,2,4,96,512]{4,3,2,1,0:T(8,128)(2,1)} async-done(((bf16[2,2,4,96,512]{4,3,2,1,0:T(8,128)(2,1)}), bf16[1,2,4,96,512]{4,3,2,1,0:T(8,128)(2,1)}) %reduce-scatter.16.cloned.1.call-update) | async-done | bytes 786448 | tf_op jit(solution)/shard_map/reduce_scatter | solution.py:76
  224.8 17.9 %reduce-scatter.12.cloned.1.call-done = bf16[1,4,64,512]{3,2,1,0:T(8,128)(2,1)} async-done(((bf16[2,4,64,512]{3,2,1,0:T(8,128)(2,1)}), bf16[1,4,64,512]{3,2,1,0:T(8,128)(2,1)}) %reduce-scatter.12.cloned.1.call-update) | async-done | bytes 262160 | tf_op jit(solution)/shard_map/reduce_scatter | solution.py:76
  242.7 19.5 %reduce-scatter.24.cloned.1.call-done = bf16[1,4,96,512]{3,2,1,0:T(8,128)(2,1)} async-done(((bf16[2,4,96,512]{3,2,1,0:T(8,128)(2,1)}), bf16[1,4,96,512]{3,2,1,0:T(8,128)(2,1)}) %reduce-scatter.24.cloned.1.call-update) | async-done | bytes 393232 | tf_op jit(solution)/shard_map/reduce_scatter | solution.py:76
  262.3 19.6 %reduce-scatter.18.cloned.1.call-done = bf16[1,4,96,512]{3,2,1,0:T(8,128)(2,1)} async-done(((bf16[2,4,96,512]{3,2,1,0:T(8,128)(2,1)}), bf16[1,4,96,512]{3,2,1,0:T(8,128)(2,1)}) %reduce-scatter.18.cloned.1.call-update) | async-done | bytes 393232 | tf_op jit(solution)/shard_map/reduce_scatter | solution.py:76
  284.2 19.6 %reduce-scatter.14.cloned.1.call-done = bf16[1,64,512]{2,1,0:T(8,128)(2,1)} async-done(((bf16[4,64,512]{2,1,0:T(8,128)(2,1)}), bf16[1,64,512]{2,1,0:T(8,128)(2,1)}) %reduce-scatter.14.cloned.1.call-update) | async-done | bytes 65552 | tf_op jit(solution)/shard_map/reduce_scatter | solution.py:76
  305.3 19.8 %reduce-scatter.26.cloned.1.call-done = bf16[1,96,512]{2,1,0:T(8,128)(2,1)} async-done(((bf16[4,96,512]{2,1,0:T(8,128)(2,1)}), bf16[1,96,512]{2,1,0:T(8,128)(2,1)}) %reduce-scatter.26.cloned.1.call-update) | async-done | bytes 98320 | tf_op jit(solution)/shard_map/reduce_scatter | solution.py:76
  325.9 20.4 %reduce-scatter.20.cloned.1.call-done = bf16[1,96,512]{2,1,0:T(8,128)(2,1)} async-done(((bf16[4,96,512]{2,1,0:T(8,128)(2,1)}), bf16[1,96,512]{2,1,0:T(8,128)(2,1)}) %reduce-scatter.20.cloned.1.call-update) | async-done | bytes 98320 | tf_op jit(solution)/shard_map/reduce_scatter | solution.py:76
  (223 shorter events, 105.7 us)
Async XLA Ops:
  12.5 18.8 %collective-permute-start = (bf16[1,16,512]{2,1,0:T(8,128)(2,1)S(1)}, bf16[1,16,512]{2,1,0:T(8,128)(2,1)S(1)}, u32[]{:S(2)}, u32[]{:S(2)}) collective-permute-start(bf16[1,16,512]{2,1,0:T(8,128)(2,1)S(1)} %get-tuple-element.28), channel_id=1, source_target_pairs={{0,4},{4,8},{8,12},{12,0},{1,5},{5,9},{9,13},{13,1},{2,6},{6,10},{... | collective-permute-start | bytes 49160 | tf_op jit(solution)/shard_map/ppermute | solution.py:13
  15.6 15.7 %collective-permute-start.1 = (bf16[1,16,512]{2,1,0:T(8,128)(2,1)S(1)}, bf16[1,16,512]{2,1,0:T(8,128)(2,1)S(1)}, u32[]{:S(2)}, u32[]{:S(2)}) collective-permute-start(bf16[1,16,512]{2,1,0:T(8,128)(2,1)S(1)} %get-tuple-element.29), channel_id=1, source_target_pairs={{4,0},{8,4},{12,8},{0,12},{5,1},{9,5},{13,9},{1,13},{6,2},{10,6},{... | collective-permute-start | bytes 49160 | tf_op jit(solution)/shard_map/ppermute | solution.py:16
  18.3 13.0 %all-to-all-start = ((bf16[4,16,512]{2,1,0:T(8,128)(2,1)}), bf16[4,16,512]{2,1,0:T(8,128)(2,1)S(1)}, u32[]{:S(2)}, u32[]{:S(2)}) async-start(bf16[4,16,512]{2,1,0:T(8,128)(2,1)} %bitcast.2), calls=%async_computation | async-start | bytes 131072 | tf_op jit(solution)/shard_map/all_to_all | solution.py:29
  42.9 8.2 %collective-permute-start.2 = (bf16[1,8,512]{2,1,0:T(8,128)(2,1)S(1)}, bf16[1,8,512]{2,1,0:T(8,128)(2,1)S(1)}, u32[]{:S(2)}, u32[]{:S(2)}) collective-permute-start(bf16[1,8,512]{2,1,0:T(8,128)(2,1)S(1)} %get-tuple-element.32), channel_id=1, source_target_pairs={{0,4},{4,8},{8,12},{12,0},{1,5},{5,9},{9,13},{13,1},{2,6},{6,10},{... | collective-permute-start | bytes 24584 | tf_op jit(solution)/shard_map/ppermute | solution.py:13
  42.9 8.2 %collective-permute-start.3 = (bf16[1,8,512]{2,1,0:T(8,128)(2,1)S(1)}, bf16[1,8,512]{2,1,0:T(8,128)(2,1)S(1)}, u32[]{:S(2)}, u32[]{:S(2)}) collective-permute-start(bf16[1,8,512]{2,1,0:T(8,128)(2,1)S(1)} %get-tuple-element.33), channel_id=1, source_target_pairs={{4,0},{8,4},{12,8},{0,12},{5,1},{9,5},{13,9},{1,13},{6,2},{10,6},{... | collective-permute-start | bytes 24584 | tf_op jit(solution)/shard_map/ppermute | solution.py:16
  46.7 7.2 %all-to-all-start.1 = ((bf16[4,8,512]{2,1,0:T(8,128)(2,1)}), bf16[4,8,512]{2,1,0:T(8,128)(2,1)S(1)}, u32[]{:S(2)}, u32[]{:S(2)}) async-start(bf16[4,8,512]{2,1,0:T(8,128)(2,1)} %slice_bitcast_fusion.5), calls=%async_computation.1 | async-start | bytes 65536 | tf_op jit(solution)/shard_map/all_to_all | solution.py:44
  69.2 13.1 %collective-permute-start.4 = (bf16[1,8,512]{2,1,0:T(8,128)(2,1)S(1)}, bf16[1,8,512]{2,1,0:T(8,128)(2,1)S(1)}, u32[]{:S(2)}, u32[]{:S(2)}) collective-permute-start(bf16[1,8,512]{2,1,0:T(8,128)(2,1)S(1)} %get-tuple-element.30), channel_id=1, source_target_pairs={{0,4},{4,8},{8,12},{12,0},{1,5},{5,9},{9,13},{13,1},{2,6},{6,10},{... | collective-permute-start | bytes 24584 | tf_op jit(solution)/shard_map/ppermute | solution.py:13
  69.2 13.1 %collective-permute-start.5 = (bf16[1,8,512]{2,1,0:T(8,128)(2,1)S(1)}, bf16[1,8,512]{2,1,0:T(8,128)(2,1)S(1)}, u32[]{:S(2)}, u32[]{:S(2)}) collective-permute-start(bf16[1,8,512]{2,1,0:T(8,128)(2,1)S(1)} %get-tuple-element.31), channel_id=1, source_target_pairs={{4,0},{8,4},{12,8},{0,12},{5,1},{9,5},{13,9},{1,13},{6,2},{10,6},{... | collective-permute-start | bytes 24584 | tf_op jit(solution)/shard_map/ppermute | solution.py:16
  73.0 9.2 %all-to-all-start.2 = ((bf16[4,8,512]{2,1,0:T(8,128)(2,1)}), bf16[4,8,512]{2,1,0:T(8,128)(2,1)S(1)}, u32[]{:S(2)}, u32[]{:S(2)}) async-start(bf16[4,8,512]{2,1,0:T(8,128)(2,1)} %slice_bitcast_fusion.4), calls=%async_computation.2 | async-start | bytes 65536 | tf_op jit(solution)/shard_map/all_to_all | solution.py:44
  114.7 8.3 %collective-permute-start.6 = (bf16[1,8,512]{2,1,0:T(8,128)(2,1)S(1)}, bf16[1,8,512]{2,1,0:T(8,128)(2,1)S(1)}, u32[]{:S(2)}, u32[]{:S(2)}) collective-permute-start(bf16[1,8,512]{2,1,0:T(8,128)(2,1)S(1)} %get-tuple-element.16), channel_id=1, source_target_pairs={{0,4},{4,8},{8,12},{12,0},{1,5},{5,9},{9,13},{13,1},{2,6},{6,10},{... | collective-permute-start | bytes 24584 | tf_op jit(solution)/shard_map/ppermute | solution.py:13
  114.7 8.3 %collective-permute-start.7 = (bf16[1,8,512]{2,1,0:T(8,128)(2,1)S(1)}, bf16[1,8,512]{2,1,0:T(8,128)(2,1)S(1)}, u32[]{:S(2)}, u32[]{:S(2)}) collective-permute-start(bf16[1,8,512]{2,1,0:T(8,128)(2,1)S(1)} %get-tuple-element.17), channel_id=1, source_target_pairs={{4,0},{8,4},{12,8},{0,12},{5,1},{9,5},{13,9},{1,13},{6,2},{10,6},{... | collective-permute-start | bytes 24584 | tf_op jit(solution)/shard_map/ppermute | solution.py:16
  119.7 7.2 %all-to-all-start.3 = ((bf16[4,8,512]{2,1,0:T(8,128)(2,1)}), bf16[4,8,512]{2,1,0:T(8,128)(2,1)S(1)}, u32[]{:S(2)}, u32[]{:S(2)}) async-start(bf16[4,8,512]{2,1,0:T(8,128)(2,1)} %slice_bitcast_fusion.3), calls=%async_computation.3 | async-start | bytes 65536 | tf_op jit(solution)/shard_map/all_to_all | solution.py:53
  154.9 9.3 %collective-permute-start.8 = (bf16[1,8,512]{2,1,0:T(8,128)(2,1)S(1)}, bf16[1,8,512]{2,1,0:T(8,128)(2,1)S(1)}, u32[]{:S(2)}, u32[]{:S(2)}) collective-permute-start(bf16[1,8,512]{2,1,0:T(8,128)(2,1)S(1)} %get-tuple-element.14), channel_id=1, source_target_pairs={{0,4},{4,8},{8,12},{12,0},{1,5},{5,9},{9,13},{13,1},{2,6},{6,10},{... | collective-permute-start | bytes 24584 | tf_op jit(solution)/shard_map/ppermute | solution.py:13
  154.9 9.3 %collective-permute-start.9 = (bf16[1,8,512]{2,1,0:T(8,128)(2,1)S(1)}, bf16[1,8,512]{2,1,0:T(8,128)(2,1)S(1)}, u32[]{:S(2)}, u32[]{:S(2)}) collective-permute-start(bf16[1,8,512]{2,1,0:T(8,128)(2,1)S(1)} %get-tuple-element.15), channel_id=1, source_target_pairs={{4,0},{8,4},{12,8},{0,12},{5,1},{9,5},{13,9},{1,13},{6,2},{10,6},{... | collective-permute-start | bytes 24584 | tf_op jit(solution)/shard_map/ppermute | solution.py:16
  174.3 10.4 %all-to-all-start.5 = ((bf16[4,16,512]{2,1,0:T(8,128)(2,1)}), bf16[4,16,512]{2,1,0:T(8,128)(2,1)S(1)}, u32[]{:S(2)}, u32[]{:S(2)}) async-start(bf16[4,16,512]{2,1,0:T(8,128)(2,1)} %bitcast.32), calls=%async_computation.5 | async-start | bytes 131072 | tf_op jit(solution)/shard_map/all_to_all | solution.py:37
  177.5 22.0 %reduce-scatter.10.cloned.1.call-start = ((), (), s32[]{:S(2)}) async-start(), calls=%async_computation.15 | async-start | bytes 1572864 | tf_op jit(solution)/shard_map/reduce_scatter | solution.py:76
  190.3 21.8 %reduce-scatter.22.cloned.1.call-start = ((), (), s32[]{:S(2)}) async-start(), calls=%async_computation.21 | async-start | bytes 2359296 | tf_op jit(solution)/shard_map/reduce_scatter | solution.py:76
  192.9 31.8 %reduce-scatter.16.cloned.1.call-start = ((), (), s32[]{:S(2)}) async-start(), calls=%async_computation.18 | async-start | bytes 2359296 | tf_op jit(solution)/shard_map/reduce_scatter | solution.py:76
  195.4 47.2 %reduce-scatter.12.cloned.1.call-start = ((), (), s32[]{:S(2)}) async-start(), calls=%async_computation.16 | async-start | bytes 786432 | tf_op jit(solution)/shard_map/reduce_scatter | solution.py:76
  199.6 62.6 %reduce-scatter.24.cloned.1.call-start = ((), (), s32[]{:S(2)}) async-start(), calls=%async_computation.22 | async-start | bytes 1179648 | tf_op jit(solution)/shard_map/reduce_scatter | solution.py:76
  212.2 69.7 %reduce-scatter.18.cloned.1.call-start = ((), (), s32[]{:S(2)}) async-start(), calls=%async_computation.19 | async-start | bytes 1179648 | tf_op jit(solution)/shard_map/reduce_scatter | solution.py:76
  224.7 79.0 %reduce-scatter.14.cloned.1.call-start = ((), (), s32[]{:S(2)}) async-start(), calls=%async_computation.17 | async-start | bytes 327680 | tf_op jit(solution)/shard_map/reduce_scatter | solution.py:76
  242.7 82.4 %reduce-scatter.26.cloned.1.call-start = ((), (), s32[]{:S(2)}) async-start(), calls=%async_computation.23 | async-start | bytes 491520 | tf_op jit(solution)/shard_map/reduce_scatter | solution.py:76
  262.3 84.0 %reduce-scatter.20.cloned.1.call-start = ((), (), s32[]{:S(2)}) async-start(), calls=%async_computation.20 | async-start | bytes 491520 | tf_op jit(solution)/shard_map/reduce_scatter | solution.py:76
  (34 other events, 474.4 us)
Sparse Core Ops, SparseCore 0:
  190.4 9.1 reduce-scatter.9
  201.9 10.1 reduce-scatter.21
  214.4 10.2 reduce-scatter.15
  226.9 15.7 reduce-scatter.11
  244.7 17.4 reduce-scatter.23
  264.4 17.4 reduce-scatter.17
  284.1 19.5 reduce-scatter.13
  306.1 18.8 reduce-scatter.25
  327.4 18.8 reduce-scatter.19

commit v2 on v0

v2 whole, which is shorter than its diff:
```python
import itertools

import jax
import jax.numpy as jnp
from jax import lax
from jax.experimental import pallas as pl
from jax.experimental.pallas import tpu as pltpu
from jax.sharding import PartitionSpec as P

BF = jnp.bfloat16
F32 = jnp.float32
NN = (((1,), (0,)), ((), ()))
NT = (((1,), (1,)), ((), ()))
TN = (((0,), (0,)), ((), ()))
BORDER = 8
GROUP = ("lon", "lat", "sub")
COLUMN = ("lat", "sub")


def dot(a, b, dims=NN):
    return lax.dot_general(a, b, dims, preferred_element_type=F32)


def low(value):
    return value.astype(BF)


def sigmoid(value):
    return 0.5 * jnp.tanh(0.5 * value) + 0.5


def silu(value):
    return value * sigmoid(value)


def silu_both(value):
    sig = sigmoid(value)
    act = value * sig
    return act, sig + act * (1.0 - sig)


def silu_slope(value):
    return silu_both(value)[1]


def iota(rows, columns, dim):
    return lax.broadcasted_iota(jnp.int32, (rows, columns), dim)


def hot(mask):
    return jnp.where(mask, 1.0, 0.0)


def pieces(value, slots, starts, sizes):
    step = value.shape[0] // slots
    found = []
    for start, size in zip(starts, sizes):
        found.append(
            jnp.concatenate(
                [value[s * step + start : s * step + start + size] for s in range(slots)], axis=0
            )
        )
    return found


def braid(parts, slots):
    rows = []
    for s in range(slots):
        for part in parts:
            size = part.shape[0] // slots
            rows.append(part[s * size : (s + 1) * size])
    return jnp.concatenate(rows, axis=0)


def receivers(senders_t, nodes, halo):
    found = jnp.zeros((halo, nodes), F32)
    ids = iota(halo, nodes, 0) + nodes
    for j in range(senders_t.shape[0]):
        found = found + hot(senders_t[j : j + 1, :] == ids)
    return found


def receivers_t(senders, halo):
    nodes, degree = senders.shape
    found = jnp.zeros((nodes, halo), F32)
    ids = iota(nodes, halo, 1) + nodes
    for j in range(degree):
        found = found + hot(senders[:, j : j + 1] == ids)
    return found


def store_blocks(ref, at, value, dims, order):
    value = low(value)
    rows = value.shape[0]
    depth = rows // (dims[0] * dims[1] * dims[2])
    if depth % 16:
        ref[at] = value
        return
    for place in itertools.product(*(range(size) for size in dims)):
        block = (place[0] * dims[1] + place[1]) * dims[2] + place[2]
        spot = 0
        for axis in order:
            spot = spot * dims[axis] + place[axis]
        ref[spot, at * depth : (at + 1) * depth, :] = value[block * depth : (block + 1) * depth]


def blocks_shape(count, rows, width, dims):
    total = dims[0] * dims[1] * dims[2]
    depth = rows // total
    if depth % 16:
        return jax.ShapeDtypeStruct((count, rows, width), BF)
    return jax.ShapeDtypeStruct((total, count * depth, width), BF)


def arrange(blocks, rows, dims, order):
    total = dims[0] * dims[1] * dims[2]
    depth = rows // total
    if depth % 16:
        count, _, width = blocks.shape
        blocks = blocks.reshape((count,) + dims + (depth, width))
        blocks = blocks.transpose(tuple(axis + 1 for axis in order) + (0, 4, 5))
        blocks = blocks.reshape(total, count * depth, width)
    return blocks


def scatter_sum(blocks, stages):
    for at, axes in enumerate(stages):
        size = lax.axis_size(axes)
        blocks = blocks.reshape((size, blocks.shape[0] // size) + blocks.shape[1:])
        moved = lax.all_to_all(blocks, axes, split_axis=0, concat_axis=0, tiled=True)
        total = moved[0].astype(F32)
        for i in range(1, size):
            total = total + moved[i].astype(F32)
        blocks = total if at == len(stages) - 1 else low(total)
    return blocks[0]


def call(kernel, name, outs, args, flops):
    size = sum(a.size * a.dtype.itemsize for a in (*args, *outs))
    return pl.pallas_call(
        kernel,
        out_shape=list(outs),
        in_specs=[pl.BlockSpec(memory_space=pltpu.VMEM)] * len(args),
        out_specs=[pl.BlockSpec(memory_space=pltpu.VMEM)] * len(outs),
        compiler_params=pltpu.CompilerParams(vmem_limit_bytes=48 * 1024 * 1024),
        cost_estimate=pl.CostEstimate(flops=flops, bytes_accessed=size, transcendentals=0),
        name=name,
    )(*args)


def exchange(payload):
    column = lax.axis_size(COLUMN)
    count = lax.axis_size("lon")
    forward = [(i, (i + 1) % count) for i in range(count)]
    backward = [(target, source) for source, target in forward]
    from_right = lax.ppermute(payload[column], "lon", backward)
    from_left = lax.ppermute(payload[column + 1], "lon", forward)
    arrived = lax.all_to_all(payload[:column], COLUMN, split_axis=0, concat_axis=0, tiled=True)
    return jnp.concatenate([arrived, from_left[None], from_right[None]], axis=0)


def shape(*dims, dtype=BF):
    return jax.ShapeDtypeStruct(dims, dtype)


def first_payload(sends_ref, senders_t_ref, grid_ref, cot_ref, out_ref):
    taken = sends_ref.shape[0]
    chosen, nodes = grid_ref.shape[0], cot_ref.shape[0]
    slots = taken // 16
    rows = dot(low(hot(sends_ref[...] == iota(taken, chosen, 1))), grid_ref[...])
    back = low(receivers(senders_t_ref[...], nodes, slots * BORDER))
    out_ref[...] = low(braid([rows, dot(back, cot_ref[...])], slots))


def embed_local(grid_ref, weight_ref, target_ref, sends_ref, sum_ref, slope_ref):
    chosen = grid_ref.shape[0]
    nodes = sum_ref.shape[0]
    taken = sends_ref.shape[0]
    pre = dot(grid_ref[...], weight_ref[...])
    act, slope = silu_both(pre)
    slope_ref[...] = low(slope)
    sent = jnp.max(hot(sends_ref[...] == iota(taken, chosen, 1)), axis=0, keepdims=True)
    label = jnp.where(sent > 0.0, nodes, target_ref[...])
    sum_ref[...] = dot(low(hot(label == iota(nodes, chosen, 0))), low(act))


def merge_nodes(
    slots, arr_ref, incoming_ref, embed_ref, local_ref, mesh_ref, weight_ref, bounds_ref,
    senders_t_ref, merged_ref, state_ref, pay_ref, slope_ref, lat_ref,
):
    nodes = mesh_ref.shape[0]
    taken = incoming_ref.shape[1]
    halo = slots * BORDER
    (lat,) = pieces(arr_ref[...].astype(F32), slots, (0,), (16,))
    lat = low(lat)
    lat_ref[...] = lat
    act, slope = silu_both(dot(lat, embed_ref[...]))
    slope_ref[...] = low(slope)
    place = low(hot(incoming_ref[...] == iota(nodes, taken, 0)))
    merged = low(local_ref[...] + dot(place, low(act)))
    merged_ref[...] = merged
    state = low(mesh_ref[...].astype(F32) + dot(merged, weight_ref[...]))
    state_ref[...] = state
    border = hot(bounds_ref[...] == iota(halo, nodes, 1))
    back = receivers(senders_t_ref[...], nodes, halo)
    pick = low(braid([border, back], slots))
    rows = pieces(dot(pick, state), slots, (0, BORDER), (BORDER, BORDER))
    pay_ref[...] = low(braid([*rows, dot(low(border), merged)], slots))


def local_edges(senders, sent, recv, each):
    nodes, degree = senders.shape
    total = jnp.zeros(recv.shape, F32)
    ids = iota(nodes, nodes, 1)
    for j in range(degree):
        named = senders[:, j : j + 1]
        act, slope = silu_both(dot(low(hot(named == ids)), sent) + recv)
        keep = hot(named < nodes)
        total = total + act * keep
        each(j, slope * keep)
    return total


def forward_local(
    state_ref, send_ref, recv_ref, senders_ref, senders_t_ref, bounds_ref,
    total_ref, slope_ref, recv_n_ref, sent_b_ref,
):
    state = state_ref[...]
    nodes = state.shape[0]
    halo = bounds_ref.shape[0]
    sent = low(dot(state, send_ref[...]))
    recv = dot(state, recv_ref[...])

    def keep(j, slope):
        slope_ref[j] = low(slope)

    total_ref[...] = local_edges(senders_ref[...], sent, recv, keep)
    back = low(receivers(senders_t_ref[...], nodes, halo))
    recv_n_ref[...] = dot(low(dot(back, state)), recv_ref[...])
    sent_b_ref[...] = low(dot(low(hot(bounds_ref[...] == iota(halo, nodes, 1))), sent))


def forward_halo(
    slots, arr_ref, recv_n_ref, total_ref, state_ref, send_ref, update_ref, senders_ref,
    senders_t_ref, bounds_ref, summed_ref, out_ref, pay_ref,
):
    nodes = state_ref.shape[0]
    halo = slots * BORDER
    (rows,) = pieces(arr_ref[...].astype(F32), slots, (0,), (BORDER,))
    pre = low(dot(low(rows), send_ref[...])).astype(F32) + recv_n_ref[...]
    place = low(receivers_t(senders_ref[...], halo))
    summed = low(total_ref[...] + dot(place, low(silu(pre))))
    summed_ref[...] = summed
    state = low(state_ref[...].astype(F32) + dot(summed, update_ref[...]))
    out_ref[...] = state
    border = hot(bounds_ref[...] == iota(halo, nodes, 1))
    back = receivers(senders_t_ref[...], nodes, halo)
    pay_ref[...] = low(dot(low(braid([border, back], slots)), state))


def turn_local(
    slots, state_ref, send_ref, recv_ref, update_ref, cot_ref, arr1_ref, arr2_ref, recv_n0_ref,
    sent_b0_ref, send0_ref, recv0_ref, senders_ref, senders_t_ref, bounds_ref,
    total_ref, grecv_ref, gsent_ref, recv_n_ref, sent_b_ref, gsum_n_ref, gsum_r_ref,
    slope_k_ref, slope_r_ref, rows_ref, merged_ref,
):
    halo = slots * BORDER
    rows0, back0, merged0 = pieces(
        arr2_ref[...].astype(F32), slots, (0, BORDER, 2 * BORDER), (BORDER,) * 3
    )
    rows_ref[...] = low(rows0)
    merged_ref[...] = low(merged0)
    pre = low(dot(low(rows0), send0_ref[...])).astype(F32) + recv_n0_ref[...]
    slope_k_ref[...] = low(silu_slope(pre))
    pre = sent_b0_ref[...].astype(F32) + dot(low(back0), recv0_ref[...])
    slope_r_ref[...] = low(silu_slope(pre))
    state = state_ref[...]
    nodes = state.shape[0]
    sent = low(dot(state, send_ref[...]))
    recv = dot(state, recv_ref[...])
    gsum = low(dot(cot_ref[...], update_ref[...], NT))
    grad = gsum.astype(F32)
    grecv_ref[...] = jnp.zeros(grecv_ref.shape, F32)
    gsent_ref[...] = jnp.zeros(gsent_ref.shape, F32)

    def back_edge(j, slope):
        gpre = grad * slope
        grecv_ref[...] += gpre
        place = low(hot(senders_t_ref[j : j + 1, :] == iota(nodes, nodes, 0)))
        gsent_ref[...] += dot(place, low(gpre))

    total_ref[...] = local_edges(senders_ref[...], sent, recv, back_edge)
    back = low(receivers(senders_t_ref[...], nodes, halo))
    recv_n_ref[...] = dot(low(dot(back, state)), recv_ref[...])
    sent_b_ref[...] = low(dot(low(hot(bounds_ref[...] == iota(halo, nodes, 1))), sent))
    gsum_n_ref[...] = low(dot(back, gsum))
    (cot_r,) = pieces(arr1_ref[...].astype(F32), slots, (16,), (BORDER,))
    gsum_r_ref[...] = low(dot(low(cot_r), update_ref[...], NT))


def turn_halo(
    slots, arr_ref, recv_n_ref, sent_b_ref, gsum_n_ref, gsum_r_ref, total_ref, grecv_ref,
    gsent_ref, cot_ref, send_ref, recv_ref, senders_ref, senders_t_ref, bounds_ref,
    summed_ref, grecv_out_ref, gsent_out_ref, gin_ref, pay_ref,
):
    nodes = cot_ref.shape[0]
    halo = slots * BORDER
    rows, back = pieces(arr_ref[...].astype(F32), slots, (0, BORDER), (BORDER,) * 2)
    pre = low(dot(low(rows), send_ref[...])).astype(F32) + recv_n_ref[...]
    act, slope = silu_both(pre)
    place = low(receivers_t(senders_ref[...], halo))
    gpre = low(gsum_n_ref[...].astype(F32) * slope)
    grecv = low(grecv_ref[...] + dot(place, gpre))
    pre = sent_b_ref[...].astype(F32) + dot(low(back), recv_ref[...])
    gpre = low(gsum_r_ref[...].astype(F32) * silu_slope(pre))
    border = low(hot(bounds_ref[...] == iota(nodes, halo, 0)))
    gsent = low(gsent_ref[...] + dot(border, gpre))
    gin = cot_ref[...].astype(F32) + dot(grecv, recv_ref[...], NT) + dot(gsent, send_ref[...], NT)
    gin = low(gin)
    gin_ref[...] = gin
    pay_ref[...] = low(dot(low(receivers(senders_t_ref[...], nodes, halo)), gin))
    summed_ref[...] = low(total_ref[...] + dot(place, low(act)))
    grecv_out_ref[...] = grecv
    gsent_out_ref[...] = gsent


def last_weights(
    dims, order, state_ref, summed_ref, cot_ref, grecv_ref, gsent_ref, update_ref, out_ref, mesh_ref
):
    state, summed = state_ref[...], summed_ref[...]
    store_blocks(out_ref, 0, dot(state, gsent_ref[...], TN), dims, order)
    store_blocks(out_ref, 1, dot(state, grecv_ref[...], TN), dims, order)
    store_blocks(out_ref, 2, dot(summed, cot_ref[...], TN), dims, order)
    mesh_ref[...] = low(state.astype(F32) + dot(summed, update_ref[...]))


def back_local(
    dims, order, gin_ref, slope_ref, slope_k_ref, send_ref, recv_ref, update_ref, senders_ref,
    senders_t_ref, state_ref, rows_ref, summed_ref, merged_ref, merged_r_ref,
    part_ref, out_ref,
):
    nodes = gin_ref.shape[0]
    halo = slope_k_ref.shape[0]
    gin = gin_ref[...]
    gsum = low(dot(gin, update_ref[...], NT))
    grad = gsum.astype(F32)
    place = low(receivers_t(senders_ref[...], halo))
    back = low(receivers(senders_t_ref[...], nodes, halo))
    gpre_k = low(dot(back, gsum) * slope_k_ref[...].astype(F32))
    grecv = dot(place, gpre_k)
    gsent = jnp.zeros(grad.shape, F32)
    for j in range(senders_t_ref.shape[0]):
        gpre = grad * slope_ref[j].astype(F32)
        grecv = grecv + gpre
        spread = low(hot(senders_t_ref[j : j + 1, :] == iota(nodes, nodes, 0)))
        gsent = gsent + dot(spread, low(gpre))
    grecv, gsent = low(grecv), low(gsent)
    part = gin.astype(F32) + dot(grecv, recv_ref[...], NT) + dot(gsent, send_ref[...], NT)
    part_ref[...] = part
    state, merged = state_ref[...], merged_ref[...]
    grad_send = dot(state, gsent, TN) + dot(rows_ref[...], gpre_k, TN)
    store_blocks(out_ref, 0, grad_send, dims, order)
    store_blocks(out_ref, 1, dot(state, grecv, TN), dims, order)
    store_blocks(out_ref, 2, dot(summed_ref[...], gin, TN), dims, order)
    far = low(dot(gpre_k, send_ref[...], NT))
    grad_merge = dot(merged, low(part), TN) + dot(merged_r_ref[...], far, TN)
    store_blocks(out_ref, 3, grad_merge, dims, order)


def embed_back(
    dims, order, arr_ref, slope_r_ref, part_ref, update_ref, send_ref, merge_ref, bounds_ref,
    target_ref, sends_ref, incoming_ref, slope_g_ref, slope_a_ref, grid_ref, lat_ref,
    out_ref, gpre_ref, gpre_a_ref,
):
    nodes = part_ref.shape[0]
    halo = arr_ref.shape[0]
    chosen = grid_ref.shape[0]
    taken = sends_ref.shape[0]
    gsum = low(dot(arr_ref[...], update_ref[...], NT)).astype(F32)
    gpre = low(gsum * slope_r_ref[...].astype(F32))
    border = low(hot(bounds_ref[...] == iota(nodes, halo, 0)))
    gin = low(part_ref[...] + dot(low(dot(border, gpre)), send_ref[...], NT))
    gmerged = low(dot(gin, merge_ref[...], NT))
    sent = jnp.max(hot(sends_ref[...] == iota(taken, chosen, 1)), axis=0, keepdims=True)
    label = jnp.where(sent > 0.0, nodes, target_ref[...])
    pick = low(hot(label == iota(nodes, chosen, 0)))
    gpre_g = low(dot(pick, gmerged, TN) * slope_g_ref[...].astype(F32))
    place = low(hot(incoming_ref[...] == iota(nodes, taken, 0)))
    gpre_a = low(dot(place, gmerged, TN) * slope_a_ref[...].astype(F32))
    grad = dot(grid_ref[...], gpre_g, TN) + dot(lat_ref[...], gpre_a, TN)
    store_blocks(out_ref, 0, grad, dims, order)
    gpre_ref[...] = gpre_g
    gpre_a_ref[...] = gpre_a


def grid_rows(gpre_ref, weight_ref, out_ref):
    out_ref[...] = low(dot(gpre_ref[...], weight_ref[...], NT))


def grid_place(gpre_ref, weight_ref, sends_ref, arr_ref, out_ref):
    chosen = gpre_ref.shape[0]
    taken = sends_ref.shape[1]
    local = dot(gpre_ref[...], weight_ref[...], NT)
    place = low(hot(sends_ref[...] == iota(chosen, taken, 0)))
    out_ref[...] = low(local + dot(place, arr_ref[...]))


def body(
    dims, stages, order,
    grid_latent, mesh_latent, cotangent, embed_weight, merge_weight, send_weight, recv_weight,
    update_weight, target_row, send_rows, incoming_rows, border_mesh_rows, mesh_senders,
):
    chosen, width = grid_latent.shape
    nodes, degree = mesh_senders.shape
    slots, capacity = send_rows.shape[1:]
    halo = slots * BORDER
    taken = slots * capacity
    sends_col = send_rows.reshape(taken, 1)
    sends_row = send_rows.reshape(1, taken)
    incoming = incoming_rows.reshape(1, taken)
    bounds_col = border_mesh_rows.reshape(halo, 1)
    bounds_row = border_mesh_rows.reshape(1, halo)
    targets = target_row.reshape(1, chosen)
    senders_t = mesh_senders.T
    unit = 2 * nodes * width * width

    send0, send1 = send_weight[0], send_weight[1]
    recv0, recv1 = recv_weight[0], recv_weight[1]
    update0, update1 = update_weight[0], update_weight[1]

    (pay1,) = call(
        first_payload, "first_payload", [shape(slots * 24, width)],
        (sends_col, senders_t, grid_latent, cotangent), flops=unit // 2,
    )
    arr1 = exchange(pay1.reshape(slots, 24, width)).reshape(slots * 24, width)
    local, slope_g = call(
        embed_local, "embed_local", [shape(nodes, width, dtype=F32), shape(chosen, width)],
        (grid_latent, embed_weight, targets, sends_col), flops=3 * unit,
    )
    merged, state0, pay2, slope_a, lat_a = call(
        lambda *refs: merge_nodes(slots, *refs), "merge_nodes",
        [shape(nodes, width), shape(nodes, width), shape(slots * 24, width),
         shape(taken, width), shape(taken, width)],
        (arr1, incoming, embed_weight, local, mesh_latent, merge_weight, bounds_col, senders_t),
        flops=2 * unit,
    )
    arr2 = exchange(pay2.reshape(slots, 24, width)).reshape(slots * 24, width)
    total0, slope0, recv_n0, sent_b0 = call(
        forward_local, "forward_local",
        [shape(nodes, width, dtype=F32), shape(degree, nodes, width),
         shape(halo, width, dtype=F32), shape(halo, width)],
        (state0, send0, recv0, mesh_senders, senders_t, bounds_col),
        flops=6 * unit,
    )
    summed0, state1, pay3 = call(
        lambda *refs: forward_halo(slots, *refs), "forward_halo",
        [shape(nodes, width), shape(nodes, width), shape(slots * 16, width)],
        (arr2, recv_n0, total0, state0, send0, update0, mesh_senders, senders_t,
         bounds_col),
        flops=2 * unit,
    )
    arr3 = exchange(pay3.reshape(slots, 16, width)).reshape(slots * 16, width)
    (total1, grecv_l, gsent_l, recv_n1, sent_b1, gsum_n1, gsum_r1, slope_k0, slope_r0, rows0,
     merged_r) = call(
        lambda *refs: turn_local(slots, *refs), "turn_local",
        [shape(nodes, width, dtype=F32), shape(nodes, width, dtype=F32),
         shape(nodes, width, dtype=F32), shape(halo, width, dtype=F32), shape(halo, width),
         shape(halo, width), shape(halo, width), shape(halo, width), shape(halo, width),
         shape(halo, width), shape(halo, width)],
        (state1, send1, recv1, update1, cotangent, arr1, arr2, recv_n0, sent_b0,
         send0, recv0, mesh_senders, senders_t, bounds_col),
        flops=10 * unit,
    )
    summed1, grecv1, gsent1, gin1, pay4 = call(
        lambda *refs: turn_halo(slots, *refs), "turn_halo",
        [shape(nodes, width)] * 4 + [shape(halo, width)],
        (arr3, recv_n1, sent_b1, gsum_n1, gsum_r1, total1, grecv_l, gsent_l, cotangent,
         send1, recv1, mesh_senders, senders_t, bounds_row),
        flops=3 * unit,
    )
    arr4 = exchange(pay4.reshape(slots, BORDER, width)).reshape(halo, width)
    blocks1, mesh_out = call(
        lambda *refs: last_weights(dims, order, *refs), "last_weights",
        [blocks_shape(3, width, width, dims), shape(nodes, width)],
        (state1, summed1, cotangent, grecv1, gsent1, update1),
        flops=4 * unit,
    )
    part0, blocks0 = call(
        lambda *refs: back_local(dims, order, *refs), "back_local",
        [shape(nodes, width, dtype=F32), blocks_shape(4, width, width, dims)],
        (gin1, slope0, slope_k0, send0, recv0, update0, mesh_senders, senders_t,
         state0, rows0, summed0, merged, merged_r),
        flops=10 * unit,
    )
    blocks_e, gpre_g, gpre_a = call(
        lambda *refs: embed_back(dims, order, *refs), "embed_back",
        [blocks_shape(1, width, width, dims), shape(chosen, width), shape(taken, width)],
        (arr4, slope_r0, part0, update0, send0, merge_weight, bounds_row, targets,
         sends_col, incoming, slope_g, slope_a, grid_latent, lat_a),
        flops=6 * unit,
    )
    (back_rows,) = call(
        grid_rows, "grid_rows", [shape(taken, width)], (gpre_a, embed_weight), flops=unit // 2
    )
    arr5 = exchange(back_rows.reshape(slots, capacity, width)).reshape(taken, width)
    (grid_grad,) = call(
        grid_place, "grid_place", [shape(chosen, width)],
        (gpre_g, embed_weight, sends_row, arr5), flops=3 * unit,
    )
    sum1 = scatter_sum(arrange(blocks1, width, dims, order), stages)
    sum0 = scatter_sum(arrange(blocks0, width, dims, order), stages)
    embed_grad = scatter_sum(arrange(blocks_e, width, dims, order), stages)
    depth = embed_grad.shape[0]
    send_grad, recv_grad, update_grad = (
        jnp.stack([sum0[i * depth : (i + 1) * depth], sum1[i * depth : (i + 1) * depth]])
        for i in range(3)
    )
    merge_grad = sum0[3 * depth :]
    return (mesh_out, grid_grad, embed_grad, merge_grad, send_grad, recv_grad, update_grad)


def solution(mesh):
    split = ("groups", "lon", "lat", "sub")
    dims = tuple(mesh.shape[axis] for axis in GROUP)
    stages = (COLUMN, ("lon",))
    order = tuple(GROUP.index(axis) for axes in stages for axis in axes)
    rows = P(split, None)
    whole = P("groups", GROUP, None)
    in_specs = (
        rows, rows, rows, P(), P(), P(), P(), P(), P(split), P(split, None, None),
        P(split, None, None), P(split, None, None), rows,
    )
    out_specs = (rows, rows, rows, rows, whole, whole, whole)
    return jax.shard_map(
        lambda *args: body(dims, stages, order, *args),
        mesh=mesh, in_specs=in_specs, out_specs=out_specs, check_vma=False,
    )
```

time: 601 us -> 241 us (0.40)
  waiting for transfers between devices: 392 us -> 50.3 us
  other arithmetic: 58.3 us -> 11.4 us
  matrix products: 33.5 us -> 0 us
  blocking collectives: 0 us -> 23.3 us
  local copies, waits for them, and re-layouts: 56.1 us -> 75.7 us
  Pallas kernels: 0 us -> 19 us
  between operations: 15 us -> 1.24 us
  starting transfers between devices: 44.9 us -> 57.2 us
    reduce_scatter x7 -> x0, waiting for transfers between devices: 317 us -> none  [the longest x2 119 us: body(): lax.psum_scatter(partials[1], ('lon', 'lat', 'sub'), scatter_dimension=0,...]
    unnamed x62 -> x197, local copies, waits for them, and re-layouts: 4.32 us -> 66.4 us
    unnamed x9 -> x0, waiting for transfers between devices: 61.2 us -> none
    all_to_all x6 -> x10, waiting for transfers between devices: 13 us -> 50.3 us  [the longest x5 46.9 us: scatter_sum(): lax.all_to_all(blocks, axes, split_axis=0, concat_axis=0, tiled=True)]
    scatter-add x5 -> x0, other arithmetic: 33.6 us -> none  [the longest x2 23.8 us: layer_backward(): jax.ops.segment_sum(edge_grad.reshape(-1, width), senders.reshape(-1), no...]
    dot_general x24 -> x0, matrix products: 33.5 us -> none  [the longest x2 4.53 us: layer_backward(): jnp.dot(summed.T, grad_out, preferred_element_type=jnp.float32)]
    all_to_all x0 -> x1, blocking collectives: none -> 23.3 us  [scatter_sum(): lax.all_to_all(blocks, axes, split_axis=0, concat_axis=0, tiled=True)]
    pallas_call x0 -> x12, Pallas kernels: none -> 19 us  [call(): pl.pallas_call(kernel, out_shape=list(outs), in_specs=[pl.BlockSpec(memor...]
  transfers between devices with their start and end apart: 26 -> 20, of which waited for: 11 -> 6; matrix products, arithmetic and copies ran while one was open for 13% -> 5% of each run, Pallas kernels for 0% -> 6%
where the time goes in v2:
time: 241 us; the launch traced here: 238 us
  local copies, waits for them, and re-layouts  75.7 us (31%)
  starting transfers between devices  57.2 us (24%)
  waiting for transfers between devices  50.3 us (21%)
  blocking collectives  23.3 us (10%)
  Pallas kernels  19 us (8%)
  other arithmetic  11.4 us (5%)
    unnamed x197, local copies, waits for them, and re-layouts  66.4 us
    all_to_all x5, waiting for transfers between devices, scatter_sum(): lax.all_to_all(blocks, axes, split_axis=0, concat_axis=0, tiled=True)  46.9 us
    all_to_all x1, blocking collectives, scatter_sum(): lax.all_to_all(blocks, axes, split_axis=0, concat_axis=0, tiled=True)  23.3 us
    pallas_call x12, Pallas kernels, call(): pl.pallas_call(kernel, out_shape=list(outs), in_specs=[pl.BlockSpec(memor...  19 us
    all_to_all x5, starting transfers between devices, scatter_sum(): lax.all_to_all(blocks, axes, split_axis=0, concat_axis=0, tiled=True)  18.8 us
    all_to_all x5, starting transfers between devices, exchange(): lax.all_to_all(payload[:column], COLUMN, split_axis=0, concat_axis=0, til...  18.6 us
    ppermute x5, starting transfers between devices, exchange(): from_right = lax.ppermute(payload[column], 'lon', backward)  15.4 us
    add x6, other arithmetic, scatter_sum(): total = total + moved[i].astype(F32)  6.71 us
  transfers between devices with their start and end apart: 20, of which 6 were waited for; matrix products, arithmetic and copies ran while one was open for 5% of the time, Pallas kernels for 6%

profile of v2, /device:TPU:0, one launch (start us, length us, event | category | flops | bytes accessed | tf_op | source)
XLA Modules:
  0.0 238.0 jit_solution(12432312553899094314)
XLA Ops:
  5.6 4.2 %all-to-all-start = ((bf16[4,24,512]{2,1,0:T(8,128)(2,1)}), bf16[4,24,512]{2,1,0:T(8,128)(2,1)S(1)}, u32[]{:S(2)}, u32[]{:S(2)}) async-start(bf16[4,24,512]{2,1,0:T(8,128)(2,1)} %bitcast.1), calls=%async_computation | async-start | bytes 196608 | tf_op jit(solution)/shard_map/all_to_all | solution.py:158
  9.8 2.2 collective-permute-start
  14.1 2.3 slice_bitcast_fusion.1
  28.5 3.9 %all-to-all-start.1 = ((bf16[4,24,512]{2,1,0:T(8,128)(2,1)}), bf16[4,24,512]{2,1,0:T(8,128)(2,1)}, u32[]{:S(2)}, u32[]{:S(2)}) async-start(bf16[4,24,512]{2,1,0:T(8,128)(2,1)} %bitcast.71), calls=%async_computation.1 | async-start | bytes 196608 | tf_op jit(solution)/shard_map/all_to_all | solution.py:158
  32.5 3.8 %collective-permute-start.3 = (bf16[24,512]{1,0:T(8,128)(2,1)}, bf16[24,512]{1,0:T(8,128)(2,1)}, u32[]{:S(2)}, u32[]{:S(2)}) collective-permute-start(bf16[24,512]{1,0:T(8,128)(2,1)} %get-tuple-element.95), channel_id=1, source_target_pairs={{4,0},{8,4},{12,8},{0,12},{5,1},{9,5},{13,9},{1,13},{6,2},{10,6},{... | collective-permute-start | bytes 73736 | tf_op jit(solution)/shard_map/ppermute | solution.py:156
  52.3 3.9 %all-to-all-start.2 = ((bf16[4,16,512]{2,1,0:T(8,128)(2,1)}), bf16[4,16,512]{2,1,0:T(8,128)(2,1)}, u32[]{:S(2)}, u32[]{:S(2)}) async-start(bf16[4,16,512]{2,1,0:T(8,128)(2,1)} %bitcast.72), calls=%async_computation.2 | async-start | bytes 131072 | tf_op jit(solution)/shard_map/all_to_all | solution.py:158
  56.3 3.8 %collective-permute-start.5 = (bf16[16,512]{1,0:T(8,128)(2,1)}, bf16[16,512]{1,0:T(8,128)(2,1)}, u32[]{:S(2)}, u32[]{:S(2)}) collective-permute-start(bf16[16,512]{1,0:T(8,128)(2,1)} %get-tuple-element.101), channel_id=1, source_target_pairs={{4,0},{8,4},{12,8},{0,12},{5,1},{9,5},{13,9},{1,13},{6,2},{10,6},{... | collective-permute-start | bytes 49160 | tf_op jit(solution)/shard_map/ppermute | solution.py:156
  68.4 3.9 %turn_local.1 = (f32[256,512]{1,0:T(8,128)S(1)}, f32[256,512]{1,0:T(8,128)S(1)}, f32[256,512]{1,0:T(8,128)S(1)}, f32[48,512]{1,0:T(8,128)S(1)}, bf16[48,512]{1,0...) custom-call(bf16[256,512]{1,0:T(8,128)(2,1)S(1)} %copy-done.66, ...), custom_call_target="tpu_custom_call" | custom-call | flops 1342177280 | bytes 5615808 | tf_op jit(solution)/shard_map/turn_local/pallas_call | solution.py:140
  92.9 3.3 %all-to-all-start.3 = ((bf16[4,8,512]{2,1,0:T(8,128)(2,1)}), bf16[4,8,512]{2,1,0:T(8,128)(2,1)S(1)}, u32[]{:S(2)}, u32[]{:S(2)}) async-start(bf16[4,8,512]{2,1,0:T(8,128)(2,1)} %slice_bitcast_fusion.7), calls=%async_computation.3 | async-start | bytes 65536 | tf_op jit(solution)/shard_map/all_to_all | solution.py:158
  96.2 3.8 %collective-permute-start.7 = (bf16[8,512]{1,0:T(8,128)(2,1)S(1)}, bf16[8,512]{1,0:T(8,128)(2,1)S(1)}, u32[]{:S(2)}, u32[]{:S(2)}) collective-permute-start(bf16[8,512]{1,0:T(8,128)(2,1)S(1)} %get-tuple-element.103), channel_id=1, source_target_pairs={{4,0},{8,4},{12,8},{0,12},{5,1},{9,5},{13,9},{1,13},{6,2},{10,6},{... | collective-permute-start | bytes 24584 | tf_op jit(solution)/shard_map/ppermute | solution.py:156
  108.7 3.9 %back_local.1 = (f32[256,512]{1,0:T(8,128)S(1)}, bf16[16,128,512]{2,1,0:T(8,128)(2,1)}) custom-call(bf16[256,512]{1,0:T(8,128)(2,1)S(1)} %copy-done.79, bf16[6,256,512]{2,1,0:T(8,128)(2,1)S(1)} %copy-done.81, bf16[48,512]{1,0:T(8,128)(2,1)S(1)} %copy-done.83, bf16[512,512]{1,0:T(8,128)(2,1)S(1)} %get-tuple-element.104.send_ref.refs_4_.refs_9_.refs_3_, ...), custom_call_target="tpu_custom_call" | custom-call | flops 1342177280 | bytes 6975488 | tf_op jit(solution)/shard_map/back_local/pallas_call | solution.py:140
  120.5 3.6 %all-to-all-start.5 = ((bf16[4,4,32,512]{3,2,1,0:T(8,128)(2,1)}), bf16[4,4,32,512]{3,2,1,0:T(8,128)(2,1)S(1)}, u32[]{:S(2)}, u32[]{:S(2)}) async-start(bf16[4,4,32,512]{3,2,1,0:T(8,128)(2,1)} %bitcast.58), calls=%async_computation.5 | async-start | bytes 1048576 | tf_op jit(solution)/shard_map/all_to_all | solution.py:130
  125.9 7.0 %all-to-all-done.5 = bf16[4,4,32,512]{3,2,1,0:T(8,128)(2,1)S(1)} async-done(((bf16[4,4,32,512]{3,2,1,0:T(8,128)(2,1)}), bf16[4,4,32,512]{3,2,1,0:T(8,128)(2,1)S(1)}, u32[]{:S(2)}, u32[]{:S(2)}) %all-to-all-start.5) | async-done | bytes 524320 | tf_op jit(solution)/shard_map/all_to_all | solution.py:130
  132.9 3.3 %all-to-all-start.4 = ((bf16[4,16,512]{2,1,0:T(8,128)(2,1)}), bf16[4,16,512]{2,1,0:T(8,128)(2,1)S(1)}, u32[]{:S(2)}, u32[]{:S(2)}) async-start(bf16[4,16,512]{2,1,0:T(8,128)(2,1)} %bitcast.24), calls=%async_computation.4 | async-start | bytes 131072 | tf_op jit(solution)/shard_map/all_to_all | solution.py:158
  136.9 3.4 %all-to-all-done.4 = bf16[4,16,512]{2,1,0:T(8,128)(2,1)S(1)} async-done(((bf16[4,16,512]{2,1,0:T(8,128)(2,1)}), bf16[4,16,512]{2,1,0:T(8,128)(2,1)S(1)}, u32[]{:S(2)}, u32[]{:S(2)}) %all-to-all-start.4) | async-done | bytes 65568 | tf_op jit(solution)/shard_map/all_to_all | solution.py:158
  140.3 3.9 %all-to-all-start.6 = ((bf16[4,1,32,512]{3,2,1,0:T(8,128)(2,1)}), bf16[4,1,32,512]{3,2,1,0:T(8,128)(2,1)}, u32[]{:S(2)}, u32[]{:S(2)}) async-start(bf16[4,1,32,512]{3,2,1,0:T(8,128)(2,1)} %fusion.2), calls=%async_computation.6 | async-start | bytes 262144 | tf_op jit(solution)/shard_map/all_to_all | solution.py:130
  150.4 23.3 %all_to_all.55 = bf16[4,4,96,512]{3,2,1,0:T(8,128)(2,1)} all-to-all(bf16[4,4,96,512]{3,2,1,0:T(8,128)(2,1)S(1)} %bitcast.53), channel_id=1, replica_groups=mesh['groups'=2,'lon'=4,'lat'=2,'sub'=2] {'lat','sub'}, dimensions={0} | all-to-all | bytes 3145728 | tf_op jit(solution)/shard_map/all_to_all | solution.py:130
  173.6 3.6 %all-to-all-start.7 = ((bf16[4,4,128,512]{3,2,1,0:T(8,128)(2,1)}), bf16[4,4,128,512]{3,2,1,0:T(8,128)(2,1)S(1)}, u32[]{:S(2)}, u32[]{:S(2)}) async-start(bf16[4,4,128,512]{3,2,1,0:T(8,128)(2,1)} %bitcast.70), calls=%async_computation.7 | async-start | bytes 4194304 | tf_op jit(solution)/shard_map/all_to_all | solution.py:130
  177.3 2.3 fusion.1
  179.6 23.3 %all-to-all-done.7 = bf16[4,4,128,512]{3,2,1,0:T(8,128)(2,1)S(1)} async-done(((bf16[4,4,128,512]{3,2,1,0:T(8,128)(2,1)}), bf16[4,4,128,512]{3,2,1,0:T(8,128)(2,1)S(1)}, u32[]{:S(2)}, u32[]{:S(2)}) %all-to-all-start.7) | async-done | bytes 2097184 | tf_op jit(solution)/shard_map/all_to_all | solution.py:130
  202.9 4.2 %all-to-all-start.10 = ((bf16[4,1,96,512]{3,2,1,0:T(8,128)(2,1)}), bf16[4,1,96,512]{3,2,1,0:T(8,128)(2,1)}, u32[]{:S(2)}, u32[]{:S(2)}) async-start(bf16[4,1,96,512]{3,2,1,0:T(8,128)(2,1)} %fusion.1), calls=%async_computation.10 | async-start | bytes 786432 | tf_op jit(solution)/shard_map/all_to_all | solution.py:130
  212.2 7.2 %all-to-all-done.10 = bf16[4,1,96,512]{3,2,1,0:T(8,128)(2,1)} async-done(((bf16[4,1,96,512]{3,2,1,0:T(8,128)(2,1)}), bf16[4,1,96,512]{3,2,1,0:T(8,128)(2,1)}, u32[]{:S(2)}, u32[]{:S(2)}) %all-to-all-start.10) | async-done | bytes 393248 | tf_op jit(solution)/shard_map/all_to_all | solution.py:130
  219.4 3.5 %all-to-all-start.8 = ((bf16[4,1,128,512]{3,2,1,0:T(8,128)(2,1)}), bf16[4,1,128,512]{3,2,1,0:T(8,128)(2,1)S(1)}, u32[]{:S(2)}, u32[]{:S(2)}) async-start(bf16[4,1,128,512]{3,2,1,0:T(8,128)(2,1)} %fusion), calls=%async_computation.8 | async-start | bytes 1048576 | tf_op jit(solution)/shard_map/all_to_all | solution.py:130
  226.8 8.5 %all-to-all-done.8 = bf16[4,1,128,512]{3,2,1,0:T(8,128)(2,1)S(1)} async-done(((bf16[4,1,128,512]{3,2,1,0:T(8,128)(2,1)}), bf16[4,1,128,512]{3,2,1,0:T(8,128)(2,1)S(1)}, u32[]{:S(2)}, u32[]{:S(2)}) %all-to-all-start.8) | async-done | bytes 524320 | tf_op jit(solution)/shard_map/all_to_all | solution.py:130
  (262 shorter events, 100.7 us)
Async XLA Ops:
  1.9 16.5 %copy-start.32 = (s32[96,1]{1,0:T(8,128)}, s32[96,1]{1,0:T(8,128)S(1)}, u32[]{:S(2)}) copy-start(s32[96,1]{1,0:T(8,128)S(1)} %reshape.456.sends_ref.refs_8_) | copy-start | bytes 1156
  5.6 15.3 %all-to-all-start = ((bf16[4,24,512]{2,1,0:T(8,128)(2,1)}), bf16[4,24,512]{2,1,0:T(8,128)(2,1)S(1)}, u32[]{:S(2)}, u32[]{:S(2)}) async-start(bf16[4,24,512]{2,1,0:T(8,128)(2,1)} %bitcast.1), calls=%async_computation | async-start | bytes 196608 | tf_op jit(solution)/shard_map/all_to_all | solution.py:158
  9.8 11.1 %collective-permute-start = (bf16[24,512]{1,0:T(8,128)(2,1)S(1)}, bf16[24,512]{1,0:T(8,128)(2,1)S(1)}, u32[]{:S(2)}, u32[]{:S(2)}) collective-permute-start(bf16[24,512]{1,0:T(8,128)(2,1)S(1)} %get-tuple-element.96), channel_id=1, source_target_pairs={{0,4},{4,8},{8,12},{12,0},{1,5},{5,9},{9,13},{13,1},{2,6},{6,10},{... | collective-permute-start | bytes 73736 | tf_op jit(solution)/shard_map/ppermute | solution.py:157
  12.0 8.9 %collective-permute-start.1 = (bf16[24,512]{1,0:T(8,128)(2,1)S(1)}, bf16[24,512]{1,0:T(8,128)(2,1)S(1)}, u32[]{:S(2)}, u32[]{:S(2)}) collective-permute-start(bf16[24,512]{1,0:T(8,128)(2,1)S(1)} %get-tuple-element.97), channel_id=1, source_target_pairs={{4,0},{8,4},{12,8},{0,12},{5,1},{9,5},{13,9},{1,13},{6,2},{10,6},{... | collective-permute-start | bytes 73736 | tf_op jit(solution)/shard_map/ppermute | solution.py:156
  28.5 15.0 %all-to-all-start.1 = ((bf16[4,24,512]{2,1,0:T(8,128)(2,1)}), bf16[4,24,512]{2,1,0:T(8,128)(2,1)}, u32[]{:S(2)}, u32[]{:S(2)}) async-start(bf16[4,24,512]{2,1,0:T(8,128)(2,1)} %bitcast.71), calls=%async_computation.1 | async-start | bytes 196608 | tf_op jit(solution)/shard_map/all_to_all | solution.py:158
  32.4 11.0 %collective-permute-start.2 = (bf16[24,512]{1,0:T(8,128)(2,1)}, bf16[24,512]{1,0:T(8,128)(2,1)}, u32[]{:S(2)}, u32[]{:S(2)}) collective-permute-start(bf16[24,512]{1,0:T(8,128)(2,1)} %get-tuple-element.94), channel_id=1, source_target_pairs={{0,4},{4,8},{8,12},{12,0},{1,5},{5,9},{9,13},{13,1},{2,6},{6,10},{... | collective-permute-start | bytes 73736 | tf_op jit(solution)/shard_map/ppermute | solution.py:157
  32.5 11.0 %collective-permute-start.3 = (bf16[24,512]{1,0:T(8,128)(2,1)}, bf16[24,512]{1,0:T(8,128)(2,1)}, u32[]{:S(2)}, u32[]{:S(2)}) collective-permute-start(bf16[24,512]{1,0:T(8,128)(2,1)} %get-tuple-element.95), channel_id=1, source_target_pairs={{4,0},{8,4},{12,8},{0,12},{5,1},{9,5},{13,9},{1,13},{6,2},{10,6},{... | collective-permute-start | bytes 73736 | tf_op jit(solution)/shard_map/ppermute | solution.py:156
  43.5 16.6 %copy-start.7 = (bf16[256,512]{1,0:T(8,128)(2,1)S(1)}, bf16[256,512]{1,0:T(8,128)(2,1)}, u32[]{:S(2)}) copy-start(bf16[256,512]{1,0:T(8,128)(2,1)} %refs_2_.3) | copy-start | bytes 786436
  52.3 27.4 %all-to-all-start.2 = ((bf16[4,16,512]{2,1,0:T(8,128)(2,1)}), bf16[4,16,512]{2,1,0:T(8,128)(2,1)}, u32[]{:S(2)}, u32[]{:S(2)}) async-start(bf16[4,16,512]{2,1,0:T(8,128)(2,1)} %bitcast.72), calls=%async_computation.2 | async-start | bytes 131072 | tf_op jit(solution)/shard_map/all_to_all | solution.py:158
  56.2 23.5 %collective-permute-start.4 = (bf16[16,512]{1,0:T(8,128)(2,1)}, bf16[16,512]{1,0:T(8,128)(2,1)}, u32[]{:S(2)}, u32[]{:S(2)}) collective-permute-start(bf16[16,512]{1,0:T(8,128)(2,1)} %get-tuple-element.100), channel_id=1, source_target_pairs={{0,4},{4,8},{8,12},{12,0},{1,5},{5,9},{9,13},{13,1},{2,6},{6,10},{... | collective-permute-start | bytes 49160 | tf_op jit(solution)/shard_map/ppermute | solution.py:157
  56.3 23.5 %collective-permute-start.5 = (bf16[16,512]{1,0:T(8,128)(2,1)}, bf16[16,512]{1,0:T(8,128)(2,1)}, u32[]{:S(2)}, u32[]{:S(2)}) collective-permute-start(bf16[16,512]{1,0:T(8,128)(2,1)} %get-tuple-element.101), channel_id=1, source_target_pairs={{4,0},{8,4},{12,8},{0,12},{5,1},{9,5},{13,9},{1,13},{6,2},{10,6},{... | collective-permute-start | bytes 49160 | tf_op jit(solution)/shard_map/ppermute | solution.py:156
  92.9 20.5 %all-to-all-start.3 = ((bf16[4,8,512]{2,1,0:T(8,128)(2,1)}), bf16[4,8,512]{2,1,0:T(8,128)(2,1)S(1)}, u32[]{:S(2)}, u32[]{:S(2)}) async-start(bf16[4,8,512]{2,1,0:T(8,128)(2,1)} %slice_bitcast_fusion.7), calls=%async_computation.3 | async-start | bytes 65536 | tf_op jit(solution)/shard_map/all_to_all | solution.py:158
  96.2 17.2 %collective-permute-start.6 = (bf16[8,512]{1,0:T(8,128)(2,1)S(1)}, bf16[8,512]{1,0:T(8,128)(2,1)S(1)}, u32[]{:S(2)}, u32[]{:S(2)}) collective-permute-start(bf16[8,512]{1,0:T(8,128)(2,1)S(1)} %get-tuple-element.102), channel_id=1, source_target_pairs={{0,4},{4,8},{8,12},{12,0},{1,5},{5,9},{9,13},{13,1},{2,6},{6,10},{... | collective-permute-start | bytes 24584 | tf_op jit(solution)/shard_map/ppermute | solution.py:157
  96.2 17.1 %collective-permute-start.7 = (bf16[8,512]{1,0:T(8,128)(2,1)S(1)}, bf16[8,512]{1,0:T(8,128)(2,1)S(1)}, u32[]{:S(2)}, u32[]{:S(2)}) collective-permute-start(bf16[8,512]{1,0:T(8,128)(2,1)S(1)} %get-tuple-element.103), channel_id=1, source_target_pairs={{4,0},{8,4},{12,8},{0,12},{5,1},{9,5},{13,9},{1,13},{6,2},{10,6},{... | collective-permute-start | bytes 24584 | tf_op jit(solution)/shard_map/ppermute | solution.py:156
  120.5 23.8 %copy-start.18 = (bf16[512,512]{1,0:T(8,128)(2,1)S(1)}, bf16[512,512]{1,0:T(8,128)(2,1)}, u32[]{:S(2)}) copy-start(bf16[512,512]{1,0:T(8,128)(2,1)} %get-tuple-element.81.refs_3_.refs_5_) | copy-start | bytes 1572868
  120.5 12.4 %all-to-all-start.5 = ((bf16[4,4,32,512]{3,2,1,0:T(8,128)(2,1)}), bf16[4,4,32,512]{3,2,1,0:T(8,128)(2,1)S(1)}, u32[]{:S(2)}, u32[]{:S(2)}) async-start(bf16[4,4,32,512]{3,2,1,0:T(8,128)(2,1)} %bitcast.58), calls=%async_computation.5 | async-start | bytes 1048576 | tf_op jit(solution)/shard_map/all_to_all | solution.py:130
  132.9 7.4 %all-to-all-start.4 = ((bf16[4,16,512]{2,1,0:T(8,128)(2,1)}), bf16[4,16,512]{2,1,0:T(8,128)(2,1)S(1)}, u32[]{:S(2)}, u32[]{:S(2)}) async-start(bf16[4,16,512]{2,1,0:T(8,128)(2,1)} %bitcast.24), calls=%async_computation.4 | async-start | bytes 131072 | tf_op jit(solution)/shard_map/all_to_all | solution.py:158
  140.3 10.1 %all-to-all-start.6 = ((bf16[4,1,32,512]{3,2,1,0:T(8,128)(2,1)}), bf16[4,1,32,512]{3,2,1,0:T(8,128)(2,1)}, u32[]{:S(2)}, u32[]{:S(2)}) async-start(bf16[4,1,32,512]{3,2,1,0:T(8,128)(2,1)} %fusion.2), calls=%async_computation.6 | async-start | bytes 262144 | tf_op jit(solution)/shard_map/all_to_all | solution.py:130
  173.6 29.3 %all-to-all-start.7 = ((bf16[4,4,128,512]{3,2,1,0:T(8,128)(2,1)}), bf16[4,4,128,512]{3,2,1,0:T(8,128)(2,1)S(1)}, u32[]{:S(2)}, u32[]{:S(2)}) async-start(bf16[4,4,128,512]{3,2,1,0:T(8,128)(2,1)} %bitcast.70), calls=%async_computation.7 | async-start | bytes 4194304 | tf_op jit(solution)/shard_map/all_to_all | solution.py:130
  177.3 29.8 %copy-start.95 = (s32[6,16]{1,0:T(8,128)S(1)}, s32[6,16]{1,0:T(8,128)}, u32[]{:S(2)}) copy-start(s32[6,16]{1,0:T(8,128)} %copy-done.94) | copy-start | bytes 1156
  202.9 16.5 %all-to-all-start.10 = ((bf16[4,1,96,512]{3,2,1,0:T(8,128)(2,1)}), bf16[4,1,96,512]{3,2,1,0:T(8,128)(2,1)}, u32[]{:S(2)}, u32[]{:S(2)}) async-start(bf16[4,1,96,512]{3,2,1,0:T(8,128)(2,1)} %fusion.1), calls=%async_computation.10 | async-start | bytes 786432 | tf_op jit(solution)/shard_map/all_to_all | solution.py:130
  207.2 15.7 %collective-permute-start.8 = (bf16[16,512]{1,0:T(8,128)(2,1)S(1)}, bf16[16,512]{1,0:T(8,128)(2,1)S(1)}, u32[]{:S(2)}, u32[]{:S(2)}) collective-permute-start(bf16[16,512]{1,0:T(8,128)(2,1)S(1)} %get-tuple-element.98), channel_id=1, source_target_pairs={{0,4},{4,8},{8,12},{12,0},{1,5},{5,9},{9,13},{13,1},{2,6},{6,10},{... | collective-permute-start | bytes 49160 | tf_op jit(solution)/shard_map/ppermute | solution.py:157
  209.2 13.7 %collective-permute-start.9 = (bf16[16,512]{1,0:T(8,128)(2,1)S(1)}, bf16[16,512]{1,0:T(8,128)(2,1)S(1)}, u32[]{:S(2)}, u32[]{:S(2)}) collective-permute-start(bf16[16,512]{1,0:T(8,128)(2,1)S(1)} %get-tuple-element.99), channel_id=1, source_target_pairs={{4,0},{8,4},{12,8},{0,12},{5,1},{9,5},{13,9},{1,13},{6,2},{10,6},{... | collective-permute-start | bytes 49160 | tf_op jit(solution)/shard_map/ppermute | solution.py:156
  219.4 15.9 %all-to-all-start.8 = ((bf16[4,1,128,512]{3,2,1,0:T(8,128)(2,1)}), bf16[4,1,128,512]{3,2,1,0:T(8,128)(2,1)S(1)}, u32[]{:S(2)}, u32[]{:S(2)}) async-start(bf16[4,1,128,512]{3,2,1,0:T(8,128)(2,1)} %fusion), calls=%async_computation.8 | async-start | bytes 1048576 | tf_op jit(solution)/shard_map/all_to_all | solution.py:130
  (94 other events, 136.0 us)

commit v3 on v2

v3 whole, which is shorter than its diff:
```python
import jax
import jax.numpy as jnp
from jax import lax
from jax.experimental import pallas as pl
from jax.experimental.pallas import tpu as pltpu
from jax.sharding import PartitionSpec as P

BF = jnp.bfloat16
F32 = jnp.float32
NN = (((1,), (0,)), ((), ()))
NT = (((1,), (1,)), ((), ()))
TN = (((0,), (0,)), ((), ()))
BORDER = 8
GROUP = ("lon", "lat", "sub")
COLUMN = ("lat", "sub")


def dot(a, b, dims=NN):
    return lax.dot_general(a, b, dims, preferred_element_type=F32)


def low(value):
    return value.astype(BF)


def sigmoid(value):
    return 0.5 * jnp.tanh(0.5 * value) + 0.5


def silu(value):
    return value * sigmoid(value)


def silu_both(value):
    sig = sigmoid(value)
    act = value * sig
    return act, sig + act * (1.0 - sig)


def silu_slope(value):
    return silu_both(value)[1]


def iota(rows, columns, dim):
    return lax.broadcasted_iota(jnp.int32, (rows, columns), dim)


def hot(mask):
    return jnp.where(mask, 1.0, 0.0)


def pieces(value, slots, starts, sizes):
    step = value.shape[0] // slots
    found = []
    for start, size in zip(starts, sizes):
        found.append(
            jnp.concatenate(
                [value[s * step + start : s * step + start + size] for s in range(slots)], axis=0
            )
        )
    return found


def braid(parts, slots):
    rows = []
    for s in range(slots):
        for part in parts:
            size = part.shape[0] // slots
            rows.append(part[s * size : (s + 1) * size])
    return jnp.concatenate(rows, axis=0)


def receivers(senders_t, nodes, halo):
    found = jnp.zeros((halo, nodes), F32)
    ids = iota(halo, nodes, 0) + nodes
    for j in range(senders_t.shape[0]):
        found = found + hot(senders_t[j : j + 1, :] == ids)
    return found


def receivers_t(senders, halo):
    nodes, degree = senders.shape
    found = jnp.zeros((nodes, halo), F32)
    ids = iota(nodes, halo, 1) + nodes
    for j in range(degree):
        found = found + hot(senders[:, j : j + 1] == ids)
    return found


def block_spot(block, dims, halving):
    lon, lat, sub = dims
    if halving:
        spot = 0
        for bit in range((lon * lat * sub - 1).bit_length()):
            spot = 2 * spot + (block >> bit) % 2
        return spot
    return (block % sub * lat + block // sub % lat) * lon + block // (lat * sub)


def store_blocks(ref, at, value, dims, halving):
    value = low(value)
    rows = value.shape[0]
    total = dims[0] * dims[1] * dims[2]
    depth = rows // total
    if depth % 16:
        ref[at] = value
        return
    for block in range(total):
        spot = block_spot(block, dims, halving)
        part = value[block * depth : (block + 1) * depth]
        if halving:
            half = total // 2
            start = spot % half * (ref.shape[1] // half) + at * depth
            ref[spot // half, start : start + depth, :] = part
        else:
            ref[spot, at * depth : (at + 1) * depth, :] = part


def fine(rows, dims):
    return (rows // (dims[0] * dims[1] * dims[2])) % 16 == 0


def blocks_shape(count, rows, width, dims):
    total = dims[0] * dims[1] * dims[2]
    if fine(rows, dims):
        return jax.ShapeDtypeStruct((total, count * rows // total, width), BF)
    return jax.ShapeDtypeStruct((count, rows, width), BF)


def scatter_offload(blocks, rows, dims):
    lon, lat, sub = dims
    if not fine(rows, dims):
        count, _, width = blocks.shape
        depth = rows // (lon * lat * sub)
        blocks = blocks.reshape(count, lon, lat, sub, depth, width)
        blocks = blocks.transpose(3, 2, 1, 0, 4, 5)
    blocks = blocks.reshape(sub, lat, lon, -1, blocks.shape[-1])
    for axis in ("sub", "lat", "lon"):
        blocks = lax.psum_scatter(blocks, axis, scatter_dimension=0, tiled=False)
    return blocks


def swap(block, bit, dims):
    total = dims[0] * dims[1] * dims[2]
    return lax.ppermute(block, GROUP, [(i, i ^ (1 << bit)) for i in range(total)])


def call(kernel, name, outs, args, flops, me=None, scratch=()):
    size = sum(a.size * a.dtype.itemsize for a in (*args, *outs))
    in_specs = [pl.BlockSpec(memory_space=pltpu.VMEM)] * len(args)
    if me is not None:
        args = (me, *args)
        in_specs = [pl.BlockSpec(memory_space=pltpu.SMEM)] + in_specs
    return pl.pallas_call(
        kernel,
        out_shape=list(outs),
        in_specs=in_specs,
        out_specs=[pl.BlockSpec(memory_space=pltpu.VMEM)] * len(outs),
        scratch_shapes=list(scratch),
        compiler_params=pltpu.CompilerParams(vmem_limit_bytes=16 * 1024 * 1024),
        cost_estimate=pl.CostEstimate(flops=flops, bytes_accessed=size, transcendentals=0),
        name=name,
    )(*args)


def exchange(parts, dims):
    column = dims[1] * dims[2]
    count = dims[0]
    forward = [(i, (i + 1) % count) for i in range(count)]
    backward = [(target, source) for source, target in forward]
    arrived = [
        lax.ppermute(parts[r - 1], COLUMN, [(i, i ^ r) for i in range(column)])
        for r in range(1, column)
    ]
    to_left, to_right = parts[column - 1 :]
    from_right = lax.ppermute(to_left, "lon", backward)
    from_left = lax.ppermute(to_right, "lon", forward)
    return (*arrived, from_left, from_right)


def slot_of(me, at, column):
    return jnp.bitwise_xor(me, at + 1) if at + 1 < column else at + 1


def spread(me, value, buf, refs):
    column = len(refs) - 1
    rows = refs[0].shape[0]
    buf[...] = value
    for at, ref in enumerate(refs):
        start = pl.multiple_of(slot_of(me, at, column) * rows, 8)
        ref[...] = low(buf[pl.ds(start, rows), :])


def collect(me, refs, buf):
    column = len(refs) - 1
    rows = refs[0].shape[0]
    buf[pl.ds(pl.multiple_of(me * rows, 8), rows), :] = jnp.zeros((rows, buf.shape[1]), F32)
    for at, ref in enumerate(refs):
        start = pl.multiple_of(slot_of(me, at, column) * rows, 8)
        buf[pl.ds(start, rows), :] = ref[...].astype(F32)
    return buf[...]


def shape(*dims, dtype=BF):
    return jax.ShapeDtypeStruct(dims, dtype)


def first_payload(me_ref, sends_ref, senders_t_ref, grid_ref, cot_ref, *rest):
    *out_refs, buf = rest
    taken = sends_ref.shape[0]
    chosen, nodes = grid_ref.shape[0], cot_ref.shape[0]
    slots = taken // 16
    rows = dot(low(hot(sends_ref[...] == iota(taken, chosen, 1))), grid_ref[...])
    back = low(receivers(senders_t_ref[...], nodes, slots * BORDER))
    spread(me_ref[0], braid([rows, dot(back, cot_ref[...])], slots), buf, out_refs)


def embed_local(grid_ref, weight_ref, target_ref, sends_ref, sum_ref, slope_ref):
    chosen = grid_ref.shape[0]
    nodes = sum_ref.shape[0]
    taken = sends_ref.shape[0]
    pre = dot(grid_ref[...], weight_ref[...])
    act, slope = silu_both(pre)
    slope_ref[...] = low(slope)
    sent = jnp.max(hot(sends_ref[...] == iota(taken, chosen, 1)), axis=0, keepdims=True)
    label = jnp.where(sent > 0.0, nodes, target_ref[...])
    sum_ref[...] = dot(low(hot(label == iota(nodes, chosen, 0))), low(act))


def merge_nodes(slots, me_ref, *refs):
    arr_refs, refs = refs[: slots - 1], refs[slots - 1 :]
    (incoming_ref, embed_ref, local_ref, mesh_ref, weight_ref, bounds_ref, senders_t_ref,
     merged_ref, state_ref, slope_ref, lat_ref, cot_ref, *pay_refs, buf) = refs
    me = me_ref[0]
    nodes = mesh_ref.shape[0]
    taken = incoming_ref.shape[1]
    halo = slots * BORDER
    lat, cot = pieces(collect(me, arr_refs, buf), slots, (0, 16), (16, BORDER))
    cot_ref[...] = low(cot)
    lat = low(lat)
    lat_ref[...] = lat
    act, slope = silu_both(dot(lat, embed_ref[...]))
    slope_ref[...] = low(slope)
    place = low(hot(incoming_ref[...] == iota(nodes, taken, 0)))
    merged = low(local_ref[...] + dot(place, low(act)))
    merged_ref[...] = merged
    state = low(mesh_ref[...].astype(F32) + dot(merged, weight_ref[...]))
    state_ref[...] = state
    border = hot(bounds_ref[...] == iota(halo, nodes, 1))
    back = receivers(senders_t_ref[...], nodes, halo)
    pick = low(braid([border, back], slots))
    rows = pieces(dot(pick, state), slots, (0, BORDER), (BORDER, BORDER))
    spread(me, braid([*rows, dot(low(border), merged)], slots), buf, pay_refs)


def local_edges(senders, sent, recv, each):
    nodes, degree = senders.shape
    total = jnp.zeros(recv.shape, F32)
    ids = iota(nodes, nodes, 1)
    for j in range(degree):
        named = senders[:, j : j + 1]
        act, slope = silu_both(dot(low(hot(named == ids)), sent) + recv)
        keep = hot(named < nodes)
        total = total + act * keep
        each(j, slope * keep)
    return total


def forward_local(
    state_ref, send_ref, recv_ref, senders_ref, senders_t_ref, bounds_ref,
    total_ref, slope_ref, recv_n_ref, sent_b_ref,
):
    state = state_ref[...]
    nodes = state.shape[0]
    halo = bounds_ref.shape[0]
    sent = low(dot(state, send_ref[...]))
    recv = dot(state, recv_ref[...])

    def keep(j, slope):
        slope_ref[j] = low(slope)

    total_ref[...] = local_edges(senders_ref[...], sent, recv, keep)
    back = low(receivers(senders_t_ref[...], nodes, halo))
    recv_n_ref[...] = dot(low(dot(back, state)), recv_ref[...])
    sent_b_ref[...] = low(dot(low(hot(bounds_ref[...] == iota(halo, nodes, 1))), sent))


def forward_halo(slots, me_ref, *refs):
    arr_refs, refs = refs[: slots - 1], refs[slots - 1 :]
    (recv_n_ref, total_ref, state_ref, send_ref, update_ref, senders_ref, senders_t_ref,
     bounds_ref, summed_ref, out_ref, pre_ref, rows_ref, back_ref, merged_ref, *pay_refs, buf,
     out_buf) = refs
    me = me_ref[0]
    nodes = state_ref.shape[0]
    halo = slots * BORDER
    rows, back, merged = pieces(
        collect(me, arr_refs, buf), slots, (0, BORDER, 2 * BORDER), (BORDER,) * 3
    )
    rows_ref[...], back_ref[...], merged_ref[...] = low(rows), low(back), low(merged)
    pre = low(dot(low(rows), send_ref[...])).astype(F32) + recv_n_ref[...]
    pre_ref[...] = pre
    place = low(receivers_t(senders_ref[...], halo))
    summed = low(total_ref[...] + dot(place, low(silu(pre))))
    summed_ref[...] = summed
    state = low(state_ref[...].astype(F32) + dot(summed, update_ref[...]))
    out_ref[...] = state
    border = hot(bounds_ref[...] == iota(halo, nodes, 1))
    back = receivers(senders_t_ref[...], nodes, halo)
    spread(me, dot(low(braid([border, back], slots)), state), out_buf, pay_refs)


def turn_local(
    slots, state_ref, send_ref, recv_ref, update_ref, cot_ref, cot_r_ref, pre_ref, back0_ref,
    sent_b0_ref, recv0_ref, senders_ref, senders_t_ref, bounds_ref,
    total_ref, grecv_ref, gsent_ref, recv_n_ref, sent_b_ref, gsum_n_ref, gsum_r_ref,
    slope_k_ref, slope_r_ref,
):
    halo = slots * BORDER
    slope_k_ref[...] = low(silu_slope(pre_ref[...]))
    pre = sent_b0_ref[...].astype(F32) + dot(back0_ref[...], recv0_ref[...])
    slope_r_ref[...] = low(silu_slope(pre))
    state = state_ref[...]
    nodes = state.shape[0]
    sent = low(dot(state, send_ref[...]))
    recv = dot(state, recv_ref[...])
    gsum = low(dot(cot_ref[...], update_ref[...], NT))
    grad = gsum.astype(F32)
    grecv_ref[...] = jnp.zeros(grecv_ref.shape, F32)
    gsent_ref[...] = jnp.zeros(gsent_ref.shape, F32)

    def back_edge(j, slope):
        gpre = grad * slope
        grecv_ref[...] += gpre
        place = low(hot(senders_t_ref[j : j + 1, :] == iota(nodes, nodes, 0)))
        gsent_ref[...] += dot(place, low(gpre))

    total_ref[...] = local_edges(senders_ref[...], sent, recv, back_edge)
    back = low(receivers(senders_t_ref[...], nodes, halo))
    recv_n_ref[...] = dot(low(dot(back, state)), recv_ref[...])
    sent_b_ref[...] = low(dot(low(hot(bounds_ref[...] == iota(halo, nodes, 1))), sent))
    gsum_n_ref[...] = low(dot(back, gsum))
    gsum_r_ref[...] = low(dot(cot_r_ref[...], update_ref[...], NT))


def turn_halo(slots, me_ref, *refs):
    arr_refs, refs = refs[: slots - 1], refs[slots - 1 :]
    (recv_n_ref, sent_b_ref, gsum_n_ref, gsum_r_ref, total_ref, grecv_ref, gsent_ref, cot_ref,
     send_ref, recv_ref, senders_ref, senders_t_ref, bounds_ref, summed_ref, grecv_out_ref,
     gsent_out_ref, gin_ref, *pay_refs, buf, out_buf) = refs
    me = me_ref[0]
    nodes = cot_ref.shape[0]
    halo = slots * BORDER
    rows, back = pieces(collect(me, arr_refs, buf), slots, (0, BORDER), (BORDER,) * 2)
    pre = low(dot(low(rows), send_ref[...])).astype(F32) + recv_n_ref[...]
    act, slope = silu_both(pre)
    place = low(receivers_t(senders_ref[...], halo))
    gpre = low(gsum_n_ref[...].astype(F32) * slope)
    grecv = low(grecv_ref[...] + dot(place, gpre))
    pre = sent_b_ref[...].astype(F32) + dot(low(back), recv_ref[...])
    gpre = low(gsum_r_ref[...].astype(F32) * silu_slope(pre))
    border = low(hot(bounds_ref[...] == iota(nodes, halo, 0)))
    gsent = low(gsent_ref[...] + dot(border, gpre))
    gin = cot_ref[...].astype(F32) + dot(grecv, recv_ref[...], NT) + dot(gsent, send_ref[...], NT)
    gin = low(gin)
    gin_ref[...] = gin
    spread(me, dot(low(receivers(senders_t_ref[...], nodes, halo)), gin), out_buf, pay_refs)
    summed_ref[...] = low(total_ref[...] + dot(place, low(act)))
    grecv_out_ref[...] = grecv
    gsent_out_ref[...] = gsent


def last_weights(
    dims, state_ref, summed_ref, cot_ref, grecv_ref, gsent_ref, update_ref, out_ref, mesh_ref
):
    state, summed = state_ref[...], summed_ref[...]
    store_blocks(out_ref, 0, dot(state, gsent_ref[...], TN), dims, False)
    store_blocks(out_ref, 1, dot(state, grecv_ref[...], TN), dims, False)
    store_blocks(out_ref, 2, dot(summed, cot_ref[...], TN), dims, False)
    mesh_ref[...] = low(state.astype(F32) + dot(summed, update_ref[...]))


def back_local(
    dims, gin_ref, slope_ref, slope_k_ref, send_ref, recv_ref, update_ref, senders_ref,
    senders_t_ref, part_ref, gpre_out_ref, grecv_out_ref, gsent_out_ref,
):
    nodes = gin_ref.shape[0]
    halo = slope_k_ref.shape[0]
    gin = gin_ref[...]
    gsum = low(dot(gin, update_ref[...], NT))
    grad = gsum.astype(F32)
    place = low(receivers_t(senders_ref[...], halo))
    back = low(receivers(senders_t_ref[...], nodes, halo))
    gpre_k = low(dot(back, gsum) * slope_k_ref[...].astype(F32))
    grecv = dot(place, gpre_k)
    gsent = jnp.zeros(grad.shape, F32)
    for j in range(senders_t_ref.shape[0]):
        gpre = grad * slope_ref[j].astype(F32)
        grecv = grecv + gpre
        target = low(hot(senders_t_ref[j : j + 1, :] == iota(nodes, nodes, 0)))
        gsent = gsent + dot(target, low(gpre))
    grecv, gsent = low(grecv), low(gsent)
    part = gin.astype(F32) + dot(grecv, recv_ref[...], NT) + dot(gsent, send_ref[...], NT)
    part_ref[...] = part
    gpre_out_ref[...], grecv_out_ref[...], gsent_out_ref[...] = gpre_k, grecv, gsent


def embed_back(slots, dims, me_ref, *refs):
    arr_refs, refs = refs[: slots - 1], refs[slots - 1 :]
    (slope_r_ref, part_ref, update_ref, send_ref, merge_ref, bounds_ref, target_ref, sends_ref,
     incoming_ref, slope_g_ref, slope_a_ref, grid_ref, lat_ref, embed_ref, state_ref, rows_ref,
     gpre_k_ref, gsent_ref, grecv_ref, summed_ref, gin1_ref, merged_ref, merged_r_ref,
     gpre_ref, keep_ref, give_ref, *pay_refs, buf, out_buf, blocks) = refs
    me = me_ref[0]
    nodes = part_ref.shape[0]
    halo = slots * BORDER
    chosen = grid_ref.shape[0]
    taken = sends_ref.shape[0]
    gsum = low(dot(low(collect(me, arr_refs, buf)), update_ref[...], NT)).astype(F32)
    gpre = low(gsum * slope_r_ref[...].astype(F32))
    border = low(hot(bounds_ref[...] == iota(nodes, halo, 0)))
    gsent_r = low(dot(border, gpre))
    gin = low(part_ref[...] + dot(gsent_r, send_ref[...], NT))
    gmerged = low(dot(gin, merge_ref[...], NT))
    place = low(hot(incoming_ref[...] == iota(nodes, taken, 0)))
    gpre_a = low(dot(place, gmerged, TN) * slope_a_ref[...].astype(F32))
    spread(me, dot(gpre_a, embed_ref[...], NT), out_buf, pay_refs)
    sent = jnp.max(hot(sends_ref[...] == iota(taken, chosen, 1)), axis=0, keepdims=True)
    label = jnp.where(sent > 0.0, nodes, target_ref[...])
    pick = low(hot(label == iota(nodes, chosen, 0)))
    gpre_g = low(dot(pick, gmerged, TN) * slope_g_ref[...].astype(F32))
    gpre_ref[...] = gpre_g
    state = state_ref[...]
    grad_embed = dot(grid_ref[...], gpre_g, TN) + dot(lat_ref[...], gpre_a, TN)
    store_blocks(blocks, 0, grad_embed, dims, True)
    store_blocks(blocks, 1, dot(merged_ref[...], gin, TN), dims, True)
    grad_send = dot(state, gsent_ref[...], TN) + dot(rows_ref[...], gpre_k_ref[...], TN)
    store_blocks(blocks, 2, grad_send, dims, True)
    store_blocks(blocks, 3, dot(state, grecv_ref[...], TN), dims, True)
    store_blocks(blocks, 4, dot(summed_ref[...], gin1_ref[...], TN), dims, True)
    if not fine(grid_ref.shape[1], dims):
        keep_ref[...] = blocks[...]
        return
    mine = me_ref[1] % 2
    keep_ref[...] = blocks[mine]
    give_ref[...] = blocks[1 - mine]


def halve(bit, me_ref, keep_ref, arr_ref, keep_out, give_out):
    half = keep_ref.shape[0] // 2
    mine = jnp.bitwise_and(jnp.right_shift(me_ref[1], bit), 1)
    for out, side in ((keep_out, mine), (give_out, 1 - mine)):
        rows = pl.ds(pl.multiple_of(side * half, 16), half)
        out[...] = low(keep_ref[rows, :].astype(F32) + arr_ref[rows, :].astype(F32))


def finish(
    keep_ref, arr_ref, last_ref, embed_ref, merge_ref, send_ref, recv_ref, update_ref
):
    total = keep_ref[...].astype(F32) + arr_ref[...].astype(F32)
    depth = embed_ref.shape[0]
    embed_ref[...] = total[:depth]
    merge_ref[...] = total[depth : 2 * depth]
    for at, ref in enumerate((send_ref, recv_ref, update_ref)):
        ref[0] = total[(at + 2) * depth : (at + 3) * depth]
        ref[1] = last_ref[at * depth : (at + 1) * depth, :].astype(F32)


def grid_place(slots, me_ref, *refs):
    arr_refs, refs = refs[: slots - 1], refs[slots - 1 :]
    gpre_ref, weight_ref, sends_ref, out_ref, buf = refs
    chosen = gpre_ref.shape[0]
    taken = sends_ref.shape[1]
    local = dot(gpre_ref[...], weight_ref[...], NT)
    place = low(hot(sends_ref[...] == iota(chosen, taken, 0)))
    out_ref[...] = low(local + dot(place, low(collect(me_ref[0], arr_refs, buf))))


def body(
    dims,
    grid_latent, mesh_latent, cotangent, embed_weight, merge_weight, send_weight, recv_weight,
    update_weight, target_row, send_rows, incoming_rows, border_mesh_rows, mesh_senders,
):
    chosen, width = grid_latent.shape
    nodes, degree = mesh_senders.shape
    slots, capacity = send_rows.shape[1:]
    peers = slots - 1
    halo = slots * BORDER
    taken = slots * capacity
    sends_col = send_rows.reshape(taken, 1)
    sends_row = send_rows.reshape(1, taken)
    incoming = incoming_rows.reshape(1, taken)
    bounds_col = border_mesh_rows.reshape(halo, 1)
    bounds_row = border_mesh_rows.reshape(1, halo)
    targets = target_row.reshape(1, chosen)
    senders_t = mesh_senders.T
    send0, send1 = send_weight[0], send_weight[1]
    recv0, recv1 = recv_weight[0], recv_weight[1]
    update0, update1 = update_weight[0], update_weight[1]
    me = jnp.stack([lax.axis_index(COLUMN), lax.axis_index(GROUP)]).astype(jnp.int32)
    unit = 2 * nodes * width * width

    def buffer(rows):
        return pltpu.VMEM((slots * rows, width), F32)

    pay1 = call(
        first_payload, "first_payload", [shape(24, width)] * peers,
        (sends_col, senders_t, grid_latent, cotangent), flops=unit // 2, me=me,
        scratch=[buffer(24)],
    )
    arr1 = exchange(pay1, dims)
    local, slope_g = call(
        embed_local, "embed_local", [shape(nodes, width, dtype=F32), shape(chosen, width)],
        (grid_latent, embed_weight, targets, sends_col), flops=3 * unit,
    )
    merged, state0, slope_a, lat_a, cot_r, *pay2 = call(
        lambda *refs: merge_nodes(slots, *refs), "merge_nodes",
        [shape(nodes, width), shape(nodes, width), shape(taken, width), shape(taken, width),
         shape(halo, width)] + [shape(24, width)] * peers,
        (*arr1, incoming, embed_weight, local, mesh_latent, merge_weight, bounds_col, senders_t),
        flops=2 * unit, me=me, scratch=[buffer(24)],
    )
    arr2 = exchange(pay2, dims)
    total0, slope0, recv_n0, sent_b0 = call(
        forward_local, "forward_local",
        [shape(nodes, width, dtype=F32), shape(degree, nodes, width),
         shape(halo, width, dtype=F32), shape(halo, width)],
        (state0, send0, recv0, mesh_senders, senders_t, bounds_col), flops=6 * unit,
    )
    summed0, state1, pre0, rows0, back0, merged_r, *pay3 = call(
        lambda *refs: forward_halo(slots, *refs), "forward_halo",
        [shape(nodes, width), shape(nodes, width), shape(halo, width, dtype=F32)]
        + [shape(halo, width)] * 3 + [shape(16, width)] * peers,
        (*arr2, recv_n0, total0, state0, send0, update0, mesh_senders, senders_t, bounds_col),
        flops=2 * unit, me=me, scratch=[buffer(24), buffer(16)],
    )
    arr3 = exchange(pay3, dims)
    (total1, grecv_l, gsent_l, recv_n1, sent_b1, gsum_n1, gsum_r1, slope_k0, slope_r0) = call(
        lambda *refs: turn_local(slots, *refs), "turn_local",
        [shape(nodes, width, dtype=F32)] * 3 + [shape(halo, width, dtype=F32)]
        + [shape(halo, width)] * 5,
        (state1, send1, recv1, update1, cotangent, cot_r, pre0, back0, sent_b0, recv0,
         mesh_senders, senders_t, bounds_col),
        flops=10 * unit,
    )
    summed1, grecv1, gsent1, gin1, *pay4 = call(
        lambda *refs: turn_halo(slots, *refs), "turn_halo",
        [shape(nodes, width)] * 4 + [shape(BORDER, width)] * peers,
        (*arr3, recv_n1, sent_b1, gsum_n1, gsum_r1, total1, grecv_l, gsent_l, cotangent,
         send1, recv1, mesh_senders, senders_t, bounds_row),
        flops=3 * unit, me=me, scratch=[buffer(16), buffer(BORDER)],
    )
    arr4 = exchange(pay4, dims)
    blocks1, mesh_out = call(
        lambda *refs: last_weights(dims, *refs), "last_weights",
        [blocks_shape(3, width, width, dims), shape(nodes, width)],
        (state1, summed1, cotangent, grecv1, gsent1, update1), flops=4 * unit,
    )
    sum1 = scatter_offload(blocks1, width, dims)
    part0, gpre_k, grecv0, gsent0 = call(
        lambda *refs: back_local(dims, *refs), "back_local",
        [shape(nodes, width, dtype=F32), shape(halo, width), shape(nodes, width),
         shape(nodes, width)],
        (gin1, slope0, slope_k0, send0, recv0, update0, mesh_senders, senders_t),
        flops=6 * unit,
    )
    total = dims[0] * dims[1] * dims[2]
    depth = width // total
    if fine(width, dims):
        scratch = pltpu.VMEM((2, total // 2 * 5 * depth, width), BF)
        given = [shape(total // 2 * 5 * depth, width)] * 2
    else:
        scratch = pltpu.VMEM((5, width, width), BF)
        given = [shape(5, width, width), shape(16, width)]
    gpre_g, keep, give, *pay5 = call(
        lambda *refs: embed_back(slots, dims, *refs), "embed_back",
        [shape(chosen, width), *given] + [shape(capacity, width)] * peers,
        (*arr4, slope_r0, part0, update0, send0, merge_weight, bounds_row, targets,
         sends_col, incoming, slope_g, slope_a, grid_latent, lat_a, embed_weight, state0, rows0,
         gpre_k, gsent0, grecv0, summed0, gin1, merged, merged_r),
        flops=10 * unit, me=me, scratch=[buffer(BORDER), buffer(capacity), scratch],
    )
    arr5 = exchange(pay5, dims)
    (grid_grad,) = call(
        lambda *refs: grid_place(slots, *refs), "grid_place", [shape(chosen, width)],
        (*arr5, gpre_g, embed_weight, sends_row), flops=3 * unit, me=me,
        scratch=[buffer(capacity)],
    )
    if not fine(width, dims):
        sum0 = scatter_offload(keep, width, dims).astype(F32)
        sum1 = sum1.astype(F32)
        parts = [sum0[i * depth : (i + 1) * depth] for i in range(5)]
        stacked = [
            jnp.stack([parts[i + 2], sum1[i * depth : (i + 1) * depth]]) for i in range(3)
        ]
        return (mesh_out, grid_grad, parts[0], parts[1], *stacked)
    bits = (total - 1).bit_length()
    arrived = swap(give, 0, dims)
    for bit in range(1, bits):
        rows = keep.shape[0] // 2
        keep, give = call(
            lambda *refs: halve(bit, *refs), "halve", [shape(rows, width)] * 2, (keep, arrived),
            flops=4 * rows * width, me=me,
        )
        arrived = swap(give, bit, dims)
    grads = call(
        finish, "finish",
        [shape(depth, width, dtype=F32)] * 2 + [shape(2, depth, width, dtype=F32)] * 3,
        (keep, arrived, sum1), flops=5 * depth * width,
    )
    return (mesh_out, grid_grad, *grads)


def solution(mesh):
    split = ("groups", "lon", "lat", "sub")
    dims = tuple(mesh.shape[axis] for axis in GROUP)
    rows = P(split, None)
    whole = P("groups", GROUP, None)
    in_specs = (
        rows, rows, rows, P(), P(), P(), P(), P(), P(split), P(split, None, None),
        P(split, None, None), P(split, None, None), rows,
    )
    out_specs = (rows, rows, rows, rows, whole, whole, whole)
    return jax.shard_map(
        lambda *args: body(dims, *args),
        mesh=mesh, in_specs=in_specs, out_specs=out_specs, check_vma=False,
    )
```

time: 241 us -> 148 us (0.61)
  local copies, waits for them, and re-layouts: 75.7 us -> 29.5 us
  starting transfers between devices: 57.2 us -> 33.9 us
  blocking collectives: 23.3 us -> 0 us
  between operations: 1.24 us -> 14.4 us
  waiting for transfers between devices: 50.3 us -> 40.7 us
  other arithmetic: 11.4 us -> 2.17 us
  Pallas kernels: 19 us -> 26.3 us
    all_to_all x10 -> x0, waiting for transfers between devices: 50.3 us -> none  [the longest x5 46.9 us: scatter_sum(): lax.all_to_all(blocks, axes, split_axis=0, concat_axis=0, tiled=True)]
    unnamed x197 -> x121, local copies, waits for them, and re-layouts: 66.4 us -> 25 us
    all_to_all x10 -> x0, starting transfers between devices: 37.3 us -> none  [the longest x5 18.8 us: scatter_sum(): lax.all_to_all(blocks, axes, split_axis=0, concat_axis=0, tiled=True)]
    ppermute x10 -> x29, waiting for transfers between devices: 0.03 us -> 26 us  [the longest x4 23.4 us: swap(): return lax.ppermute(block, GROUP, [(i, i ^ 1 << bit) for i in range(total)])]
    all_to_all x1 -> x0, blocking collectives: 23.3 us -> none  [scatter_sum(): lax.all_to_all(blocks, axes, split_axis=0, concat_axis=0, tiled=True)]
    reduce_scatter x0 -> x3, waiting for transfers between devices: none -> 14.7 us  [scatter_offload(): blocks = lax.psum_scatter(blocks, axis, scatter_dimension=0, tiled=False)]
    ppermute x10 -> x29, starting transfers between devices: 19.8 us -> 33.8 us  [the longest x5 14.9 us: exchange(): from_right = lax.ppermute(to_left, 'lon', backward)]
    pallas_call x12 -> x15, Pallas kernels: 19 us -> 26.3 us  [call(): pl.pallas_call(kernel, out_shape=list(outs), in_specs=in_specs, out_specs...]
  transfers between devices with their start and end apart: 20 -> 32, of which waited for: 6 -> 6; matrix products, arithmetic and copies ran while one was open for 5% -> 5% of each run, Pallas kernels for 6% -> 12%
where the time goes in v3:
time: 148 us; the launch traced here: 147 us
  waiting for transfers between devices  40.7 us (28%)
  starting transfers between devices  33.9 us (23%)
  local copies, waits for them, and re-layouts  29.5 us (20%)
  Pallas kernels  26.3 us (18%)
  between operations  14.4 us (10%)
  other arithmetic  2.17 us (1%)
    pallas_call x15, Pallas kernels, call(): pl.pallas_call(kernel, out_shape=list(outs), in_specs=in_specs, out_specs...  26.3 us
    unnamed x121, local copies, waits for them, and re-layouts  25 us
    ppermute x4, waiting for transfers between devices, swap(): return lax.ppermute(block, GROUP, [(i, i ^ 1 << bit) for i in range(total)])  23.4 us
    ppermute x5, starting transfers between devices, exchange(): from_right = lax.ppermute(to_left, 'lon', backward)  14.9 us
    reduce_scatter x3, waiting for transfers between devices, scatter_offload(): blocks = lax.psum_scatter(blocks, axis, scatter_dimension=0, tiled=False)  14.7 us
    ppermute x15, starting transfers between devices, exchange(): lax.ppermute(parts[r - 1], COLUMN, [(i, i ^ r) for i in range(column)])  10.6 us
    ppermute x5, starting transfers between devices, exchange(): from_left = lax.ppermute(to_right, 'lon', forward)  4.26 us
    ppermute x4, starting transfers between devices, swap(): return lax.ppermute(block, GROUP, [(i, i ^ 1 << bit) for i in range(total)])  4.05 us
  transfers between devices with their start and end apart: 32, of which 6 were waited for; matrix products, arithmetic and copies ran while one was open for 5% of the time, Pallas kernels for 12%

profile of v3, /device:TPU:0, one launch (start us, length us, event | category | flops | bytes accessed | tf_op | source)
XLA Modules:
  0.0 147.1 jit_solution(7497765118660740731)
XLA Ops:
  13.2 2.5 %collective-permute-start.1 = (bf16[24,512]{1,0:T(8,128)(2,1)}, bf16[24,512]{1,0:T(8,128)(2,1)S(1)}, u32[]{:S(2)}, u32[]{:S(2)}) collective-permute-start(bf16[24,512]{1,0:T(8,128)(2,1)} %get-tuple-element.83), channel_id=1, source_target_pairs={{0,2},{1,3},{2,0},{3,1},{4,6},{5,7},{6,4},{7,5},{8,10},{9,11},{10,... | collective-permute-start | bytes 73736 | tf_op jit(solution)/shard_map/ppermute | solution.py:172
  15.8 1.8 %collective-permute-start.3 = (bf16[24,512]{1,0:T(8,128)(2,1)S(1)}, bf16[24,512]{1,0:T(8,128)(2,1)S(1)}, u32[]{:S(2)}, u32[]{:S(2)}) collective-permute-start(bf16[24,512]{1,0:T(8,128)(2,1)S(1)} %get-tuple-element.85), channel_id=1, source_target_pairs={{0,4},{4,8},{8,12},{12,0},{1,5},{5,9},{9,13},{13,1},{2,6},{6,10},{... | collective-permute-start | bytes 73736 | tf_op jit(solution)/shard_map/ppermute | solution.py:177
  17.6 2.0 %collective-permute-start.4 = (bf16[24,512]{1,0:T(8,128)(2,1)S(1)}, bf16[24,512]{1,0:T(8,128)(2,1)S(1)}, u32[]{:S(2)}, u32[]{:S(2)}) collective-permute-start(bf16[24,512]{1,0:T(8,128)(2,1)S(1)} %get-tuple-element.86), channel_id=1, source_target_pairs={{4,0},{8,4},{12,8},{0,12},{5,1},{9,5},{13,9},{1,13},{6,2},{10,6},{... | collective-permute-start | bytes 73736 | tf_op jit(solution)/shard_map/ppermute | solution.py:176
  24.6 1.7 %slice_bitcast_fusion.1 = (bf16[512,512]{1,0:T(8,128)(2,1)S(1)}, bf16[512,512]{1,0:T(8,128)(2,1)S(1)}, bf16[512,512]{1,0:T(8,128)(2,1)S(1)}, bf16[512,512]{1,0:T(8,128)(2,1)S(1)}) fusion(bf16[2,512,512]{2,1,0:T(8,128)(2,1)} %param.19, bf16[2,512,512]{2,1,0:T(8,128)(2,1)} %param.18), kind=kLoop, calls=%fused_computation.1 | loop fusion | bytes 4194304 | tf_op jit(solution)/shard_map/squeeze | solution.py:497
  36.9 1.7 %collective-permute-start.6 = (bf16[24,512]{1,0:T(8,128)(2,1)S(1)}, bf16[24,512]{1,0:T(8,128)(2,1)S(1)}, u32[]{:S(2)}, u32[]{:S(2)}) collective-permute-start(bf16[24,512]{1,0:T(8,128)(2,1)S(1)} %get-tuple-element.89), channel_id=1, source_target_pairs={{0,2},{1,3},{2,0},{3,1},{4,6},{5,7},{6,4},{7,5},{8,10},{9,11},{10,... | collective-permute-start | bytes 73736 | tf_op jit(solution)/shard_map/ppermute | solution.py:172
  38.8 3.8 %collective-permute-start.9 = (bf16[24,512]{1,0:T(8,128)(2,1)S(1)}, bf16[24,512]{1,0:T(8,128)(2,1)S(1)}, u32[]{:S(2)}, u32[]{:S(2)}) collective-permute-start(bf16[24,512]{1,0:T(8,128)(2,1)S(1)} %get-tuple-element.92), channel_id=1, source_target_pairs={{4,0},{8,4},{12,8},{0,12},{5,1},{9,5},{13,9},{1,13},{6,2},{10,6},{... | collective-permute-start | bytes 73736 | tf_op jit(solution)/shard_map/ppermute | solution.py:176
  42.6 2.2 %forward_local.1 = (f32[256,512]{1,0:T(8,128)S(1)}, bf16[6,256,512]{2,1,0:T(8,128)(2,1)S(1)}, f32[48,512]{1,0:T(8,128)S(1)}, bf16[48,512]{1,0:T(8,128)(2,1)S(1)}) custom-call(bf16[256,512]{1,0:T(8,128)(2,1)S(1)} %get-tuple-element.93.state_ref.refs_8_.refs_20_, bf16[512,512]{1,0:T(8,128)(2,1)S(1)} %get-tuple-element.163.send_ref.refs_9_.refs_3_, ...), custom_call_target="tpu_custom_call" | custom-call | flops 805306368 | bytes 3567808 | tf_op jit(solution)/shard_map/forward_local/pallas_call | solution.py:154
  49.4 1.7 %collective-permute-start.11 = (bf16[16,512]{1,0:T(8,128)(2,1)S(1)}, bf16[16,512]{1,0:T(8,128)(2,1)S(1)}, u32[]{:S(2)}, u32[]{:S(2)}) collective-permute-start(bf16[16,512]{1,0:T(8,128)(2,1)S(1)} %get-tuple-element.98), channel_id=1, source_target_pairs={{0,2},{1,3},{2,0},{3,1},{4,6},{5,7},{6,4},{7,5},{8,10},{9,11},{10,... | collective-permute-start | bytes 49160 | tf_op jit(solution)/shard_map/ppermute | solution.py:172
  51.3 3.8 %collective-permute-start.14 = (bf16[16,512]{1,0:T(8,128)(2,1)S(1)}, bf16[16,512]{1,0:T(8,128)(2,1)S(1)}, u32[]{:S(2)}, u32[]{:S(2)}) collective-permute-start(bf16[16,512]{1,0:T(8,128)(2,1)S(1)} %get-tuple-element.101), channel_id=1, source_target_pairs={{4,0},{8,4},{12,8},{0,12},{5,1},{9,5},{13,9},{1,13},{6,2},{10,6},{... | collective-permute-start | bytes 49160 | tf_op jit(solution)/shard_map/ppermute | solution.py:176
  55.1 4.0 %turn_local.1 = (f32[256,512]{1,0:T(8,128)S(1)}, f32[256,512]{1,0:T(8,128)S(1)}, f32[256,512]{1,0:T(8,128)S(1)}, f32[48,512]{1,0:T(8,128)S(1)}, bf16[48,512]{1,0...) custom-call(bf16[256,512]{1,0:T(8,128)(2,1)S(1)} %get-tuple-element., ...), custom_call_target="tpu_custom_call" | custom-call | flops 1342177280 | bytes 4796608 | tf_op jit(solution)/shard_map/turn_local/pallas_call | solution.py:154
  60.4 1.9 %turn_halo.1 = (bf16[256,512]{1,0:T(8,128)(2,1)S(1)}, bf16[256,512]{1,0:T(8,128)(2,1)S(1)}, bf16[256,512]{1,0:T(8,128)(2,1)S(1)}, bf16[256,512]{1,0:T(8,128)(2,1...) custom-call(s32[2]{0:T(128)S(1)} %pad_add_fusion.me_ref.refs_0_, ...), custom_call_target="tpu_custom_call" | custom-call | flops 402653184 | bytes 4313280 | tf_op jit(solution)/shard_map/turn_halo/pallas_call | solution.py:154
  65.8 1.8 %collective-permute-start.16 = (bf16[8,512]{1,0:T(8,128)(2,1)}, bf16[8,512]{1,0:T(8,128)(2,1)S(1)}, u32[]{:S(2)}, u32[]{:S(2)}) collective-permute-start(bf16[8,512]{1,0:T(8,128)(2,1)} %copy-done.56), channel_id=1, source_target_pairs={{0,2},{1,3},{2,0},{3,1},{4,6},{5,7},{6,4},{7,5},{8,10},{9,11},{10,... | collective-permute-start | bytes 24584 | tf_op jit(solution)/shard_map/ppermute | solution.py:172
  67.7 3.8 %collective-permute-start.19 = (bf16[8,512]{1,0:T(8,128)(2,1)}, bf16[8,512]{1,0:T(8,128)(2,1)S(1)}, u32[]{:S(2)}, u32[]{:S(2)}) collective-permute-start(bf16[8,512]{1,0:T(8,128)(2,1)} %copy-done.53), channel_id=1, source_target_pairs={{4,0},{8,4},{12,8},{0,12},{5,1},{9,5},{13,9},{1,13},{6,2},{10,6},{... | collective-permute-start | bytes 24584 | tf_op jit(solution)/shard_map/ppermute | solution.py:176
  76.5 4.5 %embed_back.1 = (bf16[512,512]{1,0:T(8,128)(2,1)S(1)}, bf16[1280,512]{1,0:T(8,128)(2,1)S(1)}, bf16[1280,512]{1,0:T(8,128)(2,1)}, bf16[16,512]{1,0:T(8,128)(2,1)S...) custom-call(s32[2]{0:T(128)S(1)} %pad_add_fusion.me_ref.refs_0_, ...), custom_call_target="tpu_custom_call" | custom-call | flops 1342177280 | bytes 8907712 | tf_op jit(solution)/shard_map/embed_back/pallas_call | solution.py:154
  82.2 3.2 %collective-permute-done.25.refs_2_ = bf16[1280,512]{1,0:T(8,128)(2,1)S(1)} collective-permute-done((bf16[1280,512]{1,0:T(8,128)(2,1)}, bf16[1280,512]{1,0:T(8,128)(2,1)S(1)}, u32[]{:S(2)}, u32[]{:S(2)}) %collective-permute-start.25) | collective-permute-done | bytes 1310752 | tf_op jit(solution)/shard_map/ppermute | solution.py:145
  86.7 1.6 %halve.3 = (bf16[640,512]{1,0:T(8,128)(2,1)S(1)}, bf16[640,512]{1,0:T(8,128)(2,1)}) custom-call(s32[2]{0:T(128)S(1)} %pad_add_fusion.me_ref.refs_0_, bf16[1280,512]{1,0:T(8,128)(2,1)S(1)} %copy-done.8, bf16[1280,512]{1,0:T(8,128)(2,1)S(1)} %collective-permute-done.25.refs_2_), custom_call_target="tpu_custom_call" | custom-call | flops 1310720 | bytes 3932160 | tf_op jit(solution)/shard_map/halve/pallas_call | solution.py:154
  88.3 1.7 %collective-permute-start.26 = (bf16[640,512]{1,0:T(8,128)(2,1)}, bf16[640,512]{1,0:T(8,128)(2,1)S(1)}, u32[]{:S(2)}, u32[]{:S(2)}) collective-permute-start(bf16[640,512]{1,0:T(8,128)(2,1)} %get-tuple-element.146), channel_id=1, source_target_pairs={{0,2},{1,3},{2,0},{3,1},{4,6},{5,7},{6,4},{7,5},{8,10},{9,11},{10,... | collective-permute-start | bytes 1966088 | tf_op jit(solution)/shard_map/ppermute | solution.py:145
  90.0 14.7 %reduce-scatter.6.cloned.1.call-done = bf16[1,4,96,512]{3,2,1,0:T(8,128)(2,1)} async-done(((bf16[2,4,96,512]{3,2,1,0:T(8,128)(2,1)}), bf16[1,4,96,512]{3,2,1,0:T(8,128)(2,1)}) %reduce-scatter.6.cloned.1.call-update) | async-done | bytes 393232 | tf_op jit(solution)/shard_map/reduce_scatter | solution.py:139
  104.7 6.8 %collective-permute-done.26.refs_2_ = bf16[640,512]{1,0:T(8,128)(2,1)S(1)} collective-permute-done((bf16[640,512]{1,0:T(8,128)(2,1)}, bf16[640,512]{1,0:T(8,128)(2,1)S(1)}, u32[]{:S(2)}, u32[]{:S(2)}) %collective-permute-start.26) | collective-permute-done | bytes 655392 | tf_op jit(solution)/shard_map/ppermute | solution.py:145
  112.6 13.4 %collective-permute-done.27.refs_2_ = bf16[320,512]{1,0:T(8,128)(2,1)S(1)} collective-permute-done((bf16[320,512]{1,0:T(8,128)(2,1)S(1)}, bf16[320,512]{1,0:T(8,128)(2,1)S(1)}, u32[]{:S(2)}, u32[]{:S(2)}) %collective-permute-start.27) | collective-permute-done | bytes 327712 | tf_op jit(solution)/shard_map/ppermute | solution.py:145
  126.7 1.9 %collective-permute-start.28 = (bf16[160,512]{1,0:T(8,128)(2,1)S(1)}, bf16[160,512]{1,0:T(8,128)(2,1)S(1)}, u32[]{:S(2)}, u32[]{:S(2)}) collective-permute-start(bf16[160,512]{1,0:T(8,128)(2,1)S(1)} %get-tuple-element.150), channel_id=1, source_target_pairs={{0,8},{1,9},{2,10},{3,11},{4,12},{5,13},{6,14},{7,15},{8,0},{9,1},... | collective-permute-start | bytes 491528 | tf_op jit(solution)/shard_map/ppermute | solution.py:145
  130.4 2.5 %collective-permute-start.23 = (bf16[16,512]{1,0:T(8,128)(2,1)S(1)}, bf16[16,512]{1,0:T(8,128)(2,1)S(1)}, u32[]{:S(2)}, u32[]{:S(2)}) collective-permute-start(bf16[16,512]{1,0:T(8,128)(2,1)S(1)} %get-tuple-element.140), channel_id=1, source_target_pairs={{0,4},{4,8},{8,12},{12,0},{1,5},{5,9},{9,13},{13,1},{2,6},{6,10},{... | collective-permute-start | bytes 49160 | tf_op jit(solution)/shard_map/ppermute | solution.py:177
  134.3 1.7 %collective-permute-done.23.refs_4_ = bf16[16,512]{1,0:T(8,128)(2,1)S(1)} collective-permute-done((bf16[16,512]{1,0:T(8,128)(2,1)S(1)}, bf16[16,512]{1,0:T(8,128)(2,1)S(1)}, u32[]{:S(2)}, u32[]{:S(2)}) %collective-permute-start.23) | collective-permute-done | bytes 16416 | tf_op jit(solution)/shard_map/ppermute | solution.py:177
  136.9 1.9 %grid_place.1 = bf16[512,512]{1,0:T(8,128)(2,1)} custom-call(s32[2]{0:T(128)S(1)} %pad_add_fusion.me_ref.refs_0_, bf16[16,512]{1,0:T(8,128)(2,1)S(1)} %collective-permute-done.20.refs_1_, bf16[16,512]{1,0:T(8,128)(2,1)S(1)} %collective-permute-done.21.refs_2_, bf16[16,512]{1,0:T(8,128)(2,1)S(1)} %collective-permute-done.22.refs_3_, ...), custom_call_target="tpu_custom_call" | custom-call | flops 402653184 | bytes 1655168 | tf_op jit(solution)/shard_map/grid_place/pallas_call | solution.py:154
  (190 shorter events, 46.2 us)
Async XLA Ops:
  7.2 74.9 %reduce-scatter.4.cloned.1.call-start = ((), (), s32[]{:S(2)}) async-start(), calls=%async_computation.3 | async-start | bytes 2359296 | tf_op jit(solution)/shard_map/reduce_scatter | solution.py:139
  12.7 15.4 %collective-permute-start = (bf16[24,512]{1,0:T(8,128)(2,1)}, bf16[24,512]{1,0:T(8,128)(2,1)S(1)}, u32[]{:S(2)}, u32[]{:S(2)}) collective-permute-start(bf16[24,512]{1,0:T(8,128)(2,1)} %get-tuple-element.82), channel_id=1, source_target_pairs={{0,1},{1,0},{2,3},{3,2},{4,5},{5,4},{6,7},{7,6},{8,9},{9,8},{10,11... | collective-permute-start | bytes 73736 | tf_op jit(solution)/shard_map/ppermute | solution.py:172
  13.2 15.5 %collective-permute-start.1 = (bf16[24,512]{1,0:T(8,128)(2,1)}, bf16[24,512]{1,0:T(8,128)(2,1)S(1)}, u32[]{:S(2)}, u32[]{:S(2)}) collective-permute-start(bf16[24,512]{1,0:T(8,128)(2,1)} %get-tuple-element.83), channel_id=1, source_target_pairs={{0,2},{1,3},{2,0},{3,1},{4,6},{5,7},{6,4},{7,5},{8,10},{9,11},{10,... | collective-permute-start | bytes 73736 | tf_op jit(solution)/shard_map/ppermute | solution.py:172
  15.7 13.6 %collective-permute-start.2 = (bf16[24,512]{1,0:T(8,128)(2,1)S(1)}, bf16[24,512]{1,0:T(8,128)(2,1)S(1)}, u32[]{:S(2)}, u32[]{:S(2)}) collective-permute-start(bf16[24,512]{1,0:T(8,128)(2,1)S(1)} %get-tuple-element.84), channel_id=1, source_target_pairs={{0,3},{1,2},{2,1},{3,0},{4,7},{5,6},{6,5},{7,4},{8,11},{9,10},{10,... | collective-permute-start | bytes 73736 | tf_op jit(solution)/shard_map/ppermute | solution.py:172
  15.8 14.1 %collective-permute-start.3 = (bf16[24,512]{1,0:T(8,128)(2,1)S(1)}, bf16[24,512]{1,0:T(8,128)(2,1)S(1)}, u32[]{:S(2)}, u32[]{:S(2)}) collective-permute-start(bf16[24,512]{1,0:T(8,128)(2,1)S(1)} %get-tuple-element.85), channel_id=1, source_target_pairs={{0,4},{4,8},{8,12},{12,0},{1,5},{5,9},{9,13},{13,1},{2,6},{6,10},{... | collective-permute-start | bytes 73736 | tf_op jit(solution)/shard_map/ppermute | solution.py:177
  17.6 12.9 %collective-permute-start.4 = (bf16[24,512]{1,0:T(8,128)(2,1)S(1)}, bf16[24,512]{1,0:T(8,128)(2,1)S(1)}, u32[]{:S(2)}, u32[]{:S(2)}) collective-permute-start(bf16[24,512]{1,0:T(8,128)(2,1)S(1)} %get-tuple-element.86), channel_id=1, source_target_pairs={{4,0},{8,4},{12,8},{0,12},{5,1},{9,5},{13,9},{1,13},{6,2},{10,6},{... | collective-permute-start | bytes 73736 | tf_op jit(solution)/shard_map/ppermute | solution.py:176
  36.9 9.0 %collective-permute-start.5 = (bf16[24,512]{1,0:T(8,128)(2,1)S(1)}, bf16[24,512]{1,0:T(8,128)(2,1)S(1)}, u32[]{:S(2)}, u32[]{:S(2)}) collective-permute-start(bf16[24,512]{1,0:T(8,128)(2,1)S(1)} %get-tuple-element.88), channel_id=1, source_target_pairs={{0,1},{1,0},{2,3},{3,2},{4,5},{5,4},{6,7},{7,6},{8,9},{9,8},{10,11... | collective-permute-start | bytes 73736 | tf_op jit(solution)/shard_map/ppermute | solution.py:172
  36.9 9.0 %collective-permute-start.6 = (bf16[24,512]{1,0:T(8,128)(2,1)S(1)}, bf16[24,512]{1,0:T(8,128)(2,1)S(1)}, u32[]{:S(2)}, u32[]{:S(2)}) collective-permute-start(bf16[24,512]{1,0:T(8,128)(2,1)S(1)} %get-tuple-element.89), channel_id=1, source_target_pairs={{0,2},{1,3},{2,0},{3,1},{4,6},{5,7},{6,4},{7,5},{8,10},{9,11},{10,... | collective-permute-start | bytes 73736 | tf_op jit(solution)/shard_map/ppermute | solution.py:172
  38.6 7.3 %collective-permute-start.7 = (bf16[24,512]{1,0:T(8,128)(2,1)S(1)}, bf16[24,512]{1,0:T(8,128)(2,1)S(1)}, u32[]{:S(2)}, u32[]{:S(2)}) collective-permute-start(bf16[24,512]{1,0:T(8,128)(2,1)S(1)} %get-tuple-element.90), channel_id=1, source_target_pairs={{0,3},{1,2},{2,1},{3,0},{4,7},{5,6},{6,5},{7,4},{8,11},{9,10},{10,... | collective-permute-start | bytes 73736 | tf_op jit(solution)/shard_map/ppermute | solution.py:172
  49.4 11.0 %collective-permute-start.10 = (bf16[16,512]{1,0:T(8,128)(2,1)S(1)}, bf16[16,512]{1,0:T(8,128)(2,1)S(1)}, u32[]{:S(2)}, u32[]{:S(2)}) collective-permute-start(bf16[16,512]{1,0:T(8,128)(2,1)S(1)} %get-tuple-element.97), channel_id=1, source_target_pairs={{0,1},{1,0},{2,3},{3,2},{4,5},{5,4},{6,7},{7,6},{8,9},{9,8},{10,11... | collective-permute-start | bytes 49160 | tf_op jit(solution)/shard_map/ppermute | solution.py:172
  49.4 11.0 %collective-permute-start.11 = (bf16[16,512]{1,0:T(8,128)(2,1)S(1)}, bf16[16,512]{1,0:T(8,128)(2,1)S(1)}, u32[]{:S(2)}, u32[]{:S(2)}) collective-permute-start(bf16[16,512]{1,0:T(8,128)(2,1)S(1)} %get-tuple-element.98), channel_id=1, source_target_pairs={{0,2},{1,3},{2,0},{3,1},{4,6},{5,7},{6,4},{7,5},{8,10},{9,11},{10,... | collective-permute-start | bytes 49160 | tf_op jit(solution)/shard_map/ppermute | solution.py:172
  51.1 9.3 %collective-permute-start.12 = (bf16[16,512]{1,0:T(8,128)(2,1)S(1)}, bf16[16,512]{1,0:T(8,128)(2,1)S(1)}, u32[]{:S(2)}, u32[]{:S(2)}) collective-permute-start(bf16[16,512]{1,0:T(8,128)(2,1)S(1)} %get-tuple-element.99), channel_id=1, source_target_pairs={{0,3},{1,2},{2,1},{3,0},{4,7},{5,6},{6,5},{7,4},{8,11},{9,10},{10,... | collective-permute-start | bytes 49160 | tf_op jit(solution)/shard_map/ppermute | solution.py:172
  51.2 9.1 %collective-permute-start.13 = (bf16[16,512]{1,0:T(8,128)(2,1)S(1)}, bf16[16,512]{1,0:T(8,128)(2,1)S(1)}, u32[]{:S(2)}, u32[]{:S(2)}) collective-permute-start(bf16[16,512]{1,0:T(8,128)(2,1)S(1)} %get-tuple-element.100), channel_id=1, source_target_pairs={{0,4},{4,8},{8,12},{12,0},{1,5},{5,9},{9,13},{13,1},{2,6},{6,10},{... | collective-permute-start | bytes 49160 | tf_op jit(solution)/shard_map/ppermute | solution.py:177
  51.3 9.1 %collective-permute-start.14 = (bf16[16,512]{1,0:T(8,128)(2,1)S(1)}, bf16[16,512]{1,0:T(8,128)(2,1)S(1)}, u32[]{:S(2)}, u32[]{:S(2)}) collective-permute-start(bf16[16,512]{1,0:T(8,128)(2,1)S(1)} %get-tuple-element.101), channel_id=1, source_target_pairs={{4,0},{8,4},{12,8},{0,12},{5,1},{9,5},{13,9},{1,13},{6,2},{10,6},{... | collective-permute-start | bytes 49160 | tf_op jit(solution)/shard_map/ppermute | solution.py:176
  65.7 39.0 %reduce-scatter.6.cloned.1.call-start = ((), (), s32[]{:S(2)}) async-start(), calls=%async_computation.4 | async-start | bytes 1179648 | tf_op jit(solution)/shard_map/reduce_scatter | solution.py:139
  65.7 10.6 %collective-permute-start.15 = (bf16[8,512]{1,0:T(8,128)(2,1)}, bf16[8,512]{1,0:T(8,128)(2,1)S(1)}, u32[]{:S(2)}, u32[]{:S(2)}) collective-permute-start(bf16[8,512]{1,0:T(8,128)(2,1)} %copy-done.57), channel_id=1, source_target_pairs={{0,1},{1,0},{2,3},{3,2},{4,5},{5,4},{6,7},{7,6},{8,9},{9,8},{10,11... | collective-permute-start | bytes 24584 | tf_op jit(solution)/shard_map/ppermute | solution.py:172
  65.8 10.6 %collective-permute-start.16 = (bf16[8,512]{1,0:T(8,128)(2,1)}, bf16[8,512]{1,0:T(8,128)(2,1)S(1)}, u32[]{:S(2)}, u32[]{:S(2)}) collective-permute-start(bf16[8,512]{1,0:T(8,128)(2,1)} %copy-done.56), channel_id=1, source_target_pairs={{0,2},{1,3},{2,0},{3,1},{4,6},{5,7},{6,4},{7,5},{8,10},{9,11},{10,... | collective-permute-start | bytes 24584 | tf_op jit(solution)/shard_map/ppermute | solution.py:172
  67.6 8.8 %collective-permute-start.17 = (bf16[8,512]{1,0:T(8,128)(2,1)}, bf16[8,512]{1,0:T(8,128)(2,1)S(1)}, u32[]{:S(2)}, u32[]{:S(2)}) collective-permute-start(bf16[8,512]{1,0:T(8,128)(2,1)} %copy-done.55), channel_id=1, source_target_pairs={{0,3},{1,2},{2,1},{3,0},{4,7},{5,6},{6,5},{7,4},{8,11},{9,10},{10,... | collective-permute-start | bytes 24584 | tf_op jit(solution)/shard_map/ppermute | solution.py:172
  67.7 8.7 %collective-permute-start.18 = (bf16[8,512]{1,0:T(8,128)(2,1)}, bf16[8,512]{1,0:T(8,128)(2,1)S(1)}, u32[]{:S(2)}, u32[]{:S(2)}) collective-permute-start(bf16[8,512]{1,0:T(8,128)(2,1)} %copy-done.54), channel_id=1, source_target_pairs={{0,4},{4,8},{8,12},{12,0},{1,5},{5,9},{9,13},{13,1},{2,6},{6,10},{... | collective-permute-start | bytes 24584 | tf_op jit(solution)/shard_map/ppermute | solution.py:177
  67.7 8.7 %collective-permute-start.19 = (bf16[8,512]{1,0:T(8,128)(2,1)}, bf16[8,512]{1,0:T(8,128)(2,1)S(1)}, u32[]{:S(2)}, u32[]{:S(2)}) collective-permute-start(bf16[8,512]{1,0:T(8,128)(2,1)} %copy-done.53), channel_id=1, source_target_pairs={{4,0},{8,4},{12,8},{0,12},{5,1},{9,5},{13,9},{1,13},{6,2},{10,6},{... | collective-permute-start | bytes 24584 | tf_op jit(solution)/shard_map/ppermute | solution.py:176
  82.1 56.7 %reduce-scatter.8.cloned.1.call-start = ((), (), s32[]{:S(2)}) async-start(), calls=%async_computation.5 | async-start | bytes 491520 | tf_op jit(solution)/shard_map/reduce_scatter | solution.py:139
  88.3 23.2 %collective-permute-start.26 = (bf16[640,512]{1,0:T(8,128)(2,1)}, bf16[640,512]{1,0:T(8,128)(2,1)S(1)}, u32[]{:S(2)}, u32[]{:S(2)}) collective-permute-start(bf16[640,512]{1,0:T(8,128)(2,1)} %get-tuple-element.146), channel_id=1, source_target_pairs={{0,2},{1,3},{2,0},{3,1},{4,6},{5,7},{6,4},{7,5},{8,10},{9,11},{10,... | collective-permute-start | bytes 1966088 | tf_op jit(solution)/shard_map/ppermute | solution.py:145
  112.2 13.9 %collective-permute-start.27 = (bf16[320,512]{1,0:T(8,128)(2,1)S(1)}, bf16[320,512]{1,0:T(8,128)(2,1)S(1)}, u32[]{:S(2)}, u32[]{:S(2)}) collective-permute-start(bf16[320,512]{1,0:T(8,128)(2,1)S(1)} %get-tuple-element.148), channel_id=1, source_target_pairs={{0,4},{1,5},{2,6},{3,7},{4,0},{5,1},{6,2},{7,3},{8,12},{9,13},{10,... | collective-permute-start | bytes 983048 | tf_op jit(solution)/shard_map/ppermute | solution.py:145
  126.7 12.2 %collective-permute-start.28 = (bf16[160,512]{1,0:T(8,128)(2,1)S(1)}, bf16[160,512]{1,0:T(8,128)(2,1)S(1)}, u32[]{:S(2)}, u32[]{:S(2)}) collective-permute-start(bf16[160,512]{1,0:T(8,128)(2,1)S(1)} %get-tuple-element.150), channel_id=1, source_target_pairs={{0,8},{1,9},{2,10},{3,11},{4,12},{5,13},{6,14},{7,15},{8,0},{9,1},... | collective-permute-start | bytes 491528 | tf_op jit(solution)/shard_map/ppermute | solution.py:145
  (68 other events, 217.9 us)
Sparse Core Ops, SparseCore 0:
  65.8 7.4 reduce-scatter.3
  82.3 22.3 reduce-scatter.5
  106.9 24.6 reduce-scatter.7

commit v4 on v3

v4 whole, which is shorter than its diff:
```python
import jax
import jax.numpy as jnp
from jax import lax
from jax.experimental import pallas as pl
from jax.experimental.pallas import tpu as pltpu
from jax.sharding import PartitionSpec as P

BF = jnp.bfloat16
F32 = jnp.float32
I32 = jnp.int32
NN = (((1,), (0,)), ((), ()))
NT = (((1,), (1,)), ((), ()))
TN = (((0,), (0,)), ((), ()))
BORDER = 8
GROUP = ("lon", "lat", "sub")
COLUMN = ("lat", "sub")


def dot(a, b, dims=NN):
    return lax.dot_general(a, b, dims, preferred_element_type=F32)


def low(value):
    return value.astype(BF)


def sigmoid(value):
    return 0.5 * jnp.tanh(0.5 * value) + 0.5


def silu(value):
    return value * sigmoid(value)


def silu_both(value):
    sig = sigmoid(value)
    act = value * sig
    return act, sig + act * (1.0 - sig)


def silu_slope(value):
    return silu_both(value)[1]


def iota(rows, columns, dim):
    return lax.broadcasted_iota(I32, (rows, columns), dim)


def hot(mask):
    return jnp.where(mask, 1.0, 0.0)


def slot_of(at, column, me, odd):
    far = jnp.where(at == column - 1, column + 1 - odd, column + odd)
    return jnp.where(at < column - 1, jnp.bitwise_xor(at + 1, me), far)


def as_column(values, wide, column, me, odd):
    slots = values.shape[0]
    count = (slots - 1) * wide
    row = iota(count, slots, 0)
    pick = low(hot(slot_of(row // wide, column, me, odd) == iota(count, slots, 1)))
    found = 16.0 * dot(pick, low((values // 16).astype(F32)))
    found = found + dot(pick, low((values % 16).astype(F32)))
    keep = iota(count, wide, 0) % wide == iota(count, wide, 1)
    return jnp.sum(jnp.where(keep, found, 0.0), axis=1, keepdims=True).astype(I32)


def as_row(values, wide, column, me, odd):
    slots = values.shape[0]
    count = (slots - 1) * wide
    pick = low(hot(iota(wide, count, 1) % wide == iota(wide, count, 0)))
    found = 16.0 * dot(low((values // 16).astype(F32)), pick)
    found = found + dot(low((values % 16).astype(F32)), pick)
    at = iota(slots, count, 1) // wide
    keep = slot_of(at, column, me, odd) == iota(slots, count, 0)
    return jnp.sum(jnp.where(keep, found, 0.0), axis=0, keepdims=True).astype(I32)


def split_parts(refs, starts, sizes):
    values = [ref[...].astype(F32) for ref in refs]
    return [
        jnp.concatenate([value[start : start + size] for value in values], axis=0)
        for start, size in zip(starts, sizes)
    ]


def store_parts(refs, parts):
    peers = len(refs)
    for at, ref in enumerate(refs):
        rows = []
        for part in parts:
            size = part.shape[0] // peers
            rows.append(part[at * size : (at + 1) * size])
        ref[...] = low(rows[0] if len(rows) == 1 else jnp.concatenate(rows, axis=0))


def receivers(senders_t, halo):
    degree, nodes = senders_t.shape
    found = jnp.zeros((halo, nodes), F32)
    ids = iota(halo, nodes, 0) + nodes
    for j in range(degree):
        found = found + hot(senders_t[j : j + 1, :] == ids)
    return found


def receivers_t(senders, degree, halo):
    nodes = senders.shape[0]
    found = jnp.zeros((nodes, halo), F32)
    ids = iota(nodes, halo, 1) + nodes
    for j in range(degree):
        found = found + hot(senders[:, j : j + 1] == ids)
    return found


def fine(rows, dims):
    return (rows // (dims[0] * dims[1] * dims[2])) % 16 == 0


def reverse_bits(block, bits):
    spot = 0
    for bit in range(bits):
        spot = 2 * spot + (block >> bit) % 2
    return spot


def store_blocks(keep_ref, give_ref, at, count, value, dims, bits_ref):
    value = low(value)
    rows = value.shape[0]
    total = dims[0] * dims[1] * dims[2]
    depth = rows // total
    if not fine(rows, dims):
        keep_ref[at] = value
        return
    bits = (total - 1).bit_length()
    upper = bits_ref[0:1, 2:3] == 1
    for block in range(0, total, 2):
        start = reverse_bits(block, bits) * count * depth + at * depth
        first = value[block * depth : (block + 1) * depth].astype(F32)
        second = value[(block + 1) * depth : (block + 2) * depth].astype(F32)
        keep_ref[start : start + depth, :] = low(jnp.where(upper, second, first))
        give_ref[start : start + depth, :] = low(jnp.where(upper, first, second))


def blocks_shapes(count, rows, width, dims):
    if fine(rows, dims):
        return [jax.ShapeDtypeStruct((count * rows // 2, width), BF)] * 2
    return [jax.ShapeDtypeStruct((count, rows, width), BF), jax.ShapeDtypeStruct((16, width), BF)]


def halve(bit, bits_ref, keep_ref, arr_ref, keep_out, give_out):
    half = keep_ref.shape[0] // 2
    upper = bits_ref[0:1, 2 + bit : 3 + bit] == 1
    first = keep_ref[:half, :].astype(F32) + arr_ref[:half, :].astype(F32)
    second = keep_ref[half:, :].astype(F32) + arr_ref[half:, :].astype(F32)
    keep_out[...] = low(jnp.where(upper, second, first))
    give_out[...] = low(jnp.where(upper, first, second))


def swap(block, bit, dims):
    total = dims[0] * dims[1] * dims[2]
    return lax.ppermute(block, GROUP, [(i, i ^ (1 << bit)) for i in range(total)])


def scatter_halving(keep, give, place, dims):
    width = keep.shape[1]
    bits = (dims[0] * dims[1] * dims[2] - 1).bit_length()
    arrived = swap(give, 0, dims)
    for bit in range(1, bits):
        rows = keep.shape[0] // 2
        keep, give = call(
            lambda *refs: halve(bit, *refs), "halve", [shape(rows, width)] * 2,
            (place, keep, arrived), flops=4 * rows * width,
        )
        arrived = swap(give, bit, dims)
    return keep, arrived


def scatter_plain(blocks, dims):
    lon, lat, sub = dims
    count, rows, width = blocks.shape
    depth = rows // (lon * lat * sub)
    blocks = blocks.reshape(count, lon, lat, sub, depth, width)
    blocks = blocks.transpose(3, 2, 1, 0, 4, 5)
    for axis in ("sub", "lat", "lon"):
        blocks = lax.psum_scatter(blocks, axis, scatter_dimension=0, tiled=False)
    return blocks.astype(F32)


def call(kernel, name, outs, args, flops):
    size = sum(a.size * a.dtype.itemsize for a in (*args, *outs))
    return pl.pallas_call(
        kernel,
        out_shape=list(outs),
        in_specs=[pl.BlockSpec(memory_space=pltpu.VMEM)] * len(args),
        out_specs=[pl.BlockSpec(memory_space=pltpu.VMEM)] * len(outs),
        compiler_params=pltpu.CompilerParams(vmem_limit_bytes=16 * 1024 * 1024),
        cost_estimate=pl.CostEstimate(flops=flops, bytes_accessed=size, transcendentals=0),
        name=name,
    )(*args)


def exchange(parts, dims):
    column = dims[1] * dims[2]
    count = dims[0]
    arrived = [
        lax.ppermute(parts[r - 1], COLUMN, [(i, i ^ r) for i in range(column)])
        for r in range(1, column)
    ]
    near = lax.ppermute(parts[column - 1], "lon", [(i, i ^ 1) for i in range(count)])
    other = [(i, (i - 1 + 2 * (i % 2)) % count) for i in range(count)]
    far = lax.ppermute(parts[column], "lon", other)
    return (*arrived, near, far)


def shape(*dims, dtype=BF):
    return jax.ShapeDtypeStruct(dims, dtype)


def first_payload(column, capacity, ints_ref, grid_ref, sends_ref, *pay_refs):
    chosen = grid_ref.shape[0]
    ints = ints_ref[...]
    base = 2 * capacity + BORDER
    me, odd = ints[0:1, base : base + 1], ints[0:1, base + 1 : base + 2]
    sends = as_column(ints[:, :capacity], capacity, column, me, odd)
    sends_ref[...] = sends
    rows = dot(low(hot(sends == iota(sends.shape[0], chosen, 1))), grid_ref[...])
    store_parts(pay_refs, [rows])


def embed_local(
    column, capacity, ints_ref, senders_ref, grid_ref, weight_ref, target_ref, sends_ref,
    sum_ref, slope_ref, sends_row_ref, incoming_ref, bounds_ref, bounds_row_ref, senders_t_ref,
    senders_out_ref, place_ref,
):
    chosen = grid_ref.shape[0]
    nodes = sum_ref.shape[0]
    taken = sends_ref.shape[0]
    act, slope = silu_both(dot(grid_ref[...], weight_ref[...]))
    slope_ref[...] = low(slope)
    sent = jnp.max(hot(sends_ref[...] == iota(taken, chosen, 1)), axis=0, keepdims=True)
    label = jnp.where(sent > 0.0, nodes, target_ref[...])
    sum_ref[...] = dot(low(hot(label == iota(nodes, chosen, 0))), low(act))
    ints = ints_ref[...]
    base = 2 * capacity + BORDER
    place_ref[...] = ints[:, base:]
    me, odd = ints[0:1, base : base + 1], ints[0:1, base + 1 : base + 2]
    sends, incoming = ints[:, :capacity], ints[:, capacity : 2 * capacity]
    bounds = ints[:, 2 * capacity : base]
    sends_row_ref[...] = as_row(sends, capacity, column, me, odd)
    incoming_ref[...] = as_row(incoming, capacity, column, me, odd)
    bounds_ref[...] = as_column(bounds, BORDER, column, me, odd)
    bounds_row_ref[...] = as_row(bounds, BORDER, column, me, odd)
    senders = senders_ref[...]
    degree = senders.shape[0]
    offset = senders - nodes
    slot = offset // BORDER
    far = jnp.where(slot == column, column - odd, column - 1 + odd)
    at = jnp.where(slot < column, jnp.bitwise_xor(slot, me) - 1, far)
    senders = jnp.where(offset < 0, senders, nodes + at * BORDER + offset % BORDER)
    senders_t_ref[...] = senders
    filler = jnp.zeros((8 - degree, nodes), I32)
    senders_out_ref[...] = jnp.concatenate([senders, filler], axis=0).T


def merge_nodes(peers, *refs):
    arr_refs, refs = refs[:peers], refs[peers:]
    (incoming_ref, embed_ref, local_ref, mesh_ref, weight_ref, bounds_ref, senders_t_ref, cot_ref,
     merged_ref, state_ref, slope_ref, lat_ref, *pay_refs) = refs
    nodes = mesh_ref.shape[0]
    taken = incoming_ref.shape[1]
    halo = peers * BORDER
    lat = jnp.concatenate([ref[...] for ref in arr_refs], axis=0)
    lat_ref[...] = lat
    act, slope = silu_both(dot(lat, embed_ref[...]))
    slope_ref[...] = low(slope)
    place = low(hot(incoming_ref[...] == iota(nodes, taken, 0)))
    merged = low(local_ref[...] + dot(place, low(act)))
    merged_ref[...] = merged
    state = low(mesh_ref[...].astype(F32) + dot(merged, weight_ref[...]))
    state_ref[...] = state
    border = low(hot(bounds_ref[...] == iota(halo, nodes, 1)))
    back = low(receivers(senders_t_ref[...], halo))
    store_parts(
        pay_refs,
        [dot(border, state), dot(back, state), dot(border, merged), dot(back, cot_ref[...])],
    )


def local_edges(senders, degree, sent, recv, each):
    nodes = senders.shape[0]
    total = jnp.zeros(recv.shape, F32)
    ids = iota(nodes, nodes, 1)
    for j in range(degree):
        named = senders[:, j : j + 1]
        act, slope = silu_both(dot(low(hot(named == ids)), sent) + recv)
        keep = hot(named < nodes)
        total = total + act * keep
        each(j, slope * keep)
    return total


def forward_local(
    state_ref, send_ref, recv_ref, senders_ref, senders_t_ref, bounds_ref,
    total_ref, slope_ref, recv_n_ref, sent_b_ref,
):
    state = state_ref[...]
    nodes = state.shape[0]
    halo = bounds_ref.shape[0]
    sent = low(dot(state, send_ref[0]))
    recv = dot(state, recv_ref[0])

    def keep(j, slope):
        slope_ref[j] = low(slope)

    total_ref[...] = local_edges(senders_ref[...], senders_t_ref.shape[0], sent, recv, keep)
    back = low(receivers(senders_t_ref[...], halo))
    recv_n_ref[...] = dot(low(dot(back, state)), recv_ref[0])
    sent_b_ref[...] = low(dot(low(hot(bounds_ref[...] == iota(halo, nodes, 1))), sent))


def forward_halo(peers, *refs):
    arr_refs, refs = refs[:peers], refs[peers:]
    (recv_n_ref, total_ref, state_ref, send_ref, update_ref, senders_ref, senders_t_ref,
     bounds_ref, summed_ref, out_ref, pre_ref, rows_ref, back_ref, merged_ref, cot_ref,
     *pay_refs) = refs
    nodes = state_ref.shape[0]
    degree = senders_t_ref.shape[0]
    halo = peers * BORDER
    rows, back, merged, cot = split_parts(
        arr_refs, (0, BORDER, 2 * BORDER, 3 * BORDER), (BORDER,) * 4
    )
    rows_ref[...], back_ref[...] = low(rows), low(back)
    merged_ref[...], cot_ref[...] = low(merged), low(cot)
    pre = low(dot(low(rows), send_ref[0])).astype(F32) + recv_n_ref[...]
    pre_ref[...] = pre
    place = low(receivers_t(senders_ref[...], degree, halo))
    summed = low(total_ref[...] + dot(place, low(silu(pre))))
    summed_ref[...] = summed
    state = low(state_ref[...].astype(F32) + dot(summed, update_ref[0]))
    out_ref[...] = state
    border = low(hot(bounds_ref[...] == iota(halo, nodes, 1)))
    back = low(receivers(senders_t_ref[...], halo))
    store_parts(pay_refs, [dot(border, state), dot(back, state)])


def turn_local(
    state_ref, send_ref, recv_ref, update_ref, cot_ref, cot_r_ref, pre_ref, back0_ref,
    sent_b0_ref, senders_ref, senders_t_ref, bounds_ref,
    total_ref, grecv_ref, gsent_ref, recv_n_ref, sent_b_ref, gsum_n_ref, gsum_r_ref,
    slope_k_ref, slope_r_ref,
):
    halo = bounds_ref.shape[0]
    slope_k_ref[...] = low(silu_slope(pre_ref[...]))
    pre = sent_b0_ref[...].astype(F32) + dot(back0_ref[...], recv_ref[0])
    slope_r_ref[...] = low(silu_slope(pre))
    state = state_ref[...]
    nodes = state.shape[0]
    sent = low(dot(state, send_ref[1]))
    recv = dot(state, recv_ref[1])
    gsum = low(dot(cot_ref[...], update_ref[1], NT))
    grad = gsum.astype(F32)
    grecv_ref[...] = jnp.zeros(grecv_ref.shape, F32)
    gsent_ref[...] = jnp.zeros(gsent_ref.shape, F32)

    def back_edge(j, slope):
        gpre = grad * slope
        grecv_ref[...] += gpre
        target = low(hot(senders_t_ref[j : j + 1, :] == iota(nodes, nodes, 0)))
        gsent_ref[...] += dot(target, low(gpre))

    degree = senders_t_ref.shape[0]
    total_ref[...] = local_edges(senders_ref[...], degree, sent, recv, back_edge)
    back = low(receivers(senders_t_ref[...], halo))
    recv_n_ref[...] = dot(low(dot(back, state)), recv_ref[1])
    sent_b_ref[...] = low(dot(low(hot(bounds_ref[...] == iota(halo, nodes, 1))), sent))
    gsum_n_ref[...] = low(dot(back, gsum))
    gsum_r_ref[...] = low(dot(cot_r_ref[...], update_ref[1], NT))


def turn_halo(peers, *refs):
    arr_refs, refs = refs[:peers], refs[peers:]
    (recv_n_ref, sent_b_ref, gsum_n_ref, gsum_r_ref, total_ref, grecv_ref, gsent_ref, cot_ref,
     send_ref, recv_ref, senders_ref, senders_t_ref, bounds_ref, summed_ref, grecv_out_ref,
     gsent_out_ref, gin_ref, *pay_refs) = refs
    nodes = cot_ref.shape[0]
    degree = senders_t_ref.shape[0]
    halo = peers * BORDER
    rows, back = split_parts(arr_refs, (0, BORDER), (BORDER,) * 2)
    pre = low(dot(low(rows), send_ref[1])).astype(F32) + recv_n_ref[...]
    act, slope = silu_both(pre)
    place = low(receivers_t(senders_ref[...], degree, halo))
    gpre = low(gsum_n_ref[...].astype(F32) * slope)
    grecv = low(grecv_ref[...] + dot(place, gpre))
    pre = sent_b_ref[...].astype(F32) + dot(low(back), recv_ref[1])
    gpre = low(gsum_r_ref[...].astype(F32) * silu_slope(pre))
    border = low(hot(bounds_ref[...] == iota(nodes, halo, 0)))
    gsent = low(gsent_ref[...] + dot(border, gpre))
    gin = cot_ref[...].astype(F32) + dot(grecv, recv_ref[1], NT) + dot(gsent, send_ref[1], NT)
    gin = low(gin)
    gin_ref[...] = gin
    store_parts(pay_refs, [dot(low(receivers(senders_t_ref[...], halo)), gin)])
    summed_ref[...] = low(total_ref[...] + dot(place, low(act)))
    grecv_out_ref[...] = grecv
    gsent_out_ref[...] = gsent


def last_weights(
    dims, place_ref, state_ref, summed_ref, cot_ref, grecv_ref, gsent_ref, update_ref,
    keep_ref, give_ref, mesh_ref,
):
    state, summed = state_ref[...], summed_ref[...]

    def store(at, value):
        store_blocks(keep_ref, give_ref, at, 3, value, dims, place_ref)

    store(0, dot(state, gsent_ref[...], TN))
    store(1, dot(state, grecv_ref[...], TN))
    store(2, dot(summed, cot_ref[...], TN))
    mesh_ref[...] = low(state.astype(F32) + dot(summed, update_ref[1]))


def back_local(
    dims, place_ref, gin_ref, slope_ref, slope_k_ref, send_ref, recv_ref, update_ref, senders_ref,
    senders_t_ref, state_ref, rows_ref, summed_ref, merged_ref, merged_r_ref,
    part_ref, keep_ref, give_ref,
):
    nodes = gin_ref.shape[0]
    halo = slope_k_ref.shape[0]
    degree = senders_t_ref.shape[0]
    gin = gin_ref[...]
    gsum = low(dot(gin, update_ref[0], NT))
    grad = gsum.astype(F32)
    place = low(receivers_t(senders_ref[...], degree, halo))
    back = low(receivers(senders_t_ref[...], halo))
    gpre_k = low(dot(back, gsum) * slope_k_ref[...].astype(F32))
    grecv = dot(place, gpre_k)
    gsent = jnp.zeros(grad.shape, F32)
    for j in range(degree):
        gpre = grad * slope_ref[j].astype(F32)
        grecv = grecv + gpre
        target = low(hot(senders_t_ref[j : j + 1, :] == iota(nodes, nodes, 0)))
        gsent = gsent + dot(target, low(gpre))
    grecv, gsent = low(grecv), low(gsent)
    part = gin.astype(F32) + dot(grecv, recv_ref[0], NT) + dot(gsent, send_ref[0], NT)
    part_ref[...] = part
    state = state_ref[...]

    def store(at, value):
        store_blocks(keep_ref, give_ref, at, 4, value, dims, place_ref)

    store(0, dot(state, gsent, TN) + dot(rows_ref[...], gpre_k, TN))
    store(1, dot(state, grecv, TN))
    store(2, dot(summed_ref[...], gin, TN))
    far = low(dot(gpre_k, send_ref[0], NT))
    store(3, dot(merged_ref[...], low(part), TN) + dot(merged_r_ref[...], far, TN))


def embed_back(peers, dims, *refs):
    arr_refs, refs = refs[:peers], refs[peers:]
    (place_ref, slope_r_ref, part_ref, update_ref, send_ref, merge_ref, bounds_ref, target_ref,
     sends_ref, incoming_ref, slope_g_ref, slope_a_ref, grid_ref, lat_ref, embed_ref,
     gpre_ref, keep_ref, give_ref, *pay_refs) = refs
    nodes = part_ref.shape[0]
    halo = peers * BORDER
    chosen = grid_ref.shape[0]
    taken = sends_ref.shape[0]
    (arrived,) = split_parts(arr_refs, (0,), (BORDER,))
    gsum = low(dot(low(arrived), update_ref[0], NT)).astype(F32)
    gpre = low(gsum * slope_r_ref[...].astype(F32))
    border = low(hot(bounds_ref[...] == iota(nodes, halo, 0)))
    gsent = low(dot(border, gpre))
    gin = low(part_ref[...] + dot(gsent, send_ref[0], NT))
    gmerged = low(dot(gin, merge_ref[...], NT))
    place = low(hot(incoming_ref[...] == iota(nodes, taken, 0)))
    gpre_a = low(dot(place, gmerged, TN) * slope_a_ref[...].astype(F32))
    sent = jnp.max(hot(sends_ref[...] == iota(taken, chosen, 1)), axis=0, keepdims=True)
    label = jnp.where(sent > 0.0, nodes, target_ref[...])
    pick = low(hot(label == iota(nodes, chosen, 0)))
    gpre_g = low(dot(pick, gmerged, TN) * slope_g_ref[...].astype(F32))
    gpre_ref[...] = gpre_g
    grad = dot(grid_ref[...], gpre_g, TN) + dot(lat_ref[...], gpre_a, TN)
    store_blocks(keep_ref, give_ref, 0, 1, grad, dims, place_ref)
    store_parts(pay_refs, [dot(gpre_a, embed_ref[...], NT)])


def grid_place(peers, *refs):
    arr_refs, refs = refs[:peers], refs[peers:]
    gpre_ref, weight_ref, sends_ref, out_ref = refs
    chosen = gpre_ref.shape[0]
    taken = sends_ref.shape[1]
    local = dot(gpre_ref[...], weight_ref[...], NT)
    place = low(hot(sends_ref[...] == iota(chosen, taken, 0)))
    rows = jnp.concatenate([ref[...] for ref in arr_refs], axis=0)
    out_ref[...] = low(local + dot(place, rows))


def finish(
    keep1_ref, arr1_ref, keep0_ref, arr0_ref, keep_e_ref, arr_e_ref,
    embed_ref, merge_ref, send_ref, recv_ref, update_ref,
):
    last = keep1_ref[...].astype(F32) + arr1_ref[...].astype(F32)
    first = keep0_ref[...].astype(F32) + arr0_ref[...].astype(F32)
    embed_ref[...] = keep_e_ref[...].astype(F32) + arr_e_ref[...].astype(F32)
    depth = embed_ref.shape[0]
    for at, ref in enumerate((send_ref, recv_ref, update_ref)):
        ref[0] = first[at * depth : (at + 1) * depth]
        ref[1] = last[at * depth : (at + 1) * depth]
    merge_ref[...] = first[3 * depth :]


def body(
    dims,
    grid_latent, mesh_latent, cotangent, embed_weight, merge_weight, send_weight, recv_weight,
    update_weight, target_row, send_rows, incoming_rows, border_mesh_rows, mesh_senders,
):
    chosen, width = grid_latent.shape
    nodes, degree = mesh_senders.shape
    slots, capacity = send_rows.shape[1:]
    column = dims[1] * dims[2]
    peers = slots - 1
    halo = peers * BORDER
    taken = peers * capacity
    total = dims[0] * dims[1] * dims[2]
    bits = (total - 1).bit_length()
    spot = lax.axis_index(GROUP)
    place = [lax.axis_index(COLUMN), lax.axis_index("lon") % 2]
    place += [(spot >> bit) % 2 for bit in range(bits)]
    place = jnp.broadcast_to(jnp.stack(place).astype(I32)[None], (slots, 2 + bits))
    ints = jnp.concatenate([send_rows[0], incoming_rows[0], border_mesh_rows[0], place], axis=1)
    targets = target_row.reshape(1, chosen)
    unit = 2 * nodes * width * width

    sends, *pay1 = call(
        lambda *refs: first_payload(column, capacity, *refs), "first_payload",
        [shape(taken, 1, dtype=I32)] + [shape(capacity, width)] * peers,
        (ints, grid_latent), flops=unit // 2,
    )
    arr1 = exchange(pay1, dims)
    (local, slope_g, sends_row, incoming, bounds, bounds_row, senders_t, senders, place) = call(
        lambda *refs: embed_local(column, capacity, *refs), "embed_local",
        [shape(nodes, width, dtype=F32), shape(chosen, width), shape(1, taken, dtype=I32),
         shape(1, taken, dtype=I32), shape(halo, 1, dtype=I32), shape(1, halo, dtype=I32),
         shape(degree, nodes, dtype=I32), shape(nodes, 8, dtype=I32),
         shape(slots, 2 + bits, dtype=I32)],
        (ints, mesh_senders.T, grid_latent, embed_weight, targets, sends), flops=3 * unit,
    )
    merged, state0, slope_a, lat_a, *pay2 = call(
        lambda *refs: merge_nodes(peers, *refs), "merge_nodes",
        [shape(nodes, width), shape(nodes, width), shape(taken, width), shape(taken, width)]
        + [shape(4 * BORDER, width)] * peers,
        (*arr1, incoming, embed_weight, local, mesh_latent, merge_weight, bounds, senders_t,
         cotangent),
        flops=2 * unit,
    )
    arr2 = exchange(pay2, dims)
    total0, slope0, recv_n0, sent_b0 = call(
        forward_local, "forward_local",
        [shape(nodes, width, dtype=F32), shape(degree, nodes, width),
         shape(halo, width, dtype=F32), shape(halo, width)],
        (state0, send_weight, recv_weight, senders, senders_t, bounds), flops=6 * unit,
    )
    summed0, state1, pre0, rows0, back0, merged_r, cot_r, *pay3 = call(
        lambda *refs: forward_halo(peers, *refs), "forward_halo",
        [shape(nodes, width), shape(nodes, width), shape(halo, width, dtype=F32)]
        + [shape(halo, width)] * 4 + [shape(2 * BORDER, width)] * peers,
        (*arr2, recv_n0, total0, state0, send_weight, update_weight, senders, senders_t, bounds),
        flops=2 * unit,
    )
    arr3 = exchange(pay3, dims)
    (total1, grecv_l, gsent_l, recv_n1, sent_b1, gsum_n1, gsum_r1, slope_k0, slope_r0) = call(
        turn_local, "turn_local",
        [shape(nodes, width, dtype=F32)] * 3 + [shape(halo, width, dtype=F32)]
        + [shape(halo, width)] * 5,
        (state1, send_weight, recv_weight, update_weight, cotangent, cot_r, pre0, back0, sent_b0,
         senders, senders_t, bounds),
        flops=10 * unit,
    )
    summed1, grecv1, gsent1, gin1, *pay4 = call(
        lambda *refs: turn_halo(peers, *refs), "turn_halo",
        [shape(nodes, width)] * 4 + [shape(BORDER, width)] * peers,
        (*arr3, recv_n1, sent_b1, gsum_n1, gsum_r1, total1, grecv_l, gsent_l, cotangent,
         send_weight, recv_weight, senders, senders_t, bounds_row),
        flops=3 * unit,
    )
    arr4 = exchange(pay4, dims)
    keep1, give1, mesh_out = call(
        lambda *refs: last_weights(dims, *refs), "last_weights",
        blocks_shapes(3, width, width, dims) + [shape(nodes, width)],
        (place, state1, summed1, cotangent, grecv1, gsent1, update_weight), flops=4 * unit,
    )
    part0, keep0, give0 = call(
        lambda *refs: back_local(dims, *refs), "back_local",
        [shape(nodes, width, dtype=F32)] + blocks_shapes(4, width, width, dims),
        (place, gin1, slope0, slope_k0, send_weight, recv_weight, update_weight, senders,
         senders_t, state0, rows0, summed0, merged, merged_r),
        flops=10 * unit,
    )
    gpre_g, keep_e, give_e, *pay5 = call(
        lambda *refs: embed_back(peers, dims, *refs), "embed_back",
        [shape(chosen, width)] + blocks_shapes(1, width, width, dims)
        + [shape(capacity, width)] * peers,
        (*arr4, place, slope_r0, part0, update_weight, send_weight, merge_weight, bounds_row,
         targets, sends, incoming, slope_g, slope_a, grid_latent, lat_a, embed_weight),
        flops=6 * unit,
    )
    arr5 = exchange(pay5, dims)
    (grid_grad,) = call(
        lambda *refs: grid_place(peers, *refs), "grid_place", [shape(chosen, width)],
        (*arr5, gpre_g, embed_weight, sends_row), flops=3 * unit,
    )
    depth = width // total
    if not fine(width, dims):
        last, first, embed = (scatter_plain(blocks, dims) for blocks in (keep1, keep0, keep_e))
        grads = [jnp.stack([first[i], last[i]]) for i in range(3)]
        return (mesh_out, grid_grad, embed[0], first[3], *grads)
    grads = call(
        finish, "finish",
        [shape(depth, width, dtype=F32)] * 2 + [shape(2, depth, width, dtype=F32)] * 3,
        (*scatter_halving(keep1, give1, place, dims), *scatter_halving(keep0, give0, place, dims),
         *scatter_halving(keep_e, give_e, place, dims)),
        flops=8 * depth * width,
    )
    return (mesh_out, grid_grad, *grads)


def solution(mesh):
    split = ("groups", "lon", "lat", "sub")
    dims = tuple(mesh.shape[axis] for axis in GROUP)
    rows = P(split, None)
    whole = P("groups", GROUP, None)
    in_specs = (
        rows, rows, rows, P(), P(), P(), P(), P(), P(split), P(split, None, None),
        P(split, None, None), P(split, None, None), rows,
    )
    out_specs = (rows, rows, rows, rows, whole, whole, whole)
    return jax.shard_map(
        lambda *args: body(dims, *args),
        mesh=mesh, in_specs=in_specs, out_specs=out_specs, check_vma=False,
    )
```

time: 148 us -> 103 us (0.70)
  local copies, waits for them, and re-layouts: 29.5 us -> 7.98 us
  between operations: 14.4 us -> 1.06 us
  Pallas kernels: 26.3 us -> 21.3 us
  waiting for transfers between devices: 40.7 us -> 36.2 us
  other arithmetic: 2.17 us -> 0.08 us
  starting transfers between devices: 33.9 us -> 35.6 us
    ppermute x15, waiting for transfers between devices: 0.04 us -> 18.9 us  [exchange(): lax.ppermute(parts[r - 1], COLUMN, [(i, i ^ r) for i in range(column)])]
    unnamed x121 -> x32, local copies, waits for them, and re-layouts: 25 us -> 7.82 us
    ppermute x4 -> x12, waiting for transfers between devices: 23.4 us -> 7.94 us  [swap(): return lax.ppermute(block, GROUP, [(i, i ^ 1 << bit) for i in range(total)])]
    reduce_scatter x3 -> x0, waiting for transfers between devices: 14.7 us -> none  [scatter_offload(): blocks = lax.psum_scatter(blocks, axis, scatter_dimension=0, tiled=False)]
    ppermute x10, waiting for transfers between devices: 2.6 us -> 9.27 us  [the longest x5 9.26 us: exchange(): far = lax.ppermute(parts[column], 'lon', other)]
    ppermute x4 -> x12, starting transfers between devices: 4.05 us -> 9.43 us  [swap(): return lax.ppermute(block, GROUP, [(i, i ^ 1 << bit) for i in range(total)])]
    pallas_call x15 -> x21, Pallas kernels: 26.3 us -> 21.3 us  [call(): pl.pallas_call(kernel, out_shape=list(outs), in_specs=[pl.BlockSpec(memor...]
    ppermute x10, starting transfers between devices: 19.1 us -> 14.8 us  [the longest x5 9.44 us: exchange(): far = lax.ppermute(parts[column], 'lon', other)]
  transfers between devices with their start and end apart: 32 -> 37, of which waited for: 6 -> 8; matrix products, arithmetic and copies ran while one was open for 5% -> 0% of each run, Pallas kernels for 12% -> 14%
where the time goes in v4:
time: 103 us; the launch traced here: 102 us
  waiting for transfers between devices  36.2 us (35%)
  starting transfers between devices  35.6 us (35%)
  Pallas kernels  21.3 us (21%)
  local copies, waits for them, and re-layouts  7.98 us (8%)
  between operations  1.06 us (1%)
    pallas_call x21, Pallas kernels, call(): pl.pallas_call(kernel, out_shape=list(outs), in_specs=[pl.BlockSpec(memor...  21.3 us
    ppermute x15, waiting for transfers between devices, exchange(): lax.ppermute(parts[r - 1], COLUMN, [(i, i ^ r) for i in range(column)])  18.9 us
    ppermute x15, starting transfers between devices, exchange(): lax.ppermute(parts[r - 1], COLUMN, [(i, i ^ r) for i in range(column)])  11.3 us
    ppermute x5, starting transfers between devices, exchange(): far = lax.ppermute(parts[column], 'lon', other)  9.44 us
    ppermute x12, starting transfers between devices, swap(): return lax.ppermute(block, GROUP, [(i, i ^ 1 << bit) for i in range(total)])  9.43 us
    ppermute x5, waiting for transfers between devices, exchange(): far = lax.ppermute(parts[column], 'lon', other)  9.26 us
    ppermute x12, waiting for transfers between devices, swap(): return lax.ppermute(block, GROUP, [(i, i ^ 1 << bit) for i in range(total)])  7.94 us
    unnamed x32, local copies, waits for them, and re-layouts  7.82 us
  transfers between devices with their start and end apart: 37, of which 8 were waited for; matrix products, arithmetic and copies ran while one was open for 0% of the time, Pallas kernels for 14%

profile of v4, /device:TPU:0, one launch (start us, length us, event | category | flops | bytes accessed | tf_op | source)
XLA Modules:
  0.0 102.2 jit_solution(6804044209572907214)
XLA Ops:
  4.4 2.6 %collective-permute-start.1 = (bf16[16,512]{1,0:T(8,128)(2,1)S(1)}, bf16[16,512]{1,0:T(8,128)(2,1)S(1)}, u32[]{:S(2)}, u32[]{:S(2)}) collective-permute-start(bf16[16,512]{1,0:T(8,128)(2,1)S(1)} %get-tuple-element.105), channel_id=1, source_target_pairs={{0,2},{1,3},{2,0},{3,1},{4,6},{5,7},{6,4},{7,5},{8,10},{9,11},{10,... | collective-permute-start | bytes 49160 | tf_op jit(solution)/shard_map/ppermute | solution.py:207
  7.0 1.8 %collective-permute-start.3 = (bf16[16,512]{1,0:T(8,128)(2,1)S(1)}, bf16[16,512]{1,0:T(8,128)(2,1)S(1)}, u32[]{:S(2)}, u32[]{:S(2)}) collective-permute-start(bf16[16,512]{1,0:T(8,128)(2,1)S(1)} %get-tuple-element.107), channel_id=1, source_target_pairs={{0,4},{4,0},{8,12},{12,8},{1,5},{5,1},{9,13},{13,9},{2,6},{6,2},{1... | collective-permute-start | bytes 49160 | tf_op jit(solution)/shard_map/ppermute | solution.py:210
  8.8 2.5 %collective-permute-start.4 = (bf16[16,512]{1,0:T(8,128)(2,1)S(1)}, bf16[16,512]{1,0:T(8,128)(2,1)S(1)}, u32[]{:S(2)}, u32[]{:S(2)}) collective-permute-start(bf16[16,512]{1,0:T(8,128)(2,1)S(1)} %get-tuple-element.108), channel_id=1, source_target_pairs={{0,12},{4,8},{8,4},{12,0},{1,13},{5,9},{9,5},{13,1},{2,14},{6,10},... | collective-permute-start | bytes 49160 | tf_op jit(solution)/shard_map/ppermute | solution.py:212
  18.8 1.6 %collective-permute-start.6 = (bf16[32,512]{1,0:T(8,128)(2,1)S(1)}, bf16[32,512]{1,0:T(8,128)(2,1)S(1)}, u32[]{:S(2)}, u32[]{:S(2)}) collective-permute-start(bf16[32,512]{1,0:T(8,128)(2,1)S(1)} %get-tuple-element.114), channel_id=1, source_target_pairs={{0,2},{1,3},{2,0},{3,1},{4,6},{5,7},{6,4},{7,5},{8,10},{9,11},{10,... | collective-permute-start | bytes 98312 | tf_op jit(solution)/shard_map/ppermute | solution.py:207
  22.6 2.2 %forward_local.1 = (f32[256,512]{1,0:T(8,128)S(1)}, bf16[6,256,512]{2,1,0:T(8,128)(2,1)S(1)}, f32[40,512]{1,0:T(8,128)S(1)}, bf16[40,512]{1,0:T(8,128)(2,1)S(1)}) custom-call(bf16[256,512]{1,0:T(8,128)(2,1)S(1)} %get-tuple-element.118.state_ref.refs_7_.refs_9_, bf16[2,512,512]{2,1,0:T(8,128)(2,1)S(1)} %copy-done, bf16[2,512,512]{2,1,0:T(8,128)(2,1)S(1)} %copy-done.4, ...), custom_call_target="tpu_custom_call" | custom-call | flops 805306368 | bytes 4593824 | tf_op jit(solution)/shard_map/forward_local/pallas_call | solution.py:192
  24.9 2.2 %collective-permute-done.9.refs_4_ = bf16[32,512]{1,0:T(8,128)(2,1)S(1)} collective-permute-done((bf16[32,512]{1,0:T(8,128)(2,1)S(1)}, bf16[32,512]{1,0:T(8,128)(2,1)S(1)}, u32[]{:S(2)}, u32[]{:S(2)}) %collective-permute-start.9) | collective-permute-done | bytes 32800 | tf_op jit(solution)/shard_map/ppermute | solution.py:212
  28.0 1.6 %collective-permute-start.11 = (bf16[16,512]{1,0:T(8,128)(2,1)S(1)}, bf16[16,512]{1,0:T(8,128)(2,1)S(1)}, u32[]{:S(2)}, u32[]{:S(2)}) collective-permute-start(bf16[16,512]{1,0:T(8,128)(2,1)S(1)} %get-tuple-element.124), channel_id=1, source_target_pairs={{0,2},{1,3},{2,0},{3,1},{4,6},{5,7},{6,4},{7,5},{8,10},{9,11},{10,... | collective-permute-start | bytes 49160 | tf_op jit(solution)/shard_map/ppermute | solution.py:207
  29.9 2.0 %collective-permute-start.14 = (bf16[16,512]{1,0:T(8,128)(2,1)S(1)}, bf16[16,512]{1,0:T(8,128)(2,1)S(1)}, u32[]{:S(2)}, u32[]{:S(2)}) collective-permute-start(bf16[16,512]{1,0:T(8,128)(2,1)S(1)} %get-tuple-element.127), channel_id=1, source_target_pairs={{0,12},{4,8},{8,4},{12,0},{1,13},{5,9},{9,5},{13,1},{2,14},{6,10},... | collective-permute-start | bytes 49160 | tf_op jit(solution)/shard_map/ppermute | solution.py:212
  31.9 4.0 %turn_local.1 = (f32[256,512]{1,0:T(8,128)S(1)}, f32[256,512]{1,0:T(8,128)S(1)}, f32[256,512]{1,0:T(8,128)S(1)}, f32[40,512]{1,0:T(8,128)S(1)}, bf16[40,512]{1,0...) custom-call(bf16[256,512]{1,0:T(8,128)(2,1)S(1)} %get-tuple-element., ...), custom_call_target="tpu_custom_call" | custom-call | flops 1342177280 | bytes 5748896 | tf_op jit(solution)/shard_map/turn_local/pallas_call | solution.py:192
  37.3 2.7 %back_local.1 = (f32[256,512]{1,0:T(8,128)S(1)}, bf16[1024,512]{1,0:T(8,128)(2,1)S(1)}, bf16[1024,512]{1,0:T(8,128)(2,1)S(1)}) custom-call(s32[6,6]{1,0:T(8,128)S(1)} %get-tuple-element.103.refs_0_.refs_5_, bf16[256,512]{1,0:T(8,128)(2,1)S(1)} %get-tuple-element.150.refs_1_, bf16[6,256,512]{2,1,0:T(8,128)(2,1)S(1)} %get-tuple-element.151.refs_2_, ...), custom_call_target="tpu_custom_call" | custom-call | flops 1342177280 | bytes 8525968 | tf_op jit(solution)/shard_map/back_local/pallas_call | solution.py:192
  40.1 1.7 %last_weights.1 = (bf16[768,512]{1,0:T(8,128)(2,1)S(1)}, bf16[768,512]{1,0:T(8,128)(2,1)S(1)}, bf16[256,512]{1,0:T(8,128)(2,1)}) custom-call(s32[6,6]{1,0:T(8,128)S(1)} %get-tuple-element.103.refs_0_.refs_5_, bf16[256,512]{1,0:T(8,128)(2,1)S(1)} %get-tuple-element.122.state_ref.refs_1_, bf16[256,512]{1,0:T(8,128)(2,1)S(1)} %get-tuple-element.140.refs_2_, ...), custom_call_target="tpu_custom_call" | custom-call | flops 536870912 | bytes 4194448 | tf_op jit(solution)/shard_map/last_weights/pallas_call | solution.py:192
  43.3 1.5 %collective-permute-start.30 = (bf16[512,512]{1,0:T(8,128)(2,1)S(1)}, bf16[512,512]{1,0:T(8,128)(2,1)S(1)}, u32[]{:S(2)}, u32[]{:S(2)}) collective-permute-start(bf16[512,512]{1,0:T(8,128)(2,1)S(1)} %get-tuple-element.179), channel_id=1, source_target_pairs={{0,2},{1,3},{2,0},{3,1},{4,6},{5,7},{6,4},{7,5},{8,10},{9,11},{10,... | collective-permute-start | bytes 1572872 | tf_op jit(solution)/shard_map/ppermute | solution.py:162
  48.5 17.5 %collective-permute-done.16.refs_1_ = bf16[8,512]{1,0:T(8,128)(2,1)S(1)} collective-permute-done((bf16[8,512]{1,0:T(8,128)(2,1)S(1)}, bf16[8,512]{1,0:T(8,128)(2,1)S(1)}, u32[]{:S(2)}, u32[]{:S(2)}) %collective-permute-start.16) | collective-permute-done | bytes 8224 | tf_op jit(solution)/shard_map/ppermute | solution.py:207
  66.0 1.8 %collective-permute-start.19 = (bf16[8,512]{1,0:T(8,128)(2,1)S(1)}, bf16[8,512]{1,0:T(8,128)(2,1)S(1)}, u32[]{:S(2)}, u32[]{:S(2)}) collective-permute-start(bf16[8,512]{1,0:T(8,128)(2,1)S(1)} %get-tuple-element.148), channel_id=1, source_target_pairs={{0,12},{4,8},{8,4},{12,0},{1,13},{5,9},{9,5},{13,1},{2,14},{6,10},... | collective-permute-start | bytes 24584 | tf_op jit(solution)/shard_map/ppermute | solution.py:212
  67.9 3.6 %collective-permute-done.19.refs_4_ = bf16[8,512]{1,0:T(8,128)(2,1)S(1)} collective-permute-done((bf16[8,512]{1,0:T(8,128)(2,1)S(1)}, bf16[8,512]{1,0:T(8,128)(2,1)S(1)}, u32[]{:S(2)}, u32[]{:S(2)}) %collective-permute-start.19) | collective-permute-done | bytes 8224 | tf_op jit(solution)/shard_map/ppermute | solution.py:212
  71.5 1.7 %embed_back.1 = (bf16[512,512]{1,0:T(8,128)(2,1)S(1)}, bf16[256,512]{1,0:T(8,128)(2,1)S(1)}, bf16[256,512]{1,0:T(8,128)(2,1)S(1)}, bf16[16,512]{1,0:T(8,128)(2,1...) custom-call(bf16[8,512]{1,0:T(8,128)(2,1)S(1)} %collective-permute-d, ...), custom_call_target="tpu_custom_call" | custom-call | flops 805306368 | bytes 6097840 | tf_op jit(solution)/shard_map/embed_back/pallas_call | solution.py:192
  73.9 2.1 %collective-permute-start.27 = (bf16[192,512]{1,0:T(8,128)(2,1)S(1)}, bf16[192,512]{1,0:T(8,128)(2,1)S(1)}, u32[]{:S(2)}, u32[]{:S(2)}) collective-permute-start(bf16[192,512]{1,0:T(8,128)(2,1)S(1)} %get-tuple-element.173), channel_id=1, source_target_pairs={{0,4},{1,5},{2,6},{3,7},{4,0},{5,1},{6,2},{7,3},{8,12},{9,13},{10,... | collective-permute-start | bytes 589832 | tf_op jit(solution)/shard_map/ppermute | solution.py:162
  77.7 5.1 %collective-permute-done.31.refs_2_ = bf16[256,512]{1,0:T(8,128)(2,1)S(1)} collective-permute-done((bf16[256,512]{1,0:T(8,128)(2,1)S(1)}, bf16[256,512]{1,0:T(8,128)(2,1)S(1)}, u32[]{:S(2)}, u32[]{:S(2)}) %collective-permute-start.31) | collective-permute-done | bytes 262176 | tf_op jit(solution)/shard_map/ppermute | solution.py:162
  83.6 2.0 %collective-permute-start.35 = (bf16[64,512]{1,0:T(8,128)(2,1)S(1)}, bf16[64,512]{1,0:T(8,128)(2,1)S(1)}, u32[]{:S(2)}, u32[]{:S(2)}) collective-permute-start(bf16[64,512]{1,0:T(8,128)(2,1)S(1)} %get-tuple-element.189), channel_id=1, source_target_pairs={{0,4},{1,5},{2,6},{3,7},{4,0},{5,1},{6,2},{7,3},{8,12},{9,13},{10,... | collective-permute-start | bytes 196616 | tf_op jit(solution)/shard_map/ppermute | solution.py:162
  85.6 2.4 %collective-permute-done.27.refs_2_ = bf16[192,512]{1,0:T(8,128)(2,1)S(1)} collective-permute-done((bf16[192,512]{1,0:T(8,128)(2,1)S(1)}, bf16[192,512]{1,0:T(8,128)(2,1)S(1)}, u32[]{:S(2)}, u32[]{:S(2)}) %collective-permute-start.27) | collective-permute-done | bytes 196640 | tf_op jit(solution)/shard_map/ppermute | solution.py:162
  88.3 1.6 %collective-permute-start.21 = (bf16[16,512]{1,0:T(8,128)(2,1)S(1)}, bf16[16,512]{1,0:T(8,128)(2,1)S(1)}, u32[]{:S(2)}, u32[]{:S(2)}) collective-permute-start(bf16[16,512]{1,0:T(8,128)(2,1)S(1)} %get-tuple-element.162), channel_id=1, source_target_pairs={{0,2},{1,3},{2,0},{3,1},{4,6},{5,7},{6,4},{7,5},{8,10},{9,11},{10,... | collective-permute-start | bytes 49160 | tf_op jit(solution)/shard_map/ppermute | solution.py:207
  92.1 2.4 %collective-permute-start.23 = (bf16[16,512]{1,0:T(8,128)(2,1)S(1)}, bf16[16,512]{1,0:T(8,128)(2,1)S(1)}, u32[]{:S(2)}, u32[]{:S(2)}) collective-permute-start(bf16[16,512]{1,0:T(8,128)(2,1)S(1)} %get-tuple-element.164), channel_id=1, source_target_pairs={{0,4},{4,0},{8,12},{12,8},{1,5},{5,1},{9,13},{13,9},{2,6},{6,2},{1... | collective-permute-start | bytes 49160 | tf_op jit(solution)/shard_map/ppermute | solution.py:210
  94.5 1.8 %collective-permute-start.24 = (bf16[16,512]{1,0:T(8,128)(2,1)S(1)}, bf16[16,512]{1,0:T(8,128)(2,1)S(1)}, u32[]{:S(2)}, u32[]{:S(2)}) collective-permute-start(bf16[16,512]{1,0:T(8,128)(2,1)S(1)} %get-tuple-element.165), channel_id=1, source_target_pairs={{0,12},{4,8},{8,4},{12,0},{1,13},{5,9},{9,5},{13,1},{2,14},{6,10},... | collective-permute-start | bytes 49160 | tf_op jit(solution)/shard_map/ppermute | solution.py:212
  96.5 3.5 %collective-permute-done.24.refs_4_ = bf16[16,512]{1,0:T(8,128)(2,1)S(1)} collective-permute-done((bf16[16,512]{1,0:T(8,128)(2,1)S(1)}, bf16[16,512]{1,0:T(8,128)(2,1)S(1)}, u32[]{:S(2)}, u32[]{:S(2)}) %collective-permute-start.24) | collective-permute-done | bytes 16416 | tf_op jit(solution)/shard_map/ppermute | solution.py:212
  (106 shorter events, 29.5 us)
Async XLA Ops:
  3.9 10.9 %collective-permute-start = (bf16[16,512]{1,0:T(8,128)(2,1)S(1)}, bf16[16,512]{1,0:T(8,128)(2,1)S(1)}, u32[]{:S(2)}, u32[]{:S(2)}) collective-permute-start(bf16[16,512]{1,0:T(8,128)(2,1)S(1)} %get-tuple-element.104), channel_id=1, source_target_pairs={{0,1},{1,0},{2,3},{3,2},{4,5},{5,4},{6,7},{7,6},{8,9},{9,8},{10,11... | collective-permute-start | bytes 49160 | tf_op jit(solution)/shard_map/ppermute | solution.py:207
  4.4 10.4 %collective-permute-start.1 = (bf16[16,512]{1,0:T(8,128)(2,1)S(1)}, bf16[16,512]{1,0:T(8,128)(2,1)S(1)}, u32[]{:S(2)}, u32[]{:S(2)}) collective-permute-start(bf16[16,512]{1,0:T(8,128)(2,1)S(1)} %get-tuple-element.105), channel_id=1, source_target_pairs={{0,2},{1,3},{2,0},{3,1},{4,6},{5,7},{6,4},{7,5},{8,10},{9,11},{10,... | collective-permute-start | bytes 49160 | tf_op jit(solution)/shard_map/ppermute | solution.py:207
  6.9 7.8 %collective-permute-start.2 = (bf16[16,512]{1,0:T(8,128)(2,1)S(1)}, bf16[16,512]{1,0:T(8,128)(2,1)S(1)}, u32[]{:S(2)}, u32[]{:S(2)}) collective-permute-start(bf16[16,512]{1,0:T(8,128)(2,1)S(1)} %get-tuple-element.106), channel_id=1, source_target_pairs={{0,3},{1,2},{2,1},{3,0},{4,7},{5,6},{6,5},{7,4},{8,11},{9,10},{10,... | collective-permute-start | bytes 49160 | tf_op jit(solution)/shard_map/ppermute | solution.py:207
  7.0 7.8 %collective-permute-start.3 = (bf16[16,512]{1,0:T(8,128)(2,1)S(1)}, bf16[16,512]{1,0:T(8,128)(2,1)S(1)}, u32[]{:S(2)}, u32[]{:S(2)}) collective-permute-start(bf16[16,512]{1,0:T(8,128)(2,1)S(1)} %get-tuple-element.107), channel_id=1, source_target_pairs={{0,4},{4,0},{8,12},{12,8},{1,5},{5,1},{9,13},{13,9},{2,6},{6,2},{1... | collective-permute-start | bytes 49160 | tf_op jit(solution)/shard_map/ppermute | solution.py:210
  8.8 6.0 %collective-permute-start.4 = (bf16[16,512]{1,0:T(8,128)(2,1)S(1)}, bf16[16,512]{1,0:T(8,128)(2,1)S(1)}, u32[]{:S(2)}, u32[]{:S(2)}) collective-permute-start(bf16[16,512]{1,0:T(8,128)(2,1)S(1)} %get-tuple-element.108), channel_id=1, source_target_pairs={{0,12},{4,8},{8,4},{12,0},{1,13},{5,9},{9,5},{13,1},{2,14},{6,10},... | collective-permute-start | bytes 49160 | tf_op jit(solution)/shard_map/ppermute | solution.py:212
  18.7 6.1 %collective-permute-start.5 = (bf16[32,512]{1,0:T(8,128)(2,1)S(1)}, bf16[32,512]{1,0:T(8,128)(2,1)S(1)}, u32[]{:S(2)}, u32[]{:S(2)}) collective-permute-start(bf16[32,512]{1,0:T(8,128)(2,1)S(1)} %get-tuple-element.113), channel_id=1, source_target_pairs={{0,1},{1,0},{2,3},{3,2},{4,5},{5,4},{6,7},{7,6},{8,9},{9,8},{10,11... | collective-permute-start | bytes 98312 | tf_op jit(solution)/shard_map/ppermute | solution.py:207
  18.8 6.0 %collective-permute-start.6 = (bf16[32,512]{1,0:T(8,128)(2,1)S(1)}, bf16[32,512]{1,0:T(8,128)(2,1)S(1)}, u32[]{:S(2)}, u32[]{:S(2)}) collective-permute-start(bf16[32,512]{1,0:T(8,128)(2,1)S(1)} %get-tuple-element.114), channel_id=1, source_target_pairs={{0,2},{1,3},{2,0},{3,1},{4,6},{5,7},{6,4},{7,5},{8,10},{9,11},{10,... | collective-permute-start | bytes 98312 | tf_op jit(solution)/shard_map/ppermute | solution.py:207
  28.0 7.9 %collective-permute-start.10 = (bf16[16,512]{1,0:T(8,128)(2,1)S(1)}, bf16[16,512]{1,0:T(8,128)(2,1)S(1)}, u32[]{:S(2)}, u32[]{:S(2)}) collective-permute-start(bf16[16,512]{1,0:T(8,128)(2,1)S(1)} %get-tuple-element.123), channel_id=1, source_target_pairs={{0,1},{1,0},{2,3},{3,2},{4,5},{5,4},{6,7},{7,6},{8,9},{9,8},{10,11... | collective-permute-start | bytes 49160 | tf_op jit(solution)/shard_map/ppermute | solution.py:207
  28.0 7.8 %collective-permute-start.11 = (bf16[16,512]{1,0:T(8,128)(2,1)S(1)}, bf16[16,512]{1,0:T(8,128)(2,1)S(1)}, u32[]{:S(2)}, u32[]{:S(2)}) collective-permute-start(bf16[16,512]{1,0:T(8,128)(2,1)S(1)} %get-tuple-element.124), channel_id=1, source_target_pairs={{0,2},{1,3},{2,0},{3,1},{4,6},{5,7},{6,4},{7,5},{8,10},{9,11},{10,... | collective-permute-start | bytes 49160 | tf_op jit(solution)/shard_map/ppermute | solution.py:207
  29.6 6.3 %collective-permute-start.12 = (bf16[16,512]{1,0:T(8,128)(2,1)S(1)}, bf16[16,512]{1,0:T(8,128)(2,1)S(1)}, u32[]{:S(2)}, u32[]{:S(2)}) collective-permute-start(bf16[16,512]{1,0:T(8,128)(2,1)S(1)} %get-tuple-element.125), channel_id=1, source_target_pairs={{0,3},{1,2},{2,1},{3,0},{4,7},{5,6},{6,5},{7,4},{8,11},{9,10},{10,... | collective-permute-start | bytes 49160 | tf_op jit(solution)/shard_map/ppermute | solution.py:207
  29.9 6.0 %collective-permute-start.13 = (bf16[16,512]{1,0:T(8,128)(2,1)S(1)}, bf16[16,512]{1,0:T(8,128)(2,1)S(1)}, u32[]{:S(2)}, u32[]{:S(2)}) collective-permute-start(bf16[16,512]{1,0:T(8,128)(2,1)S(1)} %get-tuple-element.126), channel_id=1, source_target_pairs={{0,4},{4,0},{8,12},{12,8},{1,5},{5,1},{9,13},{13,9},{2,6},{6,2},{1... | collective-permute-start | bytes 49160 | tf_op jit(solution)/shard_map/ppermute | solution.py:210
  29.9 6.0 %collective-permute-start.14 = (bf16[16,512]{1,0:T(8,128)(2,1)S(1)}, bf16[16,512]{1,0:T(8,128)(2,1)S(1)}, u32[]{:S(2)}, u32[]{:S(2)}) collective-permute-start(bf16[16,512]{1,0:T(8,128)(2,1)S(1)} %get-tuple-element.127), channel_id=1, source_target_pairs={{0,12},{4,8},{8,4},{12,0},{1,13},{5,9},{9,5},{13,1},{2,14},{6,10},... | collective-permute-start | bytes 49160 | tf_op jit(solution)/shard_map/ppermute | solution.py:212
  43.3 30.0 %collective-permute-start.30 = (bf16[512,512]{1,0:T(8,128)(2,1)S(1)}, bf16[512,512]{1,0:T(8,128)(2,1)S(1)}, u32[]{:S(2)}, u32[]{:S(2)}) collective-permute-start(bf16[512,512]{1,0:T(8,128)(2,1)S(1)} %get-tuple-element.179), channel_id=1, source_target_pairs={{0,2},{1,3},{2,0},{3,1},{4,6},{5,7},{6,4},{7,5},{8,10},{9,11},{10,... | collective-permute-start | bytes 1572872 | tf_op jit(solution)/shard_map/ppermute | solution.py:162
  45.3 28.4 %collective-permute-start.26 = (bf16[384,512]{1,0:T(8,128)(2,1)S(1)}, bf16[384,512]{1,0:T(8,128)(2,1)S(1)}, u32[]{:S(2)}, u32[]{:S(2)}) collective-permute-start(bf16[384,512]{1,0:T(8,128)(2,1)S(1)} %get-tuple-element.171), channel_id=1, source_target_pairs={{0,2},{1,3},{2,0},{3,1},{4,6},{5,7},{6,4},{7,5},{8,10},{9,11},{10,... | collective-permute-start | bytes 1179656 | tf_op jit(solution)/shard_map/ppermute | solution.py:162
  46.2 19.8 %collective-permute-start.16 = (bf16[8,512]{1,0:T(8,128)(2,1)S(1)}, bf16[8,512]{1,0:T(8,128)(2,1)S(1)}, u32[]{:S(2)}, u32[]{:S(2)}) collective-permute-start(bf16[8,512]{1,0:T(8,128)(2,1)S(1)} %get-tuple-element.145), channel_id=1, source_target_pairs={{0,2},{1,3},{2,0},{3,1},{4,6},{5,7},{6,4},{7,5},{8,10},{9,11},{10,... | collective-permute-start | bytes 24584 | tf_op jit(solution)/shard_map/ppermute | solution.py:207
  47.4 20.5 %collective-permute-start.17 = (bf16[8,512]{1,0:T(8,128)(2,1)S(1)}, bf16[8,512]{1,0:T(8,128)(2,1)S(1)}, u32[]{:S(2)}, u32[]{:S(2)}) collective-permute-start(bf16[8,512]{1,0:T(8,128)(2,1)S(1)} %get-tuple-element.146), channel_id=1, source_target_pairs={{0,3},{1,2},{2,1},{3,0},{4,7},{5,6},{6,5},{7,4},{8,11},{9,10},{10,... | collective-permute-start | bytes 24584 | tf_op jit(solution)/shard_map/ppermute | solution.py:207
  48.0 19.9 %collective-permute-start.18 = (bf16[8,512]{1,0:T(8,128)(2,1)S(1)}, bf16[8,512]{1,0:T(8,128)(2,1)S(1)}, u32[]{:S(2)}, u32[]{:S(2)}) collective-permute-start(bf16[8,512]{1,0:T(8,128)(2,1)S(1)} %get-tuple-element.147), channel_id=1, source_target_pairs={{0,4},{4,0},{8,12},{12,8},{1,5},{5,1},{9,13},{13,9},{2,6},{6,2},{1... | collective-permute-start | bytes 24584 | tf_op jit(solution)/shard_map/ppermute | solution.py:210
  73.6 9.2 %collective-permute-start.31 = (bf16[256,512]{1,0:T(8,128)(2,1)S(1)}, bf16[256,512]{1,0:T(8,128)(2,1)S(1)}, u32[]{:S(2)}, u32[]{:S(2)}) collective-permute-start(bf16[256,512]{1,0:T(8,128)(2,1)S(1)} %get-tuple-element.181), channel_id=1, source_target_pairs={{0,4},{1,5},{2,6},{3,7},{4,0},{5,1},{6,2},{7,3},{8,12},{9,13},{10,... | collective-permute-start | bytes 786440 | tf_op jit(solution)/shard_map/ppermute | solution.py:162
  73.9 14.1 %collective-permute-start.27 = (bf16[192,512]{1,0:T(8,128)(2,1)S(1)}, bf16[192,512]{1,0:T(8,128)(2,1)S(1)}, u32[]{:S(2)}, u32[]{:S(2)}) collective-permute-start(bf16[192,512]{1,0:T(8,128)(2,1)S(1)} %get-tuple-element.173), channel_id=1, source_target_pairs={{0,4},{1,5},{2,6},{3,7},{4,0},{5,1},{6,2},{7,3},{8,12},{9,13},{10,... | collective-permute-start | bytes 589832 | tf_op jit(solution)/shard_map/ppermute | solution.py:162
  76.1 7.3 %collective-permute-start.34 = (bf16[128,512]{1,0:T(8,128)(2,1)S(1)}, bf16[128,512]{1,0:T(8,128)(2,1)S(1)}, u32[]{:S(2)}, u32[]{:S(2)}) collective-permute-start(bf16[128,512]{1,0:T(8,128)(2,1)S(1)} %get-tuple-element.187), channel_id=1, source_target_pairs={{0,2},{1,3},{2,0},{3,1},{4,6},{5,7},{6,4},{7,5},{8,10},{9,11},{10,... | collective-permute-start | bytes 393224 | tf_op jit(solution)/shard_map/ppermute | solution.py:162
  82.9 18.4 %collective-permute-start.32 = (bf16[128,512]{1,0:T(8,128)(2,1)S(1)}, bf16[128,512]{1,0:T(8,128)(2,1)S(1)}, u32[]{:S(2)}, u32[]{:S(2)}) collective-permute-start(bf16[128,512]{1,0:T(8,128)(2,1)S(1)} %get-tuple-element.183), channel_id=1, source_target_pairs={{0,8},{1,9},{2,10},{3,11},{4,12},{5,13},{6,14},{7,15},{8,0},{9,1},... | collective-permute-start | bytes 393224 | tf_op jit(solution)/shard_map/ppermute | solution.py:162
  83.6 10.9 %collective-permute-start.35 = (bf16[64,512]{1,0:T(8,128)(2,1)S(1)}, bf16[64,512]{1,0:T(8,128)(2,1)S(1)}, u32[]{:S(2)}, u32[]{:S(2)}) collective-permute-start(bf16[64,512]{1,0:T(8,128)(2,1)S(1)} %get-tuple-element.189), channel_id=1, source_target_pairs={{0,4},{1,5},{2,6},{3,7},{4,0},{5,1},{6,2},{7,3},{8,12},{9,13},{10,... | collective-permute-start | bytes 196616 | tf_op jit(solution)/shard_map/ppermute | solution.py:162
  88.1 13.3 %collective-permute-start.28 = (bf16[96,512]{1,0:T(8,128)(2,1)S(1)}, bf16[96,512]{1,0:T(8,128)(2,1)S(1)}, u32[]{:S(2)}, u32[]{:S(2)}) collective-permute-start(bf16[96,512]{1,0:T(8,128)(2,1)S(1)} %get-tuple-element.175), channel_id=1, source_target_pairs={{0,8},{1,9},{2,10},{3,11},{4,12},{5,13},{6,14},{7,15},{8,0},{9,1},... | collective-permute-start | bytes 294920 | tf_op jit(solution)/shard_map/ppermute | solution.py:162
  89.8 6.6 %collective-permute-start.22 = (bf16[16,512]{1,0:T(8,128)(2,1)S(1)}, bf16[16,512]{1,0:T(8,128)(2,1)S(1)}, u32[]{:S(2)}, u32[]{:S(2)}) collective-permute-start(bf16[16,512]{1,0:T(8,128)(2,1)S(1)} %get-tuple-element.163), channel_id=1, source_target_pairs={{0,3},{1,2},{2,1},{3,0},{4,7},{5,6},{6,5},{7,4},{8,11},{9,10},{10,... | collective-permute-start | bytes 49160 | tf_op jit(solution)/shard_map/ppermute | solution.py:207
  (28 other events, 188.6 us)

commit v5 on v4

--- a/solution.py
+++ b/solution.py
@@ -187,13 +187,20 @@
     return blocks.astype(F32)
 
 
-def call(kernel, name, outs, args, flops):
-    size = sum(a.size * a.dtype.itemsize for a in (*args, *outs))
+def call(kernel, name, outs, args, flops, loads=(), scratch=()):
+    size = sum(a.size * a.dtype.itemsize for a in (*args, *outs, *loads))
+    args = (*(pltpu.with_memory_space_constraint(a, pltpu.HBM) for a in loads), *args)
+    scratch = list(scratch)
+    if loads:
+        scratch.append(pltpu.SemaphoreType.DMA((len(loads),)))
+    in_specs = [pl.BlockSpec(memory_space=pltpu.HBM)] * len(loads)
+    in_specs += [pl.BlockSpec(memory_space=pltpu.VMEM)] * (len(args) - len(loads))
     return pl.pallas_call(
         kernel,
-        out_shape=list(outs),
-        in_specs=[pl.BlockSpec(memory_space=pltpu.VMEM)] * len(args),
-        out_specs=[pl.BlockSpec(memory_space=pltpu.VMEM)] * len(outs),
+        out_shape=[shape(*a.shape, dtype=a.dtype) for a in loads] + list(outs),
+        in_specs=in_specs,
+        out_specs=[pl.BlockSpec(memory_space=pltpu.VMEM)] * (len(outs) + len(loads)),
+        scratch_shapes=scratch,
         compiler_params=pltpu.CompilerParams(vmem_limit_bytes=16 * 1024 * 1024),
         cost_estimate=pl.CostEstimate(flops=flops, bytes_accessed=size, transcendentals=0),
         name=name,
@@ -203,36 +210,59 @@
 def exchange(parts, dims):
     column = dims[1] * dims[2]
     count = dims[0]
+    other = [(i, (i - 1 + 2 * (i % 2)) % count) for i in range(count)]
+    far = lax.ppermute(parts[column], "lon", other)
+    near = lax.ppermute(parts[column - 1], "lon", [(i, i ^ 1) for i in range(count)])
     arrived = [
         lax.ppermute(parts[r - 1], COLUMN, [(i, i ^ r) for i in range(column)])
-        for r in range(1, column)
+        for r in range(column - 1, 0, -1)
     ]
-    near = lax.ppermute(parts[column - 1], "lon", [(i, i ^ 1) for i in range(count)])
-    other = [(i, (i - 1 + 2 * (i % 2)) % count) for i in range(count)]
-    far = lax.ppermute(parts[column], "lon", other)
-    return (*arrived, near, far)
+    return (*arrived[::-1], near, far)
 
 
 def shape(*dims, dtype=BF):
     return jax.ShapeDtypeStruct(dims, dtype)
 
 
-def first_payload(column, capacity, ints_ref, grid_ref, sends_ref, *pay_refs):
+def start_loads(sources, targets, sems):
+    copies = [
+        pltpu.make_async_copy(source, target, sems.at[at])
+        for at, (source, target) in enumerate(zip(sources, targets))
+    ]
+    for copy in copies:
+        copy.start()
+    return copies
+
+
+def first_payload(
+    column, capacity, grid_far, embed_far, target_far, senders_far, ints_ref,
+    grid_ref, embed_ref, target_ref, senders_ref, sends_ref, *rest
+):
+    *pay_refs, sems = rest
+    grid_load, *loads = start_loads(
+        (grid_far, embed_far, target_far, senders_far),
+        (grid_ref, embed_ref, target_ref, senders_ref), sems,
+    )
     chosen = grid_ref.shape[0]
     ints = ints_ref[...]
     base = 2 * capacity + BORDER
     me, odd = ints[0:1, base : base + 1], ints[0:1, base + 1 : base + 2]
     sends = as_column(ints[:, :capacity], capacity, column, me, odd)
     sends_ref[...] = sends
-    rows = dot(low(hot(sends == iota(sends.shape[0], chosen, 1))), grid_ref[...])
-    store_parts(pay_refs, [rows])
+    pick = low(hot(sends == iota(sends.shape[0], chosen, 1)))
+    grid_load.wait()
+    store_parts(pay_refs, [dot(pick, grid_ref[...])])
+    for load in loads:
+        load.wait()
 
 
 def embed_local(
-    column, capacity, ints_ref, senders_ref, grid_ref, weight_ref, target_ref, sends_ref,
+    column, capacity, mesh_far, merge_far, cot_far, ints_ref, senders_ref, grid_ref, weight_ref,
+    target_ref, sends_ref, mesh_ref, merge_ref, cot_ref,
     sum_ref, slope_ref, sends_row_ref, incoming_ref, bounds_ref, bounds_row_ref, senders_t_ref,
-    senders_out_ref, place_ref,
-):
+    senders_out_ref, place_ref, sems,
+):
+    loads = start_loads((mesh_far, merge_far, cot_far), (mesh_ref, merge_ref, cot_ref), sems)
     chosen = grid_ref.shape[0]
     nodes = sum_ref.shape[0]
     taken = sends_ref.shape[0]
@@ -261,6 +291,8 @@
     senders_t_ref[...] = senders
     filler = jnp.zeros((8 - degree, nodes), I32)
     senders_out_ref[...] = jnp.concatenate([senders, filler], axis=0).T
+    for load in loads:
+        load.wait()
 
 
 def merge_nodes(peers, *refs):
@@ -289,15 +321,21 @@
 
 def local_edges(senders, degree, sent, recv, each):
     nodes = senders.shape[0]
-    total = jnp.zeros(recv.shape, F32)
+    total = None
     ids = iota(nodes, nodes, 1)
     for j in range(degree):
-        named = senders[:, j : j + 1]
-        act, slope = silu_both(dot(low(hot(named == ids)), sent) + recv)
-        keep = hot(named < nodes)
-        total = total + act * keep
-        each(j, slope * keep)
+        act, slope = silu_both(dot(low(hot(senders[:, j : j + 1] == ids)), sent) + recv)
+        total = act if total is None else total + act
+        each(j, slope)
     return total
+
+
+def edge_targets(senders_t):
+    degree, nodes = senders_t.shape
+    ids = iota(nodes, nodes, 0)
+    return jnp.concatenate(
+        [low(hot(senders_t[j : j + 1, :] == ids)) for j in range(degree)], axis=1
+    )
 
 
 def forward_local(
@@ -335,7 +373,8 @@
     pre = low(dot(low(rows), send_ref[0])).astype(F32) + recv_n_ref[...]
     pre_ref[...] = pre
     place = low(receivers_t(senders_ref[...], degree, halo))
-    summed = low(total_ref[...] + dot(place, low(silu(pre))))
+    extra = silu(pre) - silu(recv_n_ref[...])
+    summed = low(total_ref[...] + dot(place, low(extra)))
     summed_ref[...] = summed
     state = low(state_ref[...].astype(F32) + dot(summed, update_ref[0]))
     out_ref[...] = state
@@ -345,13 +384,15 @@
 
 
 def turn_local(
-    state_ref, send_ref, recv_ref, update_ref, cot_ref, cot_r_ref, pre_ref, back0_ref,
+    state_ref, send_ref, recv_ref, update_ref, cot_ref, cot_r_ref, pre_ref, recv_n0_ref, back0_ref,
     sent_b0_ref, senders_ref, senders_t_ref, bounds_ref,
     total_ref, grecv_ref, gsent_ref, recv_n_ref, sent_b_ref, gsum_n_ref, gsum_r_ref,
-    slope_k_ref, slope_r_ref,
+    slope_k_ref, slope_d_ref, slope_r_ref, gpre_ref,
 ):
     halo = bounds_ref.shape[0]
-    slope_k_ref[...] = low(silu_slope(pre_ref[...]))
+    slope = silu_slope(pre_ref[...])
+    slope_k_ref[...] = low(slope)
+    slope_d_ref[...] = low(slope - silu_slope(recv_n0_ref[...]))
     pre = sent_b0_ref[...].astype(F32) + dot(back0_ref[...], recv_ref[0])
     slope_r_ref[...] = low(silu_slope(pre))
     state = state_ref[...]
@@ -360,17 +401,17 @@
     recv = dot(state, recv_ref[1])
     gsum = low(dot(cot_ref[...], update_ref[1], NT))
     grad = gsum.astype(F32)
-    grecv_ref[...] = jnp.zeros(grecv_ref.shape, F32)
-    gsent_ref[...] = jnp.zeros(gsent_ref.shape, F32)
+    grecv = []
 
     def back_edge(j, slope):
         gpre = grad * slope
-        grecv_ref[...] += gpre
-        target = low(hot(senders_t_ref[j : j + 1, :] == iota(nodes, nodes, 0)))
-        gsent_ref[...] += dot(target, low(gpre))
+        grecv.append(gpre if j == 0 else grecv[-1] + gpre)
+        gpre_ref[j * nodes : (j + 1) * nodes, :] = low(gpre)
 
     degree = senders_t_ref.shape[0]
     total_ref[...] = local_edges(senders_ref[...], degree, sent, recv, back_edge)
+    grecv_ref[...] = grecv[-1]
+    gsent_ref[...] = dot(edge_targets(senders_t_ref[...]), gpre_ref[...])
     back = low(receivers(senders_t_ref[...], halo))
     recv_n_ref[...] = dot(low(dot(back, state)), recv_ref[1])
     sent_b_ref[...] = low(dot(low(hot(bounds_ref[...] == iota(halo, nodes, 1))), sent))
@@ -390,7 +431,8 @@
     pre = low(dot(low(rows), send_ref[1])).astype(F32) + recv_n_ref[...]
     act, slope = silu_both(pre)
     place = low(receivers_t(senders_ref[...], degree, halo))
-    gpre = low(gsum_n_ref[...].astype(F32) * slope)
+    base, base_slope = silu_both(recv_n_ref[...])
+    gpre = low(gsum_n_ref[...].astype(F32) * (slope - base_slope))
     grecv = low(grecv_ref[...] + dot(place, gpre))
     pre = sent_b_ref[...].astype(F32) + dot(low(back), recv_ref[1])
     gpre = low(gsum_r_ref[...].astype(F32) * silu_slope(pre))
@@ -400,7 +442,7 @@
     gin = low(gin)
     gin_ref[...] = gin
     store_parts(pay_refs, [dot(low(receivers(senders_t_ref[...], halo)), gin)])
-    summed_ref[...] = low(total_ref[...] + dot(place, low(act)))
+    summed_ref[...] = low(total_ref[...] + dot(place, low(act - base)))
     grecv_out_ref[...] = grecv
     gsent_out_ref[...] = gsent
 
@@ -421,26 +463,25 @@
 
 
 def back_local(
-    dims, place_ref, gin_ref, slope_ref, slope_k_ref, send_ref, recv_ref, update_ref, senders_ref,
-    senders_t_ref, state_ref, rows_ref, summed_ref, merged_ref, merged_r_ref,
-    part_ref, keep_ref, give_ref,
+    dims, place_ref, gin_ref, slope_ref, slope_k_ref, slope_d_ref, send_ref, recv_ref, update_ref,
+    senders_ref, senders_t_ref, state_ref, rows_ref, summed_ref, merged_ref, merged_r_ref,
+    part_ref, keep_ref, give_ref, gpre_ref,
 ):
     nodes = gin_ref.shape[0]
     halo = slope_k_ref.shape[0]
     degree = senders_t_ref.shape[0]
     gin = gin_ref[...]
     gsum = low(dot(gin, update_ref[0], NT))
-    grad = gsum.astype(F32)
     place = low(receivers_t(senders_ref[...], degree, halo))
     back = low(receivers(senders_t_ref[...], halo))
-    gpre_k = low(dot(back, gsum) * slope_k_ref[...].astype(F32))
-    grecv = dot(place, gpre_k)
-    gsent = jnp.zeros(grad.shape, F32)
+    gsum_n = low(dot(back, gsum))
+    gpre_k = gsum_n * slope_k_ref[...]
+    grecv = dot(place, gsum_n * slope_d_ref[...])
     for j in range(degree):
-        gpre = grad * slope_ref[j].astype(F32)
-        grecv = grecv + gpre
-        target = low(hot(senders_t_ref[j : j + 1, :] == iota(nodes, nodes, 0)))
-        gsent = gsent + dot(target, low(gpre))
+        gpre = gsum * slope_ref[j]
+        grecv = grecv + gpre.astype(F32)
+        gpre_ref[j * nodes : (j + 1) * nodes, :] = gpre
+    gsent = dot(edge_targets(senders_t_ref[...]), gpre_ref[...])
     grecv, gsent = low(grecv), low(gsent)
     part = gin.astype(F32) + dot(grecv, recv_ref[0], NT) + dot(gsent, send_ref[0], NT)
     part_ref[...] = part
@@ -528,29 +569,30 @@
     place += [(spot >> bit) % 2 for bit in range(bits)]
     place = jnp.broadcast_to(jnp.stack(place).astype(I32)[None], (slots, 2 + bits))
     ints = jnp.concatenate([send_rows[0], incoming_rows[0], border_mesh_rows[0], place], axis=1)
-    targets = target_row.reshape(1, chosen)
     unit = 2 * nodes * width * width
 
-    sends, *pay1 = call(
+    grid, embed, targets, senders_raw, sends, *pay1 = call(
         lambda *refs: first_payload(column, capacity, *refs), "first_payload",
         [shape(taken, 1, dtype=I32)] + [shape(capacity, width)] * peers,
-        (ints, grid_latent), flops=unit // 2,
+        (ints,), flops=unit // 2,
+        loads=(grid_latent, embed_weight, target_row.reshape(1, chosen), mesh_senders.T),
     )
     arr1 = exchange(pay1, dims)
-    (local, slope_g, sends_row, incoming, bounds, bounds_row, senders_t, senders, place) = call(
+    (mesh, merge, cot, local, slope_g, sends_row, incoming, bounds, bounds_row, senders_t, senders,
+     place) = call(
         lambda *refs: embed_local(column, capacity, *refs), "embed_local",
         [shape(nodes, width, dtype=F32), shape(chosen, width), shape(1, taken, dtype=I32),
          shape(1, taken, dtype=I32), shape(halo, 1, dtype=I32), shape(1, halo, dtype=I32),
          shape(degree, nodes, dtype=I32), shape(nodes, 8, dtype=I32),
          shape(slots, 2 + bits, dtype=I32)],
-        (ints, mesh_senders.T, grid_latent, embed_weight, targets, sends), flops=3 * unit,
+        (ints, senders_raw, grid, embed, targets, sends), flops=3 * unit,
+        loads=(mesh_latent, merge_weight, cotangent),
     )
     merged, state0, slope_a, lat_a, *pay2 = call(
         lambda *refs: merge_nodes(peers, *refs), "merge_nodes",
         [shape(nodes, width), shape(nodes, width), shape(taken, width), shape(taken, width)]
         + [shape(4 * BORDER, width)] * peers,
-        (*arr1, incoming, embed_weight, local, mesh_latent, merge_weight, bounds, senders_t,
-         cotangent),
+        (*arr1, incoming, embed, local, mesh, merge, bounds, senders_t, cot),
         flops=2 * unit,
     )
     arr2 = exchange(pay2, dims)
@@ -568,18 +610,19 @@
         flops=2 * unit,
     )
     arr3 = exchange(pay3, dims)
-    (total1, grecv_l, gsent_l, recv_n1, sent_b1, gsum_n1, gsum_r1, slope_k0, slope_r0) = call(
+    (total1, grecv_l, gsent_l, recv_n1, sent_b1, gsum_n1, gsum_r1, slope_k0, slope_d0,
+     slope_r0) = call(
         turn_local, "turn_local",
         [shape(nodes, width, dtype=F32)] * 3 + [shape(halo, width, dtype=F32)]
-        + [shape(halo, width)] * 5,
-        (state1, send_weight, recv_weight, update_weight, cotangent, cot_r, pre0, back0, sent_b0,
-         senders, senders_t, bounds),
-        flops=10 * unit,
+        + [shape(halo, width)] * 6,
+        (state1, send_weight, recv_weight, update_weight, cot, cot_r, pre0, recv_n0, back0,
+         sent_b0, senders, senders_t, bounds),
+        flops=10 * unit, scratch=[pltpu.VMEM((degree * nodes, width), BF)],
     )
     summed1, grecv1, gsent1, gin1, *pay4 = call(
         lambda *refs: turn_halo(peers, *refs), "turn_halo",
         [shape(nodes, width)] * 4 + [shape(BORDER, width)] * peers,
-        (*arr3, recv_n1, sent_b1, gsum_n1, gsum_r1, total1, grecv_l, gsent_l, cotangent,
+        (*arr3, recv_n1, sent_b1, gsum_n1, gsum_r1, total1, grecv_l, gsent_l, cot,
          send_weight, recv_weight, senders, senders_t, bounds_row),
         flops=3 * unit,
     )
@@ -587,27 +630,28 @@
     keep1, give1, mesh_out = call(
         lambda *refs: last_weights(dims, *refs), "last_weights",
         blocks_shapes(3, width, width, dims) + [shape(nodes, width)],
-        (place, state1, summed1, cotangent, grecv1, gsent1, update_weight), flops=4 * unit,
+        (place, state1, summed1, cot, grecv1, gsent1, update_weight), flops=4 * unit,
     )
     part0, keep0, give0 = call(
         lambda *refs: back_local(dims, *refs), "back_local",
         [shape(nodes, width, dtype=F32)] + blocks_shapes(4, width, width, dims),
-        (place, gin1, slope0, slope_k0, send_weight, recv_weight, update_weight, senders,
+        (place, gin1, slope0, slope_k0, slope_d0, send_weight, recv_weight, update_weight, senders,
          senders_t, state0, rows0, summed0, merged, merged_r),
-        flops=10 * unit,
-    )
+        flops=10 * unit, scratch=[pltpu.VMEM((degree * nodes, width), BF)],
+    )
+    give1, give0, *arr4 = lax.optimization_barrier((give1, give0, *arr4))
     gpre_g, keep_e, give_e, *pay5 = call(
         lambda *refs: embed_back(peers, dims, *refs), "embed_back",
         [shape(chosen, width)] + blocks_shapes(1, width, width, dims)
         + [shape(capacity, width)] * peers,
-        (*arr4, place, slope_r0, part0, update_weight, send_weight, merge_weight, bounds_row,
-         targets, sends, incoming, slope_g, slope_a, grid_latent, lat_a, embed_weight),
+        (*arr4, place, slope_r0, part0, update_weight, send_weight, merge, bounds_row,
+         targets, sends, incoming, slope_g, slope_a, grid, lat_a, embed),
         flops=6 * unit,
     )
     arr5 = exchange(pay5, dims)
     (grid_grad,) = call(
         lambda *refs: grid_place(peers, *refs), "grid_place", [shape(chosen, width)],
-        (*arr5, gpre_g, embed_weight, sends_row), flops=3 * unit,
+        (*arr5, gpre_g, embed, sends_row), flops=3 * unit,
     )
     depth = width // total
     if not fine(width, dims):

time: 103 us -> 91.9 us (0.89)
  waiting for transfers between devices: 36.2 us -> 27.7 us
  local copies, waits for them, and re-layouts: 7.98 us -> 1.57 us
  starting transfers between devices: 35.6 us -> 39.4 us
    ppermute x15, waiting for transfers between devices: 18.9 us -> 0.82 us  [exchange(): lax.ppermute(parts[r - 1], COLUMN, [(i, i ^ r) for i in range(column)])]
    ppermute x12, waiting for transfers between devices: 7.94 us -> 20.7 us  [swap(): return lax.ppermute(block, GROUP, [(i, i ^ 1 << bit) for i in range(total)])]
    unnamed x32 -> x8, local copies, waits for them, and re-layouts: 7.82 us -> 1.41 us
    ppermute x5, waiting for transfers between devices: 9.26 us -> 6.04 us  [exchange(): far = lax.ppermute(parts[column], 'lon', other)]
    ppermute x12, starting transfers between devices: 9.43 us -> 11 us  [swap(): return lax.ppermute(block, GROUP, [(i, i ^ 1 << bit) for i in range(total)])]
    ppermute x5, starting transfers between devices: 9.44 us -> 10.6 us  [exchange(): far = lax.ppermute(parts[column], 'lon', other)]
  transfers between devices with their start and end apart: 37 -> 37, of which waited for: 8 -> 8; matrix products, arithmetic and copies ran while one was open for 0% -> 0% of each run, Pallas kernels for 14% -> 18%
where the time goes in v5:
time: 91.9 us; the launch traced here: 91.6 us
  starting transfers between devices  39.4 us (43%)
  waiting for transfers between devices  27.7 us (30%)
  Pallas kernels  21.9 us (24%)
  local copies, waits for them, and re-layouts  1.57 us (2%)
  between operations  0.99 us (1%)
    pallas_call x21, Pallas kernels, call(): pl.pallas_call(kernel, out_shape=[shape(*a.shape, dtype=a.dtype) for a in...  21.9 us
    ppermute x12, waiting for transfers between devices, swap(): return lax.ppermute(block, GROUP, [(i, i ^ 1 << bit) for i in range(total)])  20.7 us
    ppermute x15, starting transfers between devices, exchange(): lax.ppermute(parts[r - 1], COLUMN, [(i, i ^ r) for i in range(column)])  12 us
    ppermute x12, starting transfers between devices, swap(): return lax.ppermute(block, GROUP, [(i, i ^ 1 << bit) for i in range(total)])  11 us
    ppermute x5, starting transfers between devices, exchange(): far = lax.ppermute(parts[column], 'lon', other)  10.6 us
    ppermute x5, waiting for transfers between devices, exchange(): far = lax.ppermute(parts[column], 'lon', other)  6.04 us
    ppermute x5, starting transfers between devices, exchange(): lax.ppermute(parts[column - 1], 'lon', [(i, i ^ 1) for i in range(count)])  5.86 us
  transfers between devices with their start and end apart: 37, of which 8 were waited for; matrix products, arithmetic and copies ran while one was open for 0% of the time, Pallas kernels for 18%

profile of v5, /device:TPU:0, one launch (start us, length us, event | category | flops | bytes accessed | tf_op | source)
XLA Modules:
  0.0 91.6 jit_solution(697737777160676263)
XLA Ops:
  4.1 2.6 %collective-permute-start.1 = (bf16[16,512]{1,0:T(8,128)(2,1)S(1)}, bf16[16,512]{1,0:T(8,128)(2,1)S(1)}, u32[]{:S(2)}, u32[]{:S(2)}) collective-permute-start(bf16[16,512]{1,0:T(8,128)(2,1)S(1)} %get-tuple-element.124), channel_id=1, source_target_pairs={{0,2},{1,3},{2,0},{3,1},{4,6},{5,7},{6,4},{7,5},{8,10},{9,11},{10,... | collective-permute-start | bytes 49160 | tf_op jit(solution)/shard_map/ppermute | solution.py:217
  6.8 1.8 %collective-permute-start.3 = (bf16[16,512]{1,0:T(8,128)(2,1)S(1)}, bf16[16,512]{1,0:T(8,128)(2,1)S(1)}, u32[]{:S(2)}, u32[]{:S(2)}) collective-permute-start(bf16[16,512]{1,0:T(8,128)(2,1)S(1)} %get-tuple-element.126), channel_id=1, source_target_pairs={{0,4},{4,0},{8,12},{12,8},{1,5},{5,1},{9,13},{13,9},{2,6},{6,2},{1... | collective-permute-start | bytes 49160 | tf_op jit(solution)/shard_map/ppermute | solution.py:215
  8.6 2.5 %collective-permute-start.4 = (bf16[16,512]{1,0:T(8,128)(2,1)S(1)}, bf16[16,512]{1,0:T(8,128)(2,1)S(1)}, u32[]{:S(2)}, u32[]{:S(2)}) collective-permute-start(bf16[16,512]{1,0:T(8,128)(2,1)S(1)} %get-tuple-element.127), channel_id=1, source_target_pairs={{0,12},{4,8},{8,4},{12,0},{1,13},{5,9},{9,5},{13,1},{2,14},{6,10},... | collective-permute-start | bytes 49160 | tf_op jit(solution)/shard_map/ppermute | solution.py:214
  11.1 2.1 %embed_local.1 = (bf16[256,512]{1,0:T(8,128)(2,1)S(1)}, bf16[512,512]{1,0:T(8,128)(2,1)S(1)}, bf16[256,512]{1,0:T(8,128)(2,1)S(1)}, f32[256,512]{1,0:T(8,128)S(1...) custom-call(bf16[256,512]{1,0:T(8,128)(2,1)} %refs_0_.3, ...), custom_call_target="tpu_custom_call" | custom-call | flops 402653184 | bytes 3170784 | tf_op jit(solution)/shard_map/embed_local/pallas_call | solution.py:198
  15.1 1.6 %collective-permute-start.6 = (bf16[32,512]{1,0:T(8,128)(2,1)S(1)}, bf16[32,512]{1,0:T(8,128)(2,1)S(1)}, u32[]{:S(2)}, u32[]{:S(2)}) collective-permute-start(bf16[32,512]{1,0:T(8,128)(2,1)S(1)} %get-tuple-element.136), channel_id=1, source_target_pairs={{0,2},{1,3},{2,0},{3,1},{4,6},{5,7},{6,4},{7,5},{8,10},{9,11},{10,... | collective-permute-start | bytes 98312 | tf_op jit(solution)/shard_map/ppermute | solution.py:217
  17.0 2.5 %collective-permute-start.9 = (bf16[32,512]{1,0:T(8,128)(2,1)S(1)}, bf16[32,512]{1,0:T(8,128)(2,1)S(1)}, u32[]{:S(2)}, u32[]{:S(2)}) collective-permute-start(bf16[32,512]{1,0:T(8,128)(2,1)S(1)} %get-tuple-element.139), channel_id=1, source_target_pairs={{0,12},{4,8},{8,4},{12,0},{1,13},{5,9},{9,5},{13,1},{2,14},{6,10},... | collective-permute-start | bytes 98312 | tf_op jit(solution)/shard_map/ppermute | solution.py:214
  19.5 1.9 %forward_local.1 = (f32[256,512]{1,0:T(8,128)S(1)}, bf16[6,256,512]{2,1,0:T(8,128)(2,1)S(1)}, f32[40,512]{1,0:T(8,128)S(1)}, bf16[40,512]{1,0:T(8,128)(2,1)S(1)}) custom-call(bf16[256,512]{1,0:T(8,128)(2,1)S(1)} %get-tuple-element.140.state_ref.refs_7_.refs_10_, bf16[2,512,512]{2,1,0:T(8,128)(2,1)S(1)} %copy-done, bf16[2,512,512]{2,1,0:T(8,128)(2,1)S(1)} %copy-done.2, ...), custom_call_target="tpu_custom_call" | custom-call | flops 805306368 | bytes 4593824 | tf_op jit(solution)/shard_map/forward_local/pallas_call | solution.py:198
  23.7 1.5 %collective-permute-start.11 = (bf16[16,512]{1,0:T(8,128)(2,1)S(1)}, bf16[16,512]{1,0:T(8,128)(2,1)S(1)}, u32[]{:S(2)}, u32[]{:S(2)}) collective-permute-start(bf16[16,512]{1,0:T(8,128)(2,1)S(1)} %get-tuple-element.146), channel_id=1, source_target_pairs={{0,2},{1,3},{2,0},{3,1},{4,6},{5,7},{6,4},{7,5},{8,10},{9,11},{10,... | collective-permute-start | bytes 49160 | tf_op jit(solution)/shard_map/ppermute | solution.py:217
  26.2 2.5 %collective-permute-start.14 = (bf16[16,512]{1,0:T(8,128)(2,1)S(1)}, bf16[16,512]{1,0:T(8,128)(2,1)S(1)}, u32[]{:S(2)}, u32[]{:S(2)}) collective-permute-start(bf16[16,512]{1,0:T(8,128)(2,1)S(1)} %get-tuple-element.149), channel_id=1, source_target_pairs={{0,12},{4,8},{8,4},{12,0},{1,13},{5,9},{9,5},{13,1},{2,14},{6,10},... | collective-permute-start | bytes 49160 | tf_op jit(solution)/shard_map/ppermute | solution.py:214
  28.7 3.0 %turn_local.1 = (f32[256,512]{1,0:T(8,128)S(1)}, f32[256,512]{1,0:T(8,128)S(1)}, f32[256,512]{1,0:T(8,128)S(1)}, f32[40,512]{1,0:T(8,128)S(1)}, bf16[40,512]{1,0...) custom-call(bf16[256,512]{1,0:T(8,128)(2,1)S(1)} %get-tuple-element., ...), custom_call_target="tpu_custom_call" | custom-call | flops 1342177280 | bytes 5871776 | tf_op jit(solution)/shard_map/turn_local/pallas_call | solution.py:198
  33.2 1.6 %collective-permute-start.16 = (bf16[8,512]{1,0:T(8,128)(2,1)S(1)}, bf16[8,512]{1,0:T(8,128)(2,1)S(1)}, u32[]{:S(2)}, u32[]{:S(2)}) collective-permute-start(bf16[8,512]{1,0:T(8,128)(2,1)S(1)} %get-tuple-element.177), channel_id=1, source_target_pairs={{0,2},{1,3},{2,0},{3,1},{4,6},{5,7},{6,4},{7,5},{8,10},{9,11},{10,... | collective-permute-start | bytes 24584 | tf_op jit(solution)/shard_map/ppermute | solution.py:217
  35.5 2.0 %collective-permute-start.19 = (bf16[8,512]{1,0:T(8,128)(2,1)S(1)}, bf16[8,512]{1,0:T(8,128)(2,1)S(1)}, u32[]{:S(2)}, u32[]{:S(2)}) collective-permute-start(bf16[8,512]{1,0:T(8,128)(2,1)S(1)} %get-tuple-element.180), channel_id=1, source_target_pairs={{0,12},{4,8},{8,4},{12,0},{1,13},{5,9},{9,5},{13,1},{2,14},{6,10},... | collective-permute-start | bytes 24584 | tf_op jit(solution)/shard_map/ppermute | solution.py:214
  37.5 2.7 %back_local.1 = (f32[256,512]{1,0:T(8,128)S(1)}, bf16[1024,512]{1,0:T(8,128)(2,1)S(1)}, bf16[1024,512]{1,0:T(8,128)(2,1)S(1)}) custom-call(s32[6,6]{1,0:T(8,128)S(1)} %get-tuple-element.122.refs_0_.refs_5_, bf16[256,512]{1,0:T(8,128)(2,1)S(1)} %get-tuple-element.167.refs_1_, bf16[6,256,512]{2,1,0:T(8,128)(2,1)S(1)} %get-tuple-element.168.refs_2_, ...), custom_call_target="tpu_custom_call" | custom-call | flops 1342177280 | bytes 8566928 | tf_op jit(solution)/shard_map/back_local/pallas_call | solution.py:198
  42.3 2.1 %collective-permute-done.29.refs_2_ = bf16[1024,512]{1,0:T(8,128)(2,1)S(1)} collective-permute-done((bf16[1024,512]{1,0:T(8,128)(2,1)S(1)}, bf16[1024,512]{1,0:T(8,128)(2,1)S(1)}, u32[]{:S(2)}, u32[]{:S(2)}) %collective-permute-start.29) | collective-permute-done | bytes 1048608 | tf_op jit(solution)/shard_map/ppermute | solution.py:162
  45.3 1.6 %collective-permute-start.30 = (bf16[512,512]{1,0:T(8,128)(2,1)S(1)}, bf16[512,512]{1,0:T(8,128)(2,1)S(1)}, u32[]{:S(2)}, u32[]{:S(2)}) collective-permute-start(bf16[512,512]{1,0:T(8,128)(2,1)S(1)} %get-tuple-element.209), channel_id=1, source_target_pairs={{0,2},{1,3},{2,0},{3,1},{4,6},{5,7},{6,4},{7,5},{8,10},{9,11},{10,... | collective-permute-start | bytes 1572872 | tf_op jit(solution)/shard_map/ppermute | solution.py:162
  47.8 1.7 %embed_back.1 = (bf16[512,512]{1,0:T(8,128)(2,1)S(1)}, bf16[256,512]{1,0:T(8,128)(2,1)S(1)}, bf16[256,512]{1,0:T(8,128)(2,1)S(1)}, bf16[16,512]{1,0:T(8,128)(2,1...) custom-call(bf16[8,512]{1,0:T(8,128)(2,1)S(1)} %collective-permute-d, ...), custom_call_target="tpu_custom_call" | custom-call | flops 805306368 | bytes 6097840 | tf_op jit(solution)/shard_map/embed_back/pallas_call | solution.py:198
  49.6 10.5 %collective-permute-done.30.refs_2_ = bf16[512,512]{1,0:T(8,128)(2,1)S(1)} collective-permute-done((bf16[512,512]{1,0:T(8,128)(2,1)S(1)}, bf16[512,512]{1,0:T(8,128)(2,1)S(1)}, u32[]{:S(2)}, u32[]{:S(2)}) %collective-permute-start.30) | collective-permute-done | bytes 524320 | tf_op jit(solution)/shard_map/ppermute | solution.py:162
  61.5 6.2 %collective-permute-done.26.refs_2_ = bf16[384,512]{1,0:T(8,128)(2,1)S(1)} collective-permute-done((bf16[384,512]{1,0:T(8,128)(2,1)S(1)}, bf16[384,512]{1,0:T(8,128)(2,1)S(1)}, u32[]{:S(2)}, u32[]{:S(2)}) %collective-permute-start.26) | collective-permute-done | bytes 393248 | tf_op jit(solution)/shard_map/ppermute | solution.py:162
  69.3 1.6 %collective-permute-start.34 = (bf16[128,512]{1,0:T(8,128)(2,1)S(1)}, bf16[128,512]{1,0:T(8,128)(2,1)S(1)}, u32[]{:S(2)}, u32[]{:S(2)}) collective-permute-start(bf16[128,512]{1,0:T(8,128)(2,1)S(1)} %get-tuple-element.217), channel_id=1, source_target_pairs={{0,2},{1,3},{2,0},{3,1},{4,6},{5,7},{6,4},{7,5},{8,10},{9,11},{10,... | collective-permute-start | bytes 393224 | tf_op jit(solution)/shard_map/ppermute | solution.py:162
  72.4 1.9 %collective-permute-done.34.refs_2_ = bf16[128,512]{1,0:T(8,128)(2,1)S(1)} collective-permute-done((bf16[128,512]{1,0:T(8,128)(2,1)S(1)}, bf16[128,512]{1,0:T(8,128)(2,1)S(1)}, u32[]{:S(2)}, u32[]{:S(2)}) %collective-permute-start.34) | collective-permute-done | bytes 131104 | tf_op jit(solution)/shard_map/ppermute | solution.py:162
  75.6 1.6 %collective-permute-start.28 = (bf16[96,512]{1,0:T(8,128)(2,1)S(1)}, bf16[96,512]{1,0:T(8,128)(2,1)S(1)}, u32[]{:S(2)}, u32[]{:S(2)}) collective-permute-start(bf16[96,512]{1,0:T(8,128)(2,1)S(1)} %get-tuple-element.205), channel_id=1, source_target_pairs={{0,8},{1,9},{2,10},{3,11},{4,12},{5,13},{6,14},{7,15},{8,0},{9,1},... | collective-permute-start | bytes 294920 | tf_op jit(solution)/shard_map/ppermute | solution.py:162
  77.2 2.1 %collective-permute-start.21 = (bf16[16,512]{1,0:T(8,128)(2,1)S(1)}, bf16[16,512]{1,0:T(8,128)(2,1)S(1)}, u32[]{:S(2)}, u32[]{:S(2)}) collective-permute-start(bf16[16,512]{1,0:T(8,128)(2,1)S(1)} %get-tuple-element.192), channel_id=1, source_target_pairs={{0,2},{1,3},{2,0},{3,1},{4,6},{5,7},{6,4},{7,5},{8,10},{9,11},{10,... | collective-permute-start | bytes 49160 | tf_op jit(solution)/shard_map/ppermute | solution.py:217
  81.0 2.9 %collective-permute-start.23 = (bf16[16,512]{1,0:T(8,128)(2,1)S(1)}, bf16[16,512]{1,0:T(8,128)(2,1)S(1)}, u32[]{:S(2)}, u32[]{:S(2)}) collective-permute-start(bf16[16,512]{1,0:T(8,128)(2,1)S(1)} %get-tuple-element.194), channel_id=1, source_target_pairs={{0,4},{4,0},{8,12},{12,8},{1,5},{5,1},{9,13},{13,9},{2,6},{6,2},{1... | collective-permute-start | bytes 49160 | tf_op jit(solution)/shard_map/ppermute | solution.py:215
  85.6 3.8 %collective-permute-done.24.refs_4_ = bf16[16,512]{1,0:T(8,128)(2,1)S(1)} collective-permute-done((bf16[16,512]{1,0:T(8,128)(2,1)S(1)}, bf16[16,512]{1,0:T(8,128)(2,1)S(1)}, u32[]{:S(2)}, u32[]{:S(2)}) %collective-permute-start.24) | collective-permute-done | bytes 16416 | tf_op jit(solution)/shard_map/ppermute | solution.py:214
  (82 shorter events, 26.5 us)
Async XLA Ops:
  3.6 9.6 %collective-permute-start = (bf16[16,512]{1,0:T(8,128)(2,1)S(1)}, bf16[16,512]{1,0:T(8,128)(2,1)S(1)}, u32[]{:S(2)}, u32[]{:S(2)}) collective-permute-start(bf16[16,512]{1,0:T(8,128)(2,1)S(1)} %get-tuple-element.123), channel_id=1, source_target_pairs={{0,1},{1,0},{2,3},{3,2},{4,5},{5,4},{6,7},{7,6},{8,9},{9,8},{10,11... | collective-permute-start | bytes 49160 | tf_op jit(solution)/shard_map/ppermute | solution.py:217
  4.1 9.1 %collective-permute-start.1 = (bf16[16,512]{1,0:T(8,128)(2,1)S(1)}, bf16[16,512]{1,0:T(8,128)(2,1)S(1)}, u32[]{:S(2)}, u32[]{:S(2)}) collective-permute-start(bf16[16,512]{1,0:T(8,128)(2,1)S(1)} %get-tuple-element.124), channel_id=1, source_target_pairs={{0,2},{1,3},{2,0},{3,1},{4,6},{5,7},{6,4},{7,5},{8,10},{9,11},{10,... | collective-permute-start | bytes 49160 | tf_op jit(solution)/shard_map/ppermute | solution.py:217
  6.7 6.5 %collective-permute-start.2 = (bf16[16,512]{1,0:T(8,128)(2,1)S(1)}, bf16[16,512]{1,0:T(8,128)(2,1)S(1)}, u32[]{:S(2)}, u32[]{:S(2)}) collective-permute-start(bf16[16,512]{1,0:T(8,128)(2,1)S(1)} %get-tuple-element.125), channel_id=1, source_target_pairs={{0,3},{1,2},{2,1},{3,0},{4,7},{5,6},{6,5},{7,4},{8,11},{9,10},{10,... | collective-permute-start | bytes 49160 | tf_op jit(solution)/shard_map/ppermute | solution.py:217
  6.8 6.4 %collective-permute-start.3 = (bf16[16,512]{1,0:T(8,128)(2,1)S(1)}, bf16[16,512]{1,0:T(8,128)(2,1)S(1)}, u32[]{:S(2)}, u32[]{:S(2)}) collective-permute-start(bf16[16,512]{1,0:T(8,128)(2,1)S(1)} %get-tuple-element.126), channel_id=1, source_target_pairs={{0,4},{4,0},{8,12},{12,8},{1,5},{5,1},{9,13},{13,9},{2,6},{6,2},{1... | collective-permute-start | bytes 49160 | tf_op jit(solution)/shard_map/ppermute | solution.py:215
  15.0 6.4 %collective-permute-start.5 = (bf16[32,512]{1,0:T(8,128)(2,1)S(1)}, bf16[32,512]{1,0:T(8,128)(2,1)S(1)}, u32[]{:S(2)}, u32[]{:S(2)}) collective-permute-start(bf16[32,512]{1,0:T(8,128)(2,1)S(1)} %get-tuple-element.135), channel_id=1, source_target_pairs={{0,1},{1,0},{2,3},{3,2},{4,5},{5,4},{6,7},{7,6},{8,9},{9,8},{10,11... | collective-permute-start | bytes 98312 | tf_op jit(solution)/shard_map/ppermute | solution.py:217
  15.1 6.3 %collective-permute-start.6 = (bf16[32,512]{1,0:T(8,128)(2,1)S(1)}, bf16[32,512]{1,0:T(8,128)(2,1)S(1)}, u32[]{:S(2)}, u32[]{:S(2)}) collective-permute-start(bf16[32,512]{1,0:T(8,128)(2,1)S(1)} %get-tuple-element.136), channel_id=1, source_target_pairs={{0,2},{1,3},{2,0},{3,1},{4,6},{5,7},{6,4},{7,5},{8,10},{9,11},{10,... | collective-permute-start | bytes 98312 | tf_op jit(solution)/shard_map/ppermute | solution.py:217
  23.7 8.0 %collective-permute-start.10 = (bf16[16,512]{1,0:T(8,128)(2,1)S(1)}, bf16[16,512]{1,0:T(8,128)(2,1)S(1)}, u32[]{:S(2)}, u32[]{:S(2)}) collective-permute-start(bf16[16,512]{1,0:T(8,128)(2,1)S(1)} %get-tuple-element.145), channel_id=1, source_target_pairs={{0,1},{1,0},{2,3},{3,2},{4,5},{5,4},{6,7},{7,6},{8,9},{9,8},{10,11... | collective-permute-start | bytes 49160 | tf_op jit(solution)/shard_map/ppermute | solution.py:217
  23.7 7.9 %collective-permute-start.11 = (bf16[16,512]{1,0:T(8,128)(2,1)S(1)}, bf16[16,512]{1,0:T(8,128)(2,1)S(1)}, u32[]{:S(2)}, u32[]{:S(2)}) collective-permute-start(bf16[16,512]{1,0:T(8,128)(2,1)S(1)} %get-tuple-element.146), channel_id=1, source_target_pairs={{0,2},{1,3},{2,0},{3,1},{4,6},{5,7},{6,4},{7,5},{8,10},{9,11},{10,... | collective-permute-start | bytes 49160 | tf_op jit(solution)/shard_map/ppermute | solution.py:217
  25.3 6.4 %collective-permute-start.12 = (bf16[16,512]{1,0:T(8,128)(2,1)S(1)}, bf16[16,512]{1,0:T(8,128)(2,1)S(1)}, u32[]{:S(2)}, u32[]{:S(2)}) collective-permute-start(bf16[16,512]{1,0:T(8,128)(2,1)S(1)} %get-tuple-element.147), channel_id=1, source_target_pairs={{0,3},{1,2},{2,1},{3,0},{4,7},{5,6},{6,5},{7,4},{8,11},{9,10},{10,... | collective-permute-start | bytes 49160 | tf_op jit(solution)/shard_map/ppermute | solution.py:217
  25.6 6.1 %collective-permute-start.13 = (bf16[16,512]{1,0:T(8,128)(2,1)S(1)}, bf16[16,512]{1,0:T(8,128)(2,1)S(1)}, u32[]{:S(2)}, u32[]{:S(2)}) collective-permute-start(bf16[16,512]{1,0:T(8,128)(2,1)S(1)} %get-tuple-element.148), channel_id=1, source_target_pairs={{0,4},{4,0},{8,12},{12,8},{1,5},{5,1},{9,13},{13,9},{2,6},{6,2},{1... | collective-permute-start | bytes 49160 | tf_op jit(solution)/shard_map/ppermute | solution.py:215
  33.1 8.6 %collective-permute-start.15 = (bf16[8,512]{1,0:T(8,128)(2,1)S(1)}, bf16[8,512]{1,0:T(8,128)(2,1)S(1)}, u32[]{:S(2)}, u32[]{:S(2)}) collective-permute-start(bf16[8,512]{1,0:T(8,128)(2,1)S(1)} %get-tuple-element.176), channel_id=1, source_target_pairs={{0,1},{1,0},{2,3},{3,2},{4,5},{5,4},{6,7},{7,6},{8,9},{9,8},{10,11... | collective-permute-start | bytes 24584 | tf_op jit(solution)/shard_map/ppermute | solution.py:217
  33.2 8.5 %collective-permute-start.16 = (bf16[8,512]{1,0:T(8,128)(2,1)S(1)}, bf16[8,512]{1,0:T(8,128)(2,1)S(1)}, u32[]{:S(2)}, u32[]{:S(2)}) collective-permute-start(bf16[8,512]{1,0:T(8,128)(2,1)S(1)} %get-tuple-element.177), channel_id=1, source_target_pairs={{0,2},{1,3},{2,0},{3,1},{4,6},{5,7},{6,4},{7,5},{8,10},{9,11},{10,... | collective-permute-start | bytes 24584 | tf_op jit(solution)/shard_map/ppermute | solution.py:217
  34.7 7.0 %collective-permute-start.17 = (bf16[8,512]{1,0:T(8,128)(2,1)S(1)}, bf16[8,512]{1,0:T(8,128)(2,1)S(1)}, u32[]{:S(2)}, u32[]{:S(2)}) collective-permute-start(bf16[8,512]{1,0:T(8,128)(2,1)S(1)} %get-tuple-element.178), channel_id=1, source_target_pairs={{0,3},{1,2},{2,1},{3,0},{4,7},{5,6},{6,5},{7,4},{8,11},{9,10},{10,... | collective-permute-start | bytes 24584 | tf_op jit(solution)/shard_map/ppermute | solution.py:217
  35.0 6.7 %collective-permute-start.18 = (bf16[8,512]{1,0:T(8,128)(2,1)S(1)}, bf16[8,512]{1,0:T(8,128)(2,1)S(1)}, u32[]{:S(2)}, u32[]{:S(2)}) collective-permute-start(bf16[8,512]{1,0:T(8,128)(2,1)S(1)} %get-tuple-element.179), channel_id=1, source_target_pairs={{0,4},{4,0},{8,12},{12,8},{1,5},{5,1},{9,13},{13,9},{2,6},{6,2},{1... | collective-permute-start | bytes 24584 | tf_op jit(solution)/shard_map/ppermute | solution.py:215
  35.5 6.2 %collective-permute-start.19 = (bf16[8,512]{1,0:T(8,128)(2,1)S(1)}, bf16[8,512]{1,0:T(8,128)(2,1)S(1)}, u32[]{:S(2)}, u32[]{:S(2)}) collective-permute-start(bf16[8,512]{1,0:T(8,128)(2,1)S(1)} %get-tuple-element.180), channel_id=1, source_target_pairs={{0,12},{4,8},{8,4},{12,0},{1,13},{5,9},{9,5},{13,1},{2,14},{6,10},... | collective-permute-start | bytes 24584 | tf_op jit(solution)/shard_map/ppermute | solution.py:214
  45.3 14.8 %collective-permute-start.30 = (bf16[512,512]{1,0:T(8,128)(2,1)S(1)}, bf16[512,512]{1,0:T(8,128)(2,1)S(1)}, u32[]{:S(2)}, u32[]{:S(2)}) collective-permute-start(bf16[512,512]{1,0:T(8,128)(2,1)S(1)} %get-tuple-element.209), channel_id=1, source_target_pairs={{0,2},{1,3},{2,0},{3,1},{4,6},{5,7},{6,4},{7,5},{8,10},{9,11},{10,... | collective-permute-start | bytes 1572872 | tf_op jit(solution)/shard_map/ppermute | solution.py:162
  47.2 20.5 %collective-permute-start.26 = (bf16[384,512]{1,0:T(8,128)(2,1)S(1)}, bf16[384,512]{1,0:T(8,128)(2,1)S(1)}, u32[]{:S(2)}, u32[]{:S(2)}) collective-permute-start(bf16[384,512]{1,0:T(8,128)(2,1)S(1)} %get-tuple-element.201), channel_id=1, source_target_pairs={{0,2},{1,3},{2,0},{3,1},{4,6},{5,7},{6,4},{7,5},{8,10},{9,11},{10,... | collective-permute-start | bytes 1179656 | tf_op jit(solution)/shard_map/ppermute | solution.py:162
  49.6 19.5 %collective-permute-start.33 = (bf16[256,512]{1,0:T(8,128)(2,1)S(1)}, bf16[256,512]{1,0:T(8,128)(2,1)S(1)}, u32[]{:S(2)}, u32[]{:S(2)}) collective-permute-start(bf16[256,512]{1,0:T(8,128)(2,1)S(1)} %get-tuple-element.215), channel_id=1, source_target_pairs={{0,1},{1,0},{2,3},{3,2},{4,5},{5,4},{6,7},{7,6},{8,9},{9,8},{10,11... | collective-permute-start | bytes 786440 | tf_op jit(solution)/shard_map/ppermute | solution.py:162
  60.3 10.5 %collective-permute-start.31 = (bf16[256,512]{1,0:T(8,128)(2,1)S(1)}, bf16[256,512]{1,0:T(8,128)(2,1)S(1)}, u32[]{:S(2)}, u32[]{:S(2)}) collective-permute-start(bf16[256,512]{1,0:T(8,128)(2,1)S(1)} %get-tuple-element.211), channel_id=1, source_target_pairs={{0,4},{1,5},{2,6},{3,7},{4,0},{5,1},{6,2},{7,3},{8,12},{9,13},{10,... | collective-permute-start | bytes 786440 | tf_op jit(solution)/shard_map/ppermute | solution.py:162
  67.9 7.5 %collective-permute-start.27 = (bf16[192,512]{1,0:T(8,128)(2,1)S(1)}, bf16[192,512]{1,0:T(8,128)(2,1)S(1)}, u32[]{:S(2)}, u32[]{:S(2)}) collective-permute-start(bf16[192,512]{1,0:T(8,128)(2,1)S(1)} %get-tuple-element.203), channel_id=1, source_target_pairs={{0,4},{1,5},{2,6},{3,7},{4,0},{5,1},{6,2},{7,3},{8,12},{9,13},{10,... | collective-permute-start | bytes 589832 | tf_op jit(solution)/shard_map/ppermute | solution.py:162
  71.0 19.8 %collective-permute-start.32 = (bf16[128,512]{1,0:T(8,128)(2,1)S(1)}, bf16[128,512]{1,0:T(8,128)(2,1)S(1)}, u32[]{:S(2)}, u32[]{:S(2)}) collective-permute-start(bf16[128,512]{1,0:T(8,128)(2,1)S(1)} %get-tuple-element.213), channel_id=1, source_target_pairs={{0,8},{1,9},{2,10},{3,11},{4,12},{5,13},{6,14},{7,15},{8,0},{9,1},... | collective-permute-start | bytes 393224 | tf_op jit(solution)/shard_map/ppermute | solution.py:162
  74.4 9.5 %collective-permute-start.35 = (bf16[64,512]{1,0:T(8,128)(2,1)S(1)}, bf16[64,512]{1,0:T(8,128)(2,1)S(1)}, u32[]{:S(2)}, u32[]{:S(2)}) collective-permute-start(bf16[64,512]{1,0:T(8,128)(2,1)S(1)} %get-tuple-element.219), channel_id=1, source_target_pairs={{0,4},{1,5},{2,6},{3,7},{4,0},{5,1},{6,2},{7,3},{8,12},{9,13},{10,... | collective-permute-start | bytes 196616 | tf_op jit(solution)/shard_map/ppermute | solution.py:162
  75.6 15.2 %collective-permute-start.28 = (bf16[96,512]{1,0:T(8,128)(2,1)S(1)}, bf16[96,512]{1,0:T(8,128)(2,1)S(1)}, u32[]{:S(2)}, u32[]{:S(2)}) collective-permute-start(bf16[96,512]{1,0:T(8,128)(2,1)S(1)} %get-tuple-element.205), channel_id=1, source_target_pairs={{0,8},{1,9},{2,10},{3,11},{4,12},{5,13},{6,14},{7,15},{8,0},{9,1},... | collective-permute-start | bytes 294920 | tf_op jit(solution)/shard_map/ppermute | solution.py:162
  79.3 6.0 %collective-permute-start.22 = (bf16[16,512]{1,0:T(8,128)(2,1)S(1)}, bf16[16,512]{1,0:T(8,128)(2,1)S(1)}, u32[]{:S(2)}, u32[]{:S(2)}) collective-permute-start(bf16[16,512]{1,0:T(8,128)(2,1)S(1)} %get-tuple-element.193), channel_id=1, source_target_pairs={{0,3},{1,2},{2,1},{3,0},{4,7},{5,6},{6,5},{7,4},{8,11},{9,10},{10,... | collective-permute-start | bytes 49160 | tf_op jit(solution)/shard_map/ppermute | solution.py:217
  (16 other events, 80.7 us)

commit v6 on v5

--- a/solution.py
+++ b/solution.py
@@ -162,18 +162,50 @@
     return lax.ppermute(block, GROUP, [(i, i ^ (1 << bit)) for i in range(total)])
 
 
-def scatter_halving(keep, give, place, dims):
-    width = keep.shape[1]
+def halve_step(bit, keep, arrived, place):
+    rows, width = keep.shape[0] // 2, keep.shape[1]
+    return call(
+        lambda *refs: halve(bit, *refs), "halve", [shape(rows, width)] * 2,
+        (place, keep, arrived), flops=4 * rows * width,
+    )
+
+
+def rest_of_halving(first, keep, give, place, dims):
     bits = (dims[0] * dims[1] * dims[2] - 1).bit_length()
-    arrived = swap(give, 0, dims)
-    for bit in range(1, bits):
-        rows = keep.shape[0] // 2
-        keep, give = call(
-            lambda *refs: halve(bit, *refs), "halve", [shape(rows, width)] * 2,
-            (place, keep, arrived), flops=4 * rows * width,
-        )
+    arrived = swap(give, first, dims)
+    for bit in range(first + 1, bits):
+        keep, give = halve_step(bit, keep, arrived, place)
         arrived = swap(give, bit, dims)
     return keep, arrived
+
+
+def halve_carry(bit, bits_ref, keep_ref, arr_ref, *refs):
+    *own_refs, keep_out, give_out, here_ref, on_ref = refs
+    rows = keep_ref.shape[0]
+    half = rows // 2
+    size = here_ref.shape[0]
+    upper = bits_ref[0:1, 2 + bit : 3 + bit] == 1
+    value = arr_ref[...].astype(F32)
+    first = keep_ref[:half, :].astype(F32) + value[:half]
+    second = keep_ref[half:, :].astype(F32) + value[half:rows]
+    keep_out[...] = low(jnp.where(upper, second, first))
+    here_ref[...] = low(value[rows : rows + size])
+    passed = value[rows + size : rows + 2 * size]
+    on_ref[...] = low(passed)
+    extra = [ref[...].astype(F32) for ref in own_refs]
+    if len(extra) < 2:
+        extra.append(passed)
+    give_out[...] = low(jnp.concatenate([jnp.where(upper, first, second), *extra], axis=0))
+
+
+def carry_step(bit, keep, arrived, own, place, capacity):
+    rows, width = keep.shape[0] // 2, keep.shape[1]
+    return call(
+        lambda *refs: halve_carry(bit, *refs), "halve_carry",
+        [shape(rows, width), shape(rows + min(len(own) + 1, 2) * capacity, width),
+         shape(capacity, width), shape(capacity, width)],
+        (place, keep, arrived, *own), flops=4 * rows * width,
+    )
 
 
 def scatter_plain(blocks, dims):
@@ -217,7 +249,7 @@
         lax.ppermute(parts[r - 1], COLUMN, [(i, i ^ r) for i in range(column)])
         for r in range(column - 1, 0, -1)
     ]
-    return (*arrived[::-1], near, far)
+    return (far, near, *arrived)
 
 
 def shape(*dims, dtype=BF):
@@ -296,7 +328,7 @@
 
 
 def merge_nodes(peers, *refs):
-    arr_refs, refs = refs[:peers], refs[peers:]
+    arr_refs, refs = refs[:peers][::-1], refs[peers:]
     (incoming_ref, embed_ref, local_ref, mesh_ref, weight_ref, bounds_ref, senders_t_ref, cot_ref,
      merged_ref, state_ref, slope_ref, lat_ref, *pay_refs) = refs
     nodes = mesh_ref.shape[0]
@@ -358,7 +390,7 @@
 
 
 def forward_halo(peers, *refs):
-    arr_refs, refs = refs[:peers], refs[peers:]
+    arr_refs, refs = refs[:peers][::-1], refs[peers:]
     (recv_n_ref, total_ref, state_ref, send_ref, update_ref, senders_ref, senders_t_ref,
      bounds_ref, summed_ref, out_ref, pre_ref, rows_ref, back_ref, merged_ref, cot_ref,
      *pay_refs) = refs
@@ -420,7 +452,7 @@
 
 
 def turn_halo(peers, *refs):
-    arr_refs, refs = refs[:peers], refs[peers:]
+    arr_refs, refs = refs[:peers][::-1], refs[peers:]
     (recv_n_ref, sent_b_ref, gsum_n_ref, gsum_r_ref, total_ref, grecv_ref, gsent_ref, cot_ref,
      send_ref, recv_ref, senders_ref, senders_t_ref, bounds_ref, summed_ref, grecv_out_ref,
      gsent_out_ref, gin_ref, *pay_refs) = refs
@@ -465,7 +497,7 @@
 def back_local(
     dims, place_ref, gin_ref, slope_ref, slope_k_ref, slope_d_ref, send_ref, recv_ref, update_ref,
     senders_ref, senders_t_ref, state_ref, rows_ref, summed_ref, merged_ref, merged_r_ref,
-    part_ref, keep_ref, give_ref, gpre_ref,
+    after_ref, part_ref, keep_ref, give_ref, keep2_ref, give2_ref, gpre_ref,
 ):
     nodes = gin_ref.shape[0]
     halo = slope_k_ref.shape[0]
@@ -488,17 +520,20 @@
     state = state_ref[...]
 
     def store(at, value):
-        store_blocks(keep_ref, give_ref, at, 4, value, dims, place_ref)
+        store_blocks(keep_ref, give_ref, at, 2, value, dims, place_ref)
+
+    def store2(at, value):
+        store_blocks(keep2_ref, give2_ref, at, 2, value, dims, place_ref)
 
     store(0, dot(state, gsent, TN) + dot(rows_ref[...], gpre_k, TN))
     store(1, dot(state, grecv, TN))
-    store(2, dot(summed_ref[...], gin, TN))
+    store2(0, dot(summed_ref[...], gin, TN))
     far = low(dot(gpre_k, send_ref[0], NT))
-    store(3, dot(merged_ref[...], low(part), TN) + dot(merged_r_ref[...], far, TN))
-
-
-def embed_back(peers, dims, *refs):
-    arr_refs, refs = refs[:peers], refs[peers:]
+    store2(1, dot(merged_ref[...], low(part), TN) + dot(merged_r_ref[...], far, TN))
+
+
+def embed_back(peers, dims, carry, *refs):
+    arr_refs, refs = refs[:peers][::-1], refs[peers:]
     (place_ref, slope_r_ref, part_ref, update_ref, send_ref, merge_ref, bounds_ref, target_ref,
      sends_ref, incoming_ref, slope_g_ref, slope_a_ref, grid_ref, lat_ref, embed_ref,
      gpre_ref, keep_ref, give_ref, *pay_refs) = refs
@@ -522,32 +557,42 @@
     gpre_ref[...] = gpre_g
     grad = dot(grid_ref[...], gpre_g, TN) + dot(lat_ref[...], gpre_a, TN)
     store_blocks(keep_ref, give_ref, 0, 1, grad, dims, place_ref)
-    store_parts(pay_refs, [dot(gpre_a, embed_ref[...], NT)])
+    rows = dot(gpre_a, embed_ref[...], NT)
+    store_parts(pay_refs, [rows])
+    if carry:
+        size = taken // peers
+        start = keep_ref.shape[0]
+        give_ref[start : start + 2 * size, :] = low(
+            jnp.concatenate([rows[:size], rows[2 * size : 3 * size]], axis=0)
+        )
 
 
 def grid_place(peers, *refs):
-    arr_refs, refs = refs[:peers], refs[peers:]
+    arr_refs, refs = refs[:peers][::-1], refs[peers:]
     gpre_ref, weight_ref, sends_ref, out_ref = refs
     chosen = gpre_ref.shape[0]
     taken = sends_ref.shape[1]
     local = dot(gpre_ref[...], weight_ref[...], NT)
     place = low(hot(sends_ref[...] == iota(chosen, taken, 0)))
-    rows = jnp.concatenate([ref[...] for ref in arr_refs], axis=0)
+    size = taken // peers
+    rows = [ref[...].astype(F32) for ref in arr_refs]
+    rows = low(jnp.concatenate([row[row.shape[0] - size :] for row in rows], axis=0))
     out_ref[...] = low(local + dot(place, rows))
 
 
 def finish(
-    keep1_ref, arr1_ref, keep0_ref, arr0_ref, keep_e_ref, arr_e_ref,
+    keep1_ref, arr1_ref, keep0_ref, arr0_ref, keep2_ref, arr2_ref, keep_e_ref, arr_e_ref,
     embed_ref, merge_ref, send_ref, recv_ref, update_ref,
 ):
     last = keep1_ref[...].astype(F32) + arr1_ref[...].astype(F32)
     first = keep0_ref[...].astype(F32) + arr0_ref[...].astype(F32)
-    embed_ref[...] = keep_e_ref[...].astype(F32) + arr_e_ref[...].astype(F32)
+    second = keep2_ref[...].astype(F32) + arr2_ref[...].astype(F32)
     depth = embed_ref.shape[0]
+    embed_ref[...] = keep_e_ref[...].astype(F32) + arr_e_ref[:depth, :].astype(F32)
     for at, ref in enumerate((send_ref, recv_ref, update_ref)):
-        ref[0] = first[at * depth : (at + 1) * depth]
         ref[1] = last[at * depth : (at + 1) * depth]
-    merge_ref[...] = first[3 * depth :]
+    send_ref[0], recv_ref[0], update_ref[0] = first[:depth], first[depth:], second[:depth]
+    merge_ref[...] = second[depth:]
 
 
 def body(
@@ -564,6 +609,7 @@
     taken = peers * capacity
     total = dims[0] * dims[1] * dims[2]
     bits = (total - 1).bit_length()
+    carry = dims == (4, 2, 2) and fine(width, dims)
     spot = lax.axis_index(GROUP)
     place = [lax.axis_index(COLUMN), lax.axis_index("lon") % 2]
     place += [(spot >> bit) % 2 for bit in range(bits)]
@@ -632,37 +678,67 @@
         blocks_shapes(3, width, width, dims) + [shape(nodes, width)],
         (place, state1, summed1, cot, grecv1, gsent1, update_weight), flops=4 * unit,
     )
-    part0, keep0, give0 = call(
+    part0, keep0, give0, keep2, give2 = call(
         lambda *refs: back_local(dims, *refs), "back_local",
-        [shape(nodes, width, dtype=F32)] + blocks_shapes(4, width, width, dims),
+        [shape(nodes, width, dtype=F32)] + blocks_shapes(2, width, width, dims) * 2,
         (place, gin1, slope0, slope_k0, slope_d0, send_weight, recv_weight, update_weight, senders,
-         senders_t, state0, rows0, summed0, merged, merged_r),
+         senders_t, state0, rows0, summed0, merged, merged_r, give1),
         flops=10 * unit, scratch=[pltpu.VMEM((degree * nodes, width), BF)],
     )
-    give1, give0, *arr4 = lax.optimization_barrier((give1, give0, *arr4))
+    split = fine(width, dims)
+    if split:
+        give1, last = lax.optimization_barrier((give1, arr4[-1]))
+        arr4 = (*arr4[:-1], last)
+        give0, give2, *arr4 = lax.optimization_barrier((give0, give2, *arr4))
+        keep1, give1 = halve_step(1, keep1, swap(give1, 0, dims), place)
+        keep1, *arr4 = lax.optimization_barrier((keep1, *arr4))
+    shapes = blocks_shapes(1, width, width, dims)
+    if carry:
+        shapes[1] = shape(shapes[1].shape[0] + 2 * capacity, width)
     gpre_g, keep_e, give_e, *pay5 = call(
-        lambda *refs: embed_back(peers, dims, *refs), "embed_back",
-        [shape(chosen, width)] + blocks_shapes(1, width, width, dims)
-        + [shape(capacity, width)] * peers,
+        lambda *refs: embed_back(peers, dims, carry, *refs), "embed_back",
+        [shape(chosen, width)] + shapes + [shape(capacity, width)] * peers,
         (*arr4, place, slope_r0, part0, update_weight, send_weight, merge, bounds_row,
          targets, sends, incoming, slope_g, slope_a, grid, lat_a, embed),
         flops=6 * unit,
     )
-    arr5 = exchange(pay5, dims)
+    if carry:
+        arrived = swap(give_e, 0, dims)
+        keep_e, give_e, from_sub, _ = carry_step(1, keep_e, arrived, (pay5[1],), place, capacity)
+    else:
+        arr5 = exchange(pay5, dims)
+    if split:
+        keep0, give0 = halve_step(1, keep0, swap(give0, 0, dims), place)
+        keep2, give2 = halve_step(1, keep2, swap(give2, 0, dims), place)
+        give0, give2, keep_e = lax.optimization_barrier((give0, give2, keep_e))
+    if carry:
+        arrived = swap(give_e, 1, dims)
+        keep_e, give_e, from_lat, from_diag = carry_step(
+            2, keep_e, arrived, pay5[3:], place, capacity
+        )
+        arrived = swap(give_e, 2, dims)
+        keep_e, give_e, from_near, _ = carry_step(3, keep_e, arrived, (), place, capacity)
+        arr_e = swap(give_e, 3, dims)
+        arr5 = (arr_e, from_near, from_diag, from_lat, from_sub)
     (grid_grad,) = call(
         lambda *refs: grid_place(peers, *refs), "grid_place", [shape(chosen, width)],
         (*arr5, gpre_g, embed, sends_row), flops=3 * unit,
     )
     depth = width // total
-    if not fine(width, dims):
-        last, first, embed = (scatter_plain(blocks, dims) for blocks in (keep1, keep0, keep_e))
-        grads = [jnp.stack([first[i], last[i]]) for i in range(3)]
-        return (mesh_out, grid_grad, embed[0], first[3], *grads)
+    if not split:
+        last, first, second, embed = (
+            scatter_plain(blocks, dims) for blocks in (keep1, keep0, keep2, keep_e)
+        )
+        grads = [jnp.stack([a, last[i]]) for i, a in enumerate((first[0], first[1], second[0]))]
+        return (mesh_out, grid_grad, embed[0], second[1], *grads)
+    if not carry:
+        keep_e, arr_e = rest_of_halving(0, keep_e, give_e, place, dims)
     grads = call(
         finish, "finish",
         [shape(depth, width, dtype=F32)] * 2 + [shape(2, depth, width, dtype=F32)] * 3,
-        (*scatter_halving(keep1, give1, place, dims), *scatter_halving(keep0, give0, place, dims),
-         *scatter_halving(keep_e, give_e, place, dims)),
+        (*rest_of_halving(1, keep1, give1, place, dims),
+         *rest_of_halving(1, keep0, give0, place, dims),
+         *rest_of_halving(1, keep2, give2, place, dims), keep_e, arr_e),
         flops=8 * depth * width,
     )
     return (mesh_out, grid_grad, *grads)

time: 91.9 us -> 86.1 us (0.937)
  starting transfers between devices: 39.4 us -> 35.6 us
  waiting for transfers between devices: 27.7 us -> 24.4 us
  Pallas kernels: 21.9 us -> 23.3 us
    ppermute x12 -> x16, starting transfers between devices: 11 us -> 16.8 us  [swap(): return lax.ppermute(block, GROUP, [(i, i ^ 1 << bit) for i in range(total)])]
    ppermute x5 -> x4, waiting for transfers between devices: 6.04 us -> 0.25 us  [exchange(): far = lax.ppermute(parts[column], 'lon', other)]
    ppermute x15 -> x12, starting transfers between devices: 12 us -> 6.88 us  [exchange(): lax.ppermute(parts[r - 1], COLUMN, [(i, i ^ r) for i in range(column)])]
    ppermute x5 -> x4, starting transfers between devices: 5.86 us -> 1.81 us  [exchange(): lax.ppermute(parts[column - 1], 'lon', [(i, i ^ 1) for i in range(count)])]
    ppermute x12 -> x16, waiting for transfers between devices: 20.7 us -> 22.7 us  [swap(): return lax.ppermute(block, GROUP, [(i, i ^ 1 << bit) for i in range(total)])]
    pallas_call x21 -> x24, Pallas kernels: 21.9 us -> 23.3 us  [call(): pl.pallas_call(kernel, out_shape=[shape(*a.shape, dtype=a.dtype) for a in...]
    ppermute x5 -> x4, starting transfers between devices: 10.6 us -> 10 us  [exchange(): far = lax.ppermute(parts[column], 'lon', other)]
  transfers between devices with their start and end apart: 37 -> 36, of which waited for: 8 -> 11; matrix products, arithmetic and copies ran while one was open for 0% -> 0% of each run, Pallas kernels for 18% -> 21%
where the time goes in v6:
time: 86.1 us; the launch traced here: 85.9 us
  starting transfers between devices  35.6 us (41%)
  waiting for transfers between devices  24.4 us (28%)
  Pallas kernels  23.3 us (27%)
  local copies, waits for them, and re-layouts  1.57 us (2%)
  between operations  0.96 us (1%)
    pallas_call x24, Pallas kernels, call(): pl.pallas_call(kernel, out_shape=[shape(*a.shape, dtype=a.dtype) for a in...  23.3 us
    ppermute x16, waiting for transfers between devices, swap(): return lax.ppermute(block, GROUP, [(i, i ^ 1 << bit) for i in range(total)])  22.7 us
    ppermute x16, starting transfers between devices, swap(): return lax.ppermute(block, GROUP, [(i, i ^ 1 << bit) for i in range(total)])  16.8 us
    ppermute x4, starting transfers between devices, exchange(): far = lax.ppermute(parts[column], 'lon', other)  10 us
    ppermute x12, starting transfers between devices, exchange(): lax.ppermute(parts[r - 1], COLUMN, [(i, i ^ r) for i in range(column)])  6.88 us
    ppermute x4, starting transfers between devices, exchange(): lax.ppermute(parts[column - 1], 'lon', [(i, i ^ 1) for i in range(count)])  1.81 us
  transfers between devices with their start and end apart: 36, of which 11 were waited for; matrix products, arithmetic and copies ran while one was open for 0% of the time, Pallas kernels for 21%

profile of v6, /device:TPU:0, one launch (start us, length us, event | category | flops | bytes accessed | tf_op | source)
XLA Modules:
  0.0 85.9 jit_solution(3807752267352041890)
XLA Ops:
  2.3 1.3 %first_payload.1 = (bf16[512,512]{1,0:T(8,128)(2,1)S(1)}, bf16[512,512]{1,0:T(8,128)(2,1)S(1)}, s32[1,512]{1,0:T(1,128)S(1)}, s32[6,256]{1,0:T(8,128)S(1)}, s32[...) custom-call(bf16[512,512]{1,0:T(8,128)(2,1)} %refs_0_.2, ...), custom_call_target="tpu_custom_call" | custom-call | flops 67108864 | bytes 1140112 | tf_op jit(solution)/shard_map/first_payload/pallas_call | solution.py:230
  3.6 5.1 %collective-permute-start = (bf16[16,512]{1,0:T(8,128)(2,1)S(1)}, bf16[16,512]{1,0:T(8,128)(2,1)S(1)}, u32[]{:S(2)}, u32[]{:S(2)}) collective-permute-start(bf16[16,512]{1,0:T(8,128)(2,1)S(1)} %get-tuple-element.144), channel_id=1, source_target_pairs={{0,12},{4,8},{8,4},{12,0},{1,13},{5,9},{9,5},{13,1},{2,14},{6,10},... | collective-permute-start | bytes 49160 | tf_op jit(solution)/shard_map/ppermute | solution.py:246
  10.6 2.1 %embed_local.1 = (bf16[256,512]{1,0:T(8,128)(2,1)S(1)}, bf16[512,512]{1,0:T(8,128)(2,1)S(1)}, bf16[256,512]{1,0:T(8,128)(2,1)S(1)}, f32[256,512]{1,0:T(8,128)S(1...) custom-call(bf16[256,512]{1,0:T(8,128)(2,1)} %refs_0_.3, ...), custom_call_target="tpu_custom_call" | custom-call | flops 402653184 | bytes 3170784 | tf_op jit(solution)/shard_map/embed_local/pallas_call | solution.py:230
  17.8 1.9 %forward_local.1 = (f32[256,512]{1,0:T(8,128)S(1)}, bf16[6,256,512]{2,1,0:T(8,128)(2,1)S(1)}, f32[40,512]{1,0:T(8,128)S(1)}, bf16[40,512]{1,0:T(8,128)(2,1)S(1)}) custom-call(bf16[256,512]{1,0:T(8,128)(2,1)S(1)} %get-tuple-element.161.state_ref.refs_7_.refs_10_, bf16[2,512,512]{2,1,0:T(8,128)(2,1)S(1)} %copy-done, bf16[2,512,512]{2,1,0:T(8,128)(2,1)S(1)} %copy-done.2, ...), custom_call_target="tpu_custom_call" | custom-call | flops 805306368 | bytes 4593824 | tf_op jit(solution)/shard_map/forward_local/pallas_call | solution.py:230
  21.7 2.7 %collective-permute-start.10 = (bf16[16,512]{1,0:T(8,128)(2,1)S(1)}, bf16[16,512]{1,0:T(8,128)(2,1)S(1)}, u32[]{:S(2)}, u32[]{:S(2)}) collective-permute-start(bf16[16,512]{1,0:T(8,128)(2,1)S(1)} %get-tuple-element.166), channel_id=1, source_target_pairs={{0,12},{4,8},{8,4},{12,0},{1,13},{5,9},{9,5},{13,1},{2,14},{6,10},... | collective-permute-start | bytes 49160 | tf_op jit(solution)/shard_map/ppermute | solution.py:246
  26.3 3.0 %turn_local.1 = (f32[256,512]{1,0:T(8,128)S(1)}, f32[256,512]{1,0:T(8,128)S(1)}, f32[256,512]{1,0:T(8,128)S(1)}, f32[40,512]{1,0:T(8,128)S(1)}, bf16[40,512]{1,0...) custom-call(bf16[256,512]{1,0:T(8,128)(2,1)S(1)} %get-tuple-element., ...), custom_call_target="tpu_custom_call" | custom-call | flops 1342177280 | bytes 5871776 | tf_op jit(solution)/shard_map/turn_local/pallas_call | solution.py:230
  29.4 1.4 %turn_halo.1 = (bf16[256,512]{1,0:T(8,128)(2,1)S(1)}, bf16[256,512]{1,0:T(8,128)(2,1)S(1)}, bf16[256,512]{1,0:T(8,128)(2,1)S(1)}, bf16[256,512]{1,0:T(8,128)(2,1...) custom-call(bf16[16,512]{1,0:T(8,128)(2,1)S(1)} %collective-permute-, ...), custom_call_target="tpu_custom_call" | custom-call | flops 402653184 | bytes 5322912 | tf_op jit(solution)/shard_map/turn_halo/pallas_call | solution.py:230
  30.8 1.5 %last_weights.1 = (bf16[768,512]{1,0:T(8,128)(2,1)S(1)}, bf16[768,512]{1,0:T(8,128)(2,1)S(1)}, bf16[256,512]{1,0:T(8,128)(2,1)}) custom-call(s32[6,6]{1,0:T(8,128)S(1)} %get-tuple-element.143.refs_0_.refs_5_, bf16[256,512]{1,0:T(8,128)(2,1)S(1)} %get-tuple-element.165.state_ref.refs_1_, bf16[256,512]{1,0:T(8,128)(2,1)S(1)} %get-tuple-element.183.refs_2_, ...), custom_call_target="tpu_custom_call" | custom-call | flops 536870912 | bytes 4194448 | tf_op jit(solution)/shard_map/last_weights/pallas_call | solution.py:230
  35.0 1.2 %collective-permute-start.18 = (bf16[8,512]{1,0:T(8,128)(2,1)S(1)}, bf16[8,512]{1,0:T(8,128)(2,1)S(1)}, u32[]{:S(2)}, u32[]{:S(2)}) collective-permute-start(bf16[8,512]{1,0:T(8,128)(2,1)S(1)} %get-tuple-element.202), channel_id=1, source_target_pairs={{0,2},{1,3},{2,0},{3,1},{4,6},{5,7},{6,4},{7,5},{8,10},{9,11},{10,... | collective-permute-start | bytes 24584 | tf_op jit(solution)/shard_map/ppermute | solution.py:249
  36.2 2.7 %back_local.1 = (f32[256,512]{1,0:T(8,128)S(1)}, bf16[512,512]{1,0:T(8,128)(2,1)S(1)}, bf16[512,512]{1,0:T(8,128)(2,1)S(1)}, bf16[512,512]{1,0:T(8,128)(2,1)S(1)}, bf16[512,512]{1,0:T(8,128)(2,1)S(1)}) custom-call(s32[6,6]{1,0:T(8,128)S(1)} %get-tuple-element.143.refs_0_.refs_5_, bf16[256,512]{1,0:T(8,128)(2,1)S(1)} %get-tuple-element.187.refs_1_, ...), custom_call_target="tpu_custom_call" | custom-call | flops 1342177280 | bytes 9353360 | tf_op jit(solution)/shard_map/back_local/pallas_call | solution.py:230
  40.4 2.3 %embed_back.1 = (bf16[512,512]{1,0:T(8,128)(2,1)S(1)}, bf16[256,512]{1,0:T(8,128)(2,1)S(1)}, bf16[288,512]{1,0:T(8,128)(2,1)S(1)}, bf16[16,512]{1,0:T(8,128)(2,1...) custom-call(bf16[8,512]{1,0:T(8,128)(2,1)S(1)} %collective-permute-d, ...), custom_call_target="tpu_custom_call" | custom-call | flops 805306368 | bytes 6130608 | tf_op jit(solution)/shard_map/embed_back/pallas_call | solution.py:230
  45.0 1.2 %collective-permute-start.30 = (bf16[256,512]{1,0:T(8,128)(2,1)S(1)}, bf16[256,512]{1,0:T(8,128)(2,1)S(1)}, u32[]{:S(2)}, u32[]{:S(2)}) collective-permute-start(bf16[256,512]{1,0:T(8,128)(2,1)S(1)} %get-tuple-element.252), channel_id=1, source_target_pairs={{0,2},{1,3},{2,0},{3,1},{4,6},{5,7},{6,4},{7,5},{8,10},{9,11},{10,... | collective-permute-start | bytes 786440 | tf_op jit(solution)/shard_map/ppermute | solution.py:162
  47.0 1.2 %collective-permute-start.24 = (bf16[160,512]{1,0:T(8,128)(2,1)S(1)}, bf16[160,512]{1,0:T(8,128)(2,1)S(1)}, u32[]{:S(2)}, u32[]{:S(2)}) collective-permute-start(bf16[160,512]{1,0:T(8,128)(2,1)S(1)} %get-tuple-element.233), channel_id=1, source_target_pairs={{0,2},{1,3},{2,0},{3,1},{4,6},{5,7},{6,4},{7,5},{8,10},{9,11},{10,... | collective-permute-start | bytes 491528 | tf_op jit(solution)/shard_map/ppermute | solution.py:162
  48.2 6.7 %collective-permute-done.27.refs_2_ = bf16[384,512]{1,0:T(8,128)(2,1)S(1)} collective-permute-done((bf16[384,512]{1,0:T(8,128)(2,1)S(1)}, bf16[384,512]{1,0:T(8,128)(2,1)S(1)}, u32[]{:S(2)}, u32[]{:S(2)}) %collective-permute-start.27) | collective-permute-done | bytes 393248 | tf_op jit(solution)/shard_map/ppermute | solution.py:162
  56.1 4.4 %collective-permute-done.30.refs_2_ = bf16[256,512]{1,0:T(8,128)(2,1)S(1)} collective-permute-done((bf16[256,512]{1,0:T(8,128)(2,1)S(1)}, bf16[256,512]{1,0:T(8,128)(2,1)S(1)}, u32[]{:S(2)}, u32[]{:S(2)}) %collective-permute-start.30) | collective-permute-done | bytes 262176 | tf_op jit(solution)/shard_map/ppermute | solution.py:162
  61.7 4.5 %collective-permute-done.33.refs_2_ = bf16[256,512]{1,0:T(8,128)(2,1)S(1)} collective-permute-done((bf16[256,512]{1,0:T(8,128)(2,1)S(1)}, bf16[256,512]{1,0:T(8,128)(2,1)S(1)}, u32[]{:S(2)}, u32[]{:S(2)}) %collective-permute-start.33) | collective-permute-done | bytes 262176 | tf_op jit(solution)/shard_map/ppermute | solution.py:162
  67.3 1.7 %collective-permute-done.24.refs_2_ = bf16[160,512]{1,0:T(8,128)(2,1)S(1)} collective-permute-done((bf16[160,512]{1,0:T(8,128)(2,1)S(1)}, bf16[160,512]{1,0:T(8,128)(2,1)S(1)}, u32[]{:S(2)}, u32[]{:S(2)}) %collective-permute-start.24) | collective-permute-done | bytes 163872 | tf_op jit(solution)/shard_map/ppermute | solution.py:162
  70.3 2.4 %collective-permute-start.29 = (bf16[96,512]{1,0:T(8,128)(2,1)S(1)}, bf16[96,512]{1,0:T(8,128)(2,1)S(1)}, u32[]{:S(2)}, u32[]{:S(2)}) collective-permute-start(bf16[96,512]{1,0:T(8,128)(2,1)S(1)} %get-tuple-element.250), channel_id=1, source_target_pairs={{0,8},{1,9},{2,10},{3,11},{4,12},{5,13},{6,14},{7,15},{8,0},{9,1},... | collective-permute-start | bytes 294920 | tf_op jit(solution)/shard_map/ppermute | solution.py:162
  72.6 2.3 %collective-permute-done.25.refs_2_ = bf16[96,512]{1,0:T(8,128)(2,1)S(1)} collective-permute-done((bf16[96,512]{1,0:T(8,128)(2,1)S(1)}, bf16[96,512]{1,0:T(8,128)(2,1)S(1)}, u32[]{:S(2)}, u32[]{:S(2)}) %collective-permute-start.25) | collective-permute-done | bytes 98336 | tf_op jit(solution)/shard_map/ppermute | solution.py:162
  75.5 1.7 %collective-permute-start.26 = (bf16[48,512]{1,0:T(8,128)(2,1)S(1)}, bf16[48,512]{1,0:T(8,128)(2,1)S(1)}, u32[]{:S(2)}, u32[]{:S(2)}) collective-permute-start(bf16[48,512]{1,0:T(8,128)(2,1)S(1)} %get-tuple-element.238), channel_id=1, source_target_pairs={{0,8},{1,9},{2,10},{3,11},{4,12},{5,13},{6,14},{7,15},{8,0},{9,1},... | collective-permute-start | bytes 147464 | tf_op jit(solution)/shard_map/ppermute | solution.py:162
  77.4 1.3 %collective-permute-start.32 = (bf16[64,512]{1,0:T(8,128)(2,1)S(1)}, bf16[64,512]{1,0:T(8,128)(2,1)S(1)}, u32[]{:S(2)}, u32[]{:S(2)}) collective-permute-start(bf16[64,512]{1,0:T(8,128)(2,1)S(1)} %get-tuple-element.256), channel_id=1, source_target_pairs={{0,8},{1,9},{2,10},{3,11},{4,12},{5,13},{6,14},{7,15},{8,0},{9,1},... | collective-permute-start | bytes 196616 | tf_op jit(solution)/shard_map/ppermute | solution.py:162
  78.8 1.8 %collective-permute-start.35 = (bf16[64,512]{1,0:T(8,128)(2,1)S(1)}, bf16[64,512]{1,0:T(8,128)(2,1)S(1)}, u32[]{:S(2)}, u32[]{:S(2)}) collective-permute-start(bf16[64,512]{1,0:T(8,128)(2,1)S(1)} %get-tuple-element.262), channel_id=1, source_target_pairs={{0,8},{1,9},{2,10},{3,11},{4,12},{5,13},{6,14},{7,15},{8,0},{9,1},... | collective-permute-start | bytes 196616 | tf_op jit(solution)/shard_map/ppermute | solution.py:162
  80.6 1.5 %collective-permute-done.26.refs_0_.arr_e_ref = bf16[48,512]{1,0:T(8,128)(2,1)S(1)} collective-permute-done((bf16[48,512]{1,0:T(8,128)(2,1)S(1)}, bf16[48,512]{1,0:T(8,128)(2,1)S(1)}, u32[]{:S(2)}, u32[]{:S(2)}) %collective-permute-start.26) | collective-permute-done | bytes 49184 | tf_op jit(solution)/shard_map/ppermute | solution.py:162
  82.1 1.4 %grid_place.1 = bf16[512,512]{1,0:T(8,128)(2,1)} custom-call(bf16[48,512]{1,0:T(8,128)(2,1)S(1)} %collective-permute-done.26.refs_0_.arr_e_ref, bf16[16,512]{1,0:T(8,128)(2,1)S(1)} %get-tuple-element.239.refs_1_, bf16[16,512]{1,0:T(8,128)(2,1)S(1)} %get-tuple-element.240.refs_2_, bf16[16,512]{1,0:T(8,128)(2,1)S(1)} %get-tuple-element.241.refs_3_, ...), custom_call_target="tpu_custom_call" | custom-call | flops 402653184 | bytes 1687872 | tf_op jit(solution)/shard_map/grid_place/pallas_call | solution.py:230
  (83 shorter events, 27.8 us)
Async XLA Ops:
  3.6 9.1 %collective-permute-start = (bf16[16,512]{1,0:T(8,128)(2,1)S(1)}, bf16[16,512]{1,0:T(8,128)(2,1)S(1)}, u32[]{:S(2)}, u32[]{:S(2)}) collective-permute-start(bf16[16,512]{1,0:T(8,128)(2,1)S(1)} %get-tuple-element.144), channel_id=1, source_target_pairs={{0,12},{4,8},{8,4},{12,0},{1,13},{5,9},{9,5},{13,1},{2,14},{6,10},... | collective-permute-start | bytes 49160 | tf_op jit(solution)/shard_map/ppermute | solution.py:246
  14.2 5.8 %collective-permute-start.5 = (bf16[32,512]{1,0:T(8,128)(2,1)S(1)}, bf16[32,512]{1,0:T(8,128)(2,1)S(1)}, u32[]{:S(2)}, u32[]{:S(2)}) collective-permute-start(bf16[32,512]{1,0:T(8,128)(2,1)S(1)} %get-tuple-element.156), channel_id=1, source_target_pairs={{0,12},{4,8},{8,4},{12,0},{1,13},{5,9},{9,5},{13,1},{2,14},{6,10},... | collective-permute-start | bytes 98312 | tf_op jit(solution)/shard_map/ppermute | solution.py:246
  15.3 4.7 %collective-permute-start.6 = (bf16[32,512]{1,0:T(8,128)(2,1)S(1)}, bf16[32,512]{1,0:T(8,128)(2,1)S(1)}, u32[]{:S(2)}, u32[]{:S(2)}) collective-permute-start(bf16[32,512]{1,0:T(8,128)(2,1)S(1)} %get-tuple-element.157), channel_id=1, source_target_pairs={{0,4},{4,0},{8,12},{12,8},{1,5},{5,1},{9,13},{13,9},{2,6},{6,2},{1... | collective-permute-start | bytes 98312 | tf_op jit(solution)/shard_map/ppermute | solution.py:247
  21.7 7.6 %collective-permute-start.10 = (bf16[16,512]{1,0:T(8,128)(2,1)S(1)}, bf16[16,512]{1,0:T(8,128)(2,1)S(1)}, u32[]{:S(2)}, u32[]{:S(2)}) collective-permute-start(bf16[16,512]{1,0:T(8,128)(2,1)S(1)} %get-tuple-element.166), channel_id=1, source_target_pairs={{0,12},{4,8},{8,4},{12,0},{1,13},{5,9},{9,5},{13,1},{2,14},{6,10},... | collective-permute-start | bytes 49160 | tf_op jit(solution)/shard_map/ppermute | solution.py:246
  24.4 4.9 %collective-permute-start.11 = (bf16[16,512]{1,0:T(8,128)(2,1)S(1)}, bf16[16,512]{1,0:T(8,128)(2,1)S(1)}, u32[]{:S(2)}, u32[]{:S(2)}) collective-permute-start(bf16[16,512]{1,0:T(8,128)(2,1)S(1)} %get-tuple-element.167), channel_id=1, source_target_pairs={{0,4},{4,0},{8,12},{12,8},{1,5},{5,1},{9,13},{13,9},{2,6},{6,2},{1... | collective-permute-start | bytes 49160 | tf_op jit(solution)/shard_map/ppermute | solution.py:247
  24.4 4.9 %collective-permute-start.12 = (bf16[16,512]{1,0:T(8,128)(2,1)S(1)}, bf16[16,512]{1,0:T(8,128)(2,1)S(1)}, u32[]{:S(2)}, u32[]{:S(2)}) collective-permute-start(bf16[16,512]{1,0:T(8,128)(2,1)S(1)} %get-tuple-element.168), channel_id=1, source_target_pairs={{0,3},{1,2},{2,1},{3,0},{4,7},{5,6},{6,5},{7,4},{8,11},{9,10},{10,... | collective-permute-start | bytes 49160 | tf_op jit(solution)/shard_map/ppermute | solution.py:249
  24.8 4.5 %collective-permute-start.13 = (bf16[16,512]{1,0:T(8,128)(2,1)S(1)}, bf16[16,512]{1,0:T(8,128)(2,1)S(1)}, u32[]{:S(2)}, u32[]{:S(2)}) collective-permute-start(bf16[16,512]{1,0:T(8,128)(2,1)S(1)} %get-tuple-element.169), channel_id=1, source_target_pairs={{0,2},{1,3},{2,0},{3,1},{4,6},{5,7},{6,4},{7,5},{8,10},{9,11},{10,... | collective-permute-start | bytes 49160 | tf_op jit(solution)/shard_map/ppermute | solution.py:249
  32.3 7.6 %collective-permute-start.22 = (bf16[768,512]{1,0:T(8,128)(2,1)S(1)}, bf16[768,512]{1,0:T(8,128)(2,1)S(1)}, u32[]{:S(2)}, u32[]{:S(2)}) collective-permute-start(bf16[768,512]{1,0:T(8,128)(2,1)S(1)} %get-tuple-element.211.refs_15_), channel_id=1, source_target_pairs={{0,1},{1,0},{2,3},{3,2},{4,5},{5,4},{6,7},{7,6},{8,9},{9,8},{10,11... | collective-permute-start | bytes 2359304 | tf_op jit(solution)/shard_map/ppermute | solution.py:162
  32.8 6.1 %collective-permute-start.15 = (bf16[8,512]{1,0:T(8,128)(2,1)S(1)}, bf16[8,512]{1,0:T(8,128)(2,1)S(1)}, u32[]{:S(2)}, u32[]{:S(2)}) collective-permute-start(bf16[8,512]{1,0:T(8,128)(2,1)S(1)} %get-tuple-element.199), channel_id=1, source_target_pairs={{0,12},{4,8},{8,4},{12,0},{1,13},{5,9},{9,5},{13,1},{2,14},{6,10},... | collective-permute-start | bytes 24584 | tf_op jit(solution)/shard_map/ppermute | solution.py:246
  33.9 5.0 %collective-permute-start.16 = (bf16[8,512]{1,0:T(8,128)(2,1)S(1)}, bf16[8,512]{1,0:T(8,128)(2,1)S(1)}, u32[]{:S(2)}, u32[]{:S(2)}) collective-permute-start(bf16[8,512]{1,0:T(8,128)(2,1)S(1)} %get-tuple-element.200), channel_id=1, source_target_pairs={{0,4},{4,0},{8,12},{12,8},{1,5},{5,1},{9,13},{13,9},{2,6},{6,2},{1... | collective-permute-start | bytes 24584 | tf_op jit(solution)/shard_map/ppermute | solution.py:247
  38.9 4.9 %collective-permute-start.20 = (bf16[512,512]{1,0:T(8,128)(2,1)S(1)}, bf16[512,512]{1,0:T(8,128)(2,1)S(1)}, u32[]{:S(2)}, u32[]{:S(2)}) collective-permute-start(bf16[512,512]{1,0:T(8,128)(2,1)S(1)} %get-tuple-element.205), channel_id=1, source_target_pairs={{0,1},{1,0},{2,3},{3,2},{4,5},{5,4},{6,7},{7,6},{8,9},{9,8},{10,11... | collective-permute-start | bytes 1572872 | tf_op jit(solution)/shard_map/ppermute | solution.py:162
  39.7 4.4 %collective-permute-start.21 = (bf16[512,512]{1,0:T(8,128)(2,1)S(1)}, bf16[512,512]{1,0:T(8,128)(2,1)S(1)}, u32[]{:S(2)}, u32[]{:S(2)}) collective-permute-start(bf16[512,512]{1,0:T(8,128)(2,1)S(1)} %get-tuple-element.208), channel_id=1, source_target_pairs={{0,1},{1,0},{2,3},{3,2},{4,5},{5,4},{6,7},{7,6},{8,9},{9,8},{10,11... | collective-permute-start | bytes 1572872 | tf_op jit(solution)/shard_map/ppermute | solution.py:162
  43.0 11.9 %collective-permute-start.27 = (bf16[384,512]{1,0:T(8,128)(2,1)S(1)}, bf16[384,512]{1,0:T(8,128)(2,1)S(1)}, u32[]{:S(2)}, u32[]{:S(2)}) collective-permute-start(bf16[384,512]{1,0:T(8,128)(2,1)S(1)} %get-tuple-element.246), channel_id=1, source_target_pairs={{0,2},{1,3},{2,0},{3,1},{4,6},{5,7},{6,4},{7,5},{8,10},{9,11},{10,... | collective-permute-start | bytes 1179656 | tf_op jit(solution)/shard_map/ppermute | solution.py:162
  45.0 15.5 %collective-permute-start.30 = (bf16[256,512]{1,0:T(8,128)(2,1)S(1)}, bf16[256,512]{1,0:T(8,128)(2,1)S(1)}, u32[]{:S(2)}, u32[]{:S(2)}) collective-permute-start(bf16[256,512]{1,0:T(8,128)(2,1)S(1)} %get-tuple-element.252), channel_id=1, source_target_pairs={{0,2},{1,3},{2,0},{3,1},{4,6},{5,7},{6,4},{7,5},{8,10},{9,11},{10,... | collective-permute-start | bytes 786440 | tf_op jit(solution)/shard_map/ppermute | solution.py:162
  46.2 20.0 %collective-permute-start.33 = (bf16[256,512]{1,0:T(8,128)(2,1)S(1)}, bf16[256,512]{1,0:T(8,128)(2,1)S(1)}, u32[]{:S(2)}, u32[]{:S(2)}) collective-permute-start(bf16[256,512]{1,0:T(8,128)(2,1)S(1)} %get-tuple-element.258), channel_id=1, source_target_pairs={{0,2},{1,3},{2,0},{3,1},{4,6},{5,7},{6,4},{7,5},{8,10},{9,11},{10,... | collective-permute-start | bytes 786440 | tf_op jit(solution)/shard_map/ppermute | solution.py:162
  47.0 22.0 %collective-permute-start.24 = (bf16[160,512]{1,0:T(8,128)(2,1)S(1)}, bf16[160,512]{1,0:T(8,128)(2,1)S(1)}, u32[]{:S(2)}, u32[]{:S(2)}) collective-permute-start(bf16[160,512]{1,0:T(8,128)(2,1)S(1)} %get-tuple-element.233), channel_id=1, source_target_pairs={{0,2},{1,3},{2,0},{3,1},{4,6},{5,7},{6,4},{7,5},{8,10},{9,11},{10,... | collective-permute-start | bytes 491528 | tf_op jit(solution)/shard_map/ppermute | solution.py:162
  55.1 15.0 %collective-permute-start.28 = (bf16[192,512]{1,0:T(8,128)(2,1)S(1)}, bf16[192,512]{1,0:T(8,128)(2,1)S(1)}, u32[]{:S(2)}, u32[]{:S(2)}) collective-permute-start(bf16[192,512]{1,0:T(8,128)(2,1)S(1)} %get-tuple-element.248), channel_id=1, source_target_pairs={{0,4},{1,5},{2,6},{3,7},{4,0},{5,1},{6,2},{7,3},{8,12},{9,13},{10,... | collective-permute-start | bytes 589832 | tf_op jit(solution)/shard_map/ppermute | solution.py:162
  60.7 16.6 %collective-permute-start.31 = (bf16[128,512]{1,0:T(8,128)(2,1)S(1)}, bf16[128,512]{1,0:T(8,128)(2,1)S(1)}, u32[]{:S(2)}, u32[]{:S(2)}) collective-permute-start(bf16[128,512]{1,0:T(8,128)(2,1)S(1)} %get-tuple-element.254), channel_id=1, source_target_pairs={{0,4},{1,5},{2,6},{3,7},{4,0},{5,1},{6,2},{7,3},{8,12},{9,13},{10,... | collective-permute-start | bytes 393224 | tf_op jit(solution)/shard_map/ppermute | solution.py:162
  66.3 12.4 %collective-permute-start.34 = (bf16[128,512]{1,0:T(8,128)(2,1)S(1)}, bf16[128,512]{1,0:T(8,128)(2,1)S(1)}, u32[]{:S(2)}, u32[]{:S(2)}) collective-permute-start(bf16[128,512]{1,0:T(8,128)(2,1)S(1)} %get-tuple-element.260), channel_id=1, source_target_pairs={{0,4},{1,5},{2,6},{3,7},{4,0},{5,1},{6,2},{7,3},{8,12},{9,13},{10,... | collective-permute-start | bytes 393224 | tf_op jit(solution)/shard_map/ppermute | solution.py:162
  69.1 5.8 %collective-permute-start.25 = (bf16[96,512]{1,0:T(8,128)(2,1)S(1)}, bf16[96,512]{1,0:T(8,128)(2,1)S(1)}, u32[]{:S(2)}, u32[]{:S(2)}) collective-permute-start(bf16[96,512]{1,0:T(8,128)(2,1)S(1)} %get-tuple-element.237), channel_id=1, source_target_pairs={{0,4},{1,5},{2,6},{3,7},{4,0},{5,1},{6,2},{7,3},{8,12},{9,13},{10,... | collective-permute-start | bytes 294920 | tf_op jit(solution)/shard_map/ppermute | solution.py:162
  70.3 13.2 %collective-permute-start.29 = (bf16[96,512]{1,0:T(8,128)(2,1)S(1)}, bf16[96,512]{1,0:T(8,128)(2,1)S(1)}, u32[]{:S(2)}, u32[]{:S(2)}) collective-permute-start(bf16[96,512]{1,0:T(8,128)(2,1)S(1)} %get-tuple-element.250), channel_id=1, source_target_pairs={{0,8},{1,9},{2,10},{3,11},{4,12},{5,13},{6,14},{7,15},{8,0},{9,1},... | collective-permute-start | bytes 294920 | tf_op jit(solution)/shard_map/ppermute | solution.py:162
  75.5 6.5 %collective-permute-start.26 = (bf16[48,512]{1,0:T(8,128)(2,1)S(1)}, bf16[48,512]{1,0:T(8,128)(2,1)S(1)}, u32[]{:S(2)}, u32[]{:S(2)}) collective-permute-start(bf16[48,512]{1,0:T(8,128)(2,1)S(1)} %get-tuple-element.238), channel_id=1, source_target_pairs={{0,8},{1,9},{2,10},{3,11},{4,12},{5,13},{6,14},{7,15},{8,0},{9,1},... | collective-permute-start | bytes 147464 | tf_op jit(solution)/shard_map/ppermute | solution.py:162
  77.4 7.0 %collective-permute-start.32 = (bf16[64,512]{1,0:T(8,128)(2,1)S(1)}, bf16[64,512]{1,0:T(8,128)(2,1)S(1)}, u32[]{:S(2)}, u32[]{:S(2)}) collective-permute-start(bf16[64,512]{1,0:T(8,128)(2,1)S(1)} %get-tuple-element.256), channel_id=1, source_target_pairs={{0,8},{1,9},{2,10},{3,11},{4,12},{5,13},{6,14},{7,15},{8,0},{9,1},... | collective-permute-start | bytes 196616 | tf_op jit(solution)/shard_map/ppermute | solution.py:162
  78.8 6.3 %collective-permute-start.35 = (bf16[64,512]{1,0:T(8,128)(2,1)S(1)}, bf16[64,512]{1,0:T(8,128)(2,1)S(1)}, u32[]{:S(2)}, u32[]{:S(2)}) collective-permute-start(bf16[64,512]{1,0:T(8,128)(2,1)S(1)} %get-tuple-element.262), channel_id=1, source_target_pairs={{0,8},{1,9},{2,10},{3,11},{4,12},{5,13},{6,14},{7,15},{8,0},{9,1},... | collective-permute-start | bytes 196616 | tf_op jit(solution)/shard_map/ppermute | solution.py:162
  (15 other events, 57.8 us)

commit v7 on v6

--- a/solution.py
+++ b/solution.py
@@ -166,7 +166,7 @@
     rows, width = keep.shape[0] // 2, keep.shape[1]
     return call(
         lambda *refs: halve(bit, *refs), "halve", [shape(rows, width)] * 2,
-        (place, keep, arrived), flops=4 * rows * width,
+        (place, keep, arrived), flops=4 * rows * width, size=0,
     )
 
 
@@ -204,7 +204,7 @@
         lambda *refs: halve_carry(bit, *refs), "halve_carry",
         [shape(rows, width), shape(rows + min(len(own) + 1, 2) * capacity, width),
          shape(capacity, width), shape(capacity, width)],
-        (place, keep, arrived, *own), flops=4 * rows * width,
+        (place, keep, arrived, *own), flops=4 * rows * width, size=0,
     )
 
 
@@ -219,8 +219,9 @@
     return blocks.astype(F32)
 
 
-def call(kernel, name, outs, args, flops, loads=(), scratch=()):
-    size = sum(a.size * a.dtype.itemsize for a in (*args, *outs, *loads))
+def call(kernel, name, outs, args, flops, loads=(), scratch=(), size=None):
+    if size is None:
+        size = sum(a.size * a.dtype.itemsize for a in (*args, *outs, *loads))
     args = (*(pltpu.with_memory_space_constraint(a, pltpu.HBM) for a in loads), *args)
     scratch = list(scratch)
     if loads:
@@ -266,15 +267,11 @@
     return copies
 
 
-def first_payload(
-    column, capacity, grid_far, embed_far, target_far, senders_far, ints_ref,
-    grid_ref, embed_ref, target_ref, senders_ref, sends_ref, *rest
-):
-    *pay_refs, sems = rest
-    grid_load, *loads = start_loads(
-        (grid_far, embed_far, target_far, senders_far),
-        (grid_ref, embed_ref, target_ref, senders_ref), sems,
-    )
+def first_payload(column, capacity, count, *refs):
+    sources, ints_ref, targets = refs[:count], refs[count], refs[count + 1 : 2 * count + 1]
+    sends_ref, *pay_refs, sems = refs[2 * count + 1 :]
+    grid_ref = targets[0]
+    grid_load, *loads = start_loads(sources, targets, sems)
     chosen = grid_ref.shape[0]
     ints = ints_ref[...]
     base = 2 * capacity + BORDER
@@ -289,12 +286,10 @@
 
 
 def embed_local(
-    column, capacity, mesh_far, merge_far, cot_far, ints_ref, senders_ref, grid_ref, weight_ref,
-    target_ref, sends_ref, mesh_ref, merge_ref, cot_ref,
+    column, capacity, ints_ref, senders_ref, grid_ref, weight_ref, target_ref, sends_ref,
     sum_ref, slope_ref, sends_row_ref, incoming_ref, bounds_ref, bounds_row_ref, senders_t_ref,
-    senders_out_ref, place_ref, sems,
+    senders_out_ref, place_ref,
 ):
-    loads = start_loads((mesh_far, merge_far, cot_far), (mesh_ref, merge_ref, cot_ref), sems)
     chosen = grid_ref.shape[0]
     nodes = sum_ref.shape[0]
     taken = sends_ref.shape[0]
@@ -323,8 +318,6 @@
     senders_t_ref[...] = senders
     filler = jnp.zeros((8 - degree, nodes), I32)
     senders_out_ref[...] = jnp.concatenate([senders, filler], axis=0).T
-    for load in loads:
-        load.wait()
 
 
 def merge_nodes(peers, *refs):
@@ -617,22 +610,21 @@
     ints = jnp.concatenate([send_rows[0], incoming_rows[0], border_mesh_rows[0], place], axis=1)
     unit = 2 * nodes * width * width
 
-    grid, embed, targets, senders_raw, sends, *pay1 = call(
-        lambda *refs: first_payload(column, capacity, *refs), "first_payload",
+    loads = (grid_latent, embed_weight, target_row.reshape(1, chosen), mesh_senders.T,
+             mesh_latent, merge_weight, cotangent)
+    grid, embed, targets, senders_raw, mesh, merge, cot, sends, *pay1 = call(
+        lambda *refs: first_payload(column, capacity, len(loads), *refs), "first_payload",
         [shape(taken, 1, dtype=I32)] + [shape(capacity, width)] * peers,
-        (ints,), flops=unit // 2,
-        loads=(grid_latent, embed_weight, target_row.reshape(1, chosen), mesh_senders.T),
+        (ints,), flops=unit // 2, loads=loads,
     )
     arr1 = exchange(pay1, dims)
-    (mesh, merge, cot, local, slope_g, sends_row, incoming, bounds, bounds_row, senders_t, senders,
-     place) = call(
+    (local, slope_g, sends_row, incoming, bounds, bounds_row, senders_t, senders, place) = call(
         lambda *refs: embed_local(column, capacity, *refs), "embed_local",
         [shape(nodes, width, dtype=F32), shape(chosen, width), shape(1, taken, dtype=I32),
          shape(1, taken, dtype=I32), shape(halo, 1, dtype=I32), shape(1, halo, dtype=I32),
          shape(degree, nodes, dtype=I32), shape(nodes, 8, dtype=I32),
          shape(slots, 2 + bits, dtype=I32)],
         (ints, senders_raw, grid, embed, targets, sends), flops=3 * unit,
-        loads=(mesh_latent, merge_weight, cotangent),
     )
     merged, state0, slope_a, lat_a, *pay2 = call(
         lambda *refs: merge_nodes(peers, *refs), "merge_nodes",
@@ -678,20 +670,22 @@
         blocks_shapes(3, width, width, dims) + [shape(nodes, width)],
         (place, state1, summed1, cot, grecv1, gsent1, update_weight), flops=4 * unit,
     )
+    split = fine(width, dims)
+    if split:
+        give1, last = lax.optimization_barrier((give1, arr4[-1]))
+        arr4 = (*arr4[:-1], last)
+        keep1, give1 = halve_step(1, keep1, swap(give1, 0, dims), place)
     part0, keep0, give0, keep2, give2 = call(
         lambda *refs: back_local(dims, *refs), "back_local",
         [shape(nodes, width, dtype=F32)] + blocks_shapes(2, width, width, dims) * 2,
         (place, gin1, slope0, slope_k0, slope_d0, send_weight, recv_weight, update_weight, senders,
-         senders_t, state0, rows0, summed0, merged, merged_r, give1),
+         senders_t, state0, rows0, summed0, merged, merged_r, keep1),
         flops=10 * unit, scratch=[pltpu.VMEM((degree * nodes, width), BF)],
     )
-    split = fine(width, dims)
     if split:
-        give1, last = lax.optimization_barrier((give1, arr4[-1]))
-        arr4 = (*arr4[:-1], last)
         give0, give2, *arr4 = lax.optimization_barrier((give0, give2, *arr4))
-        keep1, give1 = halve_step(1, keep1, swap(give1, 0, dims), place)
-        keep1, *arr4 = lax.optimization_barrier((keep1, *arr4))
+        keep0, give0 = halve_step(1, keep0, swap(give0, 0, dims), place)
+        keep0, *arr4 = lax.optimization_barrier((keep0, *arr4))
     shapes = blocks_shapes(1, width, width, dims)
     if carry:
         shapes[1] = shape(shapes[1].shape[0] + 2 * capacity, width)
@@ -704,13 +698,15 @@
     )
     if carry:
         arrived = swap(give_e, 0, dims)
+        arrived1 = swap(give1, 1, dims)
+        arrived, arrived1 = lax.optimization_barrier((arrived, arrived1))
+        keep1, give1 = halve_step(2, keep1, arrived1, place)
         keep_e, give_e, from_sub, _ = carry_step(1, keep_e, arrived, (pay5[1],), place, capacity)
     else:
         arr5 = exchange(pay5, dims)
     if split:
-        keep0, give0 = halve_step(1, keep0, swap(give0, 0, dims), place)
+        keep2, keep_e = lax.optimization_barrier((keep2, keep_e))
         keep2, give2 = halve_step(1, keep2, swap(give2, 0, dims), place)
-        give0, give2, keep_e = lax.optimization_barrier((give0, give2, keep_e))
     if carry:
         arrived = swap(give_e, 1, dims)
         keep_e, give_e, from_lat, from_diag = carry_step(
@@ -736,7 +732,7 @@
     grads = call(
         finish, "finish",
         [shape(depth, width, dtype=F32)] * 2 + [shape(2, depth, width, dtype=F32)] * 3,
-        (*rest_of_halving(1, keep1, give1, place, dims),
+        (*rest_of_halving(2, keep1, give1, place, dims),
          *rest_of_halving(1, keep0, give0, place, dims),
          *rest_of_halving(1, keep2, give2, place, dims), keep_e, arr_e),
         flops=8 * depth * width,

time: 86.1 us -> 84 us (0.976)
  waiting for transfers between devices: 24.4 us -> 20.8 us
  starting transfers between devices: 35.6 us -> 37.6 us
    ppermute x16, waiting for transfers between devices: 22.7 us -> 18.7 us  [swap(): return lax.ppermute(block, GROUP, [(i, i ^ 1 << bit) for i in range(total)])]
    ppermute x16, starting transfers between devices: 16.8 us -> 18.9 us  [swap(): return lax.ppermute(block, GROUP, [(i, i ^ 1 << bit) for i in range(total)])]
  transfers between devices with their start and end apart: 36 -> 36, of which waited for: 11 -> 13; matrix products, arithmetic and copies ran while one was open for 0% -> 0% of each run, Pallas kernels for 21% -> 21%
where the time goes in v7:
time: 84 us; the launch traced here: 83.8 us
  starting transfers between devices  37.6 us (45%)
  Pallas kernels  22.8 us (27%)
  waiting for transfers between devices  20.8 us (25%)
  local copies, waits for them, and re-layouts  1.56 us (2%)
  between operations  0.92 us (1%)
    pallas_call x24, Pallas kernels, call(): pl.pallas_call(kernel, out_shape=[shape(*a.shape, dtype=a.dtype) for a in...  22.8 us
    ppermute x16, starting transfers between devices, swap(): return lax.ppermute(block, GROUP, [(i, i ^ 1 << bit) for i in range(total)])  18.9 us
    ppermute x16, waiting for transfers between devices, swap(): return lax.ppermute(block, GROUP, [(i, i ^ 1 << bit) for i in range(total)])  18.7 us
    ppermute x4, starting transfers between devices, exchange(): far = lax.ppermute(parts[column], 'lon', other)  9.87 us
    ppermute x12, starting transfers between devices, exchange(): lax.ppermute(parts[r - 1], COLUMN, [(i, i ^ r) for i in range(column)])  6.88 us
    ppermute x4, starting transfers between devices, exchange(): lax.ppermute(parts[column - 1], 'lon', [(i, i ^ 1) for i in range(count)])  2 us
  transfers between devices with their start and end apart: 36, of which 13 were waited for; matrix products, arithmetic and copies ran while one was open for 0% of the time, Pallas kernels for 21%

profile of v7, /device:TPU:0, one launch (start us, length us, event | category | flops | bytes accessed | tf_op | source)
XLA Modules:
  0.0 83.8 jit_solution(14915211176175841443)
XLA Ops:
  2.3 1.6 %first_payload.1 = (bf16[512,512]{1,0:T(8,128)(2,1)S(1)}, bf16[512,512]{1,0:T(8,128)(2,1)S(1)}, s32[1,512]{1,0:T(1,128)S(1)}, s32[6,256]{1,0:T(8,128)S(1)}, bf16...) custom-call(bf16[512,512]{1,0:T(8,128)(2,1)} %refs_0_.1, ...), custom_call_target="tpu_custom_call" | custom-call | flops 67108864 | bytes 2188688 | tf_op jit(solution)/shard_map/first_payload/pallas_call | solution.py:231
  3.9 5.1 %collective-permute-start = (bf16[16,512]{1,0:T(8,128)(2,1)S(1)}, bf16[16,512]{1,0:T(8,128)(2,1)S(1)}, u32[]{:S(2)}, u32[]{:S(2)}) collective-permute-start(bf16[16,512]{1,0:T(8,128)(2,1)S(1)} %get-tuple-element.145), channel_id=1, source_target_pairs={{0,12},{4,8},{8,4},{12,0},{1,13},{5,9},{9,5},{13,1},{2,14},{6,10},... | collective-permute-start | bytes 49160 | tf_op jit(solution)/shard_map/ppermute | solution.py:247
  16.3 1.5 %collective-permute-start.8 = (bf16[32,512]{1,0:T(8,128)(2,1)S(1)}, bf16[32,512]{1,0:T(8,128)(2,1)S(1)}, u32[]{:S(2)}, u32[]{:S(2)}) collective-permute-start(bf16[32,512]{1,0:T(8,128)(2,1)S(1)} %get-tuple-element.160), channel_id=1, source_target_pairs={{0,2},{1,3},{2,0},{3,1},{4,6},{5,7},{6,4},{7,5},{8,10},{9,11},{10,... | collective-permute-start | bytes 98312 | tf_op jit(solution)/shard_map/ppermute | solution.py:250
  18.1 1.9 %forward_local.1 = (f32[256,512]{1,0:T(8,128)S(1)}, bf16[6,256,512]{2,1,0:T(8,128)(2,1)S(1)}, f32[40,512]{1,0:T(8,128)S(1)}, bf16[40,512]{1,0:T(8,128)(2,1)S(1)}) custom-call(bf16[256,512]{1,0:T(8,128)(2,1)S(1)} %get-tuple-element.162.state_ref.refs_7_.refs_10_, bf16[2,512,512]{2,1,0:T(8,128)(2,1)S(1)} %copy-done, bf16[2,512,512]{2,1,0:T(8,128)(2,1)S(1)} %copy-done.2, ...), custom_call_target="tpu_custom_call" | custom-call | flops 805306368 | bytes 4593824 | tf_op jit(solution)/shard_map/forward_local/pallas_call | solution.py:231
  21.4 2.7 %collective-permute-start.10 = (bf16[16,512]{1,0:T(8,128)(2,1)S(1)}, bf16[16,512]{1,0:T(8,128)(2,1)S(1)}, u32[]{:S(2)}, u32[]{:S(2)}) collective-permute-start(bf16[16,512]{1,0:T(8,128)(2,1)S(1)} %get-tuple-element.167), channel_id=1, source_target_pairs={{0,12},{4,8},{8,4},{12,0},{1,13},{5,9},{9,5},{13,1},{2,14},{6,10},... | collective-permute-start | bytes 49160 | tf_op jit(solution)/shard_map/ppermute | solution.py:247
  26.5 3.0 %turn_local.1 = (f32[256,512]{1,0:T(8,128)S(1)}, f32[256,512]{1,0:T(8,128)S(1)}, f32[256,512]{1,0:T(8,128)S(1)}, f32[40,512]{1,0:T(8,128)S(1)}, bf16[40,512]{1,0...) custom-call(bf16[256,512]{1,0:T(8,128)(2,1)S(1)} %get-tuple-element., ...), custom_call_target="tpu_custom_call" | custom-call | flops 1342177280 | bytes 5871776 | tf_op jit(solution)/shard_map/turn_local/pallas_call | solution.py:231
  29.6 1.4 %turn_halo.1 = (bf16[256,512]{1,0:T(8,128)(2,1)S(1)}, bf16[256,512]{1,0:T(8,128)(2,1)S(1)}, bf16[256,512]{1,0:T(8,128)(2,1)S(1)}, bf16[256,512]{1,0:T(8,128)(2,1...) custom-call(bf16[16,512]{1,0:T(8,128)(2,1)S(1)} %collective-permute-, ...), custom_call_target="tpu_custom_call" | custom-call | flops 402653184 | bytes 5322912 | tf_op jit(solution)/shard_map/turn_halo/pallas_call | solution.py:231
  31.0 1.5 %last_weights.1 = (bf16[768,512]{1,0:T(8,128)(2,1)S(1)}, bf16[768,512]{1,0:T(8,128)(2,1)S(1)}, bf16[256,512]{1,0:T(8,128)(2,1)}) custom-call(s32[6,6]{1,0:T(8,128)S(1)} %get-tuple-element.144.refs_0_.refs_5_, bf16[256,512]{1,0:T(8,128)(2,1)S(1)} %get-tuple-element.166.state_ref.refs_1_, bf16[256,512]{1,0:T(8,128)(2,1)S(1)} %get-tuple-element.184.refs_2_, ...), custom_call_target="tpu_custom_call" | custom-call | flops 536870912 | bytes 4194448 | tf_op jit(solution)/shard_map/last_weights/pallas_call | solution.py:231
  36.4 2.9 %back_local.1 = (f32[256,512]{1,0:T(8,128)S(1)}, bf16[512,512]{1,0:T(8,128)(2,1)S(1)}, bf16[512,512]{1,0:T(8,128)(2,1)S(1)}, bf16[512,512]{1,0:T(8,128)(2,1)S(1)}, bf16[512,512]{1,0:T(8,128)(2,1)S(1)}) custom-call(s32[6,6]{1,0:T(8,128)S(1)} %get-tuple-element.144.refs_0_.refs_5_, bf16[256,512]{1,0:T(8,128)(2,1)S(1)} %get-tuple-element.188.refs_1_, ...), custom_call_target="tpu_custom_call" | custom-call | flops 1342177280 | bytes 8960144 | tf_op jit(solution)/shard_map/back_local/pallas_call | solution.py:231
  41.9 2.3 %embed_back.1 = (bf16[512,512]{1,0:T(8,128)(2,1)S(1)}, bf16[256,512]{1,0:T(8,128)(2,1)S(1)}, bf16[288,512]{1,0:T(8,128)(2,1)S(1)}, bf16[16,512]{1,0:T(8,128)(2,1...) custom-call(bf16[8,512]{1,0:T(8,128)(2,1)S(1)} %collective-permute-d, ...), custom_call_target="tpu_custom_call" | custom-call | flops 805306368 | bytes 6130608 | tf_op jit(solution)/shard_map/embed_back/pallas_call | solution.py:231
  45.8 6.3 %collective-permute-done.23.refs_2_ = bf16[384,512]{1,0:T(8,128)(2,1)S(1)} collective-permute-done((bf16[384,512]{1,0:T(8,128)(2,1)S(1)}, bf16[384,512]{1,0:T(8,128)(2,1)S(1)}, u32[]{:S(2)}, u32[]{:S(2)}) %collective-permute-start.23) | collective-permute-done | bytes 393248 | tf_op jit(solution)/shard_map/ppermute | solution.py:162
  53.0 1.3 %collective-permute-start.33 = (bf16[256,512]{1,0:T(8,128)(2,1)S(1)}, bf16[256,512]{1,0:T(8,128)(2,1)S(1)}, u32[]{:S(2)}, u32[]{:S(2)}) collective-permute-start(bf16[256,512]{1,0:T(8,128)(2,1)S(1)} %get-tuple-element.260), channel_id=1, source_target_pairs={{0,2},{1,3},{2,0},{3,1},{4,6},{5,7},{6,4},{7,5},{8,10},{9,11},{10,... | collective-permute-start | bytes 786440 | tf_op jit(solution)/shard_map/ppermute | solution.py:162
  55.2 1.3 %collective-permute-start.27 = (bf16[192,512]{1,0:T(8,128)(2,1)S(1)}, bf16[192,512]{1,0:T(8,128)(2,1)S(1)}, u32[]{:S(2)}, u32[]{:S(2)}) collective-permute-start(bf16[192,512]{1,0:T(8,128)(2,1)S(1)} %get-tuple-element.248), channel_id=1, source_target_pairs={{0,4},{1,5},{2,6},{3,7},{4,0},{5,1},{6,2},{7,3},{8,12},{9,13},{10,... | collective-permute-start | bytes 589832 | tf_op jit(solution)/shard_map/ppermute | solution.py:162
  57.8 1.3 %collective-permute-start.30 = (bf16[128,512]{1,0:T(8,128)(2,1)S(1)}, bf16[128,512]{1,0:T(8,128)(2,1)S(1)}, u32[]{:S(2)}, u32[]{:S(2)}) collective-permute-start(bf16[128,512]{1,0:T(8,128)(2,1)S(1)} %get-tuple-element.254), channel_id=1, source_target_pairs={{0,4},{1,5},{2,6},{3,7},{4,0},{5,1},{6,2},{7,3},{8,12},{9,13},{10,... | collective-permute-start | bytes 393224 | tf_op jit(solution)/shard_map/ppermute | solution.py:162
  59.2 4.1 %collective-permute-done.33.refs_2_ = bf16[256,512]{1,0:T(8,128)(2,1)S(1)} collective-permute-done((bf16[256,512]{1,0:T(8,128)(2,1)S(1)}, bf16[256,512]{1,0:T(8,128)(2,1)S(1)}, u32[]{:S(2)}, u32[]{:S(2)}) %collective-permute-start.33) | collective-permute-done | bytes 262176 | tf_op jit(solution)/shard_map/ppermute | solution.py:162
  63.5 1.3 %collective-permute-start.34 = (bf16[128,512]{1,0:T(8,128)(2,1)S(1)}, bf16[128,512]{1,0:T(8,128)(2,1)S(1)}, u32[]{:S(2)}, u32[]{:S(2)}) collective-permute-start(bf16[128,512]{1,0:T(8,128)(2,1)S(1)} %get-tuple-element.262), channel_id=1, source_target_pairs={{0,4},{1,5},{2,6},{3,7},{4,0},{5,1},{6,2},{7,3},{8,12},{9,13},{10,... | collective-permute-start | bytes 393224 | tf_op jit(solution)/shard_map/ppermute | solution.py:162
  64.8 1.5 %collective-permute-done.24.refs_2_ = bf16[160,512]{1,0:T(8,128)(2,1)S(1)} collective-permute-done((bf16[160,512]{1,0:T(8,128)(2,1)S(1)}, bf16[160,512]{1,0:T(8,128)(2,1)S(1)}, u32[]{:S(2)}, u32[]{:S(2)}) %collective-permute-start.24) | collective-permute-done | bytes 163872 | tf_op jit(solution)/shard_map/ppermute | solution.py:162
  66.5 1.2 %collective-permute-start.25 = (bf16[96,512]{1,0:T(8,128)(2,1)S(1)}, bf16[96,512]{1,0:T(8,128)(2,1)S(1)}, u32[]{:S(2)}, u32[]{:S(2)}) collective-permute-start(bf16[96,512]{1,0:T(8,128)(2,1)S(1)} %get-tuple-element.238), channel_id=1, source_target_pairs={{0,4},{1,5},{2,6},{3,7},{4,0},{5,1},{6,2},{7,3},{8,12},{9,13},{10,... | collective-permute-start | bytes 294920 | tf_op jit(solution)/shard_map/ppermute | solution.py:162
  67.9 2.1 %collective-permute-start.28 = (bf16[96,512]{1,0:T(8,128)(2,1)S(1)}, bf16[96,512]{1,0:T(8,128)(2,1)S(1)}, u32[]{:S(2)}, u32[]{:S(2)}) collective-permute-start(bf16[96,512]{1,0:T(8,128)(2,1)S(1)} %get-tuple-element.250), channel_id=1, source_target_pairs={{0,8},{1,9},{2,10},{3,11},{4,12},{5,13},{6,14},{7,15},{8,0},{9,1},... | collective-permute-start | bytes 294920 | tf_op jit(solution)/shard_map/ppermute | solution.py:162
  70.0 2.3 %collective-permute-done.25.refs_2_ = bf16[96,512]{1,0:T(8,128)(2,1)S(1)} collective-permute-done((bf16[96,512]{1,0:T(8,128)(2,1)S(1)}, bf16[96,512]{1,0:T(8,128)(2,1)S(1)}, u32[]{:S(2)}, u32[]{:S(2)}) %collective-permute-start.25) | collective-permute-done | bytes 98336 | tf_op jit(solution)/shard_map/ppermute | solution.py:162
  72.8 2.3 %collective-permute-start.26 = (bf16[48,512]{1,0:T(8,128)(2,1)S(1)}, bf16[48,512]{1,0:T(8,128)(2,1)S(1)}, u32[]{:S(2)}, u32[]{:S(2)}) collective-permute-start(bf16[48,512]{1,0:T(8,128)(2,1)S(1)} %get-tuple-element.239), channel_id=1, source_target_pairs={{0,8},{1,9},{2,10},{3,11},{4,12},{5,13},{6,14},{7,15},{8,0},{9,1},... | collective-permute-start | bytes 147464 | tf_op jit(solution)/shard_map/ppermute | solution.py:162
  76.1 2.4 %collective-permute-start.35 = (bf16[64,512]{1,0:T(8,128)(2,1)S(1)}, bf16[64,512]{1,0:T(8,128)(2,1)S(1)}, u32[]{:S(2)}, u32[]{:S(2)}) collective-permute-start(bf16[64,512]{1,0:T(8,128)(2,1)S(1)} %get-tuple-element.264), channel_id=1, source_target_pairs={{0,8},{1,9},{2,10},{3,11},{4,12},{5,13},{6,14},{7,15},{8,0},{9,1},... | collective-permute-start | bytes 196616 | tf_op jit(solution)/shard_map/ppermute | solution.py:162
  78.5 1.6 %collective-permute-done.26.refs_0_.arr_e_ref = bf16[48,512]{1,0:T(8,128)(2,1)S(1)} collective-permute-done((bf16[48,512]{1,0:T(8,128)(2,1)S(1)}, bf16[48,512]{1,0:T(8,128)(2,1)S(1)}, u32[]{:S(2)}, u32[]{:S(2)}) %collective-permute-start.26) | collective-permute-done | bytes 49184 | tf_op jit(solution)/shard_map/ppermute | solution.py:162
  80.1 1.4 %grid_place.1 = bf16[512,512]{1,0:T(8,128)(2,1)} custom-call(bf16[48,512]{1,0:T(8,128)(2,1)S(1)} %collective-permute-done.26.refs_0_.arr_e_ref, bf16[16,512]{1,0:T(8,128)(2,1)S(1)} %get-tuple-element.240.refs_1_, bf16[16,512]{1,0:T(8,128)(2,1)S(1)} %get-tuple-element.241.refs_2_, bf16[16,512]{1,0:T(8,128)(2,1)S(1)} %get-tuple-element.242.refs_3_, ...), custom_call_target="tpu_custom_call" | custom-call | flops 402653184 | bytes 1687872 | tf_op jit(solution)/shard_map/grid_place/pallas_call | solution.py:231
  (83 shorter events, 28.5 us)
Async XLA Ops:
  3.9 8.0 %collective-permute-start = (bf16[16,512]{1,0:T(8,128)(2,1)S(1)}, bf16[16,512]{1,0:T(8,128)(2,1)S(1)}, u32[]{:S(2)}, u32[]{:S(2)}) collective-permute-start(bf16[16,512]{1,0:T(8,128)(2,1)S(1)} %get-tuple-element.145), channel_id=1, source_target_pairs={{0,12},{4,8},{8,4},{12,0},{1,13},{5,9},{9,5},{13,1},{2,14},{6,10},... | collective-permute-start | bytes 49160 | tf_op jit(solution)/shard_map/ppermute | solution.py:247
  14.5 5.8 %collective-permute-start.5 = (bf16[32,512]{1,0:T(8,128)(2,1)S(1)}, bf16[32,512]{1,0:T(8,128)(2,1)S(1)}, u32[]{:S(2)}, u32[]{:S(2)}) collective-permute-start(bf16[32,512]{1,0:T(8,128)(2,1)S(1)} %get-tuple-element.157), channel_id=1, source_target_pairs={{0,12},{4,8},{8,4},{12,0},{1,13},{5,9},{9,5},{13,1},{2,14},{6,10},... | collective-permute-start | bytes 98312 | tf_op jit(solution)/shard_map/ppermute | solution.py:247
  15.6 4.7 %collective-permute-start.6 = (bf16[32,512]{1,0:T(8,128)(2,1)S(1)}, bf16[32,512]{1,0:T(8,128)(2,1)S(1)}, u32[]{:S(2)}, u32[]{:S(2)}) collective-permute-start(bf16[32,512]{1,0:T(8,128)(2,1)S(1)} %get-tuple-element.158), channel_id=1, source_target_pairs={{0,4},{4,0},{8,12},{12,8},{1,5},{5,1},{9,13},{13,9},{2,6},{6,2},{1... | collective-permute-start | bytes 98312 | tf_op jit(solution)/shard_map/ppermute | solution.py:248
  21.4 8.1 %collective-permute-start.10 = (bf16[16,512]{1,0:T(8,128)(2,1)S(1)}, bf16[16,512]{1,0:T(8,128)(2,1)S(1)}, u32[]{:S(2)}, u32[]{:S(2)}) collective-permute-start(bf16[16,512]{1,0:T(8,128)(2,1)S(1)} %get-tuple-element.167), channel_id=1, source_target_pairs={{0,12},{4,8},{8,4},{12,0},{1,13},{5,9},{9,5},{13,1},{2,14},{6,10},... | collective-permute-start | bytes 49160 | tf_op jit(solution)/shard_map/ppermute | solution.py:247
  24.1 5.4 %collective-permute-start.11 = (bf16[16,512]{1,0:T(8,128)(2,1)S(1)}, bf16[16,512]{1,0:T(8,128)(2,1)S(1)}, u32[]{:S(2)}, u32[]{:S(2)}) collective-permute-start(bf16[16,512]{1,0:T(8,128)(2,1)S(1)} %get-tuple-element.168), channel_id=1, source_target_pairs={{0,4},{4,0},{8,12},{12,8},{1,5},{5,1},{9,13},{13,9},{2,6},{6,2},{1... | collective-permute-start | bytes 49160 | tf_op jit(solution)/shard_map/ppermute | solution.py:248
  24.7 4.9 %collective-permute-start.12 = (bf16[16,512]{1,0:T(8,128)(2,1)S(1)}, bf16[16,512]{1,0:T(8,128)(2,1)S(1)}, u32[]{:S(2)}, u32[]{:S(2)}) collective-permute-start(bf16[16,512]{1,0:T(8,128)(2,1)S(1)} %get-tuple-element.169), channel_id=1, source_target_pairs={{0,3},{1,2},{2,1},{3,0},{4,7},{5,6},{6,5},{7,4},{8,11},{9,10},{10,... | collective-permute-start | bytes 49160 | tf_op jit(solution)/shard_map/ppermute | solution.py:250
  25.1 4.4 %collective-permute-start.13 = (bf16[16,512]{1,0:T(8,128)(2,1)S(1)}, bf16[16,512]{1,0:T(8,128)(2,1)S(1)}, u32[]{:S(2)}, u32[]{:S(2)}) collective-permute-start(bf16[16,512]{1,0:T(8,128)(2,1)S(1)} %get-tuple-element.170), channel_id=1, source_target_pairs={{0,2},{1,3},{2,0},{3,1},{4,6},{5,7},{6,4},{7,5},{8,10},{9,11},{10,... | collective-permute-start | bytes 49160 | tf_op jit(solution)/shard_map/ppermute | solution.py:250
  33.0 6.3 %collective-permute-start.17 = (bf16[8,512]{1,0:T(8,128)(2,1)S(1)}, bf16[8,512]{1,0:T(8,128)(2,1)S(1)}, u32[]{:S(2)}, u32[]{:S(2)}) collective-permute-start(bf16[8,512]{1,0:T(8,128)(2,1)S(1)} %get-tuple-element.205), channel_id=1, source_target_pairs={{0,12},{4,8},{8,4},{12,0},{1,13},{5,9},{9,5},{13,1},{2,14},{6,10},... | collective-permute-start | bytes 24584 | tf_op jit(solution)/shard_map/ppermute | solution.py:247
  34.0 5.4 %collective-permute-start.18 = (bf16[8,512]{1,0:T(8,128)(2,1)S(1)}, bf16[8,512]{1,0:T(8,128)(2,1)S(1)}, u32[]{:S(2)}, u32[]{:S(2)}) collective-permute-start(bf16[8,512]{1,0:T(8,128)(2,1)S(1)} %get-tuple-element.206), channel_id=1, source_target_pairs={{0,4},{4,0},{8,12},{12,8},{1,5},{5,1},{9,13},{13,9},{2,6},{6,2},{1... | collective-permute-start | bytes 24584 | tf_op jit(solution)/shard_map/ppermute | solution.py:248
  34.8 4.5 %collective-permute-start.19 = (bf16[8,512]{1,0:T(8,128)(2,1)S(1)}, bf16[8,512]{1,0:T(8,128)(2,1)S(1)}, u32[]{:S(2)}, u32[]{:S(2)}) collective-permute-start(bf16[8,512]{1,0:T(8,128)(2,1)S(1)} %get-tuple-element.207), channel_id=1, source_target_pairs={{0,3},{1,2},{2,1},{3,0},{4,7},{5,6},{6,5},{7,4},{8,11},{9,10},{10,... | collective-permute-start | bytes 24584 | tf_op jit(solution)/shard_map/ppermute | solution.py:250
  40.1 12.6 %collective-permute-start.32 = (bf16[512,512]{1,0:T(8,128)(2,1)S(1)}, bf16[512,512]{1,0:T(8,128)(2,1)S(1)}, u32[]{:S(2)}, u32[]{:S(2)}) collective-permute-start(bf16[512,512]{1,0:T(8,128)(2,1)S(1)} %get-tuple-element.258), channel_id=1, source_target_pairs={{0,1},{1,0},{2,3},{3,2},{4,5},{5,4},{6,7},{7,6},{8,9},{9,8},{10,11... | collective-permute-start | bytes 1572872 | tf_op jit(solution)/shard_map/ppermute | solution.py:162
  40.1 11.9 %collective-permute-start.23 = (bf16[384,512]{1,0:T(8,128)(2,1)S(1)}, bf16[384,512]{1,0:T(8,128)(2,1)S(1)}, u32[]{:S(2)}, u32[]{:S(2)}) collective-permute-start(bf16[384,512]{1,0:T(8,128)(2,1)S(1)} %get-tuple-element.229), channel_id=1, source_target_pairs={{0,2},{1,3},{2,0},{3,1},{4,6},{5,7},{6,4},{7,5},{8,10},{9,11},{10,... | collective-permute-start | bytes 1179656 | tf_op jit(solution)/shard_map/ppermute | solution.py:162
  44.2 7.9 %collective-permute-start.22 = (bf16[288,512]{1,0:T(8,128)(2,1)S(1)}, bf16[288,512]{1,0:T(8,128)(2,1)S(1)}, u32[]{:S(2)}, u32[]{:S(2)}) collective-permute-start(bf16[288,512]{1,0:T(8,128)(2,1)S(1)} %get-tuple-element.228), channel_id=1, source_target_pairs={{0,1},{1,0},{2,3},{3,2},{4,5},{5,4},{6,7},{7,6},{8,9},{9,8},{10,11... | collective-permute-start | bytes 884744 | tf_op jit(solution)/shard_map/ppermute | solution.py:162
  44.6 13.1 %collective-permute-start.29 = (bf16[256,512]{1,0:T(8,128)(2,1)S(1)}, bf16[256,512]{1,0:T(8,128)(2,1)S(1)}, u32[]{:S(2)}, u32[]{:S(2)}) collective-permute-start(bf16[256,512]{1,0:T(8,128)(2,1)S(1)} %get-tuple-element.252), channel_id=1, source_target_pairs={{0,2},{1,3},{2,0},{3,1},{4,6},{5,7},{6,4},{7,5},{8,10},{9,11},{10,... | collective-permute-start | bytes 786440 | tf_op jit(solution)/shard_map/ppermute | solution.py:162
  53.0 10.3 %collective-permute-start.33 = (bf16[256,512]{1,0:T(8,128)(2,1)S(1)}, bf16[256,512]{1,0:T(8,128)(2,1)S(1)}, u32[]{:S(2)}, u32[]{:S(2)}) collective-permute-start(bf16[256,512]{1,0:T(8,128)(2,1)S(1)} %get-tuple-element.260), channel_id=1, source_target_pairs={{0,2},{1,3},{2,0},{3,1},{4,6},{5,7},{6,4},{7,5},{8,10},{9,11},{10,... | collective-permute-start | bytes 786440 | tf_op jit(solution)/shard_map/ppermute | solution.py:162
  54.2 12.1 %collective-permute-start.24 = (bf16[160,512]{1,0:T(8,128)(2,1)S(1)}, bf16[160,512]{1,0:T(8,128)(2,1)S(1)}, u32[]{:S(2)}, u32[]{:S(2)}) collective-permute-start(bf16[160,512]{1,0:T(8,128)(2,1)S(1)} %get-tuple-element.234), channel_id=1, source_target_pairs={{0,2},{1,3},{2,0},{3,1},{4,6},{5,7},{6,4},{7,5},{8,10},{9,11},{10,... | collective-permute-start | bytes 491528 | tf_op jit(solution)/shard_map/ppermute | solution.py:162
  55.2 12.5 %collective-permute-start.27 = (bf16[192,512]{1,0:T(8,128)(2,1)S(1)}, bf16[192,512]{1,0:T(8,128)(2,1)S(1)}, u32[]{:S(2)}, u32[]{:S(2)}) collective-permute-start(bf16[192,512]{1,0:T(8,128)(2,1)S(1)} %get-tuple-element.248), channel_id=1, source_target_pairs={{0,4},{1,5},{2,6},{3,7},{4,0},{5,1},{6,2},{7,3},{8,12},{9,13},{10,... | collective-permute-start | bytes 589832 | tf_op jit(solution)/shard_map/ppermute | solution.py:162
  57.8 17.3 %collective-permute-start.30 = (bf16[128,512]{1,0:T(8,128)(2,1)S(1)}, bf16[128,512]{1,0:T(8,128)(2,1)S(1)}, u32[]{:S(2)}, u32[]{:S(2)}) collective-permute-start(bf16[128,512]{1,0:T(8,128)(2,1)S(1)} %get-tuple-element.254), channel_id=1, source_target_pairs={{0,4},{1,5},{2,6},{3,7},{4,0},{5,1},{6,2},{7,3},{8,12},{9,13},{10,... | collective-permute-start | bytes 393224 | tf_op jit(solution)/shard_map/ppermute | solution.py:162
  63.5 12.5 %collective-permute-start.34 = (bf16[128,512]{1,0:T(8,128)(2,1)S(1)}, bf16[128,512]{1,0:T(8,128)(2,1)S(1)}, u32[]{:S(2)}, u32[]{:S(2)}) collective-permute-start(bf16[128,512]{1,0:T(8,128)(2,1)S(1)} %get-tuple-element.262), channel_id=1, source_target_pairs={{0,4},{1,5},{2,6},{3,7},{4,0},{5,1},{6,2},{7,3},{8,12},{9,13},{10,... | collective-permute-start | bytes 393224 | tf_op jit(solution)/shard_map/ppermute | solution.py:162
  66.5 5.7 %collective-permute-start.25 = (bf16[96,512]{1,0:T(8,128)(2,1)S(1)}, bf16[96,512]{1,0:T(8,128)(2,1)S(1)}, u32[]{:S(2)}, u32[]{:S(2)}) collective-permute-start(bf16[96,512]{1,0:T(8,128)(2,1)S(1)} %get-tuple-element.238), channel_id=1, source_target_pairs={{0,4},{1,5},{2,6},{3,7},{4,0},{5,1},{6,2},{7,3},{8,12},{9,13},{10,... | collective-permute-start | bytes 294920 | tf_op jit(solution)/shard_map/ppermute | solution.py:162
  67.9 14.3 %collective-permute-start.28 = (bf16[96,512]{1,0:T(8,128)(2,1)S(1)}, bf16[96,512]{1,0:T(8,128)(2,1)S(1)}, u32[]{:S(2)}, u32[]{:S(2)}) collective-permute-start(bf16[96,512]{1,0:T(8,128)(2,1)S(1)} %get-tuple-element.250), channel_id=1, source_target_pairs={{0,8},{1,9},{2,10},{3,11},{4,12},{5,13},{6,14},{7,15},{8,0},{9,1},... | collective-permute-start | bytes 294920 | tf_op jit(solution)/shard_map/ppermute | solution.py:162
  72.8 7.2 %collective-permute-start.26 = (bf16[48,512]{1,0:T(8,128)(2,1)S(1)}, bf16[48,512]{1,0:T(8,128)(2,1)S(1)}, u32[]{:S(2)}, u32[]{:S(2)}) collective-permute-start(bf16[48,512]{1,0:T(8,128)(2,1)S(1)} %get-tuple-element.239), channel_id=1, source_target_pairs={{0,8},{1,9},{2,10},{3,11},{4,12},{5,13},{6,14},{7,15},{8,0},{9,1},... | collective-permute-start | bytes 147464 | tf_op jit(solution)/shard_map/ppermute | solution.py:162
  75.3 6.9 %collective-permute-start.31 = (bf16[64,512]{1,0:T(8,128)(2,1)S(1)}, bf16[64,512]{1,0:T(8,128)(2,1)S(1)}, u32[]{:S(2)}, u32[]{:S(2)}) collective-permute-start(bf16[64,512]{1,0:T(8,128)(2,1)S(1)} %get-tuple-element.256), channel_id=1, source_target_pairs={{0,8},{1,9},{2,10},{3,11},{4,12},{5,13},{6,14},{7,15},{8,0},{9,1},... | collective-permute-start | bytes 196616 | tf_op jit(solution)/shard_map/ppermute | solution.py:162
  76.1 6.9 %collective-permute-start.35 = (bf16[64,512]{1,0:T(8,128)(2,1)S(1)}, bf16[64,512]{1,0:T(8,128)(2,1)S(1)}, u32[]{:S(2)}, u32[]{:S(2)}) collective-permute-start(bf16[64,512]{1,0:T(8,128)(2,1)S(1)} %get-tuple-element.264), channel_id=1, source_target_pairs={{0,8},{1,9},{2,10},{3,11},{4,12},{5,13},{6,14},{7,15},{8,0},{9,1},... | collective-permute-start | bytes 196616 | tf_op jit(solution)/shard_map/ppermute | solution.py:162
  (15 other events, 60.9 us)

commit v8 on v7

--- a/solution.py
+++ b/solution.py
@@ -683,7 +683,7 @@
         flops=10 * unit, scratch=[pltpu.VMEM((degree * nodes, width), BF)],
     )
     if split:
-        give0, give2, *arr4 = lax.optimization_barrier((give0, give2, *arr4))
+        give0, *arr4 = lax.optimization_barrier((give0, *arr4))
         keep0, give0 = halve_step(1, keep0, swap(give0, 0, dims), place)
         keep0, *arr4 = lax.optimization_barrier((keep0, *arr4))
     shapes = blocks_shapes(1, width, width, dims)
@@ -696,47 +696,71 @@
          targets, sends, incoming, slope_g, slope_a, grid, lat_a, embed),
         flops=6 * unit,
     )
-    if carry:
-        arrived = swap(give_e, 0, dims)
-        arrived1 = swap(give1, 1, dims)
-        arrived, arrived1 = lax.optimization_barrier((arrived, arrived1))
-        keep1, give1 = halve_step(2, keep1, arrived1, place)
-        keep_e, give_e, from_sub, _ = carry_step(1, keep_e, arrived, (pay5[1],), place, capacity)
+    depth = width // total
+    if not split:
+        arr5 = exchange(pay5, dims)
+        last, first, second, embed_sum = (
+            scatter_plain(blocks, dims) for blocks in (keep1, keep0, keep2, keep_e)
+        )
+        grads = [jnp.stack([a, last[i]]) for i, a in enumerate((first[0], first[1], second[0]))]
+        grads = [embed_sum[0], second[1], *grads]
+    elif not carry:
+        arr5 = exchange(pay5, dims)
+        sums = [
+            rest_of_halving(1, keep1, give1, place, dims),
+            rest_of_halving(1, keep0, give0, place, dims),
+            rest_of_halving(0, keep2, give2, place, dims),
+            rest_of_halving(0, keep_e, give_e, place, dims),
+        ]
     else:
-        arr5 = exchange(pay5, dims)
-    if split:
-        keep2, keep_e = lax.optimization_barrier((keep2, keep_e))
-        keep2, give2 = halve_step(1, keep2, swap(give2, 0, dims), place)
-    if carry:
-        arrived = swap(give_e, 1, dims)
+        arr1 = swap(give1, 1, dims)
+        arr0 = swap(give0, 1, dims)
+        arr_e, arr1 = lax.optimization_barrier((swap(give_e, 0, dims), arr1))
+        keep_e, give_e, from_sub, _ = carry_step(1, keep_e, arr_e, pay5[1:2], place, capacity)
+        arr_e = swap(give_e, 1, dims)
+        give2, keep1, keep_e = lax.optimization_barrier((give2, keep1, keep_e))
+        arr2 = swap(give2, 0, dims)
+        keep1, give1 = halve_step(2, keep1, arr1, place)
+        arr1 = swap(give1, 2, dims)
+        keep0, keep1 = lax.optimization_barrier((keep0, keep1))
+        keep0, give0 = halve_step(2, keep0, arr0, place)
+        arr0 = swap(give0, 2, dims)
+        keep2, keep0 = lax.optimization_barrier((keep2, keep0))
+        keep2, give2 = halve_step(1, keep2, arr2, place)
+        arr2 = swap(give2, 1, dims)
+        keep1, keep2 = lax.optimization_barrier((keep1, keep2))
+        keep1, give1 = halve_step(3, keep1, arr1, place)
+        arr1 = swap(give1, 3, dims)
+        keep_e, keep1 = lax.optimization_barrier((keep_e, keep1))
         keep_e, give_e, from_lat, from_diag = carry_step(
-            2, keep_e, arrived, pay5[3:], place, capacity
+            2, keep_e, arr_e, pay5[3:], place, capacity
         )
-        arrived = swap(give_e, 2, dims)
-        keep_e, give_e, from_near, _ = carry_step(3, keep_e, arrived, (), place, capacity)
+        arr_e = swap(give_e, 2, dims)
+        keep0, keep_e = lax.optimization_barrier((keep0, keep_e))
+        keep0, give0 = halve_step(3, keep0, arr0, place)
+        arr0 = swap(give0, 3, dims)
+        keep_e, keep0 = lax.optimization_barrier((keep_e, keep0))
+        keep_e, give_e, from_near, _ = carry_step(3, keep_e, arr_e, (), place, capacity)
         arr_e = swap(give_e, 3, dims)
+        keep2, keep_e, arr1 = lax.optimization_barrier((keep2, keep_e, arr1))
+        keep2, give2 = halve_step(2, keep2, arr2, place)
+        arr2 = swap(give2, 2, dims)
         arr5 = (arr_e, from_near, from_diag, from_lat, from_sub)
+        gpre_g, keep2 = lax.optimization_barrier((gpre_g, keep2))
     (grid_grad,) = call(
         lambda *refs: grid_place(peers, *refs), "grid_place", [shape(chosen, width)],
         (*arr5, gpre_g, embed, sends_row), flops=3 * unit,
     )
-    depth = width // total
-    if not split:
-        last, first, second, embed = (
-            scatter_plain(blocks, dims) for blocks in (keep1, keep0, keep2, keep_e)
+    if carry:
+        keep2, grid_grad, arr0 = lax.optimization_barrier((keep2, grid_grad, arr0))
+        keep2, give2 = halve_step(3, keep2, arr2, place)
+        sums = ((keep1, arr1), (keep0, arr0), (keep2, swap(give2, 3, dims)), (keep_e, arr_e))
+    if split:
+        grads = call(
+            finish, "finish",
+            [shape(depth, width, dtype=F32)] * 2 + [shape(2, depth, width, dtype=F32)] * 3,
+            [part for pair in sums for part in pair], flops=8 * depth * width,
         )
-        grads = [jnp.stack([a, last[i]]) for i, a in enumerate((first[0], first[1], second[0]))]
-        return (mesh_out, grid_grad, embed[0], second[1], *grads)
-    if not carry:
-        keep_e, arr_e = rest_of_halving(0, keep_e, give_e, place, dims)
-    grads = call(
-        finish, "finish",
-        [shape(depth, width, dtype=F32)] * 2 + [shape(2, depth, width, dtype=F32)] * 3,
-        (*rest_of_halving(2, keep1, give1, place, dims),
-         *rest_of_halving(1, keep0, give0, place, dims),
-         *rest_of_halving(1, keep2, give2, place, dims), keep_e, arr_e),
-        flops=8 * depth * width,
-    )
     return (mesh_out, grid_grad, *grads)
 
 

time: 84 us -> 88.5 us (1.054)
  waiting for transfers between devices: 20.8 us -> 25.3 us
    ppermute x16, waiting for transfers between devices: 18.7 us -> 23.1 us  [swap(): return lax.ppermute(block, GROUP, [(i, i ^ 1 << bit) for i in range(total)])]
  transfers between devices with their start and end apart: 36 -> 36, of which waited for: 13 -> 13; matrix products, arithmetic and copies ran while one was open for 0% -> 0% of each run, Pallas kernels for 21% -> 18%
where the time goes in v8:
time: 88.5 us; the launch traced here: 88.3 us
  starting transfers between devices  37.7 us (43%)
  waiting for transfers between devices  25.3 us (29%)
  Pallas kernels  22.8 us (26%)
  local copies, waits for them, and re-layouts  1.56 us (2%)
  between operations  0.92 us (1%)
    ppermute x16, waiting for transfers between devices, swap(): return lax.ppermute(block, GROUP, [(i, i ^ 1 << bit) for i in range(total)])  23.1 us
    pallas_call x24, Pallas kernels, call(): pl.pallas_call(kernel, out_shape=[shape(*a.shape, dtype=a.dtype) for a in...  22.8 us
    ppermute x16, starting transfers between devices, swap(): return lax.ppermute(block, GROUP, [(i, i ^ 1 << bit) for i in range(total)])  18.9 us
    ppermute x4, starting transfers between devices, exchange(): far = lax.ppermute(parts[column], 'lon', other)  9.87 us
    ppermute x12, starting transfers between devices, exchange(): lax.ppermute(parts[r - 1], COLUMN, [(i, i ^ r) for i in range(column)])  6.88 us
    ppermute x4, starting transfers between devices, exchange(): lax.ppermute(parts[column - 1], 'lon', [(i, i ^ 1) for i in range(count)])  2.01 us
  transfers between devices with their start and end apart: 36, of which 13 were waited for; matrix products, arithmetic and copies ran while one was open for 0% of the time, Pallas kernels for 18%

profile of v8, /device:TPU:0, one launch (start us, length us, event | category | flops | bytes accessed | tf_op | source)
XLA Modules:
  0.0 88.3 jit_solution(10933309952319737515)
XLA Ops:
  2.3 1.6 %first_payload.1 = (bf16[512,512]{1,0:T(8,128)(2,1)S(1)}, bf16[512,512]{1,0:T(8,128)(2,1)S(1)}, s32[1,512]{1,0:T(1,128)S(1)}, s32[6,256]{1,0:T(8,128)S(1)}, bf16...) custom-call(bf16[512,512]{1,0:T(8,128)(2,1)} %refs_0_.1, ...), custom_call_target="tpu_custom_call" | custom-call | flops 67108864 | bytes 2188688 | tf_op jit(solution)/shard_map/first_payload/pallas_call | solution.py:231
  3.9 5.1 %collective-permute-start = (bf16[16,512]{1,0:T(8,128)(2,1)S(1)}, bf16[16,512]{1,0:T(8,128)(2,1)S(1)}, u32[]{:S(2)}, u32[]{:S(2)}) collective-permute-start(bf16[16,512]{1,0:T(8,128)(2,1)S(1)} %get-tuple-element.165), channel_id=1, source_target_pairs={{0,12},{4,8},{8,4},{12,0},{1,13},{5,9},{9,5},{13,1},{2,14},{6,10},... | collective-permute-start | bytes 49160 | tf_op jit(solution)/shard_map/ppermute | solution.py:247
  16.3 1.5 %collective-permute-start.8 = (bf16[32,512]{1,0:T(8,128)(2,1)S(1)}, bf16[32,512]{1,0:T(8,128)(2,1)S(1)}, u32[]{:S(2)}, u32[]{:S(2)}) collective-permute-start(bf16[32,512]{1,0:T(8,128)(2,1)S(1)} %get-tuple-element.180), channel_id=1, source_target_pairs={{0,2},{1,3},{2,0},{3,1},{4,6},{5,7},{6,4},{7,5},{8,10},{9,11},{10,... | collective-permute-start | bytes 98312 | tf_op jit(solution)/shard_map/ppermute | solution.py:250
  18.1 1.9 %forward_local.1 = (f32[256,512]{1,0:T(8,128)S(1)}, bf16[6,256,512]{2,1,0:T(8,128)(2,1)S(1)}, f32[40,512]{1,0:T(8,128)S(1)}, bf16[40,512]{1,0:T(8,128)(2,1)S(1)}) custom-call(bf16[256,512]{1,0:T(8,128)(2,1)S(1)} %get-tuple-element.182.state_ref.refs_7_.refs_10_, bf16[2,512,512]{2,1,0:T(8,128)(2,1)S(1)} %copy-done, bf16[2,512,512]{2,1,0:T(8,128)(2,1)S(1)} %copy-done.2, ...), custom_call_target="tpu_custom_call" | custom-call | flops 805306368 | bytes 4593824 | tf_op jit(solution)/shard_map/forward_local/pallas_call | solution.py:231
  21.4 2.7 %collective-permute-start.10 = (bf16[16,512]{1,0:T(8,128)(2,1)S(1)}, bf16[16,512]{1,0:T(8,128)(2,1)S(1)}, u32[]{:S(2)}, u32[]{:S(2)}) collective-permute-start(bf16[16,512]{1,0:T(8,128)(2,1)S(1)} %get-tuple-element.187), channel_id=1, source_target_pairs={{0,12},{4,8},{8,4},{12,0},{1,13},{5,9},{9,5},{13,1},{2,14},{6,10},... | collective-permute-start | bytes 49160 | tf_op jit(solution)/shard_map/ppermute | solution.py:247
  26.5 3.0 %turn_local.1 = (f32[256,512]{1,0:T(8,128)S(1)}, f32[256,512]{1,0:T(8,128)S(1)}, f32[256,512]{1,0:T(8,128)S(1)}, f32[40,512]{1,0:T(8,128)S(1)}, bf16[40,512]{1,0...) custom-call(bf16[256,512]{1,0:T(8,128)(2,1)S(1)} %get-tuple-element., ...), custom_call_target="tpu_custom_call" | custom-call | flops 1342177280 | bytes 5871776 | tf_op jit(solution)/shard_map/turn_local/pallas_call | solution.py:231
  29.6 1.3 %turn_halo.1 = (bf16[256,512]{1,0:T(8,128)(2,1)S(1)}, bf16[256,512]{1,0:T(8,128)(2,1)S(1)}, bf16[256,512]{1,0:T(8,128)(2,1)S(1)}, bf16[256,512]{1,0:T(8,128)(2,1...) custom-call(bf16[16,512]{1,0:T(8,128)(2,1)S(1)} %collective-permute-, ...), custom_call_target="tpu_custom_call" | custom-call | flops 402653184 | bytes 5322912 | tf_op jit(solution)/shard_map/turn_halo/pallas_call | solution.py:231
  31.0 1.5 %last_weights.1 = (bf16[768,512]{1,0:T(8,128)(2,1)S(1)}, bf16[768,512]{1,0:T(8,128)(2,1)S(1)}, bf16[256,512]{1,0:T(8,128)(2,1)}) custom-call(s32[6,6]{1,0:T(8,128)S(1)} %get-tuple-element.164.refs_0_.refs_5_, bf16[256,512]{1,0:T(8,128)(2,1)S(1)} %get-tuple-element.186.state_ref.refs_1_, bf16[256,512]{1,0:T(8,128)(2,1)S(1)} %get-tuple-element.204.refs_2_, ...), custom_call_target="tpu_custom_call" | custom-call | flops 536870912 | bytes 4194448 | tf_op jit(solution)/shard_map/last_weights/pallas_call | solution.py:231
  36.4 2.9 %back_local.1 = (f32[256,512]{1,0:T(8,128)S(1)}, bf16[512,512]{1,0:T(8,128)(2,1)S(1)}, bf16[512,512]{1,0:T(8,128)(2,1)S(1)}, bf16[512,512]{1,0:T(8,128)(2,1)S(1)}, bf16[512,512]{1,0:T(8,128)(2,1)S(1)}) custom-call(s32[6,6]{1,0:T(8,128)S(1)} %get-tuple-element.164.refs_0_.refs_5_, bf16[256,512]{1,0:T(8,128)(2,1)S(1)} %get-tuple-element.208.refs_1_, ...), custom_call_target="tpu_custom_call" | custom-call | flops 1342177280 | bytes 8960144 | tf_op jit(solution)/shard_map/back_local/pallas_call | solution.py:231
  41.9 2.3 %embed_back.1 = (bf16[512,512]{1,0:T(8,128)(2,1)S(1)}, bf16[256,512]{1,0:T(8,128)(2,1)S(1)}, bf16[288,512]{1,0:T(8,128)(2,1)S(1)}, bf16[16,512]{1,0:T(8,128)(2,1...) custom-call(bf16[8,512]{1,0:T(8,128)(2,1)S(1)} %collective-permute-d, ...), custom_call_target="tpu_custom_call" | custom-call | flops 805306368 | bytes 6130608 | tf_op jit(solution)/shard_map/embed_back/pallas_call | solution.py:231
  44.6 6.6 %collective-permute-done.23.refs_2_ = bf16[384,512]{1,0:T(8,128)(2,1)S(1)} collective-permute-done((bf16[384,512]{1,0:T(8,128)(2,1)S(1)}, bf16[384,512]{1,0:T(8,128)(2,1)S(1)}, u32[]{:S(2)}, u32[]{:S(2)}) %collective-permute-start.23) | collective-permute-done | bytes 393248 | tf_op jit(solution)/shard_map/ppermute | solution.py:162
  53.2 1.5 %collective-permute-start.26 = (bf16[192,512]{1,0:T(8,128)(2,1)S(1)}, bf16[192,512]{1,0:T(8,128)(2,1)S(1)}, u32[]{:S(2)}, u32[]{:S(2)}) collective-permute-start(bf16[192,512]{1,0:T(8,128)(2,1)S(1)} %get-tuple-element.269), channel_id=1, source_target_pairs={{0,4},{1,5},{2,6},{3,7},{4,0},{5,1},{6,2},{7,3},{8,12},{9,13},{10,... | collective-permute-start | bytes 589832 | tf_op jit(solution)/shard_map/ppermute | solution.py:162
  55.3 5.6 %collective-permute-done.24.refs_2_ = bf16[256,512]{1,0:T(8,128)(2,1)S(1)} collective-permute-done((bf16[256,512]{1,0:T(8,128)(2,1)S(1)}, bf16[256,512]{1,0:T(8,128)(2,1)S(1)}, u32[]{:S(2)}, u32[]{:S(2)}) %collective-permute-start.24) | collective-permute-done | bytes 262176 | tf_op jit(solution)/shard_map/ppermute | solution.py:162
  62.6 1.4 %collective-permute-start.28 = (bf16[128,512]{1,0:T(8,128)(2,1)S(1)}, bf16[128,512]{1,0:T(8,128)(2,1)S(1)}, u32[]{:S(2)}, u32[]{:S(2)}) collective-permute-start(bf16[128,512]{1,0:T(8,128)(2,1)S(1)} %get-tuple-element.278), channel_id=1, source_target_pairs={{0,4},{1,5},{2,6},{3,7},{4,0},{5,1},{6,2},{7,3},{8,12},{9,13},{10,... | collective-permute-start | bytes 393224 | tf_op jit(solution)/shard_map/ppermute | solution.py:162
  64.5 1.3 %collective-permute-start.29 = (bf16[96,512]{1,0:T(8,128)(2,1)S(1)}, bf16[96,512]{1,0:T(8,128)(2,1)S(1)}, u32[]{:S(2)}, u32[]{:S(2)}) collective-permute-start(bf16[96,512]{1,0:T(8,128)(2,1)S(1)} %get-tuple-element.281), channel_id=1, source_target_pairs={{0,4},{1,5},{2,6},{3,7},{4,0},{5,1},{6,2},{7,3},{8,12},{9,13},{10,... | collective-permute-start | bytes 294920 | tf_op jit(solution)/shard_map/ppermute | solution.py:162
  65.8 2.0 %collective-permute-start.30 = (bf16[96,512]{1,0:T(8,128)(2,1)S(1)}, bf16[96,512]{1,0:T(8,128)(2,1)S(1)}, u32[]{:S(2)}, u32[]{:S(2)}) collective-permute-start(bf16[96,512]{1,0:T(8,128)(2,1)S(1)} %get-tuple-element.283), channel_id=1, source_target_pairs={{0,8},{1,9},{2,10},{3,11},{4,12},{5,13},{6,14},{7,15},{8,0},{9,1},... | collective-permute-start | bytes 294920 | tf_op jit(solution)/shard_map/ppermute | solution.py:162
  67.8 1.9 %collective-permute-done.28.refs_2_ = bf16[128,512]{1,0:T(8,128)(2,1)S(1)} collective-permute-done((bf16[128,512]{1,0:T(8,128)(2,1)S(1)}, bf16[128,512]{1,0:T(8,128)(2,1)S(1)}, u32[]{:S(2)}, u32[]{:S(2)}) %collective-permute-start.28) | collective-permute-done | bytes 131104 | tf_op jit(solution)/shard_map/ppermute | solution.py:162
  69.8 1.7 %collective-permute-done.29.refs_2_ = bf16[96,512]{1,0:T(8,128)(2,1)S(1)} collective-permute-done((bf16[96,512]{1,0:T(8,128)(2,1)S(1)}, bf16[96,512]{1,0:T(8,128)(2,1)S(1)}, u32[]{:S(2)}, u32[]{:S(2)}) %collective-permute-start.29) | collective-permute-done | bytes 98336 | tf_op jit(solution)/shard_map/ppermute | solution.py:162
  72.3 2.4 %collective-permute-start.34 = (bf16[128,512]{1,0:T(8,128)(2,1)S(1)}, bf16[128,512]{1,0:T(8,128)(2,1)S(1)}, u32[]{:S(2)}, u32[]{:S(2)}) collective-permute-start(bf16[128,512]{1,0:T(8,128)(2,1)S(1)} %get-tuple-element.302), channel_id=1, source_target_pairs={{0,4},{1,5},{2,6},{3,7},{4,0},{5,1},{6,2},{7,3},{8,12},{9,13},{10,... | collective-permute-start | bytes 393224 | tf_op jit(solution)/shard_map/ppermute | solution.py:162
  74.7 1.6 %collective-permute-start.32 = (bf16[48,512]{1,0:T(8,128)(2,1)S(1)}, bf16[48,512]{1,0:T(8,128)(2,1)S(1)}, u32[]{:S(2)}, u32[]{:S(2)}) collective-permute-start(bf16[48,512]{1,0:T(8,128)(2,1)S(1)} %get-tuple-element.288), channel_id=1, source_target_pairs={{0,8},{1,9},{2,10},{3,11},{4,12},{5,13},{6,14},{7,15},{8,0},{9,1},... | collective-permute-start | bytes 147464 | tf_op jit(solution)/shard_map/ppermute | solution.py:162
  77.6 2.6 %collective-permute-done.32.refs_0_.arr_e_ref = bf16[48,512]{1,0:T(8,128)(2,1)S(1)} collective-permute-done((bf16[48,512]{1,0:T(8,128)(2,1)S(1)}, bf16[48,512]{1,0:T(8,128)(2,1)S(1)}, u32[]{:S(2)}, u32[]{:S(2)}) %collective-permute-start.32) | collective-permute-done | bytes 49184 | tf_op jit(solution)/shard_map/ppermute | solution.py:162
  80.2 1.3 %grid_place.1 = bf16[512,512]{1,0:T(8,128)(2,1)} custom-call(bf16[48,512]{1,0:T(8,128)(2,1)S(1)} %collective-permute-done.32.refs_0_.arr_e_ref, bf16[16,512]{1,0:T(8,128)(2,1)S(1)} %get-tuple-element.289.refs_1_, bf16[16,512]{1,0:T(8,128)(2,1)S(1)} %get-tuple-element.290.refs_2_, bf16[16,512]{1,0:T(8,128)(2,1)S(1)} %get-tuple-element.291.refs_3_, ...), custom_call_target="tpu_custom_call" | custom-call | flops 402653184 | bytes 1687872 | tf_op jit(solution)/shard_map/grid_place/pallas_call | solution.py:231
  81.9 1.5 %collective-permute-start.35 = (bf16[64,512]{1,0:T(8,128)(2,1)S(1)}, bf16[64,512]{1,0:T(8,128)(2,1)S(1)}, u32[]{:S(2)}, u32[]{:S(2)}) collective-permute-start(bf16[64,512]{1,0:T(8,128)(2,1)S(1)} %get-tuple-element.304), channel_id=1, source_target_pairs={{0,8},{1,9},{2,10},{3,11},{4,12},{5,13},{6,14},{7,15},{8,0},{9,1},... | collective-permute-start | bytes 196616 | tf_op jit(solution)/shard_map/ppermute | solution.py:162
  83.5 4.0 %collective-permute-done.35.arr2_ref = bf16[64,512]{1,0:T(8,128)(2,1)S(1)} collective-permute-done((bf16[64,512]{1,0:T(8,128)(2,1)S(1)}, bf16[64,512]{1,0:T(8,128)(2,1)S(1)}, u32[]{:S(2)}, u32[]{:S(2)}) %collective-permute-start.35) | collective-permute-done | bytes 65568 | tf_op jit(solution)/shard_map/ppermute | solution.py:162
  (83 shorter events, 28.0 us)
Async XLA Ops:
  3.9 8.0 %collective-permute-start = (bf16[16,512]{1,0:T(8,128)(2,1)S(1)}, bf16[16,512]{1,0:T(8,128)(2,1)S(1)}, u32[]{:S(2)}, u32[]{:S(2)}) collective-permute-start(bf16[16,512]{1,0:T(8,128)(2,1)S(1)} %get-tuple-element.165), channel_id=1, source_target_pairs={{0,12},{4,8},{8,4},{12,0},{1,13},{5,9},{9,5},{13,1},{2,14},{6,10},... | collective-permute-start | bytes 49160 | tf_op jit(solution)/shard_map/ppermute | solution.py:247
  14.5 5.8 %collective-permute-start.5 = (bf16[32,512]{1,0:T(8,128)(2,1)S(1)}, bf16[32,512]{1,0:T(8,128)(2,1)S(1)}, u32[]{:S(2)}, u32[]{:S(2)}) collective-permute-start(bf16[32,512]{1,0:T(8,128)(2,1)S(1)} %get-tuple-element.177), channel_id=1, source_target_pairs={{0,12},{4,8},{8,4},{12,0},{1,13},{5,9},{9,5},{13,1},{2,14},{6,10},... | collective-permute-start | bytes 98312 | tf_op jit(solution)/shard_map/ppermute | solution.py:247
  15.6 4.7 %collective-permute-start.6 = (bf16[32,512]{1,0:T(8,128)(2,1)S(1)}, bf16[32,512]{1,0:T(8,128)(2,1)S(1)}, u32[]{:S(2)}, u32[]{:S(2)}) collective-permute-start(bf16[32,512]{1,0:T(8,128)(2,1)S(1)} %get-tuple-element.178), channel_id=1, source_target_pairs={{0,4},{4,0},{8,12},{12,8},{1,5},{5,1},{9,13},{13,9},{2,6},{6,2},{1... | collective-permute-start | bytes 98312 | tf_op jit(solution)/shard_map/ppermute | solution.py:248
  21.4 8.1 %collective-permute-start.10 = (bf16[16,512]{1,0:T(8,128)(2,1)S(1)}, bf16[16,512]{1,0:T(8,128)(2,1)S(1)}, u32[]{:S(2)}, u32[]{:S(2)}) collective-permute-start(bf16[16,512]{1,0:T(8,128)(2,1)S(1)} %get-tuple-element.187), channel_id=1, source_target_pairs={{0,12},{4,8},{8,4},{12,0},{1,13},{5,9},{9,5},{13,1},{2,14},{6,10},... | collective-permute-start | bytes 49160 | tf_op jit(solution)/shard_map/ppermute | solution.py:247
  24.1 5.4 %collective-permute-start.11 = (bf16[16,512]{1,0:T(8,128)(2,1)S(1)}, bf16[16,512]{1,0:T(8,128)(2,1)S(1)}, u32[]{:S(2)}, u32[]{:S(2)}) collective-permute-start(bf16[16,512]{1,0:T(8,128)(2,1)S(1)} %get-tuple-element.188), channel_id=1, source_target_pairs={{0,4},{4,0},{8,12},{12,8},{1,5},{5,1},{9,13},{13,9},{2,6},{6,2},{1... | collective-permute-start | bytes 49160 | tf_op jit(solution)/shard_map/ppermute | solution.py:248
  24.7 4.9 %collective-permute-start.12 = (bf16[16,512]{1,0:T(8,128)(2,1)S(1)}, bf16[16,512]{1,0:T(8,128)(2,1)S(1)}, u32[]{:S(2)}, u32[]{:S(2)}) collective-permute-start(bf16[16,512]{1,0:T(8,128)(2,1)S(1)} %get-tuple-element.189), channel_id=1, source_target_pairs={{0,3},{1,2},{2,1},{3,0},{4,7},{5,6},{6,5},{7,4},{8,11},{9,10},{10,... | collective-permute-start | bytes 49160 | tf_op jit(solution)/shard_map/ppermute | solution.py:250
  25.1 4.4 %collective-permute-start.13 = (bf16[16,512]{1,0:T(8,128)(2,1)S(1)}, bf16[16,512]{1,0:T(8,128)(2,1)S(1)}, u32[]{:S(2)}, u32[]{:S(2)}) collective-permute-start(bf16[16,512]{1,0:T(8,128)(2,1)S(1)} %get-tuple-element.190), channel_id=1, source_target_pairs={{0,2},{1,3},{2,0},{3,1},{4,6},{5,7},{6,4},{7,5},{8,10},{9,11},{10,... | collective-permute-start | bytes 49160 | tf_op jit(solution)/shard_map/ppermute | solution.py:250
  33.0 6.3 %collective-permute-start.17 = (bf16[8,512]{1,0:T(8,128)(2,1)S(1)}, bf16[8,512]{1,0:T(8,128)(2,1)S(1)}, u32[]{:S(2)}, u32[]{:S(2)}) collective-permute-start(bf16[8,512]{1,0:T(8,128)(2,1)S(1)} %get-tuple-element.223), channel_id=1, source_target_pairs={{0,12},{4,8},{8,4},{12,0},{1,13},{5,9},{9,5},{13,1},{2,14},{6,10},... | collective-permute-start | bytes 24584 | tf_op jit(solution)/shard_map/ppermute | solution.py:247
  34.0 5.4 %collective-permute-start.18 = (bf16[8,512]{1,0:T(8,128)(2,1)S(1)}, bf16[8,512]{1,0:T(8,128)(2,1)S(1)}, u32[]{:S(2)}, u32[]{:S(2)}) collective-permute-start(bf16[8,512]{1,0:T(8,128)(2,1)S(1)} %get-tuple-element.224), channel_id=1, source_target_pairs={{0,4},{4,0},{8,12},{12,8},{1,5},{5,1},{9,13},{13,9},{2,6},{6,2},{1... | collective-permute-start | bytes 24584 | tf_op jit(solution)/shard_map/ppermute | solution.py:248
  34.8 4.6 %collective-permute-start.19 = (bf16[8,512]{1,0:T(8,128)(2,1)S(1)}, bf16[8,512]{1,0:T(8,128)(2,1)S(1)}, u32[]{:S(2)}, u32[]{:S(2)}) collective-permute-start(bf16[8,512]{1,0:T(8,128)(2,1)S(1)} %get-tuple-element.225), channel_id=1, source_target_pairs={{0,3},{1,2},{2,1},{3,0},{4,7},{5,6},{6,5},{7,4},{8,11},{9,10},{10,... | collective-permute-start | bytes 24584 | tf_op jit(solution)/shard_map/ppermute | solution.py:250
  40.1 11.1 %collective-permute-start.23 = (bf16[384,512]{1,0:T(8,128)(2,1)S(1)}, bf16[384,512]{1,0:T(8,128)(2,1)S(1)}, u32[]{:S(2)}, u32[]{:S(2)}) collective-permute-start(bf16[384,512]{1,0:T(8,128)(2,1)S(1)} %get-tuple-element.250), channel_id=1, source_target_pairs={{0,2},{1,3},{2,0},{3,1},{4,6},{5,7},{6,4},{7,5},{8,10},{9,11},{10,... | collective-permute-start | bytes 1179656 | tf_op jit(solution)/shard_map/ppermute | solution.py:162
  44.2 7.0 %collective-permute-start.22 = (bf16[288,512]{1,0:T(8,128)(2,1)S(1)}, bf16[288,512]{1,0:T(8,128)(2,1)S(1)}, u32[]{:S(2)}, u32[]{:S(2)}) collective-permute-start(bf16[288,512]{1,0:T(8,128)(2,1)S(1)} %get-tuple-element.249), channel_id=1, source_target_pairs={{0,1},{1,0},{2,3},{3,2},{4,5},{5,4},{6,7},{7,6},{8,9},{9,8},{10,11... | collective-permute-start | bytes 884744 | tf_op jit(solution)/shard_map/ppermute | solution.py:162
  51.8 9.3 %collective-permute-start.25 = (bf16[512,512]{1,0:T(8,128)(2,1)S(1)}, bf16[512,512]{1,0:T(8,128)(2,1)S(1)}, u32[]{:S(2)}, u32[]{:S(2)}) collective-permute-start(bf16[512,512]{1,0:T(8,128)(2,1)S(1)} %get-tuple-element.263), channel_id=1, source_target_pairs={{0,1},{1,0},{2,3},{3,2},{4,5},{5,4},{6,7},{7,6},{8,9},{9,8},{10,11... | collective-permute-start | bytes 1572872 | tf_op jit(solution)/shard_map/ppermute | solution.py:162
  51.8 9.1 %collective-permute-start.24 = (bf16[256,512]{1,0:T(8,128)(2,1)S(1)}, bf16[256,512]{1,0:T(8,128)(2,1)S(1)}, u32[]{:S(2)}, u32[]{:S(2)}) collective-permute-start(bf16[256,512]{1,0:T(8,128)(2,1)S(1)} %get-tuple-element.260), channel_id=1, source_target_pairs={{0,2},{1,3},{2,0},{3,1},{4,6},{5,7},{6,4},{7,5},{8,10},{9,11},{10,... | collective-permute-start | bytes 786440 | tf_op jit(solution)/shard_map/ppermute | solution.py:162
  53.2 10.9 %collective-permute-start.26 = (bf16[192,512]{1,0:T(8,128)(2,1)S(1)}, bf16[192,512]{1,0:T(8,128)(2,1)S(1)}, u32[]{:S(2)}, u32[]{:S(2)}) collective-permute-start(bf16[192,512]{1,0:T(8,128)(2,1)S(1)} %get-tuple-element.269), channel_id=1, source_target_pairs={{0,4},{1,5},{2,6},{3,7},{4,0},{5,1},{6,2},{7,3},{8,12},{9,13},{10,... | collective-permute-start | bytes 589832 | tf_op jit(solution)/shard_map/ppermute | solution.py:162
  54.7 9.7 %collective-permute-start.27 = (bf16[160,512]{1,0:T(8,128)(2,1)S(1)}, bf16[160,512]{1,0:T(8,128)(2,1)S(1)}, u32[]{:S(2)}, u32[]{:S(2)}) collective-permute-start(bf16[160,512]{1,0:T(8,128)(2,1)S(1)} %get-tuple-element.272), channel_id=1, source_target_pairs={{0,2},{1,3},{2,0},{3,1},{4,6},{5,7},{6,4},{7,5},{8,10},{9,11},{10,... | collective-permute-start | bytes 491528 | tf_op jit(solution)/shard_map/ppermute | solution.py:162
  61.3 10.8 %collective-permute-start.31 = (bf16[256,512]{1,0:T(8,128)(2,1)S(1)}, bf16[256,512]{1,0:T(8,128)(2,1)S(1)}, u32[]{:S(2)}, u32[]{:S(2)}) collective-permute-start(bf16[256,512]{1,0:T(8,128)(2,1)S(1)} %get-tuple-element.285), channel_id=1, source_target_pairs={{0,2},{1,3},{2,0},{3,1},{4,6},{5,7},{6,4},{7,5},{8,10},{9,11},{10,... | collective-permute-start | bytes 786440 | tf_op jit(solution)/shard_map/ppermute | solution.py:162
  62.6 7.1 %collective-permute-start.28 = (bf16[128,512]{1,0:T(8,128)(2,1)S(1)}, bf16[128,512]{1,0:T(8,128)(2,1)S(1)}, u32[]{:S(2)}, u32[]{:S(2)}) collective-permute-start(bf16[128,512]{1,0:T(8,128)(2,1)S(1)} %get-tuple-element.278), channel_id=1, source_target_pairs={{0,4},{1,5},{2,6},{3,7},{4,0},{5,1},{6,2},{7,3},{8,12},{9,13},{10,... | collective-permute-start | bytes 393224 | tf_op jit(solution)/shard_map/ppermute | solution.py:162
  64.5 7.0 %collective-permute-start.29 = (bf16[96,512]{1,0:T(8,128)(2,1)S(1)}, bf16[96,512]{1,0:T(8,128)(2,1)S(1)}, u32[]{:S(2)}, u32[]{:S(2)}) collective-permute-start(bf16[96,512]{1,0:T(8,128)(2,1)S(1)} %get-tuple-element.281), channel_id=1, source_target_pairs={{0,4},{1,5},{2,6},{3,7},{4,0},{5,1},{6,2},{7,3},{8,12},{9,13},{10,... | collective-permute-start | bytes 294920 | tf_op jit(solution)/shard_map/ppermute | solution.py:162
  65.8 6.3 %collective-permute-start.30 = (bf16[96,512]{1,0:T(8,128)(2,1)S(1)}, bf16[96,512]{1,0:T(8,128)(2,1)S(1)}, u32[]{:S(2)}, u32[]{:S(2)}) collective-permute-start(bf16[96,512]{1,0:T(8,128)(2,1)S(1)} %get-tuple-element.283), channel_id=1, source_target_pairs={{0,8},{1,9},{2,10},{3,11},{4,12},{5,13},{6,14},{7,15},{8,0},{9,1},... | collective-permute-start | bytes 294920 | tf_op jit(solution)/shard_map/ppermute | solution.py:162
  72.3 9.5 %collective-permute-start.34 = (bf16[128,512]{1,0:T(8,128)(2,1)S(1)}, bf16[128,512]{1,0:T(8,128)(2,1)S(1)}, u32[]{:S(2)}, u32[]{:S(2)}) collective-permute-start(bf16[128,512]{1,0:T(8,128)(2,1)S(1)} %get-tuple-element.302), channel_id=1, source_target_pairs={{0,4},{1,5},{2,6},{3,7},{4,0},{5,1},{6,2},{7,3},{8,12},{9,13},{10,... | collective-permute-start | bytes 393224 | tf_op jit(solution)/shard_map/ppermute | solution.py:162
  74.7 5.5 %collective-permute-start.32 = (bf16[48,512]{1,0:T(8,128)(2,1)S(1)}, bf16[48,512]{1,0:T(8,128)(2,1)S(1)}, u32[]{:S(2)}, u32[]{:S(2)}) collective-permute-start(bf16[48,512]{1,0:T(8,128)(2,1)S(1)} %get-tuple-element.288), channel_id=1, source_target_pairs={{0,8},{1,9},{2,10},{3,11},{4,12},{5,13},{6,14},{7,15},{8,0},{9,1},... | collective-permute-start | bytes 147464 | tf_op jit(solution)/shard_map/ppermute | solution.py:162
  76.4 5.4 %collective-permute-start.33 = (bf16[64,512]{1,0:T(8,128)(2,1)S(1)}, bf16[64,512]{1,0:T(8,128)(2,1)S(1)}, u32[]{:S(2)}, u32[]{:S(2)}) collective-permute-start(bf16[64,512]{1,0:T(8,128)(2,1)S(1)} %get-tuple-element.295), channel_id=1, source_target_pairs={{0,8},{1,9},{2,10},{3,11},{4,12},{5,13},{6,14},{7,15},{8,0},{9,1},... | collective-permute-start | bytes 196616 | tf_op jit(solution)/shard_map/ppermute | solution.py:162
  81.9 5.6 %collective-permute-start.35 = (bf16[64,512]{1,0:T(8,128)(2,1)S(1)}, bf16[64,512]{1,0:T(8,128)(2,1)S(1)}, u32[]{:S(2)}, u32[]{:S(2)}) collective-permute-start(bf16[64,512]{1,0:T(8,128)(2,1)S(1)} %get-tuple-element.304), channel_id=1, source_target_pairs={{0,8},{1,9},{2,10},{3,11},{4,12},{5,13},{6,14},{7,15},{8,0},{9,1},... | collective-permute-start | bytes 196616 | tf_op jit(solution)/shard_map/ppermute | solution.py:162
  (15 other events, 60.9 us)

commit v9 on v8

--- a/solution.py
+++ b/solution.py
@@ -683,7 +683,7 @@
         flops=10 * unit, scratch=[pltpu.VMEM((degree * nodes, width), BF)],
     )
     if split:
-        give0, *arr4 = lax.optimization_barrier((give0, *arr4))
+        give0, give2, *arr4 = lax.optimization_barrier((give0, give2, *arr4))
         keep0, give0 = halve_step(1, keep0, swap(give0, 0, dims), place)
         keep0, *arr4 = lax.optimization_barrier((keep0, *arr4))
     shapes = blocks_shapes(1, width, width, dims)
@@ -715,46 +715,45 @@
     else:
         arr1 = swap(give1, 1, dims)
         arr0 = swap(give0, 1, dims)
+        arr2 = swap(give2, 0, dims)
         arr_e, arr1 = lax.optimization_barrier((swap(give_e, 0, dims), arr1))
+        keep1, give1 = halve_step(2, keep1, arr1, place)
+        arr1 = swap(give1, 2, dims)
+        keep_e, keep1 = lax.optimization_barrier((keep_e, keep1))
         keep_e, give_e, from_sub, _ = carry_step(1, keep_e, arr_e, pay5[1:2], place, capacity)
         arr_e = swap(give_e, 1, dims)
-        give2, keep1, keep_e = lax.optimization_barrier((give2, keep1, keep_e))
-        arr2 = swap(give2, 0, dims)
-        keep1, give1 = halve_step(2, keep1, arr1, place)
-        arr1 = swap(give1, 2, dims)
-        keep0, keep1 = lax.optimization_barrier((keep0, keep1))
+        keep2, keep_e = lax.optimization_barrier((keep2, keep_e))
+        keep2, give2 = halve_step(1, keep2, arr2, place)
+        arr2 = swap(give2, 1, dims)
+        keep0, keep2 = lax.optimization_barrier((keep0, keep2))
         keep0, give0 = halve_step(2, keep0, arr0, place)
         arr0 = swap(give0, 2, dims)
-        keep2, keep0 = lax.optimization_barrier((keep2, keep0))
-        keep2, give2 = halve_step(1, keep2, arr2, place)
-        arr2 = swap(give2, 1, dims)
-        keep1, keep2 = lax.optimization_barrier((keep1, keep2))
+        keep1, keep0 = lax.optimization_barrier((keep1, keep0))
         keep1, give1 = halve_step(3, keep1, arr1, place)
         arr1 = swap(give1, 3, dims)
-        keep_e, keep1 = lax.optimization_barrier((keep_e, keep1))
+        keep2, keep1 = lax.optimization_barrier((keep2, keep1))
+        keep2, give2 = halve_step(2, keep2, arr2, place)
+        arr2 = swap(give2, 2, dims)
+        keep0, keep2 = lax.optimization_barrier((keep0, keep2))
+        keep0, give0 = halve_step(3, keep0, arr0, place)
+        arr0 = swap(give0, 3, dims)
+        keep_e, keep0, arr1 = lax.optimization_barrier((keep_e, keep0, arr1))
         keep_e, give_e, from_lat, from_diag = carry_step(
             2, keep_e, arr_e, pay5[3:], place, capacity
         )
         arr_e = swap(give_e, 2, dims)
-        keep0, keep_e = lax.optimization_barrier((keep0, keep_e))
-        keep0, give0 = halve_step(3, keep0, arr0, place)
-        arr0 = swap(give0, 3, dims)
-        keep_e, keep0 = lax.optimization_barrier((keep_e, keep0))
+        keep2, keep_e = lax.optimization_barrier((keep2, keep_e))
+        keep2, give2 = halve_step(3, keep2, arr2, place)
+        arr2 = swap(give2, 3, dims)
+        keep_e, keep2, arr0 = lax.optimization_barrier((keep_e, keep2, arr0))
         keep_e, give_e, from_near, _ = carry_step(3, keep_e, arr_e, (), place, capacity)
         arr_e = swap(give_e, 3, dims)
-        keep2, keep_e, arr1 = lax.optimization_barrier((keep2, keep_e, arr1))
-        keep2, give2 = halve_step(2, keep2, arr2, place)
-        arr2 = swap(give2, 2, dims)
         arr5 = (arr_e, from_near, from_diag, from_lat, from_sub)
-        gpre_g, keep2 = lax.optimization_barrier((gpre_g, keep2))
+        sums = ((keep1, arr1), (keep0, arr0), (keep2, arr2), (keep_e, arr_e))
     (grid_grad,) = call(
         lambda *refs: grid_place(peers, *refs), "grid_place", [shape(chosen, width)],
         (*arr5, gpre_g, embed, sends_row), flops=3 * unit,
     )
-    if carry:
-        keep2, grid_grad, arr0 = lax.optimization_barrier((keep2, grid_grad, arr0))
-        keep2, give2 = halve_step(3, keep2, arr2, place)
-        sums = ((keep1, arr1), (keep0, arr0), (keep2, swap(give2, 3, dims)), (keep_e, arr_e))
     if split:
         grads = call(
             finish, "finish",

time: 88.5 us -> 82.5 us (0.932)
  waiting for transfers between devices: 25.3 us -> 20 us
    ppermute x16, waiting for transfers between devices: 23.1 us -> 17.9 us  [swap(): return lax.ppermute(block, GROUP, [(i, i ^ 1 << bit) for i in range(total)])]
  transfers between devices with their start and end apart: 36 -> 36, of which waited for: 13 -> 12; matrix products, arithmetic and copies ran while one was open for 0% -> 0% of each run, Pallas kernels for 18% -> 20%
where the time goes in v9:
time: 82.5 us; the launch traced here: 82.3 us
  starting transfers between devices  36.9 us (45%)
  Pallas kernels  22.8 us (28%)
  waiting for transfers between devices  20 us (24%)
  local copies, waits for them, and re-layouts  1.56 us (2%)
  between operations  0.92 us (1%)
    pallas_call x24, Pallas kernels, call(): pl.pallas_call(kernel, out_shape=[shape(*a.shape, dtype=a.dtype) for a in...  22.8 us
    ppermute x16, starting transfers between devices, swap(): return lax.ppermute(block, GROUP, [(i, i ^ 1 << bit) for i in range(total)])  18.2 us
    ppermute x16, waiting for transfers between devices, swap(): return lax.ppermute(block, GROUP, [(i, i ^ 1 << bit) for i in range(total)])  17.9 us
    ppermute x4, starting transfers between devices, exchange(): far = lax.ppermute(parts[column], 'lon', other)  9.87 us
    ppermute x12, starting transfers between devices, exchange(): lax.ppermute(parts[r - 1], COLUMN, [(i, i ^ r) for i in range(column)])  6.88 us
    ppermute x4, starting transfers between devices, exchange(): lax.ppermute(parts[column - 1], 'lon', [(i, i ^ 1) for i in range(count)])  2 us
  transfers between devices with their start and end apart: 36, of which 12 were waited for; matrix products, arithmetic and copies ran while one was open for 0% of the time, Pallas kernels for 20%

profile of v9, /device:TPU:0, one launch (start us, length us, event | category | flops | bytes accessed | tf_op | source)
XLA Modules:
  0.0 82.3 jit_solution(8045274428522763743)
XLA Ops:
  2.3 1.6 %first_payload.1 = (bf16[512,512]{1,0:T(8,128)(2,1)S(1)}, bf16[512,512]{1,0:T(8,128)(2,1)S(1)}, s32[1,512]{1,0:T(1,128)S(1)}, s32[6,256]{1,0:T(8,128)S(1)}, bf16...) custom-call(bf16[512,512]{1,0:T(8,128)(2,1)} %refs_0_.1, ...), custom_call_target="tpu_custom_call" | custom-call | flops 67108864 | bytes 2188688 | tf_op jit(solution)/shard_map/first_payload/pallas_call | solution.py:231
  3.9 5.1 %collective-permute-start = (bf16[16,512]{1,0:T(8,128)(2,1)S(1)}, bf16[16,512]{1,0:T(8,128)(2,1)S(1)}, u32[]{:S(2)}, u32[]{:S(2)}) collective-permute-start(bf16[16,512]{1,0:T(8,128)(2,1)S(1)} %get-tuple-element.163), channel_id=1, source_target_pairs={{0,12},{4,8},{8,4},{12,0},{1,13},{5,9},{9,5},{13,1},{2,14},{6,10},... | collective-permute-start | bytes 49160 | tf_op jit(solution)/shard_map/ppermute | solution.py:247
  16.3 1.5 %collective-permute-start.8 = (bf16[32,512]{1,0:T(8,128)(2,1)S(1)}, bf16[32,512]{1,0:T(8,128)(2,1)S(1)}, u32[]{:S(2)}, u32[]{:S(2)}) collective-permute-start(bf16[32,512]{1,0:T(8,128)(2,1)S(1)} %get-tuple-element.178), channel_id=1, source_target_pairs={{0,2},{1,3},{2,0},{3,1},{4,6},{5,7},{6,4},{7,5},{8,10},{9,11},{10,... | collective-permute-start | bytes 98312 | tf_op jit(solution)/shard_map/ppermute | solution.py:250
  18.1 1.9 %forward_local.1 = (f32[256,512]{1,0:T(8,128)S(1)}, bf16[6,256,512]{2,1,0:T(8,128)(2,1)S(1)}, f32[40,512]{1,0:T(8,128)S(1)}, bf16[40,512]{1,0:T(8,128)(2,1)S(1)}) custom-call(bf16[256,512]{1,0:T(8,128)(2,1)S(1)} %get-tuple-element.180.state_ref.refs_7_.refs_10_, bf16[2,512,512]{2,1,0:T(8,128)(2,1)S(1)} %copy-done, bf16[2,512,512]{2,1,0:T(8,128)(2,1)S(1)} %copy-done.2, ...), custom_call_target="tpu_custom_call" | custom-call | flops 805306368 | bytes 4593824 | tf_op jit(solution)/shard_map/forward_local/pallas_call | solution.py:231
  21.4 2.7 %collective-permute-start.10 = (bf16[16,512]{1,0:T(8,128)(2,1)S(1)}, bf16[16,512]{1,0:T(8,128)(2,1)S(1)}, u32[]{:S(2)}, u32[]{:S(2)}) collective-permute-start(bf16[16,512]{1,0:T(8,128)(2,1)S(1)} %get-tuple-element.185), channel_id=1, source_target_pairs={{0,12},{4,8},{8,4},{12,0},{1,13},{5,9},{9,5},{13,1},{2,14},{6,10},... | collective-permute-start | bytes 49160 | tf_op jit(solution)/shard_map/ppermute | solution.py:247
  26.5 3.0 %turn_local.1 = (f32[256,512]{1,0:T(8,128)S(1)}, f32[256,512]{1,0:T(8,128)S(1)}, f32[256,512]{1,0:T(8,128)S(1)}, f32[40,512]{1,0:T(8,128)S(1)}, bf16[40,512]{1,0...) custom-call(bf16[256,512]{1,0:T(8,128)(2,1)S(1)} %get-tuple-element., ...), custom_call_target="tpu_custom_call" | custom-call | flops 1342177280 | bytes 5871776 | tf_op jit(solution)/shard_map/turn_local/pallas_call | solution.py:231
  29.6 1.4 %turn_halo.1 = (bf16[256,512]{1,0:T(8,128)(2,1)S(1)}, bf16[256,512]{1,0:T(8,128)(2,1)S(1)}, bf16[256,512]{1,0:T(8,128)(2,1)S(1)}, bf16[256,512]{1,0:T(8,128)(2,1...) custom-call(bf16[16,512]{1,0:T(8,128)(2,1)S(1)} %collective-permute-, ...), custom_call_target="tpu_custom_call" | custom-call | flops 402653184 | bytes 5322912 | tf_op jit(solution)/shard_map/turn_halo/pallas_call | solution.py:231
  31.0 1.5 %last_weights.1 = (bf16[768,512]{1,0:T(8,128)(2,1)S(1)}, bf16[768,512]{1,0:T(8,128)(2,1)S(1)}, bf16[256,512]{1,0:T(8,128)(2,1)}) custom-call(s32[6,6]{1,0:T(8,128)S(1)} %get-tuple-element.162.refs_0_.refs_5_, bf16[256,512]{1,0:T(8,128)(2,1)S(1)} %get-tuple-element.184.state_ref.refs_1_, bf16[256,512]{1,0:T(8,128)(2,1)S(1)} %get-tuple-element.202.refs_2_, ...), custom_call_target="tpu_custom_call" | custom-call | flops 536870912 | bytes 4194448 | tf_op jit(solution)/shard_map/last_weights/pallas_call | solution.py:231
  36.4 2.9 %back_local.1 = (f32[256,512]{1,0:T(8,128)S(1)}, bf16[512,512]{1,0:T(8,128)(2,1)S(1)}, bf16[512,512]{1,0:T(8,128)(2,1)S(1)}, bf16[512,512]{1,0:T(8,128)(2,1)S(1)}, bf16[512,512]{1,0:T(8,128)(2,1)S(1)}) custom-call(s32[6,6]{1,0:T(8,128)S(1)} %get-tuple-element.162.refs_0_.refs_5_, bf16[256,512]{1,0:T(8,128)(2,1)S(1)} %get-tuple-element.206.refs_1_, ...), custom_call_target="tpu_custom_call" | custom-call | flops 1342177280 | bytes 8960144 | tf_op jit(solution)/shard_map/back_local/pallas_call | solution.py:231
  40.1 1.2 %collective-permute-start.23 = (bf16[384,512]{1,0:T(8,128)(2,1)S(1)}, bf16[384,512]{1,0:T(8,128)(2,1)S(1)}, u32[]{:S(2)}, u32[]{:S(2)}) collective-permute-start(bf16[384,512]{1,0:T(8,128)(2,1)S(1)} %get-tuple-element.246), channel_id=1, source_target_pairs={{0,2},{1,3},{2,0},{3,1},{4,6},{5,7},{6,4},{7,5},{8,10},{9,11},{10,... | collective-permute-start | bytes 1179656 | tf_op jit(solution)/shard_map/ppermute | solution.py:162
  41.9 2.3 %embed_back.1 = (bf16[512,512]{1,0:T(8,128)(2,1)S(1)}, bf16[256,512]{1,0:T(8,128)(2,1)S(1)}, bf16[288,512]{1,0:T(8,128)(2,1)S(1)}, bf16[16,512]{1,0:T(8,128)(2,1...) custom-call(bf16[8,512]{1,0:T(8,128)(2,1)S(1)} %collective-permute-d, ...), custom_call_target="tpu_custom_call" | custom-call | flops 805306368 | bytes 6130608 | tf_op jit(solution)/shard_map/embed_back/pallas_call | solution.py:231
  45.8 6.3 %collective-permute-done.23.refs_2_ = bf16[384,512]{1,0:T(8,128)(2,1)S(1)} collective-permute-done((bf16[384,512]{1,0:T(8,128)(2,1)S(1)}, bf16[384,512]{1,0:T(8,128)(2,1)S(1)}, u32[]{:S(2)}, u32[]{:S(2)}) %collective-permute-start.23) | collective-permute-done | bytes 393248 | tf_op jit(solution)/shard_map/ppermute | solution.py:162
  52.9 1.3 %collective-permute-start.26 = (bf16[192,512]{1,0:T(8,128)(2,1)S(1)}, bf16[192,512]{1,0:T(8,128)(2,1)S(1)}, u32[]{:S(2)}, u32[]{:S(2)}) collective-permute-start(bf16[192,512]{1,0:T(8,128)(2,1)S(1)} %get-tuple-element.265), channel_id=1, source_target_pairs={{0,4},{1,5},{2,6},{3,7},{4,0},{5,1},{6,2},{7,3},{8,12},{9,13},{10,... | collective-permute-start | bytes 589832 | tf_op jit(solution)/shard_map/ppermute | solution.py:162
  54.4 1.4 %collective-permute-start.27 = (bf16[256,512]{1,0:T(8,128)(2,1)S(1)}, bf16[256,512]{1,0:T(8,128)(2,1)S(1)}, u32[]{:S(2)}, u32[]{:S(2)}) collective-permute-start(bf16[256,512]{1,0:T(8,128)(2,1)S(1)} %get-tuple-element.268), channel_id=1, source_target_pairs={{0,2},{1,3},{2,0},{3,1},{4,6},{5,7},{6,4},{7,5},{8,10},{9,11},{10,... | collective-permute-start | bytes 786440 | tf_op jit(solution)/shard_map/ppermute | solution.py:162
  57.8 1.3 %collective-permute-start.28 = (bf16[128,512]{1,0:T(8,128)(2,1)S(1)}, bf16[128,512]{1,0:T(8,128)(2,1)S(1)}, u32[]{:S(2)}, u32[]{:S(2)}) collective-permute-start(bf16[128,512]{1,0:T(8,128)(2,1)S(1)} %get-tuple-element.273), channel_id=1, source_target_pairs={{0,4},{1,5},{2,6},{3,7},{4,0},{5,1},{6,2},{7,3},{8,12},{9,13},{10,... | collective-permute-start | bytes 393224 | tf_op jit(solution)/shard_map/ppermute | solution.py:162
  59.3 2.4 %collective-permute-start.29 = (bf16[96,512]{1,0:T(8,128)(2,1)S(1)}, bf16[96,512]{1,0:T(8,128)(2,1)S(1)}, u32[]{:S(2)}, u32[]{:S(2)}) collective-permute-start(bf16[96,512]{1,0:T(8,128)(2,1)S(1)} %get-tuple-element.275), channel_id=1, source_target_pairs={{0,8},{1,9},{2,10},{3,11},{4,12},{5,13},{6,14},{7,15},{8,0},{9,1},... | collective-permute-start | bytes 294920 | tf_op jit(solution)/shard_map/ppermute | solution.py:162
  61.7 2.0 %collective-permute-done.27.refs_2_ = bf16[256,512]{1,0:T(8,128)(2,1)S(1)} collective-permute-done((bf16[256,512]{1,0:T(8,128)(2,1)S(1)}, bf16[256,512]{1,0:T(8,128)(2,1)S(1)}, u32[]{:S(2)}, u32[]{:S(2)}) %collective-permute-start.27) | collective-permute-done | bytes 262176 | tf_op jit(solution)/shard_map/ppermute | solution.py:162
  66.5 1.2 %collective-permute-start.33 = (bf16[96,512]{1,0:T(8,128)(2,1)S(1)}, bf16[96,512]{1,0:T(8,128)(2,1)S(1)}, u32[]{:S(2)}, u32[]{:S(2)}) collective-permute-start(bf16[96,512]{1,0:T(8,128)(2,1)S(1)} %get-tuple-element.287), channel_id=1, source_target_pairs={{0,4},{1,5},{2,6},{3,7},{4,0},{5,1},{6,2},{7,3},{8,12},{9,13},{10,... | collective-permute-start | bytes 294920 | tf_op jit(solution)/shard_map/ppermute | solution.py:162
  67.7 2.0 %collective-permute-start.32 = (bf16[64,512]{1,0:T(8,128)(2,1)S(1)}, bf16[64,512]{1,0:T(8,128)(2,1)S(1)}, u32[]{:S(2)}, u32[]{:S(2)}) collective-permute-start(bf16[64,512]{1,0:T(8,128)(2,1)S(1)} %get-tuple-element.285), channel_id=1, source_target_pairs={{0,8},{1,9},{2,10},{3,11},{4,12},{5,13},{6,14},{7,15},{8,0},{9,1},... | collective-permute-start | bytes 196616 | tf_op jit(solution)/shard_map/ppermute | solution.py:162
  69.9 3.4 %collective-permute-done.32.arr0_ref = bf16[64,512]{1,0:T(8,128)(2,1)S(1)} collective-permute-done((bf16[64,512]{1,0:T(8,128)(2,1)S(1)}, bf16[64,512]{1,0:T(8,128)(2,1)S(1)}, u32[]{:S(2)}, u32[]{:S(2)}) %collective-permute-start.32) | collective-permute-done | bytes 65568 | tf_op jit(solution)/shard_map/ppermute | solution.py:162
  73.9 1.7 %collective-permute-start.34 = (bf16[48,512]{1,0:T(8,128)(2,1)S(1)}, bf16[48,512]{1,0:T(8,128)(2,1)S(1)}, u32[]{:S(2)}, u32[]{:S(2)}) collective-permute-start(bf16[48,512]{1,0:T(8,128)(2,1)S(1)} %get-tuple-element.288), channel_id=1, source_target_pairs={{0,8},{1,9},{2,10},{3,11},{4,12},{5,13},{6,14},{7,15},{8,0},{9,1},... | collective-permute-start | bytes 147464 | tf_op jit(solution)/shard_map/ppermute | solution.py:162
  75.6 1.2 %collective-permute-start.35 = (bf16[64,512]{1,0:T(8,128)(2,1)S(1)}, bf16[64,512]{1,0:T(8,128)(2,1)S(1)}, u32[]{:S(2)}, u32[]{:S(2)}) collective-permute-start(bf16[64,512]{1,0:T(8,128)(2,1)S(1)} %get-tuple-element.300), channel_id=1, source_target_pairs={{0,8},{1,9},{2,10},{3,11},{4,12},{5,13},{6,14},{7,15},{8,0},{9,1},... | collective-permute-start | bytes 196616 | tf_op jit(solution)/shard_map/ppermute | solution.py:162
  76.8 3.3 %collective-permute-done.34.refs_0_.arr_e_ref = bf16[48,512]{1,0:T(8,128)(2,1)S(1)} collective-permute-done((bf16[48,512]{1,0:T(8,128)(2,1)S(1)}, bf16[48,512]{1,0:T(8,128)(2,1)S(1)}, u32[]{:S(2)}, u32[]{:S(2)}) %collective-permute-start.34) | collective-permute-done | bytes 49184 | tf_op jit(solution)/shard_map/ppermute | solution.py:162
  80.1 1.3 %grid_place.1 = bf16[512,512]{1,0:T(8,128)(2,1)} custom-call(bf16[48,512]{1,0:T(8,128)(2,1)S(1)} %collective-permute-done.34.refs_0_.arr_e_ref, bf16[16,512]{1,0:T(8,128)(2,1)S(1)} %get-tuple-element.289.refs_1_, bf16[16,512]{1,0:T(8,128)(2,1)S(1)} %get-tuple-element.290.refs_2_, bf16[16,512]{1,0:T(8,128)(2,1)S(1)} %get-tuple-element.291.refs_3_, ...), custom_call_target="tpu_custom_call" | custom-call | flops 402653184 | bytes 1687872 | tf_op jit(solution)/shard_map/grid_place/pallas_call | solution.py:231
  (83 shorter events, 27.3 us)
Async XLA Ops:
  3.9 8.0 %collective-permute-start = (bf16[16,512]{1,0:T(8,128)(2,1)S(1)}, bf16[16,512]{1,0:T(8,128)(2,1)S(1)}, u32[]{:S(2)}, u32[]{:S(2)}) collective-permute-start(bf16[16,512]{1,0:T(8,128)(2,1)S(1)} %get-tuple-element.163), channel_id=1, source_target_pairs={{0,12},{4,8},{8,4},{12,0},{1,13},{5,9},{9,5},{13,1},{2,14},{6,10},... | collective-permute-start | bytes 49160 | tf_op jit(solution)/shard_map/ppermute | solution.py:247
  14.5 5.8 %collective-permute-start.5 = (bf16[32,512]{1,0:T(8,128)(2,1)S(1)}, bf16[32,512]{1,0:T(8,128)(2,1)S(1)}, u32[]{:S(2)}, u32[]{:S(2)}) collective-permute-start(bf16[32,512]{1,0:T(8,128)(2,1)S(1)} %get-tuple-element.175), channel_id=1, source_target_pairs={{0,12},{4,8},{8,4},{12,0},{1,13},{5,9},{9,5},{13,1},{2,14},{6,10},... | collective-permute-start | bytes 98312 | tf_op jit(solution)/shard_map/ppermute | solution.py:247
  15.6 4.7 %collective-permute-start.6 = (bf16[32,512]{1,0:T(8,128)(2,1)S(1)}, bf16[32,512]{1,0:T(8,128)(2,1)S(1)}, u32[]{:S(2)}, u32[]{:S(2)}) collective-permute-start(bf16[32,512]{1,0:T(8,128)(2,1)S(1)} %get-tuple-element.176), channel_id=1, source_target_pairs={{0,4},{4,0},{8,12},{12,8},{1,5},{5,1},{9,13},{13,9},{2,6},{6,2},{1... | collective-permute-start | bytes 98312 | tf_op jit(solution)/shard_map/ppermute | solution.py:248
  21.4 8.1 %collective-permute-start.10 = (bf16[16,512]{1,0:T(8,128)(2,1)S(1)}, bf16[16,512]{1,0:T(8,128)(2,1)S(1)}, u32[]{:S(2)}, u32[]{:S(2)}) collective-permute-start(bf16[16,512]{1,0:T(8,128)(2,1)S(1)} %get-tuple-element.185), channel_id=1, source_target_pairs={{0,12},{4,8},{8,4},{12,0},{1,13},{5,9},{9,5},{13,1},{2,14},{6,10},... | collective-permute-start | bytes 49160 | tf_op jit(solution)/shard_map/ppermute | solution.py:247
  24.1 5.4 %collective-permute-start.11 = (bf16[16,512]{1,0:T(8,128)(2,1)S(1)}, bf16[16,512]{1,0:T(8,128)(2,1)S(1)}, u32[]{:S(2)}, u32[]{:S(2)}) collective-permute-start(bf16[16,512]{1,0:T(8,128)(2,1)S(1)} %get-tuple-element.186), channel_id=1, source_target_pairs={{0,4},{4,0},{8,12},{12,8},{1,5},{5,1},{9,13},{13,9},{2,6},{6,2},{1... | collective-permute-start | bytes 49160 | tf_op jit(solution)/shard_map/ppermute | solution.py:248
  24.7 4.9 %collective-permute-start.12 = (bf16[16,512]{1,0:T(8,128)(2,1)S(1)}, bf16[16,512]{1,0:T(8,128)(2,1)S(1)}, u32[]{:S(2)}, u32[]{:S(2)}) collective-permute-start(bf16[16,512]{1,0:T(8,128)(2,1)S(1)} %get-tuple-element.187), channel_id=1, source_target_pairs={{0,3},{1,2},{2,1},{3,0},{4,7},{5,6},{6,5},{7,4},{8,11},{9,10},{10,... | collective-permute-start | bytes 49160 | tf_op jit(solution)/shard_map/ppermute | solution.py:250
  25.1 4.4 %collective-permute-start.13 = (bf16[16,512]{1,0:T(8,128)(2,1)S(1)}, bf16[16,512]{1,0:T(8,128)(2,1)S(1)}, u32[]{:S(2)}, u32[]{:S(2)}) collective-permute-start(bf16[16,512]{1,0:T(8,128)(2,1)S(1)} %get-tuple-element.188), channel_id=1, source_target_pairs={{0,2},{1,3},{2,0},{3,1},{4,6},{5,7},{6,4},{7,5},{8,10},{9,11},{10,... | collective-permute-start | bytes 49160 | tf_op jit(solution)/shard_map/ppermute | solution.py:250
  33.0 6.3 %collective-permute-start.17 = (bf16[8,512]{1,0:T(8,128)(2,1)S(1)}, bf16[8,512]{1,0:T(8,128)(2,1)S(1)}, u32[]{:S(2)}, u32[]{:S(2)}) collective-permute-start(bf16[8,512]{1,0:T(8,128)(2,1)S(1)} %get-tuple-element.222), channel_id=1, source_target_pairs={{0,12},{4,8},{8,4},{12,0},{1,13},{5,9},{9,5},{13,1},{2,14},{6,10},... | collective-permute-start | bytes 24584 | tf_op jit(solution)/shard_map/ppermute | solution.py:247
  34.0 5.4 %collective-permute-start.18 = (bf16[8,512]{1,0:T(8,128)(2,1)S(1)}, bf16[8,512]{1,0:T(8,128)(2,1)S(1)}, u32[]{:S(2)}, u32[]{:S(2)}) collective-permute-start(bf16[8,512]{1,0:T(8,128)(2,1)S(1)} %get-tuple-element.223), channel_id=1, source_target_pairs={{0,4},{4,0},{8,12},{12,8},{1,5},{5,1},{9,13},{13,9},{2,6},{6,2},{1... | collective-permute-start | bytes 24584 | tf_op jit(solution)/shard_map/ppermute | solution.py:248
  34.8 4.5 %collective-permute-start.19 = (bf16[8,512]{1,0:T(8,128)(2,1)S(1)}, bf16[8,512]{1,0:T(8,128)(2,1)S(1)}, u32[]{:S(2)}, u32[]{:S(2)}) collective-permute-start(bf16[8,512]{1,0:T(8,128)(2,1)S(1)} %get-tuple-element.224), channel_id=1, source_target_pairs={{0,3},{1,2},{2,1},{3,0},{4,7},{5,6},{6,5},{7,4},{8,11},{9,10},{10,... | collective-permute-start | bytes 24584 | tf_op jit(solution)/shard_map/ppermute | solution.py:250
  40.1 14.1 %collective-permute-start.24 = (bf16[512,512]{1,0:T(8,128)(2,1)S(1)}, bf16[512,512]{1,0:T(8,128)(2,1)S(1)}, u32[]{:S(2)}, u32[]{:S(2)}) collective-permute-start(bf16[512,512]{1,0:T(8,128)(2,1)S(1)} %get-tuple-element.257), channel_id=1, source_target_pairs={{0,1},{1,0},{2,3},{3,2},{4,5},{5,4},{6,7},{7,6},{8,9},{9,8},{10,11... | collective-permute-start | bytes 1572872 | tf_op jit(solution)/shard_map/ppermute | solution.py:162
  40.1 11.9 %collective-permute-start.23 = (bf16[384,512]{1,0:T(8,128)(2,1)S(1)}, bf16[384,512]{1,0:T(8,128)(2,1)S(1)}, u32[]{:S(2)}, u32[]{:S(2)}) collective-permute-start(bf16[384,512]{1,0:T(8,128)(2,1)S(1)} %get-tuple-element.246), channel_id=1, source_target_pairs={{0,2},{1,3},{2,0},{3,1},{4,6},{5,7},{6,4},{7,5},{8,10},{9,11},{10,... | collective-permute-start | bytes 1179656 | tf_op jit(solution)/shard_map/ppermute | solution.py:162
  44.2 7.9 %collective-permute-start.22 = (bf16[288,512]{1,0:T(8,128)(2,1)S(1)}, bf16[288,512]{1,0:T(8,128)(2,1)S(1)}, u32[]{:S(2)}, u32[]{:S(2)}) collective-permute-start(bf16[288,512]{1,0:T(8,128)(2,1)S(1)} %get-tuple-element.245), channel_id=1, source_target_pairs={{0,1},{1,0},{2,3},{3,2},{4,5},{5,4},{6,7},{7,6},{8,9},{9,8},{10,11... | collective-permute-start | bytes 884744 | tf_op jit(solution)/shard_map/ppermute | solution.py:162
  44.6 13.1 %collective-permute-start.25 = (bf16[256,512]{1,0:T(8,128)(2,1)S(1)}, bf16[256,512]{1,0:T(8,128)(2,1)S(1)}, u32[]{:S(2)}, u32[]{:S(2)}) collective-permute-start(bf16[256,512]{1,0:T(8,128)(2,1)S(1)} %get-tuple-element.260), channel_id=1, source_target_pairs={{0,2},{1,3},{2,0},{3,1},{4,6},{5,7},{6,4},{7,5},{8,10},{9,11},{10,... | collective-permute-start | bytes 786440 | tf_op jit(solution)/shard_map/ppermute | solution.py:162
  52.9 6.3 %collective-permute-start.26 = (bf16[192,512]{1,0:T(8,128)(2,1)S(1)}, bf16[192,512]{1,0:T(8,128)(2,1)S(1)}, u32[]{:S(2)}, u32[]{:S(2)}) collective-permute-start(bf16[192,512]{1,0:T(8,128)(2,1)S(1)} %get-tuple-element.265), channel_id=1, source_target_pairs={{0,4},{1,5},{2,6},{3,7},{4,0},{5,1},{6,2},{7,3},{8,12},{9,13},{10,... | collective-permute-start | bytes 589832 | tf_op jit(solution)/shard_map/ppermute | solution.py:162
  54.4 9.3 %collective-permute-start.27 = (bf16[256,512]{1,0:T(8,128)(2,1)S(1)}, bf16[256,512]{1,0:T(8,128)(2,1)S(1)}, u32[]{:S(2)}, u32[]{:S(2)}) collective-permute-start(bf16[256,512]{1,0:T(8,128)(2,1)S(1)} %get-tuple-element.268), channel_id=1, source_target_pairs={{0,2},{1,3},{2,0},{3,1},{4,6},{5,7},{6,4},{7,5},{8,10},{9,11},{10,... | collective-permute-start | bytes 786440 | tf_op jit(solution)/shard_map/ppermute | solution.py:162
  55.9 10.5 %collective-permute-start.30 = (bf16[160,512]{1,0:T(8,128)(2,1)S(1)}, bf16[160,512]{1,0:T(8,128)(2,1)S(1)}, u32[]{:S(2)}, u32[]{:S(2)}) collective-permute-start(bf16[160,512]{1,0:T(8,128)(2,1)S(1)} %get-tuple-element.277), channel_id=1, source_target_pairs={{0,2},{1,3},{2,0},{3,1},{4,6},{5,7},{6,4},{7,5},{8,10},{9,11},{10,... | collective-permute-start | bytes 491528 | tf_op jit(solution)/shard_map/ppermute | solution.py:162
  57.8 7.0 %collective-permute-start.28 = (bf16[128,512]{1,0:T(8,128)(2,1)S(1)}, bf16[128,512]{1,0:T(8,128)(2,1)S(1)}, u32[]{:S(2)}, u32[]{:S(2)}) collective-permute-start(bf16[128,512]{1,0:T(8,128)(2,1)S(1)} %get-tuple-element.273), channel_id=1, source_target_pairs={{0,4},{1,5},{2,6},{3,7},{4,0},{5,1},{6,2},{7,3},{8,12},{9,13},{10,... | collective-permute-start | bytes 393224 | tf_op jit(solution)/shard_map/ppermute | solution.py:162
  59.3 6.1 %collective-permute-start.29 = (bf16[96,512]{1,0:T(8,128)(2,1)S(1)}, bf16[96,512]{1,0:T(8,128)(2,1)S(1)}, u32[]{:S(2)}, u32[]{:S(2)}) collective-permute-start(bf16[96,512]{1,0:T(8,128)(2,1)S(1)} %get-tuple-element.275), channel_id=1, source_target_pairs={{0,8},{1,9},{2,10},{3,11},{4,12},{5,13},{6,14},{7,15},{8,0},{9,1},... | collective-permute-start | bytes 294920 | tf_op jit(solution)/shard_map/ppermute | solution.py:162
  63.9 5.8 %collective-permute-start.31 = (bf16[128,512]{1,0:T(8,128)(2,1)S(1)}, bf16[128,512]{1,0:T(8,128)(2,1)S(1)}, u32[]{:S(2)}, u32[]{:S(2)}) collective-permute-start(bf16[128,512]{1,0:T(8,128)(2,1)S(1)} %get-tuple-element.283), channel_id=1, source_target_pairs={{0,4},{1,5},{2,6},{3,7},{4,0},{5,1},{6,2},{7,3},{8,12},{9,13},{10,... | collective-permute-start | bytes 393224 | tf_op jit(solution)/shard_map/ppermute | solution.py:162
  66.5 6.8 %collective-permute-start.33 = (bf16[96,512]{1,0:T(8,128)(2,1)S(1)}, bf16[96,512]{1,0:T(8,128)(2,1)S(1)}, u32[]{:S(2)}, u32[]{:S(2)}) collective-permute-start(bf16[96,512]{1,0:T(8,128)(2,1)S(1)} %get-tuple-element.287), channel_id=1, source_target_pairs={{0,4},{1,5},{2,6},{3,7},{4,0},{5,1},{6,2},{7,3},{8,12},{9,13},{10,... | collective-permute-start | bytes 294920 | tf_op jit(solution)/shard_map/ppermute | solution.py:162
  67.7 5.6 %collective-permute-start.32 = (bf16[64,512]{1,0:T(8,128)(2,1)S(1)}, bf16[64,512]{1,0:T(8,128)(2,1)S(1)}, u32[]{:S(2)}, u32[]{:S(2)}) collective-permute-start(bf16[64,512]{1,0:T(8,128)(2,1)S(1)} %get-tuple-element.285), channel_id=1, source_target_pairs={{0,8},{1,9},{2,10},{3,11},{4,12},{5,13},{6,14},{7,15},{8,0},{9,1},... | collective-permute-start | bytes 196616 | tf_op jit(solution)/shard_map/ppermute | solution.py:162
  73.9 6.2 %collective-permute-start.34 = (bf16[48,512]{1,0:T(8,128)(2,1)S(1)}, bf16[48,512]{1,0:T(8,128)(2,1)S(1)}, u32[]{:S(2)}, u32[]{:S(2)}) collective-permute-start(bf16[48,512]{1,0:T(8,128)(2,1)S(1)} %get-tuple-element.288), channel_id=1, source_target_pairs={{0,8},{1,9},{2,10},{3,11},{4,12},{5,13},{6,14},{7,15},{8,0},{9,1},... | collective-permute-start | bytes 147464 | tf_op jit(solution)/shard_map/ppermute | solution.py:162
  75.6 5.9 %collective-permute-start.35 = (bf16[64,512]{1,0:T(8,128)(2,1)S(1)}, bf16[64,512]{1,0:T(8,128)(2,1)S(1)}, u32[]{:S(2)}, u32[]{:S(2)}) collective-permute-start(bf16[64,512]{1,0:T(8,128)(2,1)S(1)} %get-tuple-element.300), channel_id=1, source_target_pairs={{0,8},{1,9},{2,10},{3,11},{4,12},{5,13},{6,14},{7,15},{8,0},{9,1},... | collective-permute-start | bytes 196616 | tf_op jit(solution)/shard_map/ppermute | solution.py:162
  (15 other events, 60.9 us)

commit v10 on v8

--- a/solution.py
+++ b/solution.py
@@ -683,7 +683,7 @@
         flops=10 * unit, scratch=[pltpu.VMEM((degree * nodes, width), BF)],
     )
     if split:
-        give0, *arr4 = lax.optimization_barrier((give0, *arr4))
+        give0, give2, *arr4 = lax.optimization_barrier((give0, give2, *arr4))
         keep0, give0 = halve_step(1, keep0, swap(give0, 0, dims), place)
         keep0, *arr4 = lax.optimization_barrier((keep0, *arr4))
     shapes = blocks_shapes(1, width, width, dims)
@@ -715,20 +715,20 @@
     else:
         arr1 = swap(give1, 1, dims)
         arr0 = swap(give0, 1, dims)
+        arr2 = swap(give2, 0, dims)
         arr_e, arr1 = lax.optimization_barrier((swap(give_e, 0, dims), arr1))
+        keep1, give1 = halve_step(2, keep1, arr1, place)
+        arr1 = swap(give1, 2, dims)
+        keep_e, keep1 = lax.optimization_barrier((keep_e, keep1))
         keep_e, give_e, from_sub, _ = carry_step(1, keep_e, arr_e, pay5[1:2], place, capacity)
         arr_e = swap(give_e, 1, dims)
-        give2, keep1, keep_e = lax.optimization_barrier((give2, keep1, keep_e))
-        arr2 = swap(give2, 0, dims)
-        keep1, give1 = halve_step(2, keep1, arr1, place)
-        arr1 = swap(give1, 2, dims)
-        keep0, keep1 = lax.optimization_barrier((keep0, keep1))
+        keep2, keep_e = lax.optimization_barrier((keep2, keep_e))
+        keep2, give2 = halve_step(1, keep2, arr2, place)
+        arr2 = swap(give2, 1, dims)
+        keep0, keep2 = lax.optimization_barrier((keep0, keep2))
         keep0, give0 = halve_step(2, keep0, arr0, place)
         arr0 = swap(give0, 2, dims)
-        keep2, keep0 = lax.optimization_barrier((keep2, keep0))
-        keep2, give2 = halve_step(1, keep2, arr2, place)
-        arr2 = swap(give2, 1, dims)
-        keep1, keep2 = lax.optimization_barrier((keep1, keep2))
+        keep1, keep0 = lax.optimization_barrier((keep1, keep0))
         keep1, give1 = halve_step(3, keep1, arr1, place)
         arr1 = swap(give1, 3, dims)
         keep_e, keep1 = lax.optimization_barrier((keep_e, keep1))
@@ -742,9 +742,10 @@
         keep_e, keep0 = lax.optimization_barrier((keep_e, keep0))
         keep_e, give_e, from_near, _ = carry_step(3, keep_e, arr_e, (), place, capacity)
         arr_e = swap(give_e, 3, dims)
-        keep2, keep_e, arr1 = lax.optimization_barrier((keep2, keep_e, arr1))
+        keep2, keep_e = lax.optimization_barrier((keep2, keep_e))
         keep2, give2 = halve_step(2, keep2, arr2, place)
         arr2 = swap(give2, 2, dims)
+        arr_e, arr1 = lax.optimization_barrier((arr_e, arr1))
         arr5 = (arr_e, from_near, from_diag, from_lat, from_sub)
         gpre_g, keep2 = lax.optimization_barrier((gpre_g, keep2))
     (grid_grad,) = call(

time: 88.5 us -> 84 us (0.949)
  waiting for transfers between devices: 25.3 us -> 22.1 us
  starting transfers between devices: 37.7 us -> 36.2 us
    ppermute x16, waiting for transfers between devices: 23.1 us -> 20 us  [swap(): return lax.ppermute(block, GROUP, [(i, i ^ 1 << bit) for i in range(total)])]
    ppermute x16, starting transfers between devices: 18.9 us -> 17.5 us  [swap(): return lax.ppermute(block, GROUP, [(i, i ^ 1 << bit) for i in range(total)])]
  transfers between devices with their start and end apart: 36 -> 36, of which waited for: 13 -> 12; matrix products, arithmetic and copies ran while one was open for 0% -> 0% of each run, Pallas kernels for 18% -> 20%
where the time goes in v10:
time: 84 us; the launch traced here: 83.7 us
  starting transfers between devices  36.2 us (43%)
  Pallas kernels  22.8 us (27%)
  waiting for transfers between devices  22.1 us (26%)
  local copies, waits for them, and re-layouts  1.56 us (2%)
  between operations  0.92 us (1%)
    pallas_call x24, Pallas kernels, call(): pl.pallas_call(kernel, out_shape=[shape(*a.shape, dtype=a.dtype) for a in...  22.8 us
    ppermute x16, waiting for transfers between devices, swap(): return lax.ppermute(block, GROUP, [(i, i ^ 1 << bit) for i in range(total)])  20 us
    ppermute x16, starting transfers between devices, swap(): return lax.ppermute(block, GROUP, [(i, i ^ 1 << bit) for i in range(total)])  17.5 us
    ppermute x4, starting transfers between devices, exchange(): far = lax.ppermute(parts[column], 'lon', other)  9.87 us
    ppermute x12, starting transfers between devices, exchange(): lax.ppermute(parts[r - 1], COLUMN, [(i, i ^ r) for i in range(column)])  6.88 us
    ppermute x4, starting transfers between devices, exchange(): lax.ppermute(parts[column - 1], 'lon', [(i, i ^ 1) for i in range(count)])  2 us
  transfers between devices with their start and end apart: 36, of which 12 were waited for; matrix products, arithmetic and copies ran while one was open for 0% of the time, Pallas kernels for 20%

profile of v10, /device:TPU:0, one launch (start us, length us, event | category | flops | bytes accessed | tf_op | source)
XLA Modules:
  0.0 83.7 jit_solution(6509528721636758268)
XLA Ops:
  2.3 1.6 %first_payload.1 = (bf16[512,512]{1,0:T(8,128)(2,1)S(1)}, bf16[512,512]{1,0:T(8,128)(2,1)S(1)}, s32[1,512]{1,0:T(1,128)S(1)}, s32[6,256]{1,0:T(8,128)S(1)}, bf16...) custom-call(bf16[512,512]{1,0:T(8,128)(2,1)} %refs_0_.1, ...), custom_call_target="tpu_custom_call" | custom-call | flops 67108864 | bytes 2188688 | tf_op jit(solution)/shard_map/first_payload/pallas_call | solution.py:231
  3.9 5.1 %collective-permute-start = (bf16[16,512]{1,0:T(8,128)(2,1)S(1)}, bf16[16,512]{1,0:T(8,128)(2,1)S(1)}, u32[]{:S(2)}, u32[]{:S(2)}) collective-permute-start(bf16[16,512]{1,0:T(8,128)(2,1)S(1)} %get-tuple-element.166), channel_id=1, source_target_pairs={{0,12},{4,8},{8,4},{12,0},{1,13},{5,9},{9,5},{13,1},{2,14},{6,10},... | collective-permute-start | bytes 49160 | tf_op jit(solution)/shard_map/ppermute | solution.py:247
  16.3 1.5 %collective-permute-start.8 = (bf16[32,512]{1,0:T(8,128)(2,1)S(1)}, bf16[32,512]{1,0:T(8,128)(2,1)S(1)}, u32[]{:S(2)}, u32[]{:S(2)}) collective-permute-start(bf16[32,512]{1,0:T(8,128)(2,1)S(1)} %get-tuple-element.181), channel_id=1, source_target_pairs={{0,2},{1,3},{2,0},{3,1},{4,6},{5,7},{6,4},{7,5},{8,10},{9,11},{10,... | collective-permute-start | bytes 98312 | tf_op jit(solution)/shard_map/ppermute | solution.py:250
  18.1 1.9 %forward_local.1 = (f32[256,512]{1,0:T(8,128)S(1)}, bf16[6,256,512]{2,1,0:T(8,128)(2,1)S(1)}, f32[40,512]{1,0:T(8,128)S(1)}, bf16[40,512]{1,0:T(8,128)(2,1)S(1)}) custom-call(bf16[256,512]{1,0:T(8,128)(2,1)S(1)} %get-tuple-element.183.state_ref.refs_7_.refs_10_, bf16[2,512,512]{2,1,0:T(8,128)(2,1)S(1)} %copy-done, bf16[2,512,512]{2,1,0:T(8,128)(2,1)S(1)} %copy-done.2, ...), custom_call_target="tpu_custom_call" | custom-call | flops 805306368 | bytes 4593824 | tf_op jit(solution)/shard_map/forward_local/pallas_call | solution.py:231
  21.4 2.7 %collective-permute-start.10 = (bf16[16,512]{1,0:T(8,128)(2,1)S(1)}, bf16[16,512]{1,0:T(8,128)(2,1)S(1)}, u32[]{:S(2)}, u32[]{:S(2)}) collective-permute-start(bf16[16,512]{1,0:T(8,128)(2,1)S(1)} %get-tuple-element.188), channel_id=1, source_target_pairs={{0,12},{4,8},{8,4},{12,0},{1,13},{5,9},{9,5},{13,1},{2,14},{6,10},... | collective-permute-start | bytes 49160 | tf_op jit(solution)/shard_map/ppermute | solution.py:247
  26.5 3.0 %turn_local.1 = (f32[256,512]{1,0:T(8,128)S(1)}, f32[256,512]{1,0:T(8,128)S(1)}, f32[256,512]{1,0:T(8,128)S(1)}, f32[40,512]{1,0:T(8,128)S(1)}, bf16[40,512]{1,0...) custom-call(bf16[256,512]{1,0:T(8,128)(2,1)S(1)} %get-tuple-element., ...), custom_call_target="tpu_custom_call" | custom-call | flops 1342177280 | bytes 5871776 | tf_op jit(solution)/shard_map/turn_local/pallas_call | solution.py:231
  29.6 1.4 %turn_halo.1 = (bf16[256,512]{1,0:T(8,128)(2,1)S(1)}, bf16[256,512]{1,0:T(8,128)(2,1)S(1)}, bf16[256,512]{1,0:T(8,128)(2,1)S(1)}, bf16[256,512]{1,0:T(8,128)(2,1...) custom-call(bf16[16,512]{1,0:T(8,128)(2,1)S(1)} %collective-permute-, ...), custom_call_target="tpu_custom_call" | custom-call | flops 402653184 | bytes 5322912 | tf_op jit(solution)/shard_map/turn_halo/pallas_call | solution.py:231
  31.0 1.5 %last_weights.1 = (bf16[768,512]{1,0:T(8,128)(2,1)S(1)}, bf16[768,512]{1,0:T(8,128)(2,1)S(1)}, bf16[256,512]{1,0:T(8,128)(2,1)}) custom-call(s32[6,6]{1,0:T(8,128)S(1)} %get-tuple-element.165.refs_0_.refs_5_, bf16[256,512]{1,0:T(8,128)(2,1)S(1)} %get-tuple-element.187.state_ref.refs_1_, bf16[256,512]{1,0:T(8,128)(2,1)S(1)} %get-tuple-element.205.refs_2_, ...), custom_call_target="tpu_custom_call" | custom-call | flops 536870912 | bytes 4194448 | tf_op jit(solution)/shard_map/last_weights/pallas_call | solution.py:231
  36.4 2.9 %back_local.1 = (f32[256,512]{1,0:T(8,128)S(1)}, bf16[512,512]{1,0:T(8,128)(2,1)S(1)}, bf16[512,512]{1,0:T(8,128)(2,1)S(1)}, bf16[512,512]{1,0:T(8,128)(2,1)S(1)}, bf16[512,512]{1,0:T(8,128)(2,1)S(1)}) custom-call(s32[6,6]{1,0:T(8,128)S(1)} %get-tuple-element.165.refs_0_.refs_5_, bf16[256,512]{1,0:T(8,128)(2,1)S(1)} %get-tuple-element.209.refs_1_, ...), custom_call_target="tpu_custom_call" | custom-call | flops 1342177280 | bytes 8960144 | tf_op jit(solution)/shard_map/back_local/pallas_call | solution.py:231
  40.1 1.2 %collective-permute-start.23 = (bf16[384,512]{1,0:T(8,128)(2,1)S(1)}, bf16[384,512]{1,0:T(8,128)(2,1)S(1)}, u32[]{:S(2)}, u32[]{:S(2)}) collective-permute-start(bf16[384,512]{1,0:T(8,128)(2,1)S(1)} %get-tuple-element.252), channel_id=1, source_target_pairs={{0,2},{1,3},{2,0},{3,1},{4,6},{5,7},{6,4},{7,5},{8,10},{9,11},{10,... | collective-permute-start | bytes 1179656 | tf_op jit(solution)/shard_map/ppermute | solution.py:162
  41.9 2.3 %embed_back.1 = (bf16[512,512]{1,0:T(8,128)(2,1)S(1)}, bf16[256,512]{1,0:T(8,128)(2,1)S(1)}, bf16[288,512]{1,0:T(8,128)(2,1)S(1)}, bf16[16,512]{1,0:T(8,128)(2,1...) custom-call(bf16[8,512]{1,0:T(8,128)(2,1)S(1)} %collective-permute-d, ...), custom_call_target="tpu_custom_call" | custom-call | flops 805306368 | bytes 6130608 | tf_op jit(solution)/shard_map/embed_back/pallas_call | solution.py:231
  44.6 1.2 %collective-permute-start.25 = (bf16[256,512]{1,0:T(8,128)(2,1)S(1)}, bf16[256,512]{1,0:T(8,128)(2,1)S(1)}, u32[]{:S(2)}, u32[]{:S(2)}) collective-permute-start(bf16[256,512]{1,0:T(8,128)(2,1)S(1)} %get-tuple-element.265), channel_id=1, source_target_pairs={{0,2},{1,3},{2,0},{3,1},{4,6},{5,7},{6,4},{7,5},{8,10},{9,11},{10,... | collective-permute-start | bytes 786440 | tf_op jit(solution)/shard_map/ppermute | solution.py:162
  45.8 6.3 %collective-permute-done.23.refs_2_ = bf16[384,512]{1,0:T(8,128)(2,1)S(1)} collective-permute-done((bf16[384,512]{1,0:T(8,128)(2,1)S(1)}, bf16[384,512]{1,0:T(8,128)(2,1)S(1)}, u32[]{:S(2)}, u32[]{:S(2)}) %collective-permute-start.23) | collective-permute-done | bytes 393248 | tf_op jit(solution)/shard_map/ppermute | solution.py:162
  52.3 1.3 %collective-permute-start.26 = (bf16[192,512]{1,0:T(8,128)(2,1)S(1)}, bf16[192,512]{1,0:T(8,128)(2,1)S(1)}, u32[]{:S(2)}, u32[]{:S(2)}) collective-permute-start(bf16[192,512]{1,0:T(8,128)(2,1)S(1)} %get-tuple-element.270), channel_id=1, source_target_pairs={{0,4},{1,5},{2,6},{3,7},{4,0},{5,1},{6,2},{7,3},{8,12},{9,13},{10,... | collective-permute-start | bytes 589832 | tf_op jit(solution)/shard_map/ppermute | solution.py:162
  54.2 1.4 %collective-permute-start.27 = (bf16[160,512]{1,0:T(8,128)(2,1)S(1)}, bf16[160,512]{1,0:T(8,128)(2,1)S(1)}, u32[]{:S(2)}, u32[]{:S(2)}) collective-permute-start(bf16[160,512]{1,0:T(8,128)(2,1)S(1)} %get-tuple-element.273), channel_id=1, source_target_pairs={{0,2},{1,3},{2,0},{3,1},{4,6},{5,7},{6,4},{7,5},{8,10},{9,11},{10,... | collective-permute-start | bytes 491528 | tf_op jit(solution)/shard_map/ppermute | solution.py:162
  57.8 1.3 %collective-permute-start.28 = (bf16[128,512]{1,0:T(8,128)(2,1)S(1)}, bf16[128,512]{1,0:T(8,128)(2,1)S(1)}, u32[]{:S(2)}, u32[]{:S(2)}) collective-permute-start(bf16[128,512]{1,0:T(8,128)(2,1)S(1)} %get-tuple-element.279), channel_id=1, source_target_pairs={{0,4},{1,5},{2,6},{3,7},{4,0},{5,1},{6,2},{7,3},{8,12},{9,13},{10,... | collective-permute-start | bytes 393224 | tf_op jit(solution)/shard_map/ppermute | solution.py:162
  59.3 2.0 %collective-permute-done.27.refs_2_ = bf16[160,512]{1,0:T(8,128)(2,1)S(1)} collective-permute-done((bf16[160,512]{1,0:T(8,128)(2,1)S(1)}, bf16[160,512]{1,0:T(8,128)(2,1)S(1)}, u32[]{:S(2)}, u32[]{:S(2)}) %collective-permute-start.27) | collective-permute-done | bytes 163872 | tf_op jit(solution)/shard_map/ppermute | solution.py:162
  62.7 2.2 %collective-permute-start.32 = (bf16[96,512]{1,0:T(8,128)(2,1)S(1)}, bf16[96,512]{1,0:T(8,128)(2,1)S(1)}, u32[]{:S(2)}, u32[]{:S(2)}) collective-permute-start(bf16[96,512]{1,0:T(8,128)(2,1)S(1)} %get-tuple-element.289), channel_id=1, source_target_pairs={{0,8},{1,9},{2,10},{3,11},{4,12},{5,13},{6,14},{7,15},{8,0},{9,1},... | collective-permute-start | bytes 294920 | tf_op jit(solution)/shard_map/ppermute | solution.py:162
  65.0 2.0 %collective-permute-done.29.refs_2_ = bf16[96,512]{1,0:T(8,128)(2,1)S(1)} collective-permute-done((bf16[96,512]{1,0:T(8,128)(2,1)S(1)}, bf16[96,512]{1,0:T(8,128)(2,1)S(1)}, u32[]{:S(2)}, u32[]{:S(2)}) %collective-permute-start.29) | collective-permute-done | bytes 98336 | tf_op jit(solution)/shard_map/ppermute | solution.py:162
  68.8 3.1 %collective-permute-start.31 = (bf16[48,512]{1,0:T(8,128)(2,1)S(1)}, bf16[48,512]{1,0:T(8,128)(2,1)S(1)}, u32[]{:S(2)}, u32[]{:S(2)}) collective-permute-start(bf16[48,512]{1,0:T(8,128)(2,1)S(1)} %get-tuple-element.288), channel_id=1, source_target_pairs={{0,8},{1,9},{2,10},{3,11},{4,12},{5,13},{6,14},{7,15},{8,0},{9,1},... | collective-permute-start | bytes 147464 | tf_op jit(solution)/shard_map/ppermute | solution.py:162
  71.9 2.7 %collective-permute-done.31.refs_0_.arr_e_ref = bf16[48,512]{1,0:T(8,128)(2,1)S(1)} collective-permute-done((bf16[48,512]{1,0:T(8,128)(2,1)S(1)}, bf16[48,512]{1,0:T(8,128)(2,1)S(1)}, u32[]{:S(2)}, u32[]{:S(2)}) %collective-permute-start.31) | collective-permute-done | bytes 49184 | tf_op jit(solution)/shard_map/ppermute | solution.py:162
  74.6 1.3 %grid_place.1 = bf16[512,512]{1,0:T(8,128)(2,1)} custom-call(bf16[48,512]{1,0:T(8,128)(2,1)S(1)} %collective-permute-done.31.refs_0_.arr_e_ref, bf16[16,512]{1,0:T(8,128)(2,1)S(1)} %get-tuple-element.291.refs_1_, bf16[16,512]{1,0:T(8,128)(2,1)S(1)} %get-tuple-element.292.refs_2_, bf16[16,512]{1,0:T(8,128)(2,1)S(1)} %get-tuple-element.293.refs_3_, ...), custom_call_target="tpu_custom_call" | custom-call | flops 402653184 | bytes 1687872 | tf_op jit(solution)/shard_map/grid_place/pallas_call | solution.py:231
  75.9 1.3 %collective-permute-done.33.arr0_ref = bf16[64,512]{1,0:T(8,128)(2,1)S(1)} collective-permute-done((bf16[64,512]{1,0:T(8,128)(2,1)S(1)}, bf16[64,512]{1,0:T(8,128)(2,1)S(1)}, u32[]{:S(2)}, u32[]{:S(2)}) %collective-permute-start.33) | collective-permute-done | bytes 65568 | tf_op jit(solution)/shard_map/ppermute | solution.py:162
  78.5 4.4 %collective-permute-done.35.arr2_ref = bf16[64,512]{1,0:T(8,128)(2,1)S(1)} collective-permute-done((bf16[64,512]{1,0:T(8,128)(2,1)S(1)}, bf16[64,512]{1,0:T(8,128)(2,1)S(1)}, u32[]{:S(2)}, u32[]{:S(2)}) %collective-permute-start.35) | collective-permute-done | bytes 65568 | tf_op jit(solution)/shard_map/ppermute | solution.py:162
  (83 shorter events, 27.2 us)
Async XLA Ops:
  3.9 8.0 %collective-permute-start = (bf16[16,512]{1,0:T(8,128)(2,1)S(1)}, bf16[16,512]{1,0:T(8,128)(2,1)S(1)}, u32[]{:S(2)}, u32[]{:S(2)}) collective-permute-start(bf16[16,512]{1,0:T(8,128)(2,1)S(1)} %get-tuple-element.166), channel_id=1, source_target_pairs={{0,12},{4,8},{8,4},{12,0},{1,13},{5,9},{9,5},{13,1},{2,14},{6,10},... | collective-permute-start | bytes 49160 | tf_op jit(solution)/shard_map/ppermute | solution.py:247
  14.5 5.8 %collective-permute-start.5 = (bf16[32,512]{1,0:T(8,128)(2,1)S(1)}, bf16[32,512]{1,0:T(8,128)(2,1)S(1)}, u32[]{:S(2)}, u32[]{:S(2)}) collective-permute-start(bf16[32,512]{1,0:T(8,128)(2,1)S(1)} %get-tuple-element.178), channel_id=1, source_target_pairs={{0,12},{4,8},{8,4},{12,0},{1,13},{5,9},{9,5},{13,1},{2,14},{6,10},... | collective-permute-start | bytes 98312 | tf_op jit(solution)/shard_map/ppermute | solution.py:247
  15.6 4.7 %collective-permute-start.6 = (bf16[32,512]{1,0:T(8,128)(2,1)S(1)}, bf16[32,512]{1,0:T(8,128)(2,1)S(1)}, u32[]{:S(2)}, u32[]{:S(2)}) collective-permute-start(bf16[32,512]{1,0:T(8,128)(2,1)S(1)} %get-tuple-element.179), channel_id=1, source_target_pairs={{0,4},{4,0},{8,12},{12,8},{1,5},{5,1},{9,13},{13,9},{2,6},{6,2},{1... | collective-permute-start | bytes 98312 | tf_op jit(solution)/shard_map/ppermute | solution.py:248
  21.4 8.1 %collective-permute-start.10 = (bf16[16,512]{1,0:T(8,128)(2,1)S(1)}, bf16[16,512]{1,0:T(8,128)(2,1)S(1)}, u32[]{:S(2)}, u32[]{:S(2)}) collective-permute-start(bf16[16,512]{1,0:T(8,128)(2,1)S(1)} %get-tuple-element.188), channel_id=1, source_target_pairs={{0,12},{4,8},{8,4},{12,0},{1,13},{5,9},{9,5},{13,1},{2,14},{6,10},... | collective-permute-start | bytes 49160 | tf_op jit(solution)/shard_map/ppermute | solution.py:247
  24.1 5.4 %collective-permute-start.11 = (bf16[16,512]{1,0:T(8,128)(2,1)S(1)}, bf16[16,512]{1,0:T(8,128)(2,1)S(1)}, u32[]{:S(2)}, u32[]{:S(2)}) collective-permute-start(bf16[16,512]{1,0:T(8,128)(2,1)S(1)} %get-tuple-element.189), channel_id=1, source_target_pairs={{0,4},{4,0},{8,12},{12,8},{1,5},{5,1},{9,13},{13,9},{2,6},{6,2},{1... | collective-permute-start | bytes 49160 | tf_op jit(solution)/shard_map/ppermute | solution.py:248
  24.7 4.9 %collective-permute-start.12 = (bf16[16,512]{1,0:T(8,128)(2,1)S(1)}, bf16[16,512]{1,0:T(8,128)(2,1)S(1)}, u32[]{:S(2)}, u32[]{:S(2)}) collective-permute-start(bf16[16,512]{1,0:T(8,128)(2,1)S(1)} %get-tuple-element.190), channel_id=1, source_target_pairs={{0,3},{1,2},{2,1},{3,0},{4,7},{5,6},{6,5},{7,4},{8,11},{9,10},{10,... | collective-permute-start | bytes 49160 | tf_op jit(solution)/shard_map/ppermute | solution.py:250
  25.1 4.4 %collective-permute-start.13 = (bf16[16,512]{1,0:T(8,128)(2,1)S(1)}, bf16[16,512]{1,0:T(8,128)(2,1)S(1)}, u32[]{:S(2)}, u32[]{:S(2)}) collective-permute-start(bf16[16,512]{1,0:T(8,128)(2,1)S(1)} %get-tuple-element.191), channel_id=1, source_target_pairs={{0,2},{1,3},{2,0},{3,1},{4,6},{5,7},{6,4},{7,5},{8,10},{9,11},{10,... | collective-permute-start | bytes 49160 | tf_op jit(solution)/shard_map/ppermute | solution.py:250
  33.0 6.3 %collective-permute-start.17 = (bf16[8,512]{1,0:T(8,128)(2,1)S(1)}, bf16[8,512]{1,0:T(8,128)(2,1)S(1)}, u32[]{:S(2)}, u32[]{:S(2)}) collective-permute-start(bf16[8,512]{1,0:T(8,128)(2,1)S(1)} %get-tuple-element.225), channel_id=1, source_target_pairs={{0,12},{4,8},{8,4},{12,0},{1,13},{5,9},{9,5},{13,1},{2,14},{6,10},... | collective-permute-start | bytes 24584 | tf_op jit(solution)/shard_map/ppermute | solution.py:247
  34.0 5.4 %collective-permute-start.18 = (bf16[8,512]{1,0:T(8,128)(2,1)S(1)}, bf16[8,512]{1,0:T(8,128)(2,1)S(1)}, u32[]{:S(2)}, u32[]{:S(2)}) collective-permute-start(bf16[8,512]{1,0:T(8,128)(2,1)S(1)} %get-tuple-element.226), channel_id=1, source_target_pairs={{0,4},{4,0},{8,12},{12,8},{1,5},{5,1},{9,13},{13,9},{2,6},{6,2},{1... | collective-permute-start | bytes 24584 | tf_op jit(solution)/shard_map/ppermute | solution.py:248
  34.8 4.5 %collective-permute-start.19 = (bf16[8,512]{1,0:T(8,128)(2,1)S(1)}, bf16[8,512]{1,0:T(8,128)(2,1)S(1)}, u32[]{:S(2)}, u32[]{:S(2)}) collective-permute-start(bf16[8,512]{1,0:T(8,128)(2,1)S(1)} %get-tuple-element.227), channel_id=1, source_target_pairs={{0,3},{1,2},{2,1},{3,0},{4,7},{5,6},{6,5},{7,4},{8,11},{9,10},{10,... | collective-permute-start | bytes 24584 | tf_op jit(solution)/shard_map/ppermute | solution.py:250
  40.1 15.5 %collective-permute-start.24 = (bf16[512,512]{1,0:T(8,128)(2,1)S(1)}, bf16[512,512]{1,0:T(8,128)(2,1)S(1)}, u32[]{:S(2)}, u32[]{:S(2)}) collective-permute-start(bf16[512,512]{1,0:T(8,128)(2,1)S(1)} %get-tuple-element.260), channel_id=1, source_target_pairs={{0,1},{1,0},{2,3},{3,2},{4,5},{5,4},{6,7},{7,6},{8,9},{9,8},{10,11... | collective-permute-start | bytes 1572872 | tf_op jit(solution)/shard_map/ppermute | solution.py:162
  40.1 11.9 %collective-permute-start.23 = (bf16[384,512]{1,0:T(8,128)(2,1)S(1)}, bf16[384,512]{1,0:T(8,128)(2,1)S(1)}, u32[]{:S(2)}, u32[]{:S(2)}) collective-permute-start(bf16[384,512]{1,0:T(8,128)(2,1)S(1)} %get-tuple-element.252), channel_id=1, source_target_pairs={{0,2},{1,3},{2,0},{3,1},{4,6},{5,7},{6,4},{7,5},{8,10},{9,11},{10,... | collective-permute-start | bytes 1179656 | tf_op jit(solution)/shard_map/ppermute | solution.py:162
  44.2 7.9 %collective-permute-start.22 = (bf16[288,512]{1,0:T(8,128)(2,1)S(1)}, bf16[288,512]{1,0:T(8,128)(2,1)S(1)}, u32[]{:S(2)}, u32[]{:S(2)}) collective-permute-start(bf16[288,512]{1,0:T(8,128)(2,1)S(1)} %get-tuple-element.251), channel_id=1, source_target_pairs={{0,1},{1,0},{2,3},{3,2},{4,5},{5,4},{6,7},{7,6},{8,9},{9,8},{10,11... | collective-permute-start | bytes 884744 | tf_op jit(solution)/shard_map/ppermute | solution.py:162
  44.6 13.1 %collective-permute-start.25 = (bf16[256,512]{1,0:T(8,128)(2,1)S(1)}, bf16[256,512]{1,0:T(8,128)(2,1)S(1)}, u32[]{:S(2)}, u32[]{:S(2)}) collective-permute-start(bf16[256,512]{1,0:T(8,128)(2,1)S(1)} %get-tuple-element.265), channel_id=1, source_target_pairs={{0,2},{1,3},{2,0},{3,1},{4,6},{5,7},{6,4},{7,5},{8,10},{9,11},{10,... | collective-permute-start | bytes 786440 | tf_op jit(solution)/shard_map/ppermute | solution.py:162
  52.3 6.9 %collective-permute-start.26 = (bf16[192,512]{1,0:T(8,128)(2,1)S(1)}, bf16[192,512]{1,0:T(8,128)(2,1)S(1)}, u32[]{:S(2)}, u32[]{:S(2)}) collective-permute-start(bf16[192,512]{1,0:T(8,128)(2,1)S(1)} %get-tuple-element.270), channel_id=1, source_target_pairs={{0,4},{1,5},{2,6},{3,7},{4,0},{5,1},{6,2},{7,3},{8,12},{9,13},{10,... | collective-permute-start | bytes 589832 | tf_op jit(solution)/shard_map/ppermute | solution.py:162
  54.2 7.1 %collective-permute-start.27 = (bf16[160,512]{1,0:T(8,128)(2,1)S(1)}, bf16[160,512]{1,0:T(8,128)(2,1)S(1)}, u32[]{:S(2)}, u32[]{:S(2)}) collective-permute-start(bf16[160,512]{1,0:T(8,128)(2,1)S(1)} %get-tuple-element.273), channel_id=1, source_target_pairs={{0,2},{1,3},{2,0},{3,1},{4,6},{5,7},{6,4},{7,5},{8,10},{9,11},{10,... | collective-permute-start | bytes 491528 | tf_op jit(solution)/shard_map/ppermute | solution.py:162
  55.8 11.8 %collective-permute-start.30 = (bf16[256,512]{1,0:T(8,128)(2,1)S(1)}, bf16[256,512]{1,0:T(8,128)(2,1)S(1)}, u32[]{:S(2)}, u32[]{:S(2)}) collective-permute-start(bf16[256,512]{1,0:T(8,128)(2,1)S(1)} %get-tuple-element.285), channel_id=1, source_target_pairs={{0,2},{1,3},{2,0},{3,1},{4,6},{5,7},{6,4},{7,5},{8,10},{9,11},{10,... | collective-permute-start | bytes 786440 | tf_op jit(solution)/shard_map/ppermute | solution.py:162
  57.8 7.0 %collective-permute-start.28 = (bf16[128,512]{1,0:T(8,128)(2,1)S(1)}, bf16[128,512]{1,0:T(8,128)(2,1)S(1)}, u32[]{:S(2)}, u32[]{:S(2)}) collective-permute-start(bf16[128,512]{1,0:T(8,128)(2,1)S(1)} %get-tuple-element.279), channel_id=1, source_target_pairs={{0,4},{1,5},{2,6},{3,7},{4,0},{5,1},{6,2},{7,3},{8,12},{9,13},{10,... | collective-permute-start | bytes 393224 | tf_op jit(solution)/shard_map/ppermute | solution.py:162
  61.5 5.5 %collective-permute-start.29 = (bf16[96,512]{1,0:T(8,128)(2,1)S(1)}, bf16[96,512]{1,0:T(8,128)(2,1)S(1)}, u32[]{:S(2)}, u32[]{:S(2)}) collective-permute-start(bf16[96,512]{1,0:T(8,128)(2,1)S(1)} %get-tuple-element.282), channel_id=1, source_target_pairs={{0,4},{1,5},{2,6},{3,7},{4,0},{5,1},{6,2},{7,3},{8,12},{9,13},{10,... | collective-permute-start | bytes 294920 | tf_op jit(solution)/shard_map/ppermute | solution.py:162
  62.7 9.2 %collective-permute-start.32 = (bf16[96,512]{1,0:T(8,128)(2,1)S(1)}, bf16[96,512]{1,0:T(8,128)(2,1)S(1)}, u32[]{:S(2)}, u32[]{:S(2)}) collective-permute-start(bf16[96,512]{1,0:T(8,128)(2,1)S(1)} %get-tuple-element.289), channel_id=1, source_target_pairs={{0,8},{1,9},{2,10},{3,11},{4,12},{5,13},{6,14},{7,15},{8,0},{9,1},... | collective-permute-start | bytes 294920 | tf_op jit(solution)/shard_map/ppermute | solution.py:162
  67.8 9.5 %collective-permute-start.34 = (bf16[128,512]{1,0:T(8,128)(2,1)S(1)}, bf16[128,512]{1,0:T(8,128)(2,1)S(1)}, u32[]{:S(2)}, u32[]{:S(2)}) collective-permute-start(bf16[128,512]{1,0:T(8,128)(2,1)S(1)} %get-tuple-element.304), channel_id=1, source_target_pairs={{0,4},{1,5},{2,6},{3,7},{4,0},{5,1},{6,2},{7,3},{8,12},{9,13},{10,... | collective-permute-start | bytes 393224 | tf_op jit(solution)/shard_map/ppermute | solution.py:162
  68.8 5.8 %collective-permute-start.31 = (bf16[48,512]{1,0:T(8,128)(2,1)S(1)}, bf16[48,512]{1,0:T(8,128)(2,1)S(1)}, u32[]{:S(2)}, u32[]{:S(2)}) collective-permute-start(bf16[48,512]{1,0:T(8,128)(2,1)S(1)} %get-tuple-element.288), channel_id=1, source_target_pairs={{0,8},{1,9},{2,10},{3,11},{4,12},{5,13},{6,14},{7,15},{8,0},{9,1},... | collective-permute-start | bytes 147464 | tf_op jit(solution)/shard_map/ppermute | solution.py:162
  71.9 5.4 %collective-permute-start.33 = (bf16[64,512]{1,0:T(8,128)(2,1)S(1)}, bf16[64,512]{1,0:T(8,128)(2,1)S(1)}, u32[]{:S(2)}, u32[]{:S(2)}) collective-permute-start(bf16[64,512]{1,0:T(8,128)(2,1)S(1)} %get-tuple-element.297), channel_id=1, source_target_pairs={{0,8},{1,9},{2,10},{3,11},{4,12},{5,13},{6,14},{7,15},{8,0},{9,1},... | collective-permute-start | bytes 196616 | tf_op jit(solution)/shard_map/ppermute | solution.py:162
  77.4 5.5 %collective-permute-start.35 = (bf16[64,512]{1,0:T(8,128)(2,1)S(1)}, bf16[64,512]{1,0:T(8,128)(2,1)S(1)}, u32[]{:S(2)}, u32[]{:S(2)}) collective-permute-start(bf16[64,512]{1,0:T(8,128)(2,1)S(1)} %get-tuple-element.306), channel_id=1, source_target_pairs={{0,8},{1,9},{2,10},{3,11},{4,12},{5,13},{6,14},{7,15},{8,0},{9,1},... | collective-permute-start | bytes 196616 | tf_op jit(solution)/shard_map/ppermute | solution.py:162
  (15 other events, 60.9 us)

commit v11 on v10

--- a/solution.py
+++ b/solution.py
@@ -117,14 +117,14 @@
     return (rows // (dims[0] * dims[1] * dims[2])) % 16 == 0
 
 
-def reverse_bits(block, bits):
+def block_spot(block, order):
     spot = 0
-    for bit in range(bits):
+    for bit in order:
         spot = 2 * spot + (block >> bit) % 2
     return spot
 
 
-def store_blocks(keep_ref, give_ref, at, count, value, dims, bits_ref):
+def store_blocks(keep_ref, give_ref, at, count, value, dims, bits_ref, order=None):
     value = low(value)
     rows = value.shape[0]
     total = dims[0] * dims[1] * dims[2]
@@ -132,10 +132,11 @@
     if not fine(rows, dims):
         keep_ref[at] = value
         return
-    bits = (total - 1).bit_length()
+    if order is None:
+        order = range((total - 1).bit_length())
     upper = bits_ref[0:1, 2:3] == 1
     for block in range(0, total, 2):
-        start = reverse_bits(block, bits) * count * depth + at * depth
+        start = block_spot(block, order) * count * depth + at * depth
         first = value[block * depth : (block + 1) * depth].astype(F32)
         second = value[(block + 1) * depth : (block + 2) * depth].astype(F32)
         keep_ref[start : start + depth, :] = low(jnp.where(upper, second, first))
@@ -473,13 +474,13 @@
 
 
 def last_weights(
-    dims, place_ref, state_ref, summed_ref, cot_ref, grecv_ref, gsent_ref, update_ref,
+    dims, order, place_ref, state_ref, summed_ref, cot_ref, grecv_ref, gsent_ref, update_ref,
     keep_ref, give_ref, mesh_ref,
 ):
     state, summed = state_ref[...], summed_ref[...]
 
     def store(at, value):
-        store_blocks(keep_ref, give_ref, at, 3, value, dims, place_ref)
+        store_blocks(keep_ref, give_ref, at, 3, value, dims, place_ref, order)
 
     store(0, dot(state, gsent_ref[...], TN))
     store(1, dot(state, grecv_ref[...], TN))
@@ -603,6 +604,7 @@
     total = dims[0] * dims[1] * dims[2]
     bits = (total - 1).bit_length()
     carry = dims == (4, 2, 2) and fine(width, dims)
+    order1 = (0, 2, 3, 1) if carry else None
     spot = lax.axis_index(GROUP)
     place = [lax.axis_index(COLUMN), lax.axis_index("lon") % 2]
     place += [(spot >> bit) % 2 for bit in range(bits)]
@@ -666,7 +668,7 @@
     )
     arr4 = exchange(pay4, dims)
     keep1, give1, mesh_out = call(
-        lambda *refs: last_weights(dims, *refs), "last_weights",
+        lambda *refs: last_weights(dims, order1, *refs), "last_weights",
         blocks_shapes(3, width, width, dims) + [shape(nodes, width)],
         (place, state1, summed1, cot, grecv1, gsent1, update_weight), flops=4 * unit,
     )
@@ -674,7 +676,7 @@
     if split:
         give1, last = lax.optimization_barrier((give1, arr4[-1]))
         arr4 = (*arr4[:-1], last)
-        keep1, give1 = halve_step(1, keep1, swap(give1, 0, dims), place)
+        keep1, give1 = halve_step(order1[1] if carry else 1, keep1, swap(give1, 0, dims), place)
     part0, keep0, give0, keep2, give2 = call(
         lambda *refs: back_local(dims, *refs), "back_local",
         [shape(nodes, width, dtype=F32)] + blocks_shapes(2, width, width, dims) * 2,
@@ -713,12 +715,12 @@
             rest_of_halving(0, keep_e, give_e, place, dims),
         ]
     else:
-        arr1 = swap(give1, 1, dims)
+        arr1 = swap(give1, 2, dims)
         arr0 = swap(give0, 1, dims)
         arr2 = swap(give2, 0, dims)
         arr_e, arr1 = lax.optimization_barrier((swap(give_e, 0, dims), arr1))
-        keep1, give1 = halve_step(2, keep1, arr1, place)
-        arr1 = swap(give1, 2, dims)
+        keep1, give1 = halve_step(3, keep1, arr1, place)
+        arr1 = swap(give1, 3, dims)
         keep_e, keep1 = lax.optimization_barrier((keep_e, keep1))
         keep_e, give_e, from_sub, _ = carry_step(1, keep_e, arr_e, pay5[1:2], place, capacity)
         arr_e = swap(give_e, 1, dims)
@@ -728,10 +730,7 @@
         keep0, keep2 = lax.optimization_barrier((keep0, keep2))
         keep0, give0 = halve_step(2, keep0, arr0, place)
         arr0 = swap(give0, 2, dims)
-        keep1, keep0 = lax.optimization_barrier((keep1, keep0))
-        keep1, give1 = halve_step(3, keep1, arr1, place)
-        arr1 = swap(give1, 3, dims)
-        keep_e, keep1 = lax.optimization_barrier((keep_e, keep1))
+        keep_e, keep0 = lax.optimization_barrier((keep_e, keep0))
         keep_e, give_e, from_lat, from_diag = carry_step(
             2, keep_e, arr_e, pay5[3:], place, capacity
         )
@@ -742,18 +741,20 @@
         keep_e, keep0 = lax.optimization_barrier((keep_e, keep0))
         keep_e, give_e, from_near, _ = carry_step(3, keep_e, arr_e, (), place, capacity)
         arr_e = swap(give_e, 3, dims)
-        keep2, keep_e = lax.optimization_barrier((keep2, keep_e))
+        keep1, keep_e, arr0 = lax.optimization_barrier((keep1, keep_e, arr0))
+        keep1, give1 = halve_step(1, keep1, arr1, place)
+        arr1 = swap(give1, 1, dims)
+        keep2, keep1 = lax.optimization_barrier((keep2, keep1))
         keep2, give2 = halve_step(2, keep2, arr2, place)
         arr2 = swap(give2, 2, dims)
-        arr_e, arr1 = lax.optimization_barrier((arr_e, arr1))
+        gpre_g, keep2 = lax.optimization_barrier((gpre_g, keep2))
         arr5 = (arr_e, from_near, from_diag, from_lat, from_sub)
-        gpre_g, keep2 = lax.optimization_barrier((gpre_g, keep2))
     (grid_grad,) = call(
         lambda *refs: grid_place(peers, *refs), "grid_place", [shape(chosen, width)],
         (*arr5, gpre_g, embed, sends_row), flops=3 * unit,
     )
     if carry:
-        keep2, grid_grad, arr0 = lax.optimization_barrier((keep2, grid_grad, arr0))
+        keep2, grid_grad, arr1 = lax.optimization_barrier((keep2, grid_grad, arr1))
         keep2, give2 = halve_step(3, keep2, arr2, place)
         sums = ((keep1, arr1), (keep0, arr0), (keep2, swap(give2, 3, dims)), (keep_e, arr_e))
     if split:

time: 84 us -> 84.7 us (level)
  starting transfers between devices: 36.2 us -> 37.1 us
    ppermute x16, starting transfers between devices: 17.5 us -> 18.4 us  [swap(): return lax.ppermute(block, GROUP, [(i, i ^ 1 << bit) for i in range(total)])]
where the time goes in v11:
time: 84.7 us; the launch traced here: 84.5 us
  starting transfers between devices  37.1 us (44%)
  Pallas kernels  22.8 us (27%)
  waiting for transfers between devices  22 us (26%)
  local copies, waits for them, and re-layouts  1.56 us (2%)
  between operations  0.94 us (1%)
    pallas_call x24, Pallas kernels, call(): pl.pallas_call(kernel, out_shape=[shape(*a.shape, dtype=a.dtype) for a in...  22.8 us
    ppermute x16, waiting for transfers between devices, swap(): return lax.ppermute(block, GROUP, [(i, i ^ 1 << bit) for i in range(total)])  19.9 us
    ppermute x16, starting transfers between devices, swap(): return lax.ppermute(block, GROUP, [(i, i ^ 1 << bit) for i in range(total)])  18.4 us
    ppermute x4, starting transfers between devices, exchange(): far = lax.ppermute(parts[column], 'lon', other)  9.87 us
    ppermute x12, starting transfers between devices, exchange(): lax.ppermute(parts[r - 1], COLUMN, [(i, i ^ r) for i in range(column)])  6.88 us
    ppermute x4, starting transfers between devices, exchange(): lax.ppermute(parts[column - 1], 'lon', [(i, i ^ 1) for i in range(count)])  2 us
  transfers between devices with their start and end apart: 36, of which 12 were waited for; matrix products, arithmetic and copies ran while one was open for 0% of the time, Pallas kernels for 20%

profile of v11, /device:TPU:0, one launch (start us, length us, event | category | flops | bytes accessed | tf_op | source)
XLA Modules:
  0.0 84.5 jit_solution(18382763338485677985)
XLA Ops:
  2.3 1.6 %first_payload.1 = (bf16[512,512]{1,0:T(8,128)(2,1)S(1)}, bf16[512,512]{1,0:T(8,128)(2,1)S(1)}, s32[1,512]{1,0:T(1,128)S(1)}, s32[6,256]{1,0:T(8,128)S(1)}, bf16...) custom-call(bf16[512,512]{1,0:T(8,128)(2,1)} %refs_0_.1, ...), custom_call_target="tpu_custom_call" | custom-call | flops 67108864 | bytes 2188688 | tf_op jit(solution)/shard_map/first_payload/pallas_call | solution.py:232
  3.9 5.1 %collective-permute-start = (bf16[16,512]{1,0:T(8,128)(2,1)S(1)}, bf16[16,512]{1,0:T(8,128)(2,1)S(1)}, u32[]{:S(2)}, u32[]{:S(2)}) collective-permute-start(bf16[16,512]{1,0:T(8,128)(2,1)S(1)} %get-tuple-element.165), channel_id=1, source_target_pairs={{0,12},{4,8},{8,4},{12,0},{1,13},{5,9},{9,5},{13,1},{2,14},{6,10},... | collective-permute-start | bytes 49160 | tf_op jit(solution)/shard_map/ppermute | solution.py:248
  16.3 1.5 %collective-permute-start.8 = (bf16[32,512]{1,0:T(8,128)(2,1)S(1)}, bf16[32,512]{1,0:T(8,128)(2,1)S(1)}, u32[]{:S(2)}, u32[]{:S(2)}) collective-permute-start(bf16[32,512]{1,0:T(8,128)(2,1)S(1)} %get-tuple-element.180), channel_id=1, source_target_pairs={{0,2},{1,3},{2,0},{3,1},{4,6},{5,7},{6,4},{7,5},{8,10},{9,11},{10,... | collective-permute-start | bytes 98312 | tf_op jit(solution)/shard_map/ppermute | solution.py:251
  18.1 1.9 %forward_local.1 = (f32[256,512]{1,0:T(8,128)S(1)}, bf16[6,256,512]{2,1,0:T(8,128)(2,1)S(1)}, f32[40,512]{1,0:T(8,128)S(1)}, bf16[40,512]{1,0:T(8,128)(2,1)S(1)}) custom-call(bf16[256,512]{1,0:T(8,128)(2,1)S(1)} %get-tuple-element.182.state_ref.refs_7_.refs_10_, bf16[2,512,512]{2,1,0:T(8,128)(2,1)S(1)} %copy-done, bf16[2,512,512]{2,1,0:T(8,128)(2,1)S(1)} %copy-done.2, ...), custom_call_target="tpu_custom_call" | custom-call | flops 805306368 | bytes 4593824 | tf_op jit(solution)/shard_map/forward_local/pallas_call | solution.py:232
  21.4 2.7 %collective-permute-start.10 = (bf16[16,512]{1,0:T(8,128)(2,1)S(1)}, bf16[16,512]{1,0:T(8,128)(2,1)S(1)}, u32[]{:S(2)}, u32[]{:S(2)}) collective-permute-start(bf16[16,512]{1,0:T(8,128)(2,1)S(1)} %get-tuple-element.187), channel_id=1, source_target_pairs={{0,12},{4,8},{8,4},{12,0},{1,13},{5,9},{9,5},{13,1},{2,14},{6,10},... | collective-permute-start | bytes 49160 | tf_op jit(solution)/shard_map/ppermute | solution.py:248
  26.5 3.0 %turn_local.1 = (f32[256,512]{1,0:T(8,128)S(1)}, f32[256,512]{1,0:T(8,128)S(1)}, f32[256,512]{1,0:T(8,128)S(1)}, f32[40,512]{1,0:T(8,128)S(1)}, bf16[40,512]{1,0...) custom-call(bf16[256,512]{1,0:T(8,128)(2,1)S(1)} %get-tuple-element., ...), custom_call_target="tpu_custom_call" | custom-call | flops 1342177280 | bytes 5871776 | tf_op jit(solution)/shard_map/turn_local/pallas_call | solution.py:232
  29.6 1.4 %turn_halo.1 = (bf16[256,512]{1,0:T(8,128)(2,1)S(1)}, bf16[256,512]{1,0:T(8,128)(2,1)S(1)}, bf16[256,512]{1,0:T(8,128)(2,1)S(1)}, bf16[256,512]{1,0:T(8,128)(2,1...) custom-call(bf16[16,512]{1,0:T(8,128)(2,1)S(1)} %collective-permute-, ...), custom_call_target="tpu_custom_call" | custom-call | flops 402653184 | bytes 5322912 | tf_op jit(solution)/shard_map/turn_halo/pallas_call | solution.py:232
  31.0 1.5 %last_weights.1 = (bf16[768,512]{1,0:T(8,128)(2,1)S(1)}, bf16[768,512]{1,0:T(8,128)(2,1)S(1)}, bf16[256,512]{1,0:T(8,128)(2,1)}) custom-call(s32[6,6]{1,0:T(8,128)S(1)} %get-tuple-element.164.refs_0_.refs_5_, bf16[256,512]{1,0:T(8,128)(2,1)S(1)} %get-tuple-element.186.state_ref.refs_1_, bf16[256,512]{1,0:T(8,128)(2,1)S(1)} %get-tuple-element.204.refs_2_, ...), custom_call_target="tpu_custom_call" | custom-call | flops 536870912 | bytes 4194448 | tf_op jit(solution)/shard_map/last_weights/pallas_call | solution.py:232
  36.4 2.9 %back_local.1 = (f32[256,512]{1,0:T(8,128)S(1)}, bf16[512,512]{1,0:T(8,128)(2,1)S(1)}, bf16[512,512]{1,0:T(8,128)(2,1)S(1)}, bf16[512,512]{1,0:T(8,128)(2,1)S(1)}, bf16[512,512]{1,0:T(8,128)(2,1)S(1)}) custom-call(s32[6,6]{1,0:T(8,128)S(1)} %get-tuple-element.164.refs_0_.refs_5_, bf16[256,512]{1,0:T(8,128)(2,1)S(1)} %get-tuple-element.208.refs_1_, ...), custom_call_target="tpu_custom_call" | custom-call | flops 1342177280 | bytes 8960144 | tf_op jit(solution)/shard_map/back_local/pallas_call | solution.py:232
  40.1 1.3 %collective-permute-start.23 = (bf16[384,512]{1,0:T(8,128)(2,1)S(1)}, bf16[384,512]{1,0:T(8,128)(2,1)S(1)}, u32[]{:S(2)}, u32[]{:S(2)}) collective-permute-start(bf16[384,512]{1,0:T(8,128)(2,1)S(1)} %get-tuple-element.251), channel_id=1, source_target_pairs={{0,4},{1,5},{2,6},{3,7},{4,0},{5,1},{6,2},{7,3},{8,12},{9,13},{10,... | collective-permute-start | bytes 1179656 | tf_op jit(solution)/shard_map/ppermute | solution.py:163
  41.9 2.3 %embed_back.1 = (bf16[512,512]{1,0:T(8,128)(2,1)S(1)}, bf16[256,512]{1,0:T(8,128)(2,1)S(1)}, bf16[288,512]{1,0:T(8,128)(2,1)S(1)}, bf16[16,512]{1,0:T(8,128)(2,1...) custom-call(bf16[8,512]{1,0:T(8,128)(2,1)S(1)} %collective-permute-d, ...), custom_call_target="tpu_custom_call" | custom-call | flops 805306368 | bytes 6130608 | tf_op jit(solution)/shard_map/embed_back/pallas_call | solution.py:232
  45.8 5.8 %collective-permute-done.23.refs_2_ = bf16[384,512]{1,0:T(8,128)(2,1)S(1)} collective-permute-done((bf16[384,512]{1,0:T(8,128)(2,1)S(1)}, bf16[384,512]{1,0:T(8,128)(2,1)S(1)}, u32[]{:S(2)}, u32[]{:S(2)}) %collective-permute-start.23) | collective-permute-done | bytes 393248 | tf_op jit(solution)/shard_map/ppermute | solution.py:163
  56.2 2.0 %collective-permute-start.30 = (bf16[192,512]{1,0:T(8,128)(2,1)S(1)}, bf16[192,512]{1,0:T(8,128)(2,1)S(1)}, u32[]{:S(2)}, u32[]{:S(2)}) collective-permute-start(bf16[192,512]{1,0:T(8,128)(2,1)S(1)} %get-tuple-element.282), channel_id=1, source_target_pairs={{0,8},{1,9},{2,10},{3,11},{4,12},{5,13},{6,14},{7,15},{8,0},{9,1},... | collective-permute-start | bytes 589832 | tf_op jit(solution)/shard_map/ppermute | solution.py:163
  58.2 1.3 %collective-permute-done.26.refs_2_ = bf16[160,512]{1,0:T(8,128)(2,1)S(1)} collective-permute-done((bf16[160,512]{1,0:T(8,128)(2,1)S(1)}, bf16[160,512]{1,0:T(8,128)(2,1)S(1)}, u32[]{:S(2)}, u32[]{:S(2)}) %collective-permute-start.26) | collective-permute-done | bytes 163872 | tf_op jit(solution)/shard_map/ppermute | solution.py:163
  59.7 1.3 %collective-permute-start.28 = (bf16[96,512]{1,0:T(8,128)(2,1)S(1)}, bf16[96,512]{1,0:T(8,128)(2,1)S(1)}, u32[]{:S(2)}, u32[]{:S(2)}) collective-permute-start(bf16[96,512]{1,0:T(8,128)(2,1)S(1)} %get-tuple-element.278), channel_id=1, source_target_pairs={{0,4},{1,5},{2,6},{3,7},{4,0},{5,1},{6,2},{7,3},{8,12},{9,13},{10,... | collective-permute-start | bytes 294920 | tf_op jit(solution)/shard_map/ppermute | solution.py:163
  60.9 3.3 %collective-permute-done.27.refs_2_ = bf16[128,512]{1,0:T(8,128)(2,1)S(1)} collective-permute-done((bf16[128,512]{1,0:T(8,128)(2,1)S(1)}, bf16[128,512]{1,0:T(8,128)(2,1)S(1)}, u32[]{:S(2)}, u32[]{:S(2)}) %collective-permute-start.27) | collective-permute-done | bytes 131104 | tf_op jit(solution)/shard_map/ppermute | solution.py:163
  64.4 1.7 %collective-permute-done.28.refs_2_ = bf16[96,512]{1,0:T(8,128)(2,1)S(1)} collective-permute-done((bf16[96,512]{1,0:T(8,128)(2,1)S(1)}, bf16[96,512]{1,0:T(8,128)(2,1)S(1)}, u32[]{:S(2)}, u32[]{:S(2)}) %collective-permute-start.28) | collective-permute-done | bytes 98336 | tf_op jit(solution)/shard_map/ppermute | solution.py:163
  66.7 3.3 %collective-permute-done.29.arr0_ref = bf16[64,512]{1,0:T(8,128)(2,1)S(1)} collective-permute-done((bf16[64,512]{1,0:T(8,128)(2,1)S(1)}, bf16[64,512]{1,0:T(8,128)(2,1)S(1)}, u32[]{:S(2)}, u32[]{:S(2)}) %collective-permute-start.29) | collective-permute-done | bytes 65568 | tf_op jit(solution)/shard_map/ppermute | solution.py:163
  70.4 1.3 %collective-permute-start.33 = (bf16[96,512]{1,0:T(8,128)(2,1)S(1)}, bf16[96,512]{1,0:T(8,128)(2,1)S(1)}, u32[]{:S(2)}, u32[]{:S(2)}) collective-permute-start(bf16[96,512]{1,0:T(8,128)(2,1)S(1)} %get-tuple-element.295), channel_id=1, source_target_pairs={{0,2},{1,3},{2,0},{3,1},{4,6},{5,7},{6,4},{7,5},{8,10},{9,11},{10,... | collective-permute-start | bytes 294920 | tf_op jit(solution)/shard_map/ppermute | solution.py:163
  71.7 3.2 %collective-permute-start.32 = (bf16[48,512]{1,0:T(8,128)(2,1)S(1)}, bf16[48,512]{1,0:T(8,128)(2,1)S(1)}, u32[]{:S(2)}, u32[]{:S(2)}) collective-permute-start(bf16[48,512]{1,0:T(8,128)(2,1)S(1)} %get-tuple-element.288), channel_id=1, source_target_pairs={{0,8},{1,9},{2,10},{3,11},{4,12},{5,13},{6,14},{7,15},{8,0},{9,1},... | collective-permute-start | bytes 147464 | tf_op jit(solution)/shard_map/ppermute | solution.py:163
  74.9 2.1 %collective-permute-done.32.refs_0_.arr_e_ref = bf16[48,512]{1,0:T(8,128)(2,1)S(1)} collective-permute-done((bf16[48,512]{1,0:T(8,128)(2,1)S(1)}, bf16[48,512]{1,0:T(8,128)(2,1)S(1)}, u32[]{:S(2)}, u32[]{:S(2)}) %collective-permute-start.32) | collective-permute-done | bytes 49184 | tf_op jit(solution)/shard_map/ppermute | solution.py:163
  77.0 1.3 %grid_place.1 = bf16[512,512]{1,0:T(8,128)(2,1)} custom-call(bf16[48,512]{1,0:T(8,128)(2,1)S(1)} %collective-permute-done.32.refs_0_.arr_e_ref, bf16[16,512]{1,0:T(8,128)(2,1)S(1)} %get-tuple-element.289.refs_1_, bf16[16,512]{1,0:T(8,128)(2,1)S(1)} %get-tuple-element.290.refs_2_, bf16[16,512]{1,0:T(8,128)(2,1)S(1)} %get-tuple-element.291.refs_3_, ...), custom_call_target="tpu_custom_call" | custom-call | flops 402653184 | bytes 1687872 | tf_op jit(solution)/shard_map/grid_place/pallas_call | solution.py:232
  78.5 3.0 %collective-permute-start.35 = (bf16[64,512]{1,0:T(8,128)(2,1)S(1)}, bf16[64,512]{1,0:T(8,128)(2,1)S(1)}, u32[]{:S(2)}, u32[]{:S(2)}) collective-permute-start(bf16[64,512]{1,0:T(8,128)(2,1)S(1)} %get-tuple-element.304), channel_id=1, source_target_pairs={{0,8},{1,9},{2,10},{3,11},{4,12},{5,13},{6,14},{7,15},{8,0},{9,1},... | collective-permute-start | bytes 196616 | tf_op jit(solution)/shard_map/ppermute | solution.py:163
  81.4 2.2 %collective-permute-done.35.arr2_ref = bf16[64,512]{1,0:T(8,128)(2,1)S(1)} collective-permute-done((bf16[64,512]{1,0:T(8,128)(2,1)S(1)}, bf16[64,512]{1,0:T(8,128)(2,1)S(1)}, u32[]{:S(2)}, u32[]{:S(2)}) %collective-permute-start.35) | collective-permute-done | bytes 65568 | tf_op jit(solution)/shard_map/ppermute | solution.py:163
  (83 shorter events, 26.6 us)
Async XLA Ops:
  3.9 8.0 %collective-permute-start = (bf16[16,512]{1,0:T(8,128)(2,1)S(1)}, bf16[16,512]{1,0:T(8,128)(2,1)S(1)}, u32[]{:S(2)}, u32[]{:S(2)}) collective-permute-start(bf16[16,512]{1,0:T(8,128)(2,1)S(1)} %get-tuple-element.165), channel_id=1, source_target_pairs={{0,12},{4,8},{8,4},{12,0},{1,13},{5,9},{9,5},{13,1},{2,14},{6,10},... | collective-permute-start | bytes 49160 | tf_op jit(solution)/shard_map/ppermute | solution.py:248
  14.5 5.8 %collective-permute-start.5 = (bf16[32,512]{1,0:T(8,128)(2,1)S(1)}, bf16[32,512]{1,0:T(8,128)(2,1)S(1)}, u32[]{:S(2)}, u32[]{:S(2)}) collective-permute-start(bf16[32,512]{1,0:T(8,128)(2,1)S(1)} %get-tuple-element.177), channel_id=1, source_target_pairs={{0,12},{4,8},{8,4},{12,0},{1,13},{5,9},{9,5},{13,1},{2,14},{6,10},... | collective-permute-start | bytes 98312 | tf_op jit(solution)/shard_map/ppermute | solution.py:248
  15.6 4.7 %collective-permute-start.6 = (bf16[32,512]{1,0:T(8,128)(2,1)S(1)}, bf16[32,512]{1,0:T(8,128)(2,1)S(1)}, u32[]{:S(2)}, u32[]{:S(2)}) collective-permute-start(bf16[32,512]{1,0:T(8,128)(2,1)S(1)} %get-tuple-element.178), channel_id=1, source_target_pairs={{0,4},{4,0},{8,12},{12,8},{1,5},{5,1},{9,13},{13,9},{2,6},{6,2},{1... | collective-permute-start | bytes 98312 | tf_op jit(solution)/shard_map/ppermute | solution.py:249
  21.4 8.1 %collective-permute-start.10 = (bf16[16,512]{1,0:T(8,128)(2,1)S(1)}, bf16[16,512]{1,0:T(8,128)(2,1)S(1)}, u32[]{:S(2)}, u32[]{:S(2)}) collective-permute-start(bf16[16,512]{1,0:T(8,128)(2,1)S(1)} %get-tuple-element.187), channel_id=1, source_target_pairs={{0,12},{4,8},{8,4},{12,0},{1,13},{5,9},{9,5},{13,1},{2,14},{6,10},... | collective-permute-start | bytes 49160 | tf_op jit(solution)/shard_map/ppermute | solution.py:248
  24.1 5.4 %collective-permute-start.11 = (bf16[16,512]{1,0:T(8,128)(2,1)S(1)}, bf16[16,512]{1,0:T(8,128)(2,1)S(1)}, u32[]{:S(2)}, u32[]{:S(2)}) collective-permute-start(bf16[16,512]{1,0:T(8,128)(2,1)S(1)} %get-tuple-element.188), channel_id=1, source_target_pairs={{0,4},{4,0},{8,12},{12,8},{1,5},{5,1},{9,13},{13,9},{2,6},{6,2},{1... | collective-permute-start | bytes 49160 | tf_op jit(solution)/shard_map/ppermute | solution.py:249
  24.7 4.9 %collective-permute-start.12 = (bf16[16,512]{1,0:T(8,128)(2,1)S(1)}, bf16[16,512]{1,0:T(8,128)(2,1)S(1)}, u32[]{:S(2)}, u32[]{:S(2)}) collective-permute-start(bf16[16,512]{1,0:T(8,128)(2,1)S(1)} %get-tuple-element.189), channel_id=1, source_target_pairs={{0,3},{1,2},{2,1},{3,0},{4,7},{5,6},{6,5},{7,4},{8,11},{9,10},{10,... | collective-permute-start | bytes 49160 | tf_op jit(solution)/shard_map/ppermute | solution.py:251
  25.1 4.4 %collective-permute-start.13 = (bf16[16,512]{1,0:T(8,128)(2,1)S(1)}, bf16[16,512]{1,0:T(8,128)(2,1)S(1)}, u32[]{:S(2)}, u32[]{:S(2)}) collective-permute-start(bf16[16,512]{1,0:T(8,128)(2,1)S(1)} %get-tuple-element.190), channel_id=1, source_target_pairs={{0,2},{1,3},{2,0},{3,1},{4,6},{5,7},{6,4},{7,5},{8,10},{9,11},{10,... | collective-permute-start | bytes 49160 | tf_op jit(solution)/shard_map/ppermute | solution.py:251
  33.0 6.3 %collective-permute-start.17 = (bf16[8,512]{1,0:T(8,128)(2,1)S(1)}, bf16[8,512]{1,0:T(8,128)(2,1)S(1)}, u32[]{:S(2)}, u32[]{:S(2)}) collective-permute-start(bf16[8,512]{1,0:T(8,128)(2,1)S(1)} %get-tuple-element.224), channel_id=1, source_target_pairs={{0,12},{4,8},{8,4},{12,0},{1,13},{5,9},{9,5},{13,1},{2,14},{6,10},... | collective-permute-start | bytes 24584 | tf_op jit(solution)/shard_map/ppermute | solution.py:248
  34.0 5.4 %collective-permute-start.18 = (bf16[8,512]{1,0:T(8,128)(2,1)S(1)}, bf16[8,512]{1,0:T(8,128)(2,1)S(1)}, u32[]{:S(2)}, u32[]{:S(2)}) collective-permute-start(bf16[8,512]{1,0:T(8,128)(2,1)S(1)} %get-tuple-element.225), channel_id=1, source_target_pairs={{0,4},{4,0},{8,12},{12,8},{1,5},{5,1},{9,13},{13,9},{2,6},{6,2},{1... | collective-permute-start | bytes 24584 | tf_op jit(solution)/shard_map/ppermute | solution.py:249
  34.8 4.5 %collective-permute-start.19 = (bf16[8,512]{1,0:T(8,128)(2,1)S(1)}, bf16[8,512]{1,0:T(8,128)(2,1)S(1)}, u32[]{:S(2)}, u32[]{:S(2)}) collective-permute-start(bf16[8,512]{1,0:T(8,128)(2,1)S(1)} %get-tuple-element.226), channel_id=1, source_target_pairs={{0,3},{1,2},{2,1},{3,0},{4,7},{5,6},{6,5},{7,4},{8,11},{9,10},{10,... | collective-permute-start | bytes 24584 | tf_op jit(solution)/shard_map/ppermute | solution.py:251
  40.1 13.6 %collective-permute-start.24 = (bf16[512,512]{1,0:T(8,128)(2,1)S(1)}, bf16[512,512]{1,0:T(8,128)(2,1)S(1)}, u32[]{:S(2)}, u32[]{:S(2)}) collective-permute-start(bf16[512,512]{1,0:T(8,128)(2,1)S(1)} %get-tuple-element.259), channel_id=1, source_target_pairs={{0,1},{1,0},{2,3},{3,2},{4,5},{5,4},{6,7},{7,6},{8,9},{9,8},{10,11... | collective-permute-start | bytes 1572872 | tf_op jit(solution)/shard_map/ppermute | solution.py:163
  40.1 11.5 %collective-permute-start.23 = (bf16[384,512]{1,0:T(8,128)(2,1)S(1)}, bf16[384,512]{1,0:T(8,128)(2,1)S(1)}, u32[]{:S(2)}, u32[]{:S(2)}) collective-permute-start(bf16[384,512]{1,0:T(8,128)(2,1)S(1)} %get-tuple-element.251), channel_id=1, source_target_pairs={{0,4},{1,5},{2,6},{3,7},{4,0},{5,1},{6,2},{7,3},{8,12},{9,13},{10,... | collective-permute-start | bytes 1179656 | tf_op jit(solution)/shard_map/ppermute | solution.py:163
  44.2 7.4 %collective-permute-start.22 = (bf16[288,512]{1,0:T(8,128)(2,1)S(1)}, bf16[288,512]{1,0:T(8,128)(2,1)S(1)}, u32[]{:S(2)}, u32[]{:S(2)}) collective-permute-start(bf16[288,512]{1,0:T(8,128)(2,1)S(1)} %get-tuple-element.250), channel_id=1, source_target_pairs={{0,1},{1,0},{2,3},{3,2},{4,5},{5,4},{6,7},{7,6},{8,9},{9,8},{10,11... | collective-permute-start | bytes 884744 | tf_op jit(solution)/shard_map/ppermute | solution.py:163
  44.6 10.2 %collective-permute-start.25 = (bf16[256,512]{1,0:T(8,128)(2,1)S(1)}, bf16[256,512]{1,0:T(8,128)(2,1)S(1)}, u32[]{:S(2)}, u32[]{:S(2)}) collective-permute-start(bf16[256,512]{1,0:T(8,128)(2,1)S(1)} %get-tuple-element.265), channel_id=1, source_target_pairs={{0,2},{1,3},{2,0},{3,1},{4,6},{5,7},{6,4},{7,5},{8,10},{9,11},{10,... | collective-permute-start | bytes 786440 | tf_op jit(solution)/shard_map/ppermute | solution.py:163
  52.4 7.1 %collective-permute-start.26 = (bf16[160,512]{1,0:T(8,128)(2,1)S(1)}, bf16[160,512]{1,0:T(8,128)(2,1)S(1)}, u32[]{:S(2)}, u32[]{:S(2)}) collective-permute-start(bf16[160,512]{1,0:T(8,128)(2,1)S(1)} %get-tuple-element.269), channel_id=1, source_target_pairs={{0,2},{1,3},{2,0},{3,1},{4,6},{5,7},{6,4},{7,5},{8,10},{9,11},{10,... | collective-permute-start | bytes 491528 | tf_op jit(solution)/shard_map/ppermute | solution.py:163
  53.9 16.2 %collective-permute-start.31 = (bf16[256,512]{1,0:T(8,128)(2,1)S(1)}, bf16[256,512]{1,0:T(8,128)(2,1)S(1)}, u32[]{:S(2)}, u32[]{:S(2)}) collective-permute-start(bf16[256,512]{1,0:T(8,128)(2,1)S(1)} %get-tuple-element.285), channel_id=1, source_target_pairs={{0,2},{1,3},{2,0},{3,1},{4,6},{5,7},{6,4},{7,5},{8,10},{9,11},{10,... | collective-permute-start | bytes 786440 | tf_op jit(solution)/shard_map/ppermute | solution.py:163
  55.0 9.2 %collective-permute-start.27 = (bf16[128,512]{1,0:T(8,128)(2,1)S(1)}, bf16[128,512]{1,0:T(8,128)(2,1)S(1)}, u32[]{:S(2)}, u32[]{:S(2)}) collective-permute-start(bf16[128,512]{1,0:T(8,128)(2,1)S(1)} %get-tuple-element.275), channel_id=1, source_target_pairs={{0,4},{1,5},{2,6},{3,7},{4,0},{5,1},{6,2},{7,3},{8,12},{9,13},{10,... | collective-permute-start | bytes 393224 | tf_op jit(solution)/shard_map/ppermute | solution.py:163
  56.2 13.8 %collective-permute-start.30 = (bf16[192,512]{1,0:T(8,128)(2,1)S(1)}, bf16[192,512]{1,0:T(8,128)(2,1)S(1)}, u32[]{:S(2)}, u32[]{:S(2)}) collective-permute-start(bf16[192,512]{1,0:T(8,128)(2,1)S(1)} %get-tuple-element.282), channel_id=1, source_target_pairs={{0,8},{1,9},{2,10},{3,11},{4,12},{5,13},{6,14},{7,15},{8,0},{9,1},... | collective-permute-start | bytes 589832 | tf_op jit(solution)/shard_map/ppermute | solution.py:163
  59.7 6.5 %collective-permute-start.28 = (bf16[96,512]{1,0:T(8,128)(2,1)S(1)}, bf16[96,512]{1,0:T(8,128)(2,1)S(1)}, u32[]{:S(2)}, u32[]{:S(2)}) collective-permute-start(bf16[96,512]{1,0:T(8,128)(2,1)S(1)} %get-tuple-element.278), channel_id=1, source_target_pairs={{0,4},{1,5},{2,6},{3,7},{4,0},{5,1},{6,2},{7,3},{8,12},{9,13},{10,... | collective-permute-start | bytes 294920 | tf_op jit(solution)/shard_map/ppermute | solution.py:163
  64.3 5.7 %collective-permute-start.29 = (bf16[64,512]{1,0:T(8,128)(2,1)S(1)}, bf16[64,512]{1,0:T(8,128)(2,1)S(1)}, u32[]{:S(2)}, u32[]{:S(2)}) collective-permute-start(bf16[64,512]{1,0:T(8,128)(2,1)S(1)} %get-tuple-element.280), channel_id=1, source_target_pairs={{0,8},{1,9},{2,10},{3,11},{4,12},{5,13},{6,14},{7,15},{8,0},{9,1},... | collective-permute-start | bytes 196616 | tf_op jit(solution)/shard_map/ppermute | solution.py:163
  70.3 8.0 %collective-permute-start.34 = (bf16[128,512]{1,0:T(8,128)(2,1)S(1)}, bf16[128,512]{1,0:T(8,128)(2,1)S(1)}, u32[]{:S(2)}, u32[]{:S(2)}) collective-permute-start(bf16[128,512]{1,0:T(8,128)(2,1)S(1)} %get-tuple-element.302), channel_id=1, source_target_pairs={{0,4},{1,5},{2,6},{3,7},{4,0},{5,1},{6,2},{7,3},{8,12},{9,13},{10,... | collective-permute-start | bytes 393224 | tf_op jit(solution)/shard_map/ppermute | solution.py:163
  70.4 7.9 %collective-permute-start.33 = (bf16[96,512]{1,0:T(8,128)(2,1)S(1)}, bf16[96,512]{1,0:T(8,128)(2,1)S(1)}, u32[]{:S(2)}, u32[]{:S(2)}) collective-permute-start(bf16[96,512]{1,0:T(8,128)(2,1)S(1)} %get-tuple-element.295), channel_id=1, source_target_pairs={{0,2},{1,3},{2,0},{3,1},{4,6},{5,7},{6,4},{7,5},{8,10},{9,11},{10,... | collective-permute-start | bytes 294920 | tf_op jit(solution)/shard_map/ppermute | solution.py:163
  71.7 5.2 %collective-permute-start.32 = (bf16[48,512]{1,0:T(8,128)(2,1)S(1)}, bf16[48,512]{1,0:T(8,128)(2,1)S(1)}, u32[]{:S(2)}, u32[]{:S(2)}) collective-permute-start(bf16[48,512]{1,0:T(8,128)(2,1)S(1)} %get-tuple-element.288), channel_id=1, source_target_pairs={{0,8},{1,9},{2,10},{3,11},{4,12},{5,13},{6,14},{7,15},{8,0},{9,1},... | collective-permute-start | bytes 147464 | tf_op jit(solution)/shard_map/ppermute | solution.py:163
  78.5 5.2 %collective-permute-start.35 = (bf16[64,512]{1,0:T(8,128)(2,1)S(1)}, bf16[64,512]{1,0:T(8,128)(2,1)S(1)}, u32[]{:S(2)}, u32[]{:S(2)}) collective-permute-start(bf16[64,512]{1,0:T(8,128)(2,1)S(1)} %get-tuple-element.304), channel_id=1, source_target_pairs={{0,8},{1,9},{2,10},{3,11},{4,12},{5,13},{6,14},{7,15},{8,0},{9,1},... | collective-permute-start | bytes 196616 | tf_op jit(solution)/shard_map/ppermute | solution.py:163
  (15 other events, 60.9 us)

commit v12 on v9

--- a/solution.py
+++ b/solution.py
@@ -731,13 +731,13 @@
         keep1, keep0 = lax.optimization_barrier((keep1, keep0))
         keep1, give1 = halve_step(3, keep1, arr1, place)
         arr1 = swap(give1, 3, dims)
-        keep2, keep1 = lax.optimization_barrier((keep2, keep1))
+        keep0, keep1 = lax.optimization_barrier((keep0, keep1))
+        keep0, give0 = halve_step(3, keep0, arr0, place)
+        arr0 = swap(give0, 3, dims)
+        keep2, keep0 = lax.optimization_barrier((keep2, keep0))
         keep2, give2 = halve_step(2, keep2, arr2, place)
         arr2 = swap(give2, 2, dims)
-        keep0, keep2 = lax.optimization_barrier((keep0, keep2))
-        keep0, give0 = halve_step(3, keep0, arr0, place)
-        arr0 = swap(give0, 3, dims)
-        keep_e, keep0, arr1 = lax.optimization_barrier((keep_e, keep0, arr1))
+        keep_e, keep2, arr1, arr0 = lax.optimization_barrier((keep_e, keep2, arr1, arr0))
         keep_e, give_e, from_lat, from_diag = carry_step(
             2, keep_e, arr_e, pay5[3:], place, capacity
         )
@@ -745,7 +745,7 @@
         keep2, keep_e = lax.optimization_barrier((keep2, keep_e))
         keep2, give2 = halve_step(3, keep2, arr2, place)
         arr2 = swap(give2, 3, dims)
-        keep_e, keep2, arr0 = lax.optimization_barrier((keep_e, keep2, arr0))
+        keep_e, keep2 = lax.optimization_barrier((keep_e, keep2))
         keep_e, give_e, from_near, _ = carry_step(3, keep_e, arr_e, (), place, capacity)
         arr_e = swap(give_e, 3, dims)
         arr5 = (arr_e, from_near, from_diag, from_lat, from_sub)

time: 82.5 us -> 83.3 us (level)
  waiting for transfers between devices: 20 us -> 20.9 us
    ppermute x16, waiting for transfers between devices: 17.9 us -> 18.8 us  [swap(): return lax.ppermute(block, GROUP, [(i, i ^ 1 << bit) for i in range(total)])]
  transfers between devices with their start and end apart: 36 -> 36, of which waited for: 12 -> 13; matrix products, arithmetic and copies ran while one was open for 0% -> 0% of each run, Pallas kernels for 20% -> 20%
where the time goes in v12:
time: 83.3 us; the launch traced here: 83 us
  starting transfers between devices  36.8 us (44%)
  Pallas kernels  22.8 us (27%)
  waiting for transfers between devices  20.9 us (25%)
  local copies, waits for them, and re-layouts  1.56 us (2%)
  between operations  0.92 us (1%)
    pallas_call x24, Pallas kernels, call(): pl.pallas_call(kernel, out_shape=[shape(*a.shape, dtype=a.dtype) for a in...  22.8 us
    ppermute x16, waiting for transfers between devices, swap(): return lax.ppermute(block, GROUP, [(i, i ^ 1 << bit) for i in range(total)])  18.8 us
    ppermute x16, starting transfers between devices, swap(): return lax.ppermute(block, GROUP, [(i, i ^ 1 << bit) for i in range(total)])  18 us
    ppermute x4, starting transfers between devices, exchange(): far = lax.ppermute(parts[column], 'lon', other)  9.87 us
    ppermute x12, starting transfers between devices, exchange(): lax.ppermute(parts[r - 1], COLUMN, [(i, i ^ r) for i in range(column)])  6.88 us
    ppermute x4, starting transfers between devices, exchange(): lax.ppermute(parts[column - 1], 'lon', [(i, i ^ 1) for i in range(count)])  2 us
  transfers between devices with their start and end apart: 36, of which 13 were waited for; matrix products, arithmetic and copies ran while one was open for 0% of the time, Pallas kernels for 20%

profile of v12, /device:TPU:0, one launch (start us, length us, event | category | flops | bytes accessed | tf_op | source)
XLA Modules:
  0.0 83.0 jit_solution(3302654576852409948)
XLA Ops:
  2.3 1.6 %first_payload.1 = (bf16[512,512]{1,0:T(8,128)(2,1)S(1)}, bf16[512,512]{1,0:T(8,128)(2,1)S(1)}, s32[1,512]{1,0:T(1,128)S(1)}, s32[6,256]{1,0:T(8,128)S(1)}, bf16...) custom-call(bf16[512,512]{1,0:T(8,128)(2,1)} %refs_0_.1, ...), custom_call_target="tpu_custom_call" | custom-call | flops 67108864 | bytes 2188688 | tf_op jit(solution)/shard_map/first_payload/pallas_call | solution.py:231
  3.9 5.1 %collective-permute-start = (bf16[16,512]{1,0:T(8,128)(2,1)S(1)}, bf16[16,512]{1,0:T(8,128)(2,1)S(1)}, u32[]{:S(2)}, u32[]{:S(2)}) collective-permute-start(bf16[16,512]{1,0:T(8,128)(2,1)S(1)} %get-tuple-element.163), channel_id=1, source_target_pairs={{0,12},{4,8},{8,4},{12,0},{1,13},{5,9},{9,5},{13,1},{2,14},{6,10},... | collective-permute-start | bytes 49160 | tf_op jit(solution)/shard_map/ppermute | solution.py:247
  16.3 1.5 %collective-permute-start.8 = (bf16[32,512]{1,0:T(8,128)(2,1)S(1)}, bf16[32,512]{1,0:T(8,128)(2,1)S(1)}, u32[]{:S(2)}, u32[]{:S(2)}) collective-permute-start(bf16[32,512]{1,0:T(8,128)(2,1)S(1)} %get-tuple-element.178), channel_id=1, source_target_pairs={{0,2},{1,3},{2,0},{3,1},{4,6},{5,7},{6,4},{7,5},{8,10},{9,11},{10,... | collective-permute-start | bytes 98312 | tf_op jit(solution)/shard_map/ppermute | solution.py:250
  18.1 1.9 %forward_local.1 = (f32[256,512]{1,0:T(8,128)S(1)}, bf16[6,256,512]{2,1,0:T(8,128)(2,1)S(1)}, f32[40,512]{1,0:T(8,128)S(1)}, bf16[40,512]{1,0:T(8,128)(2,1)S(1)}) custom-call(bf16[256,512]{1,0:T(8,128)(2,1)S(1)} %get-tuple-element.180.state_ref.refs_7_.refs_10_, bf16[2,512,512]{2,1,0:T(8,128)(2,1)S(1)} %copy-done, bf16[2,512,512]{2,1,0:T(8,128)(2,1)S(1)} %copy-done.2, ...), custom_call_target="tpu_custom_call" | custom-call | flops 805306368 | bytes 4593824 | tf_op jit(solution)/shard_map/forward_local/pallas_call | solution.py:231
  21.4 2.7 %collective-permute-start.10 = (bf16[16,512]{1,0:T(8,128)(2,1)S(1)}, bf16[16,512]{1,0:T(8,128)(2,1)S(1)}, u32[]{:S(2)}, u32[]{:S(2)}) collective-permute-start(bf16[16,512]{1,0:T(8,128)(2,1)S(1)} %get-tuple-element.185), channel_id=1, source_target_pairs={{0,12},{4,8},{8,4},{12,0},{1,13},{5,9},{9,5},{13,1},{2,14},{6,10},... | collective-permute-start | bytes 49160 | tf_op jit(solution)/shard_map/ppermute | solution.py:247
  26.5 3.0 %turn_local.1 = (f32[256,512]{1,0:T(8,128)S(1)}, f32[256,512]{1,0:T(8,128)S(1)}, f32[256,512]{1,0:T(8,128)S(1)}, f32[40,512]{1,0:T(8,128)S(1)}, bf16[40,512]{1,0...) custom-call(bf16[256,512]{1,0:T(8,128)(2,1)S(1)} %get-tuple-element., ...), custom_call_target="tpu_custom_call" | custom-call | flops 1342177280 | bytes 5871776 | tf_op jit(solution)/shard_map/turn_local/pallas_call | solution.py:231
  29.6 1.4 %turn_halo.1 = (bf16[256,512]{1,0:T(8,128)(2,1)S(1)}, bf16[256,512]{1,0:T(8,128)(2,1)S(1)}, bf16[256,512]{1,0:T(8,128)(2,1)S(1)}, bf16[256,512]{1,0:T(8,128)(2,1...) custom-call(bf16[16,512]{1,0:T(8,128)(2,1)S(1)} %collective-permute-, ...), custom_call_target="tpu_custom_call" | custom-call | flops 402653184 | bytes 5322912 | tf_op jit(solution)/shard_map/turn_halo/pallas_call | solution.py:231
  31.0 1.5 %last_weights.1 = (bf16[768,512]{1,0:T(8,128)(2,1)S(1)}, bf16[768,512]{1,0:T(8,128)(2,1)S(1)}, bf16[256,512]{1,0:T(8,128)(2,1)}) custom-call(s32[6,6]{1,0:T(8,128)S(1)} %get-tuple-element.162.refs_0_.refs_5_, bf16[256,512]{1,0:T(8,128)(2,1)S(1)} %get-tuple-element.184.state_ref.refs_1_, bf16[256,512]{1,0:T(8,128)(2,1)S(1)} %get-tuple-element.202.refs_2_, ...), custom_call_target="tpu_custom_call" | custom-call | flops 536870912 | bytes 4194448 | tf_op jit(solution)/shard_map/last_weights/pallas_call | solution.py:231
  36.4 2.9 %back_local.1 = (f32[256,512]{1,0:T(8,128)S(1)}, bf16[512,512]{1,0:T(8,128)(2,1)S(1)}, bf16[512,512]{1,0:T(8,128)(2,1)S(1)}, bf16[512,512]{1,0:T(8,128)(2,1)S(1)}, bf16[512,512]{1,0:T(8,128)(2,1)S(1)}) custom-call(s32[6,6]{1,0:T(8,128)S(1)} %get-tuple-element.162.refs_0_.refs_5_, bf16[256,512]{1,0:T(8,128)(2,1)S(1)} %get-tuple-element.206.refs_1_, ...), custom_call_target="tpu_custom_call" | custom-call | flops 1342177280 | bytes 8960144 | tf_op jit(solution)/shard_map/back_local/pallas_call | solution.py:231
  41.9 2.3 %embed_back.1 = (bf16[512,512]{1,0:T(8,128)(2,1)S(1)}, bf16[256,512]{1,0:T(8,128)(2,1)S(1)}, bf16[288,512]{1,0:T(8,128)(2,1)S(1)}, bf16[16,512]{1,0:T(8,128)(2,1...) custom-call(bf16[8,512]{1,0:T(8,128)(2,1)S(1)} %collective-permute-d, ...), custom_call_target="tpu_custom_call" | custom-call | flops 805306368 | bytes 6130608 | tf_op jit(solution)/shard_map/embed_back/pallas_call | solution.py:231
  45.8 6.3 %collective-permute-done.23.refs_2_ = bf16[384,512]{1,0:T(8,128)(2,1)S(1)} collective-permute-done((bf16[384,512]{1,0:T(8,128)(2,1)S(1)}, bf16[384,512]{1,0:T(8,128)(2,1)S(1)}, u32[]{:S(2)}, u32[]{:S(2)}) %collective-permute-start.23) | collective-permute-done | bytes 393248 | tf_op jit(solution)/shard_map/ppermute | solution.py:162
  52.9 1.3 %collective-permute-start.26 = (bf16[192,512]{1,0:T(8,128)(2,1)S(1)}, bf16[192,512]{1,0:T(8,128)(2,1)S(1)}, u32[]{:S(2)}, u32[]{:S(2)}) collective-permute-start(bf16[192,512]{1,0:T(8,128)(2,1)S(1)} %get-tuple-element.266), channel_id=1, source_target_pairs={{0,4},{1,5},{2,6},{3,7},{4,0},{5,1},{6,2},{7,3},{8,12},{9,13},{10,... | collective-permute-start | bytes 589832 | tf_op jit(solution)/shard_map/ppermute | solution.py:162
  54.4 1.4 %collective-permute-start.28 = (bf16[256,512]{1,0:T(8,128)(2,1)S(1)}, bf16[256,512]{1,0:T(8,128)(2,1)S(1)}, u32[]{:S(2)}, u32[]{:S(2)}) collective-permute-start(bf16[256,512]{1,0:T(8,128)(2,1)S(1)} %get-tuple-element.272), channel_id=1, source_target_pairs={{0,2},{1,3},{2,0},{3,1},{4,6},{5,7},{6,4},{7,5},{8,10},{9,11},{10,... | collective-permute-start | bytes 786440 | tf_op jit(solution)/shard_map/ppermute | solution.py:162
  55.9 1.8 %collective-permute-done.25.refs_2_ = bf16[256,512]{1,0:T(8,128)(2,1)S(1)} collective-permute-done((bf16[256,512]{1,0:T(8,128)(2,1)S(1)}, bf16[256,512]{1,0:T(8,128)(2,1)S(1)}, u32[]{:S(2)}, u32[]{:S(2)}) %collective-permute-start.25) | collective-permute-done | bytes 262176 | tf_op jit(solution)/shard_map/ppermute | solution.py:162
  57.8 1.3 %collective-permute-start.27 = (bf16[128,512]{1,0:T(8,128)(2,1)S(1)}, bf16[128,512]{1,0:T(8,128)(2,1)S(1)}, u32[]{:S(2)}, u32[]{:S(2)}) collective-permute-start(bf16[128,512]{1,0:T(8,128)(2,1)S(1)} %get-tuple-element.269), channel_id=1, source_target_pairs={{0,4},{1,5},{2,6},{3,7},{4,0},{5,1},{6,2},{7,3},{8,12},{9,13},{10,... | collective-permute-start | bytes 393224 | tf_op jit(solution)/shard_map/ppermute | solution.py:162
  59.2 1.4 %collective-permute-start.31 = (bf16[160,512]{1,0:T(8,128)(2,1)S(1)}, bf16[160,512]{1,0:T(8,128)(2,1)S(1)}, u32[]{:S(2)}, u32[]{:S(2)}) collective-permute-start(bf16[160,512]{1,0:T(8,128)(2,1)S(1)} %get-tuple-element.278), channel_id=1, source_target_pairs={{0,2},{1,3},{2,0},{3,1},{4,6},{5,7},{6,4},{7,5},{8,10},{9,11},{10,... | collective-permute-start | bytes 491528 | tf_op jit(solution)/shard_map/ppermute | solution.py:162
  60.7 2.0 %collective-permute-start.29 = (bf16[96,512]{1,0:T(8,128)(2,1)S(1)}, bf16[96,512]{1,0:T(8,128)(2,1)S(1)}, u32[]{:S(2)}, u32[]{:S(2)}) collective-permute-start(bf16[96,512]{1,0:T(8,128)(2,1)S(1)} %get-tuple-element.274), channel_id=1, source_target_pairs={{0,8},{1,9},{2,10},{3,11},{4,12},{5,13},{6,14},{7,15},{8,0},{9,1},... | collective-permute-start | bytes 294920 | tf_op jit(solution)/shard_map/ppermute | solution.py:162
  63.0 3.4 %collective-permute-start.30 = (bf16[64,512]{1,0:T(8,128)(2,1)S(1)}, bf16[64,512]{1,0:T(8,128)(2,1)S(1)}, u32[]{:S(2)}, u32[]{:S(2)}) collective-permute-start(bf16[64,512]{1,0:T(8,128)(2,1)S(1)} %get-tuple-element.275), channel_id=1, source_target_pairs={{0,8},{1,9},{2,10},{3,11},{4,12},{5,13},{6,14},{7,15},{8,0},{9,1},... | collective-permute-start | bytes 196616 | tf_op jit(solution)/shard_map/ppermute | solution.py:162
  66.6 3.3 %collective-permute-done.30.arr0_ref = bf16[64,512]{1,0:T(8,128)(2,1)S(1)} collective-permute-done((bf16[64,512]{1,0:T(8,128)(2,1)S(1)}, bf16[64,512]{1,0:T(8,128)(2,1)S(1)}, u32[]{:S(2)}, u32[]{:S(2)}) %collective-permute-start.30) | collective-permute-done | bytes 65568 | tf_op jit(solution)/shard_map/ppermute | solution.py:162
  70.3 2.1 %collective-permute-done.32.refs_2_ = bf16[128,512]{1,0:T(8,128)(2,1)S(1)} collective-permute-done((bf16[128,512]{1,0:T(8,128)(2,1)S(1)}, bf16[128,512]{1,0:T(8,128)(2,1)S(1)}, u32[]{:S(2)}, u32[]{:S(2)}) %collective-permute-start.32) | collective-permute-done | bytes 131104 | tf_op jit(solution)/shard_map/ppermute | solution.py:162
  72.5 2.3 %collective-permute-done.33.refs_2_ = bf16[96,512]{1,0:T(8,128)(2,1)S(1)} collective-permute-done((bf16[96,512]{1,0:T(8,128)(2,1)S(1)}, bf16[96,512]{1,0:T(8,128)(2,1)S(1)}, u32[]{:S(2)}, u32[]{:S(2)}) %collective-permute-start.33) | collective-permute-done | bytes 98336 | tf_op jit(solution)/shard_map/ppermute | solution.py:162
  75.4 1.7 %collective-permute-start.34 = (bf16[48,512]{1,0:T(8,128)(2,1)S(1)}, bf16[48,512]{1,0:T(8,128)(2,1)S(1)}, u32[]{:S(2)}, u32[]{:S(2)}) collective-permute-start(bf16[48,512]{1,0:T(8,128)(2,1)S(1)} %get-tuple-element.288), channel_id=1, source_target_pairs={{0,8},{1,9},{2,10},{3,11},{4,12},{5,13},{6,14},{7,15},{8,0},{9,1},... | collective-permute-start | bytes 147464 | tf_op jit(solution)/shard_map/ppermute | solution.py:162
  78.3 2.5 %collective-permute-done.34.refs_0_.arr_e_ref = bf16[48,512]{1,0:T(8,128)(2,1)S(1)} collective-permute-done((bf16[48,512]{1,0:T(8,128)(2,1)S(1)}, bf16[48,512]{1,0:T(8,128)(2,1)S(1)}, u32[]{:S(2)}, u32[]{:S(2)}) %collective-permute-start.34) | collective-permute-done | bytes 49184 | tf_op jit(solution)/shard_map/ppermute | solution.py:162
  80.8 1.3 %grid_place.1 = bf16[512,512]{1,0:T(8,128)(2,1)} custom-call(bf16[48,512]{1,0:T(8,128)(2,1)S(1)} %collective-permute-done.34.refs_0_.arr_e_ref, bf16[16,512]{1,0:T(8,128)(2,1)S(1)} %get-tuple-element.289.refs_1_, bf16[16,512]{1,0:T(8,128)(2,1)S(1)} %get-tuple-element.290.refs_2_, bf16[16,512]{1,0:T(8,128)(2,1)S(1)} %get-tuple-element.291.refs_3_, ...), custom_call_target="tpu_custom_call" | custom-call | flops 402653184 | bytes 1687872 | tf_op jit(solution)/shard_map/grid_place/pallas_call | solution.py:231
  (83 shorter events, 26.2 us)
Async XLA Ops:
  3.9 8.0 %collective-permute-start = (bf16[16,512]{1,0:T(8,128)(2,1)S(1)}, bf16[16,512]{1,0:T(8,128)(2,1)S(1)}, u32[]{:S(2)}, u32[]{:S(2)}) collective-permute-start(bf16[16,512]{1,0:T(8,128)(2,1)S(1)} %get-tuple-element.163), channel_id=1, source_target_pairs={{0,12},{4,8},{8,4},{12,0},{1,13},{5,9},{9,5},{13,1},{2,14},{6,10},... | collective-permute-start | bytes 49160 | tf_op jit(solution)/shard_map/ppermute | solution.py:247
  14.5 5.8 %collective-permute-start.5 = (bf16[32,512]{1,0:T(8,128)(2,1)S(1)}, bf16[32,512]{1,0:T(8,128)(2,1)S(1)}, u32[]{:S(2)}, u32[]{:S(2)}) collective-permute-start(bf16[32,512]{1,0:T(8,128)(2,1)S(1)} %get-tuple-element.175), channel_id=1, source_target_pairs={{0,12},{4,8},{8,4},{12,0},{1,13},{5,9},{9,5},{13,1},{2,14},{6,10},... | collective-permute-start | bytes 98312 | tf_op jit(solution)/shard_map/ppermute | solution.py:247
  15.6 4.7 %collective-permute-start.6 = (bf16[32,512]{1,0:T(8,128)(2,1)S(1)}, bf16[32,512]{1,0:T(8,128)(2,1)S(1)}, u32[]{:S(2)}, u32[]{:S(2)}) collective-permute-start(bf16[32,512]{1,0:T(8,128)(2,1)S(1)} %get-tuple-element.176), channel_id=1, source_target_pairs={{0,4},{4,0},{8,12},{12,8},{1,5},{5,1},{9,13},{13,9},{2,6},{6,2},{1... | collective-permute-start | bytes 98312 | tf_op jit(solution)/shard_map/ppermute | solution.py:248
  21.4 8.1 %collective-permute-start.10 = (bf16[16,512]{1,0:T(8,128)(2,1)S(1)}, bf16[16,512]{1,0:T(8,128)(2,1)S(1)}, u32[]{:S(2)}, u32[]{:S(2)}) collective-permute-start(bf16[16,512]{1,0:T(8,128)(2,1)S(1)} %get-tuple-element.185), channel_id=1, source_target_pairs={{0,12},{4,8},{8,4},{12,0},{1,13},{5,9},{9,5},{13,1},{2,14},{6,10},... | collective-permute-start | bytes 49160 | tf_op jit(solution)/shard_map/ppermute | solution.py:247
  24.1 5.4 %collective-permute-start.11 = (bf16[16,512]{1,0:T(8,128)(2,1)S(1)}, bf16[16,512]{1,0:T(8,128)(2,1)S(1)}, u32[]{:S(2)}, u32[]{:S(2)}) collective-permute-start(bf16[16,512]{1,0:T(8,128)(2,1)S(1)} %get-tuple-element.186), channel_id=1, source_target_pairs={{0,4},{4,0},{8,12},{12,8},{1,5},{5,1},{9,13},{13,9},{2,6},{6,2},{1... | collective-permute-start | bytes 49160 | tf_op jit(solution)/shard_map/ppermute | solution.py:248
  24.7 4.9 %collective-permute-start.12 = (bf16[16,512]{1,0:T(8,128)(2,1)S(1)}, bf16[16,512]{1,0:T(8,128)(2,1)S(1)}, u32[]{:S(2)}, u32[]{:S(2)}) collective-permute-start(bf16[16,512]{1,0:T(8,128)(2,1)S(1)} %get-tuple-element.187), channel_id=1, source_target_pairs={{0,3},{1,2},{2,1},{3,0},{4,7},{5,6},{6,5},{7,4},{8,11},{9,10},{10,... | collective-permute-start | bytes 49160 | tf_op jit(solution)/shard_map/ppermute | solution.py:250
  25.1 4.4 %collective-permute-start.13 = (bf16[16,512]{1,0:T(8,128)(2,1)S(1)}, bf16[16,512]{1,0:T(8,128)(2,1)S(1)}, u32[]{:S(2)}, u32[]{:S(2)}) collective-permute-start(bf16[16,512]{1,0:T(8,128)(2,1)S(1)} %get-tuple-element.188), channel_id=1, source_target_pairs={{0,2},{1,3},{2,0},{3,1},{4,6},{5,7},{6,4},{7,5},{8,10},{9,11},{10,... | collective-permute-start | bytes 49160 | tf_op jit(solution)/shard_map/ppermute | solution.py:250
  33.0 6.3 %collective-permute-start.17 = (bf16[8,512]{1,0:T(8,128)(2,1)S(1)}, bf16[8,512]{1,0:T(8,128)(2,1)S(1)}, u32[]{:S(2)}, u32[]{:S(2)}) collective-permute-start(bf16[8,512]{1,0:T(8,128)(2,1)S(1)} %get-tuple-element.223), channel_id=1, source_target_pairs={{0,12},{4,8},{8,4},{12,0},{1,13},{5,9},{9,5},{13,1},{2,14},{6,10},... | collective-permute-start | bytes 24584 | tf_op jit(solution)/shard_map/ppermute | solution.py:247
  34.0 5.4 %collective-permute-start.18 = (bf16[8,512]{1,0:T(8,128)(2,1)S(1)}, bf16[8,512]{1,0:T(8,128)(2,1)S(1)}, u32[]{:S(2)}, u32[]{:S(2)}) collective-permute-start(bf16[8,512]{1,0:T(8,128)(2,1)S(1)} %get-tuple-element.224), channel_id=1, source_target_pairs={{0,4},{4,0},{8,12},{12,8},{1,5},{5,1},{9,13},{13,9},{2,6},{6,2},{1... | collective-permute-start | bytes 24584 | tf_op jit(solution)/shard_map/ppermute | solution.py:248
  34.8 4.5 %collective-permute-start.19 = (bf16[8,512]{1,0:T(8,128)(2,1)S(1)}, bf16[8,512]{1,0:T(8,128)(2,1)S(1)}, u32[]{:S(2)}, u32[]{:S(2)}) collective-permute-start(bf16[8,512]{1,0:T(8,128)(2,1)S(1)} %get-tuple-element.225), channel_id=1, source_target_pairs={{0,3},{1,2},{2,1},{3,0},{4,7},{5,6},{6,5},{7,4},{8,11},{9,10},{10,... | collective-permute-start | bytes 24584 | tf_op jit(solution)/shard_map/ppermute | solution.py:250
  40.1 14.1 %collective-permute-start.24 = (bf16[512,512]{1,0:T(8,128)(2,1)S(1)}, bf16[512,512]{1,0:T(8,128)(2,1)S(1)}, u32[]{:S(2)}, u32[]{:S(2)}) collective-permute-start(bf16[512,512]{1,0:T(8,128)(2,1)S(1)} %get-tuple-element.257), channel_id=1, source_target_pairs={{0,1},{1,0},{2,3},{3,2},{4,5},{5,4},{6,7},{7,6},{8,9},{9,8},{10,11... | collective-permute-start | bytes 1572872 | tf_op jit(solution)/shard_map/ppermute | solution.py:162
  40.1 11.9 %collective-permute-start.23 = (bf16[384,512]{1,0:T(8,128)(2,1)S(1)}, bf16[384,512]{1,0:T(8,128)(2,1)S(1)}, u32[]{:S(2)}, u32[]{:S(2)}) collective-permute-start(bf16[384,512]{1,0:T(8,128)(2,1)S(1)} %get-tuple-element.247), channel_id=1, source_target_pairs={{0,2},{1,3},{2,0},{3,1},{4,6},{5,7},{6,4},{7,5},{8,10},{9,11},{10,... | collective-permute-start | bytes 1179656 | tf_op jit(solution)/shard_map/ppermute | solution.py:162
  44.2 7.9 %collective-permute-start.22 = (bf16[288,512]{1,0:T(8,128)(2,1)S(1)}, bf16[288,512]{1,0:T(8,128)(2,1)S(1)}, u32[]{:S(2)}, u32[]{:S(2)}) collective-permute-start(bf16[288,512]{1,0:T(8,128)(2,1)S(1)} %get-tuple-element.246), channel_id=1, source_target_pairs={{0,1},{1,0},{2,3},{3,2},{4,5},{5,4},{6,7},{7,6},{8,9},{9,8},{10,11... | collective-permute-start | bytes 884744 | tf_op jit(solution)/shard_map/ppermute | solution.py:162
  44.6 13.1 %collective-permute-start.25 = (bf16[256,512]{1,0:T(8,128)(2,1)S(1)}, bf16[256,512]{1,0:T(8,128)(2,1)S(1)}, u32[]{:S(2)}, u32[]{:S(2)}) collective-permute-start(bf16[256,512]{1,0:T(8,128)(2,1)S(1)} %get-tuple-element.262), channel_id=1, source_target_pairs={{0,2},{1,3},{2,0},{3,1},{4,6},{5,7},{6,4},{7,5},{8,10},{9,11},{10,... | collective-permute-start | bytes 786440 | tf_op jit(solution)/shard_map/ppermute | solution.py:162
  52.9 7.7 %collective-permute-start.26 = (bf16[192,512]{1,0:T(8,128)(2,1)S(1)}, bf16[192,512]{1,0:T(8,128)(2,1)S(1)}, u32[]{:S(2)}, u32[]{:S(2)}) collective-permute-start(bf16[192,512]{1,0:T(8,128)(2,1)S(1)} %get-tuple-element.266), channel_id=1, source_target_pairs={{0,4},{1,5},{2,6},{3,7},{4,0},{5,1},{6,2},{7,3},{8,12},{9,13},{10,... | collective-permute-start | bytes 589832 | tf_op jit(solution)/shard_map/ppermute | solution.py:162
  54.4 11.9 %collective-permute-start.28 = (bf16[256,512]{1,0:T(8,128)(2,1)S(1)}, bf16[256,512]{1,0:T(8,128)(2,1)S(1)}, u32[]{:S(2)}, u32[]{:S(2)}) collective-permute-start(bf16[256,512]{1,0:T(8,128)(2,1)S(1)} %get-tuple-element.272), channel_id=1, source_target_pairs={{0,2},{1,3},{2,0},{3,1},{4,6},{5,7},{6,4},{7,5},{8,10},{9,11},{10,... | collective-permute-start | bytes 786440 | tf_op jit(solution)/shard_map/ppermute | solution.py:162
  57.8 5.0 %collective-permute-start.27 = (bf16[128,512]{1,0:T(8,128)(2,1)S(1)}, bf16[128,512]{1,0:T(8,128)(2,1)S(1)}, u32[]{:S(2)}, u32[]{:S(2)}) collective-permute-start(bf16[128,512]{1,0:T(8,128)(2,1)S(1)} %get-tuple-element.269), channel_id=1, source_target_pairs={{0,4},{1,5},{2,6},{3,7},{4,0},{5,1},{6,2},{7,3},{8,12},{9,13},{10,... | collective-permute-start | bytes 393224 | tf_op jit(solution)/shard_map/ppermute | solution.py:162
  59.2 10.8 %collective-permute-start.31 = (bf16[160,512]{1,0:T(8,128)(2,1)S(1)}, bf16[160,512]{1,0:T(8,128)(2,1)S(1)}, u32[]{:S(2)}, u32[]{:S(2)}) collective-permute-start(bf16[160,512]{1,0:T(8,128)(2,1)S(1)} %get-tuple-element.278), channel_id=1, source_target_pairs={{0,2},{1,3},{2,0},{3,1},{4,6},{5,7},{6,4},{7,5},{8,10},{9,11},{10,... | collective-permute-start | bytes 491528 | tf_op jit(solution)/shard_map/ppermute | solution.py:162
  60.7 9.3 %collective-permute-start.29 = (bf16[96,512]{1,0:T(8,128)(2,1)S(1)}, bf16[96,512]{1,0:T(8,128)(2,1)S(1)}, u32[]{:S(2)}, u32[]{:S(2)}) collective-permute-start(bf16[96,512]{1,0:T(8,128)(2,1)S(1)} %get-tuple-element.274), channel_id=1, source_target_pairs={{0,8},{1,9},{2,10},{3,11},{4,12},{5,13},{6,14},{7,15},{8,0},{9,1},... | collective-permute-start | bytes 294920 | tf_op jit(solution)/shard_map/ppermute | solution.py:162
  63.0 6.9 %collective-permute-start.30 = (bf16[64,512]{1,0:T(8,128)(2,1)S(1)}, bf16[64,512]{1,0:T(8,128)(2,1)S(1)}, u32[]{:S(2)}, u32[]{:S(2)}) collective-permute-start(bf16[64,512]{1,0:T(8,128)(2,1)S(1)} %get-tuple-element.275), channel_id=1, source_target_pairs={{0,8},{1,9},{2,10},{3,11},{4,12},{5,13},{6,14},{7,15},{8,0},{9,1},... | collective-permute-start | bytes 196616 | tf_op jit(solution)/shard_map/ppermute | solution.py:162
  66.5 5.8 %collective-permute-start.32 = (bf16[128,512]{1,0:T(8,128)(2,1)S(1)}, bf16[128,512]{1,0:T(8,128)(2,1)S(1)}, u32[]{:S(2)}, u32[]{:S(2)}) collective-permute-start(bf16[128,512]{1,0:T(8,128)(2,1)S(1)} %get-tuple-element.284), channel_id=1, source_target_pairs={{0,4},{1,5},{2,6},{3,7},{4,0},{5,1},{6,2},{7,3},{8,12},{9,13},{10,... | collective-permute-start | bytes 393224 | tf_op jit(solution)/shard_map/ppermute | solution.py:162
  70.1 4.7 %collective-permute-start.33 = (bf16[96,512]{1,0:T(8,128)(2,1)S(1)}, bf16[96,512]{1,0:T(8,128)(2,1)S(1)}, u32[]{:S(2)}, u32[]{:S(2)}) collective-permute-start(bf16[96,512]{1,0:T(8,128)(2,1)S(1)} %get-tuple-element.287), channel_id=1, source_target_pairs={{0,4},{1,5},{2,6},{3,7},{4,0},{5,1},{6,2},{7,3},{8,12},{9,13},{10,... | collective-permute-start | bytes 294920 | tf_op jit(solution)/shard_map/ppermute | solution.py:162
  75.4 5.4 %collective-permute-start.34 = (bf16[48,512]{1,0:T(8,128)(2,1)S(1)}, bf16[48,512]{1,0:T(8,128)(2,1)S(1)}, u32[]{:S(2)}, u32[]{:S(2)}) collective-permute-start(bf16[48,512]{1,0:T(8,128)(2,1)S(1)} %get-tuple-element.288), channel_id=1, source_target_pairs={{0,8},{1,9},{2,10},{3,11},{4,12},{5,13},{6,14},{7,15},{8,0},{9,1},... | collective-permute-start | bytes 147464 | tf_op jit(solution)/shard_map/ppermute | solution.py:162
  77.1 5.2 %collective-permute-start.35 = (bf16[64,512]{1,0:T(8,128)(2,1)S(1)}, bf16[64,512]{1,0:T(8,128)(2,1)S(1)}, u32[]{:S(2)}, u32[]{:S(2)}) collective-permute-start(bf16[64,512]{1,0:T(8,128)(2,1)S(1)} %get-tuple-element.300), channel_id=1, source_target_pairs={{0,8},{1,9},{2,10},{3,11},{4,12},{5,13},{6,14},{7,15},{8,0},{9,1},... | collective-permute-start | bytes 196616 | tf_op jit(solution)/shard_map/ppermute | solution.py:162
  (15 other events, 60.9 us)

commit v13 on v12

--- a/solution.py
+++ b/solution.py
@@ -340,7 +340,7 @@
     back = low(receivers(senders_t_ref[...], halo))
     store_parts(
         pay_refs,
-        [dot(border, state), dot(back, state), dot(border, merged), dot(back, cot_ref[...])],
+        [dot(border, state), dot(back, state), dot(back, cot_ref[...])],
     )
 
 
@@ -385,16 +385,12 @@
 def forward_halo(peers, *refs):
     arr_refs, refs = refs[:peers][::-1], refs[peers:]
     (recv_n_ref, total_ref, state_ref, send_ref, update_ref, senders_ref, senders_t_ref,
-     bounds_ref, summed_ref, out_ref, pre_ref, rows_ref, back_ref, merged_ref, cot_ref,
-     *pay_refs) = refs
+     bounds_ref, summed_ref, out_ref, pre_ref, back_ref, cot_ref, *pay_refs) = refs
     nodes = state_ref.shape[0]
     degree = senders_t_ref.shape[0]
     halo = peers * BORDER
-    rows, back, merged, cot = split_parts(
-        arr_refs, (0, BORDER, 2 * BORDER, 3 * BORDER), (BORDER,) * 4
-    )
-    rows_ref[...], back_ref[...] = low(rows), low(back)
-    merged_ref[...], cot_ref[...] = low(merged), low(cot)
+    rows, back, cot = split_parts(arr_refs, (0, BORDER, 2 * BORDER), (BORDER,) * 3)
+    back_ref[...], cot_ref[...] = low(back), low(cot)
     pre = low(dot(low(rows), send_ref[0])).astype(F32) + recv_n_ref[...]
     pre_ref[...] = pre
     place = low(receivers_t(senders_ref[...], degree, halo))
@@ -412,12 +408,10 @@
     state_ref, send_ref, recv_ref, update_ref, cot_ref, cot_r_ref, pre_ref, recv_n0_ref, back0_ref,
     sent_b0_ref, senders_ref, senders_t_ref, bounds_ref,
     total_ref, grecv_ref, gsent_ref, recv_n_ref, sent_b_ref, gsum_n_ref, gsum_r_ref,
-    slope_k_ref, slope_d_ref, slope_r_ref, gpre_ref,
+    slope_d_ref, slope_r_ref, gpre_ref,
 ):
     halo = bounds_ref.shape[0]
-    slope = silu_slope(pre_ref[...])
-    slope_k_ref[...] = low(slope)
-    slope_d_ref[...] = low(slope - silu_slope(recv_n0_ref[...]))
+    slope_d_ref[...] = low(silu_slope(pre_ref[...]) - silu_slope(recv_n0_ref[...]))
     pre = sent_b0_ref[...].astype(F32) + dot(back0_ref[...], recv_ref[0])
     slope_r_ref[...] = low(silu_slope(pre))
     state = state_ref[...]
@@ -481,75 +475,60 @@
     def store(at, value):
         store_blocks(keep_ref, give_ref, at, 3, value, dims, place_ref)
 
-    store(0, dot(state, gsent_ref[...], TN))
-    store(1, dot(state, grecv_ref[...], TN))
+    both = dot(state, jnp.concatenate([gsent_ref[...], grecv_ref[...]], axis=1), TN)
+    store(0, both[:, : state.shape[1]])
+    store(1, both[:, state.shape[1] :])
     store(2, dot(summed, cot_ref[...], TN))
     mesh_ref[...] = low(state.astype(F32) + dot(summed, update_ref[1]))
 
 
-def back_local(
-    dims, place_ref, gin_ref, slope_ref, slope_k_ref, slope_d_ref, send_ref, recv_ref, update_ref,
-    senders_ref, senders_t_ref, state_ref, rows_ref, summed_ref, merged_ref, merged_r_ref,
-    after_ref, part_ref, keep_ref, give_ref, keep2_ref, give2_ref, gpre_ref,
-):
+def first_layer_back(peers, dims, carry, *refs):
+    arr_refs, refs = refs[:peers][::-1], refs[peers:]
+    (place_ref, gin_ref, slope_ref, slope_d_ref, slope_r_ref, send_ref, recv_ref, update_ref,
+     merge_ref, embed_ref, senders_ref, senders_t_ref, bounds_ref, target_ref, sends_ref,
+     incoming_ref, state_ref, summed_ref, merged_ref, slope_g_ref, slope_a_ref, grid_ref, lat_ref,
+     _, gpre_g_ref, keep_ref, give_ref, keep2_ref, give2_ref, *pay_refs, gpre_ref) = refs
     nodes = gin_ref.shape[0]
-    halo = slope_k_ref.shape[0]
+    halo = peers * BORDER
     degree = senders_t_ref.shape[0]
+    chosen = grid_ref.shape[0]
+    taken = sends_ref.shape[0]
     gin = gin_ref[...]
     gsum = low(dot(gin, update_ref[0], NT))
+    back = low(receivers(senders_t_ref[...], halo))
     place = low(receivers_t(senders_ref[...], degree, halo))
-    back = low(receivers(senders_t_ref[...], halo))
-    gsum_n = low(dot(back, gsum))
-    gpre_k = gsum_n * slope_k_ref[...]
-    grecv = dot(place, gsum_n * slope_d_ref[...])
+    grecv = dot(place, low(dot(back, gsum)) * slope_d_ref[...])
     for j in range(degree):
         gpre = gsum * slope_ref[j]
         grecv = grecv + gpre.astype(F32)
         gpre_ref[j * nodes : (j + 1) * nodes, :] = gpre
+    grecv = low(grecv)
+    (arrived,) = split_parts(arr_refs, (0,), (BORDER,))
+    gsum_r = low(dot(low(arrived), update_ref[0], NT))
+    border = low(hot(bounds_ref[...] == iota(nodes, halo, 0)))
     gsent = dot(edge_targets(senders_t_ref[...]), gpre_ref[...])
-    grecv, gsent = low(grecv), low(gsent)
-    part = gin.astype(F32) + dot(grecv, recv_ref[0], NT) + dot(gsent, send_ref[0], NT)
-    part_ref[...] = part
-    state = state_ref[...]
-
-    def store(at, value):
-        store_blocks(keep_ref, give_ref, at, 2, value, dims, place_ref)
-
-    def store2(at, value):
-        store_blocks(keep2_ref, give2_ref, at, 2, value, dims, place_ref)
-
-    store(0, dot(state, gsent, TN) + dot(rows_ref[...], gpre_k, TN))
-    store(1, dot(state, grecv, TN))
-    store2(0, dot(summed_ref[...], gin, TN))
-    far = low(dot(gpre_k, send_ref[0], NT))
-    store2(1, dot(merged_ref[...], low(part), TN) + dot(merged_r_ref[...], far, TN))
-
-
-def embed_back(peers, dims, carry, *refs):
-    arr_refs, refs = refs[:peers][::-1], refs[peers:]
-    (place_ref, slope_r_ref, part_ref, update_ref, send_ref, merge_ref, bounds_ref, target_ref,
-     sends_ref, incoming_ref, slope_g_ref, slope_a_ref, grid_ref, lat_ref, embed_ref,
-     gpre_ref, keep_ref, give_ref, *pay_refs) = refs
-    nodes = part_ref.shape[0]
-    halo = peers * BORDER
-    chosen = grid_ref.shape[0]
-    taken = sends_ref.shape[0]
-    (arrived,) = split_parts(arr_refs, (0,), (BORDER,))
-    gsum = low(dot(low(arrived), update_ref[0], NT)).astype(F32)
-    gpre = low(gsum * slope_r_ref[...].astype(F32))
-    border = low(hot(bounds_ref[...] == iota(nodes, halo, 0)))
-    gsent = low(dot(border, gpre))
-    gin = low(part_ref[...] + dot(gsent, send_ref[0], NT))
-    gmerged = low(dot(gin, merge_ref[...], NT))
+    gsent = low(gsent + dot(border, gsum_r * slope_r_ref[...]))
+    gin0 = gin.astype(F32) + dot(grecv, recv_ref[0], NT) + dot(gsent, send_ref[0], NT)
+    gin0 = low(gin0)
+    gmerged = low(dot(gin0, merge_ref[...], NT))
     place = low(hot(incoming_ref[...] == iota(nodes, taken, 0)))
     gpre_a = low(dot(place, gmerged, TN) * slope_a_ref[...].astype(F32))
     sent = jnp.max(hot(sends_ref[...] == iota(taken, chosen, 1)), axis=0, keepdims=True)
     label = jnp.where(sent > 0.0, nodes, target_ref[...])
     pick = low(hot(label == iota(nodes, chosen, 0)))
     gpre_g = low(dot(pick, gmerged, TN) * slope_g_ref[...].astype(F32))
-    gpre_ref[...] = gpre_g
-    grad = dot(grid_ref[...], gpre_g, TN) + dot(lat_ref[...], gpre_a, TN)
-    store_blocks(keep_ref, give_ref, 0, 1, grad, dims, place_ref)
+    gpre_g_ref[...] = gpre_g
+    state = state_ref[...]
+
+    def store(at, value):
+        store_blocks(keep_ref, give_ref, at, 3, value, dims, place_ref)
+
+    store(0, dot(grid_ref[...], gpre_g, TN) + dot(lat_ref[...], gpre_a, TN))
+    both = dot(state, jnp.concatenate([gsent, grecv], axis=1), TN)
+    store(1, both[:, : state.shape[1]])
+    store(2, both[:, state.shape[1] :])
+    store_blocks(keep2_ref, give2_ref, 0, 2, dot(summed_ref[...], gin, TN), dims, place_ref)
+    store_blocks(keep2_ref, give2_ref, 1, 2, dot(merged_ref[...], gin0, TN), dims, place_ref)
     rows = dot(gpre_a, embed_ref[...], NT)
     store_parts(pay_refs, [rows])
     if carry:
@@ -574,18 +553,18 @@
 
 
 def finish(
-    keep1_ref, arr1_ref, keep0_ref, arr0_ref, keep2_ref, arr2_ref, keep_e_ref, arr_e_ref,
+    keep1_ref, arr1_ref, keep0_ref, arr0_ref, keep2_ref, arr2_ref,
     embed_ref, merge_ref, send_ref, recv_ref, update_ref,
 ):
+    depth = embed_ref.shape[0]
     last = keep1_ref[...].astype(F32) + arr1_ref[...].astype(F32)
-    first = keep0_ref[...].astype(F32) + arr0_ref[...].astype(F32)
+    first = keep0_ref[...].astype(F32) + arr0_ref[: 3 * depth, :].astype(F32)
     second = keep2_ref[...].astype(F32) + arr2_ref[...].astype(F32)
-    depth = embed_ref.shape[0]
-    embed_ref[...] = keep_e_ref[...].astype(F32) + arr_e_ref[:depth, :].astype(F32)
     for at, ref in enumerate((send_ref, recv_ref, update_ref)):
         ref[1] = last[at * depth : (at + 1) * depth]
-    send_ref[0], recv_ref[0], update_ref[0] = first[:depth], first[depth:], second[:depth]
-    merge_ref[...] = second[depth:]
+    embed_ref[...] = first[:depth]
+    send_ref[0], recv_ref[0] = first[depth : 2 * depth], first[2 * depth :]
+    update_ref[0], merge_ref[...] = second[:depth], second[depth:]
 
 
 def body(
@@ -629,7 +608,7 @@
     merged, state0, slope_a, lat_a, *pay2 = call(
         lambda *refs: merge_nodes(peers, *refs), "merge_nodes",
         [shape(nodes, width), shape(nodes, width), shape(taken, width), shape(taken, width)]
-        + [shape(4 * BORDER, width)] * peers,
+        + [shape(3 * BORDER, width)] * peers,
         (*arr1, incoming, embed, local, mesh, merge, bounds, senders_t, cot),
         flops=2 * unit,
     )
@@ -640,19 +619,18 @@
          shape(halo, width, dtype=F32), shape(halo, width)],
         (state0, send_weight, recv_weight, senders, senders_t, bounds), flops=6 * unit,
     )
-    summed0, state1, pre0, rows0, back0, merged_r, cot_r, *pay3 = call(
+    summed0, state1, pre0, back0, cot_r, *pay3 = call(
         lambda *refs: forward_halo(peers, *refs), "forward_halo",
         [shape(nodes, width), shape(nodes, width), shape(halo, width, dtype=F32)]
-        + [shape(halo, width)] * 4 + [shape(2 * BORDER, width)] * peers,
+        + [shape(halo, width)] * 2 + [shape(2 * BORDER, width)] * peers,
         (*arr2, recv_n0, total0, state0, send_weight, update_weight, senders, senders_t, bounds),
         flops=2 * unit,
     )
     arr3 = exchange(pay3, dims)
-    (total1, grecv_l, gsent_l, recv_n1, sent_b1, gsum_n1, gsum_r1, slope_k0, slope_d0,
-     slope_r0) = call(
+    (total1, grecv_l, gsent_l, recv_n1, sent_b1, gsum_n1, gsum_r1, slope_d0, slope_r0) = call(
         turn_local, "turn_local",
         [shape(nodes, width, dtype=F32)] * 3 + [shape(halo, width, dtype=F32)]
-        + [shape(halo, width)] * 6,
+        + [shape(halo, width)] * 5,
         (state1, send_weight, recv_weight, update_weight, cot, cot_r, pre0, recv_n0, back0,
          sent_b0, senders, senders_t, bounds),
         flops=10 * unit, scratch=[pltpu.VMEM((degree * nodes, width), BF)],
@@ -672,88 +650,71 @@
     )
     split = fine(width, dims)
     if split:
-        give1, last = lax.optimization_barrier((give1, arr4[-1]))
-        arr4 = (*arr4[:-1], last)
-        keep1, give1 = halve_step(1, keep1, swap(give1, 0, dims), place)
-    part0, keep0, give0, keep2, give2 = call(
-        lambda *refs: back_local(dims, *refs), "back_local",
-        [shape(nodes, width, dtype=F32)] + blocks_shapes(2, width, width, dims) * 2,
-        (place, gin1, slope0, slope_k0, slope_d0, send_weight, recv_weight, update_weight, senders,
-         senders_t, state0, rows0, summed0, merged, merged_r, keep1),
-        flops=10 * unit, scratch=[pltpu.VMEM((degree * nodes, width), BF)],
-    )
-    if split:
-        give0, give2, *arr4 = lax.optimization_barrier((give0, give2, *arr4))
-        keep0, give0 = halve_step(1, keep0, swap(give0, 0, dims), place)
-        keep0, *arr4 = lax.optimization_barrier((keep0, *arr4))
-    shapes = blocks_shapes(1, width, width, dims)
+        give1, *arr4 = lax.optimization_barrier((give1, *arr4))
+    shapes = blocks_shapes(3, width, width, dims)
     if carry:
         shapes[1] = shape(shapes[1].shape[0] + 2 * capacity, width)
-    gpre_g, keep_e, give_e, *pay5 = call(
-        lambda *refs: embed_back(peers, dims, carry, *refs), "embed_back",
-        [shape(chosen, width)] + shapes + [shape(capacity, width)] * peers,
-        (*arr4, place, slope_r0, part0, update_weight, send_weight, merge, bounds_row,
-         targets, sends, incoming, slope_g, slope_a, grid, lat_a, embed),
-        flops=6 * unit,
+    gpre_g, keep0, give0, keep2, give2, *pay5 = call(
+        lambda *refs: first_layer_back(peers, dims, carry, *refs), "first_layer_back",
+        [shape(chosen, width)] + shapes + blocks_shapes(2, width, width, dims)
+        + [shape(capacity, width)] * peers,
+        (*arr4, place, gin1, slope0, slope_d0, slope_r0, send_weight, recv_weight, update_weight,
+         merge, embed, senders, senders_t, bounds_row, targets, sends, incoming, state0, summed0,
+         merged, slope_g, slope_a, grid, lat_a, give1),
+        flops=16 * unit, scratch=[pltpu.VMEM((degree * nodes, width), BF)],
     )
     depth = width // total
     if not split:
         arr5 = exchange(pay5, dims)
-        last, first, second, embed_sum = (
-            scatter_plain(blocks, dims) for blocks in (keep1, keep0, keep2, keep_e)
-        )
-        grads = [jnp.stack([a, last[i]]) for i, a in enumerate((first[0], first[1], second[0]))]
-        grads = [embed_sum[0], second[1], *grads]
+        last, first, second = (scatter_plain(blocks, dims) for blocks in (keep1, keep0, keep2))
+        grads = [jnp.stack([a, last[i]]) for i, a in enumerate((first[1], first[2], second[0]))]
+        grads = [first[0], second[1], *grads]
     elif not carry:
         arr5 = exchange(pay5, dims)
         sums = [
-            rest_of_halving(1, keep1, give1, place, dims),
-            rest_of_halving(1, keep0, give0, place, dims),
+            rest_of_halving(0, keep1, give1, place, dims),
+            rest_of_halving(0, keep0, give0, place, dims),
             rest_of_halving(0, keep2, give2, place, dims),
-            rest_of_halving(0, keep_e, give_e, place, dims),
         ]
     else:
+        arr1, keep0 = lax.optimization_barrier((swap(give1, 0, dims), keep0))
+        keep1, give1 = halve_step(1, keep1, arr1, place)
         arr1 = swap(give1, 1, dims)
+        give0, give2, keep1 = lax.optimization_barrier((give0, give2, keep1))
+        arr0 = swap(give0, 0, dims)
+        arr2 = swap(give2, 0, dims)
+        keep0, give0, from_sub, _ = carry_step(1, keep0, arr0, pay5[1:2], place, capacity)
         arr0 = swap(give0, 1, dims)
-        arr2 = swap(give2, 0, dims)
-        arr_e, arr1 = lax.optimization_barrier((swap(give_e, 0, dims), arr1))
+        keep2, keep0 = lax.optimization_barrier((keep2, keep0))
+        keep2, give2 = halve_step(1, keep2, arr2, place)
+        arr2 = swap(give2, 1, dims)
+        keep1, keep2 = lax.optimization_barrier((keep1, keep2))
         keep1, give1 = halve_step(2, keep1, arr1, place)
         arr1 = swap(give1, 2, dims)
-        keep_e, keep1 = lax.optimization_barrier((keep_e, keep1))
-        keep_e, give_e, from_sub, _ = carry_step(1, keep_e, arr_e, pay5[1:2], place, capacity)
-        arr_e = swap(give_e, 1, dims)
-        keep2, keep_e = lax.optimization_barrier((keep2, keep_e))
-        keep2, give2 = halve_step(1, keep2, arr2, place)
-        arr2 = swap(give2, 1, dims)
-        keep0, keep2 = lax.optimization_barrier((keep0, keep2))
-        keep0, give0 = halve_step(2, keep0, arr0, place)
-        arr0 = swap(give0, 2, dims)
-        keep1, keep0 = lax.optimization_barrier((keep1, keep0))
         keep1, give1 = halve_step(3, keep1, arr1, place)
         arr1 = swap(give1, 3, dims)
         keep0, keep1 = lax.optimization_barrier((keep0, keep1))
-        keep0, give0 = halve_step(3, keep0, arr0, place)
-        arr0 = swap(give0, 3, dims)
+        keep0, give0, from_lat, from_diag = carry_step(
+            2, keep0, arr0, pay5[3:], place, capacity
+        )
+        arr0 = swap(give0, 2, dims)
         keep2, keep0 = lax.optimization_barrier((keep2, keep0))
         keep2, give2 = halve_step(2, keep2, arr2, place)
         arr2 = swap(give2, 2, dims)
-        keep_e, keep2, arr1, arr0 = lax.optimization_barrier((keep_e, keep2, arr1, arr0))
-        keep_e, give_e, from_lat, from_diag = carry_step(
-            2, keep_e, arr_e, pay5[3:], place, capacity
-        )
-        arr_e = swap(give_e, 2, dims)
-        keep2, keep_e = lax.optimization_barrier((keep2, keep_e))
+        keep0, keep2, arr1 = lax.optimization_barrier((keep0, keep2, arr1))
+        keep0, give0, from_near, _ = carry_step(3, keep0, arr0, (), place, capacity)
+        arr0 = swap(give0, 3, dims)
+        keep2, keep0 = lax.optimization_barrier((keep2, keep0))
         keep2, give2 = halve_step(3, keep2, arr2, place)
         arr2 = swap(give2, 3, dims)
-        keep_e, keep2 = lax.optimization_barrier((keep_e, keep2))
-        keep_e, give_e, from_near, _ = carry_step(3, keep_e, arr_e, (), place, capacity)
-        arr_e = swap(give_e, 3, dims)
-        arr5 = (arr_e, from_near, from_diag, from_lat, from_sub)
-        sums = ((keep1, arr1), (keep0, arr0), (keep2, arr2), (keep_e, arr_e))
+        arr5 = (arr0, from_near, from_diag, from_lat, from_sub)
     (grid_grad,) = call(
         lambda *refs: grid_place(peers, *refs), "grid_place", [shape(chosen, width)],
         (*arr5, gpre_g, embed, sends_row), flops=3 * unit,
     )
+    if carry:
+        keep2, grid_grad = lax.optimization_barrier((keep2, grid_grad))
+        sums = ((keep1, arr1), (keep0, arr0), (keep2, arr2))
     if split:
         grads = call(
             finish, "finish",

time: 83.3 us -> 84.9 us (1.019)
  waiting for transfers between devices: 20.9 us -> 28.1 us
  starting transfers between devices: 36.8 us -> 32.6 us
  Pallas kernels: 22.8 us -> 21.3 us
    ppermute x16 -> x12, waiting for transfers between devices: 18.8 us -> 25.4 us  [swap(): return lax.ppermute(block, GROUP, [(i, i ^ 1 << bit) for i in range(total)])]
    ppermute x16 -> x12, starting transfers between devices: 18 us -> 13.3 us  [swap(): return lax.ppermute(block, GROUP, [(i, i ^ 1 << bit) for i in range(total)])]
    pallas_call x24 -> x20, Pallas kernels: 22.8 us -> 21.3 us  [call(): pl.pallas_call(kernel, out_shape=[shape(*a.shape, dtype=a.dtype) for a in...]
  transfers between devices with their start and end apart: 36 -> 32, of which waited for: 13 -> 13; matrix products, arithmetic and copies ran while one was open for 0% -> 0% of each run, Pallas kernels for 20% -> 18%
where the time goes in v13:
time: 84.9 us; the launch traced here: 84.6 us
  starting transfers between devices  32.6 us (38%)
  waiting for transfers between devices  28.1 us (33%)
  Pallas kernels  21.3 us (25%)
  local copies, waits for them, and re-layouts  1.58 us (2%)
  between operations  0.86 us (1%)
    ppermute x12, waiting for transfers between devices, swap(): return lax.ppermute(block, GROUP, [(i, i ^ 1 << bit) for i in range(total)])  25.4 us
    pallas_call x20, Pallas kernels, call(): pl.pallas_call(kernel, out_shape=[shape(*a.shape, dtype=a.dtype) for a in...  21.3 us
    ppermute x12, starting transfers between devices, swap(): return lax.ppermute(block, GROUP, [(i, i ^ 1 << bit) for i in range(total)])  13.3 us
    ppermute x4, starting transfers between devices, exchange(): far = lax.ppermute(parts[column], 'lon', other)  10 us
    ppermute x12, starting transfers between devices, exchange(): lax.ppermute(parts[r - 1], COLUMN, [(i, i ^ r) for i in range(column)])  7.44 us
    ppermute x4, starting transfers between devices, exchange(): lax.ppermute(parts[column - 1], 'lon', [(i, i ^ 1) for i in range(count)])  1.9 us
  transfers between devices with their start and end apart: 32, of which 13 were waited for; matrix products, arithmetic and copies ran while one was open for 0% of the time, Pallas kernels for 18%

profile of v13, /device:TPU:0, one launch (start us, length us, event | category | flops | bytes accessed | tf_op | source)
XLA Modules:
  0.0 84.6 jit_solution(3080346521047278179)
XLA Ops:
  2.3 1.6 %first_payload.1 = (bf16[512,512]{1,0:T(8,128)(2,1)S(1)}, bf16[512,512]{1,0:T(8,128)(2,1)S(1)}, s32[1,512]{1,0:T(1,128)S(1)}, s32[6,256]{1,0:T(8,128)S(1)}, bf16...) custom-call(bf16[512,512]{1,0:T(8,128)(2,1)} %refs_0_.1, ...), custom_call_target="tpu_custom_call" | custom-call | flops 67108864 | bytes 2188688 | tf_op jit(solution)/shard_map/first_payload/pallas_call | solution.py:231
  3.9 5.1 %collective-permute-start = (bf16[16,512]{1,0:T(8,128)(2,1)S(1)}, bf16[16,512]{1,0:T(8,128)(2,1)S(1)}, u32[]{:S(2)}, u32[]{:S(2)}) collective-permute-start(bf16[16,512]{1,0:T(8,128)(2,1)S(1)} %get-tuple-element.140), channel_id=1, source_target_pairs={{0,12},{4,8},{8,4},{12,0},{1,13},{5,9},{9,5},{13,1},{2,14},{6,10},... | collective-permute-start | bytes 49160 | tf_op jit(solution)/shard_map/ppermute | solution.py:247
  14.5 1.1 %collective-permute-start.5 = (bf16[24,512]{1,0:T(8,128)(2,1)S(1)}, bf16[24,512]{1,0:T(8,128)(2,1)S(1)}, u32[]{:S(2)}, u32[]{:S(2)}) collective-permute-start(bf16[24,512]{1,0:T(8,128)(2,1)S(1)} %get-tuple-element.152), channel_id=1, source_target_pairs={{0,12},{4,8},{8,4},{12,0},{1,13},{5,9},{9,5},{13,1},{2,14},{6,10},... | collective-permute-start | bytes 73736 | tf_op jit(solution)/shard_map/ppermute | solution.py:247
  16.2 1.5 %collective-permute-start.8 = (bf16[24,512]{1,0:T(8,128)(2,1)S(1)}, bf16[24,512]{1,0:T(8,128)(2,1)S(1)}, u32[]{:S(2)}, u32[]{:S(2)}) collective-permute-start(bf16[24,512]{1,0:T(8,128)(2,1)S(1)} %get-tuple-element.155), channel_id=1, source_target_pairs={{0,2},{1,3},{2,0},{3,1},{4,6},{5,7},{6,4},{7,5},{8,10},{9,11},{10,... | collective-permute-start | bytes 73736 | tf_op jit(solution)/shard_map/ppermute | solution.py:250
  18.1 1.9 %forward_local.1 = (f32[256,512]{1,0:T(8,128)S(1)}, bf16[6,256,512]{2,1,0:T(8,128)(2,1)S(1)}, f32[40,512]{1,0:T(8,128)S(1)}, bf16[40,512]{1,0:T(8,128)(2,1)S(1)}) custom-call(bf16[256,512]{1,0:T(8,128)(2,1)S(1)} %get-tuple-element.157.state_ref.refs_7_.refs_21_, bf16[2,512,512]{2,1,0:T(8,128)(2,1)S(1)} %copy-done, bf16[2,512,512]{2,1,0:T(8,128)(2,1)S(1)} %copy-done.2, ...), custom_call_target="tpu_custom_call" | custom-call | flops 805306368 | bytes 4593824 | tf_op jit(solution)/shard_map/forward_local/pallas_call | solution.py:231
  21.1 2.8 %collective-permute-start.10 = (bf16[16,512]{1,0:T(8,128)(2,1)S(1)}, bf16[16,512]{1,0:T(8,128)(2,1)S(1)}, u32[]{:S(2)}, u32[]{:S(2)}) collective-permute-start(bf16[16,512]{1,0:T(8,128)(2,1)S(1)} %get-tuple-element.162), channel_id=1, source_target_pairs={{0,12},{4,8},{8,4},{12,0},{1,13},{5,9},{9,5},{13,1},{2,14},{6,10},... | collective-permute-start | bytes 49160 | tf_op jit(solution)/shard_map/ppermute | solution.py:247
  26.3 2.9 %turn_local.1 = (f32[256,512]{1,0:T(8,128)S(1)}, f32[256,512]{1,0:T(8,128)S(1)}, f32[256,512]{1,0:T(8,128)S(1)}, f32[40,512]{1,0:T(8,128)S(1)}, bf16[40,512]{1,0...) custom-call(bf16[256,512]{1,0:T(8,128)(2,1)S(1)} %get-tuple-element., ...), custom_call_target="tpu_custom_call" | custom-call | flops 1342177280 | bytes 5830816 | tf_op jit(solution)/shard_map/turn_local/pallas_call | solution.py:231
  29.3 1.3 %turn_halo.1 = (bf16[256,512]{1,0:T(8,128)(2,1)S(1)}, bf16[256,512]{1,0:T(8,128)(2,1)S(1)}, bf16[256,512]{1,0:T(8,128)(2,1)S(1)}, bf16[256,512]{1,0:T(8,128)(2,1...) custom-call(bf16[16,512]{1,0:T(8,128)(2,1)S(1)} %collective-permute-, ...), custom_call_target="tpu_custom_call" | custom-call | flops 402653184 | bytes 5322912 | tf_op jit(solution)/shard_map/turn_halo/pallas_call | solution.py:231
  34.3 1.5 %last_weights.1 = (bf16[768,512]{1,0:T(8,128)(2,1)S(1)}, bf16[768,512]{1,0:T(8,128)(2,1)S(1)}, bf16[256,512]{1,0:T(8,128)(2,1)}) custom-call(s32[6,6]{1,0:T(8,128)S(1)} %get-tuple-element.139.refs_0_.refs_5_, bf16[256,512]{1,0:T(8,128)(2,1)S(1)} %get-tuple-element.161.state_ref.refs_1_, bf16[256,512]{1,0:T(8,128)(2,1)S(1)} %get-tuple-element.179.refs_2_, ...), custom_call_target="tpu_custom_call" | custom-call | flops 536870912 | bytes 4194448 | tf_op jit(solution)/shard_map/last_weights/pallas_call | solution.py:231
  36.7 4.3 %first_layer_back.1 = (bf16[512,512]{1,0:T(8,128)(2,1)S(1)}, bf16[768,512]{1,0:T(8,128)(2,1)S(1)}, bf16[800,512]{1,0:T(8,128)(2,1)S(1)}, bf16[512,512]{1,0:T(8,1...) custom-call(bf16[8,512]{1,0:T(8,128)(2,1)S(1)} %collective-permute-d, ...), custom_call_target="tpu_custom_call" | custom-call | flops 2147483648 | bytes 12215216 | tf_op jit(solution)/shard_map/first_layer_back/pallas_call | solution.py:231
  45.8 8.2 %collective-permute-done.23.refs_2_ = bf16[384,512]{1,0:T(8,128)(2,1)S(1)} collective-permute-done((bf16[384,512]{1,0:T(8,128)(2,1)S(1)}, bf16[384,512]{1,0:T(8,128)(2,1)S(1)}, u32[]{:S(2)}, u32[]{:S(2)}) %collective-permute-start.23) | collective-permute-done | bytes 393248 | tf_op jit(solution)/shard_map/ppermute | solution.py:162
  54.1 1.4 %collective-permute-start.24 = (bf16[192,512]{1,0:T(8,128)(2,1)S(1)}, bf16[192,512]{1,0:T(8,128)(2,1)S(1)}, u32[]{:S(2)}, u32[]{:S(2)}) collective-permute-start(bf16[192,512]{1,0:T(8,128)(2,1)S(1)} %get-tuple-element.224), channel_id=1, source_target_pairs={{0,4},{1,5},{2,6},{3,7},{4,0},{5,1},{6,2},{7,3},{8,12},{9,13},{10,... | collective-permute-start | bytes 589832 | tf_op jit(solution)/shard_map/ppermute | solution.py:162
  56.4 3.8 %collective-permute-done.24.refs_2_ = bf16[192,512]{1,0:T(8,128)(2,1)S(1)} collective-permute-done((bf16[192,512]{1,0:T(8,128)(2,1)S(1)}, bf16[192,512]{1,0:T(8,128)(2,1)S(1)}, u32[]{:S(2)}, u32[]{:S(2)}) %collective-permute-start.24) | collective-permute-done | bytes 196640 | tf_op jit(solution)/shard_map/ppermute | solution.py:162
  60.4 2.7 %collective-permute-done.25.refs_2_ = bf16[416,512]{1,0:T(8,128)(2,1)S(1)} collective-permute-done((bf16[416,512]{1,0:T(8,128)(2,1)S(1)}, bf16[416,512]{1,0:T(8,128)(2,1)S(1)}, u32[]{:S(2)}, u32[]{:S(2)}) %collective-permute-start.25) | collective-permute-done | bytes 426016 | tf_op jit(solution)/shard_map/ppermute | solution.py:162
  63.3 1.4 %collective-permute-start.28 = (bf16[224,512]{1,0:T(8,128)(2,1)S(1)}, bf16[224,512]{1,0:T(8,128)(2,1)S(1)}, u32[]{:S(2)}, u32[]{:S(2)}) collective-permute-start(bf16[224,512]{1,0:T(8,128)(2,1)S(1)} %get-tuple-element.238), channel_id=1, source_target_pairs={{0,4},{1,5},{2,6},{3,7},{4,0},{5,1},{6,2},{7,3},{8,12},{9,13},{10,... | collective-permute-start | bytes 688136 | tf_op jit(solution)/shard_map/ppermute | solution.py:162
  64.6 1.9 %collective-permute-start.27 = (bf16[96,512]{1,0:T(8,128)(2,1)S(1)}, bf16[96,512]{1,0:T(8,128)(2,1)S(1)}, u32[]{:S(2)}, u32[]{:S(2)}) collective-permute-start(bf16[96,512]{1,0:T(8,128)(2,1)S(1)} %get-tuple-element.235), channel_id=1, source_target_pairs={{0,8},{1,9},{2,10},{3,11},{4,12},{5,13},{6,14},{7,15},{8,0},{9,1},... | collective-permute-start | bytes 294920 | tf_op jit(solution)/shard_map/ppermute | solution.py:162
  66.6 1.7 %collective-permute-done.26.refs_2_ = bf16[256,512]{1,0:T(8,128)(2,1)S(1)} collective-permute-done((bf16[256,512]{1,0:T(8,128)(2,1)S(1)}, bf16[256,512]{1,0:T(8,128)(2,1)S(1)}, u32[]{:S(2)}, u32[]{:S(2)}) %collective-permute-start.26) | collective-permute-done | bytes 262176 | tf_op jit(solution)/shard_map/ppermute | solution.py:162
  68.4 1.3 %collective-permute-start.29 = (bf16[128,512]{1,0:T(8,128)(2,1)S(1)}, bf16[128,512]{1,0:T(8,128)(2,1)S(1)}, u32[]{:S(2)}, u32[]{:S(2)}) collective-permute-start(bf16[128,512]{1,0:T(8,128)(2,1)S(1)} %get-tuple-element.241), channel_id=1, source_target_pairs={{0,4},{1,5},{2,6},{3,7},{4,0},{5,1},{6,2},{7,3},{8,12},{9,13},{10,... | collective-permute-start | bytes 393224 | tf_op jit(solution)/shard_map/ppermute | solution.py:162
  69.7 2.5 %collective-permute-done.27.arr1_ref = bf16[96,512]{1,0:T(8,128)(2,1)S(1)} collective-permute-done((bf16[96,512]{1,0:T(8,128)(2,1)S(1)}, bf16[96,512]{1,0:T(8,128)(2,1)S(1)}, u32[]{:S(2)}, u32[]{:S(2)}) %collective-permute-start.27) | collective-permute-done | bytes 98336 | tf_op jit(solution)/shard_map/ppermute | solution.py:162
  72.2 1.4 %collective-permute-done.28.refs_2_ = bf16[224,512]{1,0:T(8,128)(2,1)S(1)} collective-permute-done((bf16[224,512]{1,0:T(8,128)(2,1)S(1)}, bf16[224,512]{1,0:T(8,128)(2,1)S(1)}, u32[]{:S(2)}, u32[]{:S(2)}) %collective-permute-start.28) | collective-permute-done | bytes 229408 | tf_op jit(solution)/shard_map/ppermute | solution.py:162
  74.2 2.0 %collective-permute-start.30 = (bf16[112,512]{1,0:T(8,128)(2,1)S(1)}, bf16[112,512]{1,0:T(8,128)(2,1)S(1)}, u32[]{:S(2)}, u32[]{:S(2)}) collective-permute-start(bf16[112,512]{1,0:T(8,128)(2,1)S(1)} %get-tuple-element.243), channel_id=1, source_target_pairs={{0,8},{1,9},{2,10},{3,11},{4,12},{5,13},{6,14},{7,15},{8,0},{9,1},... | collective-permute-start | bytes 344072 | tf_op jit(solution)/shard_map/ppermute | solution.py:162
  76.3 2.1 %collective-permute-start.31 = (bf16[64,512]{1,0:T(8,128)(2,1)S(1)}, bf16[64,512]{1,0:T(8,128)(2,1)S(1)}, u32[]{:S(2)}, u32[]{:S(2)}) collective-permute-start(bf16[64,512]{1,0:T(8,128)(2,1)S(1)} %get-tuple-element.255), channel_id=1, source_target_pairs={{0,8},{1,9},{2,10},{3,11},{4,12},{5,13},{6,14},{7,15},{8,0},{9,1},... | collective-permute-start | bytes 196616 | tf_op jit(solution)/shard_map/ppermute | solution.py:162
  78.3 4.1 %collective-permute-done.30.refs_0_.arr0_ref = bf16[112,512]{1,0:T(8,128)(2,1)S(1)} collective-permute-done((bf16[112,512]{1,0:T(8,128)(2,1)S(1)}, bf16[112,512]{1,0:T(8,128)(2,1)S(1)}, u32[]{:S(2)}, u32[]{:S(2)}) %collective-permute-start.30) | collective-permute-done | bytes 114720 | tf_op jit(solution)/shard_map/ppermute | solution.py:162
  82.4 1.3 %grid_place.1 = bf16[512,512]{1,0:T(8,128)(2,1)} custom-call(bf16[112,512]{1,0:T(8,128)(2,1)S(1)} %collective-permute-done.30.refs_0_.arr0_ref, bf16[16,512]{1,0:T(8,128)(2,1)S(1)} %get-tuple-element.244.refs_1_, bf16[16,512]{1,0:T(8,128)(2,1)S(1)} %get-tuple-element.245.refs_2_, bf16[16,512]{1,0:T(8,128)(2,1)S(1)} %get-tuple-element.246.refs_3_, ...), custom_call_target="tpu_custom_call" | custom-call | flops 402653184 | bytes 1753408 | tf_op jit(solution)/shard_map/grid_place/pallas_call | solution.py:231
  (71 shorter events, 24.0 us)
Async XLA Ops:
  3.9 8.0 %collective-permute-start = (bf16[16,512]{1,0:T(8,128)(2,1)S(1)}, bf16[16,512]{1,0:T(8,128)(2,1)S(1)}, u32[]{:S(2)}, u32[]{:S(2)}) collective-permute-start(bf16[16,512]{1,0:T(8,128)(2,1)S(1)} %get-tuple-element.140), channel_id=1, source_target_pairs={{0,12},{4,8},{8,4},{12,0},{1,13},{5,9},{9,5},{13,1},{2,14},{6,10},... | collective-permute-start | bytes 49160 | tf_op jit(solution)/shard_map/ppermute | solution.py:247
  9.1 3.7 %collective-permute-start.1 = (bf16[16,512]{1,0:T(8,128)(2,1)S(1)}, bf16[16,512]{1,0:T(8,128)(2,1)S(1)}, u32[]{:S(2)}, u32[]{:S(2)}) collective-permute-start(bf16[16,512]{1,0:T(8,128)(2,1)S(1)} %get-tuple-element.141), channel_id=1, source_target_pairs={{0,4},{4,0},{8,12},{12,8},{1,5},{5,1},{9,13},{13,9},{2,6},{6,2},{1... | collective-permute-start | bytes 49160 | tf_op jit(solution)/shard_map/ppermute | solution.py:248
  9.1 3.7 %collective-permute-start.2 = (bf16[16,512]{1,0:T(8,128)(2,1)S(1)}, bf16[16,512]{1,0:T(8,128)(2,1)S(1)}, u32[]{:S(2)}, u32[]{:S(2)}) collective-permute-start(bf16[16,512]{1,0:T(8,128)(2,1)S(1)} %get-tuple-element.142), channel_id=1, source_target_pairs={{0,3},{1,2},{2,1},{3,0},{4,7},{5,6},{6,5},{7,4},{8,11},{9,10},{10,... | collective-permute-start | bytes 49160 | tf_op jit(solution)/shard_map/ppermute | solution.py:250
  9.7 3.9 %collective-permute-start.3 = (bf16[16,512]{1,0:T(8,128)(2,1)S(1)}, bf16[16,512]{1,0:T(8,128)(2,1)S(1)}, u32[]{:S(2)}, u32[]{:S(2)}) collective-permute-start(bf16[16,512]{1,0:T(8,128)(2,1)S(1)} %get-tuple-element.143), channel_id=1, source_target_pairs={{0,2},{1,3},{2,0},{3,1},{4,6},{5,7},{6,4},{7,5},{8,10},{9,11},{10,... | collective-permute-start | bytes 49160 | tf_op jit(solution)/shard_map/ppermute | solution.py:250
  14.5 5.7 %collective-permute-start.5 = (bf16[24,512]{1,0:T(8,128)(2,1)S(1)}, bf16[24,512]{1,0:T(8,128)(2,1)S(1)}, u32[]{:S(2)}, u32[]{:S(2)}) collective-permute-start(bf16[24,512]{1,0:T(8,128)(2,1)S(1)} %get-tuple-element.152), channel_id=1, source_target_pairs={{0,12},{4,8},{8,4},{12,0},{1,13},{5,9},{9,5},{13,1},{2,14},{6,10},... | collective-permute-start | bytes 73736 | tf_op jit(solution)/shard_map/ppermute | solution.py:247
  15.5 4.6 %collective-permute-start.6 = (bf16[24,512]{1,0:T(8,128)(2,1)S(1)}, bf16[24,512]{1,0:T(8,128)(2,1)S(1)}, u32[]{:S(2)}, u32[]{:S(2)}) collective-permute-start(bf16[24,512]{1,0:T(8,128)(2,1)S(1)} %get-tuple-element.153), channel_id=1, source_target_pairs={{0,4},{4,0},{8,12},{12,8},{1,5},{5,1},{9,13},{13,9},{2,6},{6,2},{1... | collective-permute-start | bytes 73736 | tf_op jit(solution)/shard_map/ppermute | solution.py:248
  16.2 4.0 %collective-permute-start.7 = (bf16[24,512]{1,0:T(8,128)(2,1)S(1)}, bf16[24,512]{1,0:T(8,128)(2,1)S(1)}, u32[]{:S(2)}, u32[]{:S(2)}) collective-permute-start(bf16[24,512]{1,0:T(8,128)(2,1)S(1)} %get-tuple-element.154), channel_id=1, source_target_pairs={{0,3},{1,2},{2,1},{3,0},{4,7},{5,6},{6,5},{7,4},{8,11},{9,10},{10,... | collective-permute-start | bytes 73736 | tf_op jit(solution)/shard_map/ppermute | solution.py:250
  16.2 4.0 %collective-permute-start.8 = (bf16[24,512]{1,0:T(8,128)(2,1)S(1)}, bf16[24,512]{1,0:T(8,128)(2,1)S(1)}, u32[]{:S(2)}, u32[]{:S(2)}) collective-permute-start(bf16[24,512]{1,0:T(8,128)(2,1)S(1)} %get-tuple-element.155), channel_id=1, source_target_pairs={{0,2},{1,3},{2,0},{3,1},{4,6},{5,7},{6,4},{7,5},{8,10},{9,11},{10,... | collective-permute-start | bytes 73736 | tf_op jit(solution)/shard_map/ppermute | solution.py:250
  21.1 8.1 %collective-permute-start.10 = (bf16[16,512]{1,0:T(8,128)(2,1)S(1)}, bf16[16,512]{1,0:T(8,128)(2,1)S(1)}, u32[]{:S(2)}, u32[]{:S(2)}) collective-permute-start(bf16[16,512]{1,0:T(8,128)(2,1)S(1)} %get-tuple-element.162), channel_id=1, source_target_pairs={{0,12},{4,8},{8,4},{12,0},{1,13},{5,9},{9,5},{13,1},{2,14},{6,10},... | collective-permute-start | bytes 49160 | tf_op jit(solution)/shard_map/ppermute | solution.py:247
  23.9 5.3 %collective-permute-start.11 = (bf16[16,512]{1,0:T(8,128)(2,1)S(1)}, bf16[16,512]{1,0:T(8,128)(2,1)S(1)}, u32[]{:S(2)}, u32[]{:S(2)}) collective-permute-start(bf16[16,512]{1,0:T(8,128)(2,1)S(1)} %get-tuple-element.163), channel_id=1, source_target_pairs={{0,4},{4,0},{8,12},{12,8},{1,5},{5,1},{9,13},{13,9},{2,6},{6,2},{1... | collective-permute-start | bytes 49160 | tf_op jit(solution)/shard_map/ppermute | solution.py:248
  24.4 4.8 %collective-permute-start.12 = (bf16[16,512]{1,0:T(8,128)(2,1)S(1)}, bf16[16,512]{1,0:T(8,128)(2,1)S(1)}, u32[]{:S(2)}, u32[]{:S(2)}) collective-permute-start(bf16[16,512]{1,0:T(8,128)(2,1)S(1)} %get-tuple-element.164), channel_id=1, source_target_pairs={{0,3},{1,2},{2,1},{3,0},{4,7},{5,6},{6,5},{7,4},{8,11},{9,10},{10,... | collective-permute-start | bytes 49160 | tf_op jit(solution)/shard_map/ppermute | solution.py:250
  24.9 4.4 %collective-permute-start.13 = (bf16[16,512]{1,0:T(8,128)(2,1)S(1)}, bf16[16,512]{1,0:T(8,128)(2,1)S(1)}, u32[]{:S(2)}, u32[]{:S(2)}) collective-permute-start(bf16[16,512]{1,0:T(8,128)(2,1)S(1)} %get-tuple-element.165), channel_id=1, source_target_pairs={{0,2},{1,3},{2,0},{3,1},{4,6},{5,7},{6,4},{7,5},{8,10},{9,11},{10,... | collective-permute-start | bytes 49160 | tf_op jit(solution)/shard_map/ppermute | solution.py:250
  30.6 5.5 %collective-permute-start.15 = (bf16[8,512]{1,0:T(8,128)(2,1)S(1)}, bf16[8,512]{1,0:T(8,128)(2,1)S(1)}, u32[]{:S(2)}, u32[]{:S(2)}) collective-permute-start(bf16[8,512]{1,0:T(8,128)(2,1)S(1)} %get-tuple-element.184), channel_id=1, source_target_pairs={{0,12},{4,8},{8,4},{12,0},{1,13},{5,9},{9,5},{13,1},{2,14},{6,10},... | collective-permute-start | bytes 24584 | tf_op jit(solution)/shard_map/ppermute | solution.py:247
  31.7 4.5 %collective-permute-start.16 = (bf16[8,512]{1,0:T(8,128)(2,1)S(1)}, bf16[8,512]{1,0:T(8,128)(2,1)S(1)}, u32[]{:S(2)}, u32[]{:S(2)}) collective-permute-start(bf16[8,512]{1,0:T(8,128)(2,1)S(1)} %get-tuple-element.185), channel_id=1, source_target_pairs={{0,4},{4,0},{8,12},{12,8},{1,5},{5,1},{9,13},{13,9},{2,6},{6,2},{1... | collective-permute-start | bytes 24584 | tf_op jit(solution)/shard_map/ppermute | solution.py:248
  36.7 4.3 %collective-permute-start.20 = (bf16[768,512]{1,0:T(8,128)(2,1)S(1)}, bf16[768,512]{1,0:T(8,128)(2,1)S(1)}, u32[]{:S(2)}, u32[]{:S(2)}) collective-permute-start(bf16[768,512]{1,0:T(8,128)(2,1)S(1)} %get-tuple-element.203.refs_28_), channel_id=1, source_target_pairs={{0,1},{1,0},{2,3},{3,2},{4,5},{5,4},{6,7},{7,6},{8,9},{9,8},{10,11... | collective-permute-start | bytes 2359304 | tf_op jit(solution)/shard_map/ppermute | solution.py:162
  42.0 11.9 %collective-permute-start.23 = (bf16[384,512]{1,0:T(8,128)(2,1)S(1)}, bf16[384,512]{1,0:T(8,128)(2,1)S(1)}, u32[]{:S(2)}, u32[]{:S(2)}) collective-permute-start(bf16[384,512]{1,0:T(8,128)(2,1)S(1)} %get-tuple-element.222), channel_id=1, source_target_pairs={{0,2},{1,3},{2,0},{3,1},{4,6},{5,7},{6,4},{7,5},{8,10},{9,11},{10,... | collective-permute-start | bytes 1179656 | tf_op jit(solution)/shard_map/ppermute | solution.py:162
  44.6 18.5 %collective-permute-start.25 = (bf16[416,512]{1,0:T(8,128)(2,1)S(1)}, bf16[416,512]{1,0:T(8,128)(2,1)S(1)}, u32[]{:S(2)}, u32[]{:S(2)}) collective-permute-start(bf16[416,512]{1,0:T(8,128)(2,1)S(1)} %get-tuple-element.227), channel_id=1, source_target_pairs={{0,2},{1,3},{2,0},{3,1},{4,6},{5,7},{6,4},{7,5},{8,10},{9,11},{10,... | collective-permute-start | bytes 1277960 | tf_op jit(solution)/shard_map/ppermute | solution.py:162
  54.1 6.1 %collective-permute-start.24 = (bf16[192,512]{1,0:T(8,128)(2,1)S(1)}, bf16[192,512]{1,0:T(8,128)(2,1)S(1)}, u32[]{:S(2)}, u32[]{:S(2)}) collective-permute-start(bf16[192,512]{1,0:T(8,128)(2,1)S(1)} %get-tuple-element.224), channel_id=1, source_target_pairs={{0,4},{1,5},{2,6},{3,7},{4,0},{5,1},{6,2},{7,3},{8,12},{9,13},{10,... | collective-permute-start | bytes 589832 | tf_op jit(solution)/shard_map/ppermute | solution.py:162
  55.5 12.8 %collective-permute-start.26 = (bf16[256,512]{1,0:T(8,128)(2,1)S(1)}, bf16[256,512]{1,0:T(8,128)(2,1)S(1)}, u32[]{:S(2)}, u32[]{:S(2)}) collective-permute-start(bf16[256,512]{1,0:T(8,128)(2,1)S(1)} %get-tuple-element.233), channel_id=1, source_target_pairs={{0,2},{1,3},{2,0},{3,1},{4,6},{5,7},{6,4},{7,5},{8,10},{9,11},{10,... | collective-permute-start | bytes 786440 | tf_op jit(solution)/shard_map/ppermute | solution.py:162
  63.3 10.3 %collective-permute-start.28 = (bf16[224,512]{1,0:T(8,128)(2,1)S(1)}, bf16[224,512]{1,0:T(8,128)(2,1)S(1)}, u32[]{:S(2)}, u32[]{:S(2)}) collective-permute-start(bf16[224,512]{1,0:T(8,128)(2,1)S(1)} %get-tuple-element.238), channel_id=1, source_target_pairs={{0,4},{1,5},{2,6},{3,7},{4,0},{5,1},{6,2},{7,3},{8,12},{9,13},{10,... | collective-permute-start | bytes 688136 | tf_op jit(solution)/shard_map/ppermute | solution.py:162
  64.6 7.5 %collective-permute-start.27 = (bf16[96,512]{1,0:T(8,128)(2,1)S(1)}, bf16[96,512]{1,0:T(8,128)(2,1)S(1)}, u32[]{:S(2)}, u32[]{:S(2)}) collective-permute-start(bf16[96,512]{1,0:T(8,128)(2,1)S(1)} %get-tuple-element.235), channel_id=1, source_target_pairs={{0,8},{1,9},{2,10},{3,11},{4,12},{5,13},{6,14},{7,15},{8,0},{9,1},... | collective-permute-start | bytes 294920 | tf_op jit(solution)/shard_map/ppermute | solution.py:162
  68.4 7.7 %collective-permute-start.29 = (bf16[128,512]{1,0:T(8,128)(2,1)S(1)}, bf16[128,512]{1,0:T(8,128)(2,1)S(1)}, u32[]{:S(2)}, u32[]{:S(2)}) collective-permute-start(bf16[128,512]{1,0:T(8,128)(2,1)S(1)} %get-tuple-element.241), channel_id=1, source_target_pairs={{0,4},{1,5},{2,6},{3,7},{4,0},{5,1},{6,2},{7,3},{8,12},{9,13},{10,... | collective-permute-start | bytes 393224 | tf_op jit(solution)/shard_map/ppermute | solution.py:162
  74.2 8.3 %collective-permute-start.30 = (bf16[112,512]{1,0:T(8,128)(2,1)S(1)}, bf16[112,512]{1,0:T(8,128)(2,1)S(1)}, u32[]{:S(2)}, u32[]{:S(2)}) collective-permute-start(bf16[112,512]{1,0:T(8,128)(2,1)S(1)} %get-tuple-element.243), channel_id=1, source_target_pairs={{0,8},{1,9},{2,10},{3,11},{4,12},{5,13},{6,14},{7,15},{8,0},{9,1},... | collective-permute-start | bytes 344072 | tf_op jit(solution)/shard_map/ppermute | solution.py:162
  76.3 7.5 %collective-permute-start.31 = (bf16[64,512]{1,0:T(8,128)(2,1)S(1)}, bf16[64,512]{1,0:T(8,128)(2,1)S(1)}, u32[]{:S(2)}, u32[]{:S(2)}) collective-permute-start(bf16[64,512]{1,0:T(8,128)(2,1)S(1)} %get-tuple-element.255), channel_id=1, source_target_pairs={{0,8},{1,9},{2,10},{3,11},{4,12},{5,13},{6,14},{7,15},{8,0},{9,1},... | collective-permute-start | bytes 196616 | tf_op jit(solution)/shard_map/ppermute | solution.py:162
  (11 other events, 45.5 us)

commit v14 on v9

--- a/solution.py
+++ b/solution.py
@@ -286,10 +286,12 @@
 
 
 def embed_local(
-    column, capacity, ints_ref, senders_ref, grid_ref, weight_ref, target_ref, sends_ref,
+    column, capacity, mesh_far, merge_far, cot_far, ints_ref, senders_ref, grid_ref, weight_ref,
+    target_ref, sends_ref, mesh_ref, merge_ref, cot_ref,
     sum_ref, slope_ref, sends_row_ref, incoming_ref, bounds_ref, bounds_row_ref, senders_t_ref,
-    senders_out_ref, place_ref,
+    senders_out_ref, place_ref, sems,
 ):
+    loads = start_loads((mesh_far, merge_far, cot_far), (mesh_ref, merge_ref, cot_ref), sems)
     chosen = grid_ref.shape[0]
     nodes = sum_ref.shape[0]
     taken = sends_ref.shape[0]
@@ -318,6 +320,8 @@
     senders_t_ref[...] = senders
     filler = jnp.zeros((8 - degree, nodes), I32)
     senders_out_ref[...] = jnp.concatenate([senders, filler], axis=0).T
+    for load in loads:
+        load.wait()
 
 
 def merge_nodes(peers, *refs):
@@ -481,8 +485,9 @@
     def store(at, value):
         store_blocks(keep_ref, give_ref, at, 3, value, dims, place_ref)
 
-    store(0, dot(state, gsent_ref[...], TN))
-    store(1, dot(state, grecv_ref[...], TN))
+    both = dot(state, jnp.concatenate([gsent_ref[...], grecv_ref[...]], axis=1), TN)
+    store(0, both[:, : state.shape[1]])
+    store(1, both[:, state.shape[1] :])
     store(2, dot(summed, cot_ref[...], TN))
     mesh_ref[...] = low(state.astype(F32) + dot(summed, update_ref[1]))
 
@@ -518,8 +523,9 @@
     def store2(at, value):
         store_blocks(keep2_ref, give2_ref, at, 2, value, dims, place_ref)
 
-    store(0, dot(state, gsent, TN) + dot(rows_ref[...], gpre_k, TN))
-    store(1, dot(state, grecv, TN))
+    both = dot(state, jnp.concatenate([gsent, grecv], axis=1), TN)
+    store(0, both[:, : state.shape[1]] + dot(rows_ref[...], gpre_k, TN))
+    store(1, both[:, state.shape[1] :])
     store2(0, dot(summed_ref[...], gin, TN))
     far = low(dot(gpre_k, send_ref[0], NT))
     store2(1, dot(merged_ref[...], low(part), TN) + dot(merged_r_ref[...], far, TN))
@@ -560,23 +566,28 @@
         )
 
 
-def grid_place(peers, *refs):
-    arr_refs, refs = refs[:peers][::-1], refs[peers:]
-    gpre_ref, weight_ref, sends_ref, out_ref = refs
-    chosen = gpre_ref.shape[0]
+def grid_local(gpre_ref, weight_ref, out_ref):
+    out_ref[...] = low(dot(gpre_ref[...], weight_ref[...], NT))
+
+
+def grid_patch(local_ref, sends_ref, arr_refs, out_ref):
+    chosen = local_ref.shape[0]
     taken = sends_ref.shape[1]
-    local = dot(gpre_ref[...], weight_ref[...], NT)
+    size = taken // len(arr_refs)
     place = low(hot(sends_ref[...] == iota(chosen, taken, 0)))
-    size = taken // peers
     rows = [ref[...].astype(F32) for ref in arr_refs]
     rows = low(jnp.concatenate([row[row.shape[0] - size :] for row in rows], axis=0))
-    out_ref[...] = low(local + dot(place, rows))
-
-
-def finish(
-    keep1_ref, arr1_ref, keep0_ref, arr0_ref, keep2_ref, arr2_ref, keep_e_ref, arr_e_ref,
-    embed_ref, merge_ref, send_ref, recv_ref, update_ref,
-):
+    out_ref[...] = low(local_ref[...].astype(F32) + dot(place, rows))
+
+
+def grid_place(peers, *refs):
+    arr_refs, (local_ref, sends_ref, out_ref) = refs[:peers][::-1], refs[peers:]
+    grid_patch(local_ref, sends_ref, arr_refs, out_ref)
+
+
+def sum_last(sums, outs):
+    (keep1_ref, arr1_ref, keep0_ref, arr0_ref, keep2_ref, arr2_ref, keep_e_ref, arr_e_ref) = sums
+    embed_ref, merge_ref, send_ref, recv_ref, update_ref = outs
     last = keep1_ref[...].astype(F32) + arr1_ref[...].astype(F32)
     first = keep0_ref[...].astype(F32) + arr0_ref[...].astype(F32)
     second = keep2_ref[...].astype(F32) + arr2_ref[...].astype(F32)
@@ -586,6 +597,16 @@
         ref[1] = last[at * depth : (at + 1) * depth]
     send_ref[0], recv_ref[0], update_ref[0] = first[:depth], first[depth:], second[:depth]
     merge_ref[...] = second[depth:]
+
+
+def finish(*refs):
+    sum_last(refs[:8], refs[8:])
+
+
+def finish_all(*refs):
+    sums, rows, (local_ref, sends_ref), outs = refs[:8], refs[8:12], refs[12:14], refs[14:]
+    grid_patch(local_ref, sends_ref, (*rows, sums[7]), outs[0])
+    sum_last(sums, outs[1:])
 
 
 def body(
@@ -610,21 +631,22 @@
     ints = jnp.concatenate([send_rows[0], incoming_rows[0], border_mesh_rows[0], place], axis=1)
     unit = 2 * nodes * width * width
 
-    loads = (grid_latent, embed_weight, target_row.reshape(1, chosen), mesh_senders.T,
-             mesh_latent, merge_weight, cotangent)
-    grid, embed, targets, senders_raw, mesh, merge, cot, sends, *pay1 = call(
+    loads = (grid_latent, embed_weight, target_row.reshape(1, chosen), mesh_senders.T)
+    grid, embed, targets, senders_raw, sends, *pay1 = call(
         lambda *refs: first_payload(column, capacity, len(loads), *refs), "first_payload",
         [shape(taken, 1, dtype=I32)] + [shape(capacity, width)] * peers,
         (ints,), flops=unit // 2, loads=loads,
     )
     arr1 = exchange(pay1, dims)
-    (local, slope_g, sends_row, incoming, bounds, bounds_row, senders_t, senders, place) = call(
+    (mesh, merge, cot, local, slope_g, sends_row, incoming, bounds, bounds_row, senders_t, senders,
+     place) = call(
         lambda *refs: embed_local(column, capacity, *refs), "embed_local",
         [shape(nodes, width, dtype=F32), shape(chosen, width), shape(1, taken, dtype=I32),
          shape(1, taken, dtype=I32), shape(halo, 1, dtype=I32), shape(1, halo, dtype=I32),
          shape(degree, nodes, dtype=I32), shape(nodes, 8, dtype=I32),
          shape(slots, 2 + bits, dtype=I32)],
         (ints, senders_raw, grid, embed, targets, sends), flops=3 * unit,
+        loads=(mesh_latent, merge_weight, cotangent),
     )
     merged, state0, slope_a, lat_a, *pay2 = call(
         lambda *refs: merge_nodes(peers, *refs), "merge_nodes",
@@ -702,8 +724,8 @@
         last, first, second, embed_sum = (
             scatter_plain(blocks, dims) for blocks in (keep1, keep0, keep2, keep_e)
         )
-        grads = [jnp.stack([a, last[i]]) for i, a in enumerate((first[0], first[1], second[0]))]
-        grads = [embed_sum[0], second[1], *grads]
+        plain = [jnp.stack([a, last[i]]) for i, a in enumerate((first[0], first[1], second[0]))]
+        plain = [embed_sum[0], second[1], *plain]
     elif not carry:
         arr5 = exchange(pay5, dims)
         sums = [
@@ -716,7 +738,11 @@
         arr1 = swap(give1, 1, dims)
         arr0 = swap(give0, 1, dims)
         arr2 = swap(give2, 0, dims)
+        (local_rows,) = call(
+            grid_local, "grid_local", [shape(chosen, width)], (gpre_g, embed), flops=0, size=0
+        )
         arr_e, arr1 = lax.optimization_barrier((swap(give_e, 0, dims), arr1))
+        keep1, local_rows = lax.optimization_barrier((keep1, local_rows))
         keep1, give1 = halve_step(2, keep1, arr1, place)
         arr1 = swap(give1, 2, dims)
         keep_e, keep1 = lax.optimization_barrier((keep_e, keep1))
@@ -748,18 +774,29 @@
         keep_e, keep2, arr0 = lax.optimization_barrier((keep_e, keep2, arr0))
         keep_e, give_e, from_near, _ = carry_step(3, keep_e, arr_e, (), place, capacity)
         arr_e = swap(give_e, 3, dims)
-        arr5 = (arr_e, from_near, from_diag, from_lat, from_sub)
         sums = ((keep1, arr1), (keep0, arr0), (keep2, arr2), (keep_e, arr_e))
+    grads = [shape(depth, width, dtype=F32)] * 2 + [shape(2, depth, width, dtype=F32)] * 3
+    if carry:
+        return (mesh_out, *call(
+            finish_all, "finish_all", [shape(chosen, width)] + grads,
+            (*(part for pair in sums for part in pair), from_sub, from_lat, from_diag, from_near,
+             local_rows, sends_row),
+            flops=unit,
+        ))
+    (local_rows,) = call(
+        grid_local, "grid_local", [shape(chosen, width)], (gpre_g, embed), flops=2 * unit
+    )
     (grid_grad,) = call(
         lambda *refs: grid_place(peers, *refs), "grid_place", [shape(chosen, width)],
-        (*arr5, gpre_g, embed, sends_row), flops=3 * unit,
+        (*arr5, local_rows, sends_row), flops=unit,
     )
     if split:
         grads = call(
-            finish, "finish",
-            [shape(depth, width, dtype=F32)] * 2 + [shape(2, depth, width, dtype=F32)] * 3,
-            [part for pair in sums for part in pair], flops=8 * depth * width,
+            finish, "finish", grads, [part for pair in sums for part in pair],
+            flops=8 * depth * width,
         )
+    else:
+        grads = plain
     return (mesh_out, grid_grad, *grads)
 
 

time: 82.5 us -> 81.2 us (0.984)
  starting transfers between devices: 36.9 us -> 35.3 us
    ppermute x16, starting transfers between devices: 18.2 us -> 16.5 us  [swap(): return lax.ppermute(block, GROUP, [(i, i ^ 1 << bit) for i in range(total)])]
  transfers between devices with their start and end apart: 36 -> 36, of which waited for: 12 -> 11; matrix products, arithmetic and copies ran while one was open for 0% -> 0% of each run, Pallas kernels for 20% -> 22%
where the time goes in v14:
time: 81.2 us; the launch traced here: 80.3 us
  starting transfers between devices  35.3 us (43%)
  Pallas kernels  23 us (28%)
  waiting for transfers between devices  19.4 us (24%)
  local copies, waits for them, and re-layouts  1.57 us (2%)
  between operations  0.95 us (1%)
    pallas_call x24, Pallas kernels, call(): pl.pallas_call(kernel, out_shape=[shape(*a.shape, dtype=a.dtype) for a in...  23 us
    ppermute x16, waiting for transfers between devices, swap(): return lax.ppermute(block, GROUP, [(i, i ^ 1 << bit) for i in range(total)])  17.8 us
    ppermute x16, starting transfers between devices, swap(): return lax.ppermute(block, GROUP, [(i, i ^ 1 << bit) for i in range(total)])  16.5 us
    ppermute x4, starting transfers between devices, exchange(): far = lax.ppermute(parts[column], 'lon', other)  10.1 us
    ppermute x12, starting transfers between devices, exchange(): lax.ppermute(parts[r - 1], COLUMN, [(i, i ^ r) for i in range(column)])  6.91 us
    ppermute x4, starting transfers between devices, exchange(): lax.ppermute(parts[column - 1], 'lon', [(i, i ^ 1) for i in range(count)])  1.8 us
  transfers between devices with their start and end apart: 36, of which 11 were waited for; matrix products, arithmetic and copies ran while one was open for 0% of the time, Pallas kernels for 22%

profile of v14, /device:TPU:0, one launch (start us, length us, event | category | flops | bytes accessed | tf_op | source)
XLA Modules:
  0.0 80.3 jit_solution(15089536707430122872)
XLA Ops:
  2.3 1.3 %first_payload.1 = (bf16[512,512]{1,0:T(8,128)(2,1)S(1)}, bf16[512,512]{1,0:T(8,128)(2,1)S(1)}, s32[1,512]{1,0:T(1,128)S(1)}, s32[6,256]{1,0:T(8,128)S(1)}, s32[...) custom-call(bf16[512,512]{1,0:T(8,128)(2,1)} %refs_0_.2, ...), custom_call_target="tpu_custom_call" | custom-call | flops 67108864 | bytes 1140112 | tf_op jit(solution)/shard_map/first_payload/pallas_call | solution.py:231
  3.6 5.1 %collective-permute-start = (bf16[16,512]{1,0:T(8,128)(2,1)S(1)}, bf16[16,512]{1,0:T(8,128)(2,1)S(1)}, u32[]{:S(2)}, u32[]{:S(2)}) collective-permute-start(bf16[16,512]{1,0:T(8,128)(2,1)S(1)} %get-tuple-element.166), channel_id=1, source_target_pairs={{0,12},{4,8},{8,4},{12,0},{1,13},{5,9},{9,5},{13,1},{2,14},{6,10},... | collective-permute-start | bytes 49160 | tf_op jit(solution)/shard_map/ppermute | solution.py:247
  10.6 2.1 %embed_local.1 = (bf16[256,512]{1,0:T(8,128)(2,1)S(1)}, bf16[512,512]{1,0:T(8,128)(2,1)S(1)}, bf16[256,512]{1,0:T(8,128)(2,1)S(1)}, f32[256,512]{1,0:T(8,128)S(1...) custom-call(bf16[256,512]{1,0:T(8,128)(2,1)} %refs_0_.3, ...), custom_call_target="tpu_custom_call" | custom-call | flops 402653184 | bytes 3170784 | tf_op jit(solution)/shard_map/embed_local/pallas_call | solution.py:231
  14.2 1.1 %collective-permute-start.5 = (bf16[32,512]{1,0:T(8,128)(2,1)S(1)}, bf16[32,512]{1,0:T(8,128)(2,1)S(1)}, u32[]{:S(2)}, u32[]{:S(2)}) collective-permute-start(bf16[32,512]{1,0:T(8,128)(2,1)S(1)} %get-tuple-element.178), channel_id=1, source_target_pairs={{0,12},{4,8},{8,4},{12,0},{1,13},{5,9},{9,5},{13,1},{2,14},{6,10},... | collective-permute-start | bytes 98312 | tf_op jit(solution)/shard_map/ppermute | solution.py:247
  17.8 1.9 %forward_local.1 = (f32[256,512]{1,0:T(8,128)S(1)}, bf16[6,256,512]{2,1,0:T(8,128)(2,1)S(1)}, f32[40,512]{1,0:T(8,128)S(1)}, bf16[40,512]{1,0:T(8,128)(2,1)S(1)}) custom-call(bf16[256,512]{1,0:T(8,128)(2,1)S(1)} %get-tuple-element.183.state_ref.refs_7_.refs_10_, bf16[2,512,512]{2,1,0:T(8,128)(2,1)S(1)} %copy-done, bf16[2,512,512]{2,1,0:T(8,128)(2,1)S(1)} %copy-done.2, ...), custom_call_target="tpu_custom_call" | custom-call | flops 805306368 | bytes 4593824 | tf_op jit(solution)/shard_map/forward_local/pallas_call | solution.py:231
  21.7 2.7 %collective-permute-start.10 = (bf16[16,512]{1,0:T(8,128)(2,1)S(1)}, bf16[16,512]{1,0:T(8,128)(2,1)S(1)}, u32[]{:S(2)}, u32[]{:S(2)}) collective-permute-start(bf16[16,512]{1,0:T(8,128)(2,1)S(1)} %get-tuple-element.188), channel_id=1, source_target_pairs={{0,12},{4,8},{8,4},{12,0},{1,13},{5,9},{9,5},{13,1},{2,14},{6,10},... | collective-permute-start | bytes 49160 | tf_op jit(solution)/shard_map/ppermute | solution.py:247
  26.3 3.0 %turn_local.1 = (f32[256,512]{1,0:T(8,128)S(1)}, f32[256,512]{1,0:T(8,128)S(1)}, f32[256,512]{1,0:T(8,128)S(1)}, f32[40,512]{1,0:T(8,128)S(1)}, bf16[40,512]{1,0...) custom-call(bf16[256,512]{1,0:T(8,128)(2,1)S(1)} %get-tuple-element., ...), custom_call_target="tpu_custom_call" | custom-call | flops 1342177280 | bytes 5871776 | tf_op jit(solution)/shard_map/turn_local/pallas_call | solution.py:231
  29.3 1.3 %turn_halo.1 = (bf16[256,512]{1,0:T(8,128)(2,1)S(1)}, bf16[256,512]{1,0:T(8,128)(2,1)S(1)}, bf16[256,512]{1,0:T(8,128)(2,1)S(1)}, bf16[256,512]{1,0:T(8,128)(2,1...) custom-call(bf16[16,512]{1,0:T(8,128)(2,1)S(1)} %collective-permute-, ...), custom_call_target="tpu_custom_call" | custom-call | flops 402653184 | bytes 5322912 | tf_op jit(solution)/shard_map/turn_halo/pallas_call | solution.py:231
  30.8 1.5 %last_weights.1 = (bf16[768,512]{1,0:T(8,128)(2,1)S(1)}, bf16[768,512]{1,0:T(8,128)(2,1)S(1)}, bf16[256,512]{1,0:T(8,128)(2,1)}) custom-call(s32[6,6]{1,0:T(8,128)S(1)} %get-tuple-element.165.refs_0_.refs_5_, bf16[256,512]{1,0:T(8,128)(2,1)S(1)} %get-tuple-element.187.state_ref.refs_1_, bf16[256,512]{1,0:T(8,128)(2,1)S(1)} %get-tuple-element.205.refs_2_, ...), custom_call_target="tpu_custom_call" | custom-call | flops 536870912 | bytes 4194448 | tf_op jit(solution)/shard_map/last_weights/pallas_call | solution.py:231
  32.7 1.2 %collective-permute-start.17 = (bf16[8,512]{1,0:T(8,128)(2,1)S(1)}, bf16[8,512]{1,0:T(8,128)(2,1)S(1)}, u32[]{:S(2)}, u32[]{:S(2)}) collective-permute-start(bf16[8,512]{1,0:T(8,128)(2,1)S(1)} %get-tuple-element.225), channel_id=1, source_target_pairs={{0,12},{4,8},{8,4},{12,0},{1,13},{5,9},{9,5},{13,1},{2,14},{6,10},... | collective-permute-start | bytes 24584 | tf_op jit(solution)/shard_map/ppermute | solution.py:247
  33.9 1.1 %collective-permute-start.18 = (bf16[8,512]{1,0:T(8,128)(2,1)S(1)}, bf16[8,512]{1,0:T(8,128)(2,1)S(1)}, u32[]{:S(2)}, u32[]{:S(2)}) collective-permute-start(bf16[8,512]{1,0:T(8,128)(2,1)S(1)} %get-tuple-element.226), channel_id=1, source_target_pairs={{0,4},{4,0},{8,12},{12,8},{1,5},{5,1},{9,13},{13,9},{2,6},{6,2},{1... | collective-permute-start | bytes 24584 | tf_op jit(solution)/shard_map/ppermute | solution.py:248
  35.0 1.2 %collective-permute-start.20 = (bf16[8,512]{1,0:T(8,128)(2,1)S(1)}, bf16[8,512]{1,0:T(8,128)(2,1)S(1)}, u32[]{:S(2)}, u32[]{:S(2)}) collective-permute-start(bf16[8,512]{1,0:T(8,128)(2,1)S(1)} %get-tuple-element.228), channel_id=1, source_target_pairs={{0,2},{1,3},{2,0},{3,1},{4,6},{5,7},{6,4},{7,5},{8,10},{9,11},{10,... | collective-permute-start | bytes 24584 | tf_op jit(solution)/shard_map/ppermute | solution.py:250
  36.6 2.9 %back_local.1 = (f32[256,512]{1,0:T(8,128)S(1)}, bf16[512,512]{1,0:T(8,128)(2,1)S(1)}, bf16[512,512]{1,0:T(8,128)(2,1)S(1)}, bf16[512,512]{1,0:T(8,128)(2,1)S(1)}, bf16[512,512]{1,0:T(8,128)(2,1)S(1)}) custom-call(s32[6,6]{1,0:T(8,128)S(1)} %get-tuple-element.165.refs_0_.refs_5_, bf16[256,512]{1,0:T(8,128)(2,1)S(1)} %get-tuple-element.209.refs_1_, ...), custom_call_target="tpu_custom_call" | custom-call | flops 1342177280 | bytes 8960144 | tf_op jit(solution)/shard_map/back_local/pallas_call | solution.py:231
  42.1 2.3 %embed_back.1 = (bf16[512,512]{1,0:T(8,128)(2,1)S(1)}, bf16[256,512]{1,0:T(8,128)(2,1)S(1)}, bf16[288,512]{1,0:T(8,128)(2,1)S(1)}, bf16[16,512]{1,0:T(8,128)(2,1...) custom-call(bf16[8,512]{1,0:T(8,128)(2,1)S(1)} %collective-permute-d, ...), custom_call_target="tpu_custom_call" | custom-call | flops 805306368 | bytes 6130608 | tf_op jit(solution)/shard_map/embed_back/pallas_call | solution.py:231
  46.1 6.2 %collective-permute-done.23.refs_2_ = bf16[384,512]{1,0:T(8,128)(2,1)S(1)} collective-permute-done((bf16[384,512]{1,0:T(8,128)(2,1)S(1)}, bf16[384,512]{1,0:T(8,128)(2,1)S(1)}, u32[]{:S(2)}, u32[]{:S(2)}) %collective-permute-start.23) | collective-permute-done | bytes 393248 | tf_op jit(solution)/shard_map/ppermute | solution.py:162
  54.3 1.2 %collective-permute-start.26 = (bf16[192,512]{1,0:T(8,128)(2,1)S(1)}, bf16[192,512]{1,0:T(8,128)(2,1)S(1)}, u32[]{:S(2)}, u32[]{:S(2)}) collective-permute-start(bf16[192,512]{1,0:T(8,128)(2,1)S(1)} %get-tuple-element.269), channel_id=1, source_target_pairs={{0,4},{1,5},{2,6},{3,7},{4,0},{5,1},{6,2},{7,3},{8,12},{9,13},{10,... | collective-permute-start | bytes 589832 | tf_op jit(solution)/shard_map/ppermute | solution.py:162
  56.4 1.5 %collective-permute-done.25.refs_2_ = bf16[256,512]{1,0:T(8,128)(2,1)S(1)} collective-permute-done((bf16[256,512]{1,0:T(8,128)(2,1)S(1)}, bf16[256,512]{1,0:T(8,128)(2,1)S(1)}, u32[]{:S(2)}, u32[]{:S(2)}) %collective-permute-start.25) | collective-permute-done | bytes 262176 | tf_op jit(solution)/shard_map/ppermute | solution.py:162
  60.2 3.0 %collective-permute-start.29 = (bf16[96,512]{1,0:T(8,128)(2,1)S(1)}, bf16[96,512]{1,0:T(8,128)(2,1)S(1)}, u32[]{:S(2)}, u32[]{:S(2)}) collective-permute-start(bf16[96,512]{1,0:T(8,128)(2,1)S(1)} %get-tuple-element.280), channel_id=1, source_target_pairs={{0,8},{1,9},{2,10},{3,11},{4,12},{5,13},{6,14},{7,15},{8,0},{9,1},... | collective-permute-start | bytes 294920 | tf_op jit(solution)/shard_map/ppermute | solution.py:162
  64.8 2.5 %collective-permute-done.29.refs_1_ = bf16[96,512]{1,0:T(8,128)(2,1)S(1)} collective-permute-done((bf16[96,512]{1,0:T(8,128)(2,1)S(1)}, bf16[96,512]{1,0:T(8,128)(2,1)S(1)}, u32[]{:S(2)}, u32[]{:S(2)}) %collective-permute-start.29) | collective-permute-done | bytes 98336 | tf_op jit(solution)/shard_map/ppermute | solution.py:162
  67.7 2.3 %collective-permute-start.32 = (bf16[64,512]{1,0:T(8,128)(2,1)S(1)}, bf16[64,512]{1,0:T(8,128)(2,1)S(1)}, u32[]{:S(2)}, u32[]{:S(2)}) collective-permute-start(bf16[64,512]{1,0:T(8,128)(2,1)S(1)} %get-tuple-element.293), channel_id=1, source_target_pairs={{0,8},{1,9},{2,10},{3,11},{4,12},{5,13},{6,14},{7,15},{8,0},{9,1},... | collective-permute-start | bytes 196616 | tf_op jit(solution)/shard_map/ppermute | solution.py:162
  71.0 2.5 %collective-permute-done.32.refs_3_ = bf16[64,512]{1,0:T(8,128)(2,1)S(1)} collective-permute-done((bf16[64,512]{1,0:T(8,128)(2,1)S(1)}, bf16[64,512]{1,0:T(8,128)(2,1)S(1)}, u32[]{:S(2)}, u32[]{:S(2)}) %collective-permute-start.32) | collective-permute-done | bytes 65568 | tf_op jit(solution)/shard_map/ppermute | solution.py:162
  74.1 1.9 %collective-permute-start.35 = (bf16[48,512]{1,0:T(8,128)(2,1)S(1)}, bf16[48,512]{1,0:T(8,128)(2,1)S(1)}, u32[]{:S(2)}, u32[]{:S(2)}) collective-permute-start(bf16[48,512]{1,0:T(8,128)(2,1)S(1)} %get-tuple-element.300), channel_id=1, source_target_pairs={{0,8},{1,9},{2,10},{3,11},{4,12},{5,13},{6,14},{7,15},{8,0},{9,1},... | collective-permute-start | bytes 147464 | tf_op jit(solution)/shard_map/ppermute | solution.py:162
  76.1 3.0 %collective-permute-done.35.refs_7_ = bf16[48,512]{1,0:T(8,128)(2,1)S(1)} collective-permute-done((bf16[48,512]{1,0:T(8,128)(2,1)S(1)}, bf16[48,512]{1,0:T(8,128)(2,1)S(1)}, u32[]{:S(2)}, u32[]{:S(2)}) %collective-permute-start.35) | collective-permute-done | bytes 49184 | tf_op jit(solution)/shard_map/ppermute | solution.py:162
  79.1 1.2 %finish_all.1 = (bf16[512,512]{1,0:T(8,128)(2,1)}, f32[32,512]{1,0:T(8,128)}, f32[32,512]{1,0:T(8,128)}, f32[2,32,512]{2,1,0:T(8,128)}, f32[2,32,512]{2,1,0:T(8,128)}, /*index=5*/f32[2,32,512]{2,1,0:T(8,128)}) custom-call(bf16[96,512]{1,0:T(8,128)(2,1)S(1)} %get-tuple-element.271.refs_0_, bf16[96,512]{1,0:T(8,128)(2,1)S(1)} %collective-permute-done.29.refs_1_, ...), custom_call_target="tpu_custom_call" | custom-call | flops 134217728 | bytes 2179392 | tf_op jit(solution)/shard_map/finish_all/pallas_call | solution.py:231
  (83 shorter events, 25.3 us)
Async XLA Ops:
  3.6 9.1 %collective-permute-start = (bf16[16,512]{1,0:T(8,128)(2,1)S(1)}, bf16[16,512]{1,0:T(8,128)(2,1)S(1)}, u32[]{:S(2)}, u32[]{:S(2)}) collective-permute-start(bf16[16,512]{1,0:T(8,128)(2,1)S(1)} %get-tuple-element.166), channel_id=1, source_target_pairs={{0,12},{4,8},{8,4},{12,0},{1,13},{5,9},{9,5},{13,1},{2,14},{6,10},... | collective-permute-start | bytes 49160 | tf_op jit(solution)/shard_map/ppermute | solution.py:247
  14.2 5.8 %collective-permute-start.5 = (bf16[32,512]{1,0:T(8,128)(2,1)S(1)}, bf16[32,512]{1,0:T(8,128)(2,1)S(1)}, u32[]{:S(2)}, u32[]{:S(2)}) collective-permute-start(bf16[32,512]{1,0:T(8,128)(2,1)S(1)} %get-tuple-element.178), channel_id=1, source_target_pairs={{0,12},{4,8},{8,4},{12,0},{1,13},{5,9},{9,5},{13,1},{2,14},{6,10},... | collective-permute-start | bytes 98312 | tf_op jit(solution)/shard_map/ppermute | solution.py:247
  15.3 4.7 %collective-permute-start.6 = (bf16[32,512]{1,0:T(8,128)(2,1)S(1)}, bf16[32,512]{1,0:T(8,128)(2,1)S(1)}, u32[]{:S(2)}, u32[]{:S(2)}) collective-permute-start(bf16[32,512]{1,0:T(8,128)(2,1)S(1)} %get-tuple-element.179), channel_id=1, source_target_pairs={{0,4},{4,0},{8,12},{12,8},{1,5},{5,1},{9,13},{13,9},{2,6},{6,2},{1... | collective-permute-start | bytes 98312 | tf_op jit(solution)/shard_map/ppermute | solution.py:248
  21.7 7.6 %collective-permute-start.10 = (bf16[16,512]{1,0:T(8,128)(2,1)S(1)}, bf16[16,512]{1,0:T(8,128)(2,1)S(1)}, u32[]{:S(2)}, u32[]{:S(2)}) collective-permute-start(bf16[16,512]{1,0:T(8,128)(2,1)S(1)} %get-tuple-element.188), channel_id=1, source_target_pairs={{0,12},{4,8},{8,4},{12,0},{1,13},{5,9},{9,5},{13,1},{2,14},{6,10},... | collective-permute-start | bytes 49160 | tf_op jit(solution)/shard_map/ppermute | solution.py:247
  24.4 4.9 %collective-permute-start.11 = (bf16[16,512]{1,0:T(8,128)(2,1)S(1)}, bf16[16,512]{1,0:T(8,128)(2,1)S(1)}, u32[]{:S(2)}, u32[]{:S(2)}) collective-permute-start(bf16[16,512]{1,0:T(8,128)(2,1)S(1)} %get-tuple-element.189), channel_id=1, source_target_pairs={{0,4},{4,0},{8,12},{12,8},{1,5},{5,1},{9,13},{13,9},{2,6},{6,2},{1... | collective-permute-start | bytes 49160 | tf_op jit(solution)/shard_map/ppermute | solution.py:248
  24.4 4.9 %collective-permute-start.12 = (bf16[16,512]{1,0:T(8,128)(2,1)S(1)}, bf16[16,512]{1,0:T(8,128)(2,1)S(1)}, u32[]{:S(2)}, u32[]{:S(2)}) collective-permute-start(bf16[16,512]{1,0:T(8,128)(2,1)S(1)} %get-tuple-element.190), channel_id=1, source_target_pairs={{0,3},{1,2},{2,1},{3,0},{4,7},{5,6},{6,5},{7,4},{8,11},{9,10},{10,... | collective-permute-start | bytes 49160 | tf_op jit(solution)/shard_map/ppermute | solution.py:250
  24.8 4.5 %collective-permute-start.13 = (bf16[16,512]{1,0:T(8,128)(2,1)S(1)}, bf16[16,512]{1,0:T(8,128)(2,1)S(1)}, u32[]{:S(2)}, u32[]{:S(2)}) collective-permute-start(bf16[16,512]{1,0:T(8,128)(2,1)S(1)} %get-tuple-element.191), channel_id=1, source_target_pairs={{0,2},{1,3},{2,0},{3,1},{4,6},{5,7},{6,4},{7,5},{8,10},{9,11},{10,... | collective-permute-start | bytes 49160 | tf_op jit(solution)/shard_map/ppermute | solution.py:250
  32.7 6.7 %collective-permute-start.17 = (bf16[8,512]{1,0:T(8,128)(2,1)S(1)}, bf16[8,512]{1,0:T(8,128)(2,1)S(1)}, u32[]{:S(2)}, u32[]{:S(2)}) collective-permute-start(bf16[8,512]{1,0:T(8,128)(2,1)S(1)} %get-tuple-element.225), channel_id=1, source_target_pairs={{0,12},{4,8},{8,4},{12,0},{1,13},{5,9},{9,5},{13,1},{2,14},{6,10},... | collective-permute-start | bytes 24584 | tf_op jit(solution)/shard_map/ppermute | solution.py:247
  33.9 5.6 %collective-permute-start.18 = (bf16[8,512]{1,0:T(8,128)(2,1)S(1)}, bf16[8,512]{1,0:T(8,128)(2,1)S(1)}, u32[]{:S(2)}, u32[]{:S(2)}) collective-permute-start(bf16[8,512]{1,0:T(8,128)(2,1)S(1)} %get-tuple-element.226), channel_id=1, source_target_pairs={{0,4},{4,0},{8,12},{12,8},{1,5},{5,1},{9,13},{13,9},{2,6},{6,2},{1... | collective-permute-start | bytes 24584 | tf_op jit(solution)/shard_map/ppermute | solution.py:248
  35.0 4.5 %collective-permute-start.20 = (bf16[8,512]{1,0:T(8,128)(2,1)S(1)}, bf16[8,512]{1,0:T(8,128)(2,1)S(1)}, u32[]{:S(2)}, u32[]{:S(2)}) collective-permute-start(bf16[8,512]{1,0:T(8,128)(2,1)S(1)} %get-tuple-element.228), channel_id=1, source_target_pairs={{0,2},{1,3},{2,0},{3,1},{4,6},{5,7},{6,4},{7,5},{8,10},{9,11},{10,... | collective-permute-start | bytes 24584 | tf_op jit(solution)/shard_map/ppermute | solution.py:250
  40.3 12.8 %collective-permute-start.24 = (bf16[512,512]{1,0:T(8,128)(2,1)S(1)}, bf16[512,512]{1,0:T(8,128)(2,1)S(1)}, u32[]{:S(2)}, u32[]{:S(2)}) collective-permute-start(bf16[512,512]{1,0:T(8,128)(2,1)S(1)} %get-tuple-element.261), channel_id=1, source_target_pairs={{0,1},{1,0},{2,3},{3,2},{4,5},{5,4},{6,7},{7,6},{8,9},{9,8},{10,11... | collective-permute-start | bytes 1572872 | tf_op jit(solution)/shard_map/ppermute | solution.py:162
  40.4 11.9 %collective-permute-start.23 = (bf16[384,512]{1,0:T(8,128)(2,1)S(1)}, bf16[384,512]{1,0:T(8,128)(2,1)S(1)}, u32[]{:S(2)}, u32[]{:S(2)}) collective-permute-start(bf16[384,512]{1,0:T(8,128)(2,1)S(1)} %get-tuple-element.253), channel_id=1, source_target_pairs={{0,2},{1,3},{2,0},{3,1},{4,6},{5,7},{6,4},{7,5},{8,10},{9,11},{10,... | collective-permute-start | bytes 1179656 | tf_op jit(solution)/shard_map/ppermute | solution.py:162
  44.4 7.9 %collective-permute-start.22 = (bf16[288,512]{1,0:T(8,128)(2,1)S(1)}, bf16[288,512]{1,0:T(8,128)(2,1)S(1)}, u32[]{:S(2)}, u32[]{:S(2)}) collective-permute-start(bf16[288,512]{1,0:T(8,128)(2,1)S(1)} %get-tuple-element.252), channel_id=1, source_target_pairs={{0,1},{1,0},{2,3},{3,2},{4,5},{5,4},{6,7},{7,6},{8,9},{9,8},{10,11... | collective-permute-start | bytes 884744 | tf_op jit(solution)/shard_map/ppermute | solution.py:162
  44.8 13.1 %collective-permute-start.25 = (bf16[256,512]{1,0:T(8,128)(2,1)S(1)}, bf16[256,512]{1,0:T(8,128)(2,1)S(1)}, u32[]{:S(2)}, u32[]{:S(2)}) collective-permute-start(bf16[256,512]{1,0:T(8,128)(2,1)S(1)} %get-tuple-element.266), channel_id=1, source_target_pairs={{0,2},{1,3},{2,0},{3,1},{4,6},{5,7},{6,4},{7,5},{8,10},{9,11},{10,... | collective-permute-start | bytes 786440 | tf_op jit(solution)/shard_map/ppermute | solution.py:162
  53.4 10.1 %collective-permute-start.27 = (bf16[256,512]{1,0:T(8,128)(2,1)S(1)}, bf16[256,512]{1,0:T(8,128)(2,1)S(1)}, u32[]{:S(2)}, u32[]{:S(2)}) collective-permute-start(bf16[256,512]{1,0:T(8,128)(2,1)S(1)} %get-tuple-element.275), channel_id=1, source_target_pairs={{0,2},{1,3},{2,0},{3,1},{4,6},{5,7},{6,4},{7,5},{8,10},{9,11},{10,... | collective-permute-start | bytes 786440 | tf_op jit(solution)/shard_map/ppermute | solution.py:162
  54.3 5.7 %collective-permute-start.26 = (bf16[192,512]{1,0:T(8,128)(2,1)S(1)}, bf16[192,512]{1,0:T(8,128)(2,1)S(1)}, u32[]{:S(2)}, u32[]{:S(2)}) collective-permute-start(bf16[192,512]{1,0:T(8,128)(2,1)S(1)} %get-tuple-element.269), channel_id=1, source_target_pairs={{0,4},{1,5},{2,6},{3,7},{4,0},{5,1},{6,2},{7,3},{8,12},{9,13},{10,... | collective-permute-start | bytes 589832 | tf_op jit(solution)/shard_map/ppermute | solution.py:162
  55.5 11.8 %collective-permute-start.30 = (bf16[160,512]{1,0:T(8,128)(2,1)S(1)}, bf16[160,512]{1,0:T(8,128)(2,1)S(1)}, u32[]{:S(2)}, u32[]{:S(2)}) collective-permute-start(bf16[160,512]{1,0:T(8,128)(2,1)S(1)} %get-tuple-element.285), channel_id=1, source_target_pairs={{0,2},{1,3},{2,0},{3,1},{4,6},{5,7},{6,4},{7,5},{8,10},{9,11},{10,... | collective-permute-start | bytes 491528 | tf_op jit(solution)/shard_map/ppermute | solution.py:162
  58.1 6.6 %collective-permute-start.28 = (bf16[128,512]{1,0:T(8,128)(2,1)S(1)}, bf16[128,512]{1,0:T(8,128)(2,1)S(1)}, u32[]{:S(2)}, u32[]{:S(2)}) collective-permute-start(bf16[128,512]{1,0:T(8,128)(2,1)S(1)} %get-tuple-element.278), channel_id=1, source_target_pairs={{0,4},{1,5},{2,6},{3,7},{4,0},{5,1},{6,2},{7,3},{8,12},{9,13},{10,... | collective-permute-start | bytes 393224 | tf_op jit(solution)/shard_map/ppermute | solution.py:162
  60.2 7.2 %collective-permute-start.29 = (bf16[96,512]{1,0:T(8,128)(2,1)S(1)}, bf16[96,512]{1,0:T(8,128)(2,1)S(1)}, u32[]{:S(2)}, u32[]{:S(2)}) collective-permute-start(bf16[96,512]{1,0:T(8,128)(2,1)S(1)} %get-tuple-element.280), channel_id=1, source_target_pairs={{0,8},{1,9},{2,10},{3,11},{4,12},{5,13},{6,14},{7,15},{8,0},{9,1},... | collective-permute-start | bytes 294920 | tf_op jit(solution)/shard_map/ppermute | solution.py:162
  63.7 6.3 %collective-permute-start.31 = (bf16[128,512]{1,0:T(8,128)(2,1)S(1)}, bf16[128,512]{1,0:T(8,128)(2,1)S(1)}, u32[]{:S(2)}, u32[]{:S(2)}) collective-permute-start(bf16[128,512]{1,0:T(8,128)(2,1)S(1)} %get-tuple-element.291), channel_id=1, source_target_pairs={{0,4},{1,5},{2,6},{3,7},{4,0},{5,1},{6,2},{7,3},{8,12},{9,13},{10,... | collective-permute-start | bytes 393224 | tf_op jit(solution)/shard_map/ppermute | solution.py:162
  67.5 6.0 %collective-permute-start.34 = (bf16[96,512]{1,0:T(8,128)(2,1)S(1)}, bf16[96,512]{1,0:T(8,128)(2,1)S(1)}, u32[]{:S(2)}, u32[]{:S(2)}) collective-permute-start(bf16[96,512]{1,0:T(8,128)(2,1)S(1)} %get-tuple-element.298), channel_id=1, source_target_pairs={{0,4},{1,5},{2,6},{3,7},{4,0},{5,1},{6,2},{7,3},{8,12},{9,13},{10,... | collective-permute-start | bytes 294920 | tf_op jit(solution)/shard_map/ppermute | solution.py:162
  67.7 5.8 %collective-permute-start.32 = (bf16[64,512]{1,0:T(8,128)(2,1)S(1)}, bf16[64,512]{1,0:T(8,128)(2,1)S(1)}, u32[]{:S(2)}, u32[]{:S(2)}) collective-permute-start(bf16[64,512]{1,0:T(8,128)(2,1)S(1)} %get-tuple-element.293), channel_id=1, source_target_pairs={{0,8},{1,9},{2,10},{3,11},{4,12},{5,13},{6,14},{7,15},{8,0},{9,1},... | collective-permute-start | bytes 196616 | tf_op jit(solution)/shard_map/ppermute | solution.py:162
  70.1 9.0 %collective-permute-start.33 = (bf16[64,512]{1,0:T(8,128)(2,1)S(1)}, bf16[64,512]{1,0:T(8,128)(2,1)S(1)}, u32[]{:S(2)}, u32[]{:S(2)}) collective-permute-start(bf16[64,512]{1,0:T(8,128)(2,1)S(1)} %get-tuple-element.296), channel_id=1, source_target_pairs={{0,8},{1,9},{2,10},{3,11},{4,12},{5,13},{6,14},{7,15},{8,0},{9,1},... | collective-permute-start | bytes 196616 | tf_op jit(solution)/shard_map/ppermute | solution.py:162
  74.1 5.0 %collective-permute-start.35 = (bf16[48,512]{1,0:T(8,128)(2,1)S(1)}, bf16[48,512]{1,0:T(8,128)(2,1)S(1)}, u32[]{:S(2)}, u32[]{:S(2)}) collective-permute-start(bf16[48,512]{1,0:T(8,128)(2,1)S(1)} %get-tuple-element.300), channel_id=1, source_target_pairs={{0,8},{1,9},{2,10},{3,11},{4,12},{5,13},{6,14},{7,15},{8,0},{9,1},... | collective-permute-start | bytes 147464 | tf_op jit(solution)/shard_map/ppermute | solution.py:162
  (15 other events, 59.0 us)

commit v15 on v14

--- a/solution.py
+++ b/solution.py
@@ -48,6 +48,10 @@
 
 def hot(mask):
     return jnp.where(mask, 1.0, 0.0)
+
+
+def slot_rows(ref):
+    return jnp.concatenate([ref[s] for s in range(ref.shape[0])], axis=0)
 
 
 def slot_of(at, column, me, odd):
@@ -179,31 +183,33 @@
     return keep, arrived
 
 
-def halve_carry(bit, bits_ref, keep_ref, arr_ref, *refs):
-    *own_refs, keep_out, give_out, here_ref, on_ref = refs
+def halve_carry(bit, count, bits_ref, keep_ref, arr_ref, *refs):
+    own_refs, (keep_out, give_out, *here_refs) = refs[:count], refs[count:]
     rows = keep_ref.shape[0]
     half = rows // 2
-    size = here_ref.shape[0]
+    size = here_refs[0].shape[0]
     upper = bits_ref[0:1, 2 + bit : 3 + bit] == 1
     value = arr_ref[...].astype(F32)
     first = keep_ref[:half, :].astype(F32) + value[:half]
     second = keep_ref[half:, :].astype(F32) + value[half:rows]
     keep_out[...] = low(jnp.where(upper, second, first))
-    here_ref[...] = low(value[rows : rows + size])
+    here_refs[0][...] = low(value[rows : rows + size])
     passed = value[rows + size : rows + 2 * size]
-    on_ref[...] = low(passed)
     extra = [ref[...].astype(F32) for ref in own_refs]
-    if len(extra) < 2:
+    if count < 2:
         extra.append(passed)
+    else:
+        here_refs[1][...] = low(passed)
     give_out[...] = low(jnp.concatenate([jnp.where(upper, first, second), *extra], axis=0))
 
 
 def carry_step(bit, keep, arrived, own, place, capacity):
     rows, width = keep.shape[0] // 2, keep.shape[1]
+    count = len(own)
     return call(
-        lambda *refs: halve_carry(bit, *refs), "halve_carry",
-        [shape(rows, width), shape(rows + min(len(own) + 1, 2) * capacity, width),
-         shape(capacity, width), shape(capacity, width)],
+        lambda *refs: halve_carry(bit, count, *refs), "halve_carry",
+        [shape(rows, width), shape(rows + min(count + 1, 2) * capacity, width)]
+        + [shape(capacity, width)] * (2 if count == 2 else 1),
         (place, keep, arrived, *own), flops=4 * rows * width, size=0,
     )
 
@@ -267,17 +273,17 @@
     return copies
 
 
-def first_payload(column, capacity, count, *refs):
-    sources, ints_ref, targets = refs[:count], refs[count], refs[count + 1 : 2 * count + 1]
-    sends_ref, *pay_refs, sems = refs[2 * count + 1 :]
-    grid_ref = targets[0]
-    grid_load, *loads = start_loads(sources, targets, sems)
+def first_payload(column, count, *refs):
+    sources, place_ref, targets = refs[:count], refs[count], refs[count + 1 : 2 * count + 1]
+    sends_out, *pay_refs, sems = refs[2 * count + 1 :]
+    sends_ref, grid_ref = targets[:2]
+    sends_load, grid_load, *loads = start_loads(sources, targets, sems)
     chosen = grid_ref.shape[0]
-    ints = ints_ref[...]
-    base = 2 * capacity + BORDER
-    me, odd = ints[0:1, base : base + 1], ints[0:1, base + 1 : base + 2]
-    sends = as_column(ints[:, :capacity], capacity, column, me, odd)
-    sends_ref[...] = sends
+    me, odd = place_ref[:, 0:1], place_ref[:, 1:2]
+    sends_load.wait()
+    sends = slot_rows(sends_ref)
+    sends = as_column(sends, sends.shape[1], column, me, odd)
+    sends_out[...] = sends
     pick = low(hot(sends == iota(sends.shape[0], chosen, 1)))
     grid_load.wait()
     store_parts(pay_refs, [dot(pick, grid_ref[...])])
@@ -286,9 +292,9 @@
 
 
 def embed_local(
-    column, capacity, mesh_far, merge_far, cot_far, ints_ref, senders_ref, grid_ref, weight_ref,
-    target_ref, sends_ref, mesh_ref, merge_ref, cot_ref,
-    sum_ref, slope_ref, sends_row_ref, incoming_ref, bounds_ref, bounds_row_ref, senders_t_ref,
+    column, mesh_far, merge_far, cot_far, place_in_ref, raw_sends_ref, raw_incoming_ref,
+    raw_bounds_ref, senders_ref, grid_ref, weight_ref, target_ref, sends_ref, mesh_ref, merge_ref,
+    cot_ref, sum_ref, slope_ref, sends_row_ref, incoming_ref, bounds_ref, bounds_row_ref, senders_t_ref,
     senders_out_ref, place_ref, sems,
 ):
     loads = start_loads((mesh_far, merge_far, cot_far), (mesh_ref, merge_ref, cot_ref), sems)
@@ -300,13 +306,12 @@
     sent = jnp.max(hot(sends_ref[...] == iota(taken, chosen, 1)), axis=0, keepdims=True)
     label = jnp.where(sent > 0.0, nodes, target_ref[...])
     sum_ref[...] = dot(low(hot(label == iota(nodes, chosen, 0))), low(act))
-    ints = ints_ref[...]
-    base = 2 * capacity + BORDER
-    place_ref[...] = ints[:, base:]
-    me, odd = ints[0:1, base : base + 1], ints[0:1, base + 1 : base + 2]
-    sends, incoming = ints[:, :capacity], ints[:, capacity : 2 * capacity]
-    bounds = ints[:, 2 * capacity : base]
-    sends_row_ref[...] = as_row(sends, capacity, column, me, odd)
+    place_ref[...] = place_in_ref[...]
+    me, odd = place_in_ref[:, 0:1], place_in_ref[:, 1:2]
+    raw_sends, incoming = slot_rows(raw_sends_ref), slot_rows(raw_incoming_ref)
+    bounds = slot_rows(raw_bounds_ref)
+    capacity = incoming.shape[1]
+    sends_row_ref[...] = as_row(raw_sends, capacity, column, me, odd)
     incoming_ref[...] = as_row(incoming, capacity, column, me, odd)
     bounds_ref[...] = as_column(bounds, BORDER, column, me, odd)
     bounds_row_ref[...] = as_row(bounds, BORDER, column, me, odd)
@@ -627,25 +632,27 @@
     spot = lax.axis_index(GROUP)
     place = [lax.axis_index(COLUMN), lax.axis_index("lon") % 2]
     place += [(spot >> bit) % 2 for bit in range(bits)]
-    place = jnp.broadcast_to(jnp.stack(place).astype(I32)[None], (slots, 2 + bits))
-    ints = jnp.concatenate([send_rows[0], incoming_rows[0], border_mesh_rows[0], place], axis=1)
+    place = jnp.stack(place).astype(I32).reshape(1, 2 + bits)
+    raw = [a.transpose(1, 0, 2) for a in (send_rows, incoming_rows, border_mesh_rows)]
     unit = 2 * nodes * width * width
 
-    loads = (grid_latent, embed_weight, target_row.reshape(1, chosen), mesh_senders.T)
-    grid, embed, targets, senders_raw, sends, *pay1 = call(
-        lambda *refs: first_payload(column, capacity, len(loads), *refs), "first_payload",
+    loads = (raw[0], grid_latent, embed_weight, target_row.reshape(1, chosen), mesh_senders.T,
+             *raw[1:])
+    raw_sends, grid, embed, targets, senders_raw, raw_incoming, raw_bounds, sends, *pay1 = call(
+        lambda *refs: first_payload(column, len(loads), *refs), "first_payload",
         [shape(taken, 1, dtype=I32)] + [shape(capacity, width)] * peers,
-        (ints,), flops=unit // 2, loads=loads,
+        (place,), flops=unit // 2, loads=loads,
     )
     arr1 = exchange(pay1, dims)
     (mesh, merge, cot, local, slope_g, sends_row, incoming, bounds, bounds_row, senders_t, senders,
      place) = call(
-        lambda *refs: embed_local(column, capacity, *refs), "embed_local",
+        lambda *refs: embed_local(column, *refs), "embed_local",
         [shape(nodes, width, dtype=F32), shape(chosen, width), shape(1, taken, dtype=I32),
          shape(1, taken, dtype=I32), shape(halo, 1, dtype=I32), shape(1, halo, dtype=I32),
          shape(degree, nodes, dtype=I32), shape(nodes, 8, dtype=I32),
-         shape(slots, 2 + bits, dtype=I32)],
-        (ints, senders_raw, grid, embed, targets, sends), flops=3 * unit,
+         shape(1, 2 + bits, dtype=I32)],
+        (place, raw_sends, raw_incoming, raw_bounds, senders_raw, grid, embed, targets, sends),
+        flops=3 * unit,
         loads=(mesh_latent, merge_weight, cotangent),
     )
     merged, state0, slope_a, lat_a, *pay2 = call(
@@ -746,7 +753,7 @@
         keep1, give1 = halve_step(2, keep1, arr1, place)
         arr1 = swap(give1, 2, dims)
         keep_e, keep1 = lax.optimization_barrier((keep_e, keep1))
-        keep_e, give_e, from_sub, _ = carry_step(1, keep_e, arr_e, pay5[1:2], place, capacity)
+        keep_e, give_e, from_sub = carry_step(1, keep_e, arr_e, pay5[1:2], place, capacity)
         arr_e = swap(give_e, 1, dims)
         keep2, keep_e = lax.optimization_barrier((keep2, keep_e))
         keep2, give2 = halve_step(1, keep2, arr2, place)
@@ -771,8 +778,9 @@
         keep2, keep_e = lax.optimization_barrier((keep2, keep_e))
         keep2, give2 = halve_step(3, keep2, arr2, place)
         arr2 = swap(give2, 3, dims)
-        keep_e, keep2, arr0 = lax.optimization_barrier((keep_e, keep2, arr0))
-        keep_e, give_e, from_near, _ = carry_step(3, keep_e, arr_e, (), place, capacity)
+        keep_e, keep2 = lax.optimization_barrier((keep_e, keep2))
+        keep_e, give_e, from_near = carry_step(3, keep_e, arr_e, (), place, capacity)
+        give_e, arr0 = lax.optimization_barrier((give_e, arr0))
         arr_e = swap(give_e, 3, dims)
         sums = ((keep1, arr1), (keep0, arr0), (keep2, arr2), (keep_e, arr_e))
     grads = [shape(depth, width, dtype=F32)] * 2 + [shape(2, depth, width, dtype=F32)] * 3

time: 81.2 us -> 79.8 us (0.983)
  waiting for transfers between devices: 19.4 us -> 22.7 us
  local copies, waits for them, and re-layouts: 1.57 us -> 0.1 us
  starting transfers between devices: 35.3 us -> 34 us
  Pallas kernels: 23 us -> 21.9 us
    ppermute x16, waiting for transfers between devices: 17.8 us -> 21 us  [swap(): return lax.ppermute(block, GROUP, [(i, i ^ 1 << bit) for i in range(total)])]
    unnamed x8 -> x6, local copies, waits for them, and re-layouts: 1.41 us -> 0.02 us
    ppermute x16, starting transfers between devices: 16.5 us -> 15.3 us  [swap(): return lax.ppermute(block, GROUP, [(i, i ^ 1 << bit) for i in range(total)])]
    pallas_call x24, Pallas kernels: 23 us -> 21.9 us  [call(): pl.pallas_call(kernel, out_shape=[shape(*a.shape, dtype=a.dtype) for a in...]
  transfers between devices with their start and end apart: 36 -> 36, of which waited for: 11 -> 12; matrix products, arithmetic and copies ran while one was open for 0% -> 0% of each run, Pallas kernels for 22% -> 20%
where the time goes in v15:
time: 79.8 us; the launch traced here: 79.6 us
  starting transfers between devices  34 us (43%)
  waiting for transfers between devices  22.7 us (28%)
  Pallas kernels  21.9 us (27%)
  between operations  0.94 us (1%)
    pallas_call x24, Pallas kernels, call(): pl.pallas_call(kernel, out_shape=[shape(*a.shape, dtype=a.dtype) for a in...  21.9 us
    ppermute x16, waiting for transfers between devices, swap(): return lax.ppermute(block, GROUP, [(i, i ^ 1 << bit) for i in range(total)])  21 us
    ppermute x16, starting transfers between devices, swap(): return lax.ppermute(block, GROUP, [(i, i ^ 1 << bit) for i in range(total)])  15.3 us
    ppermute x4, starting transfers between devices, exchange(): far = lax.ppermute(parts[column], 'lon', other)  10.1 us
    ppermute x12, starting transfers between devices, exchange(): lax.ppermute(parts[r - 1], COLUMN, [(i, i ^ r) for i in range(column)])  6.89 us
    ppermute x4, starting transfers between devices, exchange(): lax.ppermute(parts[column - 1], 'lon', [(i, i ^ 1) for i in range(count)])  1.8 us
  transfers between devices with their start and end apart: 36, of which 12 were waited for; matrix products, arithmetic and copies ran while one was open for 0% of the time, Pallas kernels for 20%

profile of v15, /device:TPU:0, one launch (start us, length us, event | category | flops | bytes accessed | tf_op | source)
XLA Modules:
  0.0 79.6 jit_solution(3641974853484980178)
XLA Ops:
  0.8 1.3 %first_payload.1 = (s32[6,1,16]{2,1,0:T(1,128)S(1)}, bf16[512,512]{1,0:T(8,128)(2,1)S(1)}, bf16[512,512]{1,0:T(8,128)(2,1)S(1)}, s32[1,512]{1,0:T(1,128)S(1)}, s...) custom-call(s32[6,1,16]{2,1,0:T(1,128)} %bitcast.15, ...), custom_call_target="tpu_custom_call" | custom-call | flops 67108864 | bytes 1139992 | tf_op jit(solution)/shard_map/first_payload/pallas_call | solution.py:237
  2.1 5.1 %collective-permute-start = (bf16[16,512]{1,0:T(8,128)(2,1)S(1)}, bf16[16,512]{1,0:T(8,128)(2,1)S(1)}, u32[]{:S(2)}, u32[]{:S(2)}) collective-permute-start(bf16[16,512]{1,0:T(8,128)(2,1)S(1)} %get-tuple-element.173), channel_id=1, source_target_pairs={{0,12},{4,8},{8,4},{12,0},{1,13},{5,9},{9,5},{13,1},{2,14},{6,10},... | collective-permute-start | bytes 49160 | tf_op jit(solution)/shard_map/ppermute | solution.py:253
  9.1 2.1 %embed_local.1 = (bf16[256,512]{1,0:T(8,128)(2,1)S(1)}, bf16[512,512]{1,0:T(8,128)(2,1)S(1)}, bf16[256,512]{1,0:T(8,128)(2,1)S(1)}, f32[256,512]{1,0:T(8,128)S(1...) custom-call(bf16[256,512]{1,0:T(8,128)(2,1)} %refs_0_.1, ...), custom_call_target="tpu_custom_call" | custom-call | flops 402653184 | bytes 3170544 | tf_op jit(solution)/shard_map/embed_local/pallas_call | solution.py:237
  16.3 1.9 %forward_local.1 = (f32[256,512]{1,0:T(8,128)S(1)}, bf16[6,256,512]{2,1,0:T(8,128)(2,1)S(1)}, f32[40,512]{1,0:T(8,128)S(1)}, bf16[40,512]{1,0:T(8,128)(2,1)S(1)}) custom-call(bf16[256,512]{1,0:T(8,128)(2,1)S(1)} %get-tuple-element.190.state_ref.refs_7_.refs_10_, bf16[2,512,512]{2,1,0:T(8,128)(2,1)S(1)} %copy-done, bf16[2,512,512]{2,1,0:T(8,128)(2,1)S(1)} %copy-done.2, ...), custom_call_target="tpu_custom_call" | custom-call | flops 805306368 | bytes 4593824 | tf_op jit(solution)/shard_map/forward_local/pallas_call | solution.py:237
  20.2 2.7 %collective-permute-start.10 = (bf16[16,512]{1,0:T(8,128)(2,1)S(1)}, bf16[16,512]{1,0:T(8,128)(2,1)S(1)}, u32[]{:S(2)}, u32[]{:S(2)}) collective-permute-start(bf16[16,512]{1,0:T(8,128)(2,1)S(1)} %get-tuple-element.195), channel_id=1, source_target_pairs={{0,12},{4,8},{8,4},{12,0},{1,13},{5,9},{9,5},{13,1},{2,14},{6,10},... | collective-permute-start | bytes 49160 | tf_op jit(solution)/shard_map/ppermute | solution.py:253
  24.8 3.0 %turn_local.1 = (f32[256,512]{1,0:T(8,128)S(1)}, f32[256,512]{1,0:T(8,128)S(1)}, f32[256,512]{1,0:T(8,128)S(1)}, f32[40,512]{1,0:T(8,128)S(1)}, bf16[40,512]{1,0...) custom-call(bf16[256,512]{1,0:T(8,128)(2,1)S(1)} %get-tuple-element., ...), custom_call_target="tpu_custom_call" | custom-call | flops 1342177280 | bytes 5871776 | tf_op jit(solution)/shard_map/turn_local/pallas_call | solution.py:237
  27.8 1.3 %turn_halo.1 = (bf16[256,512]{1,0:T(8,128)(2,1)S(1)}, bf16[256,512]{1,0:T(8,128)(2,1)S(1)}, bf16[256,512]{1,0:T(8,128)(2,1)S(1)}, bf16[256,512]{1,0:T(8,128)(2,1...) custom-call(bf16[16,512]{1,0:T(8,128)(2,1)S(1)} %collective-permute-, ...), custom_call_target="tpu_custom_call" | custom-call | flops 402653184 | bytes 5322912 | tf_op jit(solution)/shard_map/turn_halo/pallas_call | solution.py:237
  29.3 1.5 %last_weights.1 = (bf16[768,512]{1,0:T(8,128)(2,1)S(1)}, bf16[768,512]{1,0:T(8,128)(2,1)S(1)}, bf16[256,512]{1,0:T(8,128)(2,1)}) custom-call(s32[1,6]{1,0:T(1,128)S(1)} %get-tuple-element.172.refs_0_.refs_5_, bf16[256,512]{1,0:T(8,128)(2,1)S(1)} %get-tuple-element.194.state_ref.refs_1_, bf16[256,512]{1,0:T(8,128)(2,1)S(1)} %get-tuple-element.212.refs_2_, ...), custom_call_target="tpu_custom_call" | custom-call | flops 536870912 | bytes 4194328 | tf_op jit(solution)/shard_map/last_weights/pallas_call | solution.py:237
  31.2 1.2 %collective-permute-start.17 = (bf16[8,512]{1,0:T(8,128)(2,1)S(1)}, bf16[8,512]{1,0:T(8,128)(2,1)S(1)}, u32[]{:S(2)}, u32[]{:S(2)}) collective-permute-start(bf16[8,512]{1,0:T(8,128)(2,1)S(1)} %get-tuple-element.232), channel_id=1, source_target_pairs={{0,12},{4,8},{8,4},{12,0},{1,13},{5,9},{9,5},{13,1},{2,14},{6,10},... | collective-permute-start | bytes 24584 | tf_op jit(solution)/shard_map/ppermute | solution.py:253
  32.4 1.1 %collective-permute-start.18 = (bf16[8,512]{1,0:T(8,128)(2,1)S(1)}, bf16[8,512]{1,0:T(8,128)(2,1)S(1)}, u32[]{:S(2)}, u32[]{:S(2)}) collective-permute-start(bf16[8,512]{1,0:T(8,128)(2,1)S(1)} %get-tuple-element.233), channel_id=1, source_target_pairs={{0,4},{4,0},{8,12},{12,8},{1,5},{5,1},{9,13},{13,9},{2,6},{6,2},{1... | collective-permute-start | bytes 24584 | tf_op jit(solution)/shard_map/ppermute | solution.py:254
  33.5 1.1 %collective-permute-start.20 = (bf16[8,512]{1,0:T(8,128)(2,1)S(1)}, bf16[8,512]{1,0:T(8,128)(2,1)S(1)}, u32[]{:S(2)}, u32[]{:S(2)}) collective-permute-start(bf16[8,512]{1,0:T(8,128)(2,1)S(1)} %get-tuple-element.235), channel_id=1, source_target_pairs={{0,2},{1,3},{2,0},{3,1},{4,6},{5,7},{6,4},{7,5},{8,10},{9,11},{10,... | collective-permute-start | bytes 24584 | tf_op jit(solution)/shard_map/ppermute | solution.py:256
  35.1 2.8 %back_local.1 = (f32[256,512]{1,0:T(8,128)S(1)}, bf16[512,512]{1,0:T(8,128)(2,1)S(1)}, bf16[512,512]{1,0:T(8,128)(2,1)S(1)}, bf16[512,512]{1,0:T(8,128)(2,1)S(1)}, bf16[512,512]{1,0:T(8,128)(2,1)S(1)}) custom-call(s32[1,6]{1,0:T(1,128)S(1)} %get-tuple-element.172.refs_0_.refs_5_, bf16[256,512]{1,0:T(8,128)(2,1)S(1)} %get-tuple-element.216.refs_1_, ...), custom_call_target="tpu_custom_call" | custom-call | flops 1342177280 | bytes 8960024 | tf_op jit(solution)/shard_map/back_local/pallas_call | solution.py:237
  40.6 2.3 %embed_back.1 = (bf16[512,512]{1,0:T(8,128)(2,1)S(1)}, bf16[256,512]{1,0:T(8,128)(2,1)S(1)}, bf16[288,512]{1,0:T(8,128)(2,1)S(1)}, bf16[16,512]{1,0:T(8,128)(2,1...) custom-call(bf16[8,512]{1,0:T(8,128)(2,1)S(1)} %collective-permute-d, ...), custom_call_target="tpu_custom_call" | custom-call | flops 805306368 | bytes 6130488 | tf_op jit(solution)/shard_map/embed_back/pallas_call | solution.py:237
  44.7 6.1 %collective-permute-done.23.refs_2_ = bf16[384,512]{1,0:T(8,128)(2,1)S(1)} collective-permute-done((bf16[384,512]{1,0:T(8,128)(2,1)S(1)}, bf16[384,512]{1,0:T(8,128)(2,1)S(1)}, u32[]{:S(2)}, u32[]{:S(2)}) %collective-permute-start.23) | collective-permute-done | bytes 393248 | tf_op jit(solution)/shard_map/ppermute | solution.py:166
  52.4 1.2 %collective-permute-start.26 = (bf16[192,512]{1,0:T(8,128)(2,1)S(1)}, bf16[192,512]{1,0:T(8,128)(2,1)S(1)}, u32[]{:S(2)}, u32[]{:S(2)}) collective-permute-start(bf16[192,512]{1,0:T(8,128)(2,1)S(1)} %get-tuple-element.276), channel_id=1, source_target_pairs={{0,4},{1,5},{2,6},{3,7},{4,0},{5,1},{6,2},{7,3},{8,12},{9,13},{10,... | collective-permute-start | bytes 589832 | tf_op jit(solution)/shard_map/ppermute | solution.py:166
  54.5 2.0 %collective-permute-done.25.refs_2_ = bf16[256,512]{1,0:T(8,128)(2,1)S(1)} collective-permute-done((bf16[256,512]{1,0:T(8,128)(2,1)S(1)}, bf16[256,512]{1,0:T(8,128)(2,1)S(1)}, u32[]{:S(2)}, u32[]{:S(2)}) %collective-permute-start.25) | collective-permute-done | bytes 262176 | tf_op jit(solution)/shard_map/ppermute | solution.py:166
  58.2 2.5 %collective-permute-start.29 = (bf16[96,512]{1,0:T(8,128)(2,1)S(1)}, bf16[96,512]{1,0:T(8,128)(2,1)S(1)}, u32[]{:S(2)}, u32[]{:S(2)}) collective-permute-start(bf16[96,512]{1,0:T(8,128)(2,1)S(1)} %get-tuple-element.287), channel_id=1, source_target_pairs={{0,8},{1,9},{2,10},{3,11},{4,12},{5,13},{6,14},{7,15},{8,0},{9,1},... | collective-permute-start | bytes 294920 | tf_op jit(solution)/shard_map/ppermute | solution.py:166
  60.8 1.3 %collective-permute-done.27.refs_2_ = bf16[256,512]{1,0:T(8,128)(2,1)S(1)} collective-permute-done((bf16[256,512]{1,0:T(8,128)(2,1)S(1)}, bf16[256,512]{1,0:T(8,128)(2,1)S(1)}, u32[]{:S(2)}, u32[]{:S(2)}) %collective-permute-start.27) | collective-permute-done | bytes 262176 | tf_op jit(solution)/shard_map/ppermute | solution.py:166
  63.2 1.9 %collective-permute-done.29.refs_1_ = bf16[96,512]{1,0:T(8,128)(2,1)S(1)} collective-permute-done((bf16[96,512]{1,0:T(8,128)(2,1)S(1)}, bf16[96,512]{1,0:T(8,128)(2,1)S(1)}, u32[]{:S(2)}, u32[]{:S(2)}) %collective-permute-start.29) | collective-permute-done | bytes 98336 | tf_op jit(solution)/shard_map/ppermute | solution.py:166
  66.2 2.3 %collective-permute-start.33 = (bf16[64,512]{1,0:T(8,128)(2,1)S(1)}, bf16[64,512]{1,0:T(8,128)(2,1)S(1)}, u32[]{:S(2)}, u32[]{:S(2)}) collective-permute-start(bf16[64,512]{1,0:T(8,128)(2,1)S(1)} %get-tuple-element.303), channel_id=1, source_target_pairs={{0,8},{1,9},{2,10},{3,11},{4,12},{5,13},{6,14},{7,15},{8,0},{9,1},... | collective-permute-start | bytes 196616 | tf_op jit(solution)/shard_map/ppermute | solution.py:166
  69.5 1.2 %collective-permute-done.32.refs_2_ = bf16[96,512]{1,0:T(8,128)(2,1)S(1)} collective-permute-done((bf16[96,512]{1,0:T(8,128)(2,1)S(1)}, bf16[96,512]{1,0:T(8,128)(2,1)S(1)}, u32[]{:S(2)}, u32[]{:S(2)}) %collective-permute-start.32) | collective-permute-done | bytes 98336 | tf_op jit(solution)/shard_map/ppermute | solution.py:166
  70.8 2.7 %collective-permute-done.33.refs_3_ = bf16[64,512]{1,0:T(8,128)(2,1)S(1)} collective-permute-done((bf16[64,512]{1,0:T(8,128)(2,1)S(1)}, bf16[64,512]{1,0:T(8,128)(2,1)S(1)}, u32[]{:S(2)}, u32[]{:S(2)}) %collective-permute-start.33) | collective-permute-done | bytes 65568 | tf_op jit(solution)/shard_map/ppermute | solution.py:166
  73.8 4.6 %collective-permute-done.35.refs_7_ = bf16[48,512]{1,0:T(8,128)(2,1)S(1)} collective-permute-done((bf16[48,512]{1,0:T(8,128)(2,1)S(1)}, bf16[48,512]{1,0:T(8,128)(2,1)S(1)}, u32[]{:S(2)}, u32[]{:S(2)}) %collective-permute-start.35) | collective-permute-done | bytes 49184 | tf_op jit(solution)/shard_map/ppermute | solution.py:166
  78.4 1.2 %finish_all.1 = (bf16[512,512]{1,0:T(8,128)(2,1)}, f32[32,512]{1,0:T(8,128)}, f32[32,512]{1,0:T(8,128)}, f32[2,32,512]{2,1,0:T(8,128)}, f32[2,32,512]{2,1,0:T(8,128)}, /*index=5*/f32[2,32,512]{2,1,0:T(8,128)}) custom-call(bf16[96,512]{1,0:T(8,128)(2,1)S(1)} %get-tuple-element.278.refs_0_, bf16[96,512]{1,0:T(8,128)(2,1)S(1)} %collective-permute-done.29.refs_1_, ...), custom_call_target="tpu_custom_call" | custom-call | flops 134217728 | bytes 2179392 | tf_op jit(solution)/shard_map/finish_all/pallas_call | solution.py:237
  (79 shorter events, 24.0 us)
Async XLA Ops:
  2.1 9.1 %collective-permute-start = (bf16[16,512]{1,0:T(8,128)(2,1)S(1)}, bf16[16,512]{1,0:T(8,128)(2,1)S(1)}, u32[]{:S(2)}, u32[]{:S(2)}) collective-permute-start(bf16[16,512]{1,0:T(8,128)(2,1)S(1)} %get-tuple-element.173), channel_id=1, source_target_pairs={{0,12},{4,8},{8,4},{12,0},{1,13},{5,9},{9,5},{13,1},{2,14},{6,10},... | collective-permute-start | bytes 49160 | tf_op jit(solution)/shard_map/ppermute | solution.py:253
  12.7 5.8 %collective-permute-start.5 = (bf16[32,512]{1,0:T(8,128)(2,1)S(1)}, bf16[32,512]{1,0:T(8,128)(2,1)S(1)}, u32[]{:S(2)}, u32[]{:S(2)}) collective-permute-start(bf16[32,512]{1,0:T(8,128)(2,1)S(1)} %get-tuple-element.185), channel_id=1, source_target_pairs={{0,12},{4,8},{8,4},{12,0},{1,13},{5,9},{9,5},{13,1},{2,14},{6,10},... | collective-permute-start | bytes 98312 | tf_op jit(solution)/shard_map/ppermute | solution.py:253
  13.8 4.7 %collective-permute-start.6 = (bf16[32,512]{1,0:T(8,128)(2,1)S(1)}, bf16[32,512]{1,0:T(8,128)(2,1)S(1)}, u32[]{:S(2)}, u32[]{:S(2)}) collective-permute-start(bf16[32,512]{1,0:T(8,128)(2,1)S(1)} %get-tuple-element.186), channel_id=1, source_target_pairs={{0,4},{4,0},{8,12},{12,8},{1,5},{5,1},{9,13},{13,9},{2,6},{6,2},{1... | collective-permute-start | bytes 98312 | tf_op jit(solution)/shard_map/ppermute | solution.py:254
  20.2 7.6 %collective-permute-start.10 = (bf16[16,512]{1,0:T(8,128)(2,1)S(1)}, bf16[16,512]{1,0:T(8,128)(2,1)S(1)}, u32[]{:S(2)}, u32[]{:S(2)}) collective-permute-start(bf16[16,512]{1,0:T(8,128)(2,1)S(1)} %get-tuple-element.195), channel_id=1, source_target_pairs={{0,12},{4,8},{8,4},{12,0},{1,13},{5,9},{9,5},{13,1},{2,14},{6,10},... | collective-permute-start | bytes 49160 | tf_op jit(solution)/shard_map/ppermute | solution.py:253
  22.9 4.9 %collective-permute-start.11 = (bf16[16,512]{1,0:T(8,128)(2,1)S(1)}, bf16[16,512]{1,0:T(8,128)(2,1)S(1)}, u32[]{:S(2)}, u32[]{:S(2)}) collective-permute-start(bf16[16,512]{1,0:T(8,128)(2,1)S(1)} %get-tuple-element.196), channel_id=1, source_target_pairs={{0,4},{4,0},{8,12},{12,8},{1,5},{5,1},{9,13},{13,9},{2,6},{6,2},{1... | collective-permute-start | bytes 49160 | tf_op jit(solution)/shard_map/ppermute | solution.py:254
  22.9 4.9 %collective-permute-start.12 = (bf16[16,512]{1,0:T(8,128)(2,1)S(1)}, bf16[16,512]{1,0:T(8,128)(2,1)S(1)}, u32[]{:S(2)}, u32[]{:S(2)}) collective-permute-start(bf16[16,512]{1,0:T(8,128)(2,1)S(1)} %get-tuple-element.197), channel_id=1, source_target_pairs={{0,3},{1,2},{2,1},{3,0},{4,7},{5,6},{6,5},{7,4},{8,11},{9,10},{10,... | collective-permute-start | bytes 49160 | tf_op jit(solution)/shard_map/ppermute | solution.py:256
  31.2 6.8 %collective-permute-start.17 = (bf16[8,512]{1,0:T(8,128)(2,1)S(1)}, bf16[8,512]{1,0:T(8,128)(2,1)S(1)}, u32[]{:S(2)}, u32[]{:S(2)}) collective-permute-start(bf16[8,512]{1,0:T(8,128)(2,1)S(1)} %get-tuple-element.232), channel_id=1, source_target_pairs={{0,12},{4,8},{8,4},{12,0},{1,13},{5,9},{9,5},{13,1},{2,14},{6,10},... | collective-permute-start | bytes 24584 | tf_op jit(solution)/shard_map/ppermute | solution.py:253
  32.4 5.6 %collective-permute-start.18 = (bf16[8,512]{1,0:T(8,128)(2,1)S(1)}, bf16[8,512]{1,0:T(8,128)(2,1)S(1)}, u32[]{:S(2)}, u32[]{:S(2)}) collective-permute-start(bf16[8,512]{1,0:T(8,128)(2,1)S(1)} %get-tuple-element.233), channel_id=1, source_target_pairs={{0,4},{4,0},{8,12},{12,8},{1,5},{5,1},{9,13},{13,9},{2,6},{6,2},{1... | collective-permute-start | bytes 24584 | tf_op jit(solution)/shard_map/ppermute | solution.py:254
  33.5 4.5 %collective-permute-start.19 = (bf16[8,512]{1,0:T(8,128)(2,1)S(1)}, bf16[8,512]{1,0:T(8,128)(2,1)S(1)}, u32[]{:S(2)}, u32[]{:S(2)}) collective-permute-start(bf16[8,512]{1,0:T(8,128)(2,1)S(1)} %get-tuple-element.234), channel_id=1, source_target_pairs={{0,3},{1,2},{2,1},{3,0},{4,7},{5,6},{6,5},{7,4},{8,11},{9,10},{10,... | collective-permute-start | bytes 24584 | tf_op jit(solution)/shard_map/ppermute | solution.py:256
  33.5 4.5 %collective-permute-start.20 = (bf16[8,512]{1,0:T(8,128)(2,1)S(1)}, bf16[8,512]{1,0:T(8,128)(2,1)S(1)}, u32[]{:S(2)}, u32[]{:S(2)}) collective-permute-start(bf16[8,512]{1,0:T(8,128)(2,1)S(1)} %get-tuple-element.235), channel_id=1, source_target_pairs={{0,2},{1,3},{2,0},{3,1},{4,6},{5,7},{6,4},{7,5},{8,10},{9,11},{10,... | collective-permute-start | bytes 24584 | tf_op jit(solution)/shard_map/ppermute | solution.py:256
  38.8 12.3 %collective-permute-start.24 = (bf16[512,512]{1,0:T(8,128)(2,1)S(1)}, bf16[512,512]{1,0:T(8,128)(2,1)S(1)}, u32[]{:S(2)}, u32[]{:S(2)}) collective-permute-start(bf16[512,512]{1,0:T(8,128)(2,1)S(1)} %get-tuple-element.268), channel_id=1, source_target_pairs={{0,1},{1,0},{2,3},{3,2},{4,5},{5,4},{6,7},{7,6},{8,9},{9,8},{10,11... | collective-permute-start | bytes 1572872 | tf_op jit(solution)/shard_map/ppermute | solution.py:166
  38.9 11.9 %collective-permute-start.23 = (bf16[384,512]{1,0:T(8,128)(2,1)S(1)}, bf16[384,512]{1,0:T(8,128)(2,1)S(1)}, u32[]{:S(2)}, u32[]{:S(2)}) collective-permute-start(bf16[384,512]{1,0:T(8,128)(2,1)S(1)} %get-tuple-element.260), channel_id=1, source_target_pairs={{0,2},{1,3},{2,0},{3,1},{4,6},{5,7},{6,4},{7,5},{8,10},{9,11},{10,... | collective-permute-start | bytes 1179656 | tf_op jit(solution)/shard_map/ppermute | solution.py:166
  43.0 7.8 %collective-permute-start.22 = (bf16[288,512]{1,0:T(8,128)(2,1)S(1)}, bf16[288,512]{1,0:T(8,128)(2,1)S(1)}, u32[]{:S(2)}, u32[]{:S(2)}) collective-permute-start(bf16[288,512]{1,0:T(8,128)(2,1)S(1)} %get-tuple-element.259), channel_id=1, source_target_pairs={{0,1},{1,0},{2,3},{3,2},{4,5},{5,4},{6,7},{7,6},{8,9},{9,8},{10,11... | collective-permute-start | bytes 884744 | tf_op jit(solution)/shard_map/ppermute | solution.py:166
  43.4 13.1 %collective-permute-start.25 = (bf16[256,512]{1,0:T(8,128)(2,1)S(1)}, bf16[256,512]{1,0:T(8,128)(2,1)S(1)}, u32[]{:S(2)}, u32[]{:S(2)}) collective-permute-start(bf16[256,512]{1,0:T(8,128)(2,1)S(1)} %get-tuple-element.273), channel_id=1, source_target_pairs={{0,2},{1,3},{2,0},{3,1},{4,6},{5,7},{6,4},{7,5},{8,10},{9,11},{10,... | collective-permute-start | bytes 786440 | tf_op jit(solution)/shard_map/ppermute | solution.py:166
  51.5 10.6 %collective-permute-start.27 = (bf16[256,512]{1,0:T(8,128)(2,1)S(1)}, bf16[256,512]{1,0:T(8,128)(2,1)S(1)}, u32[]{:S(2)}, u32[]{:S(2)}) collective-permute-start(bf16[256,512]{1,0:T(8,128)(2,1)S(1)} %get-tuple-element.282), channel_id=1, source_target_pairs={{0,2},{1,3},{2,0},{3,1},{4,6},{5,7},{6,4},{7,5},{8,10},{9,11},{10,... | collective-permute-start | bytes 786440 | tf_op jit(solution)/shard_map/ppermute | solution.py:166
  52.4 5.7 %collective-permute-start.26 = (bf16[192,512]{1,0:T(8,128)(2,1)S(1)}, bf16[192,512]{1,0:T(8,128)(2,1)S(1)}, u32[]{:S(2)}, u32[]{:S(2)}) collective-permute-start(bf16[192,512]{1,0:T(8,128)(2,1)S(1)} %get-tuple-element.276), channel_id=1, source_target_pairs={{0,4},{1,5},{2,6},{3,7},{4,0},{5,1},{6,2},{7,3},{8,12},{9,13},{10,... | collective-permute-start | bytes 589832 | tf_op jit(solution)/shard_map/ppermute | solution.py:166
  53.6 11.6 %collective-permute-start.30 = (bf16[160,512]{1,0:T(8,128)(2,1)S(1)}, bf16[160,512]{1,0:T(8,128)(2,1)S(1)}, u32[]{:S(2)}, u32[]{:S(2)}) collective-permute-start(bf16[160,512]{1,0:T(8,128)(2,1)S(1)} %get-tuple-element.292), channel_id=1, source_target_pairs={{0,2},{1,3},{2,0},{3,1},{4,6},{5,7},{6,4},{7,5},{8,10},{9,11},{10,... | collective-permute-start | bytes 491528 | tf_op jit(solution)/shard_map/ppermute | solution.py:166
  56.5 6.6 %collective-permute-start.28 = (bf16[128,512]{1,0:T(8,128)(2,1)S(1)}, bf16[128,512]{1,0:T(8,128)(2,1)S(1)}, u32[]{:S(2)}, u32[]{:S(2)}) collective-permute-start(bf16[128,512]{1,0:T(8,128)(2,1)S(1)} %get-tuple-element.285), channel_id=1, source_target_pairs={{0,4},{1,5},{2,6},{3,7},{4,0},{5,1},{6,2},{7,3},{8,12},{9,13},{10,... | collective-permute-start | bytes 393224 | tf_op jit(solution)/shard_map/ppermute | solution.py:166
  58.2 6.9 %collective-permute-start.29 = (bf16[96,512]{1,0:T(8,128)(2,1)S(1)}, bf16[96,512]{1,0:T(8,128)(2,1)S(1)}, u32[]{:S(2)}, u32[]{:S(2)}) collective-permute-start(bf16[96,512]{1,0:T(8,128)(2,1)S(1)} %get-tuple-element.287), channel_id=1, source_target_pairs={{0,8},{1,9},{2,10},{3,11},{4,12},{5,13},{6,14},{7,15},{8,0},{9,1},... | collective-permute-start | bytes 294920 | tf_op jit(solution)/shard_map/ppermute | solution.py:166
  62.2 6.3 %collective-permute-start.31 = (bf16[128,512]{1,0:T(8,128)(2,1)S(1)}, bf16[128,512]{1,0:T(8,128)(2,1)S(1)}, u32[]{:S(2)}, u32[]{:S(2)}) collective-permute-start(bf16[128,512]{1,0:T(8,128)(2,1)S(1)} %get-tuple-element.298), channel_id=1, source_target_pairs={{0,4},{1,5},{2,6},{3,7},{4,0},{5,1},{6,2},{7,3},{8,12},{9,13},{10,... | collective-permute-start | bytes 393224 | tf_op jit(solution)/shard_map/ppermute | solution.py:166
  65.3 5.4 %collective-permute-start.32 = (bf16[96,512]{1,0:T(8,128)(2,1)S(1)}, bf16[96,512]{1,0:T(8,128)(2,1)S(1)}, u32[]{:S(2)}, u32[]{:S(2)}) collective-permute-start(bf16[96,512]{1,0:T(8,128)(2,1)S(1)} %get-tuple-element.301), channel_id=1, source_target_pairs={{0,4},{1,5},{2,6},{3,7},{4,0},{5,1},{6,2},{7,3},{8,12},{9,13},{10,... | collective-permute-start | bytes 294920 | tf_op jit(solution)/shard_map/ppermute | solution.py:166
  66.2 7.3 %collective-permute-start.33 = (bf16[64,512]{1,0:T(8,128)(2,1)S(1)}, bf16[64,512]{1,0:T(8,128)(2,1)S(1)}, u32[]{:S(2)}, u32[]{:S(2)}) collective-permute-start(bf16[64,512]{1,0:T(8,128)(2,1)S(1)} %get-tuple-element.303), channel_id=1, source_target_pairs={{0,8},{1,9},{2,10},{3,11},{4,12},{5,13},{6,14},{7,15},{8,0},{9,1},... | collective-permute-start | bytes 196616 | tf_op jit(solution)/shard_map/ppermute | solution.py:166
  68.6 9.9 %collective-permute-start.34 = (bf16[64,512]{1,0:T(8,128)(2,1)S(1)}, bf16[64,512]{1,0:T(8,128)(2,1)S(1)}, u32[]{:S(2)}, u32[]{:S(2)}) collective-permute-start(bf16[64,512]{1,0:T(8,128)(2,1)S(1)} %get-tuple-element.306), channel_id=1, source_target_pairs={{0,8},{1,9},{2,10},{3,11},{4,12},{5,13},{6,14},{7,15},{8,0},{9,1},... | collective-permute-start | bytes 196616 | tf_op jit(solution)/shard_map/ppermute | solution.py:166
  73.4 5.0 %collective-permute-start.35 = (bf16[48,512]{1,0:T(8,128)(2,1)S(1)}, bf16[48,512]{1,0:T(8,128)(2,1)S(1)}, u32[]{:S(2)}, u32[]{:S(2)}) collective-permute-start(bf16[48,512]{1,0:T(8,128)(2,1)S(1)} %get-tuple-element.308), channel_id=1, source_target_pairs={{0,8},{1,9},{2,10},{3,11},{4,12},{5,13},{6,14},{7,15},{8,0},{9,1},... | collective-permute-start | bytes 147464 | tf_op jit(solution)/shard_map/ppermute | solution.py:166
  (15 other events, 59.0 us)

commit v16 on v15

--- a/solution.py
+++ b/solution.py
@@ -780,7 +780,6 @@
         arr2 = swap(give2, 3, dims)
         keep_e, keep2 = lax.optimization_barrier((keep_e, keep2))
         keep_e, give_e, from_near = carry_step(3, keep_e, arr_e, (), place, capacity)
-        give_e, arr0 = lax.optimization_barrier((give_e, arr0))
         arr_e = swap(give_e, 3, dims)
         sums = ((keep1, arr1), (keep0, arr0), (keep2, arr2), (keep_e, arr_e))
     grads = [shape(depth, width, dtype=F32)] * 2 + [shape(2, depth, width, dtype=F32)] * 3

time: 79.8 us -> 78.6 us (0.985)
  waiting for transfers between devices: 22.7 us -> 19.7 us
  starting transfers between devices: 34 us -> 35.7 us
    ppermute x16, waiting for transfers between devices: 21 us -> 18.1 us  [swap(): return lax.ppermute(block, GROUP, [(i, i ^ 1 << bit) for i in range(total)])]
    ppermute x16, starting transfers between devices: 15.3 us -> 17 us  [swap(): return lax.ppermute(block, GROUP, [(i, i ^ 1 << bit) for i in range(total)])]
  transfers between devices with their start and end apart: 36 -> 36, of which waited for: 12 -> 12; matrix products, arithmetic and copies ran while one was open for 0% -> 0% of each run, Pallas kernels for 20% -> 21%
where the time goes in v16:
time: 78.6 us; the launch traced here: 78.4 us
  starting transfers between devices  35.7 us (45%)
  Pallas kernels  21.9 us (28%)
  waiting for transfers between devices  19.7 us (25%)
  between operations  0.94 us (1%)
    pallas_call x24, Pallas kernels, call(): pl.pallas_call(kernel, out_shape=[shape(*a.shape, dtype=a.dtype) for a in...  21.9 us
    ppermute x16, waiting for transfers between devices, swap(): return lax.ppermute(block, GROUP, [(i, i ^ 1 << bit) for i in range(total)])  18.1 us
    ppermute x16, starting transfers between devices, swap(): return lax.ppermute(block, GROUP, [(i, i ^ 1 << bit) for i in range(total)])  17 us
    ppermute x4, starting transfers between devices, exchange(): far = lax.ppermute(parts[column], 'lon', other)  10.1 us
    ppermute x12, starting transfers between devices, exchange(): lax.ppermute(parts[r - 1], COLUMN, [(i, i ^ r) for i in range(column)])  6.89 us
    ppermute x4, starting transfers between devices, exchange(): lax.ppermute(parts[column - 1], 'lon', [(i, i ^ 1) for i in range(count)])  1.8 us
  transfers between devices with their start and end apart: 36, of which 12 were waited for; matrix products, arithmetic and copies ran while one was open for 0% of the time, Pallas kernels for 21%

profile of v16, /device:TPU:0, one launch (start us, length us, event | category | flops | bytes accessed | tf_op | source)
XLA Modules:
  0.0 78.4 jit_solution(7899846220686567507)
XLA Ops:
  0.8 1.3 %first_payload.1 = (s32[6,1,16]{2,1,0:T(1,128)S(1)}, bf16[512,512]{1,0:T(8,128)(2,1)S(1)}, bf16[512,512]{1,0:T(8,128)(2,1)S(1)}, s32[1,512]{1,0:T(1,128)S(1)}, s...) custom-call(s32[6,1,16]{2,1,0:T(1,128)} %bitcast.15, ...), custom_call_target="tpu_custom_call" | custom-call | flops 67108864 | bytes 1139992 | tf_op jit(solution)/shard_map/first_payload/pallas_call | solution.py:237
  2.1 5.1 %collective-permute-start = (bf16[16,512]{1,0:T(8,128)(2,1)S(1)}, bf16[16,512]{1,0:T(8,128)(2,1)S(1)}, u32[]{:S(2)}, u32[]{:S(2)}) collective-permute-start(bf16[16,512]{1,0:T(8,128)(2,1)S(1)} %get-tuple-element.171), channel_id=1, source_target_pairs={{0,12},{4,8},{8,4},{12,0},{1,13},{5,9},{9,5},{13,1},{2,14},{6,10},... | collective-permute-start | bytes 49160 | tf_op jit(solution)/shard_map/ppermute | solution.py:253
  9.1 2.1 %embed_local.1 = (bf16[256,512]{1,0:T(8,128)(2,1)S(1)}, bf16[512,512]{1,0:T(8,128)(2,1)S(1)}, bf16[256,512]{1,0:T(8,128)(2,1)S(1)}, f32[256,512]{1,0:T(8,128)S(1...) custom-call(bf16[256,512]{1,0:T(8,128)(2,1)} %refs_0_.1, ...), custom_call_target="tpu_custom_call" | custom-call | flops 402653184 | bytes 3170544 | tf_op jit(solution)/shard_map/embed_local/pallas_call | solution.py:237
  16.3 1.9 %forward_local.1 = (f32[256,512]{1,0:T(8,128)S(1)}, bf16[6,256,512]{2,1,0:T(8,128)(2,1)S(1)}, f32[40,512]{1,0:T(8,128)S(1)}, bf16[40,512]{1,0:T(8,128)(2,1)S(1)}) custom-call(bf16[256,512]{1,0:T(8,128)(2,1)S(1)} %get-tuple-element.188.state_ref.refs_7_.refs_10_, bf16[2,512,512]{2,1,0:T(8,128)(2,1)S(1)} %copy-done, bf16[2,512,512]{2,1,0:T(8,128)(2,1)S(1)} %copy-done.2, ...), custom_call_target="tpu_custom_call" | custom-call | flops 805306368 | bytes 4593824 | tf_op jit(solution)/shard_map/forward_local/pallas_call | solution.py:237
  20.2 2.7 %collective-permute-start.10 = (bf16[16,512]{1,0:T(8,128)(2,1)S(1)}, bf16[16,512]{1,0:T(8,128)(2,1)S(1)}, u32[]{:S(2)}, u32[]{:S(2)}) collective-permute-start(bf16[16,512]{1,0:T(8,128)(2,1)S(1)} %get-tuple-element.193), channel_id=1, source_target_pairs={{0,12},{4,8},{8,4},{12,0},{1,13},{5,9},{9,5},{13,1},{2,14},{6,10},... | collective-permute-start | bytes 49160 | tf_op jit(solution)/shard_map/ppermute | solution.py:253
  24.8 3.0 %turn_local.1 = (f32[256,512]{1,0:T(8,128)S(1)}, f32[256,512]{1,0:T(8,128)S(1)}, f32[256,512]{1,0:T(8,128)S(1)}, f32[40,512]{1,0:T(8,128)S(1)}, bf16[40,512]{1,0...) custom-call(bf16[256,512]{1,0:T(8,128)(2,1)S(1)} %get-tuple-element., ...), custom_call_target="tpu_custom_call" | custom-call | flops 1342177280 | bytes 5871776 | tf_op jit(solution)/shard_map/turn_local/pallas_call | solution.py:237
  27.8 1.3 %turn_halo.1 = (bf16[256,512]{1,0:T(8,128)(2,1)S(1)}, bf16[256,512]{1,0:T(8,128)(2,1)S(1)}, bf16[256,512]{1,0:T(8,128)(2,1)S(1)}, bf16[256,512]{1,0:T(8,128)(2,1...) custom-call(bf16[16,512]{1,0:T(8,128)(2,1)S(1)} %collective-permute-, ...), custom_call_target="tpu_custom_call" | custom-call | flops 402653184 | bytes 5322912 | tf_op jit(solution)/shard_map/turn_halo/pallas_call | solution.py:237
  29.3 1.5 %last_weights.1 = (bf16[768,512]{1,0:T(8,128)(2,1)S(1)}, bf16[768,512]{1,0:T(8,128)(2,1)S(1)}, bf16[256,512]{1,0:T(8,128)(2,1)}) custom-call(s32[1,6]{1,0:T(1,128)S(1)} %get-tuple-element.170.refs_0_.refs_5_, bf16[256,512]{1,0:T(8,128)(2,1)S(1)} %get-tuple-element.192.state_ref.refs_1_, bf16[256,512]{1,0:T(8,128)(2,1)S(1)} %get-tuple-element.210.refs_2_, ...), custom_call_target="tpu_custom_call" | custom-call | flops 536870912 | bytes 4194328 | tf_op jit(solution)/shard_map/last_weights/pallas_call | solution.py:237
  31.2 1.2 %collective-permute-start.17 = (bf16[8,512]{1,0:T(8,128)(2,1)S(1)}, bf16[8,512]{1,0:T(8,128)(2,1)S(1)}, u32[]{:S(2)}, u32[]{:S(2)}) collective-permute-start(bf16[8,512]{1,0:T(8,128)(2,1)S(1)} %get-tuple-element.230), channel_id=1, source_target_pairs={{0,12},{4,8},{8,4},{12,0},{1,13},{5,9},{9,5},{13,1},{2,14},{6,10},... | collective-permute-start | bytes 24584 | tf_op jit(solution)/shard_map/ppermute | solution.py:253
  33.5 1.1 %collective-permute-start.20 = (bf16[8,512]{1,0:T(8,128)(2,1)S(1)}, bf16[8,512]{1,0:T(8,128)(2,1)S(1)}, u32[]{:S(2)}, u32[]{:S(2)}) collective-permute-start(bf16[8,512]{1,0:T(8,128)(2,1)S(1)} %get-tuple-element.233), channel_id=1, source_target_pairs={{0,2},{1,3},{2,0},{3,1},{4,6},{5,7},{6,4},{7,5},{8,10},{9,11},{10,... | collective-permute-start | bytes 24584 | tf_op jit(solution)/shard_map/ppermute | solution.py:256
  35.1 2.8 %back_local.1 = (f32[256,512]{1,0:T(8,128)S(1)}, bf16[512,512]{1,0:T(8,128)(2,1)S(1)}, bf16[512,512]{1,0:T(8,128)(2,1)S(1)}, bf16[512,512]{1,0:T(8,128)(2,1)S(1)}, bf16[512,512]{1,0:T(8,128)(2,1)S(1)}) custom-call(s32[1,6]{1,0:T(1,128)S(1)} %get-tuple-element.170.refs_0_.refs_5_, bf16[256,512]{1,0:T(8,128)(2,1)S(1)} %get-tuple-element.214.refs_1_, ...), custom_call_target="tpu_custom_call" | custom-call | flops 1342177280 | bytes 8960024 | tf_op jit(solution)/shard_map/back_local/pallas_call | solution.py:237
  40.6 2.3 %embed_back.1 = (bf16[512,512]{1,0:T(8,128)(2,1)S(1)}, bf16[256,512]{1,0:T(8,128)(2,1)S(1)}, bf16[288,512]{1,0:T(8,128)(2,1)S(1)}, bf16[16,512]{1,0:T(8,128)(2,1...) custom-call(bf16[8,512]{1,0:T(8,128)(2,1)S(1)} %collective-permute-d, ...), custom_call_target="tpu_custom_call" | custom-call | flops 805306368 | bytes 6130488 | tf_op jit(solution)/shard_map/embed_back/pallas_call | solution.py:237
  44.7 6.1 %collective-permute-done.23.refs_2_ = bf16[384,512]{1,0:T(8,128)(2,1)S(1)} collective-permute-done((bf16[384,512]{1,0:T(8,128)(2,1)S(1)}, bf16[384,512]{1,0:T(8,128)(2,1)S(1)}, u32[]{:S(2)}, u32[]{:S(2)}) %collective-permute-start.23) | collective-permute-done | bytes 393248 | tf_op jit(solution)/shard_map/ppermute | solution.py:166
  52.4 1.2 %collective-permute-start.26 = (bf16[192,512]{1,0:T(8,128)(2,1)S(1)}, bf16[192,512]{1,0:T(8,128)(2,1)S(1)}, u32[]{:S(2)}, u32[]{:S(2)}) collective-permute-start(bf16[192,512]{1,0:T(8,128)(2,1)S(1)} %get-tuple-element.274), channel_id=1, source_target_pairs={{0,4},{1,5},{2,6},{3,7},{4,0},{5,1},{6,2},{7,3},{8,12},{9,13},{10,... | collective-permute-start | bytes 589832 | tf_op jit(solution)/shard_map/ppermute | solution.py:166
  54.5 2.0 %collective-permute-done.25.refs_2_ = bf16[256,512]{1,0:T(8,128)(2,1)S(1)} collective-permute-done((bf16[256,512]{1,0:T(8,128)(2,1)S(1)}, bf16[256,512]{1,0:T(8,128)(2,1)S(1)}, u32[]{:S(2)}, u32[]{:S(2)}) %collective-permute-start.25) | collective-permute-done | bytes 262176 | tf_op jit(solution)/shard_map/ppermute | solution.py:166
  58.2 2.5 %collective-permute-start.29 = (bf16[96,512]{1,0:T(8,128)(2,1)S(1)}, bf16[96,512]{1,0:T(8,128)(2,1)S(1)}, u32[]{:S(2)}, u32[]{:S(2)}) collective-permute-start(bf16[96,512]{1,0:T(8,128)(2,1)S(1)} %get-tuple-element.285), channel_id=1, source_target_pairs={{0,8},{1,9},{2,10},{3,11},{4,12},{5,13},{6,14},{7,15},{8,0},{9,1},... | collective-permute-start | bytes 294920 | tf_op jit(solution)/shard_map/ppermute | solution.py:166
  60.8 1.3 %collective-permute-done.27.refs_2_ = bf16[256,512]{1,0:T(8,128)(2,1)S(1)} collective-permute-done((bf16[256,512]{1,0:T(8,128)(2,1)S(1)}, bf16[256,512]{1,0:T(8,128)(2,1)S(1)}, u32[]{:S(2)}, u32[]{:S(2)}) %collective-permute-start.27) | collective-permute-done | bytes 262176 | tf_op jit(solution)/shard_map/ppermute | solution.py:166
  63.2 1.9 %collective-permute-done.29.refs_1_ = bf16[96,512]{1,0:T(8,128)(2,1)S(1)} collective-permute-done((bf16[96,512]{1,0:T(8,128)(2,1)S(1)}, bf16[96,512]{1,0:T(8,128)(2,1)S(1)}, u32[]{:S(2)}, u32[]{:S(2)}) %collective-permute-start.29) | collective-permute-done | bytes 98336 | tf_op jit(solution)/shard_map/ppermute | solution.py:166
  66.2 2.3 %collective-permute-start.30 = (bf16[64,512]{1,0:T(8,128)(2,1)S(1)}, bf16[64,512]{1,0:T(8,128)(2,1)S(1)}, u32[]{:S(2)}, u32[]{:S(2)}) collective-permute-start(bf16[64,512]{1,0:T(8,128)(2,1)S(1)} %get-tuple-element.288), channel_id=1, source_target_pairs={{0,8},{1,9},{2,10},{3,11},{4,12},{5,13},{6,14},{7,15},{8,0},{9,1},... | collective-permute-start | bytes 196616 | tf_op jit(solution)/shard_map/ppermute | solution.py:166
  69.5 1.2 %collective-permute-done.34.refs_2_ = bf16[96,512]{1,0:T(8,128)(2,1)S(1)} collective-permute-done((bf16[96,512]{1,0:T(8,128)(2,1)S(1)}, bf16[96,512]{1,0:T(8,128)(2,1)S(1)}, u32[]{:S(2)}, u32[]{:S(2)}) %collective-permute-start.34) | collective-permute-done | bytes 98336 | tf_op jit(solution)/shard_map/ppermute | solution.py:166
  70.8 2.1 %collective-permute-start.35 = (bf16[48,512]{1,0:T(8,128)(2,1)S(1)}, bf16[48,512]{1,0:T(8,128)(2,1)S(1)}, u32[]{:S(2)}, u32[]{:S(2)}) collective-permute-start(bf16[48,512]{1,0:T(8,128)(2,1)S(1)} %get-tuple-element.304), channel_id=1, source_target_pairs={{0,8},{1,9},{2,10},{3,11},{4,12},{5,13},{6,14},{7,15},{8,0},{9,1},... | collective-permute-start | bytes 147464 | tf_op jit(solution)/shard_map/ppermute | solution.py:166
  72.8 1.8 %collective-permute-done.30.refs_3_ = bf16[64,512]{1,0:T(8,128)(2,1)S(1)} collective-permute-done((bf16[64,512]{1,0:T(8,128)(2,1)S(1)}, bf16[64,512]{1,0:T(8,128)(2,1)S(1)}, u32[]{:S(2)}, u32[]{:S(2)}) %collective-permute-start.30) | collective-permute-done | bytes 65568 | tf_op jit(solution)/shard_map/ppermute | solution.py:166
  74.7 2.6 %collective-permute-done.35.refs_7_ = bf16[48,512]{1,0:T(8,128)(2,1)S(1)} collective-permute-done((bf16[48,512]{1,0:T(8,128)(2,1)S(1)}, bf16[48,512]{1,0:T(8,128)(2,1)S(1)}, u32[]{:S(2)}, u32[]{:S(2)}) %collective-permute-start.35) | collective-permute-done | bytes 49184 | tf_op jit(solution)/shard_map/ppermute | solution.py:166
  77.2 1.2 %finish_all.1 = (bf16[512,512]{1,0:T(8,128)(2,1)}, f32[32,512]{1,0:T(8,128)}, f32[32,512]{1,0:T(8,128)}, f32[2,32,512]{2,1,0:T(8,128)}, f32[2,32,512]{2,1,0:T(8,128)}, /*index=5*/f32[2,32,512]{2,1,0:T(8,128)}) custom-call(bf16[96,512]{1,0:T(8,128)(2,1)S(1)} %get-tuple-element.276.refs_0_, bf16[96,512]{1,0:T(8,128)(2,1)S(1)} %collective-permute-done.29.refs_1_, ...), custom_call_target="tpu_custom_call" | custom-call | flops 134217728 | bytes 2179392 | tf_op jit(solution)/shard_map/finish_all/pallas_call | solution.py:237
  (79 shorter events, 24.8 us)
Async XLA Ops:
  2.1 9.1 %collective-permute-start = (bf16[16,512]{1,0:T(8,128)(2,1)S(1)}, bf16[16,512]{1,0:T(8,128)(2,1)S(1)}, u32[]{:S(2)}, u32[]{:S(2)}) collective-permute-start(bf16[16,512]{1,0:T(8,128)(2,1)S(1)} %get-tuple-element.171), channel_id=1, source_target_pairs={{0,12},{4,8},{8,4},{12,0},{1,13},{5,9},{9,5},{13,1},{2,14},{6,10},... | collective-permute-start | bytes 49160 | tf_op jit(solution)/shard_map/ppermute | solution.py:253
  12.7 5.8 %collective-permute-start.5 = (bf16[32,512]{1,0:T(8,128)(2,1)S(1)}, bf16[32,512]{1,0:T(8,128)(2,1)S(1)}, u32[]{:S(2)}, u32[]{:S(2)}) collective-permute-start(bf16[32,512]{1,0:T(8,128)(2,1)S(1)} %get-tuple-element.183), channel_id=1, source_target_pairs={{0,12},{4,8},{8,4},{12,0},{1,13},{5,9},{9,5},{13,1},{2,14},{6,10},... | collective-permute-start | bytes 98312 | tf_op jit(solution)/shard_map/ppermute | solution.py:253
  13.8 4.7 %collective-permute-start.6 = (bf16[32,512]{1,0:T(8,128)(2,1)S(1)}, bf16[32,512]{1,0:T(8,128)(2,1)S(1)}, u32[]{:S(2)}, u32[]{:S(2)}) collective-permute-start(bf16[32,512]{1,0:T(8,128)(2,1)S(1)} %get-tuple-element.184), channel_id=1, source_target_pairs={{0,4},{4,0},{8,12},{12,8},{1,5},{5,1},{9,13},{13,9},{2,6},{6,2},{1... | collective-permute-start | bytes 98312 | tf_op jit(solution)/shard_map/ppermute | solution.py:254
  20.2 7.6 %collective-permute-start.10 = (bf16[16,512]{1,0:T(8,128)(2,1)S(1)}, bf16[16,512]{1,0:T(8,128)(2,1)S(1)}, u32[]{:S(2)}, u32[]{:S(2)}) collective-permute-start(bf16[16,512]{1,0:T(8,128)(2,1)S(1)} %get-tuple-element.193), channel_id=1, source_target_pairs={{0,12},{4,8},{8,4},{12,0},{1,13},{5,9},{9,5},{13,1},{2,14},{6,10},... | collective-permute-start | bytes 49160 | tf_op jit(solution)/shard_map/ppermute | solution.py:253
  22.9 4.9 %collective-permute-start.11 = (bf16[16,512]{1,0:T(8,128)(2,1)S(1)}, bf16[16,512]{1,0:T(8,128)(2,1)S(1)}, u32[]{:S(2)}, u32[]{:S(2)}) collective-permute-start(bf16[16,512]{1,0:T(8,128)(2,1)S(1)} %get-tuple-element.194), channel_id=1, source_target_pairs={{0,4},{4,0},{8,12},{12,8},{1,5},{5,1},{9,13},{13,9},{2,6},{6,2},{1... | collective-permute-start | bytes 49160 | tf_op jit(solution)/shard_map/ppermute | solution.py:254
  22.9 4.9 %collective-permute-start.12 = (bf16[16,512]{1,0:T(8,128)(2,1)S(1)}, bf16[16,512]{1,0:T(8,128)(2,1)S(1)}, u32[]{:S(2)}, u32[]{:S(2)}) collective-permute-start(bf16[16,512]{1,0:T(8,128)(2,1)S(1)} %get-tuple-element.195), channel_id=1, source_target_pairs={{0,3},{1,2},{2,1},{3,0},{4,7},{5,6},{6,5},{7,4},{8,11},{9,10},{10,... | collective-permute-start | bytes 49160 | tf_op jit(solution)/shard_map/ppermute | solution.py:256
  31.2 6.8 %collective-permute-start.17 = (bf16[8,512]{1,0:T(8,128)(2,1)S(1)}, bf16[8,512]{1,0:T(8,128)(2,1)S(1)}, u32[]{:S(2)}, u32[]{:S(2)}) collective-permute-start(bf16[8,512]{1,0:T(8,128)(2,1)S(1)} %get-tuple-element.230), channel_id=1, source_target_pairs={{0,12},{4,8},{8,4},{12,0},{1,13},{5,9},{9,5},{13,1},{2,14},{6,10},... | collective-permute-start | bytes 24584 | tf_op jit(solution)/shard_map/ppermute | solution.py:253
  32.4 5.6 %collective-permute-start.18 = (bf16[8,512]{1,0:T(8,128)(2,1)S(1)}, bf16[8,512]{1,0:T(8,128)(2,1)S(1)}, u32[]{:S(2)}, u32[]{:S(2)}) collective-permute-start(bf16[8,512]{1,0:T(8,128)(2,1)S(1)} %get-tuple-element.231), channel_id=1, source_target_pairs={{0,4},{4,0},{8,12},{12,8},{1,5},{5,1},{9,13},{13,9},{2,6},{6,2},{1... | collective-permute-start | bytes 24584 | tf_op jit(solution)/shard_map/ppermute | solution.py:254
  33.5 4.5 %collective-permute-start.19 = (bf16[8,512]{1,0:T(8,128)(2,1)S(1)}, bf16[8,512]{1,0:T(8,128)(2,1)S(1)}, u32[]{:S(2)}, u32[]{:S(2)}) collective-permute-start(bf16[8,512]{1,0:T(8,128)(2,1)S(1)} %get-tuple-element.232), channel_id=1, source_target_pairs={{0,3},{1,2},{2,1},{3,0},{4,7},{5,6},{6,5},{7,4},{8,11},{9,10},{10,... | collective-permute-start | bytes 24584 | tf_op jit(solution)/shard_map/ppermute | solution.py:256
  33.5 4.5 %collective-permute-start.20 = (bf16[8,512]{1,0:T(8,128)(2,1)S(1)}, bf16[8,512]{1,0:T(8,128)(2,1)S(1)}, u32[]{:S(2)}, u32[]{:S(2)}) collective-permute-start(bf16[8,512]{1,0:T(8,128)(2,1)S(1)} %get-tuple-element.233), channel_id=1, source_target_pairs={{0,2},{1,3},{2,0},{3,1},{4,6},{5,7},{6,4},{7,5},{8,10},{9,11},{10,... | collective-permute-start | bytes 24584 | tf_op jit(solution)/shard_map/ppermute | solution.py:256
  38.8 12.3 %collective-permute-start.24 = (bf16[512,512]{1,0:T(8,128)(2,1)S(1)}, bf16[512,512]{1,0:T(8,128)(2,1)S(1)}, u32[]{:S(2)}, u32[]{:S(2)}) collective-permute-start(bf16[512,512]{1,0:T(8,128)(2,1)S(1)} %get-tuple-element.266), channel_id=1, source_target_pairs={{0,1},{1,0},{2,3},{3,2},{4,5},{5,4},{6,7},{7,6},{8,9},{9,8},{10,11... | collective-permute-start | bytes 1572872 | tf_op jit(solution)/shard_map/ppermute | solution.py:166
  38.9 11.9 %collective-permute-start.23 = (bf16[384,512]{1,0:T(8,128)(2,1)S(1)}, bf16[384,512]{1,0:T(8,128)(2,1)S(1)}, u32[]{:S(2)}, u32[]{:S(2)}) collective-permute-start(bf16[384,512]{1,0:T(8,128)(2,1)S(1)} %get-tuple-element.258), channel_id=1, source_target_pairs={{0,2},{1,3},{2,0},{3,1},{4,6},{5,7},{6,4},{7,5},{8,10},{9,11},{10,... | collective-permute-start | bytes 1179656 | tf_op jit(solution)/shard_map/ppermute | solution.py:166
  43.0 7.8 %collective-permute-start.22 = (bf16[288,512]{1,0:T(8,128)(2,1)S(1)}, bf16[288,512]{1,0:T(8,128)(2,1)S(1)}, u32[]{:S(2)}, u32[]{:S(2)}) collective-permute-start(bf16[288,512]{1,0:T(8,128)(2,1)S(1)} %get-tuple-element.257), channel_id=1, source_target_pairs={{0,1},{1,0},{2,3},{3,2},{4,5},{5,4},{6,7},{7,6},{8,9},{9,8},{10,11... | collective-permute-start | bytes 884744 | tf_op jit(solution)/shard_map/ppermute | solution.py:166
  43.4 13.1 %collective-permute-start.25 = (bf16[256,512]{1,0:T(8,128)(2,1)S(1)}, bf16[256,512]{1,0:T(8,128)(2,1)S(1)}, u32[]{:S(2)}, u32[]{:S(2)}) collective-permute-start(bf16[256,512]{1,0:T(8,128)(2,1)S(1)} %get-tuple-element.271), channel_id=1, source_target_pairs={{0,2},{1,3},{2,0},{3,1},{4,6},{5,7},{6,4},{7,5},{8,10},{9,11},{10,... | collective-permute-start | bytes 786440 | tf_op jit(solution)/shard_map/ppermute | solution.py:166
  51.5 10.6 %collective-permute-start.27 = (bf16[256,512]{1,0:T(8,128)(2,1)S(1)}, bf16[256,512]{1,0:T(8,128)(2,1)S(1)}, u32[]{:S(2)}, u32[]{:S(2)}) collective-permute-start(bf16[256,512]{1,0:T(8,128)(2,1)S(1)} %get-tuple-element.280), channel_id=1, source_target_pairs={{0,2},{1,3},{2,0},{3,1},{4,6},{5,7},{6,4},{7,5},{8,10},{9,11},{10,... | collective-permute-start | bytes 786440 | tf_op jit(solution)/shard_map/ppermute | solution.py:166
  52.4 5.7 %collective-permute-start.26 = (bf16[192,512]{1,0:T(8,128)(2,1)S(1)}, bf16[192,512]{1,0:T(8,128)(2,1)S(1)}, u32[]{:S(2)}, u32[]{:S(2)}) collective-permute-start(bf16[192,512]{1,0:T(8,128)(2,1)S(1)} %get-tuple-element.274), channel_id=1, source_target_pairs={{0,4},{1,5},{2,6},{3,7},{4,0},{5,1},{6,2},{7,3},{8,12},{9,13},{10,... | collective-permute-start | bytes 589832 | tf_op jit(solution)/shard_map/ppermute | solution.py:166
  53.6 11.6 %collective-permute-start.31 = (bf16[160,512]{1,0:T(8,128)(2,1)S(1)}, bf16[160,512]{1,0:T(8,128)(2,1)S(1)}, u32[]{:S(2)}, u32[]{:S(2)}) collective-permute-start(bf16[160,512]{1,0:T(8,128)(2,1)S(1)} %get-tuple-element.291), channel_id=1, source_target_pairs={{0,2},{1,3},{2,0},{3,1},{4,6},{5,7},{6,4},{7,5},{8,10},{9,11},{10,... | collective-permute-start | bytes 491528 | tf_op jit(solution)/shard_map/ppermute | solution.py:166
  56.5 6.6 %collective-permute-start.28 = (bf16[128,512]{1,0:T(8,128)(2,1)S(1)}, bf16[128,512]{1,0:T(8,128)(2,1)S(1)}, u32[]{:S(2)}, u32[]{:S(2)}) collective-permute-start(bf16[128,512]{1,0:T(8,128)(2,1)S(1)} %get-tuple-element.283), channel_id=1, source_target_pairs={{0,4},{1,5},{2,6},{3,7},{4,0},{5,1},{6,2},{7,3},{8,12},{9,13},{10,... | collective-permute-start | bytes 393224 | tf_op jit(solution)/shard_map/ppermute | solution.py:166
  58.2 6.9 %collective-permute-start.29 = (bf16[96,512]{1,0:T(8,128)(2,1)S(1)}, bf16[96,512]{1,0:T(8,128)(2,1)S(1)}, u32[]{:S(2)}, u32[]{:S(2)}) collective-permute-start(bf16[96,512]{1,0:T(8,128)(2,1)S(1)} %get-tuple-element.285), channel_id=1, source_target_pairs={{0,8},{1,9},{2,10},{3,11},{4,12},{5,13},{6,14},{7,15},{8,0},{9,1},... | collective-permute-start | bytes 294920 | tf_op jit(solution)/shard_map/ppermute | solution.py:166
  62.2 6.3 %collective-permute-start.32 = (bf16[128,512]{1,0:T(8,128)(2,1)S(1)}, bf16[128,512]{1,0:T(8,128)(2,1)S(1)}, u32[]{:S(2)}, u32[]{:S(2)}) collective-permute-start(bf16[128,512]{1,0:T(8,128)(2,1)S(1)} %get-tuple-element.297), channel_id=1, source_target_pairs={{0,4},{1,5},{2,6},{3,7},{4,0},{5,1},{6,2},{7,3},{8,12},{9,13},{10,... | collective-permute-start | bytes 393224 | tf_op jit(solution)/shard_map/ppermute | solution.py:166
  65.3 5.4 %collective-permute-start.34 = (bf16[96,512]{1,0:T(8,128)(2,1)S(1)}, bf16[96,512]{1,0:T(8,128)(2,1)S(1)}, u32[]{:S(2)}, u32[]{:S(2)}) collective-permute-start(bf16[96,512]{1,0:T(8,128)(2,1)S(1)} %get-tuple-element.302), channel_id=1, source_target_pairs={{0,4},{1,5},{2,6},{3,7},{4,0},{5,1},{6,2},{7,3},{8,12},{9,13},{10,... | collective-permute-start | bytes 294920 | tf_op jit(solution)/shard_map/ppermute | solution.py:166
  66.2 8.5 %collective-permute-start.30 = (bf16[64,512]{1,0:T(8,128)(2,1)S(1)}, bf16[64,512]{1,0:T(8,128)(2,1)S(1)}, u32[]{:S(2)}, u32[]{:S(2)}) collective-permute-start(bf16[64,512]{1,0:T(8,128)(2,1)S(1)} %get-tuple-element.288), channel_id=1, source_target_pairs={{0,8},{1,9},{2,10},{3,11},{4,12},{5,13},{6,14},{7,15},{8,0},{9,1},... | collective-permute-start | bytes 196616 | tf_op jit(solution)/shard_map/ppermute | solution.py:166
  68.6 8.7 %collective-permute-start.33 = (bf16[64,512]{1,0:T(8,128)(2,1)S(1)}, bf16[64,512]{1,0:T(8,128)(2,1)S(1)}, u32[]{:S(2)}, u32[]{:S(2)}) collective-permute-start(bf16[64,512]{1,0:T(8,128)(2,1)S(1)} %get-tuple-element.300), channel_id=1, source_target_pairs={{0,8},{1,9},{2,10},{3,11},{4,12},{5,13},{6,14},{7,15},{8,0},{9,1},... | collective-permute-start | bytes 196616 | tf_op jit(solution)/shard_map/ppermute | solution.py:166
  70.8 6.5 %collective-permute-start.35 = (bf16[48,512]{1,0:T(8,128)(2,1)S(1)}, bf16[48,512]{1,0:T(8,128)(2,1)S(1)}, u32[]{:S(2)}, u32[]{:S(2)}) collective-permute-start(bf16[48,512]{1,0:T(8,128)(2,1)S(1)} %get-tuple-element.304), channel_id=1, source_target_pairs={{0,8},{1,9},{2,10},{3,11},{4,12},{5,13},{6,14},{7,15},{8,0},{9,1},... | collective-permute-start | bytes 147464 | tf_op jit(solution)/shard_map/ppermute | solution.py:166
  (15 other events, 59.0 us)

commit v17 on v16

--- a/solution.py
+++ b/solution.py
@@ -294,8 +294,8 @@
 def embed_local(
     column, mesh_far, merge_far, cot_far, place_in_ref, raw_sends_ref, raw_incoming_ref,
     raw_bounds_ref, senders_ref, grid_ref, weight_ref, target_ref, sends_ref, mesh_ref, merge_ref,
-    cot_ref, sum_ref, slope_ref, sends_row_ref, incoming_ref, bounds_ref, bounds_row_ref, senders_t_ref,
-    senders_out_ref, place_ref, sems,
+    cot_ref, sum_ref, slope_ref, sends_row_ref, incoming_ref, border_ref, border_t_ref, back_ref,
+    back_t_ref, senders_t_ref, senders_out_ref, place_ref, sems,
 ):
     loads = start_loads((mesh_far, merge_far, cot_far), (mesh_ref, merge_ref, cot_ref), sems)
     chosen = grid_ref.shape[0]
@@ -312,9 +312,13 @@
     bounds = slot_rows(raw_bounds_ref)
     capacity = incoming.shape[1]
     sends_row_ref[...] = as_row(raw_sends, capacity, column, me, odd)
-    incoming_ref[...] = as_row(incoming, capacity, column, me, odd)
-    bounds_ref[...] = as_column(bounds, BORDER, column, me, odd)
-    bounds_row_ref[...] = as_row(bounds, BORDER, column, me, odd)
+    halo = border_ref.shape[0]
+    incoming = as_row(incoming, capacity, column, me, odd)
+    incoming_ref[...] = low(hot(incoming == iota(nodes, taken, 0)))
+    border = as_column(bounds, BORDER, column, me, odd)
+    border_ref[...] = low(hot(border == iota(halo, nodes, 1)))
+    border = as_row(bounds, BORDER, column, me, odd)
+    border_t_ref[...] = low(hot(border == iota(nodes, halo, 0)))
     senders = senders_ref[...]
     degree = senders.shape[0]
     offset = senders - nodes
@@ -324,29 +328,27 @@
     senders = jnp.where(offset < 0, senders, nodes + at * BORDER + offset % BORDER)
     senders_t_ref[...] = senders
     filler = jnp.zeros((8 - degree, nodes), I32)
-    senders_out_ref[...] = jnp.concatenate([senders, filler], axis=0).T
+    back_ref[...] = low(receivers(senders, halo))
+    senders_t = jnp.concatenate([senders, filler], axis=0).T
+    senders_out_ref[...] = senders_t
+    back_t_ref[...] = low(receivers_t(senders_t, degree, halo))
     for load in loads:
         load.wait()
 
 
 def merge_nodes(peers, *refs):
     arr_refs, refs = refs[:peers][::-1], refs[peers:]
-    (incoming_ref, embed_ref, local_ref, mesh_ref, weight_ref, bounds_ref, senders_t_ref, cot_ref,
+    (incoming_ref, embed_ref, local_ref, mesh_ref, weight_ref, border_ref, back_ref, cot_ref,
      merged_ref, state_ref, slope_ref, lat_ref, *pay_refs) = refs
-    nodes = mesh_ref.shape[0]
-    taken = incoming_ref.shape[1]
-    halo = peers * BORDER
     lat = jnp.concatenate([ref[...] for ref in arr_refs], axis=0)
     lat_ref[...] = lat
     act, slope = silu_both(dot(lat, embed_ref[...]))
     slope_ref[...] = low(slope)
-    place = low(hot(incoming_ref[...] == iota(nodes, taken, 0)))
-    merged = low(local_ref[...] + dot(place, low(act)))
+    merged = low(local_ref[...] + dot(incoming_ref[...], low(act)))
     merged_ref[...] = merged
     state = low(mesh_ref[...].astype(F32) + dot(merged, weight_ref[...]))
     state_ref[...] = state
-    border = low(hot(bounds_ref[...] == iota(halo, nodes, 1)))
-    back = low(receivers(senders_t_ref[...], halo))
+    border, back = border_ref[...], back_ref[...]
     store_parts(
         pay_refs,
         [dot(border, state), dot(back, state), dot(border, merged), dot(back, cot_ref[...])],
@@ -373,12 +375,10 @@
 
 
 def forward_local(
-    state_ref, send_ref, recv_ref, senders_ref, senders_t_ref, bounds_ref,
-    total_ref, slope_ref, recv_n_ref, sent_b_ref,
+    state_ref, send_ref, recv_ref, update_ref, cot_ref, senders_ref, senders_t_ref, border_ref,
+    back_ref, total_ref, slope_ref, recv_n_ref, sent_b_ref, gsum_ref, targets_ref,
 ):
     state = state_ref[...]
-    nodes = state.shape[0]
-    halo = bounds_ref.shape[0]
     sent = low(dot(state, send_ref[0]))
     recv = dot(state, recv_ref[0])
 
@@ -386,19 +386,17 @@
         slope_ref[j] = low(slope)
 
     total_ref[...] = local_edges(senders_ref[...], senders_t_ref.shape[0], sent, recv, keep)
-    back = low(receivers(senders_t_ref[...], halo))
-    recv_n_ref[...] = dot(low(dot(back, state)), recv_ref[0])
-    sent_b_ref[...] = low(dot(low(hot(bounds_ref[...] == iota(halo, nodes, 1))), sent))
+    recv_n_ref[...] = dot(low(dot(back_ref[...], state)), recv_ref[0])
+    sent_b_ref[...] = low(dot(border_ref[...], sent))
+    gsum_ref[...] = low(dot(cot_ref[...], update_ref[1], NT))
+    targets_ref[...] = edge_targets(senders_t_ref[...])
 
 
 def forward_halo(peers, *refs):
     arr_refs, refs = refs[:peers][::-1], refs[peers:]
-    (recv_n_ref, total_ref, state_ref, send_ref, update_ref, senders_ref, senders_t_ref,
-     bounds_ref, summed_ref, out_ref, pre_ref, rows_ref, back_ref, merged_ref, cot_ref,
+    (recv_n_ref, total_ref, state_ref, send_ref, update_ref, back_t_ref, back_in_ref,
+     border_ref, summed_ref, out_ref, pre_ref, rows_ref, back_ref, merged_ref, cot_ref,
      *pay_refs) = refs
-    nodes = state_ref.shape[0]
-    degree = senders_t_ref.shape[0]
-    halo = peers * BORDER
     rows, back, merged, cot = split_parts(
         arr_refs, (0, BORDER, 2 * BORDER, 3 * BORDER), (BORDER,) * 4
     )
@@ -406,24 +404,21 @@
     merged_ref[...], cot_ref[...] = low(merged), low(cot)
     pre = low(dot(low(rows), send_ref[0])).astype(F32) + recv_n_ref[...]
     pre_ref[...] = pre
-    place = low(receivers_t(senders_ref[...], degree, halo))
+    place = back_t_ref[...]
     extra = silu(pre) - silu(recv_n_ref[...])
     summed = low(total_ref[...] + dot(place, low(extra)))
     summed_ref[...] = summed
     state = low(state_ref[...].astype(F32) + dot(summed, update_ref[0]))
     out_ref[...] = state
-    border = low(hot(bounds_ref[...] == iota(halo, nodes, 1)))
-    back = low(receivers(senders_t_ref[...], halo))
-    store_parts(pay_refs, [dot(border, state), dot(back, state)])
+    store_parts(pay_refs, [dot(border_ref[...], state), dot(back_in_ref[...], state)])
 
 
 def turn_local(
-    state_ref, send_ref, recv_ref, update_ref, cot_ref, cot_r_ref, pre_ref, recv_n0_ref, back0_ref,
-    sent_b0_ref, senders_ref, senders_t_ref, bounds_ref,
+    state_ref, send_ref, recv_ref, update_ref, gsum_ref, cot_r_ref, pre_ref, recv_n0_ref, back0_ref,
+    sent_b0_ref, senders_ref, targets_ref, border_ref, back_ref,
     total_ref, grecv_ref, gsent_ref, recv_n_ref, sent_b_ref, gsum_n_ref, gsum_r_ref,
     slope_k_ref, slope_d_ref, slope_r_ref, gpre_ref,
 ):
-    halo = bounds_ref.shape[0]
     slope = silu_slope(pre_ref[...])
     slope_k_ref[...] = low(slope)
     slope_d_ref[...] = low(slope - silu_slope(recv_n0_ref[...]))
@@ -433,7 +428,7 @@
     nodes = state.shape[0]
     sent = low(dot(state, send_ref[1]))
     recv = dot(state, recv_ref[1])
-    gsum = low(dot(cot_ref[...], update_ref[1], NT))
+    gsum = gsum_ref[...]
     grad = gsum.astype(F32)
     grecv = []
 
@@ -442,13 +437,13 @@
         grecv.append(gpre if j == 0 else grecv[-1] + gpre)
         gpre_ref[j * nodes : (j + 1) * nodes, :] = low(gpre)
 
-    degree = senders_t_ref.shape[0]
+    degree = targets_ref.shape[1] // nodes
     total_ref[...] = local_edges(senders_ref[...], degree, sent, recv, back_edge)
     grecv_ref[...] = grecv[-1]
-    gsent_ref[...] = dot(edge_targets(senders_t_ref[...]), gpre_ref[...])
-    back = low(receivers(senders_t_ref[...], halo))
+    gsent_ref[...] = dot(targets_ref[...], gpre_ref[...])
+    back = back_ref[...]
     recv_n_ref[...] = dot(low(dot(back, state)), recv_ref[1])
-    sent_b_ref[...] = low(dot(low(hot(bounds_ref[...] == iota(halo, nodes, 1))), sent))
+    sent_b_ref[...] = low(dot(border_ref[...], sent))
     gsum_n_ref[...] = low(dot(back, gsum))
     gsum_r_ref[...] = low(dot(cot_r_ref[...], update_ref[1], NT))
 
@@ -456,26 +451,22 @@
 def turn_halo(peers, *refs):
     arr_refs, refs = refs[:peers][::-1], refs[peers:]
     (recv_n_ref, sent_b_ref, gsum_n_ref, gsum_r_ref, total_ref, grecv_ref, gsent_ref, cot_ref,
-     send_ref, recv_ref, senders_ref, senders_t_ref, bounds_ref, summed_ref, grecv_out_ref,
+     send_ref, recv_ref, back_t_ref, back_in_ref, border_t_ref, summed_ref, grecv_out_ref,
      gsent_out_ref, gin_ref, *pay_refs) = refs
-    nodes = cot_ref.shape[0]
-    degree = senders_t_ref.shape[0]
-    halo = peers * BORDER
     rows, back = split_parts(arr_refs, (0, BORDER), (BORDER,) * 2)
     pre = low(dot(low(rows), send_ref[1])).astype(F32) + recv_n_ref[...]
     act, slope = silu_both(pre)
-    place = low(receivers_t(senders_ref[...], degree, halo))
+    place = back_t_ref[...]
     base, base_slope = silu_both(recv_n_ref[...])
     gpre = low(gsum_n_ref[...].astype(F32) * (slope - base_slope))
     grecv = low(grecv_ref[...] + dot(place, gpre))
     pre = sent_b_ref[...].astype(F32) + dot(low(back), recv_ref[1])
     gpre = low(gsum_r_ref[...].astype(F32) * silu_slope(pre))
-    border = low(hot(bounds_ref[...] == iota(nodes, halo, 0)))
-    gsent = low(gsent_ref[...] + dot(border, gpre))
+    gsent = low(gsent_ref[...] + dot(border_t_ref[...], gpre))
     gin = cot_ref[...].astype(F32) + dot(grecv, recv_ref[1], NT) + dot(gsent, send_ref[1], NT)
     gin = low(gin)
     gin_ref[...] = gin
-    store_parts(pay_refs, [dot(low(receivers(senders_t_ref[...], halo)), gin)])
+    store_parts(pay_refs, [dot(back_in_ref[...], gin)])
     summed_ref[...] = low(total_ref[...] + dot(place, low(act - base)))
     grecv_out_ref[...] = grecv
     gsent_out_ref[...] = gsent
@@ -499,16 +490,14 @@
 
 def back_local(
     dims, place_ref, gin_ref, slope_ref, slope_k_ref, slope_d_ref, send_ref, recv_ref, update_ref,
-    senders_ref, senders_t_ref, state_ref, rows_ref, summed_ref, merged_ref, merged_r_ref,
+    back_t_ref, back_ref, targets_ref, state_ref, rows_ref, summed_ref, merged_ref, merged_r_ref,
     after_ref, part_ref, keep_ref, give_ref, keep2_ref, give2_ref, gpre_ref,
 ):
     nodes = gin_ref.shape[0]
-    halo = slope_k_ref.shape[0]
-    degree = senders_t_ref.shape[0]
+    degree = slope_ref.shape[0]
     gin = gin_ref[...]
     gsum = low(dot(gin, update_ref[0], NT))
-    place = low(receivers_t(senders_ref[...], degree, halo))
-    back = low(receivers(senders_t_ref[...], halo))
+    place, back = back_t_ref[...], back_ref[...]
     gsum_n = low(dot(back, gsum))
     gpre_k = gsum_n * slope_k_ref[...]
     grecv = dot(place, gsum_n * slope_d_ref[...])
@@ -516,7 +505,7 @@
         gpre = gsum * slope_ref[j]
         grecv = grecv + gpre.astype(F32)
         gpre_ref[j * nodes : (j + 1) * nodes, :] = gpre
-    gsent = dot(edge_targets(senders_t_ref[...]), gpre_ref[...])
+    gsent = dot(targets_ref[...], gpre_ref[...])
     grecv, gsent = low(grecv), low(gsent)
     part = gin.astype(F32) + dot(grecv, recv_ref[0], NT) + dot(gsent, send_ref[0], NT)
     part_ref[...] = part
@@ -538,22 +527,19 @@
 
 def embed_back(peers, dims, carry, *refs):
     arr_refs, refs = refs[:peers][::-1], refs[peers:]
-    (place_ref, slope_r_ref, part_ref, update_ref, send_ref, merge_ref, bounds_ref, target_ref,
+    (place_ref, slope_r_ref, part_ref, update_ref, send_ref, merge_ref, border_t_ref, target_ref,
      sends_ref, incoming_ref, slope_g_ref, slope_a_ref, grid_ref, lat_ref, embed_ref,
      gpre_ref, keep_ref, give_ref, *pay_refs) = refs
     nodes = part_ref.shape[0]
-    halo = peers * BORDER
     chosen = grid_ref.shape[0]
     taken = sends_ref.shape[0]
     (arrived,) = split_parts(arr_refs, (0,), (BORDER,))
     gsum = low(dot(low(arrived), update_ref[0], NT)).astype(F32)
     gpre = low(gsum * slope_r_ref[...].astype(F32))
-    border = low(hot(bounds_ref[...] == iota(nodes, halo, 0)))
-    gsent = low(dot(border, gpre))
+    gsent = low(dot(border_t_ref[...], gpre))
     gin = low(part_ref[...] + dot(gsent, send_ref[0], NT))
     gmerged = low(dot(gin, merge_ref[...], NT))
-    place = low(hot(incoming_ref[...] == iota(nodes, taken, 0)))
-    gpre_a = low(dot(place, gmerged, TN) * slope_a_ref[...].astype(F32))
+    gpre_a = low(dot(incoming_ref[...], gmerged, TN) * slope_a_ref[...].astype(F32))
     sent = jnp.max(hot(sends_ref[...] == iota(taken, chosen, 1)), axis=0, keepdims=True)
     label = jnp.where(sent > 0.0, nodes, target_ref[...])
     pick = low(hot(label == iota(nodes, chosen, 0)))
@@ -644,12 +630,12 @@
         (place,), flops=unit // 2, loads=loads,
     )
     arr1 = exchange(pay1, dims)
-    (mesh, merge, cot, local, slope_g, sends_row, incoming, bounds, bounds_row, senders_t, senders,
-     place) = call(
+    (mesh, merge, cot, local, slope_g, sends_row, incoming, border, border_t, back, back_t, senders_t,
+     senders, place) = call(
         lambda *refs: embed_local(column, *refs), "embed_local",
         [shape(nodes, width, dtype=F32), shape(chosen, width), shape(1, taken, dtype=I32),
-         shape(1, taken, dtype=I32), shape(halo, 1, dtype=I32), shape(1, halo, dtype=I32),
-         shape(degree, nodes, dtype=I32), shape(nodes, 8, dtype=I32),
+         shape(nodes, taken), shape(halo, nodes), shape(nodes, halo), shape(halo, nodes),
+         shape(nodes, halo), shape(degree, nodes, dtype=I32), shape(nodes, 8, dtype=I32),
          shape(1, 2 + bits, dtype=I32)],
         (place, raw_sends, raw_incoming, raw_bounds, senders_raw, grid, embed, targets, sends),
         flops=3 * unit,
@@ -659,21 +645,23 @@
         lambda *refs: merge_nodes(peers, *refs), "merge_nodes",
         [shape(nodes, width), shape(nodes, width), shape(taken, width), shape(taken, width)]
         + [shape(4 * BORDER, width)] * peers,
-        (*arr1, incoming, embed, local, mesh, merge, bounds, senders_t, cot),
+        (*arr1, incoming, embed, local, mesh, merge, border, back, cot),
         flops=2 * unit,
     )
     arr2 = exchange(pay2, dims)
-    total0, slope0, recv_n0, sent_b0 = call(
+    total0, slope0, recv_n0, sent_b0, gsum1, edges = call(
         forward_local, "forward_local",
         [shape(nodes, width, dtype=F32), shape(degree, nodes, width),
-         shape(halo, width, dtype=F32), shape(halo, width)],
-        (state0, send_weight, recv_weight, senders, senders_t, bounds), flops=6 * unit,
+         shape(halo, width, dtype=F32), shape(halo, width), shape(nodes, width),
+         shape(nodes, degree * nodes)],
+        (state0, send_weight, recv_weight, update_weight, cot, senders, senders_t, border, back),
+        flops=6 * unit,
     )
     summed0, state1, pre0, rows0, back0, merged_r, cot_r, *pay3 = call(
         lambda *refs: forward_halo(peers, *refs), "forward_halo",
         [shape(nodes, width), shape(nodes, width), shape(halo, width, dtype=F32)]
         + [shape(halo, width)] * 4 + [shape(2 * BORDER, width)] * peers,
-        (*arr2, recv_n0, total0, state0, send_weight, update_weight, senders, senders_t, bounds),
+        (*arr2, recv_n0, total0, state0, send_weight, update_weight, back_t, back, border),
         flops=2 * unit,
     )
     arr3 = exchange(pay3, dims)
@@ -682,15 +670,15 @@
         turn_local, "turn_local",
         [shape(nodes, width, dtype=F32)] * 3 + [shape(halo, width, dtype=F32)]
         + [shape(halo, width)] * 6,
-        (state1, send_weight, recv_weight, update_weight, cot, cot_r, pre0, recv_n0, back0,
-         sent_b0, senders, senders_t, bounds),
+        (state1, send_weight, recv_weight, update_weight, gsum1, cot_r, pre0, recv_n0, back0,
+         sent_b0, senders, edges, border, back),
         flops=10 * unit, scratch=[pltpu.VMEM((degree * nodes, width), BF)],
     )
     summed1, grecv1, gsent1, gin1, *pay4 = call(
         lambda *refs: turn_halo(peers, *refs), "turn_halo",
         [shape(nodes, width)] * 4 + [shape(BORDER, width)] * peers,
         (*arr3, recv_n1, sent_b1, gsum_n1, gsum_r1, total1, grecv_l, gsent_l, cot,
-         send_weight, recv_weight, senders, senders_t, bounds_row),
+         send_weight, recv_weight, back_t, back, border_t),
         flops=3 * unit,
     )
     arr4 = exchange(pay4, dims)
@@ -707,8 +695,8 @@
     part0, keep0, give0, keep2, give2 = call(
         lambda *refs: back_local(dims, *refs), "back_local",
         [shape(nodes, width, dtype=F32)] + blocks_shapes(2, width, width, dims) * 2,
-        (place, gin1, slope0, slope_k0, slope_d0, send_weight, recv_weight, update_weight, senders,
-         senders_t, state0, rows0, summed0, merged, merged_r, keep1),
+        (place, gin1, slope0, slope_k0, slope_d0, send_weight, recv_weight, update_weight, back_t,
+         back, edges, state0, rows0, summed0, merged, merged_r, keep1),
         flops=10 * unit, scratch=[pltpu.VMEM((degree * nodes, width), BF)],
     )
     if split:
@@ -721,7 +709,7 @@
     gpre_g, keep_e, give_e, *pay5 = call(
         lambda *refs: embed_back(peers, dims, carry, *refs), "embed_back",
         [shape(chosen, width)] + shapes + [shape(capacity, width)] * peers,
-        (*arr4, place, slope_r0, part0, update_weight, send_weight, merge, bounds_row,
+        (*arr4, place, slope_r0, part0, update_weight, send_weight, merge, border_t,
          targets, sends, incoming, slope_g, slope_a, grid, lat_a, embed),
         flops=6 * unit,
     )

time: 78.6 us -> 78 us (level)
  waiting for transfers between devices: 19.7 us -> 18.3 us
  starting transfers between devices: 35.7 us -> 36.8 us
    ppermute x16, starting transfers between devices: 17 us -> 18.2 us  [swap(): return lax.ppermute(block, GROUP, [(i, i ^ 1 << bit) for i in range(total)])]
    ppermute x16, waiting for transfers between devices: 18.1 us -> 17.2 us  [swap(): return lax.ppermute(block, GROUP, [(i, i ^ 1 << bit) for i in range(total)])]
  transfers between devices with their start and end apart: 36 -> 36, of which waited for: 12 -> 11; matrix products, arithmetic and copies ran while one was open for 0% -> 0% of each run, Pallas kernels for 21% -> 21%
where the time goes in v17:
time: 78 us; the launch traced here: 77.8 us
  starting transfers between devices  36.8 us (47%)
  Pallas kernels  21.6 us (28%)
  waiting for transfers between devices  18.3 us (23%)
  between operations  0.95 us (1%)
    pallas_call x24, Pallas kernels, call(): pl.pallas_call(kernel, out_shape=[shape(*a.shape, dtype=a.dtype) for a in...  21.6 us
    ppermute x16, starting transfers between devices, swap(): return lax.ppermute(block, GROUP, [(i, i ^ 1 << bit) for i in range(total)])  18.2 us
    ppermute x16, waiting for transfers between devices, swap(): return lax.ppermute(block, GROUP, [(i, i ^ 1 << bit) for i in range(total)])  17.2 us
    ppermute x4, starting transfers between devices, exchange(): far = lax.ppermute(parts[column], 'lon', other)  9.92 us
    ppermute x12, starting transfers between devices, exchange(): lax.ppermute(parts[r - 1], COLUMN, [(i, i ^ r) for i in range(column)])  6.81 us
    ppermute x4, starting transfers between devices, exchange(): lax.ppermute(parts[column - 1], 'lon', [(i, i ^ 1) for i in range(count)])  1.95 us
  transfers between devices with their start and end apart: 36, of which 11 were waited for; matrix products, arithmetic and copies ran while one was open for 0% of the time, Pallas kernels for 21%

profile of v17, /device:TPU:0, one launch (start us, length us, event | category | flops | bytes accessed | tf_op | source)
XLA Modules:
  0.0 77.8 jit_solution(15863002193799747103)
XLA Ops:
  0.8 1.3 %first_payload.1 = (s32[6,1,16]{2,1,0:T(1,128)S(1)}, bf16[512,512]{1,0:T(8,128)(2,1)S(1)}, bf16[512,512]{1,0:T(8,128)(2,1)S(1)}, s32[1,512]{1,0:T(1,128)S(1)}, s...) custom-call(s32[6,1,16]{2,1,0:T(1,128)} %bitcast.15, ...), custom_call_target="tpu_custom_call" | custom-call | flops 67108864 | bytes 1139992 | tf_op jit(solution)/shard_map/first_payload/pallas_call | solution.py:237
  2.1 5.1 %collective-permute-start = (bf16[16,512]{1,0:T(8,128)(2,1)S(1)}, bf16[16,512]{1,0:T(8,128)(2,1)S(1)}, u32[]{:S(2)}, u32[]{:S(2)}) collective-permute-start(bf16[16,512]{1,0:T(8,128)(2,1)S(1)} %get-tuple-element.175), channel_id=1, source_target_pairs={{0,12},{4,8},{8,4},{12,0},{1,13},{5,9},{9,5},{13,1},{2,14},{6,10},... | collective-permute-start | bytes 49160 | tf_op jit(solution)/shard_map/ppermute | solution.py:253
  9.1 2.0 %embed_local.1 = (bf16[256,512]{1,0:T(8,128)(2,1)S(1)}, bf16[512,512]{1,0:T(8,128)(2,1)S(1)}, bf16[256,512]{1,0:T(8,128)(2,1)S(1)}, f32[256,512]{1,0:T(8,128)S(1...) custom-call(bf16[256,512]{1,0:T(8,128)(2,1)} %refs_0_.1, ...), custom_call_target="tpu_custom_call" | custom-call | flops 402653184 | bytes 3292784 | tf_op jit(solution)/shard_map/embed_local/pallas_call | solution.py:237
  12.7 1.1 %collective-permute-start.5 = (bf16[32,512]{1,0:T(8,128)(2,1)S(1)}, bf16[32,512]{1,0:T(8,128)(2,1)S(1)}, u32[]{:S(2)}, u32[]{:S(2)}) collective-permute-start(bf16[32,512]{1,0:T(8,128)(2,1)S(1)} %get-tuple-element.187), channel_id=1, source_target_pairs={{0,12},{4,8},{8,4},{12,0},{1,13},{5,9},{9,5},{13,1},{2,14},{6,10},... | collective-permute-start | bytes 98312 | tf_op jit(solution)/shard_map/ppermute | solution.py:253
  16.3 2.4 %forward_local.1 = (f32[256,512]{1,0:T(8,128)S(1)}, bf16[6,256,512]{2,1,0:T(8,128)(2,1)S(1)}, f32[40,512]{1,0:T(8,128)S(1)}, bf16[40,512]{1,0:T(8,128)(2,1)S(1)}...) custom-call(bf16[256,512]{1,0:T(8,128)(2,1)S(1)} %get-tuple-element.192.state_ref.refs_7_.refs_11_, ...), custom_call_target="tpu_custom_call" | custom-call | flops 805306368 | bytes 6993920 | tf_op jit(solution)/shard_map/forward_local/pallas_call | solution.py:237
  19.9 2.7 %collective-permute-start.10 = (bf16[16,512]{1,0:T(8,128)(2,1)S(1)}, bf16[16,512]{1,0:T(8,128)(2,1)S(1)}, u32[]{:S(2)}, u32[]{:S(2)}) collective-permute-start(bf16[16,512]{1,0:T(8,128)(2,1)S(1)} %get-tuple-element.199), channel_id=1, source_target_pairs={{0,12},{4,8},{8,4},{12,0},{1,13},{5,9},{9,5},{13,1},{2,14},{6,10},... | collective-permute-start | bytes 49160 | tf_op jit(solution)/shard_map/ppermute | solution.py:253
  24.7 2.7 %turn_local.1 = (f32[256,512]{1,0:T(8,128)S(1)}, f32[256,512]{1,0:T(8,128)S(1)}, f32[256,512]{1,0:T(8,128)S(1)}, f32[40,512]{1,0:T(8,128)S(1)}, bf16[40,512]{1,0...) custom-call(bf16[256,512]{1,0:T(8,128)(2,1)S(1)} %get-tuple-element., ...), custom_call_target="tpu_custom_call" | custom-call | flops 1342177280 | bytes 6692864 | tf_op jit(solution)/shard_map/turn_local/pallas_call | solution.py:237
  27.5 1.2 %turn_halo.1 = (bf16[256,512]{1,0:T(8,128)(2,1)S(1)}, bf16[256,512]{1,0:T(8,128)(2,1)S(1)}, bf16[256,512]{1,0:T(8,128)(2,1)S(1)}, bf16[256,512]{1,0:T(8,128)(2,1...) custom-call(bf16[16,512]{1,0:T(8,128)(2,1)S(1)} %collective-permute-, ...), custom_call_target="tpu_custom_call" | custom-call | flops 402653184 | bytes 5369856 | tf_op jit(solution)/shard_map/turn_halo/pallas_call | solution.py:237
  28.8 1.5 %last_weights.1 = (bf16[768,512]{1,0:T(8,128)(2,1)S(1)}, bf16[768,512]{1,0:T(8,128)(2,1)S(1)}, bf16[256,512]{1,0:T(8,128)(2,1)}) custom-call(s32[1,6]{1,0:T(1,128)S(1)} %get-tuple-element.174.refs_0_.refs_5_, bf16[256,512]{1,0:T(8,128)(2,1)S(1)} %get-tuple-element.198.state_ref.refs_1_, bf16[256,512]{1,0:T(8,128)(2,1)S(1)} %get-tuple-element.218.refs_2_, ...), custom_call_target="tpu_custom_call" | custom-call | flops 536870912 | bytes 4194328 | tf_op jit(solution)/shard_map/last_weights/pallas_call | solution.py:237
  31.8 1.1 %collective-permute-start.18 = (bf16[8,512]{1,0:T(8,128)(2,1)S(1)}, bf16[8,512]{1,0:T(8,128)(2,1)S(1)}, u32[]{:S(2)}, u32[]{:S(2)}) collective-permute-start(bf16[8,512]{1,0:T(8,128)(2,1)S(1)} %get-tuple-element.239), channel_id=1, source_target_pairs={{0,4},{4,0},{8,12},{12,8},{1,5},{5,1},{9,13},{13,9},{2,6},{6,2},{1... | collective-permute-start | bytes 24584 | tf_op jit(solution)/shard_map/ppermute | solution.py:254
  34.5 2.7 %back_local.1 = (f32[256,512]{1,0:T(8,128)S(1)}, bf16[512,512]{1,0:T(8,128)(2,1)S(1)}, bf16[512,512]{1,0:T(8,128)(2,1)S(1)}, bf16[512,512]{1,0:T(8,128)(2,1)S(1)}, bf16[512,512]{1,0:T(8,128)(2,1)S(1)}) custom-call(s32[1,6]{1,0:T(1,128)S(1)} %get-tuple-element.174.refs_0_.refs_5_, bf16[256,512]{1,0:T(8,128)(2,1)S(1)} %get-tuple-element.222.refs_1_, ...), custom_call_target="tpu_custom_call" | custom-call | flops 1342177280 | bytes 9773080 | tf_op jit(solution)/shard_map/back_local/pallas_call | solution.py:237
  39.9 2.3 %embed_back.1 = (bf16[512,512]{1,0:T(8,128)(2,1)S(1)}, bf16[256,512]{1,0:T(8,128)(2,1)S(1)}, bf16[288,512]{1,0:T(8,128)(2,1)S(1)}, bf16[16,512]{1,0:T(8,128)(2,1...) custom-call(bf16[8,512]{1,0:T(8,128)(2,1)S(1)} %collective-permute-d, ...), custom_call_target="tpu_custom_call" | custom-call | flops 805306368 | bytes 6191448 | tf_op jit(solution)/shard_map/embed_back/pallas_call | solution.py:237
  44.0 6.1 %collective-permute-done.23.refs_2_ = bf16[384,512]{1,0:T(8,128)(2,1)S(1)} collective-permute-done((bf16[384,512]{1,0:T(8,128)(2,1)S(1)}, bf16[384,512]{1,0:T(8,128)(2,1)S(1)}, u32[]{:S(2)}, u32[]{:S(2)}) %collective-permute-start.23) | collective-permute-done | bytes 393248 | tf_op jit(solution)/shard_map/ppermute | solution.py:166
  51.7 1.5 %collective-permute-start.26 = (bf16[192,512]{1,0:T(8,128)(2,1)S(1)}, bf16[192,512]{1,0:T(8,128)(2,1)S(1)}, u32[]{:S(2)}, u32[]{:S(2)}) collective-permute-start(bf16[192,512]{1,0:T(8,128)(2,1)S(1)} %get-tuple-element.282), channel_id=1, source_target_pairs={{0,4},{1,5},{2,6},{3,7},{4,0},{5,1},{6,2},{7,3},{8,12},{9,13},{10,... | collective-permute-start | bytes 589832 | tf_op jit(solution)/shard_map/ppermute | solution.py:166
  53.9 1.8 %collective-permute-done.25.refs_2_ = bf16[256,512]{1,0:T(8,128)(2,1)S(1)} collective-permute-done((bf16[256,512]{1,0:T(8,128)(2,1)S(1)}, bf16[256,512]{1,0:T(8,128)(2,1)S(1)}, u32[]{:S(2)}, u32[]{:S(2)}) %collective-permute-start.25) | collective-permute-done | bytes 262176 | tf_op jit(solution)/shard_map/ppermute | solution.py:166
  55.8 1.1 %collective-permute-start.28 = (bf16[128,512]{1,0:T(8,128)(2,1)S(1)}, bf16[128,512]{1,0:T(8,128)(2,1)S(1)}, u32[]{:S(2)}, u32[]{:S(2)}) collective-permute-start(bf16[128,512]{1,0:T(8,128)(2,1)S(1)} %get-tuple-element.291), channel_id=1, source_target_pairs={{0,4},{1,5},{2,6},{3,7},{4,0},{5,1},{6,2},{7,3},{8,12},{9,13},{10,... | collective-permute-start | bytes 393224 | tf_op jit(solution)/shard_map/ppermute | solution.py:166
  57.5 2.6 %collective-permute-start.29 = (bf16[96,512]{1,0:T(8,128)(2,1)S(1)}, bf16[96,512]{1,0:T(8,128)(2,1)S(1)}, u32[]{:S(2)}, u32[]{:S(2)}) collective-permute-start(bf16[96,512]{1,0:T(8,128)(2,1)S(1)} %get-tuple-element.293), channel_id=1, source_target_pairs={{0,8},{1,9},{2,10},{3,11},{4,12},{5,13},{6,14},{7,15},{8,0},{9,1},... | collective-permute-start | bytes 294920 | tf_op jit(solution)/shard_map/ppermute | solution.py:166
  60.1 1.2 %collective-permute-done.27.refs_2_ = bf16[256,512]{1,0:T(8,128)(2,1)S(1)} collective-permute-done((bf16[256,512]{1,0:T(8,128)(2,1)S(1)}, bf16[256,512]{1,0:T(8,128)(2,1)S(1)}, u32[]{:S(2)}, u32[]{:S(2)}) %collective-permute-start.27) | collective-permute-done | bytes 262176 | tf_op jit(solution)/shard_map/ppermute | solution.py:166
  61.4 1.1 %collective-permute-start.32 = (bf16[128,512]{1,0:T(8,128)(2,1)S(1)}, bf16[128,512]{1,0:T(8,128)(2,1)S(1)}, u32[]{:S(2)}, u32[]{:S(2)}) collective-permute-start(bf16[128,512]{1,0:T(8,128)(2,1)S(1)} %get-tuple-element.305), channel_id=1, source_target_pairs={{0,4},{1,5},{2,6},{3,7},{4,0},{5,1},{6,2},{7,3},{8,12},{9,13},{10,... | collective-permute-start | bytes 393224 | tf_op jit(solution)/shard_map/ppermute | solution.py:166
  65.4 2.3 %collective-permute-start.30 = (bf16[64,512]{1,0:T(8,128)(2,1)S(1)}, bf16[64,512]{1,0:T(8,128)(2,1)S(1)}, u32[]{:S(2)}, u32[]{:S(2)}) collective-permute-start(bf16[64,512]{1,0:T(8,128)(2,1)S(1)} %get-tuple-element.296), channel_id=1, source_target_pairs={{0,8},{1,9},{2,10},{3,11},{4,12},{5,13},{6,14},{7,15},{8,0},{9,1},... | collective-permute-start | bytes 196616 | tf_op jit(solution)/shard_map/ppermute | solution.py:166
  67.8 1.1 %collective-permute-start.33 = (bf16[64,512]{1,0:T(8,128)(2,1)S(1)}, bf16[64,512]{1,0:T(8,128)(2,1)S(1)}, u32[]{:S(2)}, u32[]{:S(2)}) collective-permute-start(bf16[64,512]{1,0:T(8,128)(2,1)S(1)} %get-tuple-element.308), channel_id=1, source_target_pairs={{0,8},{1,9},{2,10},{3,11},{4,12},{5,13},{6,14},{7,15},{8,0},{9,1},... | collective-permute-start | bytes 196616 | tf_op jit(solution)/shard_map/ppermute | solution.py:166
  69.9 2.3 %collective-permute-start.35 = (bf16[48,512]{1,0:T(8,128)(2,1)S(1)}, bf16[48,512]{1,0:T(8,128)(2,1)S(1)}, u32[]{:S(2)}, u32[]{:S(2)}) collective-permute-start(bf16[48,512]{1,0:T(8,128)(2,1)S(1)} %get-tuple-element.312), channel_id=1, source_target_pairs={{0,8},{1,9},{2,10},{3,11},{4,12},{5,13},{6,14},{7,15},{8,0},{9,1},... | collective-permute-start | bytes 147464 | tf_op jit(solution)/shard_map/ppermute | solution.py:166
  72.3 4.3 %collective-permute-done.35.refs_7_ = bf16[48,512]{1,0:T(8,128)(2,1)S(1)} collective-permute-done((bf16[48,512]{1,0:T(8,128)(2,1)S(1)}, bf16[48,512]{1,0:T(8,128)(2,1)S(1)}, u32[]{:S(2)}, u32[]{:S(2)}) %collective-permute-start.35) | collective-permute-done | bytes 49184 | tf_op jit(solution)/shard_map/ppermute | solution.py:166
  76.6 1.2 %finish_all.1 = (bf16[512,512]{1,0:T(8,128)(2,1)}, f32[32,512]{1,0:T(8,128)}, f32[32,512]{1,0:T(8,128)}, f32[2,32,512]{2,1,0:T(8,128)}, f32[2,32,512]{2,1,0:T(8,128)}, /*index=5*/f32[2,32,512]{2,1,0:T(8,128)}) custom-call(bf16[96,512]{1,0:T(8,128)(2,1)S(1)} %get-tuple-element.284.refs_0_, bf16[96,512]{1,0:T(8,128)(2,1)S(1)} %collective-permute-done.29.refs_1_, ...), custom_call_target="tpu_custom_call" | custom-call | flops 134217728 | bytes 2179392 | tf_op jit(solution)/shard_map/finish_all/pallas_call | solution.py:237
  (79 shorter events, 24.0 us)
Async XLA Ops:
  2.1 9.0 %collective-permute-start = (bf16[16,512]{1,0:T(8,128)(2,1)S(1)}, bf16[16,512]{1,0:T(8,128)(2,1)S(1)}, u32[]{:S(2)}, u32[]{:S(2)}) collective-permute-start(bf16[16,512]{1,0:T(8,128)(2,1)S(1)} %get-tuple-element.175), channel_id=1, source_target_pairs={{0,12},{4,8},{8,4},{12,0},{1,13},{5,9},{9,5},{13,1},{2,14},{6,10},... | collective-permute-start | bytes 49160 | tf_op jit(solution)/shard_map/ppermute | solution.py:253
  12.7 6.0 %collective-permute-start.5 = (bf16[32,512]{1,0:T(8,128)(2,1)S(1)}, bf16[32,512]{1,0:T(8,128)(2,1)S(1)}, u32[]{:S(2)}, u32[]{:S(2)}) collective-permute-start(bf16[32,512]{1,0:T(8,128)(2,1)S(1)} %get-tuple-element.187), channel_id=1, source_target_pairs={{0,12},{4,8},{8,4},{12,0},{1,13},{5,9},{9,5},{13,1},{2,14},{6,10},... | collective-permute-start | bytes 98312 | tf_op jit(solution)/shard_map/ppermute | solution.py:253
  13.8 4.9 %collective-permute-start.6 = (bf16[32,512]{1,0:T(8,128)(2,1)S(1)}, bf16[32,512]{1,0:T(8,128)(2,1)S(1)}, u32[]{:S(2)}, u32[]{:S(2)}) collective-permute-start(bf16[32,512]{1,0:T(8,128)(2,1)S(1)} %get-tuple-element.188), channel_id=1, source_target_pairs={{0,4},{4,0},{8,12},{12,8},{1,5},{5,1},{9,13},{13,9},{2,6},{6,2},{1... | collective-permute-start | bytes 98312 | tf_op jit(solution)/shard_map/ppermute | solution.py:254
  19.9 7.6 %collective-permute-start.10 = (bf16[16,512]{1,0:T(8,128)(2,1)S(1)}, bf16[16,512]{1,0:T(8,128)(2,1)S(1)}, u32[]{:S(2)}, u32[]{:S(2)}) collective-permute-start(bf16[16,512]{1,0:T(8,128)(2,1)S(1)} %get-tuple-element.199), channel_id=1, source_target_pairs={{0,12},{4,8},{8,4},{12,0},{1,13},{5,9},{9,5},{13,1},{2,14},{6,10},... | collective-permute-start | bytes 49160 | tf_op jit(solution)/shard_map/ppermute | solution.py:253
  22.6 4.8 %collective-permute-start.11 = (bf16[16,512]{1,0:T(8,128)(2,1)S(1)}, bf16[16,512]{1,0:T(8,128)(2,1)S(1)}, u32[]{:S(2)}, u32[]{:S(2)}) collective-permute-start(bf16[16,512]{1,0:T(8,128)(2,1)S(1)} %get-tuple-element.200), channel_id=1, source_target_pairs={{0,4},{4,0},{8,12},{12,8},{1,5},{5,1},{9,13},{13,9},{2,6},{6,2},{1... | collective-permute-start | bytes 49160 | tf_op jit(solution)/shard_map/ppermute | solution.py:254
  22.8 4.7 %collective-permute-start.12 = (bf16[16,512]{1,0:T(8,128)(2,1)S(1)}, bf16[16,512]{1,0:T(8,128)(2,1)S(1)}, u32[]{:S(2)}, u32[]{:S(2)}) collective-permute-start(bf16[16,512]{1,0:T(8,128)(2,1)S(1)} %get-tuple-element.201), channel_id=1, source_target_pairs={{0,3},{1,2},{2,1},{3,0},{4,7},{5,6},{6,5},{7,4},{8,11},{9,10},{10,... | collective-permute-start | bytes 49160 | tf_op jit(solution)/shard_map/ppermute | solution.py:256
  23.1 4.4 %collective-permute-start.13 = (bf16[16,512]{1,0:T(8,128)(2,1)S(1)}, bf16[16,512]{1,0:T(8,128)(2,1)S(1)}, u32[]{:S(2)}, u32[]{:S(2)}) collective-permute-start(bf16[16,512]{1,0:T(8,128)(2,1)S(1)} %get-tuple-element.202), channel_id=1, source_target_pairs={{0,2},{1,3},{2,0},{3,1},{4,6},{5,7},{6,4},{7,5},{8,10},{9,11},{10,... | collective-permute-start | bytes 49160 | tf_op jit(solution)/shard_map/ppermute | solution.py:256
  30.8 6.5 %collective-permute-start.17 = (bf16[8,512]{1,0:T(8,128)(2,1)S(1)}, bf16[8,512]{1,0:T(8,128)(2,1)S(1)}, u32[]{:S(2)}, u32[]{:S(2)}) collective-permute-start(bf16[8,512]{1,0:T(8,128)(2,1)S(1)} %get-tuple-element.238), channel_id=1, source_target_pairs={{0,12},{4,8},{8,4},{12,0},{1,13},{5,9},{9,5},{13,1},{2,14},{6,10},... | collective-permute-start | bytes 24584 | tf_op jit(solution)/shard_map/ppermute | solution.py:253
  31.8 5.5 %collective-permute-start.18 = (bf16[8,512]{1,0:T(8,128)(2,1)S(1)}, bf16[8,512]{1,0:T(8,128)(2,1)S(1)}, u32[]{:S(2)}, u32[]{:S(2)}) collective-permute-start(bf16[8,512]{1,0:T(8,128)(2,1)S(1)} %get-tuple-element.239), channel_id=1, source_target_pairs={{0,4},{4,0},{8,12},{12,8},{1,5},{5,1},{9,13},{13,9},{2,6},{6,2},{1... | collective-permute-start | bytes 24584 | tf_op jit(solution)/shard_map/ppermute | solution.py:254
  32.9 4.4 %collective-permute-start.19 = (bf16[8,512]{1,0:T(8,128)(2,1)S(1)}, bf16[8,512]{1,0:T(8,128)(2,1)S(1)}, u32[]{:S(2)}, u32[]{:S(2)}) collective-permute-start(bf16[8,512]{1,0:T(8,128)(2,1)S(1)} %get-tuple-element.240), channel_id=1, source_target_pairs={{0,3},{1,2},{2,1},{3,0},{4,7},{5,6},{6,5},{7,4},{8,11},{9,10},{10,... | collective-permute-start | bytes 24584 | tf_op jit(solution)/shard_map/ppermute | solution.py:256
  38.1 12.3 %collective-permute-start.24 = (bf16[512,512]{1,0:T(8,128)(2,1)S(1)}, bf16[512,512]{1,0:T(8,128)(2,1)S(1)}, u32[]{:S(2)}, u32[]{:S(2)}) collective-permute-start(bf16[512,512]{1,0:T(8,128)(2,1)S(1)} %get-tuple-element.274), channel_id=1, source_target_pairs={{0,1},{1,0},{2,3},{3,2},{4,5},{5,4},{6,7},{7,6},{8,9},{9,8},{10,11... | collective-permute-start | bytes 1572872 | tf_op jit(solution)/shard_map/ppermute | solution.py:166
  38.2 11.9 %collective-permute-start.23 = (bf16[384,512]{1,0:T(8,128)(2,1)S(1)}, bf16[384,512]{1,0:T(8,128)(2,1)S(1)}, u32[]{:S(2)}, u32[]{:S(2)}) collective-permute-start(bf16[384,512]{1,0:T(8,128)(2,1)S(1)} %get-tuple-element.266), channel_id=1, source_target_pairs={{0,2},{1,3},{2,0},{3,1},{4,6},{5,7},{6,4},{7,5},{8,10},{9,11},{10,... | collective-permute-start | bytes 1179656 | tf_op jit(solution)/shard_map/ppermute | solution.py:166
  42.2 7.8 %collective-permute-start.22 = (bf16[288,512]{1,0:T(8,128)(2,1)S(1)}, bf16[288,512]{1,0:T(8,128)(2,1)S(1)}, u32[]{:S(2)}, u32[]{:S(2)}) collective-permute-start(bf16[288,512]{1,0:T(8,128)(2,1)S(1)} %get-tuple-element.265), channel_id=1, source_target_pairs={{0,1},{1,0},{2,3},{3,2},{4,5},{5,4},{6,7},{7,6},{8,9},{9,8},{10,11... | collective-permute-start | bytes 884744 | tf_op jit(solution)/shard_map/ppermute | solution.py:166
  42.6 13.1 %collective-permute-start.25 = (bf16[256,512]{1,0:T(8,128)(2,1)S(1)}, bf16[256,512]{1,0:T(8,128)(2,1)S(1)}, u32[]{:S(2)}, u32[]{:S(2)}) collective-permute-start(bf16[256,512]{1,0:T(8,128)(2,1)S(1)} %get-tuple-element.279), channel_id=1, source_target_pairs={{0,2},{1,3},{2,0},{3,1},{4,6},{5,7},{6,4},{7,5},{8,10},{9,11},{10,... | collective-permute-start | bytes 786440 | tf_op jit(solution)/shard_map/ppermute | solution.py:166
  50.7 10.6 %collective-permute-start.27 = (bf16[256,512]{1,0:T(8,128)(2,1)S(1)}, bf16[256,512]{1,0:T(8,128)(2,1)S(1)}, u32[]{:S(2)}, u32[]{:S(2)}) collective-permute-start(bf16[256,512]{1,0:T(8,128)(2,1)S(1)} %get-tuple-element.288), channel_id=1, source_target_pairs={{0,2},{1,3},{2,0},{3,1},{4,6},{5,7},{6,4},{7,5},{8,10},{9,11},{10,... | collective-permute-start | bytes 786440 | tf_op jit(solution)/shard_map/ppermute | solution.py:166
  51.7 5.7 %collective-permute-start.26 = (bf16[192,512]{1,0:T(8,128)(2,1)S(1)}, bf16[192,512]{1,0:T(8,128)(2,1)S(1)}, u32[]{:S(2)}, u32[]{:S(2)}) collective-permute-start(bf16[192,512]{1,0:T(8,128)(2,1)S(1)} %get-tuple-element.282), channel_id=1, source_target_pairs={{0,4},{1,5},{2,6},{3,7},{4,0},{5,1},{6,2},{7,3},{8,12},{9,13},{10,... | collective-permute-start | bytes 589832 | tf_op jit(solution)/shard_map/ppermute | solution.py:166
  53.2 11.2 %collective-permute-start.31 = (bf16[160,512]{1,0:T(8,128)(2,1)S(1)}, bf16[160,512]{1,0:T(8,128)(2,1)S(1)}, u32[]{:S(2)}, u32[]{:S(2)}) collective-permute-start(bf16[160,512]{1,0:T(8,128)(2,1)S(1)} %get-tuple-element.299), channel_id=1, source_target_pairs={{0,2},{1,3},{2,0},{3,1},{4,6},{5,7},{6,4},{7,5},{8,10},{9,11},{10,... | collective-permute-start | bytes 491528 | tf_op jit(solution)/shard_map/ppermute | solution.py:166
  55.8 6.7 %collective-permute-start.28 = (bf16[128,512]{1,0:T(8,128)(2,1)S(1)}, bf16[128,512]{1,0:T(8,128)(2,1)S(1)}, u32[]{:S(2)}, u32[]{:S(2)}) collective-permute-start(bf16[128,512]{1,0:T(8,128)(2,1)S(1)} %get-tuple-element.291), channel_id=1, source_target_pairs={{0,4},{1,5},{2,6},{3,7},{4,0},{5,1},{6,2},{7,3},{8,12},{9,13},{10,... | collective-permute-start | bytes 393224 | tf_op jit(solution)/shard_map/ppermute | solution.py:166
  57.5 5.8 %collective-permute-start.29 = (bf16[96,512]{1,0:T(8,128)(2,1)S(1)}, bf16[96,512]{1,0:T(8,128)(2,1)S(1)}, u32[]{:S(2)}, u32[]{:S(2)}) collective-permute-start(bf16[96,512]{1,0:T(8,128)(2,1)S(1)} %get-tuple-element.293), channel_id=1, source_target_pairs={{0,8},{1,9},{2,10},{3,11},{4,12},{5,13},{6,14},{7,15},{8,0},{9,1},... | collective-permute-start | bytes 294920 | tf_op jit(solution)/shard_map/ppermute | solution.py:166
  61.4 6.3 %collective-permute-start.32 = (bf16[128,512]{1,0:T(8,128)(2,1)S(1)}, bf16[128,512]{1,0:T(8,128)(2,1)S(1)}, u32[]{:S(2)}, u32[]{:S(2)}) collective-permute-start(bf16[128,512]{1,0:T(8,128)(2,1)S(1)} %get-tuple-element.305), channel_id=1, source_target_pairs={{0,4},{1,5},{2,6},{3,7},{4,0},{5,1},{6,2},{7,3},{8,12},{9,13},{10,... | collective-permute-start | bytes 393224 | tf_op jit(solution)/shard_map/ppermute | solution.py:166
  64.5 5.4 %collective-permute-start.34 = (bf16[96,512]{1,0:T(8,128)(2,1)S(1)}, bf16[96,512]{1,0:T(8,128)(2,1)S(1)}, u32[]{:S(2)}, u32[]{:S(2)}) collective-permute-start(bf16[96,512]{1,0:T(8,128)(2,1)S(1)} %get-tuple-element.310), channel_id=1, source_target_pairs={{0,4},{1,5},{2,6},{3,7},{4,0},{5,1},{6,2},{7,3},{8,12},{9,13},{10,... | collective-permute-start | bytes 294920 | tf_op jit(solution)/shard_map/ppermute | solution.py:166
  65.4 6.8 %collective-permute-start.30 = (bf16[64,512]{1,0:T(8,128)(2,1)S(1)}, bf16[64,512]{1,0:T(8,128)(2,1)S(1)}, u32[]{:S(2)}, u32[]{:S(2)}) collective-permute-start(bf16[64,512]{1,0:T(8,128)(2,1)S(1)} %get-tuple-element.296), channel_id=1, source_target_pairs={{0,8},{1,9},{2,10},{3,11},{4,12},{5,13},{6,14},{7,15},{8,0},{9,1},... | collective-permute-start | bytes 196616 | tf_op jit(solution)/shard_map/ppermute | solution.py:166
  67.8 8.8 %collective-permute-start.33 = (bf16[64,512]{1,0:T(8,128)(2,1)S(1)}, bf16[64,512]{1,0:T(8,128)(2,1)S(1)}, u32[]{:S(2)}, u32[]{:S(2)}) collective-permute-start(bf16[64,512]{1,0:T(8,128)(2,1)S(1)} %get-tuple-element.308), channel_id=1, source_target_pairs={{0,8},{1,9},{2,10},{3,11},{4,12},{5,13},{6,14},{7,15},{8,0},{9,1},... | collective-permute-start | bytes 196616 | tf_op jit(solution)/shard_map/ppermute | solution.py:166
  69.9 6.7 %collective-permute-start.35 = (bf16[48,512]{1,0:T(8,128)(2,1)S(1)}, bf16[48,512]{1,0:T(8,128)(2,1)S(1)}, u32[]{:S(2)}, u32[]{:S(2)}) collective-permute-start(bf16[48,512]{1,0:T(8,128)(2,1)S(1)} %get-tuple-element.312), channel_id=1, source_target_pairs={{0,8},{1,9},{2,10},{3,11},{4,12},{5,13},{6,14},{7,15},{8,0},{9,1},... | collective-permute-start | bytes 147464 | tf_op jit(solution)/shard_map/ppermute | solution.py:166
  (15 other events, 59.1 us)

commit v18 on v17

--- a/solution.py
+++ b/solution.py
@@ -121,14 +121,17 @@
     return (rows // (dims[0] * dims[1] * dims[2])) % 16 == 0
 
 
-def reverse_bits(block, bits):
+LON_FIRST = (0, 2, 3, 1)
+
+
+def block_spot(block, order):
     spot = 0
-    for bit in range(bits):
+    for bit in order:
         spot = 2 * spot + (block >> bit) % 2
     return spot
 
 
-def store_blocks(keep_ref, give_ref, at, count, value, dims, bits_ref):
+def store_blocks(keep_ref, give_ref, at, count, value, dims, bits_ref, order=None):
     value = low(value)
     rows = value.shape[0]
     total = dims[0] * dims[1] * dims[2]
@@ -139,7 +142,7 @@
     bits = (total - 1).bit_length()
     upper = bits_ref[0:1, 2:3] == 1
     for block in range(0, total, 2):
-        start = reverse_bits(block, bits) * count * depth + at * depth
+        start = block_spot(block, order or range(bits)) * count * depth + at * depth
         first = value[block * depth : (block + 1) * depth].astype(F32)
         second = value[(block + 1) * depth : (block + 2) * depth].astype(F32)
         keep_ref[start : start + depth, :] = low(jnp.where(upper, second, first))
@@ -194,11 +197,11 @@
     second = keep_ref[half:, :].astype(F32) + value[half:rows]
     keep_out[...] = low(jnp.where(upper, second, first))
     here_refs[0][...] = low(value[rows : rows + size])
-    passed = value[rows + size : rows + 2 * size]
+    passed = value[rows + size :]
     extra = [ref[...].astype(F32) for ref in own_refs]
     if count < 2:
         extra.append(passed)
-    else:
+    elif len(here_refs) == 2:
         here_refs[1][...] = low(passed)
     give_out[...] = low(jnp.concatenate([jnp.where(upper, first, second), *extra], axis=0))
 
@@ -206,10 +209,11 @@
 def carry_step(bit, keep, arrived, own, place, capacity):
     rows, width = keep.shape[0] // 2, keep.shape[1]
     count = len(own)
+    both = count == 2 and arrived.shape[0] == 2 * (rows + capacity)
     return call(
         lambda *refs: halve_carry(bit, count, *refs), "halve_carry",
         [shape(rows, width), shape(rows + min(count + 1, 2) * capacity, width)]
-        + [shape(capacity, width)] * (2 if count == 2 else 1),
+        + [shape(capacity, width)] * (2 if both else 1),
         (place, keep, arrived, *own), flops=4 * rows * width, size=0,
     )
 
@@ -546,7 +550,9 @@
     gpre_g = low(dot(pick, gmerged, TN) * slope_g_ref[...].astype(F32))
     gpre_ref[...] = gpre_g
     grad = dot(grid_ref[...], gpre_g, TN) + dot(lat_ref[...], gpre_a, TN)
-    store_blocks(keep_ref, give_ref, 0, 1, grad, dims, place_ref)
+    store_blocks(
+        keep_ref, give_ref, 0, 1, grad, dims, place_ref, LON_FIRST if carry else None
+    )
     rows = dot(gpre_a, embed_ref[...], NT)
     store_parts(pay_refs, [rows])
     if carry:
@@ -595,8 +601,11 @@
 
 
 def finish_all(*refs):
-    sums, rows, (local_ref, sends_ref), outs = refs[:8], refs[8:12], refs[12:14], refs[14:]
-    grid_patch(local_ref, sends_ref, (*rows, sums[7]), outs[0])
+    sums, (sub, near, far, local_ref, sends_ref), outs = refs[:8], refs[8:13], refs[13:]
+    depth = outs[1].shape[0]
+    size = sub.shape[0]
+    lat, diag = sums[7].at[depth : depth + size], sums[7].at[depth + size :]
+    grid_patch(local_ref, sends_ref, (sub, lat, diag, near, far), outs[0])
     sum_last(sums, outs[1:])
 
 
@@ -741,41 +750,38 @@
         keep1, give1 = halve_step(2, keep1, arr1, place)
         arr1 = swap(give1, 2, dims)
         keep_e, keep1 = lax.optimization_barrier((keep_e, keep1))
-        keep_e, give_e, from_sub = carry_step(1, keep_e, arr_e, pay5[1:2], place, capacity)
-        arr_e = swap(give_e, 1, dims)
+        keep_e, give_e, from_sub, on = carry_step(2, keep_e, arr_e, pay5[3:], place, capacity)
+        arr_e = swap(give_e, 2, dims)
         keep2, keep_e = lax.optimization_barrier((keep2, keep_e))
         keep2, give2 = halve_step(1, keep2, arr2, place)
         arr2 = swap(give2, 1, dims)
         keep0, keep2 = lax.optimization_barrier((keep0, keep2))
         keep0, give0 = halve_step(2, keep0, arr0, place)
         arr0 = swap(give0, 2, dims)
-        keep1, keep0 = lax.optimization_barrier((keep1, keep0))
+        keep_e, keep0 = lax.optimization_barrier((keep_e, keep0))
+        keep_e, give_e, from_near = carry_step(3, keep_e, arr_e, (), place, capacity)
+        arr_e = swap(give_e, 3, dims)
+        keep1, keep_e = lax.optimization_barrier((keep1, keep_e))
         keep1, give1 = halve_step(3, keep1, arr1, place)
         arr1 = swap(give1, 3, dims)
-        keep2, keep1 = lax.optimization_barrier((keep2, keep1))
+        keep_e, keep1 = lax.optimization_barrier((keep_e, keep1))
+        keep_e, give_e, from_far = carry_step(1, keep_e, arr_e, (pay5[1], on), place, capacity)
+        arr_e = swap(give_e, 1, dims)
+        keep0, keep_e = lax.optimization_barrier((keep0, keep_e))
+        keep0, give0 = halve_step(3, keep0, arr0, place)
+        arr0 = swap(give0, 3, dims)
+        keep2, keep0, arr1 = lax.optimization_barrier((keep2, keep0, arr1))
         keep2, give2 = halve_step(2, keep2, arr2, place)
         arr2 = swap(give2, 2, dims)
-        keep0, keep2 = lax.optimization_barrier((keep0, keep2))
-        keep0, give0 = halve_step(3, keep0, arr0, place)
-        arr0 = swap(give0, 3, dims)
-        keep_e, keep0, arr1 = lax.optimization_barrier((keep_e, keep0, arr1))
-        keep_e, give_e, from_lat, from_diag = carry_step(
-            2, keep_e, arr_e, pay5[3:], place, capacity
-        )
-        arr_e = swap(give_e, 2, dims)
-        keep2, keep_e = lax.optimization_barrier((keep2, keep_e))
         keep2, give2 = halve_step(3, keep2, arr2, place)
         arr2 = swap(give2, 3, dims)
-        keep_e, keep2 = lax.optimization_barrier((keep_e, keep2))
-        keep_e, give_e, from_near = carry_step(3, keep_e, arr_e, (), place, capacity)
-        arr_e = swap(give_e, 3, dims)
         sums = ((keep1, arr1), (keep0, arr0), (keep2, arr2), (keep_e, arr_e))
     grads = [shape(depth, width, dtype=F32)] * 2 + [shape(2, depth, width, dtype=F32)] * 3
     if carry:
         return (mesh_out, *call(
             finish_all, "finish_all", [shape(chosen, width)] + grads,
-            (*(part for pair in sums for part in pair), from_sub, from_lat, from_diag, from_near,
-             local_rows, sends_row),
+            (*(part for pair in sums for part in pair), from_sub, from_near, from_far, local_rows,
+             sends_row),
             flops=unit,
         ))
     (local_rows,) = call(

time: 78 us -> 83.4 us (1.069)
  waiting for transfers between devices: 18.3 us -> 26.4 us
  starting transfers between devices: 36.8 us -> 34.2 us
    ppermute x16, waiting for transfers between devices: 17.2 us -> 25.3 us  [swap(): return lax.ppermute(block, GROUP, [(i, i ^ 1 << bit) for i in range(total)])]
    ppermute x16, starting transfers between devices: 18.2 us -> 15.5 us  [swap(): return lax.ppermute(block, GROUP, [(i, i ^ 1 << bit) for i in range(total)])]
  transfers between devices with their start and end apart: 36 -> 36, of which waited for: 11 -> 9; matrix products, arithmetic and copies ran while one was open for 0% -> 0% of each run, Pallas kernels for 21% -> 19%
where the time goes in v18:
time: 83.4 us; the launch traced here: 83.3 us
  starting transfers between devices  34.2 us (41%)
  waiting for transfers between devices  26.4 us (32%)
  Pallas kernels  21.6 us (26%)
  between operations  0.98 us (1%)
    ppermute x16, waiting for transfers between devices, swap(): return lax.ppermute(block, GROUP, [(i, i ^ 1 << bit) for i in range(total)])  25.3 us
    pallas_call x24, Pallas kernels, call(): pl.pallas_call(kernel, out_shape=[shape(*a.shape, dtype=a.dtype) for a in...  21.6 us
    ppermute x16, starting transfers between devices, swap(): return lax.ppermute(block, GROUP, [(i, i ^ 1 << bit) for i in range(total)])  15.5 us
    ppermute x4, starting transfers between devices, exchange(): far = lax.ppermute(parts[column], 'lon', other)  9.92 us
    ppermute x12, starting transfers between devices, exchange(): lax.ppermute(parts[r - 1], COLUMN, [(i, i ^ r) for i in range(column)])  6.81 us
    ppermute x4, starting transfers between devices, exchange(): lax.ppermute(parts[column - 1], 'lon', [(i, i ^ 1) for i in range(count)])  1.95 us
  transfers between devices with their start and end apart: 36, of which 9 were waited for; matrix products, arithmetic and copies ran while one was open for 0% of the time, Pallas kernels for 19%

profile of v18, /device:TPU:0, one launch (start us, length us, event | category | flops | bytes accessed | tf_op | source)
XLA Modules:
  0.0 83.3 jit_solution(10960101544925168541)
XLA Ops:
  0.8 1.3 %first_payload.1 = (s32[6,1,16]{2,1,0:T(1,128)S(1)}, bf16[512,512]{1,0:T(8,128)(2,1)S(1)}, bf16[512,512]{1,0:T(8,128)(2,1)S(1)}, s32[1,512]{1,0:T(1,128)S(1)}, s...) custom-call(s32[6,1,16]{2,1,0:T(1,128)} %bitcast.15, ...), custom_call_target="tpu_custom_call" | custom-call | flops 67108864 | bytes 1139992 | tf_op jit(solution)/shard_map/first_payload/pallas_call | solution.py:241
  2.1 5.1 %collective-permute-start = (bf16[16,512]{1,0:T(8,128)(2,1)S(1)}, bf16[16,512]{1,0:T(8,128)(2,1)S(1)}, u32[]{:S(2)}, u32[]{:S(2)}) collective-permute-start(bf16[16,512]{1,0:T(8,128)(2,1)S(1)} %get-tuple-element.173), channel_id=1, source_target_pairs={{0,12},{4,8},{8,4},{12,0},{1,13},{5,9},{9,5},{13,1},{2,14},{6,10},... | collective-permute-start | bytes 49160 | tf_op jit(solution)/shard_map/ppermute | solution.py:257
  9.1 2.0 %embed_local.1 = (bf16[256,512]{1,0:T(8,128)(2,1)S(1)}, bf16[512,512]{1,0:T(8,128)(2,1)S(1)}, bf16[256,512]{1,0:T(8,128)(2,1)S(1)}, f32[256,512]{1,0:T(8,128)S(1...) custom-call(bf16[256,512]{1,0:T(8,128)(2,1)} %refs_0_.1, ...), custom_call_target="tpu_custom_call" | custom-call | flops 402653184 | bytes 3292784 | tf_op jit(solution)/shard_map/embed_local/pallas_call | solution.py:241
  12.7 1.1 %collective-permute-start.5 = (bf16[32,512]{1,0:T(8,128)(2,1)S(1)}, bf16[32,512]{1,0:T(8,128)(2,1)S(1)}, u32[]{:S(2)}, u32[]{:S(2)}) collective-permute-start(bf16[32,512]{1,0:T(8,128)(2,1)S(1)} %get-tuple-element.185), channel_id=1, source_target_pairs={{0,12},{4,8},{8,4},{12,0},{1,13},{5,9},{9,5},{13,1},{2,14},{6,10},... | collective-permute-start | bytes 98312 | tf_op jit(solution)/shard_map/ppermute | solution.py:257
  16.3 2.4 %forward_local.1 = (f32[256,512]{1,0:T(8,128)S(1)}, bf16[6,256,512]{2,1,0:T(8,128)(2,1)S(1)}, f32[40,512]{1,0:T(8,128)S(1)}, bf16[40,512]{1,0:T(8,128)(2,1)S(1)}...) custom-call(bf16[256,512]{1,0:T(8,128)(2,1)S(1)} %get-tuple-element.190.state_ref.refs_7_.refs_11_, ...), custom_call_target="tpu_custom_call" | custom-call | flops 805306368 | bytes 6993920 | tf_op jit(solution)/shard_map/forward_local/pallas_call | solution.py:241
  19.9 2.7 %collective-permute-start.10 = (bf16[16,512]{1,0:T(8,128)(2,1)S(1)}, bf16[16,512]{1,0:T(8,128)(2,1)S(1)}, u32[]{:S(2)}, u32[]{:S(2)}) collective-permute-start(bf16[16,512]{1,0:T(8,128)(2,1)S(1)} %get-tuple-element.197), channel_id=1, source_target_pairs={{0,12},{4,8},{8,4},{12,0},{1,13},{5,9},{9,5},{13,1},{2,14},{6,10},... | collective-permute-start | bytes 49160 | tf_op jit(solution)/shard_map/ppermute | solution.py:257
  24.7 2.7 %turn_local.1 = (f32[256,512]{1,0:T(8,128)S(1)}, f32[256,512]{1,0:T(8,128)S(1)}, f32[256,512]{1,0:T(8,128)S(1)}, f32[40,512]{1,0:T(8,128)S(1)}, bf16[40,512]{1,0...) custom-call(bf16[256,512]{1,0:T(8,128)(2,1)S(1)} %get-tuple-element., ...), custom_call_target="tpu_custom_call" | custom-call | flops 1342177280 | bytes 6692864 | tf_op jit(solution)/shard_map/turn_local/pallas_call | solution.py:241
  27.5 1.2 %turn_halo.1 = (bf16[256,512]{1,0:T(8,128)(2,1)S(1)}, bf16[256,512]{1,0:T(8,128)(2,1)S(1)}, bf16[256,512]{1,0:T(8,128)(2,1)S(1)}, bf16[256,512]{1,0:T(8,128)(2,1...) custom-call(bf16[16,512]{1,0:T(8,128)(2,1)S(1)} %collective-permute-, ...), custom_call_target="tpu_custom_call" | custom-call | flops 402653184 | bytes 5369856 | tf_op jit(solution)/shard_map/turn_halo/pallas_call | solution.py:241
  28.8 1.5 %last_weights.1 = (bf16[768,512]{1,0:T(8,128)(2,1)S(1)}, bf16[768,512]{1,0:T(8,128)(2,1)S(1)}, bf16[256,512]{1,0:T(8,128)(2,1)}) custom-call(s32[1,6]{1,0:T(1,128)S(1)} %get-tuple-element.172.refs_0_.refs_5_, bf16[256,512]{1,0:T(8,128)(2,1)S(1)} %get-tuple-element.196.state_ref.refs_1_, bf16[256,512]{1,0:T(8,128)(2,1)S(1)} %get-tuple-element.216.refs_2_, ...), custom_call_target="tpu_custom_call" | custom-call | flops 536870912 | bytes 4194328 | tf_op jit(solution)/shard_map/last_weights/pallas_call | solution.py:241
  31.8 1.1 %collective-permute-start.18 = (bf16[8,512]{1,0:T(8,128)(2,1)S(1)}, bf16[8,512]{1,0:T(8,128)(2,1)S(1)}, u32[]{:S(2)}, u32[]{:S(2)}) collective-permute-start(bf16[8,512]{1,0:T(8,128)(2,1)S(1)} %get-tuple-element.237), channel_id=1, source_target_pairs={{0,4},{4,0},{8,12},{12,8},{1,5},{5,1},{9,13},{13,9},{2,6},{6,2},{1... | collective-permute-start | bytes 24584 | tf_op jit(solution)/shard_map/ppermute | solution.py:258
  34.5 2.7 %back_local.1 = (f32[256,512]{1,0:T(8,128)S(1)}, bf16[512,512]{1,0:T(8,128)(2,1)S(1)}, bf16[512,512]{1,0:T(8,128)(2,1)S(1)}, bf16[512,512]{1,0:T(8,128)(2,1)S(1)}, bf16[512,512]{1,0:T(8,128)(2,1)S(1)}) custom-call(s32[1,6]{1,0:T(1,128)S(1)} %get-tuple-element.172.refs_0_.refs_5_, bf16[256,512]{1,0:T(8,128)(2,1)S(1)} %get-tuple-element.220.refs_1_, ...), custom_call_target="tpu_custom_call" | custom-call | flops 1342177280 | bytes 9773080 | tf_op jit(solution)/shard_map/back_local/pallas_call | solution.py:241
  39.9 2.3 %embed_back.1 = (bf16[512,512]{1,0:T(8,128)(2,1)S(1)}, bf16[256,512]{1,0:T(8,128)(2,1)S(1)}, bf16[288,512]{1,0:T(8,128)(2,1)S(1)}, bf16[16,512]{1,0:T(8,128)(2,1...) custom-call(bf16[8,512]{1,0:T(8,128)(2,1)S(1)} %collective-permute-d, ...), custom_call_target="tpu_custom_call" | custom-call | flops 805306368 | bytes 6191448 | tf_op jit(solution)/shard_map/embed_back/pallas_call | solution.py:241
  44.0 6.1 %collective-permute-done.23.refs_2_ = bf16[384,512]{1,0:T(8,128)(2,1)S(1)} collective-permute-done((bf16[384,512]{1,0:T(8,128)(2,1)S(1)}, bf16[384,512]{1,0:T(8,128)(2,1)S(1)}, u32[]{:S(2)}, u32[]{:S(2)}) %collective-permute-start.23) | collective-permute-done | bytes 393248 | tf_op jit(solution)/shard_map/ppermute | solution.py:169
  50.3 1.1 %collective-permute-start.27 = (bf16[192,512]{1,0:T(8,128)(2,1)S(1)}, bf16[192,512]{1,0:T(8,128)(2,1)S(1)}, u32[]{:S(2)}, u32[]{:S(2)}) collective-permute-start(bf16[192,512]{1,0:T(8,128)(2,1)S(1)} %get-tuple-element.285), channel_id=1, source_target_pairs={{0,4},{1,5},{2,6},{3,7},{4,0},{5,1},{6,2},{7,3},{8,12},{9,13},{10,... | collective-permute-start | bytes 589832 | tf_op jit(solution)/shard_map/ppermute | solution.py:169
  53.8 1.9 %collective-permute-done.25.refs_2_ = bf16[256,512]{1,0:T(8,128)(2,1)S(1)} collective-permute-done((bf16[256,512]{1,0:T(8,128)(2,1)S(1)}, bf16[256,512]{1,0:T(8,128)(2,1)S(1)}, u32[]{:S(2)}, u32[]{:S(2)}) %collective-permute-start.25) | collective-permute-done | bytes 262176 | tf_op jit(solution)/shard_map/ppermute | solution.py:169
  55.8 1.1 %collective-permute-start.29 = (bf16[128,512]{1,0:T(8,128)(2,1)S(1)}, bf16[128,512]{1,0:T(8,128)(2,1)S(1)}, u32[]{:S(2)}, u32[]{:S(2)}) collective-permute-start(bf16[128,512]{1,0:T(8,128)(2,1)S(1)} %get-tuple-element.296), channel_id=1, source_target_pairs={{0,4},{1,5},{2,6},{3,7},{4,0},{5,1},{6,2},{7,3},{8,12},{9,13},{10,... | collective-permute-start | bytes 393224 | tf_op jit(solution)/shard_map/ppermute | solution.py:169
  56.9 4.4 %collective-permute-done.26.refs_2_ = bf16[160,512]{1,0:T(8,128)(2,1)S(1)} collective-permute-done((bf16[160,512]{1,0:T(8,128)(2,1)S(1)}, bf16[160,512]{1,0:T(8,128)(2,1)S(1)}, u32[]{:S(2)}, u32[]{:S(2)}) %collective-permute-start.26) | collective-permute-done | bytes 163872 | tf_op jit(solution)/shard_map/ppermute | solution.py:169
  61.5 2.8 %collective-permute-start.30 = (bf16[96,512]{1,0:T(8,128)(2,1)S(1)}, bf16[96,512]{1,0:T(8,128)(2,1)S(1)}, u32[]{:S(2)}, u32[]{:S(2)}) collective-permute-start(bf16[96,512]{1,0:T(8,128)(2,1)S(1)} %get-tuple-element.298), channel_id=1, source_target_pairs={{0,8},{1,9},{2,10},{3,11},{4,12},{5,13},{6,14},{7,15},{8,0},{9,1},... | collective-permute-start | bytes 294920 | tf_op jit(solution)/shard_map/ppermute | solution.py:169
  64.5 6.0 %collective-permute-done.28.refs_2_ = bf16[80,512]{1,0:T(8,128)(2,1)S(1)} collective-permute-done((bf16[80,512]{1,0:T(8,128)(2,1)S(1)}, bf16[80,512]{1,0:T(8,128)(2,1)S(1)}, u32[]{:S(2)}, u32[]{:S(2)}) %collective-permute-start.28) | collective-permute-done | bytes 81952 | tf_op jit(solution)/shard_map/ppermute | solution.py:169
  71.0 1.1 %collective-permute-start.35 = (bf16[64,512]{1,0:T(8,128)(2,1)S(1)}, bf16[64,512]{1,0:T(8,128)(2,1)S(1)}, u32[]{:S(2)}, u32[]{:S(2)}) collective-permute-start(bf16[64,512]{1,0:T(8,128)(2,1)S(1)} %get-tuple-element.309), channel_id=1, source_target_pairs={{0,2},{1,3},{2,0},{3,1},{4,6},{5,7},{6,4},{7,5},{8,10},{9,11},{10,... | collective-permute-start | bytes 196616 | tf_op jit(solution)/shard_map/ppermute | solution.py:169
  72.1 2.6 %collective-permute-start.31 = (bf16[64,512]{1,0:T(8,128)(2,1)S(1)}, bf16[64,512]{1,0:T(8,128)(2,1)S(1)}, u32[]{:S(2)}, u32[]{:S(2)}) collective-permute-start(bf16[64,512]{1,0:T(8,128)(2,1)S(1)} %get-tuple-element.301), channel_id=1, source_target_pairs={{0,8},{1,9},{2,10},{3,11},{4,12},{5,13},{6,14},{7,15},{8,0},{9,1},... | collective-permute-start | bytes 196616 | tf_op jit(solution)/shard_map/ppermute | solution.py:169
  74.7 1.7 %collective-permute-done.33.refs_2_ = bf16[128,512]{1,0:T(8,128)(2,1)S(1)} collective-permute-done((bf16[128,512]{1,0:T(8,128)(2,1)S(1)}, bf16[128,512]{1,0:T(8,128)(2,1)S(1)}, u32[]{:S(2)}, u32[]{:S(2)}) %collective-permute-start.33) | collective-permute-done | bytes 131104 | tf_op jit(solution)/shard_map/ppermute | solution.py:169
  77.4 4.6 %collective-permute-done.34.refs_5_ = bf16[64,512]{1,0:T(8,128)(2,1)S(1)} collective-permute-done((bf16[64,512]{1,0:T(8,128)(2,1)S(1)}, bf16[64,512]{1,0:T(8,128)(2,1)S(1)}, u32[]{:S(2)}, u32[]{:S(2)}) %collective-permute-start.34) | collective-permute-done | bytes 65568 | tf_op jit(solution)/shard_map/ppermute | solution.py:169
  82.1 1.2 %finish_all.1 = (bf16[512,512]{1,0:T(8,128)(2,1)}, f32[32,512]{1,0:T(8,128)}, f32[32,512]{1,0:T(8,128)}, f32[2,32,512]{2,1,0:T(8,128)}, f32[2,32,512]{2,1,0:T(8,128)}, /*index=5*/f32[2,32,512]{2,1,0:T(8,128)}) custom-call(bf16[96,512]{1,0:T(8,128)(2,1)S(1)} %get-tuple-element.287.refs_0_, bf16[96,512]{1,0:T(8,128)(2,1)S(1)} %collective-permute-done.30.refs_1_, ...), custom_call_target="tpu_custom_call" | custom-call | flops 134217728 | bytes 2179392 | tf_op jit(solution)/shard_map/finish_all/pallas_call | solution.py:241
  (79 shorter events, 21.5 us)
Async XLA Ops:
  2.1 9.0 %collective-permute-start = (bf16[16,512]{1,0:T(8,128)(2,1)S(1)}, bf16[16,512]{1,0:T(8,128)(2,1)S(1)}, u32[]{:S(2)}, u32[]{:S(2)}) collective-permute-start(bf16[16,512]{1,0:T(8,128)(2,1)S(1)} %get-tuple-element.173), channel_id=1, source_target_pairs={{0,12},{4,8},{8,4},{12,0},{1,13},{5,9},{9,5},{13,1},{2,14},{6,10},... | collective-permute-start | bytes 49160 | tf_op jit(solution)/shard_map/ppermute | solution.py:257
  12.7 6.0 %collective-permute-start.5 = (bf16[32,512]{1,0:T(8,128)(2,1)S(1)}, bf16[32,512]{1,0:T(8,128)(2,1)S(1)}, u32[]{:S(2)}, u32[]{:S(2)}) collective-permute-start(bf16[32,512]{1,0:T(8,128)(2,1)S(1)} %get-tuple-element.185), channel_id=1, source_target_pairs={{0,12},{4,8},{8,4},{12,0},{1,13},{5,9},{9,5},{13,1},{2,14},{6,10},... | collective-permute-start | bytes 98312 | tf_op jit(solution)/shard_map/ppermute | solution.py:257
  13.8 4.9 %collective-permute-start.6 = (bf16[32,512]{1,0:T(8,128)(2,1)S(1)}, bf16[32,512]{1,0:T(8,128)(2,1)S(1)}, u32[]{:S(2)}, u32[]{:S(2)}) collective-permute-start(bf16[32,512]{1,0:T(8,128)(2,1)S(1)} %get-tuple-element.186), channel_id=1, source_target_pairs={{0,4},{4,0},{8,12},{12,8},{1,5},{5,1},{9,13},{13,9},{2,6},{6,2},{1... | collective-permute-start | bytes 98312 | tf_op jit(solution)/shard_map/ppermute | solution.py:258
  19.9 7.6 %collective-permute-start.10 = (bf16[16,512]{1,0:T(8,128)(2,1)S(1)}, bf16[16,512]{1,0:T(8,128)(2,1)S(1)}, u32[]{:S(2)}, u32[]{:S(2)}) collective-permute-start(bf16[16,512]{1,0:T(8,128)(2,1)S(1)} %get-tuple-element.197), channel_id=1, source_target_pairs={{0,12},{4,8},{8,4},{12,0},{1,13},{5,9},{9,5},{13,1},{2,14},{6,10},... | collective-permute-start | bytes 49160 | tf_op jit(solution)/shard_map/ppermute | solution.py:257
  22.6 4.8 %collective-permute-start.11 = (bf16[16,512]{1,0:T(8,128)(2,1)S(1)}, bf16[16,512]{1,0:T(8,128)(2,1)S(1)}, u32[]{:S(2)}, u32[]{:S(2)}) collective-permute-start(bf16[16,512]{1,0:T(8,128)(2,1)S(1)} %get-tuple-element.198), channel_id=1, source_target_pairs={{0,4},{4,0},{8,12},{12,8},{1,5},{5,1},{9,13},{13,9},{2,6},{6,2},{1... | collective-permute-start | bytes 49160 | tf_op jit(solution)/shard_map/ppermute | solution.py:258
  22.8 4.7 %collective-permute-start.12 = (bf16[16,512]{1,0:T(8,128)(2,1)S(1)}, bf16[16,512]{1,0:T(8,128)(2,1)S(1)}, u32[]{:S(2)}, u32[]{:S(2)}) collective-permute-start(bf16[16,512]{1,0:T(8,128)(2,1)S(1)} %get-tuple-element.199), channel_id=1, source_target_pairs={{0,3},{1,2},{2,1},{3,0},{4,7},{5,6},{6,5},{7,4},{8,11},{9,10},{10,... | collective-permute-start | bytes 49160 | tf_op jit(solution)/shard_map/ppermute | solution.py:260
  23.1 4.4 %collective-permute-start.13 = (bf16[16,512]{1,0:T(8,128)(2,1)S(1)}, bf16[16,512]{1,0:T(8,128)(2,1)S(1)}, u32[]{:S(2)}, u32[]{:S(2)}) collective-permute-start(bf16[16,512]{1,0:T(8,128)(2,1)S(1)} %get-tuple-element.200), channel_id=1, source_target_pairs={{0,2},{1,3},{2,0},{3,1},{4,6},{5,7},{6,4},{7,5},{8,10},{9,11},{10,... | collective-permute-start | bytes 49160 | tf_op jit(solution)/shard_map/ppermute | solution.py:260
  30.8 6.5 %collective-permute-start.17 = (bf16[8,512]{1,0:T(8,128)(2,1)S(1)}, bf16[8,512]{1,0:T(8,128)(2,1)S(1)}, u32[]{:S(2)}, u32[]{:S(2)}) collective-permute-start(bf16[8,512]{1,0:T(8,128)(2,1)S(1)} %get-tuple-element.236), channel_id=1, source_target_pairs={{0,12},{4,8},{8,4},{12,0},{1,13},{5,9},{9,5},{13,1},{2,14},{6,10},... | collective-permute-start | bytes 24584 | tf_op jit(solution)/shard_map/ppermute | solution.py:257
  31.8 5.5 %collective-permute-start.18 = (bf16[8,512]{1,0:T(8,128)(2,1)S(1)}, bf16[8,512]{1,0:T(8,128)(2,1)S(1)}, u32[]{:S(2)}, u32[]{:S(2)}) collective-permute-start(bf16[8,512]{1,0:T(8,128)(2,1)S(1)} %get-tuple-element.237), channel_id=1, source_target_pairs={{0,4},{4,0},{8,12},{12,8},{1,5},{5,1},{9,13},{13,9},{2,6},{6,2},{1... | collective-permute-start | bytes 24584 | tf_op jit(solution)/shard_map/ppermute | solution.py:258
  32.9 4.4 %collective-permute-start.19 = (bf16[8,512]{1,0:T(8,128)(2,1)S(1)}, bf16[8,512]{1,0:T(8,128)(2,1)S(1)}, u32[]{:S(2)}, u32[]{:S(2)}) collective-permute-start(bf16[8,512]{1,0:T(8,128)(2,1)S(1)} %get-tuple-element.238), channel_id=1, source_target_pairs={{0,3},{1,2},{2,1},{3,0},{4,7},{5,6},{6,5},{7,4},{8,11},{9,10},{10,... | collective-permute-start | bytes 24584 | tf_op jit(solution)/shard_map/ppermute | solution.py:260
  38.1 14.5 %collective-permute-start.24 = (bf16[512,512]{1,0:T(8,128)(2,1)S(1)}, bf16[512,512]{1,0:T(8,128)(2,1)S(1)}, u32[]{:S(2)}, u32[]{:S(2)}) collective-permute-start(bf16[512,512]{1,0:T(8,128)(2,1)S(1)} %get-tuple-element.275), channel_id=1, source_target_pairs={{0,1},{1,0},{2,3},{3,2},{4,5},{5,4},{6,7},{7,6},{8,9},{9,8},{10,11... | collective-permute-start | bytes 1572872 | tf_op jit(solution)/shard_map/ppermute | solution.py:169
  38.2 11.9 %collective-permute-start.23 = (bf16[384,512]{1,0:T(8,128)(2,1)S(1)}, bf16[384,512]{1,0:T(8,128)(2,1)S(1)}, u32[]{:S(2)}, u32[]{:S(2)}) collective-permute-start(bf16[384,512]{1,0:T(8,128)(2,1)S(1)} %get-tuple-element.262), channel_id=1, source_target_pairs={{0,2},{1,3},{2,0},{3,1},{4,6},{5,7},{6,4},{7,5},{8,10},{9,11},{10,... | collective-permute-start | bytes 1179656 | tf_op jit(solution)/shard_map/ppermute | solution.py:169
  42.2 7.8 %collective-permute-start.22 = (bf16[288,512]{1,0:T(8,128)(2,1)S(1)}, bf16[288,512]{1,0:T(8,128)(2,1)S(1)}, u32[]{:S(2)}, u32[]{:S(2)}) collective-permute-start(bf16[288,512]{1,0:T(8,128)(2,1)S(1)} %get-tuple-element.261), channel_id=1, source_target_pairs={{0,1},{1,0},{2,3},{3,2},{4,5},{5,4},{6,7},{7,6},{8,9},{9,8},{10,11... | collective-permute-start | bytes 884744 | tf_op jit(solution)/shard_map/ppermute | solution.py:169
  42.6 13.1 %collective-permute-start.25 = (bf16[256,512]{1,0:T(8,128)(2,1)S(1)}, bf16[256,512]{1,0:T(8,128)(2,1)S(1)}, u32[]{:S(2)}, u32[]{:S(2)}) collective-permute-start(bf16[256,512]{1,0:T(8,128)(2,1)S(1)} %get-tuple-element.278), channel_id=1, source_target_pairs={{0,2},{1,3},{2,0},{3,1},{4,6},{5,7},{6,4},{7,5},{8,10},{9,11},{10,... | collective-permute-start | bytes 786440 | tf_op jit(solution)/shard_map/ppermute | solution.py:169
  50.3 11.1 %collective-permute-start.27 = (bf16[192,512]{1,0:T(8,128)(2,1)S(1)}, bf16[192,512]{1,0:T(8,128)(2,1)S(1)}, u32[]{:S(2)}, u32[]{:S(2)}) collective-permute-start(bf16[192,512]{1,0:T(8,128)(2,1)S(1)} %get-tuple-element.285), channel_id=1, source_target_pairs={{0,4},{1,5},{2,6},{3,7},{4,0},{5,1},{6,2},{7,3},{8,12},{9,13},{10,... | collective-permute-start | bytes 589832 | tf_op jit(solution)/shard_map/ppermute | solution.py:169
  51.5 9.8 %collective-permute-start.26 = (bf16[160,512]{1,0:T(8,128)(2,1)S(1)}, bf16[160,512]{1,0:T(8,128)(2,1)S(1)}, u32[]{:S(2)}, u32[]{:S(2)}) collective-permute-start(bf16[160,512]{1,0:T(8,128)(2,1)S(1)} %get-tuple-element.281), channel_id=1, source_target_pairs={{0,4},{1,5},{2,6},{3,7},{4,0},{5,1},{6,2},{7,3},{8,12},{9,13},{10,... | collective-permute-start | bytes 491528 | tf_op jit(solution)/shard_map/ppermute | solution.py:169
  52.9 17.9 %collective-permute-start.32 = (bf16[256,512]{1,0:T(8,128)(2,1)S(1)}, bf16[256,512]{1,0:T(8,128)(2,1)S(1)}, u32[]{:S(2)}, u32[]{:S(2)}) collective-permute-start(bf16[256,512]{1,0:T(8,128)(2,1)S(1)} %get-tuple-element.303), channel_id=1, source_target_pairs={{0,2},{1,3},{2,0},{3,1},{4,6},{5,7},{6,4},{7,5},{8,10},{9,11},{10,... | collective-permute-start | bytes 786440 | tf_op jit(solution)/shard_map/ppermute | solution.py:169
  55.8 14.8 %collective-permute-start.29 = (bf16[128,512]{1,0:T(8,128)(2,1)S(1)}, bf16[128,512]{1,0:T(8,128)(2,1)S(1)}, u32[]{:S(2)}, u32[]{:S(2)}) collective-permute-start(bf16[128,512]{1,0:T(8,128)(2,1)S(1)} %get-tuple-element.296), channel_id=1, source_target_pairs={{0,4},{1,5},{2,6},{3,7},{4,0},{5,1},{6,2},{7,3},{8,12},{9,13},{10,... | collective-permute-start | bytes 393224 | tf_op jit(solution)/shard_map/ppermute | solution.py:169
  61.5 9.2 %collective-permute-start.30 = (bf16[96,512]{1,0:T(8,128)(2,1)S(1)}, bf16[96,512]{1,0:T(8,128)(2,1)S(1)}, u32[]{:S(2)}, u32[]{:S(2)}) collective-permute-start(bf16[96,512]{1,0:T(8,128)(2,1)S(1)} %get-tuple-element.298), channel_id=1, source_target_pairs={{0,8},{1,9},{2,10},{3,11},{4,12},{5,13},{6,14},{7,15},{8,0},{9,1},... | collective-permute-start | bytes 294920 | tf_op jit(solution)/shard_map/ppermute | solution.py:169
  64.3 6.3 %collective-permute-start.28 = (bf16[80,512]{1,0:T(8,128)(2,1)S(1)}, bf16[80,512]{1,0:T(8,128)(2,1)S(1)}, u32[]{:S(2)}, u32[]{:S(2)}) collective-permute-start(bf16[80,512]{1,0:T(8,128)(2,1)S(1)} %get-tuple-element.291), channel_id=1, source_target_pairs={{0,8},{1,9},{2,10},{3,11},{4,12},{5,13},{6,14},{7,15},{8,0},{9,1},... | collective-permute-start | bytes 245768 | tf_op jit(solution)/shard_map/ppermute | solution.py:169
  70.9 5.5 %collective-permute-start.33 = (bf16[128,512]{1,0:T(8,128)(2,1)S(1)}, bf16[128,512]{1,0:T(8,128)(2,1)S(1)}, u32[]{:S(2)}, u32[]{:S(2)}) collective-permute-start(bf16[128,512]{1,0:T(8,128)(2,1)S(1)} %get-tuple-element.305), channel_id=1, source_target_pairs={{0,4},{1,5},{2,6},{3,7},{4,0},{5,1},{6,2},{7,3},{8,12},{9,13},{10,... | collective-permute-start | bytes 393224 | tf_op jit(solution)/shard_map/ppermute | solution.py:169
  71.0 6.5 %collective-permute-start.35 = (bf16[64,512]{1,0:T(8,128)(2,1)S(1)}, bf16[64,512]{1,0:T(8,128)(2,1)S(1)}, u32[]{:S(2)}, u32[]{:S(2)}) collective-permute-start(bf16[64,512]{1,0:T(8,128)(2,1)S(1)} %get-tuple-element.309), channel_id=1, source_target_pairs={{0,2},{1,3},{2,0},{3,1},{4,6},{5,7},{6,4},{7,5},{8,10},{9,11},{10,... | collective-permute-start | bytes 196616 | tf_op jit(solution)/shard_map/ppermute | solution.py:169
  72.1 5.3 %collective-permute-start.31 = (bf16[64,512]{1,0:T(8,128)(2,1)S(1)}, bf16[64,512]{1,0:T(8,128)(2,1)S(1)}, u32[]{:S(2)}, u32[]{:S(2)}) collective-permute-start(bf16[64,512]{1,0:T(8,128)(2,1)S(1)} %get-tuple-element.301), channel_id=1, source_target_pairs={{0,8},{1,9},{2,10},{3,11},{4,12},{5,13},{6,14},{7,15},{8,0},{9,1},... | collective-permute-start | bytes 196616 | tf_op jit(solution)/shard_map/ppermute | solution.py:169
  76.5 5.6 %collective-permute-start.34 = (bf16[64,512]{1,0:T(8,128)(2,1)S(1)}, bf16[64,512]{1,0:T(8,128)(2,1)S(1)}, u32[]{:S(2)}, u32[]{:S(2)}) collective-permute-start(bf16[64,512]{1,0:T(8,128)(2,1)S(1)} %get-tuple-element.307), channel_id=1, source_target_pairs={{0,8},{1,9},{2,10},{3,11},{4,12},{5,13},{6,14},{7,15},{8,0},{9,1},... | collective-permute-start | bytes 196616 | tf_op jit(solution)/shard_map/ppermute | solution.py:169
  (15 other events, 59.1 us)

commit v19 on v17

--- a/solution.py
+++ b/solution.py
@@ -256,7 +256,13 @@
         lax.ppermute(parts[r - 1], COLUMN, [(i, i ^ r) for i in range(column)])
         for r in range(column - 1, 0, -1)
     ]
-    return (far, near, *arrived)
+    *others, first = arrived
+    return (far, *others[::-1], near, first)
+
+
+def in_order(arrived):
+    far, *others, near, first = arrived
+    return (first, *others, near, far)
 
 
 def shape(*dims, dtype=BF):
@@ -337,7 +343,7 @@
 
 
 def merge_nodes(peers, *refs):
-    arr_refs, refs = refs[:peers][::-1], refs[peers:]
+    arr_refs, refs = in_order(refs[:peers]), refs[peers:]
     (incoming_ref, embed_ref, local_ref, mesh_ref, weight_ref, border_ref, back_ref, cot_ref,
      merged_ref, state_ref, slope_ref, lat_ref, *pay_refs) = refs
     lat = jnp.concatenate([ref[...] for ref in arr_refs], axis=0)
@@ -393,7 +399,7 @@
 
 
 def forward_halo(peers, *refs):
-    arr_refs, refs = refs[:peers][::-1], refs[peers:]
+    arr_refs, refs = in_order(refs[:peers]), refs[peers:]
     (recv_n_ref, total_ref, state_ref, send_ref, update_ref, back_t_ref, back_in_ref,
      border_ref, summed_ref, out_ref, pre_ref, rows_ref, back_ref, merged_ref, cot_ref,
      *pay_refs) = refs
@@ -449,7 +455,7 @@
 
 
 def turn_halo(peers, *refs):
-    arr_refs, refs = refs[:peers][::-1], refs[peers:]
+    arr_refs, refs = in_order(refs[:peers]), refs[peers:]
     (recv_n_ref, sent_b_ref, gsum_n_ref, gsum_r_ref, total_ref, grecv_ref, gsent_ref, cot_ref,
      send_ref, recv_ref, back_t_ref, back_in_ref, border_t_ref, summed_ref, grecv_out_ref,
      gsent_out_ref, gin_ref, *pay_refs) = refs
@@ -526,7 +532,7 @@
 
 
 def embed_back(peers, dims, carry, *refs):
-    arr_refs, refs = refs[:peers][::-1], refs[peers:]
+    arr_refs, refs = in_order(refs[:peers]), refs[peers:]
     (place_ref, slope_r_ref, part_ref, update_ref, send_ref, merge_ref, border_t_ref, target_ref,
      sends_ref, incoming_ref, slope_g_ref, slope_a_ref, grid_ref, lat_ref, embed_ref,
      gpre_ref, keep_ref, give_ref, *pay_refs) = refs
@@ -572,7 +578,7 @@
 
 
 def grid_place(peers, *refs):
-    arr_refs, (local_ref, sends_ref, out_ref) = refs[:peers][::-1], refs[peers:]
+    arr_refs, (local_ref, sends_ref, out_ref) = in_order(refs[:peers]), refs[peers:]
     grid_patch(local_ref, sends_ref, arr_refs, out_ref)
 
 

time: 78 us -> 78.7 us (level)
  starting transfers between devices: 36.8 us -> 37.6 us
    ppermute x16, starting transfers between devices: 18.2 us -> 19.5 us  [swap(): return lax.ppermute(block, GROUP, [(i, i ^ 1 << bit) for i in range(total)])]
    ppermute x16, waiting for transfers between devices: 17.2 us -> 16.1 us  [swap(): return lax.ppermute(block, GROUP, [(i, i ^ 1 << bit) for i in range(total)])]
    ppermute x4, waiting for transfers between devices: 0.01 us -> 0.97 us  [exchange(): lax.ppermute(parts[column - 1], 'lon', [(i, i ^ 1) for i in range(count)])]
  transfers between devices with their start and end apart: 36 -> 36, of which waited for: 11 -> 14; matrix products, arithmetic and copies ran while one was open for 0% -> 0% of each run, Pallas kernels for 21% -> 21%
where the time goes in v19:
time: 78.7 us; the launch traced here: 78.5 us
  starting transfers between devices  37.6 us (48%)
  Pallas kernels  21.6 us (27%)
  waiting for transfers between devices  18.4 us (23%)
  between operations  0.92 us (1%)
    pallas_call x24, Pallas kernels, call(): pl.pallas_call(kernel, out_shape=[shape(*a.shape, dtype=a.dtype) for a in...  21.6 us
    ppermute x16, starting transfers between devices, swap(): return lax.ppermute(block, GROUP, [(i, i ^ 1 << bit) for i in range(total)])  19.5 us
    ppermute x16, waiting for transfers between devices, swap(): return lax.ppermute(block, GROUP, [(i, i ^ 1 << bit) for i in range(total)])  16.1 us
    ppermute x4, starting transfers between devices, exchange(): far = lax.ppermute(parts[column], 'lon', other)  9.25 us
    ppermute x12, starting transfers between devices, exchange(): lax.ppermute(parts[r - 1], COLUMN, [(i, i ^ r) for i in range(column)])  7.26 us
  transfers between devices with their start and end apart: 36, of which 14 were waited for; matrix products, arithmetic and copies ran while one was open for 0% of the time, Pallas kernels for 21%

profile of v19, /device:TPU:0, one launch (start us, length us, event | category | flops | bytes accessed | tf_op | source)
XLA Modules:
  0.0 78.5 jit_solution(1954108638042938882)
XLA Ops:
  0.8 1.3 %first_payload.1 = (s32[6,1,16]{2,1,0:T(1,128)S(1)}, bf16[512,512]{1,0:T(8,128)(2,1)S(1)}, bf16[512,512]{1,0:T(8,128)(2,1)S(1)}, s32[1,512]{1,0:T(1,128)S(1)}, s...) custom-call(s32[6,1,16]{2,1,0:T(1,128)} %bitcast.15, ...), custom_call_target="tpu_custom_call" | custom-call | flops 67108864 | bytes 1139992 | tf_op jit(solution)/shard_map/first_payload/pallas_call | solution.py:237
  2.1 5.1 %collective-permute-start = (bf16[16,512]{1,0:T(8,128)(2,1)S(1)}, bf16[16,512]{1,0:T(8,128)(2,1)S(1)}, u32[]{:S(2)}, u32[]{:S(2)}) collective-permute-start(bf16[16,512]{1,0:T(8,128)(2,1)S(1)} %get-tuple-element.175), channel_id=1, source_target_pairs={{0,12},{4,8},{8,4},{12,0},{1,13},{5,9},{9,5},{13,1},{2,14},{6,10},... | collective-permute-start | bytes 49160 | tf_op jit(solution)/shard_map/ppermute | solution.py:253
  7.2 1.5 %collective-permute-start.1 = (bf16[16,512]{1,0:T(8,128)(2,1)S(1)}, bf16[16,512]{1,0:T(8,128)(2,1)S(1)}, u32[]{:S(2)}, u32[]{:S(2)}) collective-permute-start(bf16[16,512]{1,0:T(8,128)(2,1)S(1)} %get-tuple-element.176), channel_id=1, source_target_pairs={{0,2},{1,3},{2,0},{3,1},{4,6},{5,7},{6,4},{7,5},{8,10},{9,11},{10,... | collective-permute-start | bytes 49160 | tf_op jit(solution)/shard_map/ppermute | solution.py:256
  9.4 2.0 %embed_local.1 = (bf16[256,512]{1,0:T(8,128)(2,1)S(1)}, bf16[512,512]{1,0:T(8,128)(2,1)S(1)}, bf16[256,512]{1,0:T(8,128)(2,1)S(1)}, f32[256,512]{1,0:T(8,128)S(1...) custom-call(bf16[256,512]{1,0:T(8,128)(2,1)} %refs_0_.1, ...), custom_call_target="tpu_custom_call" | custom-call | flops 402653184 | bytes 3292784 | tf_op jit(solution)/shard_map/embed_local/pallas_call | solution.py:237
  13.8 1.4 %collective-permute-start.6 = (bf16[32,512]{1,0:T(8,128)(2,1)S(1)}, bf16[32,512]{1,0:T(8,128)(2,1)S(1)}, u32[]{:S(2)}, u32[]{:S(2)}) collective-permute-start(bf16[32,512]{1,0:T(8,128)(2,1)S(1)} %get-tuple-element.188), channel_id=1, source_target_pairs={{0,2},{1,3},{2,0},{3,1},{4,6},{5,7},{6,4},{7,5},{8,10},{9,11},{10,... | collective-permute-start | bytes 98312 | tf_op jit(solution)/shard_map/ppermute | solution.py:256
  16.1 2.4 %forward_local.1 = (f32[256,512]{1,0:T(8,128)S(1)}, bf16[6,256,512]{2,1,0:T(8,128)(2,1)S(1)}, f32[40,512]{1,0:T(8,128)S(1)}, bf16[40,512]{1,0:T(8,128)(2,1)S(1)}...) custom-call(bf16[256,512]{1,0:T(8,128)(2,1)S(1)} %get-tuple-element.192.state_ref.refs_7_.refs_11_, ...), custom_call_target="tpu_custom_call" | custom-call | flops 805306368 | bytes 6993920 | tf_op jit(solution)/shard_map/forward_local/pallas_call | solution.py:237
  20.4 2.6 %collective-permute-start.10 = (bf16[16,512]{1,0:T(8,128)(2,1)S(1)}, bf16[16,512]{1,0:T(8,128)(2,1)S(1)}, u32[]{:S(2)}, u32[]{:S(2)}) collective-permute-start(bf16[16,512]{1,0:T(8,128)(2,1)S(1)} %get-tuple-element.199), channel_id=1, source_target_pairs={{0,12},{4,8},{8,4},{12,0},{1,13},{5,9},{9,5},{13,1},{2,14},{6,10},... | collective-permute-start | bytes 49160 | tf_op jit(solution)/shard_map/ppermute | solution.py:253
  23.0 1.4 %collective-permute-start.11 = (bf16[16,512]{1,0:T(8,128)(2,1)S(1)}, bf16[16,512]{1,0:T(8,128)(2,1)S(1)}, u32[]{:S(2)}, u32[]{:S(2)}) collective-permute-start(bf16[16,512]{1,0:T(8,128)(2,1)S(1)} %get-tuple-element.200), channel_id=1, source_target_pairs={{0,2},{1,3},{2,0},{3,1},{4,6},{5,7},{6,4},{7,5},{8,10},{9,11},{10,... | collective-permute-start | bytes 49160 | tf_op jit(solution)/shard_map/ppermute | solution.py:256
  25.4 2.7 %turn_local.1 = (f32[256,512]{1,0:T(8,128)S(1)}, f32[256,512]{1,0:T(8,128)S(1)}, f32[256,512]{1,0:T(8,128)S(1)}, f32[40,512]{1,0:T(8,128)S(1)}, bf16[40,512]{1,0...) custom-call(bf16[256,512]{1,0:T(8,128)(2,1)S(1)} %get-tuple-element., ...), custom_call_target="tpu_custom_call" | custom-call | flops 1342177280 | bytes 6692864 | tf_op jit(solution)/shard_map/turn_local/pallas_call | solution.py:237
  28.2 1.2 %turn_halo.1 = (bf16[256,512]{1,0:T(8,128)(2,1)S(1)}, bf16[256,512]{1,0:T(8,128)(2,1)S(1)}, bf16[256,512]{1,0:T(8,128)(2,1)S(1)}, bf16[256,512]{1,0:T(8,128)(2,1...) custom-call(bf16[16,512]{1,0:T(8,128)(2,1)S(1)} %collective-permute-, ...), custom_call_target="tpu_custom_call" | custom-call | flops 402653184 | bytes 5369856 | tf_op jit(solution)/shard_map/turn_halo/pallas_call | solution.py:237
  29.5 1.5 %last_weights.1 = (bf16[768,512]{1,0:T(8,128)(2,1)S(1)}, bf16[768,512]{1,0:T(8,128)(2,1)S(1)}, bf16[256,512]{1,0:T(8,128)(2,1)}) custom-call(s32[1,6]{1,0:T(1,128)S(1)} %get-tuple-element.174.refs_0_.refs_5_, bf16[256,512]{1,0:T(8,128)(2,1)S(1)} %get-tuple-element.198.state_ref.refs_1_, bf16[256,512]{1,0:T(8,128)(2,1)S(1)} %get-tuple-element.218.refs_2_, ...), custom_call_target="tpu_custom_call" | custom-call | flops 536870912 | bytes 4194328 | tf_op jit(solution)/shard_map/last_weights/pallas_call | solution.py:237
  35.0 2.7 %back_local.1 = (f32[256,512]{1,0:T(8,128)S(1)}, bf16[512,512]{1,0:T(8,128)(2,1)S(1)}, bf16[512,512]{1,0:T(8,128)(2,1)S(1)}, bf16[512,512]{1,0:T(8,128)(2,1)S(1)}, bf16[512,512]{1,0:T(8,128)(2,1)S(1)}) custom-call(s32[1,6]{1,0:T(1,128)S(1)} %get-tuple-element.174.refs_0_.refs_5_, bf16[256,512]{1,0:T(8,128)(2,1)S(1)} %get-tuple-element.222.refs_1_, ...), custom_call_target="tpu_custom_call" | custom-call | flops 1342177280 | bytes 9773080 | tf_op jit(solution)/shard_map/back_local/pallas_call | solution.py:237
  40.4 2.3 %embed_back.1 = (bf16[512,512]{1,0:T(8,128)(2,1)S(1)}, bf16[256,512]{1,0:T(8,128)(2,1)S(1)}, bf16[288,512]{1,0:T(8,128)(2,1)S(1)}, bf16[16,512]{1,0:T(8,128)(2,1...) custom-call(bf16[8,512]{1,0:T(8,128)(2,1)S(1)} %collective-permute-d, ...), custom_call_target="tpu_custom_call" | custom-call | flops 805306368 | bytes 6191448 | tf_op jit(solution)/shard_map/embed_back/pallas_call | solution.py:237
  44.6 6.0 %collective-permute-done.23.refs_2_ = bf16[384,512]{1,0:T(8,128)(2,1)S(1)} collective-permute-done((bf16[384,512]{1,0:T(8,128)(2,1)S(1)}, bf16[384,512]{1,0:T(8,128)(2,1)S(1)}, u32[]{:S(2)}, u32[]{:S(2)}) %collective-permute-start.23) | collective-permute-done | bytes 393248 | tf_op jit(solution)/shard_map/ppermute | solution.py:166
  54.5 1.7 %collective-permute-done.25.refs_2_ = bf16[256,512]{1,0:T(8,128)(2,1)S(1)} collective-permute-done((bf16[256,512]{1,0:T(8,128)(2,1)S(1)}, bf16[256,512]{1,0:T(8,128)(2,1)S(1)}, u32[]{:S(2)}, u32[]{:S(2)}) %collective-permute-start.25) | collective-permute-done | bytes 262176 | tf_op jit(solution)/shard_map/ppermute | solution.py:166
  56.3 1.2 %collective-permute-start.28 = (bf16[128,512]{1,0:T(8,128)(2,1)S(1)}, bf16[128,512]{1,0:T(8,128)(2,1)S(1)}, u32[]{:S(2)}, u32[]{:S(2)}) collective-permute-start(bf16[128,512]{1,0:T(8,128)(2,1)S(1)} %get-tuple-element.291), channel_id=1, source_target_pairs={{0,4},{1,5},{2,6},{3,7},{4,0},{5,1},{6,2},{7,3},{8,12},{9,13},{10,... | collective-permute-start | bytes 393224 | tf_op jit(solution)/shard_map/ppermute | solution.py:166
  58.2 2.9 %collective-permute-start.29 = (bf16[96,512]{1,0:T(8,128)(2,1)S(1)}, bf16[96,512]{1,0:T(8,128)(2,1)S(1)}, u32[]{:S(2)}, u32[]{:S(2)}) collective-permute-start(bf16[96,512]{1,0:T(8,128)(2,1)S(1)} %get-tuple-element.293), channel_id=1, source_target_pairs={{0,8},{1,9},{2,10},{3,11},{4,12},{5,13},{6,14},{7,15},{8,0},{9,1},... | collective-permute-start | bytes 294920 | tf_op jit(solution)/shard_map/ppermute | solution.py:166
  62.0 1.2 %collective-permute-start.32 = (bf16[128,512]{1,0:T(8,128)(2,1)S(1)}, bf16[128,512]{1,0:T(8,128)(2,1)S(1)}, u32[]{:S(2)}, u32[]{:S(2)}) collective-permute-start(bf16[128,512]{1,0:T(8,128)(2,1)S(1)} %get-tuple-element.305), channel_id=1, source_target_pairs={{0,4},{1,5},{2,6},{3,7},{4,0},{5,1},{6,2},{7,3},{8,12},{9,13},{10,... | collective-permute-start | bytes 393224 | tf_op jit(solution)/shard_map/ppermute | solution.py:166
  65.0 1.2 %collective-permute-start.34 = (bf16[96,512]{1,0:T(8,128)(2,1)S(1)}, bf16[96,512]{1,0:T(8,128)(2,1)S(1)}, u32[]{:S(2)}, u32[]{:S(2)}) collective-permute-start(bf16[96,512]{1,0:T(8,128)(2,1)S(1)} %get-tuple-element.310), channel_id=1, source_target_pairs={{0,4},{1,5},{2,6},{3,7},{4,0},{5,1},{6,2},{7,3},{8,12},{9,13},{10,... | collective-permute-start | bytes 294920 | tf_op jit(solution)/shard_map/ppermute | solution.py:166
  66.2 2.2 %collective-permute-start.30 = (bf16[64,512]{1,0:T(8,128)(2,1)S(1)}, bf16[64,512]{1,0:T(8,128)(2,1)S(1)}, u32[]{:S(2)}, u32[]{:S(2)}) collective-permute-start(bf16[64,512]{1,0:T(8,128)(2,1)S(1)} %get-tuple-element.296), channel_id=1, source_target_pairs={{0,8},{1,9},{2,10},{3,11},{4,12},{5,13},{6,14},{7,15},{8,0},{9,1},... | collective-permute-start | bytes 196616 | tf_op jit(solution)/shard_map/ppermute | solution.py:166
  70.5 2.5 %collective-permute-start.35 = (bf16[48,512]{1,0:T(8,128)(2,1)S(1)}, bf16[48,512]{1,0:T(8,128)(2,1)S(1)}, u32[]{:S(2)}, u32[]{:S(2)}) collective-permute-start(bf16[48,512]{1,0:T(8,128)(2,1)S(1)} %get-tuple-element.312), channel_id=1, source_target_pairs={{0,8},{1,9},{2,10},{3,11},{4,12},{5,13},{6,14},{7,15},{8,0},{9,1},... | collective-permute-start | bytes 147464 | tf_op jit(solution)/shard_map/ppermute | solution.py:166
  73.0 2.0 %collective-permute-done.30.refs_3_ = bf16[64,512]{1,0:T(8,128)(2,1)S(1)} collective-permute-done((bf16[64,512]{1,0:T(8,128)(2,1)S(1)}, bf16[64,512]{1,0:T(8,128)(2,1)S(1)}, u32[]{:S(2)}, u32[]{:S(2)}) %collective-permute-start.30) | collective-permute-done | bytes 65568 | tf_op jit(solution)/shard_map/ppermute | solution.py:166
  75.0 2.4 %collective-permute-done.35.refs_7_ = bf16[48,512]{1,0:T(8,128)(2,1)S(1)} collective-permute-done((bf16[48,512]{1,0:T(8,128)(2,1)S(1)}, bf16[48,512]{1,0:T(8,128)(2,1)S(1)}, u32[]{:S(2)}, u32[]{:S(2)}) %collective-permute-start.35) | collective-permute-done | bytes 49184 | tf_op jit(solution)/shard_map/ppermute | solution.py:166
  77.4 1.2 %finish_all.1 = (bf16[512,512]{1,0:T(8,128)(2,1)}, f32[32,512]{1,0:T(8,128)}, f32[32,512]{1,0:T(8,128)}, f32[2,32,512]{2,1,0:T(8,128)}, f32[2,32,512]{2,1,0:T(8,128)}, /*index=5*/f32[2,32,512]{2,1,0:T(8,128)}) custom-call(bf16[96,512]{1,0:T(8,128)(2,1)S(1)} %get-tuple-element.284.refs_0_, bf16[96,512]{1,0:T(8,128)(2,1)S(1)} %collective-permute-done.29.refs_1_, ...), custom_call_target="tpu_custom_call" | custom-call | flops 134217728 | bytes 2179392 | tf_op jit(solution)/shard_map/finish_all/pallas_call | solution.py:237
  (79 shorter events, 24.8 us)
Async XLA Ops:
  2.1 9.3 %collective-permute-start = (bf16[16,512]{1,0:T(8,128)(2,1)S(1)}, bf16[16,512]{1,0:T(8,128)(2,1)S(1)}, u32[]{:S(2)}, u32[]{:S(2)}) collective-permute-start(bf16[16,512]{1,0:T(8,128)(2,1)S(1)} %get-tuple-element.175), channel_id=1, source_target_pairs={{0,12},{4,8},{8,4},{12,0},{1,13},{5,9},{9,5},{13,1},{2,14},{6,10},... | collective-permute-start | bytes 49160 | tf_op jit(solution)/shard_map/ppermute | solution.py:253
  7.2 4.2 %collective-permute-start.1 = (bf16[16,512]{1,0:T(8,128)(2,1)S(1)}, bf16[16,512]{1,0:T(8,128)(2,1)S(1)}, u32[]{:S(2)}, u32[]{:S(2)}) collective-permute-start(bf16[16,512]{1,0:T(8,128)(2,1)S(1)} %get-tuple-element.176), channel_id=1, source_target_pairs={{0,2},{1,3},{2,0},{3,1},{4,6},{5,7},{6,4},{7,5},{8,10},{9,11},{10,... | collective-permute-start | bytes 49160 | tf_op jit(solution)/shard_map/ppermute | solution.py:256
  13.4 5.9 %collective-permute-start.5 = (bf16[32,512]{1,0:T(8,128)(2,1)S(1)}, bf16[32,512]{1,0:T(8,128)(2,1)S(1)}, u32[]{:S(2)}, u32[]{:S(2)}) collective-permute-start(bf16[32,512]{1,0:T(8,128)(2,1)S(1)} %get-tuple-element.187), channel_id=1, source_target_pairs={{0,12},{4,8},{8,4},{12,0},{1,13},{5,9},{9,5},{13,1},{2,14},{6,10},... | collective-permute-start | bytes 98312 | tf_op jit(solution)/shard_map/ppermute | solution.py:253
  13.8 5.4 %collective-permute-start.6 = (bf16[32,512]{1,0:T(8,128)(2,1)S(1)}, bf16[32,512]{1,0:T(8,128)(2,1)S(1)}, u32[]{:S(2)}, u32[]{:S(2)}) collective-permute-start(bf16[32,512]{1,0:T(8,128)(2,1)S(1)} %get-tuple-element.188), channel_id=1, source_target_pairs={{0,2},{1,3},{2,0},{3,1},{4,6},{5,7},{6,4},{7,5},{8,10},{9,11},{10,... | collective-permute-start | bytes 98312 | tf_op jit(solution)/shard_map/ppermute | solution.py:256
  15.2 4.4 %collective-permute-start.8 = (bf16[32,512]{1,0:T(8,128)(2,1)S(1)}, bf16[32,512]{1,0:T(8,128)(2,1)S(1)}, u32[]{:S(2)}, u32[]{:S(2)}) collective-permute-start(bf16[32,512]{1,0:T(8,128)(2,1)S(1)} %get-tuple-element.190), channel_id=1, source_target_pairs={{0,4},{4,0},{8,12},{12,8},{1,5},{5,1},{9,13},{13,9},{2,6},{6,2},{1... | collective-permute-start | bytes 98312 | tf_op jit(solution)/shard_map/ppermute | solution.py:254
  20.4 7.7 %collective-permute-start.10 = (bf16[16,512]{1,0:T(8,128)(2,1)S(1)}, bf16[16,512]{1,0:T(8,128)(2,1)S(1)}, u32[]{:S(2)}, u32[]{:S(2)}) collective-permute-start(bf16[16,512]{1,0:T(8,128)(2,1)S(1)} %get-tuple-element.199), channel_id=1, source_target_pairs={{0,12},{4,8},{8,4},{12,0},{1,13},{5,9},{9,5},{13,1},{2,14},{6,10},... | collective-permute-start | bytes 49160 | tf_op jit(solution)/shard_map/ppermute | solution.py:253
  23.0 5.2 %collective-permute-start.11 = (bf16[16,512]{1,0:T(8,128)(2,1)S(1)}, bf16[16,512]{1,0:T(8,128)(2,1)S(1)}, u32[]{:S(2)}, u32[]{:S(2)}) collective-permute-start(bf16[16,512]{1,0:T(8,128)(2,1)S(1)} %get-tuple-element.200), channel_id=1, source_target_pairs={{0,2},{1,3},{2,0},{3,1},{4,6},{5,7},{6,4},{7,5},{8,10},{9,11},{10,... | collective-permute-start | bytes 49160 | tf_op jit(solution)/shard_map/ppermute | solution.py:256
  31.5 6.2 %collective-permute-start.17 = (bf16[8,512]{1,0:T(8,128)(2,1)S(1)}, bf16[8,512]{1,0:T(8,128)(2,1)S(1)}, u32[]{:S(2)}, u32[]{:S(2)}) collective-permute-start(bf16[8,512]{1,0:T(8,128)(2,1)S(1)} %get-tuple-element.238), channel_id=1, source_target_pairs={{0,12},{4,8},{8,4},{12,0},{1,13},{5,9},{9,5},{13,1},{2,14},{6,10},... | collective-permute-start | bytes 24584 | tf_op jit(solution)/shard_map/ppermute | solution.py:253
  32.6 5.2 %collective-permute-start.18 = (bf16[8,512]{1,0:T(8,128)(2,1)S(1)}, bf16[8,512]{1,0:T(8,128)(2,1)S(1)}, u32[]{:S(2)}, u32[]{:S(2)}) collective-permute-start(bf16[8,512]{1,0:T(8,128)(2,1)S(1)} %get-tuple-element.239), channel_id=1, source_target_pairs={{0,2},{1,3},{2,0},{3,1},{4,6},{5,7},{6,4},{7,5},{8,10},{9,11},{10,... | collective-permute-start | bytes 24584 | tf_op jit(solution)/shard_map/ppermute | solution.py:256
  33.6 4.1 %collective-permute-start.19 = (bf16[8,512]{1,0:T(8,128)(2,1)S(1)}, bf16[8,512]{1,0:T(8,128)(2,1)S(1)}, u32[]{:S(2)}, u32[]{:S(2)}) collective-permute-start(bf16[8,512]{1,0:T(8,128)(2,1)S(1)} %get-tuple-element.240), channel_id=1, source_target_pairs={{0,3},{1,2},{2,1},{3,0},{4,7},{5,6},{6,5},{7,4},{8,11},{9,10},{10,... | collective-permute-start | bytes 24584 | tf_op jit(solution)/shard_map/ppermute | solution.py:256
  38.6 12.3 %collective-permute-start.24 = (bf16[512,512]{1,0:T(8,128)(2,1)S(1)}, bf16[512,512]{1,0:T(8,128)(2,1)S(1)}, u32[]{:S(2)}, u32[]{:S(2)}) collective-permute-start(bf16[512,512]{1,0:T(8,128)(2,1)S(1)} %get-tuple-element.274), channel_id=1, source_target_pairs={{0,1},{1,0},{2,3},{3,2},{4,5},{5,4},{6,7},{7,6},{8,9},{9,8},{10,11... | collective-permute-start | bytes 1572872 | tf_op jit(solution)/shard_map/ppermute | solution.py:166
  38.7 11.9 %collective-permute-start.23 = (bf16[384,512]{1,0:T(8,128)(2,1)S(1)}, bf16[384,512]{1,0:T(8,128)(2,1)S(1)}, u32[]{:S(2)}, u32[]{:S(2)}) collective-permute-start(bf16[384,512]{1,0:T(8,128)(2,1)S(1)} %get-tuple-element.266), channel_id=1, source_target_pairs={{0,2},{1,3},{2,0},{3,1},{4,6},{5,7},{6,4},{7,5},{8,10},{9,11},{10,... | collective-permute-start | bytes 1179656 | tf_op jit(solution)/shard_map/ppermute | solution.py:166
  42.8 7.8 %collective-permute-start.22 = (bf16[288,512]{1,0:T(8,128)(2,1)S(1)}, bf16[288,512]{1,0:T(8,128)(2,1)S(1)}, u32[]{:S(2)}, u32[]{:S(2)}) collective-permute-start(bf16[288,512]{1,0:T(8,128)(2,1)S(1)} %get-tuple-element.265), channel_id=1, source_target_pairs={{0,1},{1,0},{2,3},{3,2},{4,5},{5,4},{6,7},{7,6},{8,9},{9,8},{10,11... | collective-permute-start | bytes 884744 | tf_op jit(solution)/shard_map/ppermute | solution.py:166
  43.1 13.1 %collective-permute-start.25 = (bf16[256,512]{1,0:T(8,128)(2,1)S(1)}, bf16[256,512]{1,0:T(8,128)(2,1)S(1)}, u32[]{:S(2)}, u32[]{:S(2)}) collective-permute-start(bf16[256,512]{1,0:T(8,128)(2,1)S(1)} %get-tuple-element.279), channel_id=1, source_target_pairs={{0,2},{1,3},{2,0},{3,1},{4,6},{5,7},{6,4},{7,5},{8,10},{9,11},{10,... | collective-permute-start | bytes 786440 | tf_op jit(solution)/shard_map/ppermute | solution.py:166
  51.3 10.6 %collective-permute-start.27 = (bf16[256,512]{1,0:T(8,128)(2,1)S(1)}, bf16[256,512]{1,0:T(8,128)(2,1)S(1)}, u32[]{:S(2)}, u32[]{:S(2)}) collective-permute-start(bf16[256,512]{1,0:T(8,128)(2,1)S(1)} %get-tuple-element.288), channel_id=1, source_target_pairs={{0,2},{1,3},{2,0},{3,1},{4,6},{5,7},{6,4},{7,5},{8,10},{9,11},{10,... | collective-permute-start | bytes 786440 | tf_op jit(solution)/shard_map/ppermute | solution.py:166
  52.4 5.7 %collective-permute-start.26 = (bf16[192,512]{1,0:T(8,128)(2,1)S(1)}, bf16[192,512]{1,0:T(8,128)(2,1)S(1)}, u32[]{:S(2)}, u32[]{:S(2)}) collective-permute-start(bf16[192,512]{1,0:T(8,128)(2,1)S(1)} %get-tuple-element.282), channel_id=1, source_target_pairs={{0,4},{1,5},{2,6},{3,7},{4,0},{5,1},{6,2},{7,3},{8,12},{9,13},{10,... | collective-permute-start | bytes 589832 | tf_op jit(solution)/shard_map/ppermute | solution.py:166
  53.5 11.4 %collective-permute-start.31 = (bf16[160,512]{1,0:T(8,128)(2,1)S(1)}, bf16[160,512]{1,0:T(8,128)(2,1)S(1)}, u32[]{:S(2)}, u32[]{:S(2)}) collective-permute-start(bf16[160,512]{1,0:T(8,128)(2,1)S(1)} %get-tuple-element.299), channel_id=1, source_target_pairs={{0,2},{1,3},{2,0},{3,1},{4,6},{5,7},{6,4},{7,5},{8,10},{9,11},{10,... | collective-permute-start | bytes 491528 | tf_op jit(solution)/shard_map/ppermute | solution.py:166
  56.3 6.9 %collective-permute-start.28 = (bf16[128,512]{1,0:T(8,128)(2,1)S(1)}, bf16[128,512]{1,0:T(8,128)(2,1)S(1)}, u32[]{:S(2)}, u32[]{:S(2)}) collective-permute-start(bf16[128,512]{1,0:T(8,128)(2,1)S(1)} %get-tuple-element.291), channel_id=1, source_target_pairs={{0,4},{1,5},{2,6},{3,7},{4,0},{5,1},{6,2},{7,3},{8,12},{9,13},{10,... | collective-permute-start | bytes 393224 | tf_op jit(solution)/shard_map/ppermute | solution.py:166
  58.2 6.0 %collective-permute-start.29 = (bf16[96,512]{1,0:T(8,128)(2,1)S(1)}, bf16[96,512]{1,0:T(8,128)(2,1)S(1)}, u32[]{:S(2)}, u32[]{:S(2)}) collective-permute-start(bf16[96,512]{1,0:T(8,128)(2,1)S(1)} %get-tuple-element.293), channel_id=1, source_target_pairs={{0,8},{1,9},{2,10},{3,11},{4,12},{5,13},{6,14},{7,15},{8,0},{9,1},... | collective-permute-start | bytes 294920 | tf_op jit(solution)/shard_map/ppermute | solution.py:166
  62.0 6.5 %collective-permute-start.32 = (bf16[128,512]{1,0:T(8,128)(2,1)S(1)}, bf16[128,512]{1,0:T(8,128)(2,1)S(1)}, u32[]{:S(2)}, u32[]{:S(2)}) collective-permute-start(bf16[128,512]{1,0:T(8,128)(2,1)S(1)} %get-tuple-element.305), channel_id=1, source_target_pairs={{0,4},{1,5},{2,6},{3,7},{4,0},{5,1},{6,2},{7,3},{8,12},{9,13},{10,... | collective-permute-start | bytes 393224 | tf_op jit(solution)/shard_map/ppermute | solution.py:166
  65.0 5.4 %collective-permute-start.34 = (bf16[96,512]{1,0:T(8,128)(2,1)S(1)}, bf16[96,512]{1,0:T(8,128)(2,1)S(1)}, u32[]{:S(2)}, u32[]{:S(2)}) collective-permute-start(bf16[96,512]{1,0:T(8,128)(2,1)S(1)} %get-tuple-element.310), channel_id=1, source_target_pairs={{0,4},{1,5},{2,6},{3,7},{4,0},{5,1},{6,2},{7,3},{8,12},{9,13},{10,... | collective-permute-start | bytes 294920 | tf_op jit(solution)/shard_map/ppermute | solution.py:166
  66.2 8.8 %collective-permute-start.30 = (bf16[64,512]{1,0:T(8,128)(2,1)S(1)}, bf16[64,512]{1,0:T(8,128)(2,1)S(1)}, u32[]{:S(2)}, u32[]{:S(2)}) collective-permute-start(bf16[64,512]{1,0:T(8,128)(2,1)S(1)} %get-tuple-element.296), channel_id=1, source_target_pairs={{0,8},{1,9},{2,10},{3,11},{4,12},{5,13},{6,14},{7,15},{8,0},{9,1},... | collective-permute-start | bytes 196616 | tf_op jit(solution)/shard_map/ppermute | solution.py:166
  68.6 8.8 %collective-permute-start.33 = (bf16[64,512]{1,0:T(8,128)(2,1)S(1)}, bf16[64,512]{1,0:T(8,128)(2,1)S(1)}, u32[]{:S(2)}, u32[]{:S(2)}) collective-permute-start(bf16[64,512]{1,0:T(8,128)(2,1)S(1)} %get-tuple-element.308), channel_id=1, source_target_pairs={{0,8},{1,9},{2,10},{3,11},{4,12},{5,13},{6,14},{7,15},{8,0},{9,1},... | collective-permute-start | bytes 196616 | tf_op jit(solution)/shard_map/ppermute | solution.py:166
  70.5 6.9 %collective-permute-start.35 = (bf16[48,512]{1,0:T(8,128)(2,1)S(1)}, bf16[48,512]{1,0:T(8,128)(2,1)S(1)}, u32[]{:S(2)}, u32[]{:S(2)}) collective-permute-start(bf16[48,512]{1,0:T(8,128)(2,1)S(1)} %get-tuple-element.312), channel_id=1, source_target_pairs={{0,8},{1,9},{2,10},{3,11},{4,12},{5,13},{6,14},{7,15},{8,0},{9,1},... | collective-permute-start | bytes 147464 | tf_op jit(solution)/shard_map/ppermute | solution.py:166
  (15 other events, 57.3 us)
